TPU v7x, 32 devices: a whole 2x2x4 slice. The times are simulated.
32 devices in a mesh: group: 2 (over x), pw: 16 (over z, y, core).
Axes of the slice: x: 2, y: 2, z: 4, core: 2. Of those that a mesh axis runs over, the one named last changes fastest.
Arguments:
- band_coeffs: bfloat16 [32768, 2048], P('pw', 'group'), parts along dimension 1, may hold values from -6 to 6
- projectors: bfloat16 [32768, 1024], P('pw', 'group'), parts along dimension 1, may hold values from -0.03125 to 0.03125
- counts: int32 [4, 4], P('group'), parts along dimension 0, may hold values from 1 to 64, as said below
- atom_of: int32 [4, 256], P('group'), parts along dimension 0, may hold values from 0 to 15
- owners: int32 [4], P('group'), parts along dimension 0, may hold values from 0 to 15, as said below
- couplings: float32 [16, 512, 256], P('pw', 'group'), parts along dimension 1, may hold values from -6 to 6
Outputs:
- applied: bfloat16 [32768, 2048], P('pw', 'group'), parts along dimension 1
There are 2 independent parts, one for each index of `group`. A program takes and returns all parts, laid end to end along the dimension named above; each array names one. Nothing has to cross between parts.
Inputs may be any that keep to these rules, and one draw needn't show every extreme that they name: `counts`: some entry equals 64 and some entry equals 1. The owners are distinct.
All inputs are finite; a program needn't handle non-finite values.
Results may differ from a plain program's by a relative error of at most 0.005.
Values may be sent and summed in bfloat16 or wider, within the bound.
No kernel may reach another device: no remote copies, remote signals or barrier semaphores. Data moves between devices by JAX's collectives and lax.ppermute only.
A program may use at most 64 MiB of HBM per device.

v0:
```python
import jax
import jax.numpy as jnp
from jax import lax
from jax.sharding import PartitionSpec as P

GROUPS = 2
CHANNELS = 4
CH_CAP = 64
PCAP = 256
PROJ = 512


def from_root(x, axis, root):
    mine = lax.axis_index(axis) == root
    return lax.psum(jnp.where(mine, x, jnp.zeros_like(x)), axis)


def alive_mask(counts):
    slot_index = jnp.arange(PCAP, dtype=jnp.int32)
    channel = slot_index // CH_CAP
    within = slot_index % CH_CAP
    onehot = (channel[None, :] == jnp.arange(CHANNELS, dtype=jnp.int32)[:, None]).astype(jnp.int32)
    slot_count = jnp.sum(counts[:, :, None] * onehot[None, :, :], axis=1)
    return (within[None, :] < slot_count).astype(jnp.bfloat16).reshape(PROJ)


def apply_coupling(coupling, proj_rows):
    band_count = proj_rows.shape[1]
    grouped = proj_rows.reshape(GROUPS, PCAP, band_count)
    scaled = jnp.einsum("gij,gjb->gib", coupling, grouped, precision=lax.Precision.HIGHEST)
    return scaled.astype(jnp.bfloat16).reshape(PROJ, band_count)


def local(band_coeffs, projectors, counts, atom_of, owners, couplings):
    alive = alive_mask(counts)
    masked_proj = projectors * alive[None, :]
    partial_proj = lax.dot_general(
        masked_proj, band_coeffs, (((0,), (0,)), ((), ())), preferred_element_type=jnp.float32
    )
    own_table = couplings[0]
    fetched = []
    for group_id in range(GROUPS):
        fetched.append(from_root(own_table, "pw", owners[group_id]))
    tables = jnp.stack(fetched)
    same_atom = atom_of[:, :, None] == atom_of[:, None, :]
    coupling_full = jnp.where(same_atom, tables, jnp.zeros((), jnp.float32))
    proj_sums = lax.psum(partial_proj, "pw")
    scaled = apply_coupling(coupling_full, proj_sums)
    return jnp.dot(masked_proj, scaled, preferred_element_type=jnp.float32).astype(jnp.bfloat16)


def solution(mesh):
    placed = (
        P("pw", "group"),
        P("pw", "group"),
        P("group", None),
        P("group", None),
        P("group"),
        P("pw", "group", None),
    )
    return jax.shard_map(
        local, mesh=mesh, in_specs=placed, out_specs=P("pw", "group"), check_vma=False
    )
```

profile of v0, /device:TPU:0, one launch (start us, length us, event | category | flops | bytes accessed | tf_op | source)
XLA Modules:
  0.0 136.9 jit_solution(17096445584272889606)
XLA Ops:
  6.5 0.0 all-reduce.3.cloned.1.call-start
  6.5 1.3 fusion.16
  9.2 0.8 multiply_reduce_fusion
  9.9 1.8 %broadcast_select_fusion.1 = (f32[1,256,256]{2,1,0:T(8,128)}, f32[1,256,256]{2,1,0:T(8,128)}) fusion(f32[1,256,256]{2,1,0:T(8,128)} %param.11, pred[]{:T(512)S(6)} %eq.44, pred[]{:T(512)S(6)} %eq.45), kind=kLoop, calls=%fused_computation.15 | loop fusion | flops 131072 | bytes 786434 | tf_op jit(solution)/shard_map/jit(_where)/select_n | solution.py:15
  11.7 6.5 %fusion.1 = f32[512,1024]{1,0:T(8,128)} fusion(bf16[2048,1024]{1,0:T(8,128)(2,1)} %param.6, bf16[2048,512]{1,0:T(8,128)(2,1)} %param.7, bf16[512]{0:T(512)(128)(2,1)S(1)} %bitcast.12), kind=kOutput, calls=%fused_computation.2 | convolution fusion | flops 2148532224 | bytes 8389632 | tf_op jit(solution)/shard_map/dot_general | solution.py:37
  18.2 0.0 copy-start
  18.2 0.0 all-reduce.3.cloned.1.call-update
  18.3 0.0 copy-start.1
  18.3 103.7 %all-reduce.3.cloned.1.call-done = (f32[2,256,1024]{2,1,0:T(8,128)}, f32[1,256,256]{2,1,0:T(8,128)}, f32[1,256,256]{2,1,0:T(8,128)}) async-done(((f32[2,256,1024]{2,1,0:T(8,128)}, f32[1,256,256]{2,1,0:T(8,128)}, f32[1,256,256]{2,1,0:T(8,128)}), (f32[2,256,1024]{2,1,0:T(8,128)}, f32[1,256,256]{2,1,0:T(8,128)}, f32[1,256,256]{2,1,0:T(8,128)})) %all-reduce.3.cloned.1.call-update) | async-done | bytes 2621456 | tf_op jit(solution)/shard_map/psum | solution.py:47
  122.0 0.0 copy-done
  122.0 3.7 %convolution_convert_fusion.1 = bf16[2,256,1024]{2,1,0:T(8,128)(2,1)S(1)} fusion(f32[2,256,1024]{2,1,0:T(8,128)} %get-tuple-element.5, f32[1,256,256]{2,1,0:T(8,128)} %get-tuple-element.6, f32[1,256,256]{2,1,0:T(8,128)} %get-tuple-element.7, s32[2,256]{1,0:T(2,128)S(1)} %copy-done), kind=kOutput, calls=%fused_computation.4 | convolution fusion | flops 1611530240 | bytes 3672064 | tf_op jit(solution)/shard_map/gij,gjb->gib/dot_general | solution.py:30
  125.7 0.0 copy-done.1
  125.7 4.4 %convolution_convert_fusion = bf16[2048,1024]{1,0:T(8,128)(2,1)} fusion(bf16[512,1024]{1,0:T(8,128)(2,1)S(1)} %bitcast.11, bf16[2048,512]{1,0:T(8,128)(2,1)S(1)} %copy-done.1, bf16[512]{0:T(512)(128)(2,1)S(1)} %bitcast.13), kind=kOutput, calls=%fused_computation | convolution fusion | flops 2150629376 | bytes 7341056 | tf_op jit(solution)/shard_map/dot_general | solution.py:49
  (5 shorter events, 0.0 us)
Async XLA Ops:
  6.5 115.5 %all-reduce.3.cloned.1.call-start = ((), (), s32[]{:S(2)}) async-start(), calls=%async_computation | async-start | bytes 5242880 | tf_op jit(solution)/shard_map/psum | solution.py:47
  18.2 103.8 %copy-start = (s32[2,256]{1,0:T(2,128)S(1)}, s32[2,256]{1,0:T(2,128)}, u32[]{:S(2)}) copy-start(s32[2,256]{1,0:T(2,128)} %param.9) | copy-start | bytes 6148
  18.3 107.4 %copy-start.1 = (bf16[2048,512]{1,0:T(8,128)(2,1)S(1)}, bf16[2048,512]{1,0:T(8,128)(2,1)}, u32[]{:S(2)}) copy-start(bf16[2048,512]{1,0:T(8,128)(2,1)} %param.7) | copy-start | bytes 6291460
Sparse Core Ops, SparseCore 0:
  18.4 103.5 all-reduce.2
where the time goes:
time: 137 us
  waiting for transfers between devices  104 us (76%)
  between operations  14.7 us (11%)
  matrix products  14.5 us (11%)
  other arithmetic  2.59 us (2%)
    psum x1, waiting for transfers between devices, local(): proj_sums = lax.psum(partial_proj, 'pw')  104 us
    dot_general x1, matrix products, local(): lax.dot_general(masked_proj, band_coeffs, (((0,), (0,)), ((), ())), prefe...  6.49 us
    dot_general x1, matrix products, local(): jnp.dot(masked_proj, scaled, preferred_element_type=jnp.float32)  4.38 us
    dot_general x1, matrix products, apply_coupling(): jnp.einsum('gij,gjb->gib', coupling, grouped, precision=lax.Precision.HIG...  3.66 us
  transfers between devices with their start and end apart: 1, of which 1 were waited for; matrix products, arithmetic and copies ran while one was open for 0% of the time, Pallas kernels for 0%

commit v1 on v0

v1 whole, which is shorter than its diff:
```python
import jax
import jax.numpy as jnp
from jax import lax
from jax.sharding import PartitionSpec as P

CHANNELS = 4
CH_CAP = 64
PCAP = 256
PROJ = 512


def alive_mask(counts):
    slot = jnp.arange(CH_CAP, dtype=jnp.int32)
    return (slot[None, None, :] < counts[:, :, None]).astype(jnp.bfloat16).reshape(PROJ)


def swap(x, distance):
    count = lax.axis_size("pw")
    return lax.ppermute(x, "pw", [(i, i ^ distance) for i in range(count)])


def gathered_table(own_table, wanted, me, chips):
    sibling_table = swap(own_table, 1)
    part = jnp.where(wanted == me, own_table, jnp.where(wanted == (me ^ 1), sibling_table, 0.0))
    bit = chips // 2
    while bit:
        half = part.shape[0] // 2
        high = (me // 2) & bit != 0
        kept = jnp.where(high, part[half:], part[:half])
        sent = jnp.where(high, part[:half], part[half:])
        part = kept + swap(sent, 2 * bit)
        bit //= 2
    bit = 1
    while bit < chips:
        high = (me // 2) & bit != 0
        other = swap(part, 2 * bit)
        part = jnp.where(high, jnp.concatenate([other, part]), jnp.concatenate([part, other]))
        bit *= 2
    return part


def local(band_coeffs, projectors, counts, atom_of, owners, couplings):
    chips = lax.axis_size("pw") // 2
    me = lax.axis_index("pw")
    chip, core = me // 2, me % 2
    width = band_coeffs.shape[1] // chips

    masked = projectors * alive_mask(counts)[None, :]
    table = gathered_table(couplings[0], owners[core], me, chips)
    atoms = atom_of[core]
    coupling = jnp.where(atoms[:, None] == atoms[None, :], table, 0.0)

    def project(group):
        columns = lax.dynamic_slice_in_dim(masked, group * PCAP, PCAP, 1)
        return lax.dot_general(columns, band_coeffs, (((0,), (0,)), ((), ())), preferred_element_type=jnp.float32)

    theirs = project(1 - core).astype(jnp.bfloat16)
    sums = project(core) + swap(theirs, 1).astype(jnp.float32)

    def chunk(x, at):
        return lax.dynamic_slice_in_dim(x, at * width, width, 1)

    total = chunk(sums, chip)
    for s in range(1, chips):
        total = total + swap(chunk(sums, chip ^ s).astype(jnp.bfloat16), 2 * s).astype(jnp.float32)

    scaled = jnp.dot(coupling, total, precision=lax.Precision.HIGHEST).astype(jnp.bfloat16)
    mine = jnp.zeros((PCAP, band_coeffs.shape[1]), jnp.bfloat16)
    for s in range(chips):
        piece = scaled if s == 0 else swap(scaled, 2 * s)
        mine = lax.dynamic_update_slice_in_dim(mine, piece, (chip ^ s) * width, 1)
    other = swap(mine, 1)
    both = jnp.where(core == 0, jnp.concatenate([mine, other]), jnp.concatenate([other, mine]))
    return jnp.dot(masked, both, preferred_element_type=jnp.float32).astype(jnp.bfloat16)


def solution(mesh):
    placed = (
        P("pw", "group"),
        P("pw", "group"),
        P("group", None),
        P("group", None),
        P("group"),
        P("pw", "group", None),
    )
    return jax.shard_map(
        local, mesh=mesh, in_specs=placed, out_specs=P("pw", "group"), check_vma=False
    )
```

time: 137 us -> 82.1 us (0.60)
  waiting for transfers between devices: 104 us -> 25.8 us
  starting transfers between devices: 0.01 us -> 36.3 us
  between operations: 14.7 us -> 1.53 us
  matrix products: 14.5 us -> 12.9 us
    psum x1 -> x0, waiting for transfers between devices: 104 us -> none  [local(): proj_sums = lax.psum(partial_proj, 'pw')]
    ppermute x0 -> x23, starting transfers between devices: none -> 36.3 us  [swap(): return lax.ppermute(x, 'pw', [(i, i ^ distance) for i in range(count)])]
    ppermute x0 -> x23, waiting for transfers between devices: none -> 25.8 us  [swap(): return lax.ppermute(x, 'pw', [(i, i ^ distance) for i in range(count)])]
    mul x0 -> x1, other arithmetic: none -> 1.73 us  [local(): masked = projectors * alive_mask(counts)[None, :]]
    dot_general x3 -> x4, matrix products: 14.5 us -> 12.9 us  [the longest x2 7.06 us: project(): lax.dot_general(columns, band_coeffs, (((0,), (0,)), ((), ())), preferred...]
  transfers between devices with their start and end apart: 1 -> 23, of which waited for: 1 -> 9; matrix products, arithmetic and copies ran while one was open for 0% -> 14% of each run, Pallas kernels for 0% -> 0%
where the time goes in v1:
time: 82.1 us; the launch traced here: 81.8 us
  starting transfers between devices  36.3 us (44%)
  waiting for transfers between devices  25.8 us (31%)
  matrix products  12.9 us (16%)
  other arithmetic  3.58 us (4%)
  local copies, waits for them, and re-layouts  1.68 us (2%)
  between operations  1.53 us (2%)
    ppermute x23, starting transfers between devices, swap(): return lax.ppermute(x, 'pw', [(i, i ^ distance) for i in range(count)])  36.3 us
    ppermute x23, waiting for transfers between devices, swap(): return lax.ppermute(x, 'pw', [(i, i ^ distance) for i in range(count)])  25.8 us
    dot_general x2, matrix products, project(): lax.dot_general(columns, band_coeffs, (((0,), (0,)), ((), ())), preferred...  7.06 us
    dot_general x1, matrix products, local(): jnp.dot(masked, both, preferred_element_type=jnp.float32)  4.43 us
    mul x1, other arithmetic, local(): masked = projectors * alive_mask(counts)[None, :]  1.73 us
  transfers between devices with their start and end apart: 23, of which 9 were waited for; matrix products, arithmetic and copies ran while one was open for 14% of the time, Pallas kernels for 0%

profile of v1, /device:TPU:0, one launch (start us, length us, event | category | flops | bytes accessed | tf_op | source)
XLA Modules:
  0.0 81.8 jit_solution(6739479804730759642)
XLA Ops:
  0.0 0.0 copy-start
  0.0 0.5 collective-permute-start
  0.5 1.2 %dynamic_slice.37 = s32[1]{0:T(128)} dynamic-slice(s32[2]{0:T(128)} %param.10, s32[]{:T(128)S(6)} %select_n.143), dynamic_slice_sizes={1} | dynamic-slice | bytes 12 | tf_op jit(solution)/shard_map/dynamic_slice | solution.py:49
  3.0 0.8 fusion.41
  3.7 0.1 reshape.19
  3.8 0.0 collective-permute-done
  3.8 1.0 %select_select_fusion = f32[256,256]{1,0:T(8,128)S(1)} fusion(f32[256,256]{1,0:T(8,128)S(1)} %collective-permute-done, pred[]{:T(512)S(6)} %eq.32, pred[]{:T(512)S(6)} %eq.31, f32[1,256,256]{2,1,0:T(8,128)} %param.11), kind=kLoop, calls=%fused_computation.22 | loop fusion | flops 131072 | bytes 786434 | tf_op jit(solution)/shard_map/jit(_where)/select_n | solution.py:24
  4.9 3.7 %collective-permute-start.1 = (f32[128,256]{1,0:T(8,128)S(1)}, f32[128,256]{1,0:T(8,128)S(1)}, u32[]{:S(2)}, u32[]{:S(2)}) collective-permute-start(f32[128,256]{1,0:T(8,128)S(1)} %slice_select_fusion), channel_id=1, source_target_pairs={{0,8},{1,9},{2,10},{3,11},{4,12},{5,13},{6,14},{7,15},{8,0},{9,1},... | collective-permute-start | bytes 393224 | tf_op jit(solution)/shard_map/ppermute | solution.py:19
  8.6 1.7 %broadcast_multiply_fusion = bf16[2048,512]{1,0:T(8,128)(2,1)S(1)} fusion(bf16[2048,512]{1,0:T(8,128)(2,1)} %param.7, bf16[512]{0:T(512)(128)(2,1)S(1)} %reshape.19), kind=kLoop, calls=%fused_computation.13 | loop fusion | flops 1048576 | bytes 4195328 | tf_op jit(solution)/shard_map/mul | solution.py:48
  10.3 5.2 %collective-permute-done.1 = f32[128,256]{1,0:T(8,128)S(1)} collective-permute-done((f32[128,256]{1,0:T(8,128)S(1)}, f32[128,256]{1,0:T(8,128)S(1)}, u32[]{:S(2)}, u32[]{:S(2)}) %collective-permute-start.1) | collective-permute-done | bytes 131104 | tf_op jit(solution)/shard_map/ppermute | solution.py:19
  15.5 0.8 collective-permute-start.2
  16.3 3.5 %convolution_convert_fusion.1 = bf16[256,1024]{1,0:T(8,128)(2,1)S(1)} fusion(bf16[2048,1024]{1,0:T(8,128)(2,1)} %param.6, bf16[2048,512]{1,0:T(8,128)(2,1)S(1)} %broadcast_multiply_fusion, s32[]{:T(128)S(6)} %select_n.166), kind=kOutput, calls=%fused_computation.1 | convolution fusion | flops 1074003968 | bytes 5767172 | tf_op jit(solution)/shard_map/dot_general | solution.py:55
  19.8 0.1 collective-permute-start.7
  19.9 0.0 collective-permute-done.2
  19.9 1.6 %collective-permute-start.3 = (f32[32,256]{1,0:T(8,128)S(1)}, f32[32,256]{1,0:T(8,128)S(1)}, u32[]{:S(2)}, u32[]{:S(2)}) collective-permute-start(f32[32,256]{1,0:T(8,128)S(1)} %slice_select_fusion.2), channel_id=1, source_target_pairs={{0,2},{1,3},{2,0},{3,1},{4,6},{5,7},{6,4},{7,5},{8,10},{9,11},{10,... | collective-permute-start | bytes 98312 | tf_op jit(solution)/shard_map/ppermute | solution.py:19
  21.5 2.4 %collective-permute-done.3 = f32[32,256]{1,0:T(8,128)S(1)} collective-permute-done((f32[32,256]{1,0:T(8,128)S(1)}, f32[32,256]{1,0:T(8,128)S(1)}, u32[]{:S(2)}, u32[]{:S(2)}) %collective-permute-start.3) | collective-permute-done | bytes 32800 | tf_op jit(solution)/shard_map/ppermute | solution.py:19
  23.9 1.5 %collective-permute-start.4 = (f32[32,256]{1,0:T(8,128)S(1)}, f32[32,256]{1,0:T(8,128)S(1)}, u32[]{:S(2)}, u32[]{:S(2)}) collective-permute-start(f32[32,256]{1,0:T(8,128)S(1)} %select_add_fusion.2), channel_id=1, source_target_pairs={{0,2},{1,3},{2,0},{3,1},{4,6},{5,7},{6,4},{7,5},{8,10},{9,11},{10,... | collective-permute-start | bytes 98312 | tf_op jit(solution)/shard_map/ppermute | solution.py:19
  25.5 2.4 %collective-permute-done.4 = f32[32,256]{1,0:T(8,128)S(1)} collective-permute-done((f32[32,256]{1,0:T(8,128)S(1)}, f32[32,256]{1,0:T(8,128)S(1)}, u32[]{:S(2)}, u32[]{:S(2)}) %collective-permute-start.4) | collective-permute-done | bytes 32800 | tf_op jit(solution)/shard_map/ppermute | solution.py:19
  27.9 1.4 %collective-permute-start.5 = (f32[64,256]{1,0:T(8,128)S(1)}, f32[64,256]{1,0:T(8,128)S(1)}, u32[]{:S(2)}, u32[]{:S(2)}) collective-permute-start(f32[64,256]{1,0:T(8,128)S(1)} %maximum_select_fusion.4), channel_id=1, source_target_pairs={{0,4},{1,5},{2,6},{3,7},{4,0},{5,1},{6,2},{7,3},{8,12},{9,13},{10,... | collective-permute-start | bytes 196616 | tf_op jit(solution)/shard_map/ppermute | solution.py:19
  29.2 0.0 collective-permute-done.7
  29.2 3.6 %convert_add_fusion = f32[256,1024]{1,0:T(8,128)S(1)} fusion(bf16[256,1024]{1,0:T(8,128)(2,1)} %collective-permute-done.7, bf16[2048,1024]{1,0:T(8,128)(2,1)} %param.6, bf16[2048,512]{1,0:T(8,128)(2,1)S(1)} %broadcast_multiply_fusion, s32[]{:T(128)S(6)} %select_n.165), kind=kOutput, calls=%fused_computation.9 | convolution fusion | flops 1074266112 | bytes 6815748 | tf_op jit(solution)/shard_map/dot_general | solution.py:55
  32.8 0.0 copy-start.1
  32.8 0.1 dynamic-slice_convert_fusion.6
  33.0 1.6 %collective-permute-start.8 = (bf16[256,128]{1,0:T(8,128)(2,1)S(1)}, bf16[256,128]{1,0:T(8,128)(2,1)S(1)}, u32[]{:S(2)}, u32[]{:S(2)}) collective-permute-start(bf16[256,128]{1,0:T(8,128)(2,1)S(1)} %get-tuple-element.5), channel_id=1, source_target_pairs={{0,2},{1,3},{2,0},{3,1},{4,6},{5,7},{6,4},{7,5},{8,10},{9,11},{10,... | collective-permute-start | bytes 196616 | tf_op jit(solution)/shard_map/ppermute | solution.py:19
  34.6 3.4 %collective-permute-start.14 = (bf16[256,128]{1,0:T(8,128)(2,1)S(1)}, bf16[256,128]{1,0:T(8,128)(2,1)S(1)}, u32[]{:S(2)}, u32[]{:S(2)}) collective-permute-start(bf16[256,128]{1,0:T(8,128)(2,1)S(1)} %get-tuple-element.6), channel_id=1, source_target_pairs={{0,14},{1,15},{2,12},{3,13},{4,10},{5,11},{6,8},{7,9},{8,6},{9,7},... | collective-permute-start | bytes 196616 | tf_op jit(solution)/shard_map/ppermute | solution.py:19
  38.0 0.3 collective-permute-start.13
  38.3 0.0 collective-permute-done.5
  38.3 0.0 copy-done.1
  38.4 1.0 %collective-permute-start.6 = (f32[128,256]{1,0:T(8,128)S(1)}, f32[128,256]{1,0:T(8,128)S(1)}, u32[]{:S(2)}, u32[]{:S(2)}) collective-permute-start(f32[128,256]{1,0:T(8,128)S(1)} %maximum_select_fusion.3), channel_id=1, source_target_pairs={{0,8},{1,9},{2,10},{3,11},{4,12},{5,13},{6,14},{7,15},{8,0},{9,1},... | collective-permute-start | bytes 393224 | tf_op jit(solution)/shard_map/ppermute | solution.py:19
  39.4 3.0 %collective-permute-start.12 = (bf16[256,128]{1,0:T(8,128)(2,1)S(1)}, bf16[256,128]{1,0:T(8,128)(2,1)S(1)}, u32[]{:S(2)}, u32[]{:S(2)}) collective-permute-start(bf16[256,128]{1,0:T(8,128)(2,1)S(1)} %get-tuple-element.8), channel_id=1, source_target_pairs={{0,10},{1,11},{2,8},{3,9},{4,14},{5,15},{6,12},{7,13},{8,2},{9,3},... | collective-permute-start | bytes 196616 | tf_op jit(solution)/shard_map/ppermute | solution.py:19
  42.4 0.0 collective-permute-done.8
  42.4 0.9 %collective-permute-start.11 = (bf16[256,128]{1,0:T(8,128)(2,1)S(1)}, bf16[256,128]{1,0:T(8,128)(2,1)S(1)}, u32[]{:S(2)}, u32[]{:S(2)}) collective-permute-start(bf16[256,128]{1,0:T(8,128)(2,1)S(1)} %get-tuple-element.9), channel_id=1, source_target_pairs={{0,8},{1,9},{2,10},{3,11},{4,12},{5,13},{6,14},{7,15},{8,0},{9,1},... | collective-permute-start | bytes 196616 | tf_op jit(solution)/shard_map/ppermute | solution.py:19
  43.3 0.0 collective-permute-done.14
  43.3 4.0 %collective-permute-start.10 = (bf16[256,128]{1,0:T(8,128)(2,1)S(1)}, bf16[256,128]{1,0:T(8,128)(2,1)S(1)}, u32[]{:S(2)}, u32[]{:S(2)}) collective-permute-start(bf16[256,128]{1,0:T(8,128)(2,1)S(1)} %get-tuple-element.10), channel_id=1, source_target_pairs={{0,6},{1,7},{2,4},{3,5},{4,2},{5,3},{6,0},{7,1},{8,14},{9,15},{10,... | collective-permute-start | bytes 196616 | tf_op jit(solution)/shard_map/ppermute | solution.py:19
  47.2 0.0 collective-permute-done.13
  47.2 1.3 %collective-permute-start.9 = (bf16[256,128]{1,0:T(8,128)(2,1)S(1)}, bf16[256,128]{1,0:T(8,128)(2,1)S(1)}, u32[]{:S(2)}, u32[]{:S(2)}) collective-permute-start(bf16[256,128]{1,0:T(8,128)(2,1)S(1)} %get-tuple-element.11), channel_id=1, source_target_pairs={{0,4},{1,5},{2,6},{3,7},{4,0},{5,1},{6,2},{7,3},{8,12},{9,13},{10,... | collective-permute-start | bytes 196616 | tf_op jit(solution)/shard_map/ppermute | solution.py:19
  48.6 0.0 copy-done
  48.6 4.8 %collective-permute-done.12 = bf16[256,128]{1,0:T(8,128)(2,1)S(1)} collective-permute-done((bf16[256,128]{1,0:T(8,128)(2,1)S(1)}, bf16[256,128]{1,0:T(8,128)(2,1)S(1)}, u32[]{:S(2)}, u32[]{:S(2)}) %collective-permute-start.12) | collective-permute-done | bytes 65568 | tf_op jit(solution)/shard_map/ppermute | solution.py:19
  53.4 0.3 collective-permute-done.11
  53.7 0.0 collective-permute-done.10
  53.7 0.6 collective-permute-done.9
  54.3 0.0 collective-permute-done.6
  54.3 0.1 broadcast_in_dim.11
  54.4 1.4 %constant_dynamic-update-slice_fusion.7 = (bf16[256,1024]{1,0:T(8,128)(2,1)S(1)}, bf16[256,128]{1,0:T(8,128)(2,1)S(1)}) fusion(bf16[256,1024]{1,0:T(8,128)(2,1)S(1)} %broadcast_in_dim.11, s32[]{:T(128)S(6)} %select_n.167, bf16[256,128]{1,0:T(8,128)(2,1)S(1)} %collective-permute-done.14, bf16[256,128]{1,0:T(8,128)(2,1)S(1)} %collective-permute-done.13, ...), kind=kOutput, calls=%fused_computation.65 | convolution fusion | flops 101482496 | bytes 986624 | tf_op jit(solution)/shard_map/dot_general | solution.py:67
  55.8 1.0 %collective-permute-start.15 = (bf16[256,128]{1,0:T(8,128)(2,1)S(1)}, bf16[256,128]{1,0:T(8,128)(2,1)S(1)}, u32[]{:S(2)}, u32[]{:S(2)}) collective-permute-start(bf16[256,128]{1,0:T(8,128)(2,1)S(1)} %get-tuple-element.13), channel_id=1, source_target_pairs={{0,2},{1,3},{2,0},{3,1},{4,6},{5,7},{6,4},{7,5},{8,10},{9,11},{10,... | collective-permute-start | bytes 196616 | tf_op jit(solution)/shard_map/ppermute | solution.py:19
  56.8 2.8 %collective-permute-start.20 = (bf16[256,128]{1,0:T(8,128)(2,1)S(1)}, bf16[256,128]{1,0:T(8,128)(2,1)S(1)}, u32[]{:S(2)}, u32[]{:S(2)}) collective-permute-start(bf16[256,128]{1,0:T(8,128)(2,1)S(1)} %get-tuple-element.13), channel_id=1, source_target_pairs={{0,12},{1,13},{2,14},{3,15},{4,8},{5,9},{6,10},{7,11},{8,4},{9,5},... | collective-permute-start | bytes 196616 | tf_op jit(solution)/shard_map/ppermute | solution.py:19
  59.6 0.0 collective-permute-start.19
  59.6 3.2 %collective-permute-start.18 = (bf16[256,128]{1,0:T(8,128)(2,1)S(1)}, bf16[256,128]{1,0:T(8,128)(2,1)S(1)}, u32[]{:S(2)}, u32[]{:S(2)}) collective-permute-start(bf16[256,128]{1,0:T(8,128)(2,1)S(1)} %get-tuple-element.13), channel_id=1, source_target_pairs={{0,8},{1,9},{2,10},{3,11},{4,12},{5,13},{6,14},{7,15},{8,0},{9,1},... | collective-permute-start | bytes 196616 | tf_op jit(solution)/shard_map/ppermute | solution.py:19
  62.8 0.0 collective-permute-start.17
  62.8 0.0 collective-permute-done.15
  62.8 2.7 %collective-permute-start.16 = (bf16[256,128]{1,0:T(8,128)(2,1)S(1)}, bf16[256,128]{1,0:T(8,128)(2,1)S(1)}, u32[]{:S(2)}, u32[]{:S(2)}) collective-permute-start(bf16[256,128]{1,0:T(8,128)(2,1)S(1)} %get-tuple-element.13), channel_id=1, source_target_pairs={{0,4},{1,5},{2,6},{3,7},{4,0},{5,1},{6,2},{7,3},{8,12},{9,13},{10,... | collective-permute-start | bytes 196616 | tf_op jit(solution)/shard_map/ppermute | solution.py:19
  65.5 2.9 %collective-permute-done.16 = bf16[256,128]{1,0:T(8,128)(2,1)S(1)} collective-permute-done((bf16[256,128]{1,0:T(8,128)(2,1)S(1)}, bf16[256,128]{1,0:T(8,128)(2,1)S(1)}, u32[]{:S(2)}, u32[]{:S(2)}) %collective-permute-start.16) | collective-permute-done | bytes 65568 | tf_op jit(solution)/shard_map/ppermute | solution.py:19
  68.4 1.5 %collective-permute-start.21 = (bf16[256,128]{1,0:T(8,128)(2,1)S(1)}, bf16[256,128]{1,0:T(8,128)(2,1)S(1)}, u32[]{:S(2)}, u32[]{:S(2)}) collective-permute-start(bf16[256,128]{1,0:T(8,128)(2,1)S(1)} %get-tuple-element.13), channel_id=1, source_target_pairs={{0,14},{1,15},{2,12},{3,13},{4,10},{5,11},{6,8},{7,9},{8,6},{9,7},... | collective-permute-start | bytes 196616 | tf_op jit(solution)/shard_map/ppermute | solution.py:19
  69.9 0.0 collective-permute-done.17
  70.0 0.0 collective-permute-done.18
  70.0 0.0 collective-permute-done.19
  70.1 0.0 collective-permute-done.20
  70.1 5.3 %collective-permute-done.21 = bf16[256,128]{1,0:T(8,128)(2,1)S(1)} collective-permute-done((bf16[256,128]{1,0:T(8,128)(2,1)S(1)}, bf16[256,128]{1,0:T(8,128)(2,1)S(1)}, u32[]{:S(2)}, u32[]{:S(2)}) %collective-permute-start.21) | collective-permute-done | bytes 65568 | tf_op jit(solution)/shard_map/ppermute | solution.py:19
  75.4 0.1 collective-permute-start.22
  75.5 1.9 %collective-permute-done.22 = bf16[256,1024]{1,0:T(8,128)(2,1)S(1)} collective-permute-done((bf16[256,1024]{1,0:T(8,128)(2,1)S(1)}, bf16[256,1024]{1,0:T(8,128)(2,1)S(1)}, u32[]{:S(2)}, u32[]{:S(2)}) %collective-permute-start.22) | collective-permute-done | bytes 524320 | tf_op jit(solution)/shard_map/ppermute | solution.py:19
  77.4 4.4 %convolution_convert_fusion = bf16[2048,1024]{1,0:T(8,128)(2,1)} fusion(bf16[2048,512]{1,0:T(8,128)(2,1)S(1)} %broadcast_multiply_fusion, bf16[256,1024]{1,0:T(8,128)(2,1)S(1)} %collective-permute-done.22, bf16[256,1024]{1,0:T(8,128)(2,1)S(1)} %constant_dynamic-update-slice_fusion, pred[]{:T(512)S(6)} %eq.26), kind=kOutput, calls=%fused_computation | convolution fusion | flops 2154299392 | bytes 7340033 | tf_op jit(solution)/shard_map/dot_general | solution.py:74
  (16 shorter events, 0.3 us)
Async XLA Ops:
  0.0 48.6 %copy-start = (s32[2,256]{1,0:T(2,128)S(1)}, s32[2,256]{1,0:T(2,128)}, u32[]{:S(2)}) copy-start(s32[2,256]{1,0:T(2,128)} %param.9) | copy-start | bytes 6148
  0.0 3.8 %collective-permute-start = (f32[256,256]{1,0:T(8,128)}, f32[256,256]{1,0:T(8,128)S(1)}, u32[]{:S(2)}, u32[]{:S(2)}) collective-permute-start(f32[256,256]{1,0:T(8,128)} %bitcast.7), channel_id=1, source_target_pairs={{0,1},{1,0},{2,3},{3,2},{4,5},{5,4},{6,7},{7,6},{8,9},{9,8},{10,11... | collective-permute-start | bytes 786440 | tf_op jit(solution)/shard_map/ppermute | solution.py:19
  4.9 10.6 %collective-permute-start.1 = (f32[128,256]{1,0:T(8,128)S(1)}, f32[128,256]{1,0:T(8,128)S(1)}, u32[]{:S(2)}, u32[]{:S(2)}) collective-permute-start(f32[128,256]{1,0:T(8,128)S(1)} %slice_select_fusion), channel_id=1, source_target_pairs={{0,8},{1,9},{2,10},{3,11},{4,12},{5,13},{6,14},{7,15},{8,0},{9,1},... | collective-permute-start | bytes 393224 | tf_op jit(solution)/shard_map/ppermute | solution.py:19
  15.5 4.4 %collective-permute-start.2 = (f32[64,256]{1,0:T(8,128)S(1)}, f32[64,256]{1,0:T(8,128)S(1)}, u32[]{:S(2)}, u32[]{:S(2)}) collective-permute-start(f32[64,256]{1,0:T(8,128)S(1)} %slice_select_fusion.1), channel_id=1, source_target_pairs={{0,4},{1,5},{2,6},{3,7},{4,0},{5,1},{6,2},{7,3},{8,12},{9,13},{10,... | collective-permute-start | bytes 196616 | tf_op jit(solution)/shard_map/ppermute | solution.py:19
  19.8 9.4 %collective-permute-start.7 = (bf16[256,1024]{1,0:T(8,128)(2,1)S(1)}, bf16[256,1024]{1,0:T(8,128)(2,1)}, u32[]{:S(2)}, u32[]{:S(2)}) collective-permute-start(bf16[256,1024]{1,0:T(8,128)(2,1)S(1)} %convolution_convert_fusion.1), channel_id=1, source_target_pairs={{0,1},{1,0},{2,3},{3,2},{4,5},{5,4},{6,7},{7,6},{8,9},{9,8},{10,11... | collective-permute-start | bytes 1572872 | tf_op jit(solution)/shard_map/ppermute | solution.py:19
  19.9 4.0 %collective-permute-start.3 = (f32[32,256]{1,0:T(8,128)S(1)}, f32[32,256]{1,0:T(8,128)S(1)}, u32[]{:S(2)}, u32[]{:S(2)}) collective-permute-start(f32[32,256]{1,0:T(8,128)S(1)} %slice_select_fusion.2), channel_id=1, source_target_pairs={{0,2},{1,3},{2,0},{3,1},{4,6},{5,7},{6,4},{7,5},{8,10},{9,11},{10,... | collective-permute-start | bytes 98312 | tf_op jit(solution)/shard_map/ppermute | solution.py:19
  23.9 3.9 %collective-permute-start.4 = (f32[32,256]{1,0:T(8,128)S(1)}, f32[32,256]{1,0:T(8,128)S(1)}, u32[]{:S(2)}, u32[]{:S(2)}) collective-permute-start(f32[32,256]{1,0:T(8,128)S(1)} %select_add_fusion.2), channel_id=1, source_target_pairs={{0,2},{1,3},{2,0},{3,1},{4,6},{5,7},{6,4},{7,5},{8,10},{9,11},{10,... | collective-permute-start | bytes 98312 | tf_op jit(solution)/shard_map/ppermute | solution.py:19
  27.9 10.5 %collective-permute-start.5 = (f32[64,256]{1,0:T(8,128)S(1)}, f32[64,256]{1,0:T(8,128)S(1)}, u32[]{:S(2)}, u32[]{:S(2)}) collective-permute-start(f32[64,256]{1,0:T(8,128)S(1)} %maximum_select_fusion.4), channel_id=1, source_target_pairs={{0,4},{1,5},{2,6},{3,7},{4,0},{5,1},{6,2},{7,3},{8,12},{9,13},{10,... | collective-permute-start | bytes 196616 | tf_op jit(solution)/shard_map/ppermute | solution.py:19
  32.8 5.5 %copy-start.1 = (f32[256,1024]{1,0:T(8,128)}, f32[256,1024]{1,0:T(8,128)S(1)}, u32[]{:S(2)}) copy-start(f32[256,1024]{1,0:T(8,128)S(1)} %convert_add_fusion) | copy-start | bytes 3145732
  33.0 9.4 %collective-permute-start.8 = (bf16[256,128]{1,0:T(8,128)(2,1)S(1)}, bf16[256,128]{1,0:T(8,128)(2,1)S(1)}, u32[]{:S(2)}, u32[]{:S(2)}) collective-permute-start(bf16[256,128]{1,0:T(8,128)(2,1)S(1)} %get-tuple-element.5), channel_id=1, source_target_pairs={{0,2},{1,3},{2,0},{3,1},{4,6},{5,7},{6,4},{7,5},{8,10},{9,11},{10,... | collective-permute-start | bytes 196616 | tf_op jit(solution)/shard_map/ppermute | solution.py:19
  34.6 8.7 %collective-permute-start.14 = (bf16[256,128]{1,0:T(8,128)(2,1)S(1)}, bf16[256,128]{1,0:T(8,128)(2,1)S(1)}, u32[]{:S(2)}, u32[]{:S(2)}) collective-permute-start(bf16[256,128]{1,0:T(8,128)(2,1)S(1)} %get-tuple-element.6), channel_id=1, source_target_pairs={{0,14},{1,15},{2,12},{3,13},{4,10},{5,11},{6,8},{7,9},{8,6},{9,7},... | collective-permute-start | bytes 196616 | tf_op jit(solution)/shard_map/ppermute | solution.py:19
  38.0 9.2 %collective-permute-start.13 = (bf16[256,128]{1,0:T(8,128)(2,1)S(1)}, bf16[256,128]{1,0:T(8,128)(2,1)S(1)}, u32[]{:S(2)}, u32[]{:S(2)}) collective-permute-start(bf16[256,128]{1,0:T(8,128)(2,1)S(1)} %get-tuple-element.7), channel_id=1, source_target_pairs={{0,12},{1,13},{2,14},{3,15},{4,8},{5,9},{6,10},{7,11},{8,4},{9,5},... | collective-permute-start | bytes 196616 | tf_op jit(solution)/shard_map/ppermute | solution.py:19
  38.4 16.0 %collective-permute-start.6 = (f32[128,256]{1,0:T(8,128)S(1)}, f32[128,256]{1,0:T(8,128)S(1)}, u32[]{:S(2)}, u32[]{:S(2)}) collective-permute-start(f32[128,256]{1,0:T(8,128)S(1)} %maximum_select_fusion.3), channel_id=1, source_target_pairs={{0,8},{1,9},{2,10},{3,11},{4,12},{5,13},{6,14},{7,15},{8,0},{9,1},... | collective-permute-start | bytes 393224 | tf_op jit(solution)/shard_map/ppermute | solution.py:19
  39.4 14.0 %collective-permute-start.12 = (bf16[256,128]{1,0:T(8,128)(2,1)S(1)}, bf16[256,128]{1,0:T(8,128)(2,1)S(1)}, u32[]{:S(2)}, u32[]{:S(2)}) collective-permute-start(bf16[256,128]{1,0:T(8,128)(2,1)S(1)} %get-tuple-element.8), channel_id=1, source_target_pairs={{0,10},{1,11},{2,8},{3,9},{4,14},{5,15},{6,12},{7,13},{8,2},{9,3},... | collective-permute-start | bytes 196616 | tf_op jit(solution)/shard_map/ppermute | solution.py:19
  42.4 11.4 %collective-permute-start.11 = (bf16[256,128]{1,0:T(8,128)(2,1)S(1)}, bf16[256,128]{1,0:T(8,128)(2,1)S(1)}, u32[]{:S(2)}, u32[]{:S(2)}) collective-permute-start(bf16[256,128]{1,0:T(8,128)(2,1)S(1)} %get-tuple-element.9), channel_id=1, source_target_pairs={{0,8},{1,9},{2,10},{3,11},{4,12},{5,13},{6,14},{7,15},{8,0},{9,1},... | collective-permute-start | bytes 196616 | tf_op jit(solution)/shard_map/ppermute | solution.py:19
  43.3 10.4 %collective-permute-start.10 = (bf16[256,128]{1,0:T(8,128)(2,1)S(1)}, bf16[256,128]{1,0:T(8,128)(2,1)S(1)}, u32[]{:S(2)}, u32[]{:S(2)}) collective-permute-start(bf16[256,128]{1,0:T(8,128)(2,1)S(1)} %get-tuple-element.10), channel_id=1, source_target_pairs={{0,6},{1,7},{2,4},{3,5},{4,2},{5,3},{6,0},{7,1},{8,14},{9,15},{10,... | collective-permute-start | bytes 196616 | tf_op jit(solution)/shard_map/ppermute | solution.py:19
  47.2 7.1 %collective-permute-start.9 = (bf16[256,128]{1,0:T(8,128)(2,1)S(1)}, bf16[256,128]{1,0:T(8,128)(2,1)S(1)}, u32[]{:S(2)}, u32[]{:S(2)}) collective-permute-start(bf16[256,128]{1,0:T(8,128)(2,1)S(1)} %get-tuple-element.11), channel_id=1, source_target_pairs={{0,4},{1,5},{2,6},{3,7},{4,0},{5,1},{6,2},{7,3},{8,12},{9,13},{10,... | collective-permute-start | bytes 196616 | tf_op jit(solution)/shard_map/ppermute | solution.py:19
  55.8 7.0 %collective-permute-start.15 = (bf16[256,128]{1,0:T(8,128)(2,1)S(1)}, bf16[256,128]{1,0:T(8,128)(2,1)S(1)}, u32[]{:S(2)}, u32[]{:S(2)}) collective-permute-start(bf16[256,128]{1,0:T(8,128)(2,1)S(1)} %get-tuple-element.13), channel_id=1, source_target_pairs={{0,2},{1,3},{2,0},{3,1},{4,6},{5,7},{6,4},{7,5},{8,10},{9,11},{10,... | collective-permute-start | bytes 196616 | tf_op jit(solution)/shard_map/ppermute | solution.py:19
  56.8 13.3 %collective-permute-start.20 = (bf16[256,128]{1,0:T(8,128)(2,1)S(1)}, bf16[256,128]{1,0:T(8,128)(2,1)S(1)}, u32[]{:S(2)}, u32[]{:S(2)}) collective-permute-start(bf16[256,128]{1,0:T(8,128)(2,1)S(1)} %get-tuple-element.13), channel_id=1, source_target_pairs={{0,12},{1,13},{2,14},{3,15},{4,8},{5,9},{6,10},{7,11},{8,4},{9,5},... | collective-permute-start | bytes 196616 | tf_op jit(solution)/shard_map/ppermute | solution.py:19
  59.6 10.4 %collective-permute-start.19 = (bf16[256,128]{1,0:T(8,128)(2,1)S(1)}, bf16[256,128]{1,0:T(8,128)(2,1)S(1)}, u32[]{:S(2)}, u32[]{:S(2)}) collective-permute-start(bf16[256,128]{1,0:T(8,128)(2,1)S(1)} %get-tuple-element.13), channel_id=1, source_target_pairs={{0,10},{1,11},{2,8},{3,9},{4,14},{5,15},{6,12},{7,13},{8,2},{9,3},... | collective-permute-start | bytes 196616 | tf_op jit(solution)/shard_map/ppermute | solution.py:19
  59.6 10.3 %collective-permute-start.18 = (bf16[256,128]{1,0:T(8,128)(2,1)S(1)}, bf16[256,128]{1,0:T(8,128)(2,1)S(1)}, u32[]{:S(2)}, u32[]{:S(2)}) collective-permute-start(bf16[256,128]{1,0:T(8,128)(2,1)S(1)} %get-tuple-element.13), channel_id=1, source_target_pairs={{0,8},{1,9},{2,10},{3,11},{4,12},{5,13},{6,14},{7,15},{8,0},{9,1},... | collective-permute-start | bytes 196616 | tf_op jit(solution)/shard_map/ppermute | solution.py:19
  62.8 7.1 %collective-permute-start.17 = (bf16[256,128]{1,0:T(8,128)(2,1)S(1)}, bf16[256,128]{1,0:T(8,128)(2,1)S(1)}, u32[]{:S(2)}, u32[]{:S(2)}) collective-permute-start(bf16[256,128]{1,0:T(8,128)(2,1)S(1)} %get-tuple-element.13), channel_id=1, source_target_pairs={{0,6},{1,7},{2,4},{3,5},{4,2},{5,3},{6,0},{7,1},{8,14},{9,15},{10,... | collective-permute-start | bytes 196616 | tf_op jit(solution)/shard_map/ppermute | solution.py:19
  62.8 5.6 %collective-permute-start.16 = (bf16[256,128]{1,0:T(8,128)(2,1)S(1)}, bf16[256,128]{1,0:T(8,128)(2,1)S(1)}, u32[]{:S(2)}, u32[]{:S(2)}) collective-permute-start(bf16[256,128]{1,0:T(8,128)(2,1)S(1)} %get-tuple-element.13), channel_id=1, source_target_pairs={{0,4},{1,5},{2,6},{3,7},{4,0},{5,1},{6,2},{7,3},{8,12},{9,13},{10,... | collective-permute-start | bytes 196616 | tf_op jit(solution)/shard_map/ppermute | solution.py:19
  68.4 7.0 %collective-permute-start.21 = (bf16[256,128]{1,0:T(8,128)(2,1)S(1)}, bf16[256,128]{1,0:T(8,128)(2,1)S(1)}, u32[]{:S(2)}, u32[]{:S(2)}) collective-permute-start(bf16[256,128]{1,0:T(8,128)(2,1)S(1)} %get-tuple-element.13), channel_id=1, source_target_pairs={{0,14},{1,15},{2,12},{3,13},{4,10},{5,11},{6,8},{7,9},{8,6},{9,7},... | collective-permute-start | bytes 196616 | tf_op jit(solution)/shard_map/ppermute | solution.py:19
  75.4 2.0 %collective-permute-start.22 = (bf16[256,1024]{1,0:T(8,128)(2,1)S(1)}, bf16[256,1024]{1,0:T(8,128)(2,1)S(1)}, u32[]{:S(2)}, u32[]{:S(2)}) collective-permute-start(bf16[256,1024]{1,0:T(8,128)(2,1)S(1)} %constant_dynamic-update-slice_fusion), channel_id=1, source_target_pairs={{0,1},{1,0},{2,3},{3,2},{4,5},{5,4},{6,7},{7,6},{8,9},{9,8},{10,11... | collective-permute-start | bytes 1572872 | tf_op jit(solution)/shard_map/ppermute | solution.py:19

commit v2 on v0

v2 whole, which is shorter than its diff:
```python
import jax
import jax.numpy as jnp
from jax import lax
from jax.experimental import pallas as pl
from jax.experimental.pallas import tpu as pltpu
from jax.sharding import PartitionSpec as P

CHANNELS = 4
CH_CAP = 64
PCAP = 256
COLUMNS = 256
VMEM_LIMIT = 40 * 1024 * 1024


def swap_cores(x):
    count = lax.axis_size("pw")
    return lax.ppermute(x, "pw", [(i, i ^ 1) for i in range(count)])


def exchange(x):
    count = lax.axis_size("pw")
    same_core = [list(range(core, count, 2)) for core in range(2)]
    return lax.all_to_all(x, "pw", 0, 0, axis_index_groups=same_core)


def project_kernel(where, projectors, bands, out, flipped):
    @pl.when(pl.program_id(0) == 0)
    def _():
        flipped[...] = projectors[...].T

    sums = jnp.dot(flipped[...], bands[...], preferred_element_type=jnp.float32)
    width = out.shape[2]
    for at in range(out.shape[0]):
        out[at] = sums[:, at * width : (at + 1) * width].astype(out.dtype)


def project(group, projectors, band_coeffs, chips, dtype):
    depth, bands = band_coeffs.shape
    width = bands // chips
    return pl.pallas_call(
        project_kernel,
        grid_spec=pltpu.PrefetchScalarGridSpec(
            num_scalar_prefetch=1,
            grid=(bands // COLUMNS,),
            in_specs=[
                pl.BlockSpec((depth, PCAP), lambda j, where: (0, where[0])),
                pl.BlockSpec((depth, COLUMNS), lambda j, where: (0, j)),
            ],
            out_specs=pl.BlockSpec((COLUMNS // width, PCAP, width), lambda j, where: (j, 0, 0)),
            scratch_shapes=[pltpu.VMEM((PCAP, depth), jnp.bfloat16)],
        ),
        out_shape=jax.ShapeDtypeStruct((chips, PCAP, width), dtype),
        compiler_params=pltpu.CompilerParams(vmem_limit_bytes=VMEM_LIMIT),
        cost_estimate=pl.CostEstimate(
            flops=2 * depth * PCAP * bands, bytes_accessed=2 * depth * (bands + PCAP), transcendentals=0
        ),
        name="project",
    )(group, projectors, band_coeffs)


def pack_kernel(where, sums, theirs, table_rows, message, own):
    chips = sums.shape[0]
    for at in range(chips):
        message[at, :PCAP] = (sums[at] + theirs[at].astype(jnp.float32)).astype(jnp.bfloat16)
        message[at, PCAP:] = table_rows[...]
    chip = where[1]
    own[...] = sums[chip] + theirs[chip].astype(jnp.float32)


def pack(where, sums, theirs, table_rows):
    chips, _, width = sums.shape
    vmem = pl.BlockSpec(memory_space=pltpu.VMEM)
    return pl.pallas_call(
        pack_kernel,
        in_specs=[pl.BlockSpec(memory_space=pltpu.SMEM), vmem, vmem, vmem],
        out_specs=[vmem, vmem],
        out_shape=[
            jax.ShapeDtypeStruct((chips, PCAP + table_rows.shape[0], width), jnp.bfloat16),
            jax.ShapeDtypeStruct((PCAP, width), jnp.float32),
        ],
        compiler_params=pltpu.CompilerParams(vmem_limit_bytes=VMEM_LIMIT),
        name="pack",
    )(where, sums, theirs, table_rows)


def couple_kernel(where, counts, atom_of, message, own, out, table):
    chips, _, width = out.shape
    rows = PCAP // chips
    core, chip = where[0], where[1]
    total = own[...]
    for at in range(chips):
        got = message[at, :PCAP].astype(jnp.float32)
        total = total + jnp.where(at == chip, 0.0, got)
        for piece in range(PCAP // width):
            first = PCAP + piece * rows
            table[at * rows : (at + 1) * rows, piece * width : (piece + 1) * width] = message[
                at, first : first + rows
            ].astype(jnp.float32)
    slot = lax.broadcasted_iota(jnp.int32, (1, PCAP), 1)
    limit = jnp.zeros((1, PCAP), jnp.int32)
    for channel in range(CHANNELS):
        limit = jnp.where(slot >= channel * CH_CAP, channel * CH_CAP + counts[core, channel], limit)
    atoms = jnp.where(core == 0, atom_of[0:1], atom_of[1:2])
    code = jnp.broadcast_to(jnp.where(slot < limit, atoms, -1), (PCAP, PCAP))
    coupling = jnp.where((code == code.T) & (code >= 0), table[...], 0.0)
    scaled = jnp.dot(
        coupling, total, precision=lax.Precision.HIGHEST, preferred_element_type=jnp.float32
    ).astype(jnp.bfloat16)
    for at in range(chips):
        out[at] = scaled


def couple(where, counts, atom_of, message, own):
    chips = message.shape[0]
    vmem = pl.BlockSpec(memory_space=pltpu.VMEM)
    smem = pl.BlockSpec(memory_space=pltpu.SMEM)
    return pl.pallas_call(
        couple_kernel,
        in_specs=[smem, smem, vmem, vmem, vmem],
        out_specs=vmem,
        out_shape=jax.ShapeDtypeStruct((chips,) + own.shape, jnp.bfloat16),
        scratch_shapes=[pltpu.VMEM((PCAP, PCAP), jnp.float32)],
        compiler_params=pltpu.CompilerParams(vmem_limit_bytes=VMEM_LIMIT),
        name="couple",
    )(where, counts, atom_of, message, own)


def apply_kernel(where, projectors, mine, other, out, scaled):
    @pl.when(pl.program_id(0) == 0)
    def _():
        chips, _, width = mine.shape
        core = where[0]
        for part, group in ((mine, core), (other, 1 - core)):
            first = pl.multiple_of(group * PCAP, PCAP)
            for at in range(chips):
                scaled[pl.ds(first, PCAP), at * width : (at + 1) * width] = part[at]

    out[...] = jnp.dot(projectors[...], scaled[...], preferred_element_type=jnp.float32).astype(out.dtype)


def apply(where, projectors, mine, other):
    depth, slots = projectors.shape
    chips, _, width = mine.shape
    block = depth // 8
    whole = pl.BlockSpec((chips, PCAP, width), lambda i, where: (0, 0, 0))
    return pl.pallas_call(
        apply_kernel,
        grid_spec=pltpu.PrefetchScalarGridSpec(
            num_scalar_prefetch=1,
            grid=(depth // block,),
            in_specs=[pl.BlockSpec((block, slots), lambda i, where: (i, 0)), whole, whole],
            out_specs=pl.BlockSpec((block, chips * width), lambda i, where: (i, 0)),
            scratch_shapes=[pltpu.VMEM((slots, chips * width), jnp.bfloat16)],
        ),
        out_shape=jax.ShapeDtypeStruct((depth, chips * width), jnp.bfloat16),
        compiler_params=pltpu.CompilerParams(vmem_limit_bytes=VMEM_LIMIT),
        cost_estimate=pl.CostEstimate(
            flops=2 * depth * slots * chips * width,
            bytes_accessed=2 * depth * (slots + chips * width),
            transcendentals=0,
        ),
        name="apply",
    )(where, projectors, mine, other)


def local(band_coeffs, projectors, counts, atom_of, owners, couplings):
    devices = lax.axis_size("pw")
    chips = devices // 2
    me = lax.axis_index("pw")
    chip, core = me // 2, me % 2
    width = band_coeffs.shape[1] // chips
    rows = PCAP // chips
    where = jnp.stack([core, chip])

    slices = couplings[0].astype(jnp.bfloat16).reshape(chips, rows, PCAP // width, width).transpose(0, 2, 1, 3)
    slices = jnp.broadcast_to(slices.reshape(chips, 1, -1, width), (chips, 2, rows * PCAP // width, width))
    slices = lax.all_to_all(slices.reshape(devices, -1, width), "pw", 0, 0)
    table_rows = lax.dynamic_index_in_dim(slices, owners[core], 0, keepdims=False)

    theirs = swap_cores(project((1 - core)[None], projectors, band_coeffs, chips, jnp.bfloat16))
    sums = project(core[None], projectors, band_coeffs, chips, jnp.float32)
    message, own = pack(where, sums, theirs, table_rows)
    message = exchange(message)
    mine = exchange(couple(where, counts, atom_of, message, own))
    return apply(where, projectors, mine, swap_cores(mine))


def solution(mesh):
    placed = (
        P("pw", "group"),
        P("pw", "group"),
        P("group", None),
        P("group", None),
        P("group"),
        P("pw", "group", None),
    )
    return jax.shard_map(
        local, mesh=mesh, in_specs=placed, out_specs=P("pw", "group"), check_vma=False
    )
```

time: 137 us -> 76.2 us (0.56)
  waiting for transfers between devices: 104 us -> 1.91 us
  blocking collectives: 0 us -> 41.1 us
  Pallas kernels: 0 us -> 14.7 us
  matrix products: 14.5 us -> 0 us
  between operations: 14.7 us -> 1.8 us
  starting transfers between devices: 0.01 us -> 7.78 us
  local copies, waits for them, and re-layouts: 1.36 us -> 7.37 us
  other arithmetic: 2.59 us -> 1.04 us
    psum x1 -> x0, waiting for transfers between devices: 104 us -> none  [local(): proj_sums = lax.psum(partial_proj, 'pw')]
    all_to_all x0 -> x2, blocking collectives: none -> 41.1 us  [exchange(): return lax.all_to_all(x, 'pw', 0, 0, axis_index_groups=same_core)]
    pallas_call x0 -> x5, Pallas kernels: none -> 14.7 us  [the longest x2 6.33 us: project(): pl.pallas_call(project_kernel, grid_spec=pltpu.PrefetchScalarGridSpec(num...]
    dot_general x3 -> x0, matrix products: 14.5 us -> none  [the longest x1 6.49 us: local(): lax.dot_general(masked_proj, band_coeffs, (((0,), (0,)), ((), ())), prefe...]
    all_to_all x0 -> x1, starting transfers between devices: none -> 7.39 us  [local(): slices = lax.all_to_all(slices.reshape(devices, -1, width), 'pw', 0, 0)]
    unnamed x5 -> x14, local copies, waits for them, and re-layouts: 0.02 us -> 5.97 us
    ppermute x0 -> x2, waiting for transfers between devices: none -> 1.91 us  [swap_cores(): return lax.ppermute(x, 'pw', [(i, i ^ 1) for i in range(count)])]
    select_n x3 -> x0, other arithmetic: 1.81 us -> none  [the longest x1 1.8 us: from_root(): return lax.psum(jnp.where(mine, x, jnp.zeros_like(x)), axis)]
  transfers between devices with their start and end apart: 1 -> 3, of which waited for: 1 -> 1; matrix products, arithmetic and copies ran while one was open for 0% -> 1% of each run, Pallas kernels for 0% -> 8%
where the time goes in v2:
time: 76.2 us; the launch traced here: 75.7 us
  blocking collectives  41.1 us (54%)
  Pallas kernels  14.7 us (19%)
  starting transfers between devices  7.78 us (10%)
  local copies, waits for them, and re-layouts  7.37 us (10%)
  waiting for transfers between devices  1.91 us (3%)
  between operations  1.8 us (2%)
  other arithmetic  1.04 us (1%)
    all_to_all x2, blocking collectives, exchange(): return lax.all_to_all(x, 'pw', 0, 0, axis_index_groups=same_core)  41.1 us
    all_to_all x1, starting transfers between devices, local(): slices = lax.all_to_all(slices.reshape(devices, -1, width), 'pw', 0, 0)  7.39 us
    pallas_call x2, Pallas kernels, project(): pl.pallas_call(project_kernel, grid_spec=pltpu.PrefetchScalarGridSpec(num...  6.33 us
    pallas_call x1, Pallas kernels, apply(): pl.pallas_call(apply_kernel, grid_spec=pltpu.PrefetchScalarGridSpec(num_s...  6.24 us
    unnamed x14, local copies, waits for them, and re-layouts  5.97 us
    ppermute x2, waiting for transfers between devices, swap_cores(): return lax.ppermute(x, 'pw', [(i, i ^ 1) for i in range(count)])  1.91 us
  transfers between devices with their start and end apart: 3, of which 1 were waited for; matrix products, arithmetic and copies ran while one was open for 1% of the time, Pallas kernels for 8%

profile of v2, /device:TPU:0, one launch (start us, length us, event | category | flops | bytes accessed | tf_op | source)
XLA Modules:
  0.0 75.7 jit_solution(15114877150944216094)
XLA Ops:
  0.0 1.0 %convert_element_type.7 = bf16[1,256,256]{2,1,0:T(8,128)(2,1)S(1)} convert(f32[1,256,256]{2,1,0:T(8,128)} %param.11) | non-fusion elementwise | flops 65536 | bytes 393216 | tf_op jit(solution)/shard_map/convert_element_type | solution.py:175
  1.0 0.0 copy-start.6
  1.0 0.8 broadcast_in_dim.13
  1.8 7.4 %all-to-all-start = ((bf16[16,64,128]{2,1,0:T(8,128)(2,1)}), bf16[16,64,128]{2,1,0:T(8,128)(2,1)S(1)}, u32[]{:S(2)}, u32[]{:S(2)}) async-start(bf16[16,64,128]{2,1,0:T(8,128)(2,1)} %bitcast.5), calls=%async_computation | async-start | bytes 524288 | tf_op jit(solution)/shard_map/all_to_all | solution.py:177
  9.2 0.0 copy-start
  9.2 2.2 %copy-done = bf16[2048,1024]{1,0:T(8,128)(2,1)S(1)} copy-done((bf16[2048,1024]{1,0:T(8,128)(2,1)S(1)}, bf16[2048,1024]{1,0:T(8,128)(2,1)}, u32[]{:S(2)}) %copy-start) | copy-done | bytes 4194328
  11.4 0.0 copy-start.2
  11.4 1.6 %copy-done.2 = bf16[2048,512]{1,0:T(8,128)(2,1)S(1)} copy-done((bf16[2048,512]{1,0:T(8,128)(2,1)S(1)}, bf16[2048,512]{1,0:T(8,128)(2,1)}, u32[]{:S(2)}) %copy-start.2) | copy-done | bytes 2097176
  13.0 0.0 copy-start.3
  13.0 3.5 %project.3 = bf16[8,256,128]{2,1,0:T(8,128)(2,1)} custom-call(s32[1]{0:T(128)} %bitcast.2.where, bf16[2048,512]{1,0:T(8,128)(2,1)S(1)} %copy-done.2, bf16[2048,1024]{1,0:T(8,128)(2,1)S(1)} %copy-done), custom_call_target="tpu_custom_call" | custom-call | flops 1073741824 | bytes 5242880 | tf_op jit(solution)/shard_map/project/pallas_call | solution.py:40
  16.5 0.4 collective-permute-start
  16.9 0.0 copy-done.6
  16.9 0.6 dynamic_slice.7
  19.2 0.0 copy-done.3
  19.2 0.0 copy-start.1
  19.2 2.2 %copy-done.1 = bf16[2048,1024]{1,0:T(8,128)(2,1)S(1)} copy-done((bf16[2048,1024]{1,0:T(8,128)(2,1)S(1)}, bf16[2048,1024]{1,0:T(8,128)(2,1)}, u32[]{:S(2)}) %copy-start.1) | copy-done | bytes 4194328
  21.4 0.0 copy-start.4
  21.4 0.0 copy-start.5
  21.4 2.8 %project.2.sums = f32[8,256,128]{2,1,0:T(8,128)S(1)} custom-call(s32[1]{0:T(128)} %bitcast.where, bf16[2048,512]{1,0:T(8,128)(2,1)S(1)} %copy-done.3, bf16[2048,1024]{1,0:T(8,128)(2,1)S(1)} %copy-done.1), custom_call_target="tpu_custom_call" | custom-call | flops 1073741824 | bytes 5242880 | tf_op jit(solution)/shard_map/project/pallas_call | solution.py:40
  24.2 0.1 pad_add_fusion.where
  24.3 0.0 all-to-all-done
  24.3 0.0 collective-permute-done.theirs
  24.3 1.2 %pack.1 = (bf16[8,320,128]{2,1,0:T(8,128)(2,1)S(1)}, f32[256,128]{1,0:T(8,128)S(1)}) custom-call(s32[2]{0:T(128)S(1)} %pad_add_fusion.where, f32[8,256,128]{2,1,0:T(8,128)S(1)} %project.2.sums, bf16[8,256,128]{2,1,0:T(8,128)(2,1)} %collective-permute-done.theirs, bf16[64,128]{1,0:T(8,128)(2,1)S(1)} %dynamic-slice_bitcast_fusion.table_rows), custom_call_target="tpu_custom_call" | custom-call | tf_op jit(solution)/shard_map/pack/pallas_call | solution.py:73
  25.5 23.6 %all_to_all.15.message = bf16[8,320,128]{2,1,0:T(8,128)(2,1)S(1)} all-to-all(bf16[8,320,128]{2,1,0:T(8,128)(2,1)S(1)} %get-tuple-element.7), channel_id=1, replica_groups={{0,2,4,6,8,10,12,14},{1,3,5,7,9,11,13,15},{16,18,20,22,24,26,28,30},{17..., dimensions={0} | all-to-all | bytes 1310720 | tf_op jit(solution)/shard_map/all_to_all | solution.py:23
  49.1 0.0 copy-done.4
  49.1 0.0 copy-done.5
  49.1 1.0 %couple.1 = bf16[8,256,128]{2,1,0:T(8,128)(2,1)S(1)} custom-call(s32[2]{0:T(128)S(1)} %pad_add_fusion.where, s32[2,4]{1,0:T(2,128)S(1)} %copy-done.5, s32[2,256]{1,0:T(2,128)S(1)} %copy-done.4, bf16[8,320,128]{2,1,0:T(8,128)(2,1)S(1)} %all_to_all.15.message, f32[256,128]{1,0:T(8,128)S(1)} %get-tuple-element.8.own), custom_call_target="tpu_custom_call" | custom-call | tf_op jit(solution)/shard_map/couple/pallas_call | solution.py:117
  50.1 17.4 %all_to_all.16.mine = bf16[8,256,128]{2,1,0:T(8,128)(2,1)S(1)} all-to-all(bf16[8,256,128]{2,1,0:T(8,128)(2,1)S(1)} %couple.1), channel_id=1, replica_groups={{0,2,4,6,8,10,12,14},{1,3,5,7,9,11,13,15},{16,18,20,22,24,26,28,30},{17..., dimensions={0} | all-to-all | bytes 1048576 | tf_op jit(solution)/shard_map/all_to_all | solution.py:23
  67.5 0.0 collective-permute-start.1
  67.5 1.9 %collective-permute-done.1.other = bf16[8,256,128]{2,1,0:T(8,128)(2,1)S(1)} collective-permute-done((bf16[8,256,128]{2,1,0:T(8,128)(2,1)S(1)}, bf16[8,256,128]{2,1,0:T(8,128)(2,1)S(1)}, u32[]{:S(2)}, u32[]{:S(2)}) %collective-permute-start.1) | collective-permute-done | bytes 524320 | tf_op jit(solution)/shard_map/ppermute | solution.py:17
  69.5 6.2 %apply.1 = bf16[2048,1024]{1,0:T(8,128)(2,1)} custom-call(s32[2]{0:T(128)S(1)} %pad_add_fusion.where, bf16[2048,512]{1,0:T(8,128)(2,1)S(1)} %copy-done.3, bf16[8,256,128]{2,1,0:T(8,128)(2,1)S(1)} %all_to_all.16.mine, bf16[8,256,128]{2,1,0:T(8,128)(2,1)S(1)} %collective-permute-done.1.other), custom_call_target="tpu_custom_call" | custom-call | flops 2147483648 | bytes 6291456 | tf_op jit(solution)/shard_map/apply/pallas_call | solution.py:146
  (3 shorter events, 0.1 us)
Async XLA Ops:
  1.0 15.9 %copy-start.6 = (s32[2]{0:T(128)S(1)}, s32[2]{0:T(128)}, u32[]{:S(2)}) copy-start(s32[2]{0:T(128)} %param.10) | copy-start | bytes 28
  1.8 22.5 %all-to-all-start = ((bf16[16,64,128]{2,1,0:T(8,128)(2,1)}), bf16[16,64,128]{2,1,0:T(8,128)(2,1)S(1)}, u32[]{:S(2)}, u32[]{:S(2)}) async-start(bf16[16,64,128]{2,1,0:T(8,128)(2,1)} %bitcast.5), calls=%async_computation | async-start | bytes 524288 | tf_op jit(solution)/shard_map/all_to_all | solution.py:177
  9.2 2.2 %copy-start = (bf16[2048,1024]{1,0:T(8,128)(2,1)S(1)}, bf16[2048,1024]{1,0:T(8,128)(2,1)}, u32[]{:S(2)}) copy-start(bf16[2048,1024]{1,0:T(8,128)(2,1)} %bands.3) | copy-start | bytes 12582916
  11.4 1.6 %copy-start.2 = (bf16[2048,512]{1,0:T(8,128)(2,1)S(1)}, bf16[2048,512]{1,0:T(8,128)(2,1)}, u32[]{:S(2)}) copy-start(bf16[2048,512]{1,0:T(8,128)(2,1)} %projectors.5) | copy-start | bytes 6291460
  13.0 6.2 %copy-start.3 = (bf16[2048,512]{1,0:T(8,128)(2,1)S(1)}, bf16[2048,512]{1,0:T(8,128)(2,1)}, u32[]{:S(2)}) copy-start(bf16[2048,512]{1,0:T(8,128)(2,1)} %projectors.5) | copy-start | bytes 6291460
  16.5 7.8 %collective-permute-start = (bf16[8,256,128]{2,1,0:T(8,128)(2,1)}, bf16[8,256,128]{2,1,0:T(8,128)(2,1)}, u32[]{:S(2)}, u32[]{:S(2)}) collective-permute-start(bf16[8,256,128]{2,1,0:T(8,128)(2,1)} %project.3), channel_id=1, source_target_pairs={{0,1},{1,0},{2,3},{3,2},{4,5},{5,4},{6,7},{7,6},{8,9},{9,8},{10,11... | collective-permute-start | bytes 1572872 | tf_op jit(solution)/shard_map/ppermute | solution.py:17
  19.2 2.2 %copy-start.1 = (bf16[2048,1024]{1,0:T(8,128)(2,1)S(1)}, bf16[2048,1024]{1,0:T(8,128)(2,1)}, u32[]{:S(2)}) copy-start(bf16[2048,1024]{1,0:T(8,128)(2,1)} %bands.3) | copy-start | bytes 12582916
  21.4 27.7 %copy-start.4 = (s32[2,256]{1,0:T(2,128)S(1)}, s32[2,256]{1,0:T(2,128)}, u32[]{:S(2)}) copy-start(s32[2,256]{1,0:T(2,128)} %atom_of.1) | copy-start | bytes 6148
  21.4 27.7 %copy-start.5 = (s32[2,4]{1,0:T(2,128)S(1)}, s32[2,4]{1,0:T(2,128)}, u32[]{:S(2)}) copy-start(s32[2,4]{1,0:T(2,128)} %counts.1) | copy-start | bytes 100
  67.5 1.9 %collective-permute-start.1 = (bf16[8,256,128]{2,1,0:T(8,128)(2,1)S(1)}, bf16[8,256,128]{2,1,0:T(8,128)(2,1)S(1)}, u32[]{:S(2)}, u32[]{:S(2)}) collective-permute-start(bf16[8,256,128]{2,1,0:T(8,128)(2,1)S(1)} %all_to_all.16.mine), channel_id=1, source_target_pairs={{0,1},{1,0},{2,3},{3,2},{4,5},{5,4},{6,7},{7,6},{8,9},{9,8},{10,11... | collective-permute-start | bytes 1572872 | tf_op jit(solution)/shard_map/ppermute | solution.py:17

commit v3 on v0

v3 whole, which is shorter than its diff:
```python
import jax
import jax.numpy as jnp
from jax import lax
from jax.experimental import pallas as pl
from jax.experimental.pallas import tpu as pltpu
from jax.sharding import PartitionSpec as P

CHANNELS = 4
CH_CAP = 64
PCAP = 256
LANES = 128
ROW_BLOCK = 512
PARAMS = pltpu.CompilerParams(vmem_limit_bytes=32 * 1024 * 1024)
VMEM = pl.BlockSpec(memory_space=pltpu.VMEM)
SMEM = pl.BlockSpec(memory_space=pltpu.SMEM)
HBM = pl.BlockSpec(memory_space=pltpu.HBM)


def bit_order(chips, core):
    bits = list(range(chips.bit_length() - 1))
    if core == 1 and len(bits) > 2:
        bits[0], bits[1] = bits[1], bits[0]
    return bits


def offsets(chips, core):
    order = bit_order(chips, core)
    count = len(order)
    return [
        sum(((p >> (count - 1 - i)) & 1) << bit for i, bit in enumerate(order)) for p in range(chips)
    ]


def chunk_of(chips, chip, group, position):
    return chip ^ jnp.where(group == 0, offsets(chips, 0)[position], offsets(chips, 1)[position])


def swap_cores(x):
    count = lax.axis_size("pw")
    return lax.ppermute(x, "pw", [(i, i ^ 1) for i in range(count)])


def swap_bits(x, bits):
    count = lax.axis_size("pw")
    return lax.ppermute(x, "pw", [(i, i ^ (2 << bits[i % 2])) for i in range(count)])


def swap_stage(x, stage):
    chips = lax.axis_size("pw") // 2
    return swap_bits(x, [bit_order(chips, core)[stage] for core in range(2)])


def project_kernel(chips, own, first, where, projectors, bands, *refs):
    fresh = len(refs) == 6
    if fresh:
        out, flipped, columns, slots, column_sems, slot_sem = refs
    else:
        out, columns, column_sems = refs
        flipped = projectors
    core, chip = where[0], where[1]
    group = core if own else 1 - core
    copies = []
    if fresh:
        start = pl.multiple_of(group * PCAP, PCAP)
        slot_copy = pltpu.make_async_copy(projectors.at[:, pl.ds(start, PCAP)], slots, slot_sem)
        slot_copy.start()
    for at in range(out.shape[0]):
        start = pl.multiple_of(chunk_of(chips, chip, group, first + at) * LANES, LANES)
        copies.append(
            pltpu.make_async_copy(
                bands.at[:, pl.ds(start, LANES)],
                columns.at[at // 2, :, (at % 2) * LANES : (at % 2 + 1) * LANES],
                column_sems.at[at],
            )
        )
        copies[-1].start()
    if fresh:
        slot_copy.wait()
        flipped[...] = slots[...].T
    for pair in range(out.shape[0] // 2):
        copies[2 * pair].wait()
        copies[2 * pair + 1].wait()
        sums = jnp.dot(flipped[...], columns[pair], preferred_element_type=jnp.float32)
        out[2 * pair] = sums[:, :LANES].astype(out.dtype)
        out[2 * pair + 1] = sums[:, LANES:].astype(out.dtype)


def project(where, projectors, flipped, band_coeffs, own, first):
    depth, bands = band_coeffs.shape
    chips = lax.axis_size("pw") // 2
    width = bands // chips
    half = chips // 2
    dtype = jnp.float32 if own else jnp.bfloat16
    if width != LANES:
        group = where[0] if own else 1 - where[0]
        chunks = jnp.stack([chunk_of(chips, where[1], group, first + at) for at in range(half)])
        slots = lax.dynamic_slice_in_dim(projectors, group * PCAP, PCAP, 1)
        columns = jnp.take(band_coeffs.reshape(depth, chips, width), chunks, axis=1)
        return jnp.einsum("ds,dhw->hsw", slots, columns, preferred_element_type=jnp.float32).astype(dtype), None
    shape = jax.ShapeDtypeStruct((half, PCAP, width), dtype)
    flipped_shape = jax.ShapeDtypeStruct((PCAP, depth), jnp.bfloat16)
    columns = pltpu.VMEM((half // 2, depth, 2 * LANES), jnp.bfloat16)
    sems = pltpu.SemaphoreType.DMA((half,))
    fresh = flipped is None

    def kernel(*refs):
        project_kernel(chips, own, first, *refs)

    cost = pl.CostEstimate(
        flops=2 * depth * PCAP * half * width, bytes_accessed=2 * depth * half * width, transcendentals=0
    )
    bands_in_hbm = pltpu.with_memory_space_constraint(band_coeffs, pltpu.HBM)
    if fresh:
        return pl.pallas_call(
            kernel,
            in_specs=[SMEM, HBM, HBM],
            out_specs=[VMEM, VMEM],
            out_shape=[shape, flipped_shape],
            scratch_shapes=[
                columns, pltpu.VMEM((depth, PCAP), jnp.bfloat16), sems, pltpu.SemaphoreType.DMA
            ],
            compiler_params=PARAMS,
            cost_estimate=cost,
            name="project_first",
        )(where, pltpu.with_memory_space_constraint(projectors, pltpu.HBM), bands_in_hbm)
    return pl.pallas_call(
        kernel,
        in_specs=[SMEM, VMEM, HBM],
        out_specs=VMEM,
        out_shape=shape,
        scratch_shapes=[columns, sems],
        compiler_params=PARAMS,
        cost_estimate=cost,
        name="project_rest",
    )(where, flipped, bands_in_hbm), None


def fold_kernel(*refs):
    *terms, kept, message = refs
    half = kept.shape[0]
    for at in range(2 * half):
        total = terms[0][at]
        for term in terms[1:]:
            total = total + term[at].astype(jnp.float32)
        if at < half:
            kept[at] = total
        else:
            message[at - half] = total.astype(message.dtype)


def fold(*terms):
    count, rows, width = terms[0].shape
    return pl.pallas_call(
        fold_kernel,
        in_specs=[VMEM] * len(terms),
        out_specs=[VMEM, VMEM],
        out_shape=[
            jax.ShapeDtypeStruct((count // 2, rows, width), jnp.float32),
            jax.ShapeDtypeStruct((count // 2, rows, width), jnp.bfloat16),
        ],
        compiler_params=PARAMS,
        name="fold",
    )(*terms)


def add_kernel(left, right, out):
    for at in range(out.shape[0]):
        out[at] = (left[at] + right[at].astype(jnp.float32)).astype(out.dtype)


def add(left, right):
    return pl.pallas_call(
        add_kernel,
        in_specs=[VMEM, VMEM],
        out_specs=VMEM,
        out_shape=jax.ShapeDtypeStruct(left.shape, jnp.bfloat16),
        compiler_params=PARAMS,
        name="add",
    )(left, right)


def choose_kernel(where, owners, own, sibling, kept, sent):
    core, chip, me = where[0], where[1], where[2]
    owner = jnp.where(core == 0, owners[0], owners[1])
    half = PCAP // 2
    side = chip & 1
    for out, which in ((kept, side), (sent, 1 - side)):
        rows = pl.ds(pl.multiple_of(which * half, half), half)
        part = jnp.where(owner == me, own[rows], jnp.where(owner == (me ^ 1), sibling[rows], 0.0))
        out[...] = part.astype(out.dtype)


def choose(where, owners, own, sibling):
    shape = jax.ShapeDtypeStruct((PCAP // 2, PCAP), jnp.bfloat16)
    return pl.pallas_call(
        choose_kernel,
        in_specs=[SMEM, SMEM, VMEM, VMEM],
        out_specs=[VMEM, VMEM],
        out_shape=[shape, shape],
        compiler_params=PARAMS,
        name="choose",
    )(where, owners, own, sibling)


def couple_kernel(where, counts, atom_of, kept, got, near, far, out, table):
    core, chip = where[0], where[1]
    half = PCAP // 2
    side = chip & 1
    table[pl.ds(pl.multiple_of(side * half, half), half)] = near[...].astype(jnp.float32)
    table[pl.ds(pl.multiple_of((1 - side) * half, half), half)] = far[...].astype(jnp.float32)
    total = kept[0] + got[0].astype(jnp.float32)
    slot = lax.broadcasted_iota(jnp.int32, (1, PCAP), 1)
    limit = jnp.zeros((1, PCAP), jnp.int32)
    for channel in range(CHANNELS):
        limit = jnp.where(slot >= channel * CH_CAP, channel * CH_CAP + counts[core, channel], limit)
    atoms = jnp.where(core == 0, atom_of[0:1], atom_of[1:2])
    code = jnp.broadcast_to(jnp.where(slot < limit, atoms, -1), (PCAP, PCAP))
    coupling = jnp.where((code == code.T) & (code >= 0), table[...], 0.0)
    out[0] = jnp.dot(
        coupling, total, precision=lax.Precision.HIGHEST, preferred_element_type=jnp.float32
    ).astype(out.dtype)


def couple(where, counts, atom_of, kept, got, near, far):
    return pl.pallas_call(
        couple_kernel,
        in_specs=[SMEM, SMEM] + [VMEM] * 5,
        out_specs=VMEM,
        out_shape=jax.ShapeDtypeStruct(kept.shape, jnp.bfloat16),
        scratch_shapes=[pltpu.VMEM((PCAP, PCAP), jnp.float32)],
        compiler_params=PARAMS,
        name="couple",
    )(where, counts, atom_of, kept, got, near, far)


def apply_kernel(chips, where, projectors, *refs):
    *pieces, out, scaled, blocks, sems = refs
    core, chip = where[0], where[1]
    count = len(pieces) // 2
    for own, parts in ((True, pieces[:count]), (False, pieces[count:])):
        group = core if own else 1 - core
        rows = pl.ds(pl.multiple_of(group * PCAP, PCAP), PCAP)
        position = 0
        for part in parts:
            for at in range(part.shape[0]):
                start = pl.multiple_of(chunk_of(chips, chip, group, position) * LANES, LANES)
                scaled[rows, pl.ds(start, LANES)] = part[at]
                position += 1
    copies = []
    for block in range(projectors.shape[0] // ROW_BLOCK):
        rows = slice(block * ROW_BLOCK, (block + 1) * ROW_BLOCK)
        slot = block % 2
        if block >= 2:
            copies[block - 2].wait()
        blocks[slot] = jnp.dot(
            projectors[rows], scaled[...], preferred_element_type=jnp.float32
        ).astype(jnp.bfloat16)
        copies.append(pltpu.make_async_copy(blocks.at[slot], out.at[rows], sems.at[slot]))
        copies[-1].start()
    for copy in copies[-2:]:
        copy.wait()


def apply(where, projectors, pieces):
    depth, slots = projectors.shape
    chips = lax.axis_size("pw") // 2
    width = pieces[0].shape[2]
    bands = chips * width
    if width != LANES:
        count = len(pieces) // 2
        rows = []
        for group in range(2):
            chunks = jnp.stack([chunk_of(chips, where[1], group, at) for at in range(chips)])
            mine = jnp.concatenate(pieces[:count])
            other = jnp.concatenate(pieces[count:])
            blocks = jnp.where(where[0] == group, mine, other)
            rows.append(jnp.zeros_like(blocks).at[chunks].set(blocks).transpose(1, 0, 2).reshape(PCAP, bands))
        return jnp.dot(projectors, jnp.concatenate(rows), preferred_element_type=jnp.float32).astype(jnp.bfloat16)

    def kernel(*refs):
        apply_kernel(chips, *refs)

    return pl.pallas_call(
        kernel,
        in_specs=[SMEM, VMEM] + [VMEM] * len(pieces),
        out_specs=HBM,
        out_shape=jax.ShapeDtypeStruct((depth, bands), jnp.bfloat16),
        scratch_shapes=[
            pltpu.VMEM((slots, bands), jnp.bfloat16),
            pltpu.VMEM((2, ROW_BLOCK, bands), jnp.bfloat16),
            pltpu.SemaphoreType.DMA((2,)),
        ],
        compiler_params=PARAMS,
        cost_estimate=pl.CostEstimate(
            flops=2 * depth * slots * bands, bytes_accessed=2 * depth * (slots + bands), transcendentals=0
        ),
        name="apply",
    )(where, projectors, *pieces)


def local(band_coeffs, projectors, counts, atom_of, owners, couplings):
    chips = lax.axis_size("pw") // 2
    stages = chips.bit_length() - 1
    half = chips // 2
    me = lax.axis_index("pw")
    where = jnp.stack([me % 2, me // 2, me])

    own_table = couplings[0]
    near, far = choose(where, owners, own_table, swap_cores(own_table))
    near = near + swap_bits(far, [0, 0])
    for bit in range(stages - 1, 0, -1):
        near = near + swap_bits(near, [bit, bit])
    far = swap_bits(near, [0, 0])

    theirs, their_flipped = project(where, projectors, None, band_coeffs, False, half)
    theirs = swap_cores(theirs)
    ours, our_flipped = project(where, projectors, None, band_coeffs, True, half)
    got = swap_stage(add(ours, theirs), 0)
    theirs, _ = project(where, projectors, their_flipped, band_coeffs, False, 0)
    theirs = swap_cores(theirs)
    ours, _ = project(where, projectors, our_flipped, band_coeffs, True, 0)
    kept, message = fold(ours, theirs, got)
    for stage in range(1, stages):
        got = swap_stage(message, stage)
        if stage < stages - 1:
            kept, message = fold(kept, got)

    scaled = couple(where, counts, atom_of, kept, got, near, far)
    mine = jnp.concatenate([scaled, swap_stage(scaled, stages - 1)])
    pieces = [mine]
    others = [swap_cores(mine)]
    for stage in range(stages - 2, -1, -1):
        got = swap_stage(mine, stage)
        pieces.append(got)
        others.append(swap_cores(got))
        if stage:
            mine = jnp.concatenate([mine, got])
    return apply(where, projectors, pieces + others)


def solution(mesh):
    placed = (
        P("pw", "group"),
        P("pw", "group"),
        P("group", None),
        P("group", None),
        P("group"),
        P("pw", "group", None),
    )
    return jax.shard_map(
        local, mesh=mesh, in_specs=placed, out_specs=P("pw", "group"), check_vma=False
    )
```

time: 137 us -> 67.5 us (0.49)
  waiting for transfers between devices: 104 us -> 33.7 us
  Pallas kernels: 0 us -> 21.3 us
  between operations: 14.7 us -> 0.16 us
  matrix products: 14.5 us -> 0 us
  starting transfers between devices: 0.01 us -> 12.1 us
  other arithmetic: 2.59 us -> 0.17 us
    psum x1 -> x0, waiting for transfers between devices: 104 us -> none  [local(): proj_sums = lax.psum(partial_proj, 'pw')]
    ppermute x0 -> x16, waiting for transfers between devices: none -> 33.7 us  [the longest x10 32.3 us: swap_bits(): lax.ppermute(x, 'pw', [(i, i ^ 2 << bits[i % 2]) for i in range(count)])]
    pallas_call x0 -> x10, Pallas kernels: none -> 21.3 us  [the longest x2 8.14 us: project(): pl.pallas_call(kernel, in_specs=[SMEM, HBM, HBM], out_specs=[VMEM, VMEM],...]
    dot_general x3 -> x0, matrix products: 14.5 us -> none  [the longest x1 6.49 us: local(): lax.dot_general(masked_proj, band_coeffs, (((0,), (0,)), ((), ())), prefe...]
    ppermute x0 -> x16, starting transfers between devices: none -> 12.1 us  [the longest x10 10.5 us: swap_bits(): lax.ppermute(x, 'pw', [(i, i ^ 2 << bits[i % 2]) for i in range(count)])]
    select_n x3 -> x0, other arithmetic: 1.81 us -> none  [the longest x1 1.8 us: from_root(): return lax.psum(jnp.where(mine, x, jnp.zeros_like(x)), axis)]
  transfers between devices with their start and end apart: 1 -> 16, of which waited for: 1 -> 9; matrix products, arithmetic and copies ran while one was open for 0% -> 0% of each run, Pallas kernels for 0% -> 17%
where the time goes in v3:
time: 67.5 us; the launch traced here: 67.3 us
  waiting for transfers between devices  33.7 us (50%)
  Pallas kernels  21.3 us (32%)
  starting transfers between devices  12.1 us (18%)
    ppermute x10, waiting for transfers between devices, swap_bits(): lax.ppermute(x, 'pw', [(i, i ^ 2 << bits[i % 2]) for i in range(count)])  32.3 us
    ppermute x10, starting transfers between devices, swap_bits(): lax.ppermute(x, 'pw', [(i, i ^ 2 << bits[i % 2]) for i in range(count)])  10.5 us
    pallas_call x2, Pallas kernels, project(): pl.pallas_call(kernel, in_specs=[SMEM, HBM, HBM], out_specs=[VMEM, VMEM],...  8.14 us
    pallas_call x2, Pallas kernels, project(): pl.pallas_call(kernel, in_specs=[SMEM, VMEM, HBM], out_specs=VMEM, out_sh...  6.43 us
    pallas_call x1, Pallas kernels, apply(): pl.pallas_call(kernel, in_specs=[SMEM, VMEM] + [VMEM] * len(pieces), out_...  4.96 us
    ppermute x6, starting transfers between devices, swap_cores(): return lax.ppermute(x, 'pw', [(i, i ^ 1) for i in range(count)])  1.61 us
    ppermute x6, waiting for transfers between devices, swap_cores(): return lax.ppermute(x, 'pw', [(i, i ^ 1) for i in range(count)])  1.41 us
  transfers between devices with their start and end apart: 16, of which 9 were waited for; matrix products, arithmetic and copies ran while one was open for 0% of the time, Pallas kernels for 17%

profile of v3, /device:TPU:0, one launch (start us, length us, event | category | flops | bytes accessed | tf_op | source)
XLA Modules:
  0.0 67.3 jit_solution(9428789003913202634)
XLA Ops:
  0.0 0.0 copy-start.1
  0.0 0.1 pad_add_fusion.refs_0_.where
  0.1 4.1 %project_first.3 = (bf16[4,256,128]{2,1,0:T(8,128)(2,1)S(1)}, bf16[256,2048]{1,0:T(8,128)(2,1)S(1)}) custom-call(s32[3]{0:T(128)S(1)} %pad_add_fusion.refs_0_.where, bf16[2048,512]{1,0:T(8,128)(2,1)} %refs_1_.5, bf16[2048,1024]{1,0:T(8,128)(2,1)} %refs_2_.7), custom_call_target="tpu_custom_call" | custom-call | flops 536870912 | bytes 2097152 | tf_op jit(solution)/shard_map/project_first/pallas_call | solution.py:114
  4.2 0.5 collective-permute-start.1
  4.7 0.0 copy-done.1
  4.7 0.1 collective-permute-start.5
  4.8 3.2 %project_rest.3 = bf16[4,256,128]{2,1,0:T(8,128)(2,1)S(1)} custom-call(s32[3]{0:T(128)S(1)} %pad_add_fusion.refs_0_.where, bf16[256,2048]{1,0:T(8,128)(2,1)S(1)} %get-tuple-element.16.refs_1_, bf16[2048,1024]{1,0:T(8,128)(2,1)} %refs_2_.7), custom_call_target="tpu_custom_call" | custom-call | flops 536870912 | bytes 2097152 | tf_op jit(solution)/shard_map/project_rest/pallas_call | solution.py:126
  8.0 0.0 copy-start.4
  8.0 0.5 collective-permute-start
  8.5 4.1 %project_first.2 = (f32[4,256,128]{2,1,0:T(8,128)S(1)}, bf16[256,2048]{1,0:T(8,128)(2,1)S(1)}) custom-call(s32[3]{0:T(128)S(1)} %pad_add_fusion.refs_0_.where, bf16[2048,512]{1,0:T(8,128)(2,1)} %refs_1_.5, bf16[2048,1024]{1,0:T(8,128)(2,1)} %refs_2_.7), custom_call_target="tpu_custom_call" | custom-call | flops 536870912 | bytes 2097152 | tf_op jit(solution)/shard_map/project_first/pallas_call | solution.py:114
  12.5 0.0 collective-permute-done.1.right
  12.6 0.0 copy-start.2
  12.6 0.0 copy-start.3
  12.6 2.7 %collective-permute-start.2 = (bf16[4,256,128]{2,1,0:T(8,128)(2,1)S(1)}, bf16[4,256,128]{2,1,0:T(8,128)(2,1)S(1)}, u32[]{:S(2)}, u32[]{:S(2)}) collective-permute-start(bf16[4,256,128]{2,1,0:T(8,128)(2,1)S(1)} %add.23), channel_id=1, source_target_pairs={{0,2},{1,5},{2,0},{3,7},{4,6},{5,1},{6,4},{7,3},{8,10},{9,13},{10,... | collective-permute-start | bytes 786440 | tf_op jit(solution)/shard_map/ppermute | solution.py:45
  15.3 0.0 collective-permute-done.5.sibling
  15.3 0.0 copy-done.4
  15.3 0.6 choose.1
  15.9 0.1 collective-permute-start.6
  16.0 5.1 %collective-permute-done.6 = bf16[128,256]{1,0:T(8,128)(2,1)S(1)} collective-permute-done((bf16[128,256]{1,0:T(8,128)(2,1)S(1)}, bf16[128,256]{1,0:T(8,128)(2,1)S(1)}, u32[]{:S(2)}, u32[]{:S(2)}) %collective-permute-start.6) | collective-permute-done | bytes 65568 | tf_op jit(solution)/shard_map/ppermute | solution.py:45
  21.1 3.2 %collective-permute-start.7 = (bf16[128,256]{1,0:T(8,128)(2,1)S(1)}, bf16[128,256]{1,0:T(8,128)(2,1)S(1)}, u32[]{:S(2)}, u32[]{:S(2)}) collective-permute-start(bf16[128,256]{1,0:T(8,128)(2,1)S(1)} %add.16), channel_id=1, source_target_pairs={{0,8},{1,9},{2,10},{3,11},{4,12},{5,13},{6,14},{7,15},{8,0},{9,1},... | collective-permute-start | bytes 196616 | tf_op jit(solution)/shard_map/ppermute | solution.py:45
  24.2 0.0 copy-start
  24.2 3.3 %project_rest.2.refs_0_ = f32[4,256,128]{2,1,0:T(8,128)S(1)} custom-call(s32[3]{0:T(128)S(1)} %pad_add_fusion.refs_0_.where, bf16[256,2048]{1,0:T(8,128)(2,1)S(1)} %get-tuple-element.15.refs_1_, bf16[2048,1024]{1,0:T(8,128)(2,1)} %refs_2_.7), custom_call_target="tpu_custom_call" | custom-call | flops 536870912 | bytes 2097152 | tf_op jit(solution)/shard_map/project_rest/pallas_call | solution.py:126
  27.5 0.0 collective-permute-done.refs_1_
  27.5 0.0 collective-permute-done.2.refs_2_
  27.5 0.1 fold.2
  27.6 1.6 %collective-permute-start.3 = (bf16[2,256,128]{2,1,0:T(8,128)(2,1)S(1)}, bf16[2,256,128]{2,1,0:T(8,128)(2,1)S(1)}, u32[]{:S(2)}, u32[]{:S(2)}) collective-permute-start(bf16[2,256,128]{2,1,0:T(8,128)(2,1)S(1)} %get-tuple-element.20), channel_id=1, source_target_pairs={{0,4},{1,3},{2,6},{3,1},{4,0},{5,7},{6,2},{7,5},{8,12},{9,11},{10,... | collective-permute-start | bytes 393224 | tf_op jit(solution)/shard_map/ppermute | solution.py:45
  29.3 0.0 collective-permute-done.7
  29.3 0.5 collective-permute-start.8
  29.8 3.8 %collective-permute-done.8 = bf16[128,256]{1,0:T(8,128)(2,1)S(1)} collective-permute-done((bf16[128,256]{1,0:T(8,128)(2,1)S(1)}, bf16[128,256]{1,0:T(8,128)(2,1)S(1)}, u32[]{:S(2)}, u32[]{:S(2)}) %collective-permute-start.8) | collective-permute-done | bytes 65568 | tf_op jit(solution)/shard_map/ppermute | solution.py:45
  33.6 1.6 %collective-permute-start.9 = (bf16[128,256]{1,0:T(8,128)(2,1)S(1)}, bf16[128,256]{1,0:T(8,128)(2,1)S(1)}, u32[]{:S(2)}, u32[]{:S(2)}) collective-permute-start(bf16[128,256]{1,0:T(8,128)(2,1)S(1)} %add.18.near), channel_id=1, source_target_pairs={{0,2},{1,3},{2,0},{3,1},{4,6},{5,7},{6,4},{7,5},{8,10},{9,11},{10,... | collective-permute-start | bytes 196616 | tf_op jit(solution)/shard_map/ppermute | solution.py:45
  35.2 0.0 collective-permute-done.3.refs_1_
  35.3 0.4 collective-permute-start.4
  35.7 2.3 %collective-permute-done.9.far = bf16[128,256]{1,0:T(8,128)(2,1)S(1)} collective-permute-done((bf16[128,256]{1,0:T(8,128)(2,1)S(1)}, bf16[128,256]{1,0:T(8,128)(2,1)S(1)}, u32[]{:S(2)}, u32[]{:S(2)}) %collective-permute-start.9) | collective-permute-done | bytes 65568 | tf_op jit(solution)/shard_map/ppermute | solution.py:45
  38.0 4.3 %collective-permute-done.4.got = bf16[1,256,128]{2,1,0:T(8,128)(2,1)S(1)} collective-permute-done((bf16[1,256,128]{2,1,0:T(8,128)(2,1)S(1)}, bf16[1,256,128]{2,1,0:T(8,128)(2,1)S(1)}, u32[]{:S(2)}, u32[]{:S(2)}) %collective-permute-start.4) | collective-permute-done | bytes 65568 | tf_op jit(solution)/shard_map/ppermute | solution.py:45
  42.3 0.0 copy-done.2
  42.3 0.0 copy-done.3
  42.3 1.0 %couple.1 = bf16[1,256,128]{2,1,0:T(8,128)(2,1)S(1)} custom-call(s32[3]{0:T(128)S(1)} %pad_add_fusion.refs_0_.where, s32[2,4]{1,0:T(2,128)S(1)} %copy-done.3, s32[2,256]{1,0:T(2,128)S(1)} %copy-done.2, f32[1,256,128]{2,1,0:T(8,128)S(1)} %get-tuple-element.21.kept, bf16[1,256,128]{2,1,0:T(8,128)(2,1)S(1)} %collective-permute-done.4.got, ...), custom_call_target="tpu_custom_call" | custom-call | tf_op jit(solution)/shard_map/couple/pallas_call | solution.py:225
  43.2 0.1 collective-permute-start.10
  43.3 5.6 %collective-permute-done.10 = bf16[1,256,128]{2,1,0:T(8,128)(2,1)S(1)} collective-permute-done((bf16[1,256,128]{2,1,0:T(8,128)(2,1)S(1)}, bf16[1,256,128]{2,1,0:T(8,128)(2,1)S(1)}, u32[]{:S(2)}, u32[]{:S(2)}) %collective-permute-start.10) | collective-permute-done | bytes 65568 | tf_op jit(solution)/shard_map/ppermute | solution.py:45
  49.0 0.3 collective-permute-start.11
  49.2 4.8 %collective-permute-done.11.refs_3_ = bf16[2,256,128]{2,1,0:T(8,128)(2,1)S(1)} collective-permute-done((bf16[2,256,128]{2,1,0:T(8,128)(2,1)S(1)}, bf16[2,256,128]{2,1,0:T(8,128)(2,1)S(1)}, u32[]{:S(2)}, u32[]{:S(2)}) %collective-permute-start.11) | collective-permute-done | bytes 131104 | tf_op jit(solution)/shard_map/ppermute | solution.py:45
  54.0 0.1 collective-permute-start.12
  54.1 6.4 %collective-permute-done.12.refs_4_ = bf16[4,256,128]{2,1,0:T(8,128)(2,1)S(1)} collective-permute-done((bf16[4,256,128]{2,1,0:T(8,128)(2,1)S(1)}, bf16[4,256,128]{2,1,0:T(8,128)(2,1)S(1)}, u32[]{:S(2)}, u32[]{:S(2)}) %collective-permute-start.12) | collective-permute-done | bytes 262176 | tf_op jit(solution)/shard_map/ppermute | solution.py:45
  60.5 0.0 collective-permute-start.15
  60.5 0.5 collective-permute-start.13
  61.0 0.0 collective-permute-start.14
  61.0 1.2 %collective-permute-done.13.refs_5_ = bf16[2,256,128]{2,1,0:T(8,128)(2,1)S(1)} collective-permute-done((bf16[2,256,128]{2,1,0:T(8,128)(2,1)S(1)}, bf16[2,256,128]{2,1,0:T(8,128)(2,1)S(1)}, u32[]{:S(2)}, u32[]{:S(2)}) %collective-permute-start.13) | collective-permute-done | bytes 131104 | tf_op jit(solution)/shard_map/ppermute | solution.py:40
  62.2 0.2 collective-permute-done.14.refs_6_
  62.4 0.0 collective-permute-done.15.refs_7_
  62.4 0.0 copy-done
  62.4 5.0 %apply.1 = bf16[2048,1024]{1,0:T(8,128)(2,1)} custom-call(s32[3]{0:T(128)S(1)} %pad_add_fusion.refs_0_.where, bf16[2048,512]{1,0:T(8,128)(2,1)S(1)} %copy-done, bf16[2,256,128]{2,1,0:T(8,128)(2,1)S(1)} %pad_maximum_fusion.1.refs_2_, bf16[2,256,128]{2,1,0:T(8,128)(2,1)S(1)} %collective-permute-done.11.refs_3_, ...), custom_call_target="tpu_custom_call" | custom-call | flops 2147483648 | bytes 6291456 | tf_op jit(solution)/shard_map/apply/pallas_call | solution.py:283
  (7 shorter events, 0.2 us)
Async XLA Ops:
  0.0 4.7 %copy-start.1 = (f32[1,256,256]{2,1,0:T(8,128)S(1)}, f32[1,256,256]{2,1,0:T(8,128)}, u32[]{:S(2)}) copy-start(f32[1,256,256]{2,1,0:T(8,128)} %param.11) | copy-start | bytes 786436
  4.2 8.4 %collective-permute-start.1 = (bf16[4,256,128]{2,1,0:T(8,128)(2,1)S(1)}, bf16[4,256,128]{2,1,0:T(8,128)(2,1)S(1)}, u32[]{:S(2)}, u32[]{:S(2)}) collective-permute-start(bf16[4,256,128]{2,1,0:T(8,128)(2,1)S(1)} %get-tuple-element.18), channel_id=1, source_target_pairs={{0,1},{1,0},{2,3},{3,2},{4,5},{5,4},{6,7},{7,6},{8,9},{9,8},{10,11... | collective-permute-start | bytes 786440 | tf_op jit(solution)/shard_map/ppermute | solution.py:40
  4.7 10.6 %collective-permute-start.5 = (f32[256,256]{1,0:T(8,128)S(1)}, f32[256,256]{1,0:T(8,128)S(1)}, u32[]{:S(2)}, u32[]{:S(2)}) collective-permute-start(f32[256,256]{1,0:T(8,128)S(1)} %bitcast.4), channel_id=1, source_target_pairs={{0,1},{1,0},{2,3},{3,2},{4,5},{5,4},{6,7},{7,6},{8,9},{9,8},{10,11... | collective-permute-start | bytes 786440 | tf_op jit(solution)/shard_map/ppermute | solution.py:40
  8.0 7.3 %copy-start.4 = (s32[2]{0:T(128)S(1)}, s32[2]{0:T(128)}, u32[]{:S(2)}) copy-start(s32[2]{0:T(128)} %owners.1) | copy-start | bytes 28
  8.0 19.5 %collective-permute-start = (bf16[4,256,128]{2,1,0:T(8,128)(2,1)S(1)}, bf16[4,256,128]{2,1,0:T(8,128)(2,1)S(1)}, u32[]{:S(2)}, u32[]{:S(2)}) collective-permute-start(bf16[4,256,128]{2,1,0:T(8,128)(2,1)S(1)} %project_rest.3), channel_id=1, source_target_pairs={{0,1},{1,0},{2,3},{3,2},{4,5},{5,4},{6,7},{7,6},{8,9},{9,8},{10,11... | collective-permute-start | bytes 786440 | tf_op jit(solution)/shard_map/ppermute | solution.py:40
  12.6 29.7 %copy-start.2 = (s32[2,256]{1,0:T(2,128)S(1)}, s32[2,256]{1,0:T(2,128)}, u32[]{:S(2)}) copy-start(s32[2,256]{1,0:T(2,128)} %atom_of.1) | copy-start | bytes 6148
  12.6 29.6 %copy-start.3 = (s32[2,4]{1,0:T(2,128)S(1)}, s32[2,4]{1,0:T(2,128)}, u32[]{:S(2)}) copy-start(s32[2,4]{1,0:T(2,128)} %counts.1) | copy-start | bytes 100
  12.6 14.9 %collective-permute-start.2 = (bf16[4,256,128]{2,1,0:T(8,128)(2,1)S(1)}, bf16[4,256,128]{2,1,0:T(8,128)(2,1)S(1)}, u32[]{:S(2)}, u32[]{:S(2)}) collective-permute-start(bf16[4,256,128]{2,1,0:T(8,128)(2,1)S(1)} %add.23), channel_id=1, source_target_pairs={{0,2},{1,5},{2,0},{3,7},{4,6},{5,1},{6,4},{7,3},{8,10},{9,13},{10,... | collective-permute-start | bytes 786440 | tf_op jit(solution)/shard_map/ppermute | solution.py:45
  15.9 5.2 %collective-permute-start.6 = (bf16[128,256]{1,0:T(8,128)(2,1)S(1)}, bf16[128,256]{1,0:T(8,128)(2,1)S(1)}, u32[]{:S(2)}, u32[]{:S(2)}) collective-permute-start(bf16[128,256]{1,0:T(8,128)(2,1)S(1)} %get-tuple-element.24), channel_id=1, source_target_pairs={{0,2},{1,3},{2,0},{3,1},{4,6},{5,7},{6,4},{7,5},{8,10},{9,11},{10,... | collective-permute-start | bytes 196616 | tf_op jit(solution)/shard_map/ppermute | solution.py:45
  21.1 8.2 %collective-permute-start.7 = (bf16[128,256]{1,0:T(8,128)(2,1)S(1)}, bf16[128,256]{1,0:T(8,128)(2,1)S(1)}, u32[]{:S(2)}, u32[]{:S(2)}) collective-permute-start(bf16[128,256]{1,0:T(8,128)(2,1)S(1)} %add.16), channel_id=1, source_target_pairs={{0,8},{1,9},{2,10},{3,11},{4,12},{5,13},{6,14},{7,15},{8,0},{9,1},... | collective-permute-start | bytes 196616 | tf_op jit(solution)/shard_map/ppermute | solution.py:45
  24.2 38.2 %copy-start = (bf16[2048,512]{1,0:T(8,128)(2,1)S(1)}, bf16[2048,512]{1,0:T(8,128)(2,1)}, u32[]{:S(2)}) copy-start(bf16[2048,512]{1,0:T(8,128)(2,1)} %refs_1_.5) | copy-start | bytes 6291460
  27.6 7.6 %collective-permute-start.3 = (bf16[2,256,128]{2,1,0:T(8,128)(2,1)S(1)}, bf16[2,256,128]{2,1,0:T(8,128)(2,1)S(1)}, u32[]{:S(2)}, u32[]{:S(2)}) collective-permute-start(bf16[2,256,128]{2,1,0:T(8,128)(2,1)S(1)} %get-tuple-element.20), channel_id=1, source_target_pairs={{0,4},{1,3},{2,6},{3,1},{4,0},{5,7},{6,2},{7,5},{8,12},{9,11},{10,... | collective-permute-start | bytes 393224 | tf_op jit(solution)/shard_map/ppermute | solution.py:45
  29.3 4.3 %collective-permute-start.8 = (bf16[128,256]{1,0:T(8,128)(2,1)S(1)}, bf16[128,256]{1,0:T(8,128)(2,1)S(1)}, u32[]{:S(2)}, u32[]{:S(2)}) collective-permute-start(bf16[128,256]{1,0:T(8,128)(2,1)S(1)} %add.17), channel_id=1, source_target_pairs={{0,4},{1,5},{2,6},{3,7},{4,0},{5,1},{6,2},{7,3},{8,12},{9,13},{10,... | collective-permute-start | bytes 196616 | tf_op jit(solution)/shard_map/ppermute | solution.py:45
  33.6 4.3 %collective-permute-start.9 = (bf16[128,256]{1,0:T(8,128)(2,1)S(1)}, bf16[128,256]{1,0:T(8,128)(2,1)S(1)}, u32[]{:S(2)}, u32[]{:S(2)}) collective-permute-start(bf16[128,256]{1,0:T(8,128)(2,1)S(1)} %add.18.near), channel_id=1, source_target_pairs={{0,2},{1,3},{2,0},{3,1},{4,6},{5,7},{6,4},{7,5},{8,10},{9,11},{10,... | collective-permute-start | bytes 196616 | tf_op jit(solution)/shard_map/ppermute | solution.py:45
  35.3 7.0 %collective-permute-start.4 = (bf16[1,256,128]{2,1,0:T(8,128)(2,1)S(1)}, bf16[1,256,128]{2,1,0:T(8,128)(2,1)S(1)}, u32[]{:S(2)}, u32[]{:S(2)}) collective-permute-start(bf16[1,256,128]{2,1,0:T(8,128)(2,1)S(1)} %get-tuple-element.22), channel_id=1, source_target_pairs={{0,8},{1,9},{2,10},{3,11},{4,12},{5,13},{6,14},{7,15},{8,0},{9,1},... | collective-permute-start | bytes 196616 | tf_op jit(solution)/shard_map/ppermute | solution.py:45
  43.2 5.7 %collective-permute-start.10 = (bf16[1,256,128]{2,1,0:T(8,128)(2,1)S(1)}, bf16[1,256,128]{2,1,0:T(8,128)(2,1)S(1)}, u32[]{:S(2)}, u32[]{:S(2)}) collective-permute-start(bf16[1,256,128]{2,1,0:T(8,128)(2,1)S(1)} %couple.1), channel_id=1, source_target_pairs={{0,8},{1,9},{2,10},{3,11},{4,12},{5,13},{6,14},{7,15},{8,0},{9,1},... | collective-permute-start | bytes 196616 | tf_op jit(solution)/shard_map/ppermute | solution.py:45
  49.0 5.0 %collective-permute-start.11 = (bf16[2,256,128]{2,1,0:T(8,128)(2,1)S(1)}, bf16[2,256,128]{2,1,0:T(8,128)(2,1)S(1)}, u32[]{:S(2)}, u32[]{:S(2)}) collective-permute-start(bf16[2,256,128]{2,1,0:T(8,128)(2,1)S(1)} %pad_maximum_fusion.1.refs_2_), channel_id=1, source_target_pairs={{0,4},{1,3},{2,6},{3,1},{4,0},{5,7},{6,2},{7,5},{8,12},{9,11},{10,... | collective-permute-start | bytes 393224 | tf_op jit(solution)/shard_map/ppermute | solution.py:45
  54.0 6.4 %collective-permute-start.12 = (bf16[4,256,128]{2,1,0:T(8,128)(2,1)S(1)}, bf16[4,256,128]{2,1,0:T(8,128)(2,1)S(1)}, u32[]{:S(2)}, u32[]{:S(2)}) collective-permute-start(bf16[4,256,128]{2,1,0:T(8,128)(2,1)S(1)} %pad_maximum_fusion), channel_id=1, source_target_pairs={{0,2},{1,5},{2,0},{3,7},{4,6},{5,1},{6,4},{7,3},{8,10},{9,13},{10,... | collective-permute-start | bytes 786440 | tf_op jit(solution)/shard_map/ppermute | solution.py:45
  60.5 1.9 %collective-permute-start.15 = (bf16[4,256,128]{2,1,0:T(8,128)(2,1)S(1)}, bf16[4,256,128]{2,1,0:T(8,128)(2,1)S(1)}, u32[]{:S(2)}, u32[]{:S(2)}) collective-permute-start(bf16[4,256,128]{2,1,0:T(8,128)(2,1)S(1)} %collective-permute-done.12.refs_4_), channel_id=1, source_target_pairs={{0,1},{1,0},{2,3},{3,2},{4,5},{5,4},{6,7},{7,6},{8,9},{9,8},{10,11... | collective-permute-start | bytes 786440 | tf_op jit(solution)/shard_map/ppermute | solution.py:40
  60.5 1.7 %collective-permute-start.13 = (bf16[2,256,128]{2,1,0:T(8,128)(2,1)S(1)}, bf16[2,256,128]{2,1,0:T(8,128)(2,1)S(1)}, u32[]{:S(2)}, u32[]{:S(2)}) collective-permute-start(bf16[2,256,128]{2,1,0:T(8,128)(2,1)S(1)} %pad_maximum_fusion.1.refs_2_), channel_id=1, source_target_pairs={{0,1},{1,0},{2,3},{3,2},{4,5},{5,4},{6,7},{7,6},{8,9},{9,8},{10,11... | collective-permute-start | bytes 393224 | tf_op jit(solution)/shard_map/ppermute | solution.py:40
  61.0 1.4 %collective-permute-start.14 = (bf16[2,256,128]{2,1,0:T(8,128)(2,1)S(1)}, bf16[2,256,128]{2,1,0:T(8,128)(2,1)S(1)}, u32[]{:S(2)}, u32[]{:S(2)}) collective-permute-start(bf16[2,256,128]{2,1,0:T(8,128)(2,1)S(1)} %collective-permute-done.11.refs_3_), channel_id=1, source_target_pairs={{0,1},{1,0},{2,3},{3,2},{4,5},{5,4},{6,7},{7,6},{8,9},{9,8},{10,11... | collective-permute-start | bytes 393224 | tf_op jit(solution)/shard_map/ppermute | solution.py:40

commit v4 on v3

v4 whole, which is shorter than its diff:
```python
import jax
import jax.numpy as jnp
from jax import lax
from jax.experimental import pallas as pl
from jax.experimental.pallas import tpu as pltpu
from jax.sharding import PartitionSpec as P

CHANNELS = 4
CH_CAP = 64
PCAP = 256
LANES = 128
COLUMNS = 256
PARAMS = pltpu.CompilerParams(vmem_limit_bytes=32 * 1024 * 1024)
VMEM = pl.BlockSpec(memory_space=pltpu.VMEM)
SMEM = pl.BlockSpec(memory_space=pltpu.SMEM)
HBM = pl.BlockSpec(memory_space=pltpu.HBM)
ANY = pl.BlockSpec(memory_space=pl.ANY)


def bit_order(chips, core):
    bits = list(range(chips.bit_length() - 1))
    if core == 1 and len(bits) > 2:
        bits[0], bits[1] = bits[1], bits[0]
    return bits


def offsets(chips, core):
    order = bit_order(chips, core)
    count = len(order)
    return [
        sum(((p >> (count - 1 - i)) & 1) << bit for i, bit in enumerate(order)) for p in range(chips)
    ]


def chunk_of(chips, chip, group, position):
    return chip ^ jnp.where(group == 0, offsets(chips, 0)[position], offsets(chips, 1)[position])


def swap_cores(x):
    count = lax.axis_size("pw")
    return lax.ppermute(x, "pw", [(i, i ^ 1) for i in range(count)])


def swap_bits(x, bits):
    count = lax.axis_size("pw")
    return lax.ppermute(x, "pw", [(i, i ^ (2 << bits[i % 2])) for i in range(count)])


def swap_stage(x, stage):
    chips = lax.axis_size("pw") // 2
    return swap_bits(x, [bit_order(chips, core)[stage] for core in range(2)])


def project_kernel(chips, fresh, where, projectors, bands, *refs):
    if fresh:
        theirs, ours, flipped, columns, slots, slot_sems, column_sems = refs
    else:
        theirs, ours = refs
        flipped, columns = projectors, bands
    core, chip = where[0], where[1]
    half = chips // 2
    first = half if fresh else 0
    if fresh:
        slot_copies, column_copies = [], []
        for copies, source, target, sems in (
            (slot_copies, projectors, slots, slot_sems),
            (column_copies, bands, columns, column_sems),
        ):
            block = source.shape[0] // sems.shape[0]
            for at in range(sems.shape[0]):
                rows = slice(at * block, (at + 1) * block)
                copies.append(pltpu.make_async_copy(source.at[rows], target.at[rows], sems.at[at]))
                copies[-1].start()
        block = slots.shape[0] // len(slot_copies)
        for at, copy in enumerate(slot_copies):
            copy.wait()
            rows = slice(at * block, (at + 1) * block)
            for place, group in enumerate((core, 1 - core)):
                start = pl.multiple_of(group * PCAP, PCAP)
                flipped[place * PCAP : (place + 1) * PCAP, rows] = slots[rows, pl.ds(start, PCAP)].T
        for copy in column_copies:
            copy.wait()

    def pair_of_blocks(group, position):
        starts = [
            pl.multiple_of(chunk_of(chips, chip, group, position + at) * LANES, LANES) for at in range(2)
        ]
        return jnp.concatenate([columns[:, pl.ds(start, LANES)] for start in starts], axis=1)

    def keep(out, at, sums):
        out[at] = sums[:, :LANES].astype(out.dtype)
        out[at + 1] = sums[:, LANES:].astype(out.dtype)

    for at in range(half - 2, -1, -2):
        position = first + at
        if offsets(chips, 0)[position] == offsets(chips, 1)[position]:
            sums = jnp.dot(flipped[...], pair_of_blocks(core, position), preferred_element_type=jnp.float32)
            keep(ours, at, sums[:PCAP])
            keep(theirs, at, sums[PCAP:])
        else:
            for out, rows, group in ((ours, slice(0, PCAP), core), (theirs, slice(PCAP, 2 * PCAP), 1 - core)):
                keep(
                    out,
                    at,
                    jnp.dot(flipped[rows], pair_of_blocks(group, position), preferred_element_type=jnp.float32),
                )


def project_plain(where, projectors, band_coeffs, first):
    depth, bands = band_coeffs.shape
    chips = lax.axis_size("pw") // 2
    half = chips // 2
    outs = []
    for group, dtype in ((1 - where[0], jnp.bfloat16), (where[0], jnp.float32)):
        chunks = jnp.stack([chunk_of(chips, where[1], group, first + at) for at in range(half)])
        slots = lax.dynamic_slice_in_dim(projectors, group * PCAP, PCAP, 1)
        columns = jnp.take(band_coeffs.reshape(depth, chips, bands // chips), chunks, axis=1)
        sums = jnp.einsum("ds,dhw->hsw", slots, columns, preferred_element_type=jnp.float32)
        outs.append(sums.astype(dtype))
    return outs


def project(where, projectors, band_coeffs, fresh):
    depth, bands = band_coeffs.shape
    chips = lax.axis_size("pw") // 2
    half, width = chips // 2, bands // chips

    def kernel(*refs):
        project_kernel(chips, fresh, *refs)

    out_shape = [
        jax.ShapeDtypeStruct((half, PCAP, width), jnp.bfloat16),
        jax.ShapeDtypeStruct((half, PCAP, width), jnp.float32),
    ]
    scratch = []
    if fresh:
        slots = projectors.shape[1]
        out_shape += [
            jax.ShapeDtypeStruct((slots, depth), jnp.bfloat16),
            jax.ShapeDtypeStruct((depth, bands), jnp.bfloat16),
        ]
        scratch = [
            pltpu.VMEM((depth, slots), jnp.bfloat16),
            pltpu.SemaphoreType.DMA((4,)),
            pltpu.SemaphoreType.DMA((8,)),
        ]
        projectors = pltpu.with_memory_space_constraint(projectors, pltpu.HBM)
        band_coeffs = pltpu.with_memory_space_constraint(band_coeffs, pltpu.HBM)
    return pl.pallas_call(
        kernel,
        in_specs=[SMEM, HBM, HBM] if fresh else [SMEM, VMEM, VMEM],
        out_specs=[VMEM] * len(out_shape),
        out_shape=out_shape,
        scratch_shapes=scratch,
        compiler_params=PARAMS,
        cost_estimate=pl.CostEstimate(
            flops=2 * depth * PCAP * bands, bytes_accessed=2 * depth * bands, transcendentals=0
        ),
        name="project_sent" if fresh else "project_kept",
    )(where, projectors, band_coeffs)


def fold_kernel(*refs):
    *terms, kept, message = refs
    half = kept.shape[0]
    for at in range(2 * half):
        total = terms[0][at]
        for term in terms[1:]:
            total = total + term[at].astype(jnp.float32)
        if at < half:
            kept[at] = total
        else:
            message[at - half] = total.astype(message.dtype)


def fold(*terms):
    count, rows, width = terms[0].shape
    return pl.pallas_call(
        fold_kernel,
        in_specs=[VMEM] * len(terms),
        out_specs=[VMEM, VMEM],
        out_shape=[
            jax.ShapeDtypeStruct((count // 2, rows, width), jnp.float32),
            jax.ShapeDtypeStruct((count // 2, rows, width), jnp.bfloat16),
        ],
        compiler_params=PARAMS,
        name="fold",
    )(*terms)


def add_kernel(left, right, out):
    for at in range(out.shape[0]):
        out[at] = (left[at] + right[at].astype(jnp.float32)).astype(out.dtype)


def add(left, right):
    return pl.pallas_call(
        add_kernel,
        in_specs=[VMEM, VMEM],
        out_specs=VMEM,
        out_shape=jax.ShapeDtypeStruct(left.shape, jnp.bfloat16),
        compiler_params=PARAMS,
        name="add",
    )(left, right)


def choose_kernel(where, owners, own, sibling, after, kept, sent):
    del after
    core, chip, me = where[0], where[1], where[2]
    owner = jnp.where(core == 0, owners[0], owners[1])
    half = PCAP // 2
    side = chip & 1
    for out, which in ((kept, side), (sent, 1 - side)):
        rows = pl.ds(pl.multiple_of(which * half, half), half)
        part = jnp.where(owner == me, own[rows], jnp.where(owner == (me ^ 1), sibling[rows], 0.0))
        out[...] = part.astype(out.dtype)


def choose(where, owners, own, sibling, after):
    shape = jax.ShapeDtypeStruct((PCAP // 2, PCAP), jnp.bfloat16)
    return pl.pallas_call(
        choose_kernel,
        in_specs=[SMEM, SMEM, VMEM, VMEM, ANY],
        out_specs=[VMEM, VMEM],
        out_shape=[shape, shape],
        compiler_params=PARAMS,
        name="choose",
    )(where, owners, own, sibling, after)


def merge_kernel(left, right, after, out):
    del after
    out[...] = left[...] + right[...]


def merge(left, right, after):
    return pl.pallas_call(
        merge_kernel,
        in_specs=[VMEM, VMEM, ANY],
        out_specs=VMEM,
        out_shape=jax.ShapeDtypeStruct(left.shape, left.dtype),
        compiler_params=PARAMS,
        name="merge",
    )(left, right, after)


def mask_kernel(where, counts, atom_of, after, out):
    del after
    core = where[0]
    slot = lax.broadcasted_iota(jnp.int32, (1, PCAP), 1)
    limit = jnp.zeros((1, PCAP), jnp.int32)
    for channel in range(CHANNELS):
        limit = jnp.where(slot >= channel * CH_CAP, channel * CH_CAP + counts[core, channel], limit)
    atoms = jnp.where(core == 0, atom_of[0:1], atom_of[1:2])
    code = jnp.broadcast_to(jnp.where(slot < limit, atoms, -1), (PCAP, PCAP))
    out[...] = jnp.where((code == code.T) & (code >= 0), 1.0, 0.0).astype(out.dtype)


def mask(where, counts, atom_of, after):
    return pl.pallas_call(
        mask_kernel,
        in_specs=[SMEM, SMEM, VMEM, ANY],
        out_specs=VMEM,
        out_shape=jax.ShapeDtypeStruct((PCAP, PCAP), jnp.bfloat16),
        compiler_params=PARAMS,
        name="mask",
    )(where, counts, atom_of, after)


def couple_kernel(where, kept, got, allowed, near, far, out, table):
    half = PCAP // 2
    width = out.shape[2]
    side = where[1] & 1
    for part, which in ((near, side), (far, 1 - side)):
        rows = pl.ds(pl.multiple_of(which * half, half), half)
        table[rows] = part[...] * allowed[rows]
    total = kept[0] + got[0].astype(jnp.float32)
    high = total.astype(jnp.bfloat16)
    low = (total - high.astype(jnp.float32)).astype(jnp.bfloat16)
    both = jnp.dot(table[...], jnp.concatenate([high, low], axis=1), preferred_element_type=jnp.float32)
    out[0] = (both[:, :width] + both[:, width:]).astype(out.dtype)


def couple(where, kept, got, allowed, near, far):
    return pl.pallas_call(
        couple_kernel,
        in_specs=[SMEM] + [VMEM] * 5,
        out_specs=VMEM,
        out_shape=jax.ShapeDtypeStruct(kept.shape, jnp.bfloat16),
        scratch_shapes=[pltpu.VMEM((PCAP, PCAP), jnp.bfloat16)],
        compiler_params=PARAMS,
        name="couple",
    )(where, kept, got, allowed, near, far)


def apply_kernel(chips, where, projectors, *refs):
    *pieces, out, scaled, blocks, sems = refs
    core, chip = where[0], where[1]
    count = len(pieces) // 2
    for own, parts in ((True, pieces[:count]), (False, pieces[count:])):
        group = core if own else 1 - core
        rows = pl.ds(pl.multiple_of(group * PCAP, PCAP), PCAP)
        position = 0
        for part in parts:
            for at in range(part.shape[0]):
                start = pl.multiple_of(chunk_of(chips, chip, group, position) * LANES, LANES)
                scaled[rows, pl.ds(start, LANES)] = part[at]
                position += 1
    copies = []
    for block in range(out.shape[1] // COLUMNS):
        columns = slice(block * COLUMNS, (block + 1) * COLUMNS)
        slot = block % 2
        if block >= 2:
            copies[block - 2].wait()
        blocks[slot] = jnp.dot(
            projectors[...], scaled[:, columns], preferred_element_type=jnp.float32
        ).astype(jnp.bfloat16)
        copies.append(pltpu.make_async_copy(blocks.at[slot], out.at[:, columns], sems.at[slot]))
        copies[-1].start()
    for copy in copies[-2:]:
        copy.wait()


def apply(where, projectors, pieces):
    depth, slots = projectors.shape
    chips = lax.axis_size("pw") // 2
    width = pieces[0].shape[2]
    bands = chips * width
    if width != LANES:
        count = len(pieces) // 2
        rows = []
        for group in range(2):
            chunks = jnp.stack([chunk_of(chips, where[1], group, at) for at in range(chips)])
            mine = jnp.concatenate(pieces[:count])
            other = jnp.concatenate(pieces[count:])
            blocks = jnp.where(where[0] == group, mine, other)
            rows.append(jnp.zeros_like(blocks).at[chunks].set(blocks).transpose(1, 0, 2).reshape(PCAP, bands))
        return jnp.dot(projectors, jnp.concatenate(rows), preferred_element_type=jnp.float32).astype(jnp.bfloat16)

    def kernel(*refs):
        apply_kernel(chips, *refs)

    return pl.pallas_call(
        kernel,
        in_specs=[SMEM, VMEM] + [VMEM] * len(pieces),
        out_specs=HBM,
        out_shape=jax.ShapeDtypeStruct((depth, bands), jnp.bfloat16),
        scratch_shapes=[
            pltpu.VMEM((slots, bands), jnp.bfloat16),
            pltpu.VMEM((2, depth, COLUMNS), jnp.bfloat16),
            pltpu.SemaphoreType.DMA((2,)),
        ],
        compiler_params=PARAMS,
        cost_estimate=pl.CostEstimate(
            flops=2 * depth * slots * bands, bytes_accessed=2 * depth * (slots + bands), transcendentals=0
        ),
        name="apply",
    )(where, projectors, *pieces)


def local(band_coeffs, projectors, counts, atom_of, owners, couplings):
    chips = lax.axis_size("pw") // 2
    stages = chips.bit_length() - 1
    half = chips // 2
    width = band_coeffs.shape[1] // chips
    me = lax.axis_index("pw")
    where = jnp.stack([me % 2, me // 2, me])

    own_table = couplings[0]
    sibling_table = swap_cores(own_table)
    if width == LANES:
        theirs, ours, flipped, columns = project(where, projectors, band_coeffs, True)
    else:
        theirs, ours = project_plain(where, projectors, band_coeffs, half)
    near, far = choose(where, owners, own_table, sibling_table, theirs)
    theirs = swap_cores(theirs)
    far = swap_bits(far, [0, 0])
    if width == LANES:
        flipped, far = lax.optimization_barrier((flipped, far))
        low_theirs, low_ours = project(where, flipped, columns, False)
    else:
        low_theirs, low_ours = project_plain(where, projectors, band_coeffs, 0)
    message = add(ours, theirs)
    got = swap_stage(message, 0)
    low_theirs = swap_cores(low_theirs)
    allowed = mask(where, counts, atom_of, message)
    for stage in range(1, stages):
        near = merge(near, far, message)
        far = swap_bits(near, [stages - stage] * 2)
        if stage == 1:
            kept, message = fold(low_ours, low_theirs, got)
        else:
            kept, message = fold(kept, got)
        got = swap_stage(message, stage)
    near = merge(near, far, message)
    far = swap_bits(near, [0, 0])

    scaled = couple(where, kept, got, allowed, near, far)
    mine = jnp.concatenate([scaled, swap_stage(scaled, stages - 1)])
    pieces = [mine]
    others = [swap_cores(mine)]
    for stage in range(stages - 2, -1, -1):
        if stage < stages - 2:
            mine, others[0] = lax.optimization_barrier((mine, others[0]))
        got = swap_stage(mine, stage)
        got, others[-1] = lax.optimization_barrier((got, others[-1]))
        pieces.append(got)
        others.append(swap_cores(got))
        if stage:
            mine = jnp.concatenate([mine, got])
    return apply(where, projectors, pieces + others)


def solution(mesh):
    placed = (
        P("pw", "group"),
        P("pw", "group"),
        P("group", None),
        P("group", None),
        P("group"),
        P("pw", "group", None),
    )
    return jax.shard_map(
        local, mesh=mesh, in_specs=placed, out_specs=P("pw", "group"), check_vma=False
    )
```

time: 67.5 us -> 59.3 us (0.88)
  waiting for transfers between devices: 33.7 us -> 24 us
  starting transfers between devices: 12.1 us -> 19.3 us
  Pallas kernels: 21.3 us -> 15.6 us
    ppermute x10, waiting for transfers between devices: 32.3 us -> 21.1 us  [swap_bits(): lax.ppermute(x, 'pw', [(i, i ^ 2 << bits[i % 2]) for i in range(count)])]
    ppermute x10, starting transfers between devices: 10.5 us -> 18.7 us  [swap_bits(): lax.ppermute(x, 'pw', [(i, i ^ 2 << bits[i % 2]) for i in range(count)])]
    pallas_call x6 -> x8, Pallas kernels: 16.1 us -> 8.84 us  [the longest x2 6.83 us: project(): pl.pallas_call(kernel, in_specs=[SMEM, HBM, HBM] if fresh else [SMEM, VME...]
    pallas_call x1, Pallas kernels: 4.96 us -> 6.57 us  [apply(): pl.pallas_call(kernel, in_specs=[SMEM, VMEM] + [VMEM] * len(pieces), out_...]
    ppermute x6, waiting for transfers between devices: 1.41 us -> 2.89 us  [swap_cores(): return lax.ppermute(x, 'pw', [(i, i ^ 1) for i in range(count)])]
    ppermute x6, starting transfers between devices: 1.61 us -> 0.64 us  [swap_cores(): return lax.ppermute(x, 'pw', [(i, i ^ 1) for i in range(count)])]
  transfers between devices with their start and end apart: 16 -> 16, of which waited for: 9 -> 11; matrix products, arithmetic and copies ran while one was open for 0% -> 0% of each run, Pallas kernels for 17% -> 14%
where the time goes in v4:
time: 59.3 us; the launch traced here: 59.1 us
  waiting for transfers between devices  24 us (40%)
  starting transfers between devices  19.3 us (33%)
  Pallas kernels  15.6 us (26%)
    ppermute x10, waiting for transfers between devices, swap_bits(): lax.ppermute(x, 'pw', [(i, i ^ 2 << bits[i % 2]) for i in range(count)])  21.1 us
    ppermute x10, starting transfers between devices, swap_bits(): lax.ppermute(x, 'pw', [(i, i ^ 2 << bits[i % 2]) for i in range(count)])  18.7 us
    pallas_call x2, Pallas kernels, project(): pl.pallas_call(kernel, in_specs=[SMEM, HBM, HBM] if fresh else [SMEM, VME...  6.83 us
    pallas_call x1, Pallas kernels, apply(): pl.pallas_call(kernel, in_specs=[SMEM, VMEM] + [VMEM] * len(pieces), out_...  6.57 us
    ppermute x6, waiting for transfers between devices, swap_cores(): return lax.ppermute(x, 'pw', [(i, i ^ 1) for i in range(count)])  2.89 us
  transfers between devices with their start and end apart: 16, of which 11 were waited for; matrix products, arithmetic and copies ran while one was open for 0% of the time, Pallas kernels for 14%

profile of v4, /device:TPU:0, one launch (start us, length us, event | category | flops | bytes accessed | tf_op | source)
XLA Modules:
  0.0 59.1 jit_solution(5751394590501164718)
XLA Ops:
  0.0 0.0 copy-start.1
  0.0 0.0 copy-start.4
  0.0 0.5 collective-permute-start
  0.5 0.1 pad_add_fusion.refs_0_.where
  0.5 4.9 %project_sent.1 = (bf16[4,256,128]{2,1,0:T(8,128)(2,1)S(1)}, f32[4,256,128]{2,1,0:T(8,128)S(1)}, bf16[512,2048]{1,0:T(8,128)(2,1)S(1)}, bf16[2048,1024]{1,0:T(8,128)(2,1)S(1)}) custom-call(s32[3]{0:T(128)S(1)} %pad_add_fusion.refs_0_.where, bf16[2048,512]{1,0:T(8,128)(2,1)} %refs_1_.3, bf16[2048,1024]{1,0:T(8,128)(2,1)} %refs_2_.1), custom_call_target="tpu_custom_call" | custom-call | flops 1073741824 | bytes 4194304 | tf_op jit(solution)/shard_map/project_sent/pallas_call | solution.py:149
  5.4 0.1 collective-permute-start.3
  5.5 0.0 collective-permute-done.sibling
  5.5 0.0 copy-done.1
  5.5 0.0 copy-done.4
  5.5 0.6 choose.1
  6.1 3.0 %collective-permute-start.1 = (bf16[128,256]{1,0:T(8,128)(2,1)S(1)}, bf16[128,256]{1,0:T(8,128)(2,1)S(1)}, u32[]{:S(2)}, u32[]{:S(2)}) collective-permute-start(bf16[128,256]{1,0:T(8,128)(2,1)S(1)} %get-tuple-element.27), channel_id=1, source_target_pairs={{0,2},{1,3},{2,0},{3,1},{4,6},{5,7},{6,4},{7,5},{8,10},{9,11},{10,... | collective-permute-start | bytes 196616 | tf_op jit(solution)/shard_map/ppermute | solution.py:46
  9.2 0.0 collective-permute-done.3.right
  9.2 0.1 add.11.after
  9.2 0.6 collective-permute-start.4
  9.8 1.7 %collective-permute-done.1.right = bf16[128,256]{1,0:T(8,128)(2,1)S(1)} collective-permute-done((bf16[128,256]{1,0:T(8,128)(2,1)S(1)}, bf16[128,256]{1,0:T(8,128)(2,1)S(1)}, u32[]{:S(2)}, u32[]{:S(2)}) %collective-permute-start.1) | collective-permute-done | bytes 65568 | tf_op jit(solution)/shard_map/ppermute | solution.py:46
  11.4 0.0 copy-start.2
  11.4 0.0 copy-start.3
  11.4 0.0 copy-start
  11.4 2.0 %project_kept.1 = (bf16[4,256,128]{2,1,0:T(8,128)(2,1)S(1)}, f32[4,256,128]{2,1,0:T(8,128)S(1)}) custom-call(s32[3]{0:T(128)S(1)} %pad_add_fusion.refs_0_.where, bf16[512,2048]{1,0:T(8,128)(2,1)S(1)} %get-tuple-element.28.refs_1_, bf16[2048,1024]{1,0:T(8,128)(2,1)S(1)} %get-tuple-element.29.refs_2_), custom_call_target="tpu_custom_call" | custom-call | flops 1073741824 | bytes 4194304 | tf_op jit(solution)/shard_map/project_kept/pallas_call | solution.py:149
  13.4 0.1 collective-permute-start.2
  13.5 2.1 %collective-permute-done.4.refs_2_ = bf16[4,256,128]{2,1,0:T(8,128)(2,1)S(1)} collective-permute-done((bf16[4,256,128]{2,1,0:T(8,128)(2,1)S(1)}, bf16[4,256,128]{2,1,0:T(8,128)(2,1)S(1)}, u32[]{:S(2)}, u32[]{:S(2)}) %collective-permute-start.4) | collective-permute-done | bytes 262176 | tf_op jit(solution)/shard_map/ppermute | solution.py:46
  15.7 0.0 collective-permute-done.2.refs_1_
  15.7 0.1 fold.2
  15.8 1.6 %collective-permute-start.5 = (bf16[2,256,128]{2,1,0:T(8,128)(2,1)S(1)}, bf16[2,256,128]{2,1,0:T(8,128)(2,1)S(1)}, u32[]{:S(2)}, u32[]{:S(2)}) collective-permute-start(bf16[2,256,128]{2,1,0:T(8,128)(2,1)S(1)} %get-tuple-element.34.after), channel_id=1, source_target_pairs={{0,4},{1,3},{2,6},{3,1},{4,0},{5,7},{6,2},{7,5},{8,12},{9,11},{10,... | collective-permute-start | bytes 393224 | tf_op jit(solution)/shard_map/ppermute | solution.py:46
  17.4 2.6 %collective-permute-start.7 = (bf16[128,256]{1,0:T(8,128)(2,1)S(1)}, bf16[128,256]{1,0:T(8,128)(2,1)S(1)}, u32[]{:S(2)}, u32[]{:S(2)}) collective-permute-start(bf16[128,256]{1,0:T(8,128)(2,1)S(1)} %merge.3.left), channel_id=1, source_target_pairs={{0,8},{1,9},{2,10},{3,11},{4,12},{5,13},{6,14},{7,15},{8,0},{9,1},... | collective-permute-start | bytes 196616 | tf_op jit(solution)/shard_map/ppermute | solution.py:46
  20.0 3.1 %collective-permute-done.7.right = bf16[128,256]{1,0:T(8,128)(2,1)S(1)} collective-permute-done((bf16[128,256]{1,0:T(8,128)(2,1)S(1)}, bf16[128,256]{1,0:T(8,128)(2,1)S(1)}, u32[]{:S(2)}, u32[]{:S(2)}) %collective-permute-start.7) | collective-permute-done | bytes 65568 | tf_op jit(solution)/shard_map/ppermute | solution.py:46
  23.1 1.7 %collective-permute-start.8 = (bf16[128,256]{1,0:T(8,128)(2,1)S(1)}, bf16[128,256]{1,0:T(8,128)(2,1)S(1)}, u32[]{:S(2)}, u32[]{:S(2)}) collective-permute-start(bf16[128,256]{1,0:T(8,128)(2,1)S(1)} %merge.4.left), channel_id=1, source_target_pairs={{0,4},{1,5},{2,6},{3,7},{4,0},{5,1},{6,2},{7,3},{8,12},{9,13},{10,... | collective-permute-start | bytes 196616 | tf_op jit(solution)/shard_map/ppermute | solution.py:46
  24.9 0.0 collective-permute-done.5.refs_1_
  24.9 2.6 %collective-permute-done.8.right = bf16[128,256]{1,0:T(8,128)(2,1)S(1)} collective-permute-done((bf16[128,256]{1,0:T(8,128)(2,1)S(1)}, bf16[128,256]{1,0:T(8,128)(2,1)S(1)}, u32[]{:S(2)}, u32[]{:S(2)}) %collective-permute-start.8) | collective-permute-done | bytes 65568 | tf_op jit(solution)/shard_map/ppermute | solution.py:46
  27.5 0.9 %collective-permute-start.9 = (bf16[128,256]{1,0:T(8,128)(2,1)S(1)}, bf16[128,256]{1,0:T(8,128)(2,1)S(1)}, u32[]{:S(2)}, u32[]{:S(2)}) collective-permute-start(bf16[128,256]{1,0:T(8,128)(2,1)S(1)} %merge.5.near), channel_id=1, source_target_pairs={{0,2},{1,3},{2,0},{3,1},{4,6},{5,7},{6,4},{7,5},{8,10},{9,11},{10,... | collective-permute-start | bytes 196616 | tf_op jit(solution)/shard_map/ppermute | solution.py:46
  28.4 2.6 %collective-permute-start.6 = (bf16[1,256,128]{2,1,0:T(8,128)(2,1)S(1)}, bf16[1,256,128]{2,1,0:T(8,128)(2,1)S(1)}, u32[]{:S(2)}, u32[]{:S(2)}) collective-permute-start(bf16[1,256,128]{2,1,0:T(8,128)(2,1)S(1)} %get-tuple-element.36.after), channel_id=1, source_target_pairs={{0,8},{1,9},{2,10},{3,11},{4,12},{5,13},{6,14},{7,15},{8,0},{9,1},... | collective-permute-start | bytes 196616 | tf_op jit(solution)/shard_map/ppermute | solution.py:46
  31.0 0.0 copy-done.2
  31.0 0.0 copy-done.3
  31.0 0.7 %mask.1.allowed = bf16[256,256]{1,0:T(8,128)(2,1)S(1)} custom-call(s32[3]{0:T(128)S(1)} %pad_add_fusion.refs_0_.where, s32[2,4]{1,0:T(2,128)S(1)} %copy-done.3, s32[2,256]{1,0:T(2,128)S(1)} %copy-done.2, bf16[4,256,128]{2,1,0:T(8,128)(2,1)S(1)} %add.11.after), custom_call_target="tpu_custom_call" | custom-call | tf_op jit(solution)/shard_map/mask/pallas_call | solution.py:260
  31.6 0.2 collective-permute-done.9.far
  31.8 1.7 %collective-permute-done.6.got = bf16[1,256,128]{2,1,0:T(8,128)(2,1)S(1)} collective-permute-done((bf16[1,256,128]{2,1,0:T(8,128)(2,1)S(1)}, bf16[1,256,128]{2,1,0:T(8,128)(2,1)S(1)}, u32[]{:S(2)}, u32[]{:S(2)}) %collective-permute-start.6) | collective-permute-done | bytes 65568 | tf_op jit(solution)/shard_map/ppermute | solution.py:46
  33.5 0.7 %couple.1 = bf16[1,256,128]{2,1,0:T(8,128)(2,1)S(1)} custom-call(s32[3]{0:T(128)S(1)} %pad_add_fusion.refs_0_.where, f32[1,256,128]{2,1,0:T(8,128)S(1)} %get-tuple-element.35.kept, bf16[1,256,128]{2,1,0:T(8,128)(2,1)S(1)} %collective-permute-done.6.got, bf16[256,256]{1,0:T(8,128)(2,1)S(1)} %mask.1.allowed, bf16[128,256]{1,0:T(8,128)(2,1)S(1)} %merge.5.near, ...), custom_call_target="tpu_custom_call" | custom-call | tf_op jit(solution)/shard_map/couple/pallas_call | solution.py:285
  34.3 2.8 %collective-permute-start.10 = (bf16[1,256,128]{2,1,0:T(8,128)(2,1)S(1)}, bf16[1,256,128]{2,1,0:T(8,128)(2,1)S(1)}, u32[]{:S(2)}, u32[]{:S(2)}) collective-permute-start(bf16[1,256,128]{2,1,0:T(8,128)(2,1)S(1)} %couple.1), channel_id=1, source_target_pairs={{0,8},{1,9},{2,10},{3,11},{4,12},{5,13},{6,14},{7,15},{8,0},{9,1},... | collective-permute-start | bytes 196616 | tf_op jit(solution)/shard_map/ppermute | solution.py:46
  37.0 2.5 %collective-permute-done.10 = bf16[1,256,128]{2,1,0:T(8,128)(2,1)S(1)} collective-permute-done((bf16[1,256,128]{2,1,0:T(8,128)(2,1)S(1)}, bf16[1,256,128]{2,1,0:T(8,128)(2,1)S(1)}, u32[]{:S(2)}, u32[]{:S(2)}) %collective-permute-start.10) | collective-permute-done | bytes 65568 | tf_op jit(solution)/shard_map/ppermute | solution.py:46
  39.5 1.6 %collective-permute-start.11 = (bf16[2,256,128]{2,1,0:T(8,128)(2,1)S(1)}, bf16[2,256,128]{2,1,0:T(8,128)(2,1)S(1)}, u32[]{:S(2)}, u32[]{:S(2)}) collective-permute-start(bf16[2,256,128]{2,1,0:T(8,128)(2,1)S(1)} %pad_maximum_fusion.1.refs_2_), channel_id=1, source_target_pairs={{0,4},{1,3},{2,6},{3,1},{4,0},{5,7},{6,2},{7,5},{8,12},{9,11},{10,... | collective-permute-start | bytes 393224 | tf_op jit(solution)/shard_map/ppermute | solution.py:46
  41.1 0.0 collective-permute-start.12
  41.1 3.5 %collective-permute-done.11.refs_3_ = bf16[2,256,128]{2,1,0:T(8,128)(2,1)S(1)} collective-permute-done((bf16[2,256,128]{2,1,0:T(8,128)(2,1)S(1)}, bf16[2,256,128]{2,1,0:T(8,128)(2,1)S(1)}, u32[]{:S(2)}, u32[]{:S(2)}) %collective-permute-start.11) | collective-permute-done | bytes 131104 | tf_op jit(solution)/shard_map/ppermute | solution.py:46
  44.6 0.0 collective-permute-done.12.refs_5_
  44.6 1.3 %collective-permute-start.13 = (bf16[4,256,128]{2,1,0:T(8,128)(2,1)S(1)}, bf16[4,256,128]{2,1,0:T(8,128)(2,1)S(1)}, u32[]{:S(2)}, u32[]{:S(2)}) collective-permute-start(bf16[4,256,128]{2,1,0:T(8,128)(2,1)S(1)} %pad_maximum_fusion), channel_id=1, source_target_pairs={{0,2},{1,5},{2,0},{3,7},{4,6},{5,1},{6,4},{7,3},{8,10},{9,13},{10,... | collective-permute-start | bytes 786440 | tf_op jit(solution)/shard_map/ppermute | solution.py:46
  45.9 0.0 collective-permute-start.14
  45.9 1.3 %collective-permute-done.14.refs_6_ = bf16[2,256,128]{2,1,0:T(8,128)(2,1)S(1)} collective-permute-done((bf16[2,256,128]{2,1,0:T(8,128)(2,1)S(1)}, bf16[2,256,128]{2,1,0:T(8,128)(2,1)S(1)}, u32[]{:S(2)}, u32[]{:S(2)}) %collective-permute-start.14) | collective-permute-done | bytes 131104 | tf_op jit(solution)/shard_map/ppermute | solution.py:41
  47.2 3.8 %collective-permute-done.13.refs_4_ = bf16[4,256,128]{2,1,0:T(8,128)(2,1)S(1)} collective-permute-done((bf16[4,256,128]{2,1,0:T(8,128)(2,1)S(1)}, bf16[4,256,128]{2,1,0:T(8,128)(2,1)S(1)}, u32[]{:S(2)}, u32[]{:S(2)}) %collective-permute-start.13) | collective-permute-done | bytes 262176 | tf_op jit(solution)/shard_map/ppermute | solution.py:46
  51.0 0.0 collective-permute-start.15
  51.0 1.5 %collective-permute-done.15.refs_7_ = bf16[4,256,128]{2,1,0:T(8,128)(2,1)S(1)} collective-permute-done((bf16[4,256,128]{2,1,0:T(8,128)(2,1)S(1)}, bf16[4,256,128]{2,1,0:T(8,128)(2,1)S(1)}, u32[]{:S(2)}, u32[]{:S(2)}) %collective-permute-start.15) | collective-permute-done | bytes 262176 | tf_op jit(solution)/shard_map/ppermute | solution.py:41
  52.6 0.0 copy-done
  52.6 6.6 %apply.1 = bf16[2048,1024]{1,0:T(8,128)(2,1)} custom-call(s32[3]{0:T(128)S(1)} %pad_add_fusion.refs_0_.where, bf16[2048,512]{1,0:T(8,128)(2,1)S(1)} %copy-done, bf16[2,256,128]{2,1,0:T(8,128)(2,1)S(1)} %pad_maximum_fusion.1.refs_2_, bf16[2,256,128]{2,1,0:T(8,128)(2,1)S(1)} %collective-permute-done.11.refs_3_, ...), custom_call_target="tpu_custom_call" | custom-call | flops 2147483648 | bytes 6291456 | tf_op jit(solution)/shard_map/apply/pallas_call | solution.py:343
  (6 shorter events, 0.1 us)
Async XLA Ops:
  0.0 5.5 %copy-start.1 = (f32[1,256,256]{2,1,0:T(8,128)S(1)}, f32[1,256,256]{2,1,0:T(8,128)}, u32[]{:S(2)}) copy-start(f32[1,256,256]{2,1,0:T(8,128)} %param.11) | copy-start | bytes 786436
  0.0 5.5 %copy-start.4 = (s32[2]{0:T(128)S(1)}, s32[2]{0:T(128)}, u32[]{:S(2)}) copy-start(s32[2]{0:T(128)} %owners.1) | copy-start | bytes 28
  0.0 5.5 %collective-permute-start = (f32[256,256]{1,0:T(8,128)}, f32[256,256]{1,0:T(8,128)S(1)}, u32[]{:S(2)}, u32[]{:S(2)}) collective-permute-start(f32[256,256]{1,0:T(8,128)} %bitcast.4), channel_id=1, source_target_pairs={{0,1},{1,0},{2,3},{3,2},{4,5},{5,4},{6,7},{7,6},{8,9},{9,8},{10,11... | collective-permute-start | bytes 786440 | tf_op jit(solution)/shard_map/ppermute | solution.py:41
  5.4 3.8 %collective-permute-start.3 = (bf16[4,256,128]{2,1,0:T(8,128)(2,1)S(1)}, bf16[4,256,128]{2,1,0:T(8,128)(2,1)S(1)}, u32[]{:S(2)}, u32[]{:S(2)}) collective-permute-start(bf16[4,256,128]{2,1,0:T(8,128)(2,1)S(1)} %get-tuple-element.26.after), channel_id=1, source_target_pairs={{0,1},{1,0},{2,3},{3,2},{4,5},{5,4},{6,7},{7,6},{8,9},{9,8},{10,11... | collective-permute-start | bytes 786440 | tf_op jit(solution)/shard_map/ppermute | solution.py:41
  6.1 5.3 %collective-permute-start.1 = (bf16[128,256]{1,0:T(8,128)(2,1)S(1)}, bf16[128,256]{1,0:T(8,128)(2,1)S(1)}, u32[]{:S(2)}, u32[]{:S(2)}) collective-permute-start(bf16[128,256]{1,0:T(8,128)(2,1)S(1)} %get-tuple-element.27), channel_id=1, source_target_pairs={{0,2},{1,3},{2,0},{3,1},{4,6},{5,7},{6,4},{7,5},{8,10},{9,11},{10,... | collective-permute-start | bytes 196616 | tf_op jit(solution)/shard_map/ppermute | solution.py:46
  9.2 6.4 %collective-permute-start.4 = (bf16[4,256,128]{2,1,0:T(8,128)(2,1)S(1)}, bf16[4,256,128]{2,1,0:T(8,128)(2,1)S(1)}, u32[]{:S(2)}, u32[]{:S(2)}) collective-permute-start(bf16[4,256,128]{2,1,0:T(8,128)(2,1)S(1)} %add.11.after), channel_id=1, source_target_pairs={{0,2},{1,5},{2,0},{3,7},{4,6},{5,1},{6,4},{7,3},{8,10},{9,13},{10,... | collective-permute-start | bytes 786440 | tf_op jit(solution)/shard_map/ppermute | solution.py:46
  11.4 19.5 %copy-start.2 = (s32[2,256]{1,0:T(2,128)S(1)}, s32[2,256]{1,0:T(2,128)}, u32[]{:S(2)}) copy-start(s32[2,256]{1,0:T(2,128)} %atom_of.1) | copy-start | bytes 6148
  11.4 19.5 %copy-start.3 = (s32[2,4]{1,0:T(2,128)S(1)}, s32[2,4]{1,0:T(2,128)}, u32[]{:S(2)}) copy-start(s32[2,4]{1,0:T(2,128)} %counts.1) | copy-start | bytes 100
  11.4 41.1 %copy-start = (bf16[2048,512]{1,0:T(8,128)(2,1)S(1)}, bf16[2048,512]{1,0:T(8,128)(2,1)}, u32[]{:S(2)}) copy-start(bf16[2048,512]{1,0:T(8,128)(2,1)} %refs_1_.3) | copy-start | bytes 6291460
  13.4 2.2 %collective-permute-start.2 = (bf16[4,256,128]{2,1,0:T(8,128)(2,1)S(1)}, bf16[4,256,128]{2,1,0:T(8,128)(2,1)S(1)}, u32[]{:S(2)}, u32[]{:S(2)}) collective-permute-start(bf16[4,256,128]{2,1,0:T(8,128)(2,1)S(1)} %get-tuple-element.31), channel_id=1, source_target_pairs={{0,1},{1,0},{2,3},{3,2},{4,5},{5,4},{6,7},{7,6},{8,9},{9,8},{10,11... | collective-permute-start | bytes 786440 | tf_op jit(solution)/shard_map/ppermute | solution.py:41
  15.8 9.1 %collective-permute-start.5 = (bf16[2,256,128]{2,1,0:T(8,128)(2,1)S(1)}, bf16[2,256,128]{2,1,0:T(8,128)(2,1)S(1)}, u32[]{:S(2)}, u32[]{:S(2)}) collective-permute-start(bf16[2,256,128]{2,1,0:T(8,128)(2,1)S(1)} %get-tuple-element.34.after), channel_id=1, source_target_pairs={{0,4},{1,3},{2,6},{3,1},{4,0},{5,7},{6,2},{7,5},{8,12},{9,11},{10,... | collective-permute-start | bytes 393224 | tf_op jit(solution)/shard_map/ppermute | solution.py:46
  17.4 5.7 %collective-permute-start.7 = (bf16[128,256]{1,0:T(8,128)(2,1)S(1)}, bf16[128,256]{1,0:T(8,128)(2,1)S(1)}, u32[]{:S(2)}, u32[]{:S(2)}) collective-permute-start(bf16[128,256]{1,0:T(8,128)(2,1)S(1)} %merge.3.left), channel_id=1, source_target_pairs={{0,8},{1,9},{2,10},{3,11},{4,12},{5,13},{6,14},{7,15},{8,0},{9,1},... | collective-permute-start | bytes 196616 | tf_op jit(solution)/shard_map/ppermute | solution.py:46
  23.1 4.3 %collective-permute-start.8 = (bf16[128,256]{1,0:T(8,128)(2,1)S(1)}, bf16[128,256]{1,0:T(8,128)(2,1)S(1)}, u32[]{:S(2)}, u32[]{:S(2)}) collective-permute-start(bf16[128,256]{1,0:T(8,128)(2,1)S(1)} %merge.4.left), channel_id=1, source_target_pairs={{0,4},{1,5},{2,6},{3,7},{4,0},{5,1},{6,2},{7,3},{8,12},{9,13},{10,... | collective-permute-start | bytes 196616 | tf_op jit(solution)/shard_map/ppermute | solution.py:46
  27.5 4.3 %collective-permute-start.9 = (bf16[128,256]{1,0:T(8,128)(2,1)S(1)}, bf16[128,256]{1,0:T(8,128)(2,1)S(1)}, u32[]{:S(2)}, u32[]{:S(2)}) collective-permute-start(bf16[128,256]{1,0:T(8,128)(2,1)S(1)} %merge.5.near), channel_id=1, source_target_pairs={{0,2},{1,3},{2,0},{3,1},{4,6},{5,7},{6,4},{7,5},{8,10},{9,11},{10,... | collective-permute-start | bytes 196616 | tf_op jit(solution)/shard_map/ppermute | solution.py:46
  28.4 5.2 %collective-permute-start.6 = (bf16[1,256,128]{2,1,0:T(8,128)(2,1)S(1)}, bf16[1,256,128]{2,1,0:T(8,128)(2,1)S(1)}, u32[]{:S(2)}, u32[]{:S(2)}) collective-permute-start(bf16[1,256,128]{2,1,0:T(8,128)(2,1)S(1)} %get-tuple-element.36.after), channel_id=1, source_target_pairs={{0,8},{1,9},{2,10},{3,11},{4,12},{5,13},{6,14},{7,15},{8,0},{9,1},... | collective-permute-start | bytes 196616 | tf_op jit(solution)/shard_map/ppermute | solution.py:46
  34.3 5.2 %collective-permute-start.10 = (bf16[1,256,128]{2,1,0:T(8,128)(2,1)S(1)}, bf16[1,256,128]{2,1,0:T(8,128)(2,1)S(1)}, u32[]{:S(2)}, u32[]{:S(2)}) collective-permute-start(bf16[1,256,128]{2,1,0:T(8,128)(2,1)S(1)} %couple.1), channel_id=1, source_target_pairs={{0,8},{1,9},{2,10},{3,11},{4,12},{5,13},{6,14},{7,15},{8,0},{9,1},... | collective-permute-start | bytes 196616 | tf_op jit(solution)/shard_map/ppermute | solution.py:46
  39.5 5.0 %collective-permute-start.11 = (bf16[2,256,128]{2,1,0:T(8,128)(2,1)S(1)}, bf16[2,256,128]{2,1,0:T(8,128)(2,1)S(1)}, u32[]{:S(2)}, u32[]{:S(2)}) collective-permute-start(bf16[2,256,128]{2,1,0:T(8,128)(2,1)S(1)} %pad_maximum_fusion.1.refs_2_), channel_id=1, source_target_pairs={{0,4},{1,3},{2,6},{3,1},{4,0},{5,7},{6,2},{7,5},{8,12},{9,11},{10,... | collective-permute-start | bytes 393224 | tf_op jit(solution)/shard_map/ppermute | solution.py:46
  41.1 3.5 %collective-permute-start.12 = (bf16[2,256,128]{2,1,0:T(8,128)(2,1)S(1)}, bf16[2,256,128]{2,1,0:T(8,128)(2,1)S(1)}, u32[]{:S(2)}, u32[]{:S(2)}) collective-permute-start(bf16[2,256,128]{2,1,0:T(8,128)(2,1)S(1)} %pad_maximum_fusion.1.refs_2_), channel_id=1, source_target_pairs={{0,1},{1,0},{2,3},{3,2},{4,5},{5,4},{6,7},{7,6},{8,9},{9,8},{10,11... | collective-permute-start | bytes 393224 | tf_op jit(solution)/shard_map/ppermute | solution.py:41
  44.6 6.4 %collective-permute-start.13 = (bf16[4,256,128]{2,1,0:T(8,128)(2,1)S(1)}, bf16[4,256,128]{2,1,0:T(8,128)(2,1)S(1)}, u32[]{:S(2)}, u32[]{:S(2)}) collective-permute-start(bf16[4,256,128]{2,1,0:T(8,128)(2,1)S(1)} %pad_maximum_fusion), channel_id=1, source_target_pairs={{0,2},{1,5},{2,0},{3,7},{4,6},{5,1},{6,4},{7,3},{8,10},{9,13},{10,... | collective-permute-start | bytes 786440 | tf_op jit(solution)/shard_map/ppermute | solution.py:46
  45.9 1.3 %collective-permute-start.14 = (bf16[2,256,128]{2,1,0:T(8,128)(2,1)S(1)}, bf16[2,256,128]{2,1,0:T(8,128)(2,1)S(1)}, u32[]{:S(2)}, u32[]{:S(2)}) collective-permute-start(bf16[2,256,128]{2,1,0:T(8,128)(2,1)S(1)} %collective-permute-done.11.refs_3_), channel_id=1, source_target_pairs={{0,1},{1,0},{2,3},{3,2},{4,5},{5,4},{6,7},{7,6},{8,9},{9,8},{10,11... | collective-permute-start | bytes 393224 | tf_op jit(solution)/shard_map/ppermute | solution.py:41
  51.0 1.5 %collective-permute-start.15 = (bf16[4,256,128]{2,1,0:T(8,128)(2,1)S(1)}, bf16[4,256,128]{2,1,0:T(8,128)(2,1)S(1)}, u32[]{:S(2)}, u32[]{:S(2)}) collective-permute-start(bf16[4,256,128]{2,1,0:T(8,128)(2,1)S(1)} %collective-permute-done.13.refs_4_), channel_id=1, source_target_pairs={{0,1},{1,0},{2,3},{3,2},{4,5},{5,4},{6,7},{7,6},{8,9},{9,8},{10,11... | collective-permute-start | bytes 786440 | tf_op jit(solution)/shard_map/ppermute | solution.py:41

commit v5 on v4

--- a/solution.py
+++ b/solution.py
@@ -9,7 +9,7 @@
 CH_CAP = 64
 PCAP = 256
 LANES = 128
-COLUMNS = 256
+ROW_BLOCK = 512
 PARAMS = pltpu.CompilerParams(vmem_limit_bytes=32 * 1024 * 1024)
 VMEM = pl.BlockSpec(memory_space=pltpu.VMEM)
 SMEM = pl.BlockSpec(memory_space=pltpu.SMEM)
@@ -51,35 +51,39 @@
     return swap_bits(x, [bit_order(chips, core)[stage] for core in range(2)])
 
 
-def project_kernel(chips, fresh, where, projectors, bands, *refs):
-    if fresh:
-        theirs, ours, flipped, columns, slots, slot_sems, column_sems = refs
-    else:
-        theirs, ours = refs
-        flipped, columns = projectors, bands
+def load_kernel(where, projectors, flipped, slots, sems):
+    core = where[0]
+    count = sems.shape[0]
+    block = slots.shape[0] // count
+    copies = []
+    for at in range(count):
+        rows = slice(at * block, (at + 1) * block)
+        copies.append(pltpu.make_async_copy(projectors.at[rows], slots.at[rows], sems.at[at]))
+        copies[-1].start()
+    for at, copy in enumerate(copies):
+        copy.wait()
+        rows = slice(at * block, (at + 1) * block)
+        for place, group in enumerate((core, 1 - core)):
+            start = pl.multiple_of(group * PCAP, PCAP)
+            flipped[place * PCAP : (place + 1) * PCAP, rows] = slots[rows, pl.ds(start, PCAP)].T
+
+
+def load(where, projectors):
+    depth, slots = projectors.shape
+    return pl.pallas_call(
+        load_kernel,
+        in_specs=[SMEM, HBM],
+        out_specs=VMEM,
+        out_shape=jax.ShapeDtypeStruct((slots, depth), jnp.bfloat16),
+        scratch_shapes=[pltpu.VMEM((depth, slots), jnp.bfloat16), pltpu.SemaphoreType.DMA((4,))],
+        compiler_params=PARAMS,
+        name="load",
+    )(where, pltpu.with_memory_space_constraint(projectors, pltpu.HBM))
+
+
+def project_kernel(chips, first, where, flipped, columns, theirs, ours):
     core, chip = where[0], where[1]
     half = chips // 2
-    first = half if fresh else 0
-    if fresh:
-        slot_copies, column_copies = [], []
-        for copies, source, target, sems in (
-            (slot_copies, projectors, slots, slot_sems),
-            (column_copies, bands, columns, column_sems),
-        ):
-            block = source.shape[0] // sems.shape[0]
-            for at in range(sems.shape[0]):
-                rows = slice(at * block, (at + 1) * block)
-                copies.append(pltpu.make_async_copy(source.at[rows], target.at[rows], sems.at[at]))
-                copies[-1].start()
-        block = slots.shape[0] // len(slot_copies)
-        for at, copy in enumerate(slot_copies):
-            copy.wait()
-            rows = slice(at * block, (at + 1) * block)
-            for place, group in enumerate((core, 1 - core)):
-                start = pl.multiple_of(group * PCAP, PCAP)
-                flipped[place * PCAP : (place + 1) * PCAP, rows] = slots[rows, pl.ds(start, PCAP)].T
-        for copy in column_copies:
-            copy.wait()
 
     def pair_of_blocks(group, position):
         starts = [
@@ -106,6 +110,30 @@
                 )
 
 
+def project(where, flipped, band_coeffs, first):
+    depth, bands = band_coeffs.shape
+    chips = lax.axis_size("pw") // 2
+    half, width = chips // 2, bands // chips
+
+    def kernel(*refs):
+        project_kernel(chips, first, *refs)
+
+    return pl.pallas_call(
+        kernel,
+        in_specs=[SMEM, VMEM, VMEM],
+        out_specs=[VMEM, VMEM],
+        out_shape=[
+            jax.ShapeDtypeStruct((half, PCAP, width), jnp.bfloat16),
+            jax.ShapeDtypeStruct((half, PCAP, width), jnp.float32),
+        ],
+        compiler_params=PARAMS,
+        cost_estimate=pl.CostEstimate(
+            flops=2 * depth * PCAP * bands, bytes_accessed=2 * depth * bands, transcendentals=0
+        ),
+        name="project",
+    )(where, flipped, pltpu.with_memory_space_constraint(band_coeffs, pltpu.VMEM))
+
+
 def project_plain(where, projectors, band_coeffs, first):
     depth, bands = band_coeffs.shape
     chips = lax.axis_size("pw") // 2
@@ -120,46 +148,6 @@
     return outs
 
 
-def project(where, projectors, band_coeffs, fresh):
-    depth, bands = band_coeffs.shape
-    chips = lax.axis_size("pw") // 2
-    half, width = chips // 2, bands // chips
-
-    def kernel(*refs):
-        project_kernel(chips, fresh, *refs)
-
-    out_shape = [
-        jax.ShapeDtypeStruct((half, PCAP, width), jnp.bfloat16),
-        jax.ShapeDtypeStruct((half, PCAP, width), jnp.float32),
-    ]
-    scratch = []
-    if fresh:
-        slots = projectors.shape[1]
-        out_shape += [
-            jax.ShapeDtypeStruct((slots, depth), jnp.bfloat16),
-            jax.ShapeDtypeStruct((depth, bands), jnp.bfloat16),
-        ]
-        scratch = [
-            pltpu.VMEM((depth, slots), jnp.bfloat16),
-            pltpu.SemaphoreType.DMA((4,)),
-            pltpu.SemaphoreType.DMA((8,)),
-        ]
-        projectors = pltpu.with_memory_space_constraint(projectors, pltpu.HBM)
-        band_coeffs = pltpu.with_memory_space_constraint(band_coeffs, pltpu.HBM)
-    return pl.pallas_call(
-        kernel,
-        in_specs=[SMEM, HBM, HBM] if fresh else [SMEM, VMEM, VMEM],
-        out_specs=[VMEM] * len(out_shape),
-        out_shape=out_shape,
-        scratch_shapes=scratch,
-        compiler_params=PARAMS,
-        cost_estimate=pl.CostEstimate(
-            flops=2 * depth * PCAP * bands, bytes_accessed=2 * depth * bands, transcendentals=0
-        ),
-        name="project_sent" if fresh else "project_kept",
-    )(where, projectors, band_coeffs)
-
-
 def fold_kernel(*refs):
     *terms, kept, message = refs
     half = kept.shape[0]
@@ -293,69 +281,112 @@
     )(where, kept, got, allowed, near, far)
 
 
-def apply_kernel(chips, where, projectors, *refs):
-    *pieces, out, scaled, blocks, sems = refs
+def place(scaled, core, own, other):
+    for part, group in ((own, core), (other, 1 - core)):
+        rows = pl.ds(pl.multiple_of(group * PCAP, PCAP), PCAP)
+        scaled[rows, :LANES] = part[0]
+        scaled[rows, LANES:] = part[1]
+
+
+def begin_kernel(where, projectors, own_first, own_second, other_first, other_second, done, own, other, scaled):
+    core = where[0]
+    place(scaled, core, own_first[...], other_first[...])
+    for block in range(projectors.shape[0] // ROW_BLOCK):
+        rows = slice(block * ROW_BLOCK, (block + 1) * ROW_BLOCK)
+        done[rows] = jnp.dot(projectors[rows], scaled[...], preferred_element_type=jnp.float32).astype(done.dtype)
+        for out, part, group in ((own, own_second, core), (other, other_second, 1 - core)):
+            slots = pl.ds(pl.multiple_of(group * PCAP, PCAP), PCAP)
+            weights = jnp.concatenate([part[0], part[1]], axis=1)
+            out[rows] = jnp.dot(projectors[rows, slots], weights, preferred_element_type=jnp.float32)
+
+
+def begin(where, projectors, own_first, own_second, other_first, other_second):
+    depth, slots = projectors.shape
+    pair = 2 * LANES
+    return pl.pallas_call(
+        begin_kernel,
+        in_specs=[SMEM] + [VMEM] * 5,
+        out_specs=[VMEM] * 3,
+        out_shape=[
+            jax.ShapeDtypeStruct((depth, pair), jnp.bfloat16),
+            jax.ShapeDtypeStruct((depth, pair), jnp.float32),
+            jax.ShapeDtypeStruct((depth, pair), jnp.float32),
+        ],
+        scratch_shapes=[pltpu.VMEM((slots, pair), jnp.bfloat16)],
+        compiler_params=PARAMS,
+        cost_estimate=pl.CostEstimate(
+            flops=4 * depth * slots * pair, bytes_accessed=2 * depth * slots, transcendentals=0
+        ),
+        name="begin",
+    )(where, projectors, own_first, own_second, other_first, other_second)
+
+
+def finish_kernel(chips, where, projectors, done, own, other, own_rest, other_rest, out, scaled, blocks, sems):
     core, chip = where[0], where[1]
-    count = len(pieces) // 2
-    for own, parts in ((True, pieces[:count]), (False, pieces[count:])):
-        group = core if own else 1 - core
-        rows = pl.ds(pl.multiple_of(group * PCAP, PCAP), PCAP)
-        position = 0
-        for part in parts:
-            for at in range(part.shape[0]):
-                start = pl.multiple_of(chunk_of(chips, chip, group, position) * LANES, LANES)
-                scaled[rows, pl.ds(start, LANES)] = part[at]
-                position += 1
+    place(scaled, core, own_rest[2:], other_rest[2:])
     copies = []
-    for block in range(out.shape[1] // COLUMNS):
-        columns = slice(block * COLUMNS, (block + 1) * COLUMNS)
+    for block in range(projectors.shape[0] // ROW_BLOCK):
+        rows = slice(block * ROW_BLOCK, (block + 1) * ROW_BLOCK)
         slot = block % 2
         if block >= 2:
             copies[block - 2].wait()
-        blocks[slot] = jnp.dot(
-            projectors[...], scaled[:, columns], preferred_element_type=jnp.float32
-        ).astype(jnp.bfloat16)
-        copies.append(pltpu.make_async_copy(blocks.at[slot], out.at[:, columns], sems.at[slot]))
+
+        def put(group, position, sums):
+            for at in range(2):
+                start = pl.multiple_of(chunk_of(chips, chip, group, position + at) * LANES, LANES)
+                blocks[slot, :, pl.ds(start, LANES)] = sums[:, at * LANES : (at + 1) * LANES].astype(blocks.dtype)
+
+        put(core, 0, done[rows])
+        put(core, 6, jnp.dot(projectors[rows], scaled[...], preferred_element_type=jnp.float32))
+        for partial, part, group in ((own, other_rest, 1 - core), (other, own_rest, core)):
+            slots = pl.ds(pl.multiple_of(group * PCAP, PCAP), PCAP)
+            weights = jnp.concatenate([part[0], part[1]], axis=1)
+            put(
+                group,
+                4,
+                partial[rows] + jnp.dot(projectors[rows, slots], weights, preferred_element_type=jnp.float32),
+            )
+        copies.append(pltpu.make_async_copy(blocks.at[slot], out.at[rows], sems.at[slot]))
         copies[-1].start()
     for copy in copies[-2:]:
         copy.wait()
 
 
-def apply(where, projectors, pieces):
+def finish(where, projectors, done, own, other, own_rest, other_rest):
     depth, slots = projectors.shape
     chips = lax.axis_size("pw") // 2
-    width = pieces[0].shape[2]
-    bands = chips * width
-    if width != LANES:
-        count = len(pieces) // 2
-        rows = []
-        for group in range(2):
-            chunks = jnp.stack([chunk_of(chips, where[1], group, at) for at in range(chips)])
-            mine = jnp.concatenate(pieces[:count])
-            other = jnp.concatenate(pieces[count:])
-            blocks = jnp.where(where[0] == group, mine, other)
-            rows.append(jnp.zeros_like(blocks).at[chunks].set(blocks).transpose(1, 0, 2).reshape(PCAP, bands))
-        return jnp.dot(projectors, jnp.concatenate(rows), preferred_element_type=jnp.float32).astype(jnp.bfloat16)
+    bands = chips * LANES
 
     def kernel(*refs):
-        apply_kernel(chips, *refs)
+        finish_kernel(chips, *refs)
 
     return pl.pallas_call(
         kernel,
-        in_specs=[SMEM, VMEM] + [VMEM] * len(pieces),
+        in_specs=[SMEM] + [VMEM] * 6,
         out_specs=HBM,
         out_shape=jax.ShapeDtypeStruct((depth, bands), jnp.bfloat16),
         scratch_shapes=[
-            pltpu.VMEM((slots, bands), jnp.bfloat16),
-            pltpu.VMEM((2, depth, COLUMNS), jnp.bfloat16),
+            pltpu.VMEM((slots, 2 * LANES), jnp.bfloat16),
+            pltpu.VMEM((2, ROW_BLOCK, bands), jnp.bfloat16),
             pltpu.SemaphoreType.DMA((2,)),
         ],
         compiler_params=PARAMS,
         cost_estimate=pl.CostEstimate(
-            flops=2 * depth * slots * bands, bytes_accessed=2 * depth * (slots + bands), transcendentals=0
+            flops=depth * slots * bands, bytes_accessed=2 * depth * (slots + bands), transcendentals=0
         ),
-        name="apply",
-    )(where, projectors, *pieces)
+        name="finish",
+    )(where, projectors, done, own, other, own_rest, other_rest)
+
+
+def apply_plain(where, projectors, mine, other):
+    chips, _, width = mine.shape
+    rows = []
+    for group in range(2):
+        chunks = jnp.stack([chunk_of(chips, where[1], group, at) for at in range(chips)])
+        blocks = jnp.where(where[0] == group, mine, other)
+        blocks = jnp.zeros_like(blocks).at[chunks].set(blocks)
+        rows.append(blocks.transpose(1, 0, 2).reshape(PCAP, chips * width))
+    return jnp.dot(projectors, jnp.concatenate(rows), preferred_element_type=jnp.float32).astype(jnp.bfloat16)
 
 
 def local(band_coeffs, projectors, counts, atom_of, owners, couplings):
@@ -366,34 +397,41 @@
     me = lax.axis_index("pw")
     where = jnp.stack([me % 2, me // 2, me])
 
+    fast = width == LANES and stages == 3
     own_table = couplings[0]
     sibling_table = swap_cores(own_table)
-    if width == LANES:
-        theirs, ours, flipped, columns = project(where, projectors, band_coeffs, True)
+    if fast:
+        flipped = load(where, projectors)
+    else:
+        flipped = projectors
+    near, far = choose(where, owners, own_table, sibling_table, flipped)
+    far = swap_bits(far, [0, 0])
+    if fast:
+        flipped, near = lax.optimization_barrier((flipped, near))
+        theirs, ours = project(where, flipped, band_coeffs, half)
     else:
         theirs, ours = project_plain(where, projectors, band_coeffs, half)
-    near, far = choose(where, owners, own_table, sibling_table, theirs)
     theirs = swap_cores(theirs)
-    far = swap_bits(far, [0, 0])
-    if width == LANES:
-        flipped, far = lax.optimization_barrier((flipped, far))
-        low_theirs, low_ours = project(where, flipped, columns, False)
+    near = merge(near, far, ours)
+    theirs, near = lax.optimization_barrier((theirs, near))
+    far = swap_bits(near, [stages - 1] * 2)
+    message = add(ours, theirs)
+    got = swap_stage(message, 0)
+    if fast:
+        low_theirs, low_ours = project(where, flipped, band_coeffs, 0)
     else:
         low_theirs, low_ours = project_plain(where, projectors, band_coeffs, 0)
-    message = add(ours, theirs)
-    got = swap_stage(message, 0)
     low_theirs = swap_cores(low_theirs)
     allowed = mask(where, counts, atom_of, message)
     for stage in range(1, stages):
         near = merge(near, far, message)
-        far = swap_bits(near, [stages - stage] * 2)
+        got, near = lax.optimization_barrier((got, near))
+        far = swap_bits(near, [stages - 1 - stage] * 2)
         if stage == 1:
             kept, message = fold(low_ours, low_theirs, got)
         else:
             kept, message = fold(kept, got)
         got = swap_stage(message, stage)
-    near = merge(near, far, message)
-    far = swap_bits(near, [0, 0])
 
     scaled = couple(where, kept, got, allowed, near, far)
     mine = jnp.concatenate([scaled, swap_stage(scaled, stages - 1)])
@@ -408,7 +446,10 @@
         others.append(swap_cores(got))
         if stage:
             mine = jnp.concatenate([mine, got])
-    return apply(where, projectors, pieces + others)
+    if not fast:
+        return apply_plain(where, projectors, jnp.concatenate(pieces), jnp.concatenate(others))
+    begun = begin(where, projectors, *pieces[:2], *others[:2])
+    return finish(where, projectors, *begun, pieces[2], others[2])
 
 
 def solution(mesh):

time: 59.3 us -> 59.5 us (level)
  waiting for transfers between devices: 24 us -> 26.5 us
  starting transfers between devices: 19.3 us -> 17.1 us
    ppermute x10, waiting for transfers between devices: 21.1 us -> 25.2 us  [swap_bits(): lax.ppermute(x, 'pw', [(i, i ^ 2 << bits[i % 2]) for i in range(count)])]
    ppermute x10, starting transfers between devices: 18.7 us -> 16.3 us  [swap_bits(): lax.ppermute(x, 'pw', [(i, i ^ 2 << bits[i % 2]) for i in range(count)])]
    ppermute x6, waiting for transfers between devices: 2.89 us -> 1.23 us  [swap_cores(): return lax.ppermute(x, 'pw', [(i, i ^ 1) for i in range(count)])]
    pallas_call x3 -> x5, Pallas kernels: 13.4 us -> 13.2 us  [the longest x1 4.7 us: finish(): pl.pallas_call(kernel, in_specs=[SMEM] + [VMEM] * 6, out_specs=HBM, out_s...]
  transfers between devices with their start and end apart: 16 -> 16, of which waited for: 11 -> 9; matrix products, arithmetic and copies ran while one was open for 0% -> 0% of each run, Pallas kernels for 14% -> 12%
where the time goes in v5:
time: 59.5 us; the launch traced here: 59.3 us
  waiting for transfers between devices  26.5 us (45%)
  starting transfers between devices  17.1 us (29%)
  Pallas kernels  15.4 us (26%)
    ppermute x10, waiting for transfers between devices, swap_bits(): lax.ppermute(x, 'pw', [(i, i ^ 2 << bits[i % 2]) for i in range(count)])  25.2 us
    ppermute x10, starting transfers between devices, swap_bits(): lax.ppermute(x, 'pw', [(i, i ^ 2 << bits[i % 2]) for i in range(count)])  16.3 us
    pallas_call x1, Pallas kernels, finish(): pl.pallas_call(kernel, in_specs=[SMEM] + [VMEM] * 6, out_specs=HBM, out_s...  4.7 us
    pallas_call x2, Pallas kernels, project(): pl.pallas_call(kernel, in_specs=[SMEM, VMEM, VMEM], out_specs=[VMEM, VMEM...  3.88 us
    pallas_call x1, Pallas kernels, load(): pl.pallas_call(load_kernel, in_specs=[SMEM, HBM], out_specs=VMEM, out_sha...  2.69 us
    pallas_call x1, Pallas kernels, begin(): pl.pallas_call(begin_kernel, in_specs=[SMEM] + [VMEM] * 5, out_specs=[VME...  1.88 us
    ppermute x6, waiting for transfers between devices, swap_cores(): return lax.ppermute(x, 'pw', [(i, i ^ 1) for i in range(count)])  1.23 us
  transfers between devices with their start and end apart: 16, of which 9 were waited for; matrix products, arithmetic and copies ran while one was open for 0% of the time, Pallas kernels for 12%

profile of v5, /device:TPU:0, one launch (start us, length us, event | category | flops | bytes accessed | tf_op | source)
XLA Modules:
  0.0 59.3 jit_solution(15164080207415135083)
XLA Ops:
  0.0 0.5 collective-permute-start
  0.5 0.0 copy-start.2
  0.5 0.0 copy-start.5
  0.5 0.1 pad_add_fusion.where.refs_0_
  0.5 0.0 copy-start
  0.5 2.7 %load.1.after.refs_1_ = bf16[512,2048]{1,0:T(8,128)(2,1)S(1)} custom-call(s32[3]{0:T(128)S(1)} %pad_add_fusion.where.refs_0_, bf16[2048,512]{1,0:T(8,128)(2,1)} %refs_1_.1), custom_call_target="tpu_custom_call" | custom-call | tf_op jit(solution)/shard_map/load/pallas_call | solution.py:73
  3.2 0.0 collective-permute-done.sibling
  3.2 0.0 copy-done.2
  3.3 0.0 copy-done.5
  3.3 0.6 choose.1
  3.9 0.0 copy-done
  3.9 1.9 %project.3 = (bf16[4,256,128]{2,1,0:T(8,128)(2,1)S(1)}, f32[4,256,128]{2,1,0:T(8,128)S(1)}) custom-call(s32[3]{0:T(128)S(1)} %pad_add_fusion.where.refs_0_, bf16[512,2048]{1,0:T(8,128)(2,1)S(1)} %load.1.after.refs_1_, bf16[2048,1024]{1,0:T(8,128)(2,1)S(1)} %copy-done), custom_call_target="tpu_custom_call" | custom-call | flops 1073741824 | bytes 4194304 | tf_op jit(solution)/shard_map/project/pallas_call | solution.py:121
  5.8 0.1 collective-permute-start.2
  5.9 3.0 %collective-permute-start.3 = (bf16[128,256]{1,0:T(8,128)(2,1)S(1)}, bf16[128,256]{1,0:T(8,128)(2,1)S(1)}, u32[]{:S(2)}, u32[]{:S(2)}) collective-permute-start(bf16[128,256]{1,0:T(8,128)(2,1)S(1)} %get-tuple-element.39), channel_id=1, source_target_pairs={{0,2},{1,3},{2,0},{3,1},{4,6},{5,7},{6,4},{7,5},{8,10},{9,11},{10,... | collective-permute-start | bytes 196616 | tf_op jit(solution)/shard_map/ppermute | solution.py:46
  8.9 2.3 %collective-permute-done.3.right = bf16[128,256]{1,0:T(8,128)(2,1)S(1)} collective-permute-done((bf16[128,256]{1,0:T(8,128)(2,1)S(1)}, bf16[128,256]{1,0:T(8,128)(2,1)S(1)}, u32[]{:S(2)}, u32[]{:S(2)}) %collective-permute-start.3) | collective-permute-done | bytes 65568 | tf_op jit(solution)/shard_map/ppermute | solution.py:46
  11.2 0.0 collective-permute-done.2.right
  11.2 0.1 add.11.after
  11.3 2.0 %collective-permute-start.4 = (bf16[4,256,128]{2,1,0:T(8,128)(2,1)S(1)}, bf16[4,256,128]{2,1,0:T(8,128)(2,1)S(1)}, u32[]{:S(2)}, u32[]{:S(2)}) collective-permute-start(bf16[4,256,128]{2,1,0:T(8,128)(2,1)S(1)} %add.11.after), channel_id=1, source_target_pairs={{0,2},{1,5},{2,0},{3,7},{4,6},{5,1},{6,4},{7,3},{8,10},{9,13},{10,... | collective-permute-start | bytes 786440 | tf_op jit(solution)/shard_map/ppermute | solution.py:46
  13.3 2.0 %project.2 = (bf16[4,256,128]{2,1,0:T(8,128)(2,1)S(1)}, f32[4,256,128]{2,1,0:T(8,128)S(1)}) custom-call(s32[3]{0:T(128)S(1)} %pad_add_fusion.where.refs_0_, bf16[512,2048]{1,0:T(8,128)(2,1)S(1)} %load.1.after.refs_1_, bf16[2048,1024]{1,0:T(8,128)(2,1)S(1)} %copy-done), custom_call_target="tpu_custom_call" | custom-call | flops 1073741824 | bytes 4194304 | tf_op jit(solution)/shard_map/project/pallas_call | solution.py:121
  15.3 0.0 copy-start.3
  15.3 0.0 copy-start.4
  15.3 0.0 copy-start.1
  15.3 0.1 collective-permute-start.1
  15.4 2.7 %collective-permute-start.5 = (bf16[128,256]{1,0:T(8,128)(2,1)S(1)}, bf16[128,256]{1,0:T(8,128)(2,1)S(1)}, u32[]{:S(2)}, u32[]{:S(2)}) collective-permute-start(bf16[128,256]{1,0:T(8,128)(2,1)S(1)} %merge.3.left), channel_id=1, source_target_pairs={{0,8},{1,9},{2,10},{3,11},{4,12},{5,13},{6,14},{7,15},{8,0},{9,1},... | collective-permute-start | bytes 196616 | tf_op jit(solution)/shard_map/ppermute | solution.py:46
  18.1 4.1 %collective-permute-done.5.right = bf16[128,256]{1,0:T(8,128)(2,1)S(1)} collective-permute-done((bf16[128,256]{1,0:T(8,128)(2,1)S(1)}, bf16[128,256]{1,0:T(8,128)(2,1)S(1)}, u32[]{:S(2)}, u32[]{:S(2)}) %collective-permute-start.5) | collective-permute-done | bytes 65568 | tf_op jit(solution)/shard_map/ppermute | solution.py:46
  22.2 0.0 collective-permute-done.4.refs_2_
  22.2 0.0 collective-permute-done.1.refs_1_
  22.2 0.1 fold.2
  22.3 0.8 %collective-permute-start.6 = (bf16[2,256,128]{2,1,0:T(8,128)(2,1)S(1)}, bf16[2,256,128]{2,1,0:T(8,128)(2,1)S(1)}, u32[]{:S(2)}, u32[]{:S(2)}) collective-permute-start(bf16[2,256,128]{2,1,0:T(8,128)(2,1)S(1)} %get-tuple-element.44.after), channel_id=1, source_target_pairs={{0,4},{1,3},{2,6},{3,1},{4,0},{5,7},{6,2},{7,5},{8,12},{9,11},{10,... | collective-permute-start | bytes 393224 | tf_op jit(solution)/shard_map/ppermute | solution.py:46
  23.1 1.3 %collective-permute-start.7 = (bf16[128,256]{1,0:T(8,128)(2,1)S(1)}, bf16[128,256]{1,0:T(8,128)(2,1)S(1)}, u32[]{:S(2)}, u32[]{:S(2)}) collective-permute-start(bf16[128,256]{1,0:T(8,128)(2,1)S(1)} %merge.4.left), channel_id=1, source_target_pairs={{0,4},{1,5},{2,6},{3,7},{4,0},{5,1},{6,2},{7,3},{8,12},{9,13},{10,... | collective-permute-start | bytes 196616 | tf_op jit(solution)/shard_map/ppermute | solution.py:46
  24.4 3.6 %collective-permute-done.7.right = bf16[128,256]{1,0:T(8,128)(2,1)S(1)} collective-permute-done((bf16[128,256]{1,0:T(8,128)(2,1)S(1)}, bf16[128,256]{1,0:T(8,128)(2,1)S(1)}, u32[]{:S(2)}, u32[]{:S(2)}) %collective-permute-start.7) | collective-permute-done | bytes 65568 | tf_op jit(solution)/shard_map/ppermute | solution.py:46
  28.1 0.0 collective-permute-done.6.refs_1_
  28.1 2.7 %collective-permute-start.8 = (bf16[1,256,128]{2,1,0:T(8,128)(2,1)S(1)}, bf16[1,256,128]{2,1,0:T(8,128)(2,1)S(1)}, u32[]{:S(2)}, u32[]{:S(2)}) collective-permute-start(bf16[1,256,128]{2,1,0:T(8,128)(2,1)S(1)} %get-tuple-element.48), channel_id=1, source_target_pairs={{0,8},{1,9},{2,10},{3,11},{4,12},{5,13},{6,14},{7,15},{8,0},{9,1},... | collective-permute-start | bytes 196616 | tf_op jit(solution)/shard_map/ppermute | solution.py:46
  30.9 0.6 %collective-permute-start.9 = (bf16[128,256]{1,0:T(8,128)(2,1)S(1)}, bf16[128,256]{1,0:T(8,128)(2,1)S(1)}, u32[]{:S(2)}, u32[]{:S(2)}) collective-permute-start(bf16[128,256]{1,0:T(8,128)(2,1)S(1)} %merge.5.near), channel_id=1, source_target_pairs={{0,2},{1,3},{2,0},{3,1},{4,6},{5,7},{6,4},{7,5},{8,10},{9,11},{10,... | collective-permute-start | bytes 196616 | tf_op jit(solution)/shard_map/ppermute | solution.py:46
  31.4 0.0 copy-done.3
  31.5 0.0 copy-done.4
  31.5 0.7 %mask.1.allowed = bf16[256,256]{1,0:T(8,128)(2,1)S(1)} custom-call(s32[3]{0:T(128)S(1)} %pad_add_fusion.where.refs_0_, s32[2,4]{1,0:T(2,128)S(1)} %copy-done.4, s32[2,256]{1,0:T(2,128)S(1)} %copy-done.3, bf16[4,256,128]{2,1,0:T(8,128)(2,1)S(1)} %add.11.after), custom_call_target="tpu_custom_call" | custom-call | tf_op jit(solution)/shard_map/mask/pallas_call | solution.py:248
  32.1 1.2 %collective-permute-done.8.got = bf16[1,256,128]{2,1,0:T(8,128)(2,1)S(1)} collective-permute-done((bf16[1,256,128]{2,1,0:T(8,128)(2,1)S(1)}, bf16[1,256,128]{2,1,0:T(8,128)(2,1)S(1)}, u32[]{:S(2)}, u32[]{:S(2)}) %collective-permute-start.8) | collective-permute-done | bytes 65568 | tf_op jit(solution)/shard_map/ppermute | solution.py:46
  33.4 1.8 %collective-permute-done.9.far = bf16[128,256]{1,0:T(8,128)(2,1)S(1)} collective-permute-done((bf16[128,256]{1,0:T(8,128)(2,1)S(1)}, bf16[128,256]{1,0:T(8,128)(2,1)S(1)}, u32[]{:S(2)}, u32[]{:S(2)}) %collective-permute-start.9) | collective-permute-done | bytes 65568 | tf_op jit(solution)/shard_map/ppermute | solution.py:46
  35.1 0.7 %couple.1 = bf16[1,256,128]{2,1,0:T(8,128)(2,1)S(1)} custom-call(s32[3]{0:T(128)S(1)} %pad_add_fusion.where.refs_0_, f32[1,256,128]{2,1,0:T(8,128)S(1)} %get-tuple-element.47.kept, bf16[1,256,128]{2,1,0:T(8,128)(2,1)S(1)} %collective-permute-done.8.got, bf16[256,256]{1,0:T(8,128)(2,1)S(1)} %mask.1.allowed, bf16[128,256]{1,0:T(8,128)(2,1)S(1)} %merge.5.near, ...), custom_call_target="tpu_custom_call" | custom-call | tf_op jit(solution)/shard_map/couple/pallas_call | solution.py:273
  35.9 1.1 %collective-permute-start.10 = (bf16[1,256,128]{2,1,0:T(8,128)(2,1)S(1)}, bf16[1,256,128]{2,1,0:T(8,128)(2,1)S(1)}, u32[]{:S(2)}, u32[]{:S(2)}) collective-permute-start(bf16[1,256,128]{2,1,0:T(8,128)(2,1)S(1)} %couple.1), channel_id=1, source_target_pairs={{0,8},{1,9},{2,10},{3,11},{4,12},{5,13},{6,14},{7,15},{8,0},{9,1},... | collective-permute-start | bytes 196616 | tf_op jit(solution)/shard_map/ppermute | solution.py:46
  36.9 4.2 %collective-permute-done.10 = bf16[1,256,128]{2,1,0:T(8,128)(2,1)S(1)} collective-permute-done((bf16[1,256,128]{2,1,0:T(8,128)(2,1)S(1)}, bf16[1,256,128]{2,1,0:T(8,128)(2,1)S(1)}, u32[]{:S(2)}, u32[]{:S(2)}) %collective-permute-start.10) | collective-permute-done | bytes 65568 | tf_op jit(solution)/shard_map/ppermute | solution.py:46
  41.1 0.1 collective-permute-start.12
  41.2 1.5 %collective-permute-start.11 = (bf16[2,256,128]{2,1,0:T(8,128)(2,1)S(1)}, bf16[2,256,128]{2,1,0:T(8,128)(2,1)S(1)}, u32[]{:S(2)}, u32[]{:S(2)}) collective-permute-start(bf16[2,256,128]{2,1,0:T(8,128)(2,1)S(1)} %pad_maximum_fusion.1.own_first), channel_id=1, source_target_pairs={{0,4},{1,3},{2,6},{3,1},{4,0},{5,7},{6,2},{7,5},{8,12},{9,11},{10,... | collective-permute-start | bytes 393224 | tf_op jit(solution)/shard_map/ppermute | solution.py:46
  42.7 0.0 collective-permute-done.12.other_first
  42.7 3.5 %collective-permute-done.11.own_second = bf16[2,256,128]{2,1,0:T(8,128)(2,1)S(1)} collective-permute-done((bf16[2,256,128]{2,1,0:T(8,128)(2,1)S(1)}, bf16[2,256,128]{2,1,0:T(8,128)(2,1)S(1)}, u32[]{:S(2)}, u32[]{:S(2)}) %collective-permute-start.11) | collective-permute-done | bytes 131104 | tf_op jit(solution)/shard_map/ppermute | solution.py:46
  46.3 0.7 %collective-permute-start.13 = (bf16[4,256,128]{2,1,0:T(8,128)(2,1)S(1)}, bf16[4,256,128]{2,1,0:T(8,128)(2,1)S(1)}, u32[]{:S(2)}, u32[]{:S(2)}) collective-permute-start(bf16[4,256,128]{2,1,0:T(8,128)(2,1)S(1)} %pad_maximum_fusion), channel_id=1, source_target_pairs={{0,2},{1,5},{2,0},{3,7},{4,6},{5,1},{6,4},{7,3},{8,10},{9,13},{10,... | collective-permute-start | bytes 786440 | tf_op jit(solution)/shard_map/ppermute | solution.py:46
  46.9 0.1 collective-permute-start.14
  47.1 1.2 %collective-permute-done.14.other_second = bf16[2,256,128]{2,1,0:T(8,128)(2,1)S(1)} collective-permute-done((bf16[2,256,128]{2,1,0:T(8,128)(2,1)S(1)}, bf16[2,256,128]{2,1,0:T(8,128)(2,1)S(1)}, u32[]{:S(2)}, u32[]{:S(2)}) %collective-permute-start.14) | collective-permute-done | bytes 131104 | tf_op jit(solution)/shard_map/ppermute | solution.py:41
  48.3 4.4 %collective-permute-done.13.refs_5_ = bf16[4,256,128]{2,1,0:T(8,128)(2,1)S(1)} collective-permute-done((bf16[4,256,128]{2,1,0:T(8,128)(2,1)S(1)}, bf16[4,256,128]{2,1,0:T(8,128)(2,1)S(1)}, u32[]{:S(2)}, u32[]{:S(2)}) %collective-permute-start.13) | collective-permute-done | bytes 262176 | tf_op jit(solution)/shard_map/ppermute | solution.py:46
  52.7 0.0 collective-permute-start.15
  52.7 0.0 copy-done.1
  52.7 1.9 %begin.1 = (bf16[2048,256]{1,0:T(8,128)(2,1)S(1)}, f32[2048,256]{1,0:T(8,128)S(1)}, f32[2048,256]{1,0:T(8,128)S(1)}) custom-call(s32[3]{0:T(128)S(1)} %pad_add_fusion.where.refs_0_, bf16[2048,512]{1,0:T(8,128)(2,1)S(1)} %copy-done.1, bf16[2,256,128]{2,1,0:T(8,128)(2,1)S(1)} %pad_maximum_fusion.1.own_first, ...), custom_call_target="tpu_custom_call" | custom-call | flops 1073741824 | bytes 2097152 | tf_op jit(solution)/shard_map/begin/pallas_call | solution.py:306
  54.6 0.0 collective-permute-done.15.refs_6_
  54.6 4.7 %finish.1 = bf16[2048,1024]{1,0:T(8,128)(2,1)} custom-call(s32[3]{0:T(128)S(1)} %pad_add_fusion.where.refs_0_, bf16[2048,512]{1,0:T(8,128)(2,1)S(1)} %copy-done.1, bf16[2048,256]{1,0:T(8,128)(2,1)S(1)} %get-tuple-element.55.refs_2_, f32[2048,256]{1,0:T(8,128)S(1)} %get-tuple-element.56.refs_3_, f32[2048,256]{1,0:T(8,128)S(1)} %get-tuple-element.57.refs_4_, ...), custom_call_target="tpu_custom_call" | custom-call | flops 1073741824 | bytes 6291456 | tf_op jit(solution)/shard_map/finish/pallas_call | solution.py:363
  (6 shorter events, 0.1 us)
Async XLA Ops:
  0.0 3.2 %collective-permute-start = (f32[256,256]{1,0:T(8,128)}, f32[256,256]{1,0:T(8,128)S(1)}, u32[]{:S(2)}, u32[]{:S(2)}) collective-permute-start(f32[256,256]{1,0:T(8,128)} %bitcast.4), channel_id=1, source_target_pairs={{0,1},{1,0},{2,3},{3,2},{4,5},{5,4},{6,7},{7,6},{8,9},{9,8},{10,11... | collective-permute-start | bytes 786440 | tf_op jit(solution)/shard_map/ppermute | solution.py:41
  0.5 2.8 %copy-start.2 = (f32[1,256,256]{2,1,0:T(8,128)S(1)}, f32[1,256,256]{2,1,0:T(8,128)}, u32[]{:S(2)}) copy-start(f32[1,256,256]{2,1,0:T(8,128)} %param.11) | copy-start | bytes 786436
  0.5 2.8 %copy-start.5 = (s32[2]{0:T(128)S(1)}, s32[2]{0:T(128)}, u32[]{:S(2)}) copy-start(s32[2]{0:T(128)} %owners.1) | copy-start | bytes 28
  0.5 3.3 %copy-start = (bf16[2048,1024]{1,0:T(8,128)(2,1)S(1)}, bf16[2048,1024]{1,0:T(8,128)(2,1)}, u32[]{:S(2)}) copy-start(bf16[2048,1024]{1,0:T(8,128)(2,1)} %refs_2_.3) | copy-start | bytes 12582916
  5.8 5.4 %collective-permute-start.2 = (bf16[4,256,128]{2,1,0:T(8,128)(2,1)S(1)}, bf16[4,256,128]{2,1,0:T(8,128)(2,1)S(1)}, u32[]{:S(2)}, u32[]{:S(2)}) collective-permute-start(bf16[4,256,128]{2,1,0:T(8,128)(2,1)S(1)} %get-tuple-element.37), channel_id=1, source_target_pairs={{0,1},{1,0},{2,3},{3,2},{4,5},{5,4},{6,7},{7,6},{8,9},{9,8},{10,11... | collective-permute-start | bytes 786440 | tf_op jit(solution)/shard_map/ppermute | solution.py:41
  5.9 5.3 %collective-permute-start.3 = (bf16[128,256]{1,0:T(8,128)(2,1)S(1)}, bf16[128,256]{1,0:T(8,128)(2,1)S(1)}, u32[]{:S(2)}, u32[]{:S(2)}) collective-permute-start(bf16[128,256]{1,0:T(8,128)(2,1)S(1)} %get-tuple-element.39), channel_id=1, source_target_pairs={{0,2},{1,3},{2,0},{3,1},{4,6},{5,7},{6,4},{7,5},{8,10},{9,11},{10,... | collective-permute-start | bytes 196616 | tf_op jit(solution)/shard_map/ppermute | solution.py:46
  11.3 10.9 %collective-permute-start.4 = (bf16[4,256,128]{2,1,0:T(8,128)(2,1)S(1)}, bf16[4,256,128]{2,1,0:T(8,128)(2,1)S(1)}, u32[]{:S(2)}, u32[]{:S(2)}) collective-permute-start(bf16[4,256,128]{2,1,0:T(8,128)(2,1)S(1)} %add.11.after), channel_id=1, source_target_pairs={{0,2},{1,5},{2,0},{3,7},{4,6},{5,1},{6,4},{7,3},{8,10},{9,13},{10,... | collective-permute-start | bytes 786440 | tf_op jit(solution)/shard_map/ppermute | solution.py:46
  15.3 16.2 %copy-start.3 = (s32[2,256]{1,0:T(2,128)S(1)}, s32[2,256]{1,0:T(2,128)}, u32[]{:S(2)}) copy-start(s32[2,256]{1,0:T(2,128)} %atom_of.1) | copy-start | bytes 6148
  15.3 16.2 %copy-start.4 = (s32[2,4]{1,0:T(2,128)S(1)}, s32[2,4]{1,0:T(2,128)}, u32[]{:S(2)}) copy-start(s32[2,4]{1,0:T(2,128)} %counts.1) | copy-start | bytes 100
  15.3 37.4 %copy-start.1 = (bf16[2048,512]{1,0:T(8,128)(2,1)S(1)}, bf16[2048,512]{1,0:T(8,128)(2,1)}, u32[]{:S(2)}) copy-start(bf16[2048,512]{1,0:T(8,128)(2,1)} %refs_1_.1) | copy-start | bytes 6291460
  15.3 6.9 %collective-permute-start.1 = (bf16[4,256,128]{2,1,0:T(8,128)(2,1)S(1)}, bf16[4,256,128]{2,1,0:T(8,128)(2,1)S(1)}, u32[]{:S(2)}, u32[]{:S(2)}) collective-permute-start(bf16[4,256,128]{2,1,0:T(8,128)(2,1)S(1)} %get-tuple-element.35), channel_id=1, source_target_pairs={{0,1},{1,0},{2,3},{3,2},{4,5},{5,4},{6,7},{7,6},{8,9},{9,8},{10,11... | collective-permute-start | bytes 786440 | tf_op jit(solution)/shard_map/ppermute | solution.py:41
  15.4 6.8 %collective-permute-start.5 = (bf16[128,256]{1,0:T(8,128)(2,1)S(1)}, bf16[128,256]{1,0:T(8,128)(2,1)S(1)}, u32[]{:S(2)}, u32[]{:S(2)}) collective-permute-start(bf16[128,256]{1,0:T(8,128)(2,1)S(1)} %merge.3.left), channel_id=1, source_target_pairs={{0,8},{1,9},{2,10},{3,11},{4,12},{5,13},{6,14},{7,15},{8,0},{9,1},... | collective-permute-start | bytes 196616 | tf_op jit(solution)/shard_map/ppermute | solution.py:46
  22.3 5.8 %collective-permute-start.6 = (bf16[2,256,128]{2,1,0:T(8,128)(2,1)S(1)}, bf16[2,256,128]{2,1,0:T(8,128)(2,1)S(1)}, u32[]{:S(2)}, u32[]{:S(2)}) collective-permute-start(bf16[2,256,128]{2,1,0:T(8,128)(2,1)S(1)} %get-tuple-element.44.after), channel_id=1, source_target_pairs={{0,4},{1,3},{2,6},{3,1},{4,0},{5,7},{6,2},{7,5},{8,12},{9,11},{10,... | collective-permute-start | bytes 393224 | tf_op jit(solution)/shard_map/ppermute | solution.py:46
  23.1 5.0 %collective-permute-start.7 = (bf16[128,256]{1,0:T(8,128)(2,1)S(1)}, bf16[128,256]{1,0:T(8,128)(2,1)S(1)}, u32[]{:S(2)}, u32[]{:S(2)}) collective-permute-start(bf16[128,256]{1,0:T(8,128)(2,1)S(1)} %merge.4.left), channel_id=1, source_target_pairs={{0,4},{1,5},{2,6},{3,7},{4,0},{5,1},{6,2},{7,3},{8,12},{9,13},{10,... | collective-permute-start | bytes 196616 | tf_op jit(solution)/shard_map/ppermute | solution.py:46
  28.1 5.2 %collective-permute-start.8 = (bf16[1,256,128]{2,1,0:T(8,128)(2,1)S(1)}, bf16[1,256,128]{2,1,0:T(8,128)(2,1)S(1)}, u32[]{:S(2)}, u32[]{:S(2)}) collective-permute-start(bf16[1,256,128]{2,1,0:T(8,128)(2,1)S(1)} %get-tuple-element.48), channel_id=1, source_target_pairs={{0,8},{1,9},{2,10},{3,11},{4,12},{5,13},{6,14},{7,15},{8,0},{9,1},... | collective-permute-start | bytes 196616 | tf_op jit(solution)/shard_map/ppermute | solution.py:46
  30.9 4.3 %collective-permute-start.9 = (bf16[128,256]{1,0:T(8,128)(2,1)S(1)}, bf16[128,256]{1,0:T(8,128)(2,1)S(1)}, u32[]{:S(2)}, u32[]{:S(2)}) collective-permute-start(bf16[128,256]{1,0:T(8,128)(2,1)S(1)} %merge.5.near), channel_id=1, source_target_pairs={{0,2},{1,3},{2,0},{3,1},{4,6},{5,7},{6,4},{7,5},{8,10},{9,11},{10,... | collective-permute-start | bytes 196616 | tf_op jit(solution)/shard_map/ppermute | solution.py:46
  35.9 5.2 %collective-permute-start.10 = (bf16[1,256,128]{2,1,0:T(8,128)(2,1)S(1)}, bf16[1,256,128]{2,1,0:T(8,128)(2,1)S(1)}, u32[]{:S(2)}, u32[]{:S(2)}) collective-permute-start(bf16[1,256,128]{2,1,0:T(8,128)(2,1)S(1)} %couple.1), channel_id=1, source_target_pairs={{0,8},{1,9},{2,10},{3,11},{4,12},{5,13},{6,14},{7,15},{8,0},{9,1},... | collective-permute-start | bytes 196616 | tf_op jit(solution)/shard_map/ppermute | solution.py:46
  41.1 1.6 %collective-permute-start.12 = (bf16[2,256,128]{2,1,0:T(8,128)(2,1)S(1)}, bf16[2,256,128]{2,1,0:T(8,128)(2,1)S(1)}, u32[]{:S(2)}, u32[]{:S(2)}) collective-permute-start(bf16[2,256,128]{2,1,0:T(8,128)(2,1)S(1)} %pad_maximum_fusion.1.own_first), channel_id=1, source_target_pairs={{0,1},{1,0},{2,3},{3,2},{4,5},{5,4},{6,7},{7,6},{8,9},{9,8},{10,11... | collective-permute-start | bytes 393224 | tf_op jit(solution)/shard_map/ppermute | solution.py:41
  41.2 5.0 %collective-permute-start.11 = (bf16[2,256,128]{2,1,0:T(8,128)(2,1)S(1)}, bf16[2,256,128]{2,1,0:T(8,128)(2,1)S(1)}, u32[]{:S(2)}, u32[]{:S(2)}) collective-permute-start(bf16[2,256,128]{2,1,0:T(8,128)(2,1)S(1)} %pad_maximum_fusion.1.own_first), channel_id=1, source_target_pairs={{0,4},{1,3},{2,6},{3,1},{4,0},{5,7},{6,2},{7,5},{8,12},{9,11},{10,... | collective-permute-start | bytes 393224 | tf_op jit(solution)/shard_map/ppermute | solution.py:46
  46.3 6.4 %collective-permute-start.13 = (bf16[4,256,128]{2,1,0:T(8,128)(2,1)S(1)}, bf16[4,256,128]{2,1,0:T(8,128)(2,1)S(1)}, u32[]{:S(2)}, u32[]{:S(2)}) collective-permute-start(bf16[4,256,128]{2,1,0:T(8,128)(2,1)S(1)} %pad_maximum_fusion), channel_id=1, source_target_pairs={{0,2},{1,5},{2,0},{3,7},{4,6},{5,1},{6,4},{7,3},{8,10},{9,13},{10,... | collective-permute-start | bytes 786440 | tf_op jit(solution)/shard_map/ppermute | solution.py:46
  46.9 1.3 %collective-permute-start.14 = (bf16[2,256,128]{2,1,0:T(8,128)(2,1)S(1)}, bf16[2,256,128]{2,1,0:T(8,128)(2,1)S(1)}, u32[]{:S(2)}, u32[]{:S(2)}) collective-permute-start(bf16[2,256,128]{2,1,0:T(8,128)(2,1)S(1)} %collective-permute-done.11.own_second), channel_id=1, source_target_pairs={{0,1},{1,0},{2,3},{3,2},{4,5},{5,4},{6,7},{7,6},{8,9},{9,8},{10,11... | collective-permute-start | bytes 393224 | tf_op jit(solution)/shard_map/ppermute | solution.py:41
  52.7 1.9 %collective-permute-start.15 = (bf16[4,256,128]{2,1,0:T(8,128)(2,1)S(1)}, bf16[4,256,128]{2,1,0:T(8,128)(2,1)S(1)}, u32[]{:S(2)}, u32[]{:S(2)}) collective-permute-start(bf16[4,256,128]{2,1,0:T(8,128)(2,1)S(1)} %collective-permute-done.13.refs_5_), channel_id=1, source_target_pairs={{0,1},{1,0},{2,3},{3,2},{4,5},{5,4},{6,7},{7,6},{8,9},{9,8},{10,11... | collective-permute-start | bytes 786440 | tf_op jit(solution)/shard_map/ppermute | solution.py:41

commit v6 on v5

--- a/solution.py
+++ b/solution.py
@@ -10,6 +10,7 @@
 PCAP = 256
 LANES = 128
 ROW_BLOCK = 512
+COPY_ROWS = 128
 PARAMS = pltpu.CompilerParams(vmem_limit_bytes=32 * 1024 * 1024)
 VMEM = pl.BlockSpec(memory_space=pltpu.VMEM)
 SMEM = pl.BlockSpec(memory_space=pltpu.SMEM)
@@ -192,20 +193,43 @@
     )(left, right)
 
 
-def choose_kernel(where, owners, own, sibling, after, kept, sent):
+def halve_kernel(where, table, kept, sent, rows, sems):
+    half = PCAP // 2
+    side = where[1] & 1
+    copies = []
+    for at, which in enumerate((1 - side, side)):
+        start = pl.multiple_of(which * half, half)
+        copies.append(pltpu.make_async_copy(table.at[0, pl.ds(start, half)], rows.at[at], sems.at[at]))
+        copies[-1].start()
+    for at, out in enumerate((sent, kept)):
+        copies[at].wait()
+        out[...] = rows[at].astype(out.dtype)
+
+
+def halve(where, couplings):
+    half = PCAP // 2
+    shape = jax.ShapeDtypeStruct((half, PCAP), jnp.bfloat16)
+    return pl.pallas_call(
+        halve_kernel,
+        in_specs=[SMEM, HBM],
+        out_specs=[VMEM, VMEM],
+        out_shape=[shape, shape],
+        scratch_shapes=[pltpu.VMEM((2, half, PCAP), jnp.float32), pltpu.SemaphoreType.DMA((2,))],
+        compiler_params=PARAMS,
+        name="halve",
+    )(where, pltpu.with_memory_space_constraint(couplings, pltpu.HBM))
+
+
+def choose_kernel(where, owners, kept, got, after, near, sent):
     del after
-    core, chip, me = where[0], where[1], where[2]
-    owner = jnp.where(core == 0, owners[0], owners[1])
-    half = PCAP // 2
-    side = chip & 1
-    for out, which in ((kept, side), (sent, 1 - side)):
-        rows = pl.ds(pl.multiple_of(which * half, half), half)
-        part = jnp.where(owner == me, own[rows], jnp.where(owner == (me ^ 1), sibling[rows], 0.0))
-        out[...] = part.astype(out.dtype)
-
-
-def choose(where, owners, own, sibling, after):
-    shape = jax.ShapeDtypeStruct((PCAP // 2, PCAP), jnp.bfloat16)
+    core, me = where[0], where[2]
+    for out, group in ((near, core), (sent, 1 - core)):
+        owner = jnp.where(group == 0, owners[0], owners[1])
+        out[...] = jnp.where(owner == me, kept[...], jnp.where(owner == (me ^ 2), got[...], jnp.zeros_like(got)))
+
+
+def choose(where, owners, kept, got, after):
+    shape = jax.ShapeDtypeStruct(kept.shape, kept.dtype)
     return pl.pallas_call(
         choose_kernel,
         in_specs=[SMEM, SMEM, VMEM, VMEM, ANY],
@@ -213,7 +237,7 @@
         out_shape=[shape, shape],
         compiler_params=PARAMS,
         name="choose",
-    )(where, owners, own, sibling, after)
+    )(where, owners, kept, got, after)
 
 
 def merge_kernel(left, right, after, out):
@@ -288,67 +312,89 @@
         scaled[rows, LANES:] = part[1]
 
 
-def begin_kernel(where, projectors, own_first, own_second, other_first, other_second, done, own, other, scaled):
-    core = where[0]
-    place(scaled, core, own_first[...], other_first[...])
-    for block in range(projectors.shape[0] // ROW_BLOCK):
-        rows = slice(block * ROW_BLOCK, (block + 1) * ROW_BLOCK)
-        done[rows] = jnp.dot(projectors[rows], scaled[...], preferred_element_type=jnp.float32).astype(done.dtype)
-        for out, part, group in ((own, own_second, core), (other, other_second, 1 - core)):
-            slots = pl.ds(pl.multiple_of(group * PCAP, PCAP), PCAP)
-            weights = jnp.concatenate([part[0], part[1]], axis=1)
+def begin_kernel(where, projectors, own, first, second, held):
+    slots = pl.ds(pl.multiple_of(where[0] * PCAP, PCAP), PCAP)
+    held[...] = own[...]
+    for out, at in ((first, 0), (second, 2)):
+        weights = jnp.concatenate([own[at], own[at + 1]], axis=1)
+        for block in range(projectors.shape[0] // ROW_BLOCK):
+            rows = slice(block * ROW_BLOCK, (block + 1) * ROW_BLOCK)
             out[rows] = jnp.dot(projectors[rows, slots], weights, preferred_element_type=jnp.float32)
 
 
-def begin(where, projectors, own_first, own_second, other_first, other_second):
+def begin(where, projectors, own):
+    depth, slots = projectors.shape
+    shape = jax.ShapeDtypeStruct((depth, 2 * LANES), jnp.float32)
+
+    return pl.pallas_call(
+        begin_kernel,
+        in_specs=[SMEM, VMEM, VMEM],
+        out_specs=[VMEM] * 3,
+        out_shape=[shape, shape, jax.ShapeDtypeStruct(own.shape, own.dtype)],
+        compiler_params=PARAMS,
+        cost_estimate=pl.CostEstimate(
+            flops=4 * depth * slots * LANES, bytes_accessed=2 * depth * slots, transcendentals=0
+        ),
+        name="begin",
+    )(where, projectors, own)
+
+
+def extend_kernel(where, projectors, partial, other, done, second):
+    slots = pl.ds(pl.multiple_of((1 - where[0]) * PCAP, PCAP), PCAP)
+    for out, at in ((done, 0), (second, 2)):
+        weights = jnp.concatenate([other[at], other[at + 1]], axis=1)
+        for block in range(projectors.shape[0] // ROW_BLOCK):
+            rows = slice(block * ROW_BLOCK, (block + 1) * ROW_BLOCK)
+            sums = jnp.dot(projectors[rows, slots], weights, preferred_element_type=jnp.float32)
+            if at == 0:
+                sums = sums + partial[rows]
+            out[rows] = sums.astype(out.dtype)
+
+
+def extend(where, projectors, partial, other):
     depth, slots = projectors.shape
     pair = 2 * LANES
     return pl.pallas_call(
-        begin_kernel,
-        in_specs=[SMEM] + [VMEM] * 5,
-        out_specs=[VMEM] * 3,
+        extend_kernel,
+        in_specs=[SMEM, VMEM, VMEM, VMEM],
+        out_specs=[VMEM] * 2,
         out_shape=[
             jax.ShapeDtypeStruct((depth, pair), jnp.bfloat16),
             jax.ShapeDtypeStruct((depth, pair), jnp.float32),
-            jax.ShapeDtypeStruct((depth, pair), jnp.float32),
         ],
-        scratch_shapes=[pltpu.VMEM((slots, pair), jnp.bfloat16)],
         compiler_params=PARAMS,
         cost_estimate=pl.CostEstimate(
-            flops=4 * depth * slots * pair, bytes_accessed=2 * depth * slots, transcendentals=0
+            flops=4 * depth * slots * LANES, bytes_accessed=2 * depth * slots, transcendentals=0
         ),
-        name="begin",
-    )(where, projectors, own_first, own_second, other_first, other_second)
+        name="extend",
+    )(where, projectors, partial, other)
 
 
 def finish_kernel(chips, where, projectors, done, own, other, own_rest, other_rest, out, scaled, blocks, sems):
     core, chip = where[0], where[1]
     place(scaled, core, own_rest[2:], other_rest[2:])
     copies = []
+
+    def put(rows, group, position, sums):
+        for at in range(2):
+            start = pl.multiple_of(chunk_of(chips, chip, group, position + at) * LANES, LANES)
+            blocks[rows, pl.ds(start, LANES)] = sums[:, at * LANES : (at + 1) * LANES].astype(blocks.dtype)
+
     for block in range(projectors.shape[0] // ROW_BLOCK):
         rows = slice(block * ROW_BLOCK, (block + 1) * ROW_BLOCK)
-        slot = block % 2
-        if block >= 2:
-            copies[block - 2].wait()
-
-        def put(group, position, sums):
-            for at in range(2):
-                start = pl.multiple_of(chunk_of(chips, chip, group, position + at) * LANES, LANES)
-                blocks[slot, :, pl.ds(start, LANES)] = sums[:, at * LANES : (at + 1) * LANES].astype(blocks.dtype)
-
-        put(core, 0, done[rows])
-        put(core, 6, jnp.dot(projectors[rows], scaled[...], preferred_element_type=jnp.float32))
+        put(rows, core, 0, done[rows])
+        put(rows, core, 6, jnp.dot(projectors[rows], scaled[...], preferred_element_type=jnp.float32))
         for partial, part, group in ((own, other_rest, 1 - core), (other, own_rest, core)):
             slots = pl.ds(pl.multiple_of(group * PCAP, PCAP), PCAP)
             weights = jnp.concatenate([part[0], part[1]], axis=1)
-            put(
-                group,
-                4,
-                partial[rows] + jnp.dot(projectors[rows, slots], weights, preferred_element_type=jnp.float32),
-            )
-        copies.append(pltpu.make_async_copy(blocks.at[slot], out.at[rows], sems.at[slot]))
-        copies[-1].start()
-    for copy in copies[-2:]:
+            sums = jnp.dot(projectors[rows, slots], weights, preferred_element_type=jnp.float32)
+            put(rows, group, 4, partial[rows] + sums)
+        for piece in range(ROW_BLOCK // COPY_ROWS):
+            start = block * ROW_BLOCK + piece * COPY_ROWS
+            written = slice(start, start + COPY_ROWS)
+            copies.append(pltpu.make_async_copy(blocks.at[written], out.at[written], sems.at[len(copies)]))
+            copies[-1].start()
+    for copy in copies:
         copy.wait()
 
 
@@ -367,8 +413,8 @@
         out_shape=jax.ShapeDtypeStruct((depth, bands), jnp.bfloat16),
         scratch_shapes=[
             pltpu.VMEM((slots, 2 * LANES), jnp.bfloat16),
-            pltpu.VMEM((2, ROW_BLOCK, bands), jnp.bfloat16),
-            pltpu.SemaphoreType.DMA((2,)),
+            pltpu.VMEM((depth, bands), jnp.bfloat16),
+            pltpu.SemaphoreType.DMA((depth // COPY_ROWS,)),
         ],
         compiler_params=PARAMS,
         cost_estimate=pl.CostEstimate(
@@ -398,58 +444,54 @@
     where = jnp.stack([me % 2, me // 2, me])
 
     fast = width == LANES and stages == 3
-    own_table = couplings[0]
-    sibling_table = swap_cores(own_table)
+    kept, sent = halve(where, couplings)
+    early, sent = lax.optimization_barrier((projectors, sent))
+    got = swap_bits(sent, [0, 0])
     if fast:
-        flipped = load(where, projectors)
-    else:
-        flipped = projectors
-    near, far = choose(where, owners, own_table, sibling_table, flipped)
-    far = swap_bits(far, [0, 0])
-    if fast:
-        flipped, near = lax.optimization_barrier((flipped, near))
+        flipped = load(where, early)
+        flipped, got = lax.optimization_barrier((flipped, got))
         theirs, ours = project(where, flipped, band_coeffs, half)
     else:
         theirs, ours = project_plain(where, projectors, band_coeffs, half)
+    near, far = choose(where, owners, kept, got, ours)
     theirs = swap_cores(theirs)
-    near = merge(near, far, ours)
-    theirs, near = lax.optimization_barrier((theirs, near))
+    far = swap_cores(far)
+    message = add(ours, theirs)
+    near = merge(near, far, message)
+    got = swap_stage(message, 0)
     far = swap_bits(near, [stages - 1] * 2)
-    message = add(ours, theirs)
-    got = swap_stage(message, 0)
     if fast:
+        flipped, near = lax.optimization_barrier((flipped, near))
         low_theirs, low_ours = project(where, flipped, band_coeffs, 0)
     else:
         low_theirs, low_ours = project_plain(where, projectors, band_coeffs, 0)
+    near = merge(near, far, message)
+    low_theirs, near = lax.optimization_barrier((low_theirs, near))
     low_theirs = swap_cores(low_theirs)
     allowed = mask(where, counts, atom_of, message)
     for stage in range(1, stages):
-        near = merge(near, far, message)
-        got, near = lax.optimization_barrier((got, near))
         far = swap_bits(near, [stages - 1 - stage] * 2)
         if stage == 1:
             kept, message = fold(low_ours, low_theirs, got)
         else:
             kept, message = fold(kept, got)
         got = swap_stage(message, stage)
+        if stage < stages - 1:
+            near = merge(near, far, message)
+            got, near = lax.optimization_barrier((got, near))
 
     scaled = couple(where, kept, got, allowed, near, far)
     mine = jnp.concatenate([scaled, swap_stage(scaled, stages - 1)])
-    pieces = [mine]
-    others = [swap_cores(mine)]
-    for stage in range(stages - 2, -1, -1):
-        if stage < stages - 2:
-            mine, others[0] = lax.optimization_barrier((mine, others[0]))
-        got = swap_stage(mine, stage)
-        got, others[-1] = lax.optimization_barrier((got, others[-1]))
-        pieces.append(got)
-        others.append(swap_cores(got))
-        if stage:
-            mine = jnp.concatenate([mine, got])
+    for stage in range(stages - 2, 0, -1):
+        mine = jnp.concatenate([mine, swap_stage(mine, stage)])
+    got = swap_stage(mine, 0)
     if not fast:
-        return apply_plain(where, projectors, jnp.concatenate(pieces), jnp.concatenate(others))
-    begun = begin(where, projectors, *pieces[:2], *others[:2])
-    return finish(where, projectors, *begun, pieces[2], others[2])
+        mine = jnp.concatenate([mine, got])
+        return apply_plain(where, projectors, mine, swap_cores(mine))
+    first, own, held = begin(where, projectors, mine)
+    done, other = extend(where, projectors, first, swap_cores(held))
+    got, done = lax.optimization_barrier((got, done))
+    return finish(where, projectors, done, own, other, got, swap_cores(got))
 
 
 def solution(mesh):

time: 59.5 us -> 57.5 us (0.966)
  waiting for transfers between devices: 26.5 us -> 21.9 us
  Pallas kernels: 15.4 us -> 16.7 us
  starting transfers between devices: 17.1 us -> 18.4 us
    ppermute x10, waiting for transfers between devices: 25.2 us -> 19.5 us  [swap_bits(): lax.ppermute(x, 'pw', [(i, i ^ 2 << bits[i % 2]) for i in range(count)])]
    pallas_call x1 -> x3, Pallas kernels: 1.88 us -> 4.08 us  [the longest x1 1.54 us: halve(): pl.pallas_call(halve_kernel, in_specs=[SMEM, HBM], out_specs=[VMEM, VMEM]...]
    ppermute x10, starting transfers between devices: 16.3 us -> 17.7 us  [swap_bits(): lax.ppermute(x, 'pw', [(i, i ^ 2 << bits[i % 2]) for i in range(count)])]
    ppermute x6 -> x5, waiting for transfers between devices: 1.23 us -> 2.4 us  [swap_cores(): return lax.ppermute(x, 'pw', [(i, i ^ 1) for i in range(count)])]
  transfers between devices with their start and end apart: 16 -> 15, of which waited for: 9 -> 11; matrix products, arithmetic and copies ran while one was open for 0% -> 0% of each run, Pallas kernels for 12% -> 12%
where the time goes in v6:
time: 57.5 us; the launch traced here: 57.4 us
  waiting for transfers between devices  21.9 us (38%)
  starting transfers between devices  18.4 us (32%)
  Pallas kernels  16.7 us (29%)
    ppermute x10, waiting for transfers between devices, swap_bits(): lax.ppermute(x, 'pw', [(i, i ^ 2 << bits[i % 2]) for i in range(count)])  19.5 us
    ppermute x10, starting transfers between devices, swap_bits(): lax.ppermute(x, 'pw', [(i, i ^ 2 << bits[i % 2]) for i in range(count)])  17.7 us
    pallas_call x1, Pallas kernels, finish(): pl.pallas_call(kernel, in_specs=[SMEM] + [VMEM] * 6, out_specs=HBM, out_s...  4.13 us
    pallas_call x2, Pallas kernels, project(): pl.pallas_call(kernel, in_specs=[SMEM, VMEM, VMEM], out_specs=[VMEM, VMEM...  3.88 us
    pallas_call x1, Pallas kernels, load(): pl.pallas_call(load_kernel, in_specs=[SMEM, HBM], out_specs=VMEM, out_sha...  2.42 us
    ppermute x5, waiting for transfers between devices, swap_cores(): return lax.ppermute(x, 'pw', [(i, i ^ 1) for i in range(count)])  2.4 us
    pallas_call x1, Pallas kernels, halve(): pl.pallas_call(halve_kernel, in_specs=[SMEM, HBM], out_specs=[VMEM, VMEM]...  1.54 us
    pallas_call x1, Pallas kernels, extend(): pl.pallas_call(extend_kernel, in_specs=[SMEM, VMEM, VMEM, VMEM], out_spec...  1.28 us
  transfers between devices with their start and end apart: 15, of which 11 were waited for; matrix products, arithmetic and copies ran while one was open for 0% of the time, Pallas kernels for 12%

profile of v6, /device:TPU:0, one launch (start us, length us, event | category | flops | bytes accessed | tf_op | source)
XLA Modules:
  0.0 57.4 jit_solution(15770379144334999650)
XLA Ops:
  0.0 0.1 pad_add_fusion.where.refs_0_
  0.1 1.5 %halve.1 = (bf16[128,256]{1,0:T(8,128)(2,1)S(1)}, bf16[128,256]{1,0:T(8,128)(2,1)S(1)}) custom-call(s32[3]{0:T(128)S(1)} %pad_add_fusion.where.refs_0_, f32[1,256,256]{2,1,0:T(8,128)} %table.1), custom_call_target="tpu_custom_call" | custom-call | tf_op jit(solution)/shard_map/halve/pallas_call | solution.py:212
  1.6 0.0 copy-start.1
  1.6 3.0 %collective-permute-start = (bf16[128,256]{1,0:T(8,128)(2,1)S(1)}, bf16[128,256]{1,0:T(8,128)(2,1)S(1)}, u32[]{:S(2)}, u32[]{:S(2)}) collective-permute-start(bf16[128,256]{1,0:T(8,128)(2,1)S(1)} %get-tuple-element.36), channel_id=1, source_target_pairs={{0,2},{1,3},{2,0},{3,1},{4,6},{5,7},{6,4},{7,5},{8,10},{9,11},{10,... | collective-permute-start | bytes 196616 | tf_op jit(solution)/shard_map/ppermute | solution.py:47
  4.7 2.4 %load.1.refs_1_ = bf16[512,2048]{1,0:T(8,128)(2,1)S(1)} custom-call(s32[3]{0:T(128)S(1)} %pad_add_fusion.where.refs_0_, bf16[2048,512]{1,0:T(8,128)(2,1)} %refs_1_.1), custom_call_target="tpu_custom_call" | custom-call | tf_op jit(solution)/shard_map/load/pallas_call | solution.py:74
  7.1 0.0 copy-start.4
  7.1 0.0 collective-permute-done.got
  7.1 0.0 copy-done.1
  7.1 1.9 %project.2 = (bf16[4,256,128]{2,1,0:T(8,128)(2,1)S(1)}, f32[4,256,128]{2,1,0:T(8,128)S(1)}) custom-call(s32[3]{0:T(128)S(1)} %pad_add_fusion.where.refs_0_, bf16[512,2048]{1,0:T(8,128)(2,1)S(1)} %load.1.refs_1_, bf16[2048,1024]{1,0:T(8,128)(2,1)S(1)} %copy-done.1), custom_call_target="tpu_custom_call" | custom-call | flops 1073741824 | bytes 4194304 | tf_op jit(solution)/shard_map/project/pallas_call | solution.py:122
  9.0 0.1 collective-permute-start.2
  9.1 0.0 copy-done.4
  9.1 0.6 choose.1
  9.7 0.6 collective-permute-start.1
  10.3 0.4 collective-permute-done.2.right
  10.7 0.5 collective-permute-done.1.right
  11.2 2.9 %collective-permute-start.3 = (bf16[128,256]{1,0:T(8,128)(2,1)S(1)}, bf16[128,256]{1,0:T(8,128)(2,1)S(1)}, u32[]{:S(2)}, u32[]{:S(2)}) collective-permute-start(bf16[128,256]{1,0:T(8,128)(2,1)S(1)} %merge.3.left), channel_id=1, source_target_pairs={{0,8},{1,9},{2,10},{3,11},{4,12},{5,13},{6,14},{7,15},{8,0},{9,1},... | collective-permute-start | bytes 196616 | tf_op jit(solution)/shard_map/ppermute | solution.py:47
  14.1 1.5 %collective-permute-start.5 = (bf16[4,256,128]{2,1,0:T(8,128)(2,1)S(1)}, bf16[4,256,128]{2,1,0:T(8,128)(2,1)S(1)}, u32[]{:S(2)}, u32[]{:S(2)}) collective-permute-start(bf16[4,256,128]{2,1,0:T(8,128)(2,1)S(1)} %add.11.after), channel_id=1, source_target_pairs={{0,2},{1,5},{2,0},{3,7},{4,6},{5,1},{6,4},{7,3},{8,10},{9,13},{10,... | collective-permute-start | bytes 786440 | tf_op jit(solution)/shard_map/ppermute | solution.py:47
  15.6 2.0 %project.3 = (bf16[4,256,128]{2,1,0:T(8,128)(2,1)S(1)}, f32[4,256,128]{2,1,0:T(8,128)S(1)}) custom-call(s32[3]{0:T(128)S(1)} %pad_add_fusion.where.refs_0_, bf16[512,2048]{1,0:T(8,128)(2,1)S(1)} %load.1.refs_1_, bf16[2048,1024]{1,0:T(8,128)(2,1)S(1)} %copy-done.1), custom_call_target="tpu_custom_call" | custom-call | flops 1073741824 | bytes 4194304 | tf_op jit(solution)/shard_map/project/pallas_call | solution.py:122
  17.6 0.0 copy-start.2
  17.6 0.0 copy-start.3
  17.6 0.0 copy-start
  17.6 0.3 collective-permute-done.3.right
  17.9 0.1 collective-permute-start.4
  18.0 2.5 %collective-permute-done.5.refs_2_ = bf16[4,256,128]{2,1,0:T(8,128)(2,1)S(1)} collective-permute-done((bf16[4,256,128]{2,1,0:T(8,128)(2,1)S(1)}, bf16[4,256,128]{2,1,0:T(8,128)(2,1)S(1)}, u32[]{:S(2)}, u32[]{:S(2)}) %collective-permute-start.5) | collective-permute-done | bytes 262176 | tf_op jit(solution)/shard_map/ppermute | solution.py:47
  20.5 0.0 collective-permute-done.4.refs_1_
  20.5 0.1 fold.2
  20.6 1.6 %collective-permute-start.6 = (bf16[2,256,128]{2,1,0:T(8,128)(2,1)S(1)}, bf16[2,256,128]{2,1,0:T(8,128)(2,1)S(1)}, u32[]{:S(2)}, u32[]{:S(2)}) collective-permute-start(bf16[2,256,128]{2,1,0:T(8,128)(2,1)S(1)} %get-tuple-element.50.after), channel_id=1, source_target_pairs={{0,4},{1,3},{2,6},{3,1},{4,0},{5,7},{6,2},{7,5},{8,12},{9,11},{10,... | collective-permute-start | bytes 393224 | tf_op jit(solution)/shard_map/ppermute | solution.py:47
  22.2 0.5 collective-permute-start.7
  22.7 4.1 %collective-permute-done.7.right = bf16[128,256]{1,0:T(8,128)(2,1)S(1)} collective-permute-done((bf16[128,256]{1,0:T(8,128)(2,1)S(1)}, bf16[128,256]{1,0:T(8,128)(2,1)S(1)}, u32[]{:S(2)}, u32[]{:S(2)}) %collective-permute-start.7) | collective-permute-done | bytes 65568 | tf_op jit(solution)/shard_map/ppermute | solution.py:47
  26.8 0.0 collective-permute-done.6.refs_1_
  26.9 1.7 %collective-permute-start.8 = (bf16[1,256,128]{2,1,0:T(8,128)(2,1)S(1)}, bf16[1,256,128]{2,1,0:T(8,128)(2,1)S(1)}, u32[]{:S(2)}, u32[]{:S(2)}) collective-permute-start(bf16[1,256,128]{2,1,0:T(8,128)(2,1)S(1)} %get-tuple-element.54), channel_id=1, source_target_pairs={{0,8},{1,9},{2,10},{3,11},{4,12},{5,13},{6,14},{7,15},{8,0},{9,1},... | collective-permute-start | bytes 196616 | tf_op jit(solution)/shard_map/ppermute | solution.py:47
  28.6 1.4 %collective-permute-start.9 = (bf16[128,256]{1,0:T(8,128)(2,1)S(1)}, bf16[128,256]{1,0:T(8,128)(2,1)S(1)}, u32[]{:S(2)}, u32[]{:S(2)}) collective-permute-start(bf16[128,256]{1,0:T(8,128)(2,1)S(1)} %merge.5.near), channel_id=1, source_target_pairs={{0,2},{1,3},{2,0},{3,1},{4,6},{5,7},{6,4},{7,5},{8,10},{9,11},{10,... | collective-permute-start | bytes 196616 | tf_op jit(solution)/shard_map/ppermute | solution.py:47
  30.0 0.0 copy-done.2
  30.0 0.0 copy-done.3
  30.0 0.7 %mask.1.allowed = bf16[256,256]{1,0:T(8,128)(2,1)S(1)} custom-call(s32[3]{0:T(128)S(1)} %pad_add_fusion.where.refs_0_, s32[2,4]{1,0:T(2,128)S(1)} %copy-done.3, s32[2,256]{1,0:T(2,128)S(1)} %copy-done.2, bf16[4,256,128]{2,1,0:T(8,128)(2,1)S(1)} %add.11.after), custom_call_target="tpu_custom_call" | custom-call | tf_op jit(solution)/shard_map/mask/pallas_call | solution.py:272
  30.7 1.4 %collective-permute-done.8.got = bf16[1,256,128]{2,1,0:T(8,128)(2,1)S(1)} collective-permute-done((bf16[1,256,128]{2,1,0:T(8,128)(2,1)S(1)}, bf16[1,256,128]{2,1,0:T(8,128)(2,1)S(1)}, u32[]{:S(2)}, u32[]{:S(2)}) %collective-permute-start.8) | collective-permute-done | bytes 65568 | tf_op jit(solution)/shard_map/ppermute | solution.py:47
  32.1 0.8 %collective-permute-done.9.far = bf16[128,256]{1,0:T(8,128)(2,1)S(1)} collective-permute-done((bf16[128,256]{1,0:T(8,128)(2,1)S(1)}, bf16[128,256]{1,0:T(8,128)(2,1)S(1)}, u32[]{:S(2)}, u32[]{:S(2)}) %collective-permute-start.9) | collective-permute-done | bytes 65568 | tf_op jit(solution)/shard_map/ppermute | solution.py:47
  32.9 0.7 %couple.1 = bf16[1,256,128]{2,1,0:T(8,128)(2,1)S(1)} custom-call(s32[3]{0:T(128)S(1)} %pad_add_fusion.where.refs_0_, f32[1,256,128]{2,1,0:T(8,128)S(1)} %get-tuple-element.53.kept, bf16[1,256,128]{2,1,0:T(8,128)(2,1)S(1)} %collective-permute-done.8.got, bf16[256,256]{1,0:T(8,128)(2,1)S(1)} %mask.1.allowed, bf16[128,256]{1,0:T(8,128)(2,1)S(1)} %merge.5.near, ...), custom_call_target="tpu_custom_call" | custom-call | tf_op jit(solution)/shard_map/couple/pallas_call | solution.py:297
  33.6 1.3 %collective-permute-start.10 = (bf16[1,256,128]{2,1,0:T(8,128)(2,1)S(1)}, bf16[1,256,128]{2,1,0:T(8,128)(2,1)S(1)}, u32[]{:S(2)}, u32[]{:S(2)}) collective-permute-start(bf16[1,256,128]{2,1,0:T(8,128)(2,1)S(1)} %couple.1), channel_id=1, source_target_pairs={{0,8},{1,9},{2,10},{3,11},{4,12},{5,13},{6,14},{7,15},{8,0},{9,1},... | collective-permute-start | bytes 196616 | tf_op jit(solution)/shard_map/ppermute | solution.py:47
  34.9 3.9 %collective-permute-done.10 = bf16[1,256,128]{2,1,0:T(8,128)(2,1)S(1)} collective-permute-done((bf16[1,256,128]{2,1,0:T(8,128)(2,1)S(1)}, bf16[1,256,128]{2,1,0:T(8,128)(2,1)S(1)}, u32[]{:S(2)}, u32[]{:S(2)}) %collective-permute-start.10) | collective-permute-done | bytes 65568 | tf_op jit(solution)/shard_map/ppermute | solution.py:47
  38.9 2.1 %collective-permute-start.11 = (bf16[2,256,128]{2,1,0:T(8,128)(2,1)S(1)}, bf16[2,256,128]{2,1,0:T(8,128)(2,1)S(1)}, u32[]{:S(2)}, u32[]{:S(2)}) collective-permute-start(bf16[2,256,128]{2,1,0:T(8,128)(2,1)S(1)} %pad_maximum_fusion.1), channel_id=1, source_target_pairs={{0,4},{1,3},{2,6},{3,1},{4,0},{5,7},{6,2},{7,5},{8,12},{9,11},{10,... | collective-permute-start | bytes 393224 | tf_op jit(solution)/shard_map/ppermute | solution.py:47
  40.9 2.9 %collective-permute-done.11 = bf16[2,256,128]{2,1,0:T(8,128)(2,1)S(1)} collective-permute-done((bf16[2,256,128]{2,1,0:T(8,128)(2,1)S(1)}, bf16[2,256,128]{2,1,0:T(8,128)(2,1)S(1)}, u32[]{:S(2)}, u32[]{:S(2)}) %collective-permute-start.11) | collective-permute-done | bytes 131104 | tf_op jit(solution)/shard_map/ppermute | solution.py:47
  43.9 0.0 copy-done
  43.9 1.3 %begin.1 = (f32[2048,256]{1,0:T(8,128)S(1)}, f32[2048,256]{1,0:T(8,128)S(1)}, bf16[4,256,128]{2,1,0:T(8,128)(2,1)S(1)}) custom-call(s32[3]{0:T(128)S(1)} %pad_add_fusion.where.refs_0_, bf16[2048,512]{1,0:T(8,128)(2,1)S(1)} %copy-done, bf16[4,256,128]{2,1,0:T(8,128)(2,1)S(1)} %pad_maximum_fusion.own), custom_call_target="tpu_custom_call" | custom-call | flops 536870912 | bytes 2097152 | tf_op jit(solution)/shard_map/begin/pallas_call | solution.py:329
  45.2 0.1 collective-permute-start.13
  45.3 1.5 %collective-permute-start.12 = (bf16[4,256,128]{2,1,0:T(8,128)(2,1)S(1)}, bf16[4,256,128]{2,1,0:T(8,128)(2,1)S(1)}, u32[]{:S(2)}, u32[]{:S(2)}) collective-permute-start(bf16[4,256,128]{2,1,0:T(8,128)(2,1)S(1)} %pad_maximum_fusion.own), channel_id=1, source_target_pairs={{0,2},{1,5},{2,0},{3,7},{4,6},{5,1},{6,4},{7,3},{8,10},{9,13},{10,... | collective-permute-start | bytes 786440 | tf_op jit(solution)/shard_map/ppermute | solution.py:47
  46.8 0.0 collective-permute-done.13.other
  46.8 1.3 %extend.1 = (bf16[2048,256]{1,0:T(8,128)(2,1)S(1)}, f32[2048,256]{1,0:T(8,128)S(1)}) custom-call(s32[3]{0:T(128)S(1)} %pad_add_fusion.where.refs_0_, bf16[2048,512]{1,0:T(8,128)(2,1)S(1)} %copy-done, f32[2048,256]{1,0:T(8,128)S(1)} %get-tuple-element.56.partial, bf16[4,256,128]{2,1,0:T(8,128)(2,1)S(1)} %collective-permute-done.13.other), custom_call_target="tpu_custom_call" | custom-call | flops 536870912 | bytes 2097152 | tf_op jit(solution)/shard_map/extend/pallas_call | solution.py:357
  48.1 3.6 %collective-permute-done.12.refs_5_ = bf16[4,256,128]{2,1,0:T(8,128)(2,1)S(1)} collective-permute-done((bf16[4,256,128]{2,1,0:T(8,128)(2,1)S(1)}, bf16[4,256,128]{2,1,0:T(8,128)(2,1)S(1)}, u32[]{:S(2)}, u32[]{:S(2)}) %collective-permute-start.12) | collective-permute-done | bytes 262176 | tf_op jit(solution)/shard_map/ppermute | solution.py:47
  51.7 0.0 collective-permute-start.14
  51.7 1.5 %collective-permute-done.14.refs_6_ = bf16[4,256,128]{2,1,0:T(8,128)(2,1)S(1)} collective-permute-done((bf16[4,256,128]{2,1,0:T(8,128)(2,1)S(1)}, bf16[4,256,128]{2,1,0:T(8,128)(2,1)S(1)}, u32[]{:S(2)}, u32[]{:S(2)}) %collective-permute-start.14) | collective-permute-done | bytes 262176 | tf_op jit(solution)/shard_map/ppermute | solution.py:42
  53.3 4.1 %finish.1 = bf16[2048,1024]{1,0:T(8,128)(2,1)} custom-call(s32[3]{0:T(128)S(1)} %pad_add_fusion.where.refs_0_, bf16[2048,512]{1,0:T(8,128)(2,1)S(1)} %copy-done, bf16[2048,256]{1,0:T(8,128)(2,1)S(1)} %get-tuple-element.59.refs_2_, f32[2048,256]{1,0:T(8,128)S(1)} %get-tuple-element.60.refs_3_, f32[2048,256]{1,0:T(8,128)S(1)} %get-tuple-element.61.refs_4_, ...), custom_call_target="tpu_custom_call" | custom-call | flops 1073741824 | bytes 6291456 | tf_op jit(solution)/shard_map/finish/pallas_call | solution.py:409
  (7 shorter events, 0.1 us)
Async XLA Ops:
  1.6 5.5 %copy-start.1 = (bf16[2048,1024]{1,0:T(8,128)(2,1)S(1)}, bf16[2048,1024]{1,0:T(8,128)(2,1)}, u32[]{:S(2)}) copy-start(bf16[2048,1024]{1,0:T(8,128)(2,1)} %refs_2_.3) | copy-start | bytes 12582916
  1.6 5.5 %collective-permute-start = (bf16[128,256]{1,0:T(8,128)(2,1)S(1)}, bf16[128,256]{1,0:T(8,128)(2,1)S(1)}, u32[]{:S(2)}, u32[]{:S(2)}) collective-permute-start(bf16[128,256]{1,0:T(8,128)(2,1)S(1)} %get-tuple-element.36), channel_id=1, source_target_pairs={{0,2},{1,3},{2,0},{3,1},{4,6},{5,7},{6,4},{7,5},{8,10},{9,11},{10,... | collective-permute-start | bytes 196616 | tf_op jit(solution)/shard_map/ppermute | solution.py:47
  7.1 2.0 %copy-start.4 = (s32[2]{0:T(128)S(1)}, s32[2]{0:T(128)}, u32[]{:S(2)}) copy-start(s32[2]{0:T(128)} %owners.1) | copy-start | bytes 28
  9.0 1.6 %collective-permute-start.2 = (bf16[4,256,128]{2,1,0:T(8,128)(2,1)S(1)}, bf16[4,256,128]{2,1,0:T(8,128)(2,1)S(1)}, u32[]{:S(2)}, u32[]{:S(2)}) collective-permute-start(bf16[4,256,128]{2,1,0:T(8,128)(2,1)S(1)} %get-tuple-element.43), channel_id=1, source_target_pairs={{0,1},{1,0},{2,3},{3,2},{4,5},{5,4},{6,7},{7,6},{8,9},{9,8},{10,11... | collective-permute-start | bytes 786440 | tf_op jit(solution)/shard_map/ppermute | solution.py:42
  9.7 1.5 %collective-permute-start.1 = (bf16[128,256]{1,0:T(8,128)(2,1)S(1)}, bf16[128,256]{1,0:T(8,128)(2,1)S(1)}, u32[]{:S(2)}, u32[]{:S(2)}) collective-permute-start(bf16[128,256]{1,0:T(8,128)(2,1)S(1)} %get-tuple-element.42), channel_id=1, source_target_pairs={{0,1},{1,0},{2,3},{3,2},{4,5},{5,4},{6,7},{7,6},{8,9},{9,8},{10,11... | collective-permute-start | bytes 196616 | tf_op jit(solution)/shard_map/ppermute | solution.py:42
  11.2 6.8 %collective-permute-start.3 = (bf16[128,256]{1,0:T(8,128)(2,1)S(1)}, bf16[128,256]{1,0:T(8,128)(2,1)S(1)}, u32[]{:S(2)}, u32[]{:S(2)}) collective-permute-start(bf16[128,256]{1,0:T(8,128)(2,1)S(1)} %merge.3.left), channel_id=1, source_target_pairs={{0,8},{1,9},{2,10},{3,11},{4,12},{5,13},{6,14},{7,15},{8,0},{9,1},... | collective-permute-start | bytes 196616 | tf_op jit(solution)/shard_map/ppermute | solution.py:47
  14.1 6.4 %collective-permute-start.5 = (bf16[4,256,128]{2,1,0:T(8,128)(2,1)S(1)}, bf16[4,256,128]{2,1,0:T(8,128)(2,1)S(1)}, u32[]{:S(2)}, u32[]{:S(2)}) collective-permute-start(bf16[4,256,128]{2,1,0:T(8,128)(2,1)S(1)} %add.11.after), channel_id=1, source_target_pairs={{0,2},{1,5},{2,0},{3,7},{4,6},{5,1},{6,4},{7,3},{8,10},{9,13},{10,... | collective-permute-start | bytes 786440 | tf_op jit(solution)/shard_map/ppermute | solution.py:47
  17.6 12.4 %copy-start.2 = (s32[2,256]{1,0:T(2,128)S(1)}, s32[2,256]{1,0:T(2,128)}, u32[]{:S(2)}) copy-start(s32[2,256]{1,0:T(2,128)} %atom_of.1) | copy-start | bytes 6148
  17.6 12.4 %copy-start.3 = (s32[2,4]{1,0:T(2,128)S(1)}, s32[2,4]{1,0:T(2,128)}, u32[]{:S(2)}) copy-start(s32[2,4]{1,0:T(2,128)} %counts.1) | copy-start | bytes 100
  17.6 26.3 %copy-start = (bf16[2048,512]{1,0:T(8,128)(2,1)S(1)}, bf16[2048,512]{1,0:T(8,128)(2,1)}, u32[]{:S(2)}) copy-start(bf16[2048,512]{1,0:T(8,128)(2,1)} %refs_1_.1) | copy-start | bytes 6291460
  17.9 2.6 %collective-permute-start.4 = (bf16[4,256,128]{2,1,0:T(8,128)(2,1)S(1)}, bf16[4,256,128]{2,1,0:T(8,128)(2,1)S(1)}, u32[]{:S(2)}, u32[]{:S(2)}) collective-permute-start(bf16[4,256,128]{2,1,0:T(8,128)(2,1)S(1)} %get-tuple-element.48), channel_id=1, source_target_pairs={{0,1},{1,0},{2,3},{3,2},{4,5},{5,4},{6,7},{7,6},{8,9},{9,8},{10,11... | collective-permute-start | bytes 786440 | tf_op jit(solution)/shard_map/ppermute | solution.py:42
  20.6 6.2 %collective-permute-start.6 = (bf16[2,256,128]{2,1,0:T(8,128)(2,1)S(1)}, bf16[2,256,128]{2,1,0:T(8,128)(2,1)S(1)}, u32[]{:S(2)}, u32[]{:S(2)}) collective-permute-start(bf16[2,256,128]{2,1,0:T(8,128)(2,1)S(1)} %get-tuple-element.50.after), channel_id=1, source_target_pairs={{0,4},{1,3},{2,6},{3,1},{4,0},{5,7},{6,2},{7,5},{8,12},{9,11},{10,... | collective-permute-start | bytes 393224 | tf_op jit(solution)/shard_map/ppermute | solution.py:47
  22.2 4.6 %collective-permute-start.7 = (bf16[128,256]{1,0:T(8,128)(2,1)S(1)}, bf16[128,256]{1,0:T(8,128)(2,1)S(1)}, u32[]{:S(2)}, u32[]{:S(2)}) collective-permute-start(bf16[128,256]{1,0:T(8,128)(2,1)S(1)} %merge.4.left), channel_id=1, source_target_pairs={{0,4},{1,5},{2,6},{3,7},{4,0},{5,1},{6,2},{7,3},{8,12},{9,13},{10,... | collective-permute-start | bytes 196616 | tf_op jit(solution)/shard_map/ppermute | solution.py:47
  26.9 5.2 %collective-permute-start.8 = (bf16[1,256,128]{2,1,0:T(8,128)(2,1)S(1)}, bf16[1,256,128]{2,1,0:T(8,128)(2,1)S(1)}, u32[]{:S(2)}, u32[]{:S(2)}) collective-permute-start(bf16[1,256,128]{2,1,0:T(8,128)(2,1)S(1)} %get-tuple-element.54), channel_id=1, source_target_pairs={{0,8},{1,9},{2,10},{3,11},{4,12},{5,13},{6,14},{7,15},{8,0},{9,1},... | collective-permute-start | bytes 196616 | tf_op jit(solution)/shard_map/ppermute | solution.py:47
  28.6 4.3 %collective-permute-start.9 = (bf16[128,256]{1,0:T(8,128)(2,1)S(1)}, bf16[128,256]{1,0:T(8,128)(2,1)S(1)}, u32[]{:S(2)}, u32[]{:S(2)}) collective-permute-start(bf16[128,256]{1,0:T(8,128)(2,1)S(1)} %merge.5.near), channel_id=1, source_target_pairs={{0,2},{1,3},{2,0},{3,1},{4,6},{5,7},{6,4},{7,5},{8,10},{9,11},{10,... | collective-permute-start | bytes 196616 | tf_op jit(solution)/shard_map/ppermute | solution.py:47
  33.6 5.2 %collective-permute-start.10 = (bf16[1,256,128]{2,1,0:T(8,128)(2,1)S(1)}, bf16[1,256,128]{2,1,0:T(8,128)(2,1)S(1)}, u32[]{:S(2)}, u32[]{:S(2)}) collective-permute-start(bf16[1,256,128]{2,1,0:T(8,128)(2,1)S(1)} %couple.1), channel_id=1, source_target_pairs={{0,8},{1,9},{2,10},{3,11},{4,12},{5,13},{6,14},{7,15},{8,0},{9,1},... | collective-permute-start | bytes 196616 | tf_op jit(solution)/shard_map/ppermute | solution.py:47
  38.9 5.0 %collective-permute-start.11 = (bf16[2,256,128]{2,1,0:T(8,128)(2,1)S(1)}, bf16[2,256,128]{2,1,0:T(8,128)(2,1)S(1)}, u32[]{:S(2)}, u32[]{:S(2)}) collective-permute-start(bf16[2,256,128]{2,1,0:T(8,128)(2,1)S(1)} %pad_maximum_fusion.1), channel_id=1, source_target_pairs={{0,4},{1,3},{2,6},{3,1},{4,0},{5,7},{6,2},{7,5},{8,12},{9,11},{10,... | collective-permute-start | bytes 393224 | tf_op jit(solution)/shard_map/ppermute | solution.py:47
  45.2 1.6 %collective-permute-start.13 = (bf16[4,256,128]{2,1,0:T(8,128)(2,1)S(1)}, bf16[4,256,128]{2,1,0:T(8,128)(2,1)S(1)}, u32[]{:S(2)}, u32[]{:S(2)}) collective-permute-start(bf16[4,256,128]{2,1,0:T(8,128)(2,1)S(1)} %get-tuple-element.57), channel_id=1, source_target_pairs={{0,1},{1,0},{2,3},{3,2},{4,5},{5,4},{6,7},{7,6},{8,9},{9,8},{10,11... | collective-permute-start | bytes 786440 | tf_op jit(solution)/shard_map/ppermute | solution.py:42
  45.3 6.4 %collective-permute-start.12 = (bf16[4,256,128]{2,1,0:T(8,128)(2,1)S(1)}, bf16[4,256,128]{2,1,0:T(8,128)(2,1)S(1)}, u32[]{:S(2)}, u32[]{:S(2)}) collective-permute-start(bf16[4,256,128]{2,1,0:T(8,128)(2,1)S(1)} %pad_maximum_fusion.own), channel_id=1, source_target_pairs={{0,2},{1,5},{2,0},{3,7},{4,6},{5,1},{6,4},{7,3},{8,10},{9,13},{10,... | collective-permute-start | bytes 786440 | tf_op jit(solution)/shard_map/ppermute | solution.py:47
  51.7 1.5 %collective-permute-start.14 = (bf16[4,256,128]{2,1,0:T(8,128)(2,1)S(1)}, bf16[4,256,128]{2,1,0:T(8,128)(2,1)S(1)}, u32[]{:S(2)}, u32[]{:S(2)}) collective-permute-start(bf16[4,256,128]{2,1,0:T(8,128)(2,1)S(1)} %collective-permute-done.12.refs_5_), channel_id=1, source_target_pairs={{0,1},{1,0},{2,3},{3,2},{4,5},{5,4},{6,7},{7,6},{8,9},{9,8},{10,11... | collective-permute-start | bytes 786440 | tf_op jit(solution)/shard_map/ppermute | solution.py:42

commit v7 on v6

--- a/solution.py
+++ b/solution.py
@@ -177,6 +177,27 @@
     )(*terms)
 
 
+def total_kernel(left, right, kept, message):
+    for at in range(kept.shape[0]):
+        total = left[at] + right[at].astype(jnp.float32)
+        kept[at] = total
+        message[at ^ 1] = total.astype(message.dtype)
+
+
+def total_of(left, right):
+    return pl.pallas_call(
+        total_kernel,
+        in_specs=[VMEM, VMEM],
+        out_specs=[VMEM, VMEM],
+        out_shape=[
+            jax.ShapeDtypeStruct(left.shape, jnp.float32),
+            jax.ShapeDtypeStruct(left.shape, jnp.bfloat16),
+        ],
+        compiler_params=PARAMS,
+        name="total",
+    )(left, right)
+
+
 def add_kernel(left, right, out):
     for at in range(out.shape[0]):
         out[at] = (left[at] + right[at].astype(jnp.float32)).astype(out.dtype)
@@ -193,43 +214,20 @@
     )(left, right)
 
 
-def halve_kernel(where, table, kept, sent, rows, sems):
+def choose_kernel(where, owners, own, sibling, after, kept, sent):
+    del after
+    core, chip, me = where[0], where[1], where[2]
+    owner = jnp.where(core == 0, owners[0], owners[1])
     half = PCAP // 2
-    side = where[1] & 1
-    copies = []
-    for at, which in enumerate((1 - side, side)):
-        start = pl.multiple_of(which * half, half)
-        copies.append(pltpu.make_async_copy(table.at[0, pl.ds(start, half)], rows.at[at], sems.at[at]))
-        copies[-1].start()
-    for at, out in enumerate((sent, kept)):
-        copies[at].wait()
-        out[...] = rows[at].astype(out.dtype)
-
-
-def halve(where, couplings):
-    half = PCAP // 2
-    shape = jax.ShapeDtypeStruct((half, PCAP), jnp.bfloat16)
-    return pl.pallas_call(
-        halve_kernel,
-        in_specs=[SMEM, HBM],
-        out_specs=[VMEM, VMEM],
-        out_shape=[shape, shape],
-        scratch_shapes=[pltpu.VMEM((2, half, PCAP), jnp.float32), pltpu.SemaphoreType.DMA((2,))],
-        compiler_params=PARAMS,
-        name="halve",
-    )(where, pltpu.with_memory_space_constraint(couplings, pltpu.HBM))
-
-
-def choose_kernel(where, owners, kept, got, after, near, sent):
-    del after
-    core, me = where[0], where[2]
-    for out, group in ((near, core), (sent, 1 - core)):
-        owner = jnp.where(group == 0, owners[0], owners[1])
-        out[...] = jnp.where(owner == me, kept[...], jnp.where(owner == (me ^ 2), got[...], jnp.zeros_like(got)))
-
-
-def choose(where, owners, kept, got, after):
-    shape = jax.ShapeDtypeStruct(kept.shape, kept.dtype)
+    side = chip & 1
+    for out, which in ((kept, side), (sent, 1 - side)):
+        rows = pl.ds(pl.multiple_of(which * half, half), half)
+        part = jnp.where(owner == me, own[rows], jnp.where(owner == (me ^ 1), sibling[rows], 0.0))
+        out[...] = part.astype(out.dtype)
+
+
+def choose(where, owners, own, sibling, after):
+    shape = jax.ShapeDtypeStruct((PCAP // 2, PCAP), jnp.bfloat16)
     return pl.pallas_call(
         choose_kernel,
         in_specs=[SMEM, SMEM, VMEM, VMEM, ANY],
@@ -237,7 +235,7 @@
         out_shape=[shape, shape],
         compiler_params=PARAMS,
         name="choose",
-    )(where, owners, kept, got, after)
+    )(where, owners, own, sibling, after)
 
 
 def merge_kernel(left, right, after, out):
@@ -279,30 +277,42 @@
     )(where, counts, atom_of, after)
 
 
-def couple_kernel(where, kept, got, allowed, near, far, out, table):
+def coupling_kernel(where, allowed, near, far, out):
     half = PCAP // 2
-    width = out.shape[2]
     side = where[1] & 1
     for part, which in ((near, side), (far, 1 - side)):
         rows = pl.ds(pl.multiple_of(which * half, half), half)
-        table[rows] = part[...] * allowed[rows]
-    total = kept[0] + got[0].astype(jnp.float32)
-    high = total.astype(jnp.bfloat16)
-    low = (total - high.astype(jnp.float32)).astype(jnp.bfloat16)
-    both = jnp.dot(table[...], jnp.concatenate([high, low], axis=1), preferred_element_type=jnp.float32)
-    out[0] = (both[:, :width] + both[:, width:]).astype(out.dtype)
-
-
-def couple(where, kept, got, allowed, near, far):
-    return pl.pallas_call(
-        couple_kernel,
-        in_specs=[SMEM] + [VMEM] * 5,
+        out[rows] = part[...] * allowed[rows]
+
+
+def coupling_of(where, allowed, near, far):
+    return pl.pallas_call(
+        coupling_kernel,
+        in_specs=[SMEM] + [VMEM] * 3,
         out_specs=VMEM,
-        out_shape=jax.ShapeDtypeStruct(kept.shape, jnp.bfloat16),
-        scratch_shapes=[pltpu.VMEM((PCAP, PCAP), jnp.bfloat16)],
+        out_shape=jax.ShapeDtypeStruct((PCAP, PCAP), jnp.bfloat16),
+        compiler_params=PARAMS,
+        name="coupling",
+    )(where, allowed, near, far)
+
+
+def scale(coupling, sums, out):
+    width = out.shape[2]
+    wide = jnp.concatenate([sums[at] for at in range(out.shape[0])], axis=1)
+    scaled = jnp.dot(coupling[...], wide, preferred_element_type=jnp.float32).astype(out.dtype)
+    for at in range(out.shape[0]):
+        out[at] = scaled[:, at * width : (at + 1) * width]
+
+
+def couple(coupling, sums):
+    return pl.pallas_call(
+        scale,
+        in_specs=[VMEM, VMEM],
+        out_specs=VMEM,
+        out_shape=jax.ShapeDtypeStruct(sums.shape, jnp.bfloat16),
         compiler_params=PARAMS,
         name="couple",
-    )(where, kept, got, allowed, near, far)
+    )(coupling, sums)
 
 
 def place(scaled, core, own, other):
@@ -312,31 +322,30 @@
         scaled[rows, LANES:] = part[1]
 
 
-def begin_kernel(where, projectors, own, first, second, held):
+def begin_kernel(where, projectors, coupling, sums, first, second, scaled):
     slots = pl.ds(pl.multiple_of(where[0] * PCAP, PCAP), PCAP)
-    held[...] = own[...]
+    scale(coupling, sums, scaled)
     for out, at in ((first, 0), (second, 2)):
-        weights = jnp.concatenate([own[at], own[at + 1]], axis=1)
+        weights = jnp.concatenate([scaled[at], scaled[at + 1]], axis=1)
         for block in range(projectors.shape[0] // ROW_BLOCK):
             rows = slice(block * ROW_BLOCK, (block + 1) * ROW_BLOCK)
             out[rows] = jnp.dot(projectors[rows, slots], weights, preferred_element_type=jnp.float32)
 
 
-def begin(where, projectors, own):
+def begin(where, projectors, coupling, sums):
     depth, slots = projectors.shape
     shape = jax.ShapeDtypeStruct((depth, 2 * LANES), jnp.float32)
-
     return pl.pallas_call(
         begin_kernel,
-        in_specs=[SMEM, VMEM, VMEM],
+        in_specs=[SMEM, VMEM, VMEM, VMEM],
         out_specs=[VMEM] * 3,
-        out_shape=[shape, shape, jax.ShapeDtypeStruct(own.shape, own.dtype)],
+        out_shape=[shape, shape, jax.ShapeDtypeStruct(sums.shape, sums.dtype)],
         compiler_params=PARAMS,
         cost_estimate=pl.CostEstimate(
             flops=4 * depth * slots * LANES, bytes_accessed=2 * depth * slots, transcendentals=0
         ),
         name="begin",
-    )(where, projectors, own)
+    )(where, projectors, coupling, sums)
 
 
 def extend_kernel(where, projectors, partial, other, done, second):
@@ -444,53 +453,51 @@
     where = jnp.stack([me % 2, me // 2, me])
 
     fast = width == LANES and stages == 3
-    kept, sent = halve(where, couplings)
-    early, sent = lax.optimization_barrier((projectors, sent))
-    got = swap_bits(sent, [0, 0])
+    own_table = couplings[0]
+    sibling_table = swap_cores(own_table)
     if fast:
-        flipped = load(where, early)
-        flipped, got = lax.optimization_barrier((flipped, got))
+        flipped = load(where, projectors)
         theirs, ours = project(where, flipped, band_coeffs, half)
     else:
         theirs, ours = project_plain(where, projectors, band_coeffs, half)
-    near, far = choose(where, owners, kept, got, ours)
-    theirs = swap_cores(theirs)
-    far = swap_cores(far)
-    message = add(ours, theirs)
-    near = merge(near, far, message)
-    got = swap_stage(message, 0)
-    far = swap_bits(near, [stages - 1] * 2)
     if fast:
-        flipped, near = lax.optimization_barrier((flipped, near))
         low_theirs, low_ours = project(where, flipped, band_coeffs, 0)
     else:
         low_theirs, low_ours = project_plain(where, projectors, band_coeffs, 0)
+    theirs, low_ours = lax.optimization_barrier((swap_cores(theirs), low_ours))
+    message = add(ours, theirs)
+    got = swap_stage(message, 0)
+    low_theirs = swap_cores(low_theirs)
+    near, far = choose(where, owners, own_table, sibling_table, message)
+    far = swap_bits(far, [0, 0])
+    allowed = mask(where, counts, atom_of, message)
     near = merge(near, far, message)
-    low_theirs, near = lax.optimization_barrier((low_theirs, near))
-    low_theirs = swap_cores(low_theirs)
-    allowed = mask(where, counts, atom_of, message)
+    got, near = lax.optimization_barrier((got, near))
+    kept, message = fold(low_ours, low_theirs, got)
     for stage in range(1, stages):
-        far = swap_bits(near, [stages - 1 - stage] * 2)
+        got = swap_stage(message, stage)
+        far = swap_bits(near, [stages - stage] * 2)
+        near = merge(near, far, message)
+        got, near = lax.optimization_barrier((got, near))
+        if stage < stages - 2:
+            kept, message = fold(kept, got)
+        elif stage == stages - 2:
+            kept, message = total_of(kept, got)
+    mine = add(kept, got)
+    far = swap_bits(near, [0, 0])
+    for stage in range(stages - 2, 0, -1):
+        got = swap_stage(mine, stage)
         if stage == 1:
-            kept, message = fold(low_ours, low_theirs, got)
-        else:
-            kept, message = fold(kept, got)
-        got = swap_stage(message, stage)
-        if stage < stages - 1:
-            near = merge(near, far, message)
-            got, near = lax.optimization_barrier((got, near))
-
-    scaled = couple(where, kept, got, allowed, near, far)
-    mine = jnp.concatenate([scaled, swap_stage(scaled, stages - 1)])
-    for stage in range(stages - 2, 0, -1):
-        mine = jnp.concatenate([mine, swap_stage(mine, stage)])
+            got, far = lax.optimization_barrier((got, far))
+        mine = jnp.concatenate([mine, got])
+    coupling = coupling_of(where, allowed, near, far)
     got = swap_stage(mine, 0)
     if not fast:
-        mine = jnp.concatenate([mine, got])
+        mine = couple(coupling, jnp.concatenate([mine, got]))
         return apply_plain(where, projectors, mine, swap_cores(mine))
-    first, own, held = begin(where, projectors, mine)
-    done, other = extend(where, projectors, first, swap_cores(held))
-    got, done = lax.optimization_barrier((got, done))
+    first, own, scaled = begin(where, projectors, coupling, mine)
+    done, other = extend(where, projectors, first, swap_cores(scaled))
+    got = couple(coupling, got)
     return finish(where, projectors, done, own, other, got, swap_cores(got))
 
 

time: 57.5 us -> 49.9 us (0.87)
  waiting for transfers between devices: 21.9 us -> 15.8 us
  Pallas kernels: 16.7 us -> 15.7 us
  starting transfers between devices: 18.4 us -> 17.8 us
    ppermute x10 -> x9, waiting for transfers between devices: 19.5 us -> 15.6 us  [swap_bits(): lax.ppermute(x, 'pw', [(i, i ^ 2 << bits[i % 2]) for i in range(count)])]
    ppermute x5, waiting for transfers between devices: 2.4 us -> 0.24 us  [swap_cores(): return lax.ppermute(x, 'pw', [(i, i ^ 1) for i in range(count)])]
    pallas_call x3 -> x4, Pallas kernels: 3.55 us -> 2.28 us  [the longest x1 1.46 us: begin(): pl.pallas_call(begin_kernel, in_specs=[SMEM, VMEM, VMEM, VMEM], out_specs...]
    ppermute x10 -> x9, starting transfers between devices: 17.7 us -> 17.1 us  [swap_bits(): lax.ppermute(x, 'pw', [(i, i ^ 2 << bits[i % 2]) for i in range(count)])]
  transfers between devices with their start and end apart: 15 -> 14, of which waited for: 11 -> 8; matrix products, arithmetic and copies ran while one was open for 0% -> 0% of each run, Pallas kernels for 12% -> 14%
where the time goes in v7:
time: 49.9 us; the launch traced here: 49.7 us
  starting transfers between devices  17.8 us (36%)
  waiting for transfers between devices  15.8 us (32%)
  Pallas kernels  15.7 us (31%)
    ppermute x9, starting transfers between devices, swap_bits(): lax.ppermute(x, 'pw', [(i, i ^ 2 << bits[i % 2]) for i in range(count)])  17.1 us
    ppermute x9, waiting for transfers between devices, swap_bits(): lax.ppermute(x, 'pw', [(i, i ^ 2 << bits[i % 2]) for i in range(count)])  15.6 us
    pallas_call x1, Pallas kernels, finish(): pl.pallas_call(kernel, in_specs=[SMEM] + [VMEM] * 6, out_specs=HBM, out_s...  4.13 us
    pallas_call x2, Pallas kernels, project(): pl.pallas_call(kernel, in_specs=[SMEM, VMEM, VMEM], out_specs=[VMEM, VMEM...  3.88 us
    pallas_call x1, Pallas kernels, load(): pl.pallas_call(load_kernel, in_specs=[SMEM, HBM], out_specs=VMEM, out_sha...  2.68 us
    pallas_call x1, Pallas kernels, begin(): pl.pallas_call(begin_kernel, in_specs=[SMEM, VMEM, VMEM, VMEM], out_specs...  1.46 us
    pallas_call x1, Pallas kernels, extend(): pl.pallas_call(extend_kernel, in_specs=[SMEM, VMEM, VMEM, VMEM], out_spec...  1.28 us
  transfers between devices with their start and end apart: 14, of which 8 were waited for; matrix products, arithmetic and copies ran while one was open for 0% of the time, Pallas kernels for 14%

profile of v7, /device:TPU:0, one launch (start us, length us, event | category | flops | bytes accessed | tf_op | source)
XLA Modules:
  0.0 49.7 jit_solution(13247236630718153554)
XLA Ops:
  0.0 0.1 pad_add_fusion.where.refs_0_
  0.1 0.0 copy-start.1
  0.1 2.7 %load.1.refs_1_ = bf16[512,2048]{1,0:T(8,128)(2,1)S(1)} custom-call(s32[3]{0:T(128)S(1)} %pad_add_fusion.where.refs_0_, bf16[2048,512]{1,0:T(8,128)(2,1)} %refs_1_.1), custom_call_target="tpu_custom_call" | custom-call | tf_op jit(solution)/shard_map/load/pallas_call | solution.py:74
  2.8 0.1 copy-done.1
  2.9 0.0 copy-start.2
  2.9 1.9 %project.2 = (bf16[4,256,128]{2,1,0:T(8,128)(2,1)S(1)}, f32[4,256,128]{2,1,0:T(8,128)S(1)}) custom-call(s32[3]{0:T(128)S(1)} %pad_add_fusion.where.refs_0_, bf16[512,2048]{1,0:T(8,128)(2,1)S(1)} %load.1.refs_1_, bf16[2048,1024]{1,0:T(8,128)(2,1)S(1)} %copy-done.1), custom_call_target="tpu_custom_call" | custom-call | flops 1073741824 | bytes 4194304 | tf_op jit(solution)/shard_map/project/pallas_call | solution.py:122
  4.8 0.5 %collective-permute-start = (bf16[4,256,128]{2,1,0:T(8,128)(2,1)S(1)}, bf16[4,256,128]{2,1,0:T(8,128)(2,1)S(1)}, u32[]{:S(2)}, u32[]{:S(2)}) collective-permute-start(bf16[4,256,128]{2,1,0:T(8,128)(2,1)S(1)} %get-tuple-element.31), channel_id=1, source_target_pairs={{0,1},{1,0},{2,3},{3,2},{4,5},{5,4},{6,7},{7,6},{8,9},{9,8},{10,11... | collective-permute-start | bytes 786440 | tf_op jit(solution)/shard_map/ppermute | solution.py:42
  5.3 0.0 copy-done.2
  5.3 0.0 copy-start.5
  5.3 0.1 collective-permute-start.3
  5.4 2.0 %project.3 = (bf16[4,256,128]{2,1,0:T(8,128)(2,1)S(1)}, f32[4,256,128]{2,1,0:T(8,128)S(1)}) custom-call(s32[3]{0:T(128)S(1)} %pad_add_fusion.where.refs_0_, bf16[512,2048]{1,0:T(8,128)(2,1)S(1)} %load.1.refs_1_, bf16[2048,1024]{1,0:T(8,128)(2,1)S(1)} %copy-done.1), custom_call_target="tpu_custom_call" | custom-call | flops 1073741824 | bytes 4194304 | tf_op jit(solution)/shard_map/project/pallas_call | solution.py:122
  7.4 0.0 collective-permute-done.right
  7.5 3.0 %collective-permute-start.2 = (bf16[4,256,128]{2,1,0:T(8,128)(2,1)S(1)}, bf16[4,256,128]{2,1,0:T(8,128)(2,1)S(1)}, u32[]{:S(2)}, u32[]{:S(2)}) collective-permute-start(bf16[4,256,128]{2,1,0:T(8,128)(2,1)S(1)} %add.12.after), channel_id=1, source_target_pairs={{0,2},{1,5},{2,0},{3,7},{4,6},{5,1},{6,4},{7,3},{8,10},{9,13},{10,... | collective-permute-start | bytes 786440 | tf_op jit(solution)/shard_map/ppermute | solution.py:47
  10.5 0.0 copy-start.3
  10.5 0.0 copy-start.4
  10.5 0.0 collective-permute-start.1
  10.5 0.0 collective-permute-done.3.sibling
  10.5 0.0 copy-done.5
  10.5 0.6 %choose.1 = (bf16[128,256]{1,0:T(8,128)(2,1)S(1)}, bf16[128,256]{1,0:T(8,128)(2,1)S(1)}) custom-call(s32[3]{0:T(128)S(1)} %pad_add_fusion.where.refs_0_, s32[2]{0:T(128)S(1)} %copy-done.5, f32[256,256]{1,0:T(8,128)S(1)} %bitcast.5, f32[256,256]{1,0:T(8,128)S(1)} %collective-permute-done.3.sibling, bf16[4,256,128]{2,1,0:T(8,128)(2,1)S(1)} %add.12.after), custom_call_target="tpu_custom_call" | custom-call | tf_op jit(solution)/shard_map/choose/pallas_call | solution.py:231
  11.1 1.4 %collective-permute-start.4 = (bf16[128,256]{1,0:T(8,128)(2,1)S(1)}, bf16[128,256]{1,0:T(8,128)(2,1)S(1)}, u32[]{:S(2)}, u32[]{:S(2)}) collective-permute-start(bf16[128,256]{1,0:T(8,128)(2,1)S(1)} %get-tuple-element.37), channel_id=1, source_target_pairs={{0,2},{1,3},{2,0},{3,1},{4,6},{5,7},{6,4},{7,5},{8,10},{9,11},{10,... | collective-permute-start | bytes 196616 | tf_op jit(solution)/shard_map/ppermute | solution.py:47
  12.5 3.7 %collective-permute-done.4.right = bf16[128,256]{1,0:T(8,128)(2,1)S(1)} collective-permute-done((bf16[128,256]{1,0:T(8,128)(2,1)S(1)}, bf16[128,256]{1,0:T(8,128)(2,1)S(1)}, u32[]{:S(2)}, u32[]{:S(2)}) %collective-permute-start.4) | collective-permute-done | bytes 65568 | tf_op jit(solution)/shard_map/ppermute | solution.py:47
  16.2 0.0 copy-start
  16.2 0.0 collective-permute-done.2.refs_2_
  16.3 0.0 collective-permute-done.1.refs_1_
  16.3 0.1 fold.1
  16.4 2.2 %collective-permute-start.5 = (bf16[2,256,128]{2,1,0:T(8,128)(2,1)S(1)}, bf16[2,256,128]{2,1,0:T(8,128)(2,1)S(1)}, u32[]{:S(2)}, u32[]{:S(2)}) collective-permute-start(bf16[2,256,128]{2,1,0:T(8,128)(2,1)S(1)} %get-tuple-element.40.after), channel_id=1, source_target_pairs={{0,4},{1,3},{2,6},{3,1},{4,0},{5,7},{6,2},{7,5},{8,12},{9,11},{10,... | collective-permute-start | bytes 393224 | tf_op jit(solution)/shard_map/ppermute | solution.py:47
  18.5 2.6 %collective-permute-start.6 = (bf16[128,256]{1,0:T(8,128)(2,1)S(1)}, bf16[128,256]{1,0:T(8,128)(2,1)S(1)}, u32[]{:S(2)}, u32[]{:S(2)}) collective-permute-start(bf16[128,256]{1,0:T(8,128)(2,1)S(1)} %merge.3.left), channel_id=1, source_target_pairs={{0,8},{1,9},{2,10},{3,11},{4,12},{5,13},{6,14},{7,15},{8,0},{9,1},... | collective-permute-start | bytes 196616 | tf_op jit(solution)/shard_map/ppermute | solution.py:47
  21.1 2.6 %collective-permute-done.6.right = bf16[128,256]{1,0:T(8,128)(2,1)S(1)} collective-permute-done((bf16[128,256]{1,0:T(8,128)(2,1)S(1)}, bf16[128,256]{1,0:T(8,128)(2,1)S(1)}, u32[]{:S(2)}, u32[]{:S(2)}) %collective-permute-start.6) | collective-permute-done | bytes 65568 | tf_op jit(solution)/shard_map/ppermute | solution.py:47
  23.7 0.0 collective-permute-done.5.right
  23.7 2.7 %collective-permute-start.7 = (bf16[2,256,128]{2,1,0:T(8,128)(2,1)S(1)}, bf16[2,256,128]{2,1,0:T(8,128)(2,1)S(1)}, u32[]{:S(2)}, u32[]{:S(2)}) collective-permute-start(bf16[2,256,128]{2,1,0:T(8,128)(2,1)S(1)} %get-tuple-element.43.after), channel_id=1, source_target_pairs={{0,8},{1,9},{2,10},{3,11},{4,12},{5,13},{6,14},{7,15},{8,0},{9,1},... | collective-permute-start | bytes 393224 | tf_op jit(solution)/shard_map/ppermute | solution.py:47
  26.4 0.7 %collective-permute-start.8 = (bf16[128,256]{1,0:T(8,128)(2,1)S(1)}, bf16[128,256]{1,0:T(8,128)(2,1)S(1)}, u32[]{:S(2)}, u32[]{:S(2)}) collective-permute-start(bf16[128,256]{1,0:T(8,128)(2,1)S(1)} %merge.4.left), channel_id=1, source_target_pairs={{0,4},{1,5},{2,6},{3,7},{4,0},{5,1},{6,2},{7,3},{8,12},{9,13},{10,... | collective-permute-start | bytes 196616 | tf_op jit(solution)/shard_map/ppermute | solution.py:47
  27.1 3.5 %collective-permute-done.8.right = bf16[128,256]{1,0:T(8,128)(2,1)S(1)} collective-permute-done((bf16[128,256]{1,0:T(8,128)(2,1)S(1)}, bf16[128,256]{1,0:T(8,128)(2,1)S(1)}, u32[]{:S(2)}, u32[]{:S(2)}) %collective-permute-start.8) | collective-permute-done | bytes 65568 | tf_op jit(solution)/shard_map/ppermute | solution.py:47
  30.7 0.4 collective-permute-done.7.right
  31.1 1.1 %collective-permute-start.9 = (bf16[2,256,128]{2,1,0:T(8,128)(2,1)S(1)}, bf16[2,256,128]{2,1,0:T(8,128)(2,1)S(1)}, u32[]{:S(2)}, u32[]{:S(2)}) collective-permute-start(bf16[2,256,128]{2,1,0:T(8,128)(2,1)S(1)} %add.13), channel_id=1, source_target_pairs={{0,4},{1,3},{2,6},{3,1},{4,0},{5,7},{6,2},{7,5},{8,12},{9,11},{10,... | collective-permute-start | bytes 393224 | tf_op jit(solution)/shard_map/ppermute | solution.py:47
  32.2 1.5 %collective-permute-start.10 = (bf16[128,256]{1,0:T(8,128)(2,1)S(1)}, bf16[128,256]{1,0:T(8,128)(2,1)S(1)}, u32[]{:S(2)}, u32[]{:S(2)}) collective-permute-start(bf16[128,256]{1,0:T(8,128)(2,1)S(1)} %merge.5.near), channel_id=1, source_target_pairs={{0,2},{1,3},{2,0},{3,1},{4,6},{5,7},{6,4},{7,5},{8,10},{9,11},{10,... | collective-permute-start | bytes 196616 | tf_op jit(solution)/shard_map/ppermute | solution.py:47
  33.8 2.7 %collective-permute-done.10.far = bf16[128,256]{1,0:T(8,128)(2,1)S(1)} collective-permute-done((bf16[128,256]{1,0:T(8,128)(2,1)S(1)}, bf16[128,256]{1,0:T(8,128)(2,1)S(1)}, u32[]{:S(2)}, u32[]{:S(2)}) %collective-permute-start.10) | collective-permute-done | bytes 65568 | tf_op jit(solution)/shard_map/ppermute | solution.py:47
  36.5 0.8 %collective-permute-done.9 = bf16[2,256,128]{2,1,0:T(8,128)(2,1)S(1)} collective-permute-done((bf16[2,256,128]{2,1,0:T(8,128)(2,1)S(1)}, bf16[2,256,128]{2,1,0:T(8,128)(2,1)S(1)}, u32[]{:S(2)}, u32[]{:S(2)}) %collective-permute-start.9) | collective-permute-done | bytes 131104 | tf_op jit(solution)/shard_map/ppermute | solution.py:47
  37.3 1.8 %collective-permute-start.12 = (bf16[4,256,128]{2,1,0:T(8,128)(2,1)S(1)}, bf16[4,256,128]{2,1,0:T(8,128)(2,1)S(1)}, u32[]{:S(2)}, u32[]{:S(2)}) collective-permute-start(bf16[4,256,128]{2,1,0:T(8,128)(2,1)S(1)} %pad_maximum_fusion.sums), channel_id=1, source_target_pairs={{0,2},{1,5},{2,0},{3,7},{4,6},{5,1},{6,4},{7,3},{8,10},{9,13},{10,... | collective-permute-start | bytes 786440 | tf_op jit(solution)/shard_map/ppermute | solution.py:47
  39.1 0.0 copy-done.3
  39.1 0.0 copy-done.4
  39.2 0.7 %mask.1.allowed = bf16[256,256]{1,0:T(8,128)(2,1)S(1)} custom-call(s32[3]{0:T(128)S(1)} %pad_add_fusion.where.refs_0_, s32[2,4]{1,0:T(2,128)S(1)} %copy-done.4, s32[2,256]{1,0:T(2,128)S(1)} %copy-done.3, bf16[4,256,128]{2,1,0:T(8,128)(2,1)S(1)} %add.12.after), custom_call_target="tpu_custom_call" | custom-call | tf_op jit(solution)/shard_map/mask/pallas_call | solution.py:270
  39.8 0.6 %coupling.1 = bf16[256,256]{1,0:T(8,128)(2,1)S(1)} custom-call(s32[3]{0:T(128)S(1)} %pad_add_fusion.where.refs_0_, bf16[256,256]{1,0:T(8,128)(2,1)S(1)} %mask.1.allowed, bf16[128,256]{1,0:T(8,128)(2,1)S(1)} %merge.5.near, bf16[128,256]{1,0:T(8,128)(2,1)S(1)} %collective-permute-done.10.far), custom_call_target="tpu_custom_call" | custom-call | tf_op jit(solution)/shard_map/coupling/pallas_call | solution.py:289
  40.4 0.0 copy-done
  40.4 1.5 %begin.1 = (f32[2048,256]{1,0:T(8,128)S(1)}, f32[2048,256]{1,0:T(8,128)S(1)}, bf16[4,256,128]{2,1,0:T(8,128)(2,1)S(1)}) custom-call(s32[3]{0:T(128)S(1)} %pad_add_fusion.where.refs_0_, bf16[2048,512]{1,0:T(8,128)(2,1)S(1)} %copy-done, bf16[256,256]{1,0:T(8,128)(2,1)S(1)} %coupling.1, bf16[4,256,128]{2,1,0:T(8,128)(2,1)S(1)} %pad_maximum_fusion.sums), custom_call_target="tpu_custom_call" | custom-call | flops 536870912 | bytes 2097152 | tf_op jit(solution)/shard_map/begin/pallas_call | solution.py:338
  41.9 0.1 collective-permute-start.11
  41.9 1.8 %collective-permute-done.12.sums = bf16[4,256,128]{2,1,0:T(8,128)(2,1)S(1)} collective-permute-done((bf16[4,256,128]{2,1,0:T(8,128)(2,1)S(1)}, bf16[4,256,128]{2,1,0:T(8,128)(2,1)S(1)}, u32[]{:S(2)}, u32[]{:S(2)}) %collective-permute-start.12) | collective-permute-done | bytes 262176 | tf_op jit(solution)/shard_map/ppermute | solution.py:47
  43.8 0.2 couple.1.refs_5_
  44.0 0.1 collective-permute-start.13
  44.1 0.0 collective-permute-done.11.other
  44.1 1.3 %extend.1 = (bf16[2048,256]{1,0:T(8,128)(2,1)S(1)}, f32[2048,256]{1,0:T(8,128)S(1)}) custom-call(s32[3]{0:T(128)S(1)} %pad_add_fusion.where.refs_0_, bf16[2048,512]{1,0:T(8,128)(2,1)S(1)} %copy-done, f32[2048,256]{1,0:T(8,128)S(1)} %get-tuple-element.50.partial, bf16[4,256,128]{2,1,0:T(8,128)(2,1)S(1)} %collective-permute-done.11.other), custom_call_target="tpu_custom_call" | custom-call | flops 536870912 | bytes 2097152 | tf_op jit(solution)/shard_map/extend/pallas_call | solution.py:366
  45.4 0.2 collective-permute-done.13.refs_6_
  45.6 4.1 %finish.1 = bf16[2048,1024]{1,0:T(8,128)(2,1)} custom-call(s32[3]{0:T(128)S(1)} %pad_add_fusion.where.refs_0_, bf16[2048,512]{1,0:T(8,128)(2,1)S(1)} %copy-done, bf16[2048,256]{1,0:T(8,128)(2,1)S(1)} %get-tuple-element.52.refs_2_, f32[2048,256]{1,0:T(8,128)S(1)} %get-tuple-element.53.refs_3_, f32[2048,256]{1,0:T(8,128)S(1)} %get-tuple-element.54.refs_4_, ...), custom_call_target="tpu_custom_call" | custom-call | flops 1073741824 | bytes 6291456 | tf_op jit(solution)/shard_map/finish/pallas_call | solution.py:418
  (7 shorter events, 0.2 us)
Async XLA Ops:
  0.1 2.8 %copy-start.1 = (bf16[2048,1024]{1,0:T(8,128)(2,1)S(1)}, bf16[2048,1024]{1,0:T(8,128)(2,1)}, u32[]{:S(2)}) copy-start(bf16[2048,1024]{1,0:T(8,128)(2,1)} %refs_2_.3) | copy-start | bytes 12582916
  2.9 2.4 %copy-start.2 = (f32[1,256,256]{2,1,0:T(8,128)S(1)}, f32[1,256,256]{2,1,0:T(8,128)}, u32[]{:S(2)}) copy-start(f32[1,256,256]{2,1,0:T(8,128)} %param.11) | copy-start | bytes 786436
  4.8 2.6 %collective-permute-start = (bf16[4,256,128]{2,1,0:T(8,128)(2,1)S(1)}, bf16[4,256,128]{2,1,0:T(8,128)(2,1)S(1)}, u32[]{:S(2)}, u32[]{:S(2)}) collective-permute-start(bf16[4,256,128]{2,1,0:T(8,128)(2,1)S(1)} %get-tuple-element.31), channel_id=1, source_target_pairs={{0,1},{1,0},{2,3},{3,2},{4,5},{5,4},{6,7},{7,6},{8,9},{9,8},{10,11... | collective-permute-start | bytes 786440 | tf_op jit(solution)/shard_map/ppermute | solution.py:42
  5.3 5.2 %copy-start.5 = (s32[2]{0:T(128)S(1)}, s32[2]{0:T(128)}, u32[]{:S(2)}) copy-start(s32[2]{0:T(128)} %owners.1) | copy-start | bytes 28
  5.3 5.2 %collective-permute-start.3 = (f32[256,256]{1,0:T(8,128)S(1)}, f32[256,256]{1,0:T(8,128)S(1)}, u32[]{:S(2)}, u32[]{:S(2)}) collective-permute-start(f32[256,256]{1,0:T(8,128)S(1)} %bitcast.4), channel_id=1, source_target_pairs={{0,1},{1,0},{2,3},{3,2},{4,5},{5,4},{6,7},{7,6},{8,9},{9,8},{10,11... | collective-permute-start | bytes 786440 | tf_op jit(solution)/shard_map/ppermute | solution.py:42
  7.5 8.8 %collective-permute-start.2 = (bf16[4,256,128]{2,1,0:T(8,128)(2,1)S(1)}, bf16[4,256,128]{2,1,0:T(8,128)(2,1)S(1)}, u32[]{:S(2)}, u32[]{:S(2)}) collective-permute-start(bf16[4,256,128]{2,1,0:T(8,128)(2,1)S(1)} %add.12.after), channel_id=1, source_target_pairs={{0,2},{1,5},{2,0},{3,7},{4,6},{5,1},{6,4},{7,3},{8,10},{9,13},{10,... | collective-permute-start | bytes 786440 | tf_op jit(solution)/shard_map/ppermute | solution.py:47
  10.5 28.7 %copy-start.3 = (s32[2,256]{1,0:T(2,128)S(1)}, s32[2,256]{1,0:T(2,128)}, u32[]{:S(2)}) copy-start(s32[2,256]{1,0:T(2,128)} %atom_of.1) | copy-start | bytes 6148
  10.5 28.7 %copy-start.4 = (s32[2,4]{1,0:T(2,128)S(1)}, s32[2,4]{1,0:T(2,128)}, u32[]{:S(2)}) copy-start(s32[2,4]{1,0:T(2,128)} %counts.1) | copy-start | bytes 100
  10.5 5.8 %collective-permute-start.1 = (bf16[4,256,128]{2,1,0:T(8,128)(2,1)S(1)}, bf16[4,256,128]{2,1,0:T(8,128)(2,1)S(1)}, u32[]{:S(2)}, u32[]{:S(2)}) collective-permute-start(bf16[4,256,128]{2,1,0:T(8,128)(2,1)S(1)} %get-tuple-element.35), channel_id=1, source_target_pairs={{0,1},{1,0},{2,3},{3,2},{4,5},{5,4},{6,7},{7,6},{8,9},{9,8},{10,11... | collective-permute-start | bytes 786440 | tf_op jit(solution)/shard_map/ppermute | solution.py:42
  11.1 5.1 %collective-permute-start.4 = (bf16[128,256]{1,0:T(8,128)(2,1)S(1)}, bf16[128,256]{1,0:T(8,128)(2,1)S(1)}, u32[]{:S(2)}, u32[]{:S(2)}) collective-permute-start(bf16[128,256]{1,0:T(8,128)(2,1)S(1)} %get-tuple-element.37), channel_id=1, source_target_pairs={{0,2},{1,3},{2,0},{3,1},{4,6},{5,7},{6,4},{7,5},{8,10},{9,11},{10,... | collective-permute-start | bytes 196616 | tf_op jit(solution)/shard_map/ppermute | solution.py:47
  16.2 24.2 %copy-start = (bf16[2048,512]{1,0:T(8,128)(2,1)S(1)}, bf16[2048,512]{1,0:T(8,128)(2,1)}, u32[]{:S(2)}) copy-start(bf16[2048,512]{1,0:T(8,128)(2,1)} %refs_1_.1) | copy-start | bytes 6291460
  16.4 7.3 %collective-permute-start.5 = (bf16[2,256,128]{2,1,0:T(8,128)(2,1)S(1)}, bf16[2,256,128]{2,1,0:T(8,128)(2,1)S(1)}, u32[]{:S(2)}, u32[]{:S(2)}) collective-permute-start(bf16[2,256,128]{2,1,0:T(8,128)(2,1)S(1)} %get-tuple-element.40.after), channel_id=1, source_target_pairs={{0,4},{1,3},{2,6},{3,1},{4,0},{5,7},{6,2},{7,5},{8,12},{9,11},{10,... | collective-permute-start | bytes 393224 | tf_op jit(solution)/shard_map/ppermute | solution.py:47
  18.5 5.2 %collective-permute-start.6 = (bf16[128,256]{1,0:T(8,128)(2,1)S(1)}, bf16[128,256]{1,0:T(8,128)(2,1)S(1)}, u32[]{:S(2)}, u32[]{:S(2)}) collective-permute-start(bf16[128,256]{1,0:T(8,128)(2,1)S(1)} %merge.3.left), channel_id=1, source_target_pairs={{0,8},{1,9},{2,10},{3,11},{4,12},{5,13},{6,14},{7,15},{8,0},{9,1},... | collective-permute-start | bytes 196616 | tf_op jit(solution)/shard_map/ppermute | solution.py:47
  23.7 7.3 %collective-permute-start.7 = (bf16[2,256,128]{2,1,0:T(8,128)(2,1)S(1)}, bf16[2,256,128]{2,1,0:T(8,128)(2,1)S(1)}, u32[]{:S(2)}, u32[]{:S(2)}) collective-permute-start(bf16[2,256,128]{2,1,0:T(8,128)(2,1)S(1)} %get-tuple-element.43.after), channel_id=1, source_target_pairs={{0,8},{1,9},{2,10},{3,11},{4,12},{5,13},{6,14},{7,15},{8,0},{9,1},... | collective-permute-start | bytes 393224 | tf_op jit(solution)/shard_map/ppermute | solution.py:47
  26.4 4.3 %collective-permute-start.8 = (bf16[128,256]{1,0:T(8,128)(2,1)S(1)}, bf16[128,256]{1,0:T(8,128)(2,1)S(1)}, u32[]{:S(2)}, u32[]{:S(2)}) collective-permute-start(bf16[128,256]{1,0:T(8,128)(2,1)S(1)} %merge.4.left), channel_id=1, source_target_pairs={{0,4},{1,5},{2,6},{3,7},{4,0},{5,1},{6,2},{7,3},{8,12},{9,13},{10,... | collective-permute-start | bytes 196616 | tf_op jit(solution)/shard_map/ppermute | solution.py:47
  31.1 6.2 %collective-permute-start.9 = (bf16[2,256,128]{2,1,0:T(8,128)(2,1)S(1)}, bf16[2,256,128]{2,1,0:T(8,128)(2,1)S(1)}, u32[]{:S(2)}, u32[]{:S(2)}) collective-permute-start(bf16[2,256,128]{2,1,0:T(8,128)(2,1)S(1)} %add.13), channel_id=1, source_target_pairs={{0,4},{1,3},{2,6},{3,1},{4,0},{5,7},{6,2},{7,5},{8,12},{9,11},{10,... | collective-permute-start | bytes 393224 | tf_op jit(solution)/shard_map/ppermute | solution.py:47
  32.2 4.3 %collective-permute-start.10 = (bf16[128,256]{1,0:T(8,128)(2,1)S(1)}, bf16[128,256]{1,0:T(8,128)(2,1)S(1)}, u32[]{:S(2)}, u32[]{:S(2)}) collective-permute-start(bf16[128,256]{1,0:T(8,128)(2,1)S(1)} %merge.5.near), channel_id=1, source_target_pairs={{0,2},{1,3},{2,0},{3,1},{4,6},{5,7},{6,4},{7,5},{8,10},{9,11},{10,... | collective-permute-start | bytes 196616 | tf_op jit(solution)/shard_map/ppermute | solution.py:47
  37.3 6.4 %collective-permute-start.12 = (bf16[4,256,128]{2,1,0:T(8,128)(2,1)S(1)}, bf16[4,256,128]{2,1,0:T(8,128)(2,1)S(1)}, u32[]{:S(2)}, u32[]{:S(2)}) collective-permute-start(bf16[4,256,128]{2,1,0:T(8,128)(2,1)S(1)} %pad_maximum_fusion.sums), channel_id=1, source_target_pairs={{0,2},{1,5},{2,0},{3,7},{4,6},{5,1},{6,4},{7,3},{8,10},{9,13},{10,... | collective-permute-start | bytes 786440 | tf_op jit(solution)/shard_map/ppermute | solution.py:47
  41.9 2.2 %collective-permute-start.11 = (bf16[4,256,128]{2,1,0:T(8,128)(2,1)S(1)}, bf16[4,256,128]{2,1,0:T(8,128)(2,1)S(1)}, u32[]{:S(2)}, u32[]{:S(2)}) collective-permute-start(bf16[4,256,128]{2,1,0:T(8,128)(2,1)S(1)} %get-tuple-element.51), channel_id=1, source_target_pairs={{0,1},{1,0},{2,3},{3,2},{4,5},{5,4},{6,7},{7,6},{8,9},{9,8},{10,11... | collective-permute-start | bytes 786440 | tf_op jit(solution)/shard_map/ppermute | solution.py:42
  44.0 1.6 %collective-permute-start.13 = (bf16[4,256,128]{2,1,0:T(8,128)(2,1)S(1)}, bf16[4,256,128]{2,1,0:T(8,128)(2,1)S(1)}, u32[]{:S(2)}, u32[]{:S(2)}) collective-permute-start(bf16[4,256,128]{2,1,0:T(8,128)(2,1)S(1)} %couple.1.refs_5_), channel_id=1, source_target_pairs={{0,1},{1,0},{2,3},{3,2},{4,5},{5,4},{6,7},{7,6},{8,9},{9,8},{10,11... | collective-permute-start | bytes 786440 | tf_op jit(solution)/shard_map/ppermute | solution.py:42

commit v8 on v0

v8 whole, which is shorter than its diff:
```python
import jax
import jax.numpy as jnp
from jax import lax
from jax.experimental import pallas as pl
from jax.experimental.pallas import tpu as pltpu
from jax.sharding import PartitionSpec as P

CHANNELS = 4
CH_CAP = 64
PCAP = 256
LANES = 128
SQUARE = 4
QUARTER = PCAP // SQUARE
ROW_BLOCK = 512
COPY_ROWS = 128
PARAMS = pltpu.CompilerParams(vmem_limit_bytes=40 * 1024 * 1024)
VMEM = pl.BlockSpec(memory_space=pltpu.VMEM)
SMEM = pl.BlockSpec(memory_space=pltpu.SMEM)
HBM = pl.BlockSpec(memory_space=pltpu.HBM)
ANY = pl.BlockSpec(memory_space=pl.ANY)


def block_of(chip, part, entry):
    return chip ^ (part + SQUARE * entry)


def swap(x, distance):
    count = lax.axis_size("pw")
    return lax.ppermute(x, "pw", [(i, i ^ distance) for i in range(count)])


def swap_cores(x):
    return swap(x, 1)


def swap_square(x, part):
    return swap(x, 2 * part)


def load_kernel(where, projectors, flipped, slots, sems):
    core = where[0]
    count = sems.shape[0]
    block = slots.shape[0] // count
    copies = []
    for at in range(count):
        rows = slice(at * block, (at + 1) * block)
        copies.append(pltpu.make_async_copy(projectors.at[rows], slots.at[rows], sems.at[at]))
        copies[-1].start()
    for at, copy in enumerate(copies):
        copy.wait()
        rows = slice(at * block, (at + 1) * block)
        for place, group in enumerate((core, 1 - core)):
            start = pl.multiple_of(group * PCAP, PCAP)
            flipped[place * PCAP : (place + 1) * PCAP, rows] = slots[rows, pl.ds(start, PCAP)].T


def load(where, projectors):
    depth, slots = projectors.shape
    return pl.pallas_call(
        load_kernel,
        in_specs=[SMEM, HBM],
        out_specs=VMEM,
        out_shape=jax.ShapeDtypeStruct((slots, depth), jnp.bfloat16),
        scratch_shapes=[pltpu.VMEM((depth, slots), jnp.bfloat16), pltpu.SemaphoreType.DMA((4,))],
        compiler_params=PARAMS,
        name="load",
    )(where, pltpu.with_memory_space_constraint(projectors, pltpu.HBM))


def project_kernel(parts, where, flipped, columns, theirs, ours):
    chip = where[1]
    for at, part in enumerate(parts):
        starts = [pl.multiple_of(block_of(chip, part, entry) * LANES, LANES) for entry in range(2)]
        pair = jnp.concatenate([columns[:, pl.ds(start, LANES)] for start in starts], axis=1)
        sums = jnp.dot(flipped[...], pair, preferred_element_type=jnp.float32)
        for entry in range(2):
            lanes = slice(entry * LANES, (entry + 1) * LANES)
            ours[2 * at + entry] = sums[:PCAP, lanes]
            theirs[2 * at + entry] = sums[PCAP:, lanes].astype(theirs.dtype)


def project(where, flipped, band_coeffs, parts):
    depth, bands = band_coeffs.shape
    count = 2 * len(parts)

    def kernel(*refs):
        project_kernel(parts, *refs)

    return pl.pallas_call(
        kernel,
        in_specs=[SMEM, VMEM, VMEM],
        out_specs=[VMEM, VMEM],
        out_shape=[
            jax.ShapeDtypeStruct((count, PCAP, LANES), jnp.bfloat16),
            jax.ShapeDtypeStruct((count, PCAP, LANES), jnp.float32),
        ],
        compiler_params=PARAMS,
        cost_estimate=pl.CostEstimate(
            flops=4 * depth * PCAP * count * LANES, bytes_accessed=2 * depth * count * LANES, transcendentals=0
        ),
        name="project",
    )(where, flipped, pltpu.with_memory_space_constraint(band_coeffs, pltpu.VMEM))


def project_plain(where, projectors, band_coeffs, parts):
    depth, bands = band_coeffs.shape
    chips = lax.axis_size("pw") // 2
    blocks = jnp.stack([block_of(where[1], q, r) for q in parts for r in range(chips // SQUARE)])
    columns = jnp.take(band_coeffs.reshape(depth, chips, bands // chips), blocks, axis=1)
    outs = []
    for group, dtype in ((1 - where[0], jnp.bfloat16), (where[0], jnp.float32)):
        slots = lax.dynamic_slice_in_dim(projectors, group * PCAP, PCAP, 1)
        sums = jnp.einsum("ds,dhw->hsw", slots, columns, preferred_element_type=jnp.float32)
        outs.append(sums.astype(dtype))
    return outs


def choose_kernel(where, owners, own, sibling, after, out):
    del after
    core, chip, me = where[0], where[1], where[2]
    owner = jnp.where(core == 0, owners[0], owners[1])
    width = out.shape[2]
    for part in range(SQUARE):
        rows = pl.ds(pl.multiple_of(((chip & 3) ^ part) * QUARTER, QUARTER), QUARTER)
        piece = jnp.where(owner == me, own[rows], jnp.where(owner == (me ^ 1), sibling[rows], 0.0))
        for cut in range(PCAP // width):
            out[part, cut * QUARTER : (cut + 1) * QUARTER] = piece[:, cut * width : (cut + 1) * width].astype(
                out.dtype
            )


def choose(where, owners, own, sibling, width, after):
    return pl.pallas_call(
        choose_kernel,
        in_specs=[SMEM, SMEM, VMEM, VMEM, ANY],
        out_specs=VMEM,
        out_shape=jax.ShapeDtypeStruct((SQUARE, QUARTER * PCAP // width, width), jnp.bfloat16),
        compiler_params=PARAMS,
        name="choose",
    )(where, owners, own, sibling, after)


def pack_kernel(ours, theirs, quarters, *messages):
    entries = ours.shape[0] // len(messages)
    for at, message in enumerate(messages):
        for entry in range(entries):
            place = at * entries + entry
            total = ours[place] + theirs[place].astype(jnp.float32)
            message[entry * PCAP : (entry + 1) * PCAP] = total.astype(message.dtype)
        message[entries * PCAP :] = quarters[at + 1]


def pack(ours, theirs, quarters):
    entries, _, width = ours.shape
    entries //= SQUARE - 1
    shape = jax.ShapeDtypeStruct((entries * PCAP + quarters.shape[1], width), jnp.bfloat16)
    return pl.pallas_call(
        pack_kernel,
        in_specs=[VMEM] * 3,
        out_specs=[VMEM] * (SQUARE - 1),
        out_shape=[shape] * (SQUARE - 1),
        compiler_params=PARAMS,
        name="pack",
    )(ours, theirs, quarters)


def fold_kernel(ours, theirs, quarters, *refs):
    *gots, kept, message = refs
    entries = ours.shape[0]
    for entry in range(entries):
        rows = slice(entry * PCAP, (entry + 1) * PCAP)
        total = ours[entry] + theirs[entry].astype(jnp.float32)
        for got in gots:
            total = total + got[rows].astype(jnp.float32)
        kept[rows] = total
        away = entry ^ 1
        message[away * PCAP : (away + 1) * PCAP] = total.astype(message.dtype)
    table = quarters[0]
    for got in gots:
        table = table + got[entries * PCAP :]
    kept[entries * PCAP :] = table.astype(kept.dtype)
    message[entries * PCAP :] = table


def fold(ours, theirs, quarters, gots):
    shape = gots[0].shape
    return pl.pallas_call(
        fold_kernel,
        in_specs=[VMEM] * (3 + len(gots)),
        out_specs=[VMEM, VMEM],
        out_shape=[jax.ShapeDtypeStruct(shape, jnp.float32), jax.ShapeDtypeStruct(shape, jnp.bfloat16)],
        compiler_params=PARAMS,
        name="fold",
    )(ours, theirs, quarters, *gots)


def add_kernel(left, right, out):
    out[...] = (left[...] + right[...].astype(jnp.float32)).astype(out.dtype)


def add(left, right):
    return pl.pallas_call(
        add_kernel,
        in_specs=[VMEM, VMEM],
        out_specs=VMEM,
        out_shape=jax.ShapeDtypeStruct(left.shape, jnp.bfloat16),
        compiler_params=PARAMS,
        name="add",
    )(left, right)


def mask_kernel(where, counts, atom_of, after, out):
    del after
    core = where[0]
    slot = lax.broadcasted_iota(jnp.int32, (1, PCAP), 1)
    limit = jnp.zeros((1, PCAP), jnp.int32)
    for channel in range(CHANNELS):
        limit = jnp.where(slot >= channel * CH_CAP, channel * CH_CAP + counts[core, channel], limit)
    atoms = jnp.where(core == 0, atom_of[0:1], atom_of[1:2])
    code = jnp.broadcast_to(jnp.where(slot < limit, atoms, -1), (PCAP, PCAP))
    out[...] = jnp.where((code == code.T) & (code >= 0), 1.0, 0.0).astype(out.dtype)


def mask(where, counts, atom_of, after):
    return pl.pallas_call(
        mask_kernel,
        in_specs=[SMEM, SMEM, VMEM, ANY],
        out_specs=VMEM,
        out_shape=jax.ShapeDtypeStruct((PCAP, PCAP), jnp.bfloat16),
        compiler_params=PARAMS,
        name="mask",
    )(where, counts, atom_of, after)


def couple_kernel(where, allowed, *refs):
    *messages, out, coupling = refs
    width = out.shape[2]
    entries = out.shape[0] // SQUARE
    for part, message in enumerate(messages):
        start = pl.multiple_of(((where[1] & 3) ^ part) * QUARTER, QUARTER)
        for cut in range(PCAP // width):
            lanes = slice(cut * width, (cut + 1) * width)
            first = entries * PCAP + cut * QUARTER
            coupling[pl.ds(start, QUARTER), lanes] = (
                message[first : first + QUARTER] * allowed[pl.ds(start, QUARTER), lanes]
            )
    for part, message in enumerate(messages):
        wide = jnp.concatenate([message[e * PCAP : (e + 1) * PCAP] for e in range(entries)], axis=1)
        scaled = jnp.dot(coupling[...], wide, preferred_element_type=jnp.float32).astype(out.dtype)
        for entry in range(entries):
            out[part * entries + entry] = scaled[:, entry * width : (entry + 1) * width]


def couple(where, allowed, messages):
    rows, width = messages[0].shape
    entries = (rows - QUARTER * PCAP // width) // PCAP
    return pl.pallas_call(
        couple_kernel,
        in_specs=[SMEM] + [VMEM] * (1 + SQUARE),
        out_specs=VMEM,
        out_shape=jax.ShapeDtypeStruct((SQUARE * entries, PCAP, width), jnp.bfloat16),
        scratch_shapes=[pltpu.VMEM((PCAP, PCAP), jnp.bfloat16)],
        compiler_params=PARAMS,
        name="couple",
    )(where, allowed, *messages)


def begin_kernel(where, projectors, scaled, *outs):
    slots = pl.ds(pl.multiple_of(where[0] * PCAP, PCAP), PCAP)
    for part, out in enumerate(outs):
        weights = jnp.concatenate([scaled[2 * part], scaled[2 * part + 1]], axis=1)
        for block in range(projectors.shape[0] // ROW_BLOCK):
            rows = slice(block * ROW_BLOCK, (block + 1) * ROW_BLOCK)
            out[rows] = jnp.dot(projectors[rows, slots], weights, preferred_element_type=jnp.float32)


def begin(where, projectors, scaled):
    depth, slots = projectors.shape
    count = SQUARE - 1
    return pl.pallas_call(
        begin_kernel,
        in_specs=[SMEM, VMEM, VMEM],
        out_specs=[VMEM] * count,
        out_shape=[jax.ShapeDtypeStruct((depth, 2 * LANES), jnp.float32)] * count,
        compiler_params=PARAMS,
        cost_estimate=pl.CostEstimate(
            flops=2 * depth * slots * LANES * count, bytes_accessed=2 * depth * slots, transcendentals=0
        ),
        name="begin",
    )(where, projectors, scaled)


def finish_kernel(where, projectors, mine, other, *refs):
    *begun, out, weights, blocks, sems = refs
    core, chip = where[0], where[1]
    last = 2 * len(begun)
    for part, group in ((mine, core), (other, 1 - core)):
        rows = pl.ds(pl.multiple_of(group * PCAP, PCAP), PCAP)
        weights[rows, :LANES] = part[last]
        weights[rows, LANES:] = part[last + 1]
    slots = pl.ds(pl.multiple_of((1 - core) * PCAP, PCAP), PCAP)
    copies = []

    def put(rows, part, sums):
        for entry in range(2):
            start = pl.multiple_of(block_of(chip, part, entry) * LANES, LANES)
            blocks[rows, pl.ds(start, LANES)] = sums[:, entry * LANES : (entry + 1) * LANES].astype(blocks.dtype)

    for block in range(projectors.shape[0] // ROW_BLOCK):
        rows = slice(block * ROW_BLOCK, (block + 1) * ROW_BLOCK)
        put(rows, len(begun), jnp.dot(projectors[rows], weights[...], preferred_element_type=jnp.float32))
        for part, partial in enumerate(begun):
            pair = jnp.concatenate([other[2 * part], other[2 * part + 1]], axis=1)
            sums = jnp.dot(projectors[rows, slots], pair, preferred_element_type=jnp.float32)
            put(rows, part, partial[rows] + sums)
        for piece in range(ROW_BLOCK // COPY_ROWS):
            start = block * ROW_BLOCK + piece * COPY_ROWS
            written = slice(start, start + COPY_ROWS)
            copies.append(pltpu.make_async_copy(blocks.at[written], out.at[written], sems.at[len(copies)]))
            copies[-1].start()
    for copy in copies:
        copy.wait()


def finish(where, projectors, mine, other, begun):
    depth, slots = projectors.shape
    bands = mine.shape[0] * LANES
    return pl.pallas_call(
        finish_kernel,
        in_specs=[SMEM] + [VMEM] * (3 + len(begun)),
        out_specs=HBM,
        out_shape=jax.ShapeDtypeStruct((depth, bands), jnp.bfloat16),
        scratch_shapes=[
            pltpu.VMEM((slots, 2 * LANES), jnp.bfloat16),
            pltpu.VMEM((depth, bands), jnp.bfloat16),
            pltpu.SemaphoreType.DMA((depth // COPY_ROWS,)),
        ],
        compiler_params=PARAMS,
        cost_estimate=pl.CostEstimate(
            flops=depth * slots * bands, bytes_accessed=2 * depth * (slots + bands), transcendentals=0
        ),
        name="finish",
    )(where, projectors, mine, other, *begun)


def apply_plain(where, projectors, mine, other):
    chips, _, width = mine.shape
    blocks = jnp.stack([block_of(where[1], q, r) for q in range(SQUARE) for r in range(chips // SQUARE)])
    rows = []
    for group in range(2):
        part = jnp.where(where[0] == group, mine, other)
        part = jnp.zeros_like(part).at[blocks].set(part)
        rows.append(part.transpose(1, 0, 2).reshape(PCAP, chips * width))
    return jnp.dot(projectors, jnp.concatenate(rows), preferred_element_type=jnp.float32).astype(jnp.bfloat16)


def local(band_coeffs, projectors, counts, atom_of, owners, couplings):
    chips = lax.axis_size("pw") // 2
    entries = chips // SQUARE
    width = band_coeffs.shape[1] // chips
    fast = width == LANES and entries == 2
    me = lax.axis_index("pw")
    where = jnp.stack([me % 2, me // 2, me])

    own_table = couplings[0]
    sibling_table = swap_cores(own_table)
    sent, kept = tuple(range(1, SQUARE)), (0,)
    if fast:
        flipped = load(where, projectors)
        theirs, ours = project(where, flipped, band_coeffs, sent)
        low_theirs, low_ours = project(where, flipped, band_coeffs, kept)
    else:
        theirs, ours = project_plain(where, projectors, band_coeffs, sent)
        low_theirs, low_ours = project_plain(where, projectors, band_coeffs, kept)
    quarters = choose(where, owners, own_table, sibling_table, width, ours)
    theirs, low_ours = lax.optimization_barrier((swap_cores(theirs), low_ours))
    messages = pack(ours, theirs, quarters)
    low_theirs = swap_cores(low_theirs)
    gots = [swap_square(message, part) for message, part in zip(messages, sent)]
    allowed = mask(where, counts, atom_of, messages[0])

    total, message = fold(low_ours, low_theirs, quarters, gots)
    mine = add(total, swap_square(message, SQUARE))
    distance = 2 * SQUARE
    while distance < chips:
        body = mine[: entries * PCAP].reshape(entries, PCAP, width)
        order = [entry ^ (distance // SQUARE) for entry in range(entries)]
        message = jnp.concatenate([body[jnp.array(order)].reshape(-1, width), mine[entries * PCAP :]])
        mine = add(mine.astype(jnp.float32), swap_square(message, distance))
        distance *= 2

    gathered = [mine] + [swap_square(mine, part) for part in sent]
    scaled = couple(where, allowed, gathered)
    other = swap_cores(scaled)
    if not fast:
        return apply_plain(where, projectors, scaled, other)
    return finish(where, projectors, scaled, other, begin(where, projectors, scaled))


def solution(mesh):
    placed = (
        P("pw", "group"),
        P("pw", "group"),
        P("group", None),
        P("group", None),
        P("group"),
        P("pw", "group", None),
    )
    return jax.shard_map(
        local, mesh=mesh, in_specs=placed, out_specs=P("pw", "group"), check_vma=False
    )
```

time: 137 us -> 48.3 us (0.35)
  waiting for transfers between devices: 104 us -> 21.9 us
  Pallas kernels: 0 us -> 14.6 us
  between operations: 14.7 us -> 0.11 us
  matrix products: 14.5 us -> 0 us
  starting transfers between devices: 0.01 us -> 11.4 us
  other arithmetic: 2.59 us -> 0.08 us
    psum x1 -> x0, waiting for transfers between devices: 104 us -> none  [local(): proj_sums = lax.psum(partial_proj, 'pw')]
    ppermute x0 -> x11, waiting for transfers between devices: none -> 21.9 us  [swap(): return lax.ppermute(x, 'pw', [(i, i ^ distance) for i in range(count)])]
    pallas_call x0 -> x11, Pallas kernels: none -> 14.6 us  [the longest x1 4.29 us: finish(): pl.pallas_call(finish_kernel, in_specs=[SMEM] + [VMEM] * (3 + len(begun))...]
    dot_general x3 -> x0, matrix products: 14.5 us -> none  [the longest x1 6.49 us: local(): lax.dot_general(masked_proj, band_coeffs, (((0,), (0,)), ((), ())), prefe...]
    ppermute x0 -> x11, starting transfers between devices: none -> 11.4 us  [swap(): return lax.ppermute(x, 'pw', [(i, i ^ distance) for i in range(count)])]
    select_n x3 -> x0, other arithmetic: 1.81 us -> none  [the longest x1 1.8 us: from_root(): return lax.psum(jnp.where(mine, x, jnp.zeros_like(x)), axis)]
  transfers between devices with their start and end apart: 1 -> 11, of which waited for: 1 -> 9; matrix products, arithmetic and copies ran while one was open for 0% -> 0% of each run, Pallas kernels for 0% -> 8%
where the time goes in v8:
time: 48.3 us; the launch traced here: 48.2 us
  waiting for transfers between devices  21.9 us (45%)
  Pallas kernels  14.6 us (30%)
  starting transfers between devices  11.4 us (24%)
    ppermute x11, waiting for transfers between devices, swap(): return lax.ppermute(x, 'pw', [(i, i ^ distance) for i in range(count)])  21.9 us
    ppermute x11, starting transfers between devices, swap(): return lax.ppermute(x, 'pw', [(i, i ^ distance) for i in range(count)])  11.4 us
    pallas_call x1, Pallas kernels, finish(): pl.pallas_call(finish_kernel, in_specs=[SMEM] + [VMEM] * (3 + len(begun))...  4.29 us
    pallas_call x2, Pallas kernels, project(): pl.pallas_call(kernel, in_specs=[SMEM, VMEM, VMEM], out_specs=[VMEM, VMEM...  3.79 us
    pallas_call x1, Pallas kernels, load(): pl.pallas_call(load_kernel, in_specs=[SMEM, HBM], out_specs=VMEM, out_sha...  2.68 us
    pallas_call x1, Pallas kernels, begin(): pl.pallas_call(begin_kernel, in_specs=[SMEM, VMEM, VMEM], out_specs=[VMEM...  1.52 us
  transfers between devices with their start and end apart: 11, of which 9 were waited for; matrix products, arithmetic and copies ran while one was open for 0% of the time, Pallas kernels for 8%

profile of v8, /device:TPU:0, one launch (start us, length us, event | category | flops | bytes accessed | tf_op | source)
XLA Modules:
  0.0 48.2 jit_solution(14530332972805705680)
XLA Ops:
  0.0 0.1 pad_add_fusion.where.refs_0_
  0.1 0.0 copy-start
  0.1 2.7 %load.1.refs_1_ = bf16[512,2048]{1,0:T(8,128)(2,1)S(1)} custom-call(s32[3]{0:T(128)S(1)} %pad_add_fusion.where.refs_0_, bf16[2048,512]{1,0:T(8,128)(2,1)} %projectors.5), custom_call_target="tpu_custom_call" | custom-call | tf_op jit(solution)/shard_map/load/pallas_call | solution.py:59
  2.8 0.1 copy-done
  2.9 0.0 copy-start.2
  2.9 2.5 %project.2 = (bf16[6,256,128]{2,1,0:T(8,128)(2,1)S(1)}, f32[6,256,128]{2,1,0:T(8,128)S(1)}) custom-call(s32[3]{0:T(128)S(1)} %pad_add_fusion.where.refs_0_, bf16[512,2048]{1,0:T(8,128)(2,1)S(1)} %load.1.refs_1_, bf16[2048,1024]{1,0:T(8,128)(2,1)S(1)} %copy-done), custom_call_target="tpu_custom_call" | custom-call | flops 1610612736 | bytes 3145728 | tf_op jit(solution)/shard_map/project/pallas_call | solution.py:89
  5.4 0.5 %collective-permute-start = (bf16[6,256,128]{2,1,0:T(8,128)(2,1)S(1)}, bf16[6,256,128]{2,1,0:T(8,128)(2,1)S(1)}, u32[]{:S(2)}, u32[]{:S(2)}) collective-permute-start(bf16[6,256,128]{2,1,0:T(8,128)(2,1)S(1)} %get-tuple-element.20), channel_id=1, source_target_pairs={{0,1},{1,0},{2,3},{3,2},{4,5},{5,4},{6,7},{7,6},{8,9},{9,8},{10,11... | collective-permute-start | bytes 1179656 | tf_op jit(solution)/shard_map/ppermute | solution.py:29
  5.9 0.0 copy-done.2
  5.9 0.0 copy-start.5
  5.9 0.1 collective-permute-start.1
  6.0 1.3 %project.3 = (bf16[2,256,128]{2,1,0:T(8,128)(2,1)S(1)}, f32[2,256,128]{2,1,0:T(8,128)S(1)}) custom-call(s32[3]{0:T(128)S(1)} %pad_add_fusion.where.refs_0_, bf16[512,2048]{1,0:T(8,128)(2,1)S(1)} %load.1.refs_1_, bf16[2048,1024]{1,0:T(8,128)(2,1)S(1)} %copy-done), custom_call_target="tpu_custom_call" | custom-call | flops 536870912 | bytes 1048576 | tf_op jit(solution)/shard_map/project/pallas_call | solution.py:89
  7.3 0.3 collective-permute-done.1.sibling
  7.6 0.0 copy-done.5
  7.6 0.0 copy-start.3
  7.6 0.0 copy-start.4
  7.6 0.6 %choose.1.quarters = bf16[4,128,128]{2,1,0:T(8,128)(2,1)S(1)} custom-call(s32[3]{0:T(128)S(1)} %pad_add_fusion.where.refs_0_, s32[2]{0:T(128)S(1)} %copy-done.5, f32[256,256]{1,0:T(8,128)S(1)} %bitcast.5, f32[256,256]{1,0:T(8,128)S(1)} %collective-permute-done.1.sibling, f32[6,256,128]{2,1,0:T(8,128)S(1)} %get-tuple-element.19.after.ours), custom_call_target="tpu_custom_call" | custom-call | tf_op jit(solution)/shard_map/choose/pallas_call | solution.py:133
  8.2 0.0 collective-permute-done.theirs
  8.2 0.0 copy-start.1
  8.2 0.1 pack.1
  8.3 3.0 %collective-permute-start.4 = (bf16[640,128]{1,0:T(8,128)(2,1)S(1)}, bf16[640,128]{1,0:T(8,128)(2,1)S(1)}, u32[]{:S(2)}, u32[]{:S(2)}) collective-permute-start(bf16[640,128]{1,0:T(8,128)(2,1)S(1)} %get-tuple-element.26), channel_id=1, source_target_pairs={{0,4},{1,5},{2,6},{3,7},{4,0},{5,1},{6,2},{7,3},{8,12},{9,13},{10,... | collective-permute-start | bytes 491528 | tf_op jit(solution)/shard_map/ppermute | solution.py:29
  11.3 1.4 %collective-permute-start.5 = (bf16[640,128]{1,0:T(8,128)(2,1)S(1)}, bf16[640,128]{1,0:T(8,128)(2,1)S(1)}, u32[]{:S(2)}, u32[]{:S(2)}) collective-permute-start(bf16[640,128]{1,0:T(8,128)(2,1)S(1)} %get-tuple-element.27), channel_id=1, source_target_pairs={{0,6},{1,7},{2,4},{3,5},{4,2},{5,3},{6,0},{7,1},{8,14},{9,15},{10,... | collective-permute-start | bytes 491528 | tf_op jit(solution)/shard_map/ppermute | solution.py:29
  12.7 0.1 collective-permute-start.3
  12.8 0.0 collective-permute-start.2
  12.8 1.3 %collective-permute-done.2.theirs = bf16[2,256,128]{2,1,0:T(8,128)(2,1)S(1)} collective-permute-done((bf16[2,256,128]{2,1,0:T(8,128)(2,1)S(1)}, bf16[2,256,128]{2,1,0:T(8,128)(2,1)S(1)}, u32[]{:S(2)}, u32[]{:S(2)}) %collective-permute-start.2) | collective-permute-done | bytes 131104 | tf_op jit(solution)/shard_map/ppermute | solution.py:29
  14.2 2.1 %collective-permute-done.4.refs_1_ = bf16[640,128]{1,0:T(8,128)(2,1)S(1)} collective-permute-done((bf16[640,128]{1,0:T(8,128)(2,1)S(1)}, bf16[640,128]{1,0:T(8,128)(2,1)S(1)}, u32[]{:S(2)}, u32[]{:S(2)}) %collective-permute-start.4) | collective-permute-done | bytes 163872 | tf_op jit(solution)/shard_map/ppermute | solution.py:29
  16.3 4.3 %collective-permute-done.5.refs_2_ = bf16[640,128]{1,0:T(8,128)(2,1)S(1)} collective-permute-done((bf16[640,128]{1,0:T(8,128)(2,1)S(1)}, bf16[640,128]{1,0:T(8,128)(2,1)S(1)}, u32[]{:S(2)}, u32[]{:S(2)}) %collective-permute-start.5) | collective-permute-done | bytes 163872 | tf_op jit(solution)/shard_map/ppermute | solution.py:29
  20.6 1.4 %collective-permute-done.3.refs_0_ = bf16[640,128]{1,0:T(8,128)(2,1)S(1)} collective-permute-done((bf16[640,128]{1,0:T(8,128)(2,1)S(1)}, bf16[640,128]{1,0:T(8,128)(2,1)S(1)}, u32[]{:S(2)}, u32[]{:S(2)}) %collective-permute-start.3) | collective-permute-done | bytes 163872 | tf_op jit(solution)/shard_map/ppermute | solution.py:29
  21.9 0.1 fold.1
  22.0 2.6 %collective-permute-start.6 = (bf16[640,128]{1,0:T(8,128)(2,1)S(1)}, bf16[640,128]{1,0:T(8,128)(2,1)S(1)}, u32[]{:S(2)}, u32[]{:S(2)}) collective-permute-start(bf16[640,128]{1,0:T(8,128)(2,1)S(1)} %get-tuple-element.29), channel_id=1, source_target_pairs={{0,8},{1,9},{2,10},{3,11},{4,12},{5,13},{6,14},{7,15},{8,0},{9,1},... | collective-permute-start | bytes 491528 | tf_op jit(solution)/shard_map/ppermute | solution.py:29
  24.7 5.8 %collective-permute-done.6.right = bf16[640,128]{1,0:T(8,128)(2,1)S(1)} collective-permute-done((bf16[640,128]{1,0:T(8,128)(2,1)S(1)}, bf16[640,128]{1,0:T(8,128)(2,1)S(1)}, u32[]{:S(2)}, u32[]{:S(2)}) %collective-permute-start.6) | collective-permute-done | bytes 163872 | tf_op jit(solution)/shard_map/ppermute | solution.py:29
  30.5 0.7 %collective-permute-start.9 = (bf16[640,128]{1,0:T(8,128)(2,1)S(1)}, bf16[640,128]{1,0:T(8,128)(2,1)S(1)}, u32[]{:S(2)}, u32[]{:S(2)}) collective-permute-start(bf16[640,128]{1,0:T(8,128)(2,1)S(1)} %add.11.refs_0_), channel_id=1, source_target_pairs={{0,6},{1,7},{2,4},{3,5},{4,2},{5,3},{6,0},{7,1},{8,14},{9,15},{10,... | collective-permute-start | bytes 491528 | tf_op jit(solution)/shard_map/ppermute | solution.py:29
  31.2 2.4 %collective-permute-start.8 = (bf16[640,128]{1,0:T(8,128)(2,1)S(1)}, bf16[640,128]{1,0:T(8,128)(2,1)S(1)}, u32[]{:S(2)}, u32[]{:S(2)}) collective-permute-start(bf16[640,128]{1,0:T(8,128)(2,1)S(1)} %add.11.refs_0_), channel_id=1, source_target_pairs={{0,4},{1,5},{2,6},{3,7},{4,0},{5,1},{6,2},{7,3},{8,12},{9,13},{10,... | collective-permute-start | bytes 491528 | tf_op jit(solution)/shard_map/ppermute | solution.py:29
  33.6 0.5 %collective-permute-start.7 = (bf16[640,128]{1,0:T(8,128)(2,1)S(1)}, bf16[640,128]{1,0:T(8,128)(2,1)S(1)}, u32[]{:S(2)}, u32[]{:S(2)}) collective-permute-start(bf16[640,128]{1,0:T(8,128)(2,1)S(1)} %add.11.refs_0_), channel_id=1, source_target_pairs={{0,2},{1,3},{2,0},{3,1},{4,6},{5,7},{6,4},{7,5},{8,10},{9,11},{10,... | collective-permute-start | bytes 491528 | tf_op jit(solution)/shard_map/ppermute | solution.py:29
  34.1 0.0 copy-done.3
  34.1 0.0 copy-done.4
  34.1 0.7 %mask.1.allowed = bf16[256,256]{1,0:T(8,128)(2,1)S(1)} custom-call(s32[3]{0:T(128)S(1)} %pad_add_fusion.where.refs_0_, s32[2,4]{1,0:T(2,128)S(1)} %copy-done.4, s32[2,256]{1,0:T(2,128)S(1)} %copy-done.3, bf16[640,128]{1,0:T(8,128)(2,1)S(1)} %get-tuple-element.23.after), custom_call_target="tpu_custom_call" | custom-call | tf_op jit(solution)/shard_map/mask/pallas_call | solution.py:225
  34.8 2.9 %collective-permute-done.9.refs_3_ = bf16[640,128]{1,0:T(8,128)(2,1)S(1)} collective-permute-done((bf16[640,128]{1,0:T(8,128)(2,1)S(1)}, bf16[640,128]{1,0:T(8,128)(2,1)S(1)}, u32[]{:S(2)}, u32[]{:S(2)}) %collective-permute-start.9) | collective-permute-done | bytes 163872 | tf_op jit(solution)/shard_map/ppermute | solution.py:29
  37.7 3.4 %collective-permute-done.8.refs_2_ = bf16[640,128]{1,0:T(8,128)(2,1)S(1)} collective-permute-done((bf16[640,128]{1,0:T(8,128)(2,1)S(1)}, bf16[640,128]{1,0:T(8,128)(2,1)S(1)}, u32[]{:S(2)}, u32[]{:S(2)}) %collective-permute-start.8) | collective-permute-done | bytes 163872 | tf_op jit(solution)/shard_map/ppermute | solution.py:29
  41.0 0.0 collective-permute-done.7.refs_1_
  41.0 0.9 %couple.1.scaled.mine = bf16[8,256,128]{2,1,0:T(8,128)(2,1)S(1)} custom-call(s32[3]{0:T(128)S(1)} %pad_add_fusion.where.refs_0_, bf16[256,256]{1,0:T(8,128)(2,1)S(1)} %mask.1.allowed, bf16[640,128]{1,0:T(8,128)(2,1)S(1)} %add.11.refs_0_, bf16[640,128]{1,0:T(8,128)(2,1)S(1)} %collective-permute-done.7.refs_1_, ...), custom_call_target="tpu_custom_call" | custom-call | tf_op jit(solution)/shard_map/couple/pallas_call | solution.py:257
  41.9 0.1 collective-permute-start.10
  42.0 0.0 copy-done.1
  42.0 1.5 %begin.1 = (f32[2048,256]{1,0:T(8,128)S(1)}, f32[2048,256]{1,0:T(8,128)S(1)}, f32[2048,256]{1,0:T(8,128)S(1)}) custom-call(s32[3]{0:T(128)S(1)} %pad_add_fusion.where.refs_0_, bf16[2048,512]{1,0:T(8,128)(2,1)S(1)} %copy-done.1, bf16[8,256,128]{2,1,0:T(8,128)(2,1)S(1)} %couple.1.scaled.mine), custom_call_target="tpu_custom_call" | custom-call | flops 805306368 | bytes 2097152 | tf_op jit(solution)/shard_map/begin/pallas_call | solution.py:280
  43.5 0.4 collective-permute-done.10.other
  43.9 4.3 %finish.1 = bf16[2048,1024]{1,0:T(8,128)(2,1)} custom-call(s32[3]{0:T(128)S(1)} %pad_add_fusion.where.refs_0_, bf16[2048,512]{1,0:T(8,128)(2,1)S(1)} %copy-done.1, bf16[8,256,128]{2,1,0:T(8,128)(2,1)S(1)} %couple.1.scaled.mine, bf16[8,256,128]{2,1,0:T(8,128)(2,1)S(1)} %collective-permute-done.10.other, f32[2048,256]{1,0:T(8,128)S(1)} %get-tuple-element.30.refs_0_, ...), custom_call_target="tpu_custom_call" | custom-call | flops 1073741824 | bytes 6291456 | tf_op jit(solution)/shard_map/finish/pallas_call | solution.py:328
  (1 shorter events, 0.0 us)
Async XLA Ops:
  0.1 2.8 %copy-start = (bf16[2048,1024]{1,0:T(8,128)(2,1)S(1)}, bf16[2048,1024]{1,0:T(8,128)(2,1)}, u32[]{:S(2)}) copy-start(bf16[2048,1024]{1,0:T(8,128)(2,1)} %refs_2_.3) | copy-start | bytes 12582916
  2.9 3.0 %copy-start.2 = (f32[1,256,256]{2,1,0:T(8,128)S(1)}, f32[1,256,256]{2,1,0:T(8,128)}, u32[]{:S(2)}) copy-start(f32[1,256,256]{2,1,0:T(8,128)} %param.11) | copy-start | bytes 786436
  5.4 2.8 %collective-permute-start = (bf16[6,256,128]{2,1,0:T(8,128)(2,1)S(1)}, bf16[6,256,128]{2,1,0:T(8,128)(2,1)S(1)}, u32[]{:S(2)}, u32[]{:S(2)}) collective-permute-start(bf16[6,256,128]{2,1,0:T(8,128)(2,1)S(1)} %get-tuple-element.20), channel_id=1, source_target_pairs={{0,1},{1,0},{2,3},{3,2},{4,5},{5,4},{6,7},{7,6},{8,9},{9,8},{10,11... | collective-permute-start | bytes 1179656 | tf_op jit(solution)/shard_map/ppermute | solution.py:29
  5.9 1.7 %copy-start.5 = (s32[2]{0:T(128)S(1)}, s32[2]{0:T(128)}, u32[]{:S(2)}) copy-start(s32[2]{0:T(128)} %owners.1) | copy-start | bytes 28
  5.9 1.7 %collective-permute-start.1 = (f32[256,256]{1,0:T(8,128)S(1)}, f32[256,256]{1,0:T(8,128)S(1)}, u32[]{:S(2)}, u32[]{:S(2)}) collective-permute-start(f32[256,256]{1,0:T(8,128)S(1)} %bitcast.4), channel_id=1, source_target_pairs={{0,1},{1,0},{2,3},{3,2},{4,5},{5,4},{6,7},{7,6},{8,9},{9,8},{10,11... | collective-permute-start | bytes 786440 | tf_op jit(solution)/shard_map/ppermute | solution.py:29
  7.6 26.5 %copy-start.3 = (s32[2,256]{1,0:T(2,128)S(1)}, s32[2,256]{1,0:T(2,128)}, u32[]{:S(2)}) copy-start(s32[2,256]{1,0:T(2,128)} %atom_of.1) | copy-start | bytes 6148
  7.6 26.5 %copy-start.4 = (s32[2,4]{1,0:T(2,128)S(1)}, s32[2,4]{1,0:T(2,128)}, u32[]{:S(2)}) copy-start(s32[2,4]{1,0:T(2,128)} %counts.1) | copy-start | bytes 100
  8.2 33.8 %copy-start.1 = (bf16[2048,512]{1,0:T(8,128)(2,1)S(1)}, bf16[2048,512]{1,0:T(8,128)(2,1)}, u32[]{:S(2)}) copy-start(bf16[2048,512]{1,0:T(8,128)(2,1)} %projectors.5) | copy-start | bytes 6291460
  8.3 8.0 %collective-permute-start.4 = (bf16[640,128]{1,0:T(8,128)(2,1)S(1)}, bf16[640,128]{1,0:T(8,128)(2,1)S(1)}, u32[]{:S(2)}, u32[]{:S(2)}) collective-permute-start(bf16[640,128]{1,0:T(8,128)(2,1)S(1)} %get-tuple-element.26), channel_id=1, source_target_pairs={{0,4},{1,5},{2,6},{3,7},{4,0},{5,1},{6,2},{7,3},{8,12},{9,13},{10,... | collective-permute-start | bytes 491528 | tf_op jit(solution)/shard_map/ppermute | solution.py:29
  11.3 9.3 %collective-permute-start.5 = (bf16[640,128]{1,0:T(8,128)(2,1)S(1)}, bf16[640,128]{1,0:T(8,128)(2,1)S(1)}, u32[]{:S(2)}, u32[]{:S(2)}) collective-permute-start(bf16[640,128]{1,0:T(8,128)(2,1)S(1)} %get-tuple-element.27), channel_id=1, source_target_pairs={{0,6},{1,7},{2,4},{3,5},{4,2},{5,3},{6,0},{7,1},{8,14},{9,15},{10,... | collective-permute-start | bytes 491528 | tf_op jit(solution)/shard_map/ppermute | solution.py:29
  12.7 9.2 %collective-permute-start.3 = (bf16[640,128]{1,0:T(8,128)(2,1)S(1)}, bf16[640,128]{1,0:T(8,128)(2,1)S(1)}, u32[]{:S(2)}, u32[]{:S(2)}) collective-permute-start(bf16[640,128]{1,0:T(8,128)(2,1)S(1)} %get-tuple-element.23.after), channel_id=1, source_target_pairs={{0,2},{1,3},{2,0},{3,1},{4,6},{5,7},{6,4},{7,5},{8,10},{9,11},{10,... | collective-permute-start | bytes 491528 | tf_op jit(solution)/shard_map/ppermute | solution.py:29
  12.8 1.3 %collective-permute-start.2 = (bf16[2,256,128]{2,1,0:T(8,128)(2,1)S(1)}, bf16[2,256,128]{2,1,0:T(8,128)(2,1)S(1)}, u32[]{:S(2)}, u32[]{:S(2)}) collective-permute-start(bf16[2,256,128]{2,1,0:T(8,128)(2,1)S(1)} %get-tuple-element.25), channel_id=1, source_target_pairs={{0,1},{1,0},{2,3},{3,2},{4,5},{5,4},{6,7},{7,6},{8,9},{9,8},{10,11... | collective-permute-start | bytes 393224 | tf_op jit(solution)/shard_map/ppermute | solution.py:29
  22.0 8.5 %collective-permute-start.6 = (bf16[640,128]{1,0:T(8,128)(2,1)S(1)}, bf16[640,128]{1,0:T(8,128)(2,1)S(1)}, u32[]{:S(2)}, u32[]{:S(2)}) collective-permute-start(bf16[640,128]{1,0:T(8,128)(2,1)S(1)} %get-tuple-element.29), channel_id=1, source_target_pairs={{0,8},{1,9},{2,10},{3,11},{4,12},{5,13},{6,14},{7,15},{8,0},{9,1},... | collective-permute-start | bytes 491528 | tf_op jit(solution)/shard_map/ppermute | solution.py:29
  30.5 7.2 %collective-permute-start.9 = (bf16[640,128]{1,0:T(8,128)(2,1)S(1)}, bf16[640,128]{1,0:T(8,128)(2,1)S(1)}, u32[]{:S(2)}, u32[]{:S(2)}) collective-permute-start(bf16[640,128]{1,0:T(8,128)(2,1)S(1)} %add.11.refs_0_), channel_id=1, source_target_pairs={{0,6},{1,7},{2,4},{3,5},{4,2},{5,3},{6,0},{7,1},{8,14},{9,15},{10,... | collective-permute-start | bytes 491528 | tf_op jit(solution)/shard_map/ppermute | solution.py:29
  31.2 9.8 %collective-permute-start.8 = (bf16[640,128]{1,0:T(8,128)(2,1)S(1)}, bf16[640,128]{1,0:T(8,128)(2,1)S(1)}, u32[]{:S(2)}, u32[]{:S(2)}) collective-permute-start(bf16[640,128]{1,0:T(8,128)(2,1)S(1)} %add.11.refs_0_), channel_id=1, source_target_pairs={{0,4},{1,5},{2,6},{3,7},{4,0},{5,1},{6,2},{7,3},{8,12},{9,13},{10,... | collective-permute-start | bytes 491528 | tf_op jit(solution)/shard_map/ppermute | solution.py:29
  33.6 7.5 %collective-permute-start.7 = (bf16[640,128]{1,0:T(8,128)(2,1)S(1)}, bf16[640,128]{1,0:T(8,128)(2,1)S(1)}, u32[]{:S(2)}, u32[]{:S(2)}) collective-permute-start(bf16[640,128]{1,0:T(8,128)(2,1)S(1)} %add.11.refs_0_), channel_id=1, source_target_pairs={{0,2},{1,3},{2,0},{3,1},{4,6},{5,7},{6,4},{7,5},{8,10},{9,11},{10,... | collective-permute-start | bytes 491528 | tf_op jit(solution)/shard_map/ppermute | solution.py:29
  41.9 2.0 %collective-permute-start.10 = (bf16[8,256,128]{2,1,0:T(8,128)(2,1)S(1)}, bf16[8,256,128]{2,1,0:T(8,128)(2,1)S(1)}, u32[]{:S(2)}, u32[]{:S(2)}) collective-permute-start(bf16[8,256,128]{2,1,0:T(8,128)(2,1)S(1)} %couple.1.scaled.mine), channel_id=1, source_target_pairs={{0,1},{1,0},{2,3},{3,2},{4,5},{5,4},{6,7},{7,6},{8,9},{9,8},{10,11... | collective-permute-start | bytes 1572872 | tf_op jit(solution)/shard_map/ppermute | solution.py:29

commit v9 on v8

v9 whole, which is shorter than its diff:
```python
import jax
import jax.numpy as jnp
from jax import lax
from jax.experimental import pallas as pl
from jax.experimental.pallas import tpu as pltpu
from jax.sharding import PartitionSpec as P

CHANNELS = 4
CH_CAP = 64
PCAP = 256
LANES = 128
SQUARE = 4
QUARTER = PCAP // SQUARE
ROW_BLOCK = 512
COPY_ROWS = 128
PARAMS = pltpu.CompilerParams(vmem_limit_bytes=40 * 1024 * 1024)
VMEM = pl.BlockSpec(memory_space=pltpu.VMEM)
SMEM = pl.BlockSpec(memory_space=pltpu.SMEM)
HBM = pl.BlockSpec(memory_space=pltpu.HBM)
ANY = pl.BlockSpec(memory_space=pl.ANY)


def block_of(chip, part, entry):
    return chip ^ (part + SQUARE * entry)


def swap(x, distance):
    count = lax.axis_size("pw")
    return lax.ppermute(x, "pw", [(i, i ^ distance) for i in range(count)])


def swap_cores(x):
    return swap(x, 1)


def swap_square(x, part):
    return swap(x, 2 * part)


def load_kernel(where, projectors, flipped, slots, sems):
    core = where[0]
    count = sems.shape[0]
    block = slots.shape[0] // count
    copies = []
    for at in range(count):
        rows = slice(at * block, (at + 1) * block)
        copies.append(pltpu.make_async_copy(projectors.at[rows], slots.at[rows], sems.at[at]))
        copies[-1].start()
    for at, copy in enumerate(copies):
        copy.wait()
        rows = slice(at * block, (at + 1) * block)
        for place, group in enumerate((core, 1 - core)):
            start = pl.multiple_of(group * PCAP, PCAP)
            flipped[place * PCAP : (place + 1) * PCAP, rows] = slots[rows, pl.ds(start, PCAP)].T


def load(where, projectors):
    depth, slots = projectors.shape
    return pl.pallas_call(
        load_kernel,
        in_specs=[SMEM, HBM],
        out_specs=VMEM,
        out_shape=jax.ShapeDtypeStruct((slots, depth), jnp.bfloat16),
        scratch_shapes=[pltpu.VMEM((depth, slots), jnp.bfloat16), pltpu.SemaphoreType.DMA((4,))],
        compiler_params=PARAMS,
        name="load",
    )(where, pltpu.with_memory_space_constraint(projectors, pltpu.HBM))


def project_kernel(parts, where, flipped, columns, theirs, ours):
    chip = where[1]
    for at, part in enumerate(parts):
        starts = [pl.multiple_of(block_of(chip, part, entry) * LANES, LANES) for entry in range(2)]
        pair = jnp.concatenate([columns[:, pl.ds(start, LANES)] for start in starts], axis=1)
        sums = jnp.dot(flipped[...], pair, preferred_element_type=jnp.float32)
        for entry in range(2):
            lanes = slice(entry * LANES, (entry + 1) * LANES)
            ours[2 * at + entry] = sums[:PCAP, lanes]
            theirs[2 * at + entry] = sums[PCAP:, lanes].astype(theirs.dtype)


def project(where, flipped, band_coeffs, parts):
    depth, bands = band_coeffs.shape
    count = 2 * len(parts)

    def kernel(*refs):
        project_kernel(parts, *refs)

    return pl.pallas_call(
        kernel,
        in_specs=[SMEM, VMEM, VMEM],
        out_specs=[VMEM, VMEM],
        out_shape=[
            jax.ShapeDtypeStruct((count, PCAP, LANES), jnp.bfloat16),
            jax.ShapeDtypeStruct((count, PCAP, LANES), jnp.float32),
        ],
        compiler_params=PARAMS,
        cost_estimate=pl.CostEstimate(
            flops=4 * depth * PCAP * count * LANES, bytes_accessed=2 * depth * count * LANES, transcendentals=0
        ),
        name="project",
    )(where, flipped, pltpu.with_memory_space_constraint(band_coeffs, pltpu.VMEM))


def project_plain(where, projectors, band_coeffs, parts):
    depth, bands = band_coeffs.shape
    chips = lax.axis_size("pw") // 2
    blocks = jnp.stack([block_of(where[1], q, r) for q in parts for r in range(chips // SQUARE)])
    columns = jnp.take(band_coeffs.reshape(depth, chips, bands // chips), blocks, axis=1)
    outs = []
    for group, dtype in ((1 - where[0], jnp.bfloat16), (where[0], jnp.float32)):
        slots = lax.dynamic_slice_in_dim(projectors, group * PCAP, PCAP, 1)
        sums = jnp.einsum("ds,dhw->hsw", slots, columns, preferred_element_type=jnp.float32)
        outs.append(sums.astype(dtype))
    return outs


def chosen(where, owners, group, own, across):
    me = where[2]
    owner = jnp.where(group == 0, owners[0], owners[1])
    part = jnp.where(owner == me, own, jnp.where(owner == (me ^ (2 * SQUARE)), across, 0.0))
    return part.astype(jnp.bfloat16)


def cuts(table, width):
    return jnp.concatenate([table[:, cut : cut + width] for cut in range(0, PCAP, width)], axis=0)


def choose_kernel(where, owners, own, across, theirs, near, message):
    core = where[0]
    entries, _, width = theirs.shape
    near[...] = chosen(where, owners, core, own[...], across[...])
    for entry in range(entries):
        message[entry * PCAP : (entry + 1) * PCAP] = theirs[entry]
    message[entries * PCAP :] = cuts(chosen(where, owners, 1 - core, own[...], across[...]), width)


def choose(where, owners, own, across, theirs):
    entries, _, width = theirs.shape
    return pl.pallas_call(
        choose_kernel,
        in_specs=[SMEM, SMEM, VMEM, VMEM, VMEM],
        out_specs=[VMEM, VMEM],
        out_shape=[
            jax.ShapeDtypeStruct(own.shape, jnp.bfloat16),
            jax.ShapeDtypeStruct((entries * PCAP + PCAP * PCAP // width, width), jnp.bfloat16),
        ],
        compiler_params=PARAMS,
        name="choose",
    )(where, owners, own, across, theirs)


def choose_plain(where, owners, own, across, theirs, chips):
    entries, _, width = theirs.shape
    tables = [chosen(where, owners, group, own, across) for group in (where[0], 1 - where[0])]
    distance = 2 * SQUARE
    while distance < chips:
        tables = [table + swap_square(table, distance) for table in tables]
        distance *= 2
    return tables[0], jnp.concatenate([theirs.reshape(entries * PCAP, width), cuts(tables[1], width)])


def quarter_kernel(where, near, got, *quarters):
    width = got.shape[1]
    first = got.shape[0] - PCAP * PCAP // width
    for part, quarter in enumerate(quarters):
        start = pl.multiple_of(((where[1] & 3) ^ part) * QUARTER, QUARTER)
        for cut in range(PCAP // width):
            piece = near[pl.ds(start, QUARTER), cut * width : (cut + 1) * width]
            quarter[cut * QUARTER : (cut + 1) * QUARTER] = piece + got[pl.ds(first + cut * PCAP + start, QUARTER)]


def quarters_of(where, near, got):
    width = got.shape[1]
    shape = jax.ShapeDtypeStruct((QUARTER * PCAP // width, width), jnp.bfloat16)
    return pl.pallas_call(
        quarter_kernel,
        in_specs=[SMEM, VMEM, VMEM],
        out_specs=[VMEM] * SQUARE,
        out_shape=[shape] * SQUARE,
        compiler_params=PARAMS,
        name="quarter",
    )(where, near, got)


def pack_kernel(ours, theirs, *messages):
    entries = messages[0].shape[0]
    for at, message in enumerate(messages):
        for entry in range(entries):
            place = at * entries + entry
            message[entry] = (ours[place] + theirs[place].astype(jnp.float32)).astype(message.dtype)


def pack(ours, theirs):
    count, _, width = ours.shape
    shape = jax.ShapeDtypeStruct((count // (SQUARE - 1), PCAP, width), jnp.bfloat16)
    return pl.pallas_call(
        pack_kernel,
        in_specs=[VMEM, VMEM],
        out_specs=[VMEM] * (SQUARE - 1),
        out_shape=[shape] * (SQUARE - 1),
        compiler_params=PARAMS,
        name="pack",
    )(ours, theirs)


def fold_kernel(ours, theirs, *refs):
    gots, quarters, (kept, message, quarter) = refs[: SQUARE - 1], refs[SQUARE - 1 : -3], refs[-3:]
    for entry in range(ours.shape[0]):
        total = ours[entry] + theirs[entry * PCAP : (entry + 1) * PCAP].astype(jnp.float32)
        for got in gots:
            total = total + got[entry].astype(jnp.float32)
        kept[entry] = total
        message[entry ^ 1] = total.astype(message.dtype)
    table = quarters[0][...]
    for got in quarters[1:]:
        table = table + got[...]
    quarter[...] = table


def fold(ours, theirs, gots, quarters):
    return pl.pallas_call(
        fold_kernel,
        in_specs=[VMEM] * (1 + 2 * SQUARE),
        out_specs=[VMEM] * 3,
        out_shape=[
            jax.ShapeDtypeStruct(ours.shape, jnp.float32),
            jax.ShapeDtypeStruct(ours.shape, jnp.bfloat16),
            jax.ShapeDtypeStruct(quarters[0].shape, jnp.bfloat16),
        ],
        compiler_params=PARAMS,
        name="fold",
    )(ours, theirs, *gots, *quarters)


def mask_kernel(where, counts, atom_of, after, out):
    del after
    core = where[0]
    slot = lax.broadcasted_iota(jnp.int32, (1, PCAP), 1)
    limit = jnp.zeros((1, PCAP), jnp.int32)
    for channel in range(CHANNELS):
        limit = jnp.where(slot >= channel * CH_CAP, channel * CH_CAP + counts[core, channel], limit)
    atoms = jnp.where(core == 0, atom_of[0:1], atom_of[1:2])
    code = jnp.broadcast_to(jnp.where(slot < limit, atoms, -1), (PCAP, PCAP))
    out[...] = jnp.where((code == code.T) & (code >= 0), 1.0, 0.0).astype(out.dtype)


def mask(where, counts, atom_of, after):
    return pl.pallas_call(
        mask_kernel,
        in_specs=[SMEM, SMEM, VMEM, ANY],
        out_specs=VMEM,
        out_shape=jax.ShapeDtypeStruct((PCAP, PCAP), jnp.bfloat16),
        compiler_params=PARAMS,
        name="mask",
    )(where, counts, atom_of, after)


def coupling_kernel(where, allowed, *refs):
    *quarters, out = refs
    width = quarters[0].shape[1]
    for part, quarter in enumerate(quarters):
        rows = pl.ds(pl.multiple_of(((where[1] & 3) ^ part) * QUARTER, QUARTER), QUARTER)
        for cut in range(PCAP // width):
            lanes = slice(cut * width, (cut + 1) * width)
            out[rows, lanes] = quarter[cut * QUARTER : (cut + 1) * QUARTER] * allowed[rows, lanes]


def coupling_of(where, allowed, quarters):
    return pl.pallas_call(
        coupling_kernel,
        in_specs=[SMEM] + [VMEM] * (1 + SQUARE),
        out_specs=VMEM,
        out_shape=jax.ShapeDtypeStruct((PCAP, PCAP), jnp.bfloat16),
        compiler_params=PARAMS,
        name="coupling",
    )(where, allowed, *quarters)


def couple_kernel(coupling, kept, got, out):
    entries, _, width = out.shape
    totals = [kept[e] + got[e].astype(jnp.float32) for e in range(entries)]
    high = [total.astype(jnp.bfloat16) for total in totals]
    low = [(total - part.astype(jnp.float32)).astype(jnp.bfloat16) for total, part in zip(totals, high)]
    both = jnp.dot(coupling[...], jnp.concatenate(high + low, axis=1), preferred_element_type=jnp.float32)
    for e in range(entries):
        first, second = e * width, (entries + e) * width
        out[e] = (both[:, first : first + width] + both[:, second : second + width]).astype(out.dtype)


def couple(coupling, kept, got):
    return pl.pallas_call(
        couple_kernel,
        in_specs=[VMEM] * 3,
        out_specs=VMEM,
        out_shape=jax.ShapeDtypeStruct(kept.shape, jnp.bfloat16),
        compiler_params=PARAMS,
        name="couple",
    )(coupling, kept, got)


def apply_kernel(part, where, projectors, mine, other, *refs):
    out, weights, blocks, sems = refs[-4:]
    core, chip = where[0], where[1]
    for scaled, group in ((mine, core), (other, 1 - core)):
        rows = pl.ds(pl.multiple_of(group * PCAP, PCAP), PCAP)
        weights[rows, :LANES] = scaled[0]
        weights[rows, LANES:] = scaled[1]
    copies = []
    for block in range(projectors.shape[0] // ROW_BLOCK):
        rows = slice(block * ROW_BLOCK, (block + 1) * ROW_BLOCK)
        blocks[rows] = jnp.dot(
            projectors[rows], weights[...], preferred_element_type=jnp.float32
        ).astype(blocks.dtype)
        for entry in range(2):
            start = pl.multiple_of(block_of(chip, part, entry) * LANES, LANES)
            copies.append(
                pltpu.make_async_copy(
                    blocks.at[rows, entry * LANES : (entry + 1) * LANES],
                    out.at[rows, pl.ds(start, LANES)],
                    sems.at[len(copies)],
                )
            )
            copies[-1].start()
    for copy in copies:
        copy.wait()


def apply(where, projectors, mine, other, part, out):
    depth, slots = projectors.shape
    pair = 2 * LANES

    def kernel(*refs):
        apply_kernel(part, *refs)

    operands = [where, projectors, mine, other] + ([] if out is None else [out])
    return pl.pallas_call(
        kernel,
        in_specs=[SMEM, VMEM, VMEM, VMEM] + ([] if out is None else [HBM]),
        out_specs=HBM,
        out_shape=jax.ShapeDtypeStruct((depth, SQUARE * pair), jnp.bfloat16),
        input_output_aliases={} if out is None else {4: 0},
        scratch_shapes=[
            pltpu.VMEM((slots, pair), jnp.bfloat16),
            pltpu.VMEM((depth, pair), jnp.bfloat16),
            pltpu.SemaphoreType.DMA((2 * depth // ROW_BLOCK,)),
        ],
        compiler_params=PARAMS,
        cost_estimate=pl.CostEstimate(
            flops=2 * depth * slots * pair, bytes_accessed=2 * depth * (slots + pair), transcendentals=0
        ),
        name="apply",
    )(*operands)


def apply_plain(where, projectors, mine, other):
    chips, _, width = mine.shape
    blocks = jnp.stack([block_of(where[1], q, r) for q in range(SQUARE) for r in range(chips // SQUARE)])
    rows = []
    for group in range(2):
        part = jnp.where(where[0] == group, mine, other)
        part = jnp.zeros_like(part).at[blocks].set(part)
        rows.append(part.transpose(1, 0, 2).reshape(PCAP, chips * width))
    return jnp.dot(projectors, jnp.concatenate(rows), preferred_element_type=jnp.float32).astype(jnp.bfloat16)


def local(band_coeffs, projectors, counts, atom_of, owners, couplings):
    chips = lax.axis_size("pw") // 2
    entries = chips // SQUARE
    width = band_coeffs.shape[1] // chips
    fast = width == LANES and entries == 2
    me = lax.axis_index("pw")
    where = jnp.stack([me % 2, me // 2, me])

    own_table = couplings[0]
    across = swap_square(own_table, SQUARE)
    sent, kept = tuple(range(1, SQUARE)), (0,)
    if fast:
        flipped = load(where, projectors)
        theirs, ours = project(where, flipped, band_coeffs, sent)
        low_theirs, low_ours = project(where, flipped, band_coeffs, kept)
        near, low_theirs = choose(where, owners, own_table, across, low_theirs)
    else:
        theirs, ours = project_plain(where, projectors, band_coeffs, sent)
        low_theirs, low_ours = project_plain(where, projectors, band_coeffs, kept)
        near, low_theirs = choose_plain(where, owners, own_table, across, low_theirs, chips)
    theirs, near = lax.optimization_barrier((swap_cores(theirs), near))
    messages = pack(ours, theirs)
    low_theirs = swap_cores(low_theirs)
    gots = [swap_square(message, part) for message, part in zip(messages, sent)]
    quarters = quarters_of(where, near, low_theirs)
    quarters = [quarters[0]] + [swap_square(quarters[part], part) for part in sent]
    allowed = mask(where, counts, atom_of, messages[0])

    total, message, quarter = fold(low_ours, low_theirs, gots, quarters)
    got = swap_square(message, SQUARE)
    coupling = coupling_of(where, allowed, [quarter] + [swap_square(quarter, part) for part in sent])
    distance = SQUARE
    while 2 * distance < chips:
        distance *= 2
        total = total + got.astype(jnp.float32)
        order = jnp.array([entry ^ (distance // SQUARE) for entry in range(entries)])
        got = swap_square(total[order].astype(jnp.bfloat16), distance)

    scaled = couple(coupling, total, got)
    gathered = [scaled] + [swap_square(scaled, part) for part in sent]
    if not fast:
        mine = jnp.concatenate(gathered)
        return apply_plain(where, projectors, mine, swap_cores(mine))
    first, second, third = gathered[3], gathered[1], gathered[2]
    out = apply(where, projectors, scaled, swap_cores(scaled), 0, None)
    first, out = lax.optimization_barrier((first, out))
    others = swap_cores(first), swap_cores(second)
    out = apply(where, projectors, first, others[0], 3, out)
    third, out = lax.optimization_barrier((third, out))
    last = swap_cores(third)
    out = apply(where, projectors, second, others[1], 1, out)
    return apply(where, projectors, third, last, 2, out)


def solution(mesh):
    placed = (
        P("pw", "group"),
        P("pw", "group"),
        P("group", None),
        P("group", None),
        P("group"),
        P("pw", "group", None),
    )
    return jax.shard_map(
        local, mesh=mesh, in_specs=placed, out_specs=P("pw", "group"), check_vma=False
    )
```

time: 48.3 us -> 56.7 us (1.17)
  starting transfers between devices: 11.4 us -> 22 us
  waiting for transfers between devices: 21.9 us -> 16.1 us
  Pallas kernels: 14.6 us -> 18.1 us
    ppermute x11 -> x20, starting transfers between devices: 11.4 us -> 22 us  [swap(): return lax.ppermute(x, 'pw', [(i, i ^ distance) for i in range(count)])]
    ppermute x11 -> x20, waiting for transfers between devices: 21.9 us -> 16.1 us  [swap(): return lax.ppermute(x, 'pw', [(i, i ^ distance) for i in range(count)])]
    pallas_call x7 -> x10, Pallas kernels: 7.45 us -> 10.9 us  [the longest x4 8.74 us: apply(): pl.pallas_call(kernel, in_specs=[SMEM, VMEM, VMEM, VMEM] + ([] if out is...]
  transfers between devices with their start and end apart: 11 -> 20, of which waited for: 9 -> 9; matrix products, arithmetic and copies ran while one was open for 0% -> 0% of each run, Pallas kernels for 8% -> 28%
where the time goes in v9:
time: 56.7 us; the launch traced here: 56.5 us
  starting transfers between devices  22 us (39%)
  Pallas kernels  18.1 us (32%)
  waiting for transfers between devices  16.1 us (28%)
    ppermute x20, starting transfers between devices, swap(): return lax.ppermute(x, 'pw', [(i, i ^ distance) for i in range(count)])  22 us
    ppermute x20, waiting for transfers between devices, swap(): return lax.ppermute(x, 'pw', [(i, i ^ distance) for i in range(count)])  16.1 us
    pallas_call x4, Pallas kernels, apply(): pl.pallas_call(kernel, in_specs=[SMEM, VMEM, VMEM, VMEM] + ([] if out is...  8.74 us
    pallas_call x2, Pallas kernels, project(): pl.pallas_call(kernel, in_specs=[SMEM, VMEM, VMEM], out_specs=[VMEM, VMEM...  3.79 us
    pallas_call x1, Pallas kernels, load(): pl.pallas_call(load_kernel, in_specs=[SMEM, HBM], out_specs=VMEM, out_sha...  2.73 us
  transfers between devices with their start and end apart: 20, of which 9 were waited for; matrix products, arithmetic and copies ran while one was open for 0% of the time, Pallas kernels for 28%

profile of v9, /device:TPU:0, one launch (start us, length us, event | category | flops | bytes accessed | tf_op | source)
XLA Modules:
  0.0 56.5 jit_solution(703441168061261167)
XLA Ops:
  0.0 4.0 %collective-permute-start.1 = (f32[256,256]{1,0:T(8,128)}, f32[256,256]{1,0:T(8,128)S(1)}, u32[]{:S(2)}, u32[]{:S(2)}) collective-permute-start(f32[256,256]{1,0:T(8,128)} %bitcast.4), channel_id=1, source_target_pairs={{0,8},{1,9},{2,10},{3,11},{4,12},{5,13},{6,14},{7,15},{8,0},{9,1},... | collective-permute-start | bytes 786440 | tf_op jit(solution)/shard_map/ppermute | solution.py:29
  4.0 0.1 pad_add_fusion.where.refs_0_
  4.1 2.7 %load.1.refs_1_ = bf16[512,2048]{1,0:T(8,128)(2,1)S(1)} custom-call(s32[3]{0:T(128)S(1)} %pad_add_fusion.where.refs_0_, bf16[2048,512]{1,0:T(8,128)(2,1)} %refs_1_.7), custom_call_target="tpu_custom_call" | custom-call | tf_op jit(solution)/shard_map/load/pallas_call | solution.py:59
  6.8 0.0 copy-done.1
  6.9 2.5 %project.2 = (bf16[6,256,128]{2,1,0:T(8,128)(2,1)S(1)}, f32[6,256,128]{2,1,0:T(8,128)S(1)}) custom-call(s32[3]{0:T(128)S(1)} %pad_add_fusion.where.refs_0_, bf16[512,2048]{1,0:T(8,128)(2,1)S(1)} %load.1.refs_1_, bf16[2048,1024]{1,0:T(8,128)(2,1)S(1)} %copy-done.1), custom_call_target="tpu_custom_call" | custom-call | flops 1610612736 | bytes 3145728 | tf_op jit(solution)/shard_map/project/pallas_call | solution.py:89
  9.3 0.0 copy-start.2
  9.3 0.0 copy-start.5
  9.4 0.0 copy-start.3
  9.4 0.0 copy-start.4
  9.4 0.0 copy-start
  9.4 0.1 collective-permute-start
  9.5 1.3 %project.3 = (bf16[2,256,128]{2,1,0:T(8,128)(2,1)S(1)}, f32[2,256,128]{2,1,0:T(8,128)S(1)}) custom-call(s32[3]{0:T(128)S(1)} %pad_add_fusion.where.refs_0_, bf16[512,2048]{1,0:T(8,128)(2,1)S(1)} %load.1.refs_1_, bf16[2048,1024]{1,0:T(8,128)(2,1)S(1)} %copy-done.1), custom_call_target="tpu_custom_call" | custom-call | flops 536870912 | bytes 1048576 | tf_op jit(solution)/shard_map/project/pallas_call | solution.py:89
  10.8 5.4 %collective-permute-done.1.across = f32[256,256]{1,0:T(8,128)S(1)} collective-permute-done((f32[256,256]{1,0:T(8,128)}, f32[256,256]{1,0:T(8,128)S(1)}, u32[]{:S(2)}, u32[]{:S(2)}) %collective-permute-start.1) | collective-permute-done | bytes 262176 | tf_op jit(solution)/shard_map/ppermute | solution.py:29
  16.2 0.0 copy-done.2
  16.2 0.0 copy-done.5
  16.2 0.6 %choose.1 = (bf16[256,256]{1,0:T(8,128)(2,1)S(1)}, bf16[1024,128]{1,0:T(8,128)(2,1)S(1)}) custom-call(s32[3]{0:T(128)S(1)} %pad_add_fusion.where.refs_0_, s32[2]{0:T(128)S(1)} %copy-done.5, f32[256,256]{1,0:T(8,128)S(1)} %bitcast.5, f32[256,256]{1,0:T(8,128)S(1)} %collective-permute-done.1.across, bf16[2,256,128]{2,1,0:T(8,128)(2,1)S(1)} %get-tuple-element.29.theirs), custom_call_target="tpu_custom_call" | custom-call | tf_op jit(solution)/shard_map/choose/pallas_call | solution.py:140
  16.8 0.1 collective-permute-start.2
  16.9 0.0 collective-permute-done.theirs
  16.9 0.1 pack.1
  17.0 1.6 %collective-permute-start.3 = (bf16[2,256,128]{2,1,0:T(8,128)(2,1)S(1)}, bf16[2,256,128]{2,1,0:T(8,128)(2,1)S(1)}, u32[]{:S(2)}, u32[]{:S(2)}) collective-permute-start(bf16[2,256,128]{2,1,0:T(8,128)(2,1)S(1)} %get-tuple-element.32.after), channel_id=1, source_target_pairs={{0,2},{1,3},{2,0},{3,1},{4,6},{5,7},{6,4},{7,5},{8,10},{9,11},{10,... | collective-permute-start | bytes 393224 | tf_op jit(solution)/shard_map/ppermute | solution.py:29
  18.6 0.8 %collective-permute-start.4 = (bf16[2,256,128]{2,1,0:T(8,128)(2,1)S(1)}, bf16[2,256,128]{2,1,0:T(8,128)(2,1)S(1)}, u32[]{:S(2)}, u32[]{:S(2)}) collective-permute-start(bf16[2,256,128]{2,1,0:T(8,128)(2,1)S(1)} %get-tuple-element.35), channel_id=1, source_target_pairs={{0,4},{1,5},{2,6},{3,7},{4,0},{5,1},{6,2},{7,3},{8,12},{9,13},{10,... | collective-permute-start | bytes 393224 | tf_op jit(solution)/shard_map/ppermute | solution.py:29
  19.4 1.1 %collective-permute-start.5 = (bf16[2,256,128]{2,1,0:T(8,128)(2,1)S(1)}, bf16[2,256,128]{2,1,0:T(8,128)(2,1)S(1)}, u32[]{:S(2)}, u32[]{:S(2)}) collective-permute-start(bf16[2,256,128]{2,1,0:T(8,128)(2,1)S(1)} %get-tuple-element.36), channel_id=1, source_target_pairs={{0,6},{1,7},{2,4},{3,5},{4,2},{5,3},{6,0},{7,1},{8,14},{9,15},{10,... | collective-permute-start | bytes 393224 | tf_op jit(solution)/shard_map/ppermute | solution.py:29
  20.5 0.0 collective-permute-done.2.got.theirs
  20.5 0.6 %quarter.1 = (bf16[128,128]{1,0:T(8,128)(2,1)S(1)}, bf16[128,128]{1,0:T(8,128)(2,1)S(1)}, bf16[128,128]{1,0:T(8,128)(2,1)S(1)}, bf16[128,128]{1,0:T(8,128)(2,1)S(1)}) custom-call(s32[3]{0:T(128)S(1)} %pad_add_fusion.where.refs_0_, bf16[256,256]{1,0:T(8,128)(2,1)S(1)} %get-tuple-element.37.near, bf16[1024,128]{1,0:T(8,128)(2,1)S(1)} %collective-permute-done.2.got.theirs), custom_call_target="tpu_custom_call" | custom-call | tf_op jit(solution)/shard_map/quarter/pallas_call | solution.py:176
  21.1 1.6 %collective-permute-start.6 = (bf16[128,128]{1,0:T(8,128)(2,1)S(1)}, bf16[128,128]{1,0:T(8,128)(2,1)S(1)}, u32[]{:S(2)}, u32[]{:S(2)}) collective-permute-start(bf16[128,128]{1,0:T(8,128)(2,1)S(1)} %get-tuple-element.39), channel_id=1, source_target_pairs={{0,2},{1,3},{2,0},{3,1},{4,6},{5,7},{6,4},{7,5},{8,10},{9,11},{10,... | collective-permute-start | bytes 98312 | tf_op jit(solution)/shard_map/ppermute | solution.py:29
  22.7 0.8 %collective-permute-start.7 = (bf16[128,128]{1,0:T(8,128)(2,1)S(1)}, bf16[128,128]{1,0:T(8,128)(2,1)S(1)}, u32[]{:S(2)}, u32[]{:S(2)}) collective-permute-start(bf16[128,128]{1,0:T(8,128)(2,1)S(1)} %get-tuple-element.40), channel_id=1, source_target_pairs={{0,4},{1,5},{2,6},{3,7},{4,0},{5,1},{6,2},{7,3},{8,12},{9,13},{10,... | collective-permute-start | bytes 98312 | tf_op jit(solution)/shard_map/ppermute | solution.py:29
  23.5 0.0 collective-permute-done.3.refs_0_
  23.5 1.2 %collective-permute-start.8 = (bf16[128,128]{1,0:T(8,128)(2,1)S(1)}, bf16[128,128]{1,0:T(8,128)(2,1)S(1)}, u32[]{:S(2)}, u32[]{:S(2)}) collective-permute-start(bf16[128,128]{1,0:T(8,128)(2,1)S(1)} %get-tuple-element.41), channel_id=1, source_target_pairs={{0,6},{1,7},{2,4},{3,5},{4,2},{5,3},{6,0},{7,1},{8,14},{9,15},{10,... | collective-permute-start | bytes 98312 | tf_op jit(solution)/shard_map/ppermute | solution.py:29
  24.7 0.2 collective-permute-done.4.refs_1_
  24.9 2.7 %collective-permute-done.5.refs_2_ = bf16[2,256,128]{2,1,0:T(8,128)(2,1)S(1)} collective-permute-done((bf16[2,256,128]{2,1,0:T(8,128)(2,1)S(1)}, bf16[2,256,128]{2,1,0:T(8,128)(2,1)S(1)}, u32[]{:S(2)}, u32[]{:S(2)}) %collective-permute-start.5) | collective-permute-done | bytes 131104 | tf_op jit(solution)/shard_map/ppermute | solution.py:29
  27.6 0.0 collective-permute-done.6.refs_4_
  27.6 0.5 collective-permute-done.7.refs_5_
  28.1 0.2 collective-permute-done.8.refs_6_
  28.3 0.1 fold.1
  28.4 3.3 %collective-permute-start.12 = (bf16[2,256,128]{2,1,0:T(8,128)(2,1)S(1)}, bf16[2,256,128]{2,1,0:T(8,128)(2,1)S(1)}, u32[]{:S(2)}, u32[]{:S(2)}) collective-permute-start(bf16[2,256,128]{2,1,0:T(8,128)(2,1)S(1)} %get-tuple-element.44), channel_id=1, source_target_pairs={{0,8},{1,9},{2,10},{3,11},{4,12},{5,13},{6,14},{7,15},{8,0},{9,1},... | collective-permute-start | bytes 393224 | tf_op jit(solution)/shard_map/ppermute | solution.py:29
  31.8 0.8 %collective-permute-start.10 = (bf16[128,128]{1,0:T(8,128)(2,1)S(1)}, bf16[128,128]{1,0:T(8,128)(2,1)S(1)}, u32[]{:S(2)}, u32[]{:S(2)}) collective-permute-start(bf16[128,128]{1,0:T(8,128)(2,1)S(1)} %get-tuple-element.42.refs_0_), channel_id=1, source_target_pairs={{0,4},{1,5},{2,6},{3,7},{4,0},{5,1},{6,2},{7,3},{8,12},{9,13},{10,... | collective-permute-start | bytes 98312 | tf_op jit(solution)/shard_map/ppermute | solution.py:29
  32.6 1.2 %collective-permute-start.11 = (bf16[128,128]{1,0:T(8,128)(2,1)S(1)}, bf16[128,128]{1,0:T(8,128)(2,1)S(1)}, u32[]{:S(2)}, u32[]{:S(2)}) collective-permute-start(bf16[128,128]{1,0:T(8,128)(2,1)S(1)} %get-tuple-element.42.refs_0_), channel_id=1, source_target_pairs={{0,6},{1,7},{2,4},{3,5},{4,2},{5,3},{6,0},{7,1},{8,14},{9,15},{10,... | collective-permute-start | bytes 98312 | tf_op jit(solution)/shard_map/ppermute | solution.py:29
  33.9 1.4 %collective-permute-start.9 = (bf16[128,128]{1,0:T(8,128)(2,1)S(1)}, bf16[128,128]{1,0:T(8,128)(2,1)S(1)}, u32[]{:S(2)}, u32[]{:S(2)}) collective-permute-start(bf16[128,128]{1,0:T(8,128)(2,1)S(1)} %get-tuple-element.42.refs_0_), channel_id=1, source_target_pairs={{0,2},{1,3},{2,0},{3,1},{4,6},{5,7},{6,4},{7,5},{8,10},{9,11},{10,... | collective-permute-start | bytes 98312 | tf_op jit(solution)/shard_map/ppermute | solution.py:29
  35.3 0.0 copy-done.3
  35.3 0.7 %mask.1.allowed = bf16[256,256]{1,0:T(8,128)(2,1)S(1)} custom-call(s32[3]{0:T(128)S(1)} %pad_add_fusion.where.refs_0_, s32[2,4]{1,0:T(2,128)S(1)} %copy-done.4, s32[2,256]{1,0:T(2,128)S(1)} %copy-done.3, bf16[2,256,128]{2,1,0:T(8,128)(2,1)S(1)} %get-tuple-element.32.after), custom_call_target="tpu_custom_call" | custom-call | tf_op jit(solution)/shard_map/mask/pallas_call | solution.py:249
  35.9 0.0 collective-permute-done.10.refs_2_
  36.0 2.4 %collective-permute-done.11.refs_3_ = bf16[128,128]{1,0:T(8,128)(2,1)S(1)} collective-permute-done((bf16[128,128]{1,0:T(8,128)(2,1)S(1)}, bf16[128,128]{1,0:T(8,128)(2,1)S(1)}, u32[]{:S(2)}, u32[]{:S(2)}) %collective-permute-start.11) | collective-permute-done | bytes 32800 | tf_op jit(solution)/shard_map/ppermute | solution.py:29
  38.4 0.0 collective-permute-done.9.refs_1_
  38.4 0.6 %coupling.1 = bf16[256,256]{1,0:T(8,128)(2,1)S(1)} custom-call(s32[3]{0:T(128)S(1)} %pad_add_fusion.where.refs_0_, bf16[256,256]{1,0:T(8,128)(2,1)S(1)} %mask.1.allowed, bf16[128,128]{1,0:T(8,128)(2,1)S(1)} %get-tuple-element.42.refs_0_, bf16[128,128]{1,0:T(8,128)(2,1)S(1)} %collective-permute-done.9.refs_1_, ...), custom_call_target="tpu_custom_call" | custom-call | tf_op jit(solution)/shard_map/coupling/pallas_call | solution.py:270
  38.9 0.0 collective-permute-done.12.got
  39.0 0.2 couple.1.refs_2_
  39.2 0.1 collective-permute-start.15
  39.3 1.2 %collective-permute-start.14 = (bf16[2,256,128]{2,1,0:T(8,128)(2,1)S(1)}, bf16[2,256,128]{2,1,0:T(8,128)(2,1)S(1)}, u32[]{:S(2)}, u32[]{:S(2)}) collective-permute-start(bf16[2,256,128]{2,1,0:T(8,128)(2,1)S(1)} %couple.1.refs_2_), channel_id=1, source_target_pairs={{0,6},{1,7},{2,4},{3,5},{4,2},{5,3},{6,0},{7,1},{8,14},{9,15},{10,... | collective-permute-start | bytes 393224 | tf_op jit(solution)/shard_map/ppermute | solution.py:29
  40.4 1.5 %collective-permute-start.18 = (bf16[2,256,128]{2,1,0:T(8,128)(2,1)S(1)}, bf16[2,256,128]{2,1,0:T(8,128)(2,1)S(1)}, u32[]{:S(2)}, u32[]{:S(2)}) collective-permute-start(bf16[2,256,128]{2,1,0:T(8,128)(2,1)S(1)} %couple.1.refs_2_), channel_id=1, source_target_pairs={{0,2},{1,3},{2,0},{3,1},{4,6},{5,7},{6,4},{7,5},{8,10},{9,11},{10,... | collective-permute-start | bytes 393224 | tf_op jit(solution)/shard_map/ppermute | solution.py:29
  42.0 0.0 collective-permute-done.15.refs_3_
  42.0 2.2 %apply.4.refs_4_ = bf16[2048,1024]{1,0:T(8,128)(2,1)} custom-call(s32[3]{0:T(128)S(1)} %pad_add_fusion.where.refs_0_, bf16[2048,512]{1,0:T(8,128)(2,1)S(1)} %copy-done, bf16[2,256,128]{2,1,0:T(8,128)(2,1)S(1)} %couple.1.refs_2_, bf16[2,256,128]{2,1,0:T(8,128)(2,1)S(1)} %collective-permute-done.15.refs_3_), custom_call_target="tpu_custom_call" | custom-call | flops 536870912 | bytes 3145728 | tf_op jit(solution)/shard_map/apply/pallas_call | solution.py:337
  44.2 2.0 %collective-permute-done.14.refs_2_ = bf16[2,256,128]{2,1,0:T(8,128)(2,1)S(1)} collective-permute-done((bf16[2,256,128]{2,1,0:T(8,128)(2,1)S(1)}, bf16[2,256,128]{2,1,0:T(8,128)(2,1)S(1)}, u32[]{:S(2)}, u32[]{:S(2)}) %collective-permute-start.14) | collective-permute-done | bytes 131104 | tf_op jit(solution)/shard_map/ppermute | solution.py:29
  46.2 0.0 collective-permute-start.16
  46.2 1.1 %collective-permute-start.13 = (bf16[2,256,128]{2,1,0:T(8,128)(2,1)S(1)}, bf16[2,256,128]{2,1,0:T(8,128)(2,1)S(1)}, u32[]{:S(2)}, u32[]{:S(2)}) collective-permute-start(bf16[2,256,128]{2,1,0:T(8,128)(2,1)S(1)} %couple.1.refs_2_), channel_id=1, source_target_pairs={{0,4},{1,5},{2,6},{3,7},{4,0},{5,1},{6,2},{7,3},{8,12},{9,13},{10,... | collective-permute-start | bytes 393224 | tf_op jit(solution)/shard_map/ppermute | solution.py:29
  47.4 1.5 %collective-permute-done.18.refs_2_ = bf16[2,256,128]{2,1,0:T(8,128)(2,1)S(1)} collective-permute-done((bf16[2,256,128]{2,1,0:T(8,128)(2,1)S(1)}, bf16[2,256,128]{2,1,0:T(8,128)(2,1)S(1)}, u32[]{:S(2)}, u32[]{:S(2)}) %collective-permute-start.18) | collective-permute-done | bytes 131104 | tf_op jit(solution)/shard_map/ppermute | solution.py:29
  48.8 0.0 collective-permute-start.19
  48.8 0.0 collective-permute-done.16.refs_3_
  48.8 2.2 %apply.5.refs_4_ = bf16[2048,1024]{1,0:T(8,128)(2,1)} custom-call(s32[3]{0:T(128)S(1)} %pad_add_fusion.where.refs_0_, bf16[2048,512]{1,0:T(8,128)(2,1)S(1)} %copy-done, bf16[2,256,128]{2,1,0:T(8,128)(2,1)S(1)} %collective-permute-done.14.refs_2_, bf16[2,256,128]{2,1,0:T(8,128)(2,1)S(1)} %collective-permute-done.16.refs_3_, ...), custom_call_target="tpu_custom_call", output_to_operand_aliasing={{}: (4, {})} | custom-call | flops 536870912 | bytes 3145728 | tf_op jit(solution)/shard_map/apply/pallas_call | solution.py:337
  51.0 1.1 %collective-permute-done.13.refs_2_ = bf16[2,256,128]{2,1,0:T(8,128)(2,1)S(1)} collective-permute-done((bf16[2,256,128]{2,1,0:T(8,128)(2,1)S(1)}, bf16[2,256,128]{2,1,0:T(8,128)(2,1)S(1)}, u32[]{:S(2)}, u32[]{:S(2)}) %collective-permute-start.13) | collective-permute-done | bytes 131104 | tf_op jit(solution)/shard_map/ppermute | solution.py:29
  52.1 0.0 collective-permute-start.17
  52.1 0.0 collective-permute-done.19.refs_3_
  52.1 2.2 %apply.6.refs_4_ = bf16[2048,1024]{1,0:T(8,128)(2,1)} custom-call(s32[3]{0:T(128)S(1)} %pad_add_fusion.where.refs_0_, bf16[2048,512]{1,0:T(8,128)(2,1)S(1)} %copy-done, bf16[2,256,128]{2,1,0:T(8,128)(2,1)S(1)} %collective-permute-done.18.refs_2_, bf16[2,256,128]{2,1,0:T(8,128)(2,1)S(1)} %collective-permute-done.19.refs_3_, ...), custom_call_target="tpu_custom_call", output_to_operand_aliasing={{}: (4, {})} | custom-call | flops 536870912 | bytes 3145728 | tf_op jit(solution)/shard_map/apply/pallas_call | solution.py:337
  54.3 0.0 collective-permute-done.17.refs_3_
  54.3 2.2 %apply.7 = bf16[2048,1024]{1,0:T(8,128)(2,1)} custom-call(s32[3]{0:T(128)S(1)} %pad_add_fusion.where.refs_0_, bf16[2048,512]{1,0:T(8,128)(2,1)S(1)} %copy-done, bf16[2,256,128]{2,1,0:T(8,128)(2,1)S(1)} %collective-permute-done.13.refs_2_, bf16[2,256,128]{2,1,0:T(8,128)(2,1)S(1)} %collective-permute-done.17.refs_3_, ...), custom_call_target="tpu_custom_call", output_to_operand_aliasing={{}: (4, {})} | custom-call | flops 536870912 | bytes 3145728 | tf_op jit(solution)/shard_map/apply/pallas_call | solution.py:337
  (3 shorter events, 0.0 us)
Async XLA Ops:
  0.0 16.2 %collective-permute-start.1 = (f32[256,256]{1,0:T(8,128)}, f32[256,256]{1,0:T(8,128)S(1)}, u32[]{:S(2)}, u32[]{:S(2)}) collective-permute-start(f32[256,256]{1,0:T(8,128)} %bitcast.4), channel_id=1, source_target_pairs={{0,8},{1,9},{2,10},{3,11},{4,12},{5,13},{6,14},{7,15},{8,0},{9,1},... | collective-permute-start | bytes 786440 | tf_op jit(solution)/shard_map/ppermute | solution.py:29
  4.0 2.8 %copy-start.1 = (bf16[2048,1024]{1,0:T(8,128)(2,1)S(1)}, bf16[2048,1024]{1,0:T(8,128)(2,1)}, u32[]{:S(2)}) copy-start(bf16[2048,1024]{1,0:T(8,128)(2,1)} %refs_2_.3) | copy-start | bytes 12582916
  9.3 6.8 %copy-start.2 = (f32[1,256,256]{2,1,0:T(8,128)S(1)}, f32[1,256,256]{2,1,0:T(8,128)}, u32[]{:S(2)}) copy-start(f32[1,256,256]{2,1,0:T(8,128)} %param.11) | copy-start | bytes 786436
  9.3 6.8 %copy-start.5 = (s32[2]{0:T(128)S(1)}, s32[2]{0:T(128)}, u32[]{:S(2)}) copy-start(s32[2]{0:T(128)} %owners.1) | copy-start | bytes 28
  9.4 25.9 %copy-start.3 = (s32[2,256]{1,0:T(2,128)S(1)}, s32[2,256]{1,0:T(2,128)}, u32[]{:S(2)}) copy-start(s32[2,256]{1,0:T(2,128)} %atom_of.1) | copy-start | bytes 6148
  9.4 25.9 %copy-start.4 = (s32[2,4]{1,0:T(2,128)S(1)}, s32[2,4]{1,0:T(2,128)}, u32[]{:S(2)}) copy-start(s32[2,4]{1,0:T(2,128)} %counts.1) | copy-start | bytes 100
  9.4 32.6 %copy-start = (bf16[2048,512]{1,0:T(8,128)(2,1)S(1)}, bf16[2048,512]{1,0:T(8,128)(2,1)}, u32[]{:S(2)}) copy-start(bf16[2048,512]{1,0:T(8,128)(2,1)} %refs_1_.7) | copy-start | bytes 6291460
  9.4 7.5 %collective-permute-start = (bf16[6,256,128]{2,1,0:T(8,128)(2,1)S(1)}, bf16[6,256,128]{2,1,0:T(8,128)(2,1)S(1)}, u32[]{:S(2)}, u32[]{:S(2)}) collective-permute-start(bf16[6,256,128]{2,1,0:T(8,128)(2,1)S(1)} %get-tuple-element.28), channel_id=1, source_target_pairs={{0,1},{1,0},{2,3},{3,2},{4,5},{5,4},{6,7},{7,6},{8,9},{9,8},{10,11... | collective-permute-start | bytes 1179656 | tf_op jit(solution)/shard_map/ppermute | solution.py:29
  16.8 3.7 %collective-permute-start.2 = (bf16[1024,128]{1,0:T(8,128)(2,1)S(1)}, bf16[1024,128]{1,0:T(8,128)(2,1)S(1)}, u32[]{:S(2)}, u32[]{:S(2)}) collective-permute-start(bf16[1024,128]{1,0:T(8,128)(2,1)S(1)} %get-tuple-element.34), channel_id=1, source_target_pairs={{0,1},{1,0},{2,3},{3,2},{4,5},{5,4},{6,7},{7,6},{8,9},{9,8},{10,11... | collective-permute-start | bytes 786440 | tf_op jit(solution)/shard_map/ppermute | solution.py:29
  17.0 6.6 %collective-permute-start.3 = (bf16[2,256,128]{2,1,0:T(8,128)(2,1)S(1)}, bf16[2,256,128]{2,1,0:T(8,128)(2,1)S(1)}, u32[]{:S(2)}, u32[]{:S(2)}) collective-permute-start(bf16[2,256,128]{2,1,0:T(8,128)(2,1)S(1)} %get-tuple-element.32.after), channel_id=1, source_target_pairs={{0,2},{1,3},{2,0},{3,1},{4,6},{5,7},{6,4},{7,5},{8,10},{9,11},{10,... | collective-permute-start | bytes 393224 | tf_op jit(solution)/shard_map/ppermute | solution.py:29
  18.6 6.3 %collective-permute-start.4 = (bf16[2,256,128]{2,1,0:T(8,128)(2,1)S(1)}, bf16[2,256,128]{2,1,0:T(8,128)(2,1)S(1)}, u32[]{:S(2)}, u32[]{:S(2)}) collective-permute-start(bf16[2,256,128]{2,1,0:T(8,128)(2,1)S(1)} %get-tuple-element.35), channel_id=1, source_target_pairs={{0,4},{1,5},{2,6},{3,7},{4,0},{5,1},{6,2},{7,3},{8,12},{9,13},{10,... | collective-permute-start | bytes 393224 | tf_op jit(solution)/shard_map/ppermute | solution.py:29
  19.4 8.3 %collective-permute-start.5 = (bf16[2,256,128]{2,1,0:T(8,128)(2,1)S(1)}, bf16[2,256,128]{2,1,0:T(8,128)(2,1)S(1)}, u32[]{:S(2)}, u32[]{:S(2)}) collective-permute-start(bf16[2,256,128]{2,1,0:T(8,128)(2,1)S(1)} %get-tuple-element.36), channel_id=1, source_target_pairs={{0,6},{1,7},{2,4},{3,5},{4,2},{5,3},{6,0},{7,1},{8,14},{9,15},{10,... | collective-permute-start | bytes 393224 | tf_op jit(solution)/shard_map/ppermute | solution.py:29
  21.1 6.5 %collective-permute-start.6 = (bf16[128,128]{1,0:T(8,128)(2,1)S(1)}, bf16[128,128]{1,0:T(8,128)(2,1)S(1)}, u32[]{:S(2)}, u32[]{:S(2)}) collective-permute-start(bf16[128,128]{1,0:T(8,128)(2,1)S(1)} %get-tuple-element.39), channel_id=1, source_target_pairs={{0,2},{1,3},{2,0},{3,1},{4,6},{5,7},{6,4},{7,5},{8,10},{9,11},{10,... | collective-permute-start | bytes 98312 | tf_op jit(solution)/shard_map/ppermute | solution.py:29
  22.7 5.4 %collective-permute-start.7 = (bf16[128,128]{1,0:T(8,128)(2,1)S(1)}, bf16[128,128]{1,0:T(8,128)(2,1)S(1)}, u32[]{:S(2)}, u32[]{:S(2)}) collective-permute-start(bf16[128,128]{1,0:T(8,128)(2,1)S(1)} %get-tuple-element.40), channel_id=1, source_target_pairs={{0,4},{1,5},{2,6},{3,7},{4,0},{5,1},{6,2},{7,3},{8,12},{9,13},{10,... | collective-permute-start | bytes 98312 | tf_op jit(solution)/shard_map/ppermute | solution.py:29
  23.5 4.8 %collective-permute-start.8 = (bf16[128,128]{1,0:T(8,128)(2,1)S(1)}, bf16[128,128]{1,0:T(8,128)(2,1)S(1)}, u32[]{:S(2)}, u32[]{:S(2)}) collective-permute-start(bf16[128,128]{1,0:T(8,128)(2,1)S(1)} %get-tuple-element.41), channel_id=1, source_target_pairs={{0,6},{1,7},{2,4},{3,5},{4,2},{5,3},{6,0},{7,1},{8,14},{9,15},{10,... | collective-permute-start | bytes 98312 | tf_op jit(solution)/shard_map/ppermute | solution.py:29
  28.4 10.5 %collective-permute-start.12 = (bf16[2,256,128]{2,1,0:T(8,128)(2,1)S(1)}, bf16[2,256,128]{2,1,0:T(8,128)(2,1)S(1)}, u32[]{:S(2)}, u32[]{:S(2)}) collective-permute-start(bf16[2,256,128]{2,1,0:T(8,128)(2,1)S(1)} %get-tuple-element.44), channel_id=1, source_target_pairs={{0,8},{1,9},{2,10},{3,11},{4,12},{5,13},{6,14},{7,15},{8,0},{9,1},... | collective-permute-start | bytes 393224 | tf_op jit(solution)/shard_map/ppermute | solution.py:29
  31.8 4.2 %collective-permute-start.10 = (bf16[128,128]{1,0:T(8,128)(2,1)S(1)}, bf16[128,128]{1,0:T(8,128)(2,1)S(1)}, u32[]{:S(2)}, u32[]{:S(2)}) collective-permute-start(bf16[128,128]{1,0:T(8,128)(2,1)S(1)} %get-tuple-element.42.refs_0_), channel_id=1, source_target_pairs={{0,4},{1,5},{2,6},{3,7},{4,0},{5,1},{6,2},{7,3},{8,12},{9,13},{10,... | collective-permute-start | bytes 98312 | tf_op jit(solution)/shard_map/ppermute | solution.py:29
  32.6 5.7 %collective-permute-start.11 = (bf16[128,128]{1,0:T(8,128)(2,1)S(1)}, bf16[128,128]{1,0:T(8,128)(2,1)S(1)}, u32[]{:S(2)}, u32[]{:S(2)}) collective-permute-start(bf16[128,128]{1,0:T(8,128)(2,1)S(1)} %get-tuple-element.42.refs_0_), channel_id=1, source_target_pairs={{0,6},{1,7},{2,4},{3,5},{4,2},{5,3},{6,0},{7,1},{8,14},{9,15},{10,... | collective-permute-start | bytes 98312 | tf_op jit(solution)/shard_map/ppermute | solution.py:29
  33.9 4.5 %collective-permute-start.9 = (bf16[128,128]{1,0:T(8,128)(2,1)S(1)}, bf16[128,128]{1,0:T(8,128)(2,1)S(1)}, u32[]{:S(2)}, u32[]{:S(2)}) collective-permute-start(bf16[128,128]{1,0:T(8,128)(2,1)S(1)} %get-tuple-element.42.refs_0_), channel_id=1, source_target_pairs={{0,2},{1,3},{2,0},{3,1},{4,6},{5,7},{6,4},{7,5},{8,10},{9,11},{10,... | collective-permute-start | bytes 98312 | tf_op jit(solution)/shard_map/ppermute | solution.py:29
  39.2 2.8 %collective-permute-start.15 = (bf16[2,256,128]{2,1,0:T(8,128)(2,1)S(1)}, bf16[2,256,128]{2,1,0:T(8,128)(2,1)S(1)}, u32[]{:S(2)}, u32[]{:S(2)}) collective-permute-start(bf16[2,256,128]{2,1,0:T(8,128)(2,1)S(1)} %couple.1.refs_2_), channel_id=1, source_target_pairs={{0,1},{1,0},{2,3},{3,2},{4,5},{5,4},{6,7},{7,6},{8,9},{9,8},{10,11... | collective-permute-start | bytes 393224 | tf_op jit(solution)/shard_map/ppermute | solution.py:29
  39.3 6.9 %collective-permute-start.14 = (bf16[2,256,128]{2,1,0:T(8,128)(2,1)S(1)}, bf16[2,256,128]{2,1,0:T(8,128)(2,1)S(1)}, u32[]{:S(2)}, u32[]{:S(2)}) collective-permute-start(bf16[2,256,128]{2,1,0:T(8,128)(2,1)S(1)} %couple.1.refs_2_), channel_id=1, source_target_pairs={{0,6},{1,7},{2,4},{3,5},{4,2},{5,3},{6,0},{7,1},{8,14},{9,15},{10,... | collective-permute-start | bytes 393224 | tf_op jit(solution)/shard_map/ppermute | solution.py:29
  40.4 8.4 %collective-permute-start.18 = (bf16[2,256,128]{2,1,0:T(8,128)(2,1)S(1)}, bf16[2,256,128]{2,1,0:T(8,128)(2,1)S(1)}, u32[]{:S(2)}, u32[]{:S(2)}) collective-permute-start(bf16[2,256,128]{2,1,0:T(8,128)(2,1)S(1)} %couple.1.refs_2_), channel_id=1, source_target_pairs={{0,2},{1,3},{2,0},{3,1},{4,6},{5,7},{6,4},{7,5},{8,10},{9,11},{10,... | collective-permute-start | bytes 393224 | tf_op jit(solution)/shard_map/ppermute | solution.py:29
  46.2 2.6 %collective-permute-start.16 = (bf16[2,256,128]{2,1,0:T(8,128)(2,1)S(1)}, bf16[2,256,128]{2,1,0:T(8,128)(2,1)S(1)}, u32[]{:S(2)}, u32[]{:S(2)}) collective-permute-start(bf16[2,256,128]{2,1,0:T(8,128)(2,1)S(1)} %collective-permute-done.14.refs_2_), channel_id=1, source_target_pairs={{0,1},{1,0},{2,3},{3,2},{4,5},{5,4},{6,7},{7,6},{8,9},{9,8},{10,11... | collective-permute-start | bytes 393224 | tf_op jit(solution)/shard_map/ppermute | solution.py:29
  46.2 5.9 %collective-permute-start.13 = (bf16[2,256,128]{2,1,0:T(8,128)(2,1)S(1)}, bf16[2,256,128]{2,1,0:T(8,128)(2,1)S(1)}, u32[]{:S(2)}, u32[]{:S(2)}) collective-permute-start(bf16[2,256,128]{2,1,0:T(8,128)(2,1)S(1)} %couple.1.refs_2_), channel_id=1, source_target_pairs={{0,4},{1,5},{2,6},{3,7},{4,0},{5,1},{6,2},{7,3},{8,12},{9,13},{10,... | collective-permute-start | bytes 393224 | tf_op jit(solution)/shard_map/ppermute | solution.py:29
  48.8 3.3 %collective-permute-start.19 = (bf16[2,256,128]{2,1,0:T(8,128)(2,1)S(1)}, bf16[2,256,128]{2,1,0:T(8,128)(2,1)S(1)}, u32[]{:S(2)}, u32[]{:S(2)}) collective-permute-start(bf16[2,256,128]{2,1,0:T(8,128)(2,1)S(1)} %collective-permute-done.18.refs_2_), channel_id=1, source_target_pairs={{0,1},{1,0},{2,3},{3,2},{4,5},{5,4},{6,7},{7,6},{8,9},{9,8},{10,11... | collective-permute-start | bytes 393224 | tf_op jit(solution)/shard_map/ppermute | solution.py:29
  52.1 2.2 %collective-permute-start.17 = (bf16[2,256,128]{2,1,0:T(8,128)(2,1)S(1)}, bf16[2,256,128]{2,1,0:T(8,128)(2,1)S(1)}, u32[]{:S(2)}, u32[]{:S(2)}) collective-permute-start(bf16[2,256,128]{2,1,0:T(8,128)(2,1)S(1)} %collective-permute-done.13.refs_2_), channel_id=1, source_target_pairs={{0,1},{1,0},{2,3},{3,2},{4,5},{5,4},{6,7},{7,6},{8,9},{9,8},{10,11... | collective-permute-start | bytes 393224 | tf_op jit(solution)/shard_map/ppermute | solution.py:29

commit v10 on v0

v10 whole, which is shorter than its diff:
```python
import jax
import jax.numpy as jnp
from jax import lax
from jax.experimental import pallas as pl
from jax.experimental.pallas import tpu as pltpu
from jax.sharding import PartitionSpec as P

CHANNELS = 4
CH_CAP = 64
PCAP = 256
LANES = 128
SQUARE = 4
QUARTER = PCAP // SQUARE
ROW_BLOCK = 512
COPY_ROWS = 128
PARAMS = pltpu.CompilerParams(vmem_limit_bytes=40 * 1024 * 1024)
VMEM = pl.BlockSpec(memory_space=pltpu.VMEM)
SMEM = pl.BlockSpec(memory_space=pltpu.SMEM)
HBM = pl.BlockSpec(memory_space=pltpu.HBM)
ANY = pl.BlockSpec(memory_space=pl.ANY)


def swap(x, distance):
    count = lax.axis_size("pw")
    return lax.ppermute(x, "pw", [(i, i ^ distance) for i in range(count)])


def swap_cores(x):
    return swap(x, 1)


def swap_square(x, part):
    return swap(x, 2 * part)


def load_kernel(where, projectors, flipped, slots, sems):
    core = where[0]
    count = sems.shape[0]
    block = slots.shape[0] // count
    copies = []
    for at in range(count):
        rows = slice(at * block, (at + 1) * block)
        copies.append(pltpu.make_async_copy(projectors.at[rows], slots.at[rows], sems.at[at]))
        copies[-1].start()
    for at, copy in enumerate(copies):
        copy.wait()
        rows = slice(at * block, (at + 1) * block)
        for place, group in enumerate((core, 1 - core)):
            start = pl.multiple_of(group * PCAP, PCAP)
            flipped[place * PCAP : (place + 1) * PCAP, rows] = slots[rows, pl.ds(start, PCAP)].T


def load(where, projectors):
    depth, slots = projectors.shape
    return pl.pallas_call(
        load_kernel,
        in_specs=[SMEM, HBM],
        out_specs=VMEM,
        out_shape=jax.ShapeDtypeStruct((slots, depth), jnp.bfloat16),
        scratch_shapes=[pltpu.VMEM((depth, slots), jnp.bfloat16), pltpu.SemaphoreType.DMA((4,))],
        compiler_params=PARAMS,
        name="load",
    )(where, pltpu.with_memory_space_constraint(projectors, pltpu.HBM))


def project_kernel(where, flipped, columns, theirs, ours):
    corner = where[1] & 3
    for first in range(0, SQUARE, 2):
        lanes = slice(first * LANES, (first + 2) * LANES)
        sums = jnp.dot(flipped[...], columns[:, lanes], preferred_element_type=jnp.float32)
        for at in range(2):
            part = corner ^ (first + at)
            block = sums[:, at * LANES : (at + 1) * LANES]
            ours[part] = block[:PCAP]
            theirs[part] = block[PCAP:].astype(theirs.dtype)


def project(where, flipped, band_coeffs, half):
    depth, bands = band_coeffs.shape
    wide = bands // 2
    return pl.pallas_call(
        project_kernel,
        grid=(1,),
        in_specs=[
            SMEM,
            pl.BlockSpec(flipped.shape, lambda i: (0, 0)),
            pl.BlockSpec((depth, wide), lambda i: (0, half)),
        ],
        out_specs=[pl.BlockSpec((SQUARE, PCAP, LANES), lambda i: (0, 0, 0))] * 2,
        out_shape=[
            jax.ShapeDtypeStruct((SQUARE, PCAP, LANES), jnp.bfloat16),
            jax.ShapeDtypeStruct((SQUARE, PCAP, LANES), jnp.float32),
        ],
        compiler_params=PARAMS,
        cost_estimate=pl.CostEstimate(
            flops=4 * depth * PCAP * wide, bytes_accessed=2 * depth * wide, transcendentals=0
        ),
        name="project",
    )(where, flipped, pltpu.with_memory_space_constraint(band_coeffs, pltpu.VMEM))


def parts_plain(where, blocks):
    order = jnp.arange(SQUARE) ^ (where[1] & 3)
    return jnp.take(blocks, order, axis=1)


def project_plain(where, projectors, band_coeffs, half):
    depth, bands = band_coeffs.shape
    width = 2 * bands // lax.axis_size("pw")
    columns = band_coeffs[:, half * bands // 2 : (half + 1) * bands // 2]
    outs = []
    for group, dtype in ((1 - where[0], jnp.bfloat16), (where[0], jnp.float32)):
        slots = lax.dynamic_slice_in_dim(projectors, group * PCAP, PCAP, 1)
        sums = lax.dot_general(slots, columns, (((0,), (0,)), ((), ())), preferred_element_type=jnp.float32)
        blocks = sums.reshape(PCAP, -1, SQUARE, width).transpose(1, 2, 0, 3)
        blocks = parts_plain(where, blocks).transpose(1, 0, 2, 3)
        outs.append(blocks.reshape(SQUARE, -1, width).astype(dtype))
    return outs


def quarter_of(where, owners, own, sibling, part, width):
    core, chip, me = where[0], where[1], where[2]
    owner = jnp.where(core == 0, owners[0], owners[1])
    rows = pl.ds(pl.multiple_of(((chip & 3) ^ part) * QUARTER, QUARTER), QUARTER)
    piece = jnp.where(owner == me, own[rows], jnp.where(owner == (me ^ 1), sibling[rows], 0.0))
    piece = piece.astype(jnp.bfloat16)
    return jnp.concatenate([piece[:, cut : cut + width] for cut in range(0, PCAP, width)], axis=0)


def pack_kernel(ours, theirs, *messages):
    for at, message in enumerate(messages):
        message[...] = (ours[at + 1] + theirs[at + 1].astype(jnp.float32)).astype(message.dtype)


def pack_table_kernel(where, owners, ours, theirs, own, sibling, quarter, *messages):
    _, rows, width = ours.shape
    for at, message in enumerate(messages):
        message[:rows] = (ours[at + 1] + theirs[at + 1].astype(jnp.float32)).astype(message.dtype)
        message[rows:] = quarter_of(where, owners, own, sibling, at + 1, width)
    quarter[...] = quarter_of(where, owners, own, sibling, 0, width)


def pack(where, owners, ours, theirs, tables):
    _, rows, width = ours.shape
    kernel, in_specs, operands, out_shape = pack_kernel, [VMEM, VMEM], (ours, theirs), []
    if tables is not None:
        kernel = pack_table_kernel
        in_specs = [SMEM, SMEM] + [VMEM] * 4
        operands = (where, owners, ours, theirs) + tables
        extra = QUARTER * PCAP // width
        out_shape = [jax.ShapeDtypeStruct((extra, width), jnp.bfloat16)]
        rows += extra
    out_shape = out_shape + [jax.ShapeDtypeStruct((rows, width), jnp.bfloat16)] * (SQUARE - 1)
    return pl.pallas_call(
        kernel,
        in_specs=in_specs,
        out_specs=[VMEM] * len(out_shape),
        out_shape=out_shape,
        compiler_params=PARAMS,
        name="pack",
    )(*operands)


def fold_kernel(ours, theirs, *refs):
    gots, quarters, (kept, message) = refs[: SQUARE - 1], refs[SQUARE - 1 : -2], refs[-2:]
    rows = ours.shape[1]
    total = ours[0] + theirs[0].astype(jnp.float32)
    for got in gots:
        total = total + got[:rows].astype(jnp.float32)
    kept[:rows] = total
    message[:rows] = total.astype(message.dtype)
    for quarter in quarters:
        table = quarter[...]
        for got in gots:
            table = table + got[rows:]
        kept[rows:] = table.astype(kept.dtype)
        message[rows:] = table


def fold(ours, theirs, gots, quarters):
    shape = gots[0].shape
    return pl.pallas_call(
        fold_kernel,
        in_specs=[VMEM] * (1 + SQUARE + len(quarters)),
        out_specs=[VMEM, VMEM],
        out_shape=[jax.ShapeDtypeStruct(shape, jnp.float32), jax.ShapeDtypeStruct(shape, jnp.bfloat16)],
        compiler_params=PARAMS,
        name="fold",
    )(ours, theirs, *gots, *quarters)


def add_kernel(left, right, out):
    out[...] = (left[...] + right[...].astype(jnp.float32)).astype(out.dtype)


def add(left, right):
    return pl.pallas_call(
        add_kernel,
        in_specs=[VMEM, VMEM],
        out_specs=VMEM,
        out_shape=jax.ShapeDtypeStruct(left.shape, jnp.bfloat16),
        compiler_params=PARAMS,
        name="add",
    )(left, right)


def mask_kernel(where, counts, atom_of, after, out):
    del after
    core = where[0]
    slot = lax.broadcasted_iota(jnp.int32, (1, PCAP), 1)
    limit = jnp.zeros((1, PCAP), jnp.int32)
    for channel in range(CHANNELS):
        limit = jnp.where(slot >= channel * CH_CAP, channel * CH_CAP + counts[core, channel], limit)
    atoms = jnp.where(core == 0, atom_of[0:1], atom_of[1:2])
    code = jnp.broadcast_to(jnp.where(slot < limit, atoms, -1), (PCAP, PCAP))
    out[...] = jnp.where((code == code.T) & (code >= 0), 1.0, 0.0).astype(out.dtype)


def mask(where, counts, atom_of, after):
    return pl.pallas_call(
        mask_kernel,
        in_specs=[SMEM, SMEM, VMEM, ANY],
        out_specs=VMEM,
        out_shape=jax.ShapeDtypeStruct((PCAP, PCAP), jnp.bfloat16),
        compiler_params=PARAMS,
        name="mask",
    )(where, counts, atom_of, after)


def scale(coupling, messages, rows, out):
    width = out.shape[2]
    wide = [message[at : at + PCAP] for message in messages for at in range(0, rows, PCAP)]
    scaled = jnp.dot(coupling[...], jnp.concatenate(wide, axis=1), preferred_element_type=jnp.float32)
    scaled = scaled.astype(out.dtype)
    for at in range(len(wide)):
        part, first = at * PCAP // rows, at * PCAP % rows
        out[part, first : first + PCAP] = scaled[:, at * width : (at + 1) * width]


def couple_first_kernel(where, allowed, *refs):
    *messages, out, coupling = refs
    _, rows, width = out.shape
    for part, message in enumerate(messages):
        start = pl.multiple_of(((where[1] & 3) ^ part) * QUARTER, QUARTER)
        for cut in range(PCAP // width):
            lanes = slice(cut * width, (cut + 1) * width)
            first = rows + cut * QUARTER
            coupling[pl.ds(start, QUARTER), lanes] = (
                message[first : first + QUARTER] * allowed[pl.ds(start, QUARTER), lanes]
            )
    scale(coupling, messages, rows, out)


def couple_first(where, allowed, messages, rows):
    width = messages[0].shape[1]
    return pl.pallas_call(
        couple_first_kernel,
        in_specs=[SMEM] + [VMEM] * (1 + SQUARE),
        out_specs=[VMEM, VMEM],
        out_shape=[
            jax.ShapeDtypeStruct((SQUARE, rows, width), jnp.bfloat16),
            jax.ShapeDtypeStruct((PCAP, PCAP), jnp.bfloat16),
        ],
        compiler_params=PARAMS,
        name="couple_first",
    )(where, allowed, *messages)


def couple_kernel(coupling, *refs):
    *messages, out = refs
    scale(coupling, messages, out.shape[1], out)


def couple(coupling, messages):
    rows, width = messages[0].shape
    return pl.pallas_call(
        couple_kernel,
        in_specs=[VMEM] * (1 + SQUARE),
        out_specs=VMEM,
        out_shape=jax.ShapeDtypeStruct((SQUARE, rows, width), jnp.bfloat16),
        compiler_params=PARAMS,
        name="couple",
    )(coupling, *messages)


def apply_kernel(half, where, projectors, mine, other, *refs):
    out, weights, blocks, sems = refs[-4:]
    core, corner = where[0], where[1] & 3
    for scaled, group in ((mine, core), (other, 1 - core)):
        rows = pl.ds(pl.multiple_of(group * PCAP, PCAP), PCAP)
        for part in range(SQUARE):
            start = pl.multiple_of((corner ^ part) * LANES, LANES)
            weights[rows, pl.ds(start, LANES)] = scaled[part]
    wide = weights.shape[1]
    copies = []
    for block in range(projectors.shape[0] // ROW_BLOCK):
        rows = slice(block * ROW_BLOCK, (block + 1) * ROW_BLOCK)
        blocks[rows] = jnp.dot(
            projectors[rows], weights[...], preferred_element_type=jnp.float32
        ).astype(blocks.dtype)
        for start in range(block * ROW_BLOCK, (block + 1) * ROW_BLOCK, COPY_ROWS):
            written = slice(start, start + COPY_ROWS)
            copies.append(
                pltpu.make_async_copy(
                    blocks.at[written],
                    out.at[written, half * wide : (half + 1) * wide],
                    sems.at[len(copies)],
                )
            )
            copies[-1].start()
    for copy in copies:
        copy.wait()


def apply(where, projectors, mine, other, half, out):
    depth, slots = projectors.shape
    wide = SQUARE * LANES

    def kernel(*refs):
        apply_kernel(half, *refs)

    operands = [where, projectors, mine, other] + ([] if out is None else [out])
    return pl.pallas_call(
        kernel,
        in_specs=[SMEM, VMEM, VMEM, VMEM] + ([] if out is None else [HBM]),
        out_specs=HBM,
        out_shape=jax.ShapeDtypeStruct((depth, 2 * wide), jnp.bfloat16),
        input_output_aliases={} if out is None else {4: 0},
        scratch_shapes=[
            pltpu.VMEM((slots, wide), jnp.bfloat16),
            pltpu.VMEM((depth, wide), jnp.bfloat16),
            pltpu.SemaphoreType.DMA((depth // COPY_ROWS,)),
        ],
        compiler_params=PARAMS,
        cost_estimate=pl.CostEstimate(
            flops=2 * depth * slots * wide, bytes_accessed=2 * depth * (slots + wide), transcendentals=0
        ),
        name="apply",
    )(*operands)


def apply_plain(where, projectors, halves):
    columns = []
    for mine, other in halves:
        rows = []
        for group in range(2):
            blocks = jnp.where(where[0] == group, mine, other)
            width = blocks.shape[2]
            blocks = blocks.reshape(SQUARE, -1, PCAP, width).transpose(1, 0, 2, 3)
            blocks = parts_plain(where, blocks).transpose(2, 0, 1, 3)
            rows.append(blocks.reshape(PCAP, -1))
        columns.append(jnp.concatenate(rows))
    scaled = jnp.concatenate(columns, axis=1)
    return jnp.dot(projectors, scaled, preferred_element_type=jnp.float32).astype(jnp.bfloat16)


def local(band_coeffs, projectors, counts, atom_of, owners, couplings):
    chips = lax.axis_size("pw") // 2
    width = band_coeffs.shape[1] // chips
    rows = chips // (2 * SQUARE) * PCAP
    fast = width == LANES and rows == PCAP
    me = lax.axis_index("pw")
    where = jnp.stack([me % 2, me // 2, me])
    sent = range(1, SQUARE)

    def partial(half):
        if fast:
            return project(where, flipped, band_coeffs, half)
        return project_plain(where, projectors, band_coeffs, half)

    def scatter(messages):
        return [swap_square(message, part) for message, part in zip(messages, sent)]

    def across(total, got):
        distance = 2 * SQUARE
        while distance < chips:
            mine = add(total, got)
            total, got = mine.astype(jnp.float32), swap_square(mine, distance)
            distance *= 2
        return add(total, got)

    def gather(mine):
        return [mine] + [swap_square(mine, part) for part in sent]

    own_table = couplings[0]
    sibling_table = swap_cores(own_table)
    flipped = load(where, projectors) if fast else None
    theirs, ours = partial(0)
    late_theirs, late_ours = partial(1)
    theirs, late_ours = lax.optimization_barrier((swap_cores(theirs), late_ours))
    late_theirs = swap_cores(late_theirs)
    quarter, *messages = pack(where, owners, ours, theirs, (own_table, sibling_table))
    allowed = mask(where, counts, atom_of, quarter)
    gots = scatter(messages)
    late_messages = pack(where, owners, late_ours, late_theirs, None)
    gots[0], late_messages = lax.optimization_barrier((gots[0], late_messages))
    late_gots = scatter(late_messages)
    total, message = fold(ours, theirs, gots, [quarter])
    got = swap_square(message, SQUARE)
    late_total, message = fold(late_ours, late_theirs, late_gots, [])
    got, message = lax.optimization_barrier((got, message))
    late_got = swap_square(message, SQUARE)
    gathered = gather(across(total, got))
    late_mine = across(late_total, late_got)
    gathered[1], late_mine = lax.optimization_barrier((gathered[1], late_mine))
    late_gathered = gather(late_mine)

    scaled, coupling = couple_first(where, allowed, gathered, rows)
    halves = [(scaled, swap_cores(scaled))]
    if fast:
        out = apply(where, projectors, *halves[0], 0, None)
        late_gathered[1], out = lax.optimization_barrier((late_gathered[1], out))
    scaled = couple(coupling, late_gathered)
    halves.append((scaled, swap_cores(scaled)))
    if not fast:
        return apply_plain(where, projectors, halves)
    return apply(where, projectors, *halves[1], 1, out)


def solution(mesh):
    placed = (
        P("pw", "group"),
        P("pw", "group"),
        P("group", None),
        P("group", None),
        P("group"),
        P("pw", "group", None),
    )
    return jax.shard_map(
        local, mesh=mesh, in_specs=placed, out_specs=P("pw", "group"), check_vma=False
    )
```

time: 137 us -> 50.7 us (0.37)
  waiting for transfers between devices: 104 us -> 16.8 us
  starting transfers between devices: 0.01 us -> 19 us
  between operations: 14.7 us -> 0.19 us
  matrix products: 14.5 us -> 0 us
  Pallas kernels: 0 us -> 14.5 us
  other arithmetic: 2.59 us -> 0.08 us
    psum x1 -> x0, waiting for transfers between devices: 104 us -> none  [local(): proj_sums = lax.psum(partial_proj, 'pw')]
    ppermute x0 -> x19, starting transfers between devices: none -> 19 us  [swap(): return lax.ppermute(x, 'pw', [(i, i ^ distance) for i in range(count)])]
    ppermute x0 -> x19, waiting for transfers between devices: none -> 16.8 us  [swap(): return lax.ppermute(x, 'pw', [(i, i ^ distance) for i in range(count)])]
    dot_general x3 -> x0, matrix products: 14.5 us -> none  [the longest x1 6.49 us: local(): lax.dot_general(masked_proj, band_coeffs, (((0,), (0,)), ((), ())), prefe...]
    pallas_call x0 -> x14, Pallas kernels: none -> 14.5 us  [the longest x2 5.64 us: apply(): pl.pallas_call(kernel, in_specs=[SMEM, VMEM, VMEM, VMEM] + ([] if out is...]
    select_n x3 -> x0, other arithmetic: 1.81 us -> none  [the longest x1 1.8 us: from_root(): return lax.psum(jnp.where(mine, x, jnp.zeros_like(x)), axis)]
  transfers between devices with their start and end apart: 1 -> 19, of which waited for: 1 -> 9; matrix products, arithmetic and copies ran while one was open for 0% -> 0% of each run, Pallas kernels for 0% -> 21%
where the time goes in v10:
time: 50.7 us; the launch traced here: 50.6 us
  starting transfers between devices  19 us (37%)
  waiting for transfers between devices  16.8 us (33%)
  Pallas kernels  14.5 us (29%)
    ppermute x19, starting transfers between devices, swap(): return lax.ppermute(x, 'pw', [(i, i ^ distance) for i in range(count)])  19 us
    ppermute x19, waiting for transfers between devices, swap(): return lax.ppermute(x, 'pw', [(i, i ^ distance) for i in range(count)])  16.8 us
    pallas_call x2, Pallas kernels, apply(): pl.pallas_call(kernel, in_specs=[SMEM, VMEM, VMEM, VMEM] + ([] if out is...  5.64 us
    pallas_call x2, Pallas kernels, project(): pl.pallas_call(project_kernel, grid=(1,), in_specs=[SMEM, pl.BlockSpec(fl...  3.63 us
    pallas_call x1, Pallas kernels, load(): pl.pallas_call(load_kernel, in_specs=[SMEM, HBM], out_specs=VMEM, out_sha...  2.73 us
  transfers between devices with their start and end apart: 19, of which 9 were waited for; matrix products, arithmetic and copies ran while one was open for 0% of the time, Pallas kernels for 21%

profile of v10, /device:TPU:0, one launch (start us, length us, event | category | flops | bytes accessed | tf_op | source)
XLA Modules:
  0.0 50.6 jit_solution(17820022525007949880)
XLA Ops:
  0.0 0.5 collective-permute-start.1
  0.5 0.0 copy-start.1
  0.5 0.1 pad_add_fusion.where.refs_0_
  0.5 2.7 %load.1.flipped = bf16[512,2048]{1,0:T(8,128)(2,1)S(1)} custom-call(s32[3]{0:T(128)S(1)} %pad_add_fusion.where.refs_0_, bf16[2048,512]{1,0:T(8,128)(2,1)} %refs_1_.3), custom_call_target="tpu_custom_call" | custom-call | tf_op jit(solution)/shard_map/load/pallas_call | solution.py:55
  3.3 0.0 copy-done.1
  3.3 1.8 %project.2 = (bf16[4,256,128]{2,1,0:T(8,128)(2,1)S(1)}, f32[4,256,128]{2,1,0:T(8,128)S(1)}) custom-call(s32[3]{0:T(128)S(1)} %pad_add_fusion.where.refs_0_, bf16[512,2048]{1,0:T(8,128)(2,1)S(1)} %load.1.flipped, bf16[2048,1024]{1,0:T(8,128)(2,1)S(1)} %copy-done.1), custom_call_target="tpu_custom_call" | custom-call | flops 1073741824 | bytes 2097152 | tf_op jit(solution)/shard_map/project/pallas_call | solution.py:81
  5.1 0.0 copy-start.2
  5.1 0.0 copy-start.5
  5.1 0.0 copy-start.3
  5.1 0.0 copy-start.4
  5.1 0.1 collective-permute-start
  5.3 1.8 %project.3 = (bf16[4,256,128]{2,1,0:T(8,128)(2,1)S(1)}, f32[4,256,128]{2,1,0:T(8,128)S(1)}) custom-call(s32[3]{0:T(128)S(1)} %pad_add_fusion.where.refs_0_, bf16[512,2048]{1,0:T(8,128)(2,1)S(1)} %load.1.flipped, bf16[2048,1024]{1,0:T(8,128)(2,1)S(1)} %copy-done.1), custom_call_target="tpu_custom_call" | custom-call | flops 1073741824 | bytes 2097152 | tf_op jit(solution)/shard_map/project/pallas_call | solution.py:81
  7.1 0.0 copy-start
  7.1 0.5 %collective-permute-start.3 = (bf16[4,256,128]{2,1,0:T(8,128)(2,1)S(1)}, bf16[4,256,128]{2,1,0:T(8,128)(2,1)S(1)}, u32[]{:S(2)}, u32[]{:S(2)}) collective-permute-start(bf16[4,256,128]{2,1,0:T(8,128)(2,1)S(1)} %get-tuple-element.41), channel_id=1, source_target_pairs={{0,1},{1,0},{2,3},{3,2},{4,5},{5,4},{6,7},{7,6},{8,9},{9,8},{10,11... | collective-permute-start | bytes 786440 | tf_op jit(solution)/shard_map/ppermute | solution.py:25
  7.6 0.0 collective-permute-done.theirs
  7.6 0.0 collective-permute-done.1.sibling
  7.6 0.0 copy-done.2
  7.6 0.0 copy-done.5
  7.6 0.6 %pack.2 = (bf16[128,128]{1,0:T(8,128)(2,1)S(1)}, bf16[384,128]{1,0:T(8,128)(2,1)S(1)}, bf16[384,128]{1,0:T(8,128)(2,1)S(1)}, bf16[384,128]{1,0:T(8,128)(2,1)S(1)}) custom-call(s32[3]{0:T(128)S(1)} %pad_add_fusion.where.refs_0_, s32[2]{0:T(128)S(1)} %copy-done.5, f32[4,256,128]{2,1,0:T(8,128)S(1)} %get-tuple-element.34.ours, ...), custom_call_target="tpu_custom_call" | custom-call | tf_op jit(solution)/shard_map/pack/pallas_call | solution.py:154
  8.3 2.6 %collective-permute-start.2 = (bf16[384,128]{1,0:T(8,128)(2,1)S(1)}, bf16[384,128]{1,0:T(8,128)(2,1)S(1)}, u32[]{:S(2)}, u32[]{:S(2)}) collective-permute-start(bf16[384,128]{1,0:T(8,128)(2,1)S(1)} %get-tuple-element.39), channel_id=1, source_target_pairs={{0,2},{1,3},{2,0},{3,1},{4,6},{5,7},{6,4},{7,5},{8,10},{9,11},{10,... | collective-permute-start | bytes 294920 | tf_op jit(solution)/shard_map/ppermute | solution.py:25
  10.9 1.6 %collective-permute-start.4 = (bf16[384,128]{1,0:T(8,128)(2,1)S(1)}, bf16[384,128]{1,0:T(8,128)(2,1)S(1)}, u32[]{:S(2)}, u32[]{:S(2)}) collective-permute-start(bf16[384,128]{1,0:T(8,128)(2,1)S(1)} %get-tuple-element.46), channel_id=1, source_target_pairs={{0,4},{1,5},{2,6},{3,7},{4,0},{5,1},{6,2},{7,3},{8,12},{9,13},{10,... | collective-permute-start | bytes 294920 | tf_op jit(solution)/shard_map/ppermute | solution.py:25
  12.5 0.0 collective-permute-start.5
  12.5 0.0 collective-permute-done.3.theirs
  12.5 1.8 %collective-permute-done.2.refs_0_ = bf16[384,128]{1,0:T(8,128)(2,1)S(1)} collective-permute-done((bf16[384,128]{1,0:T(8,128)(2,1)S(1)}, bf16[384,128]{1,0:T(8,128)(2,1)S(1)}, u32[]{:S(2)}, u32[]{:S(2)}) %collective-permute-start.2) | collective-permute-done | bytes 98336 | tf_op jit(solution)/shard_map/ppermute | solution.py:25
  14.3 2.2 %collective-permute-done.4.refs_1_ = bf16[384,128]{1,0:T(8,128)(2,1)S(1)} collective-permute-done((bf16[384,128]{1,0:T(8,128)(2,1)S(1)}, bf16[384,128]{1,0:T(8,128)(2,1)S(1)}, u32[]{:S(2)}, u32[]{:S(2)}) %collective-permute-start.4) | collective-permute-done | bytes 98336 | tf_op jit(solution)/shard_map/ppermute | solution.py:25
  16.5 1.5 %collective-permute-done.5.refs_2_ = bf16[384,128]{1,0:T(8,128)(2,1)S(1)} collective-permute-done((bf16[384,128]{1,0:T(8,128)(2,1)S(1)}, bf16[384,128]{1,0:T(8,128)(2,1)S(1)}, u32[]{:S(2)}, u32[]{:S(2)}) %collective-permute-start.5) | collective-permute-done | bytes 98336 | tf_op jit(solution)/shard_map/ppermute | solution.py:25
  18.0 0.1 fold.2
  18.0 2.7 %collective-permute-start.6 = (bf16[384,128]{1,0:T(8,128)(2,1)S(1)}, bf16[384,128]{1,0:T(8,128)(2,1)S(1)}, u32[]{:S(2)}, u32[]{:S(2)}) collective-permute-start(bf16[384,128]{1,0:T(8,128)(2,1)S(1)} %get-tuple-element.49), channel_id=1, source_target_pairs={{0,8},{1,9},{2,10},{3,11},{4,12},{5,13},{6,14},{7,15},{8,0},{9,1},... | collective-permute-start | bytes 294920 | tf_op jit(solution)/shard_map/ppermute | solution.py:25
  20.7 1.4 %collective-permute-start.7 = (bf16[256,128]{1,0:T(8,128)(2,1)S(1)}, bf16[256,128]{1,0:T(8,128)(2,1)S(1)}, u32[]{:S(2)}, u32[]{:S(2)}) collective-permute-start(bf16[256,128]{1,0:T(8,128)(2,1)S(1)} %get-tuple-element.50), channel_id=1, source_target_pairs={{0,2},{1,3},{2,0},{3,1},{4,6},{5,7},{6,4},{7,5},{8,10},{9,11},{10,... | collective-permute-start | bytes 196616 | tf_op jit(solution)/shard_map/ppermute | solution.py:25
  22.1 1.6 %collective-permute-start.8 = (bf16[256,128]{1,0:T(8,128)(2,1)S(1)}, bf16[256,128]{1,0:T(8,128)(2,1)S(1)}, u32[]{:S(2)}, u32[]{:S(2)}) collective-permute-start(bf16[256,128]{1,0:T(8,128)(2,1)S(1)} %get-tuple-element.51), channel_id=1, source_target_pairs={{0,4},{1,5},{2,6},{3,7},{4,0},{5,1},{6,2},{7,3},{8,12},{9,13},{10,... | collective-permute-start | bytes 196616 | tf_op jit(solution)/shard_map/ppermute | solution.py:25
  23.6 0.5 %collective-permute-start.9 = (bf16[256,128]{1,0:T(8,128)(2,1)S(1)}, bf16[256,128]{1,0:T(8,128)(2,1)S(1)}, u32[]{:S(2)}, u32[]{:S(2)}) collective-permute-start(bf16[256,128]{1,0:T(8,128)(2,1)S(1)} %get-tuple-element.52), channel_id=1, source_target_pairs={{0,6},{1,7},{2,4},{3,5},{4,2},{5,3},{6,0},{7,1},{8,14},{9,15},{10,... | collective-permute-start | bytes 196616 | tf_op jit(solution)/shard_map/ppermute | solution.py:25
  24.2 0.8 %collective-permute-done.7.refs_0_ = bf16[256,128]{1,0:T(8,128)(2,1)S(1)} collective-permute-done((bf16[256,128]{1,0:T(8,128)(2,1)S(1)}, bf16[256,128]{1,0:T(8,128)(2,1)S(1)}, u32[]{:S(2)}, u32[]{:S(2)}) %collective-permute-start.7) | collective-permute-done | bytes 65568 | tf_op jit(solution)/shard_map/ppermute | solution.py:25
  25.0 1.4 %collective-permute-done.8.refs_1_ = bf16[256,128]{1,0:T(8,128)(2,1)S(1)} collective-permute-done((bf16[256,128]{1,0:T(8,128)(2,1)S(1)}, bf16[256,128]{1,0:T(8,128)(2,1)S(1)}, u32[]{:S(2)}, u32[]{:S(2)}) %collective-permute-start.8) | collective-permute-done | bytes 65568 | tf_op jit(solution)/shard_map/ppermute | solution.py:25
  26.3 2.5 %collective-permute-done.9.refs_2_ = bf16[256,128]{1,0:T(8,128)(2,1)S(1)} collective-permute-done((bf16[256,128]{1,0:T(8,128)(2,1)S(1)}, bf16[256,128]{1,0:T(8,128)(2,1)S(1)}, u32[]{:S(2)}, u32[]{:S(2)}) %collective-permute-start.9) | collective-permute-done | bytes 65568 | tf_op jit(solution)/shard_map/ppermute | solution.py:25
  28.9 0.0 collective-permute-done.6.right
  28.9 0.6 %collective-permute-start.10 = (bf16[384,128]{1,0:T(8,128)(2,1)S(1)}, bf16[384,128]{1,0:T(8,128)(2,1)S(1)}, u32[]{:S(2)}, u32[]{:S(2)}) collective-permute-start(bf16[384,128]{1,0:T(8,128)(2,1)S(1)} %add.12.refs_0_), channel_id=1, source_target_pairs={{0,2},{1,3},{2,0},{3,1},{4,6},{5,7},{6,4},{7,5},{8,10},{9,11},{10,... | collective-permute-start | bytes 294920 | tf_op jit(solution)/shard_map/ppermute | solution.py:25
  29.5 1.4 %collective-permute-start.13 = (bf16[384,128]{1,0:T(8,128)(2,1)S(1)}, bf16[384,128]{1,0:T(8,128)(2,1)S(1)}, u32[]{:S(2)}, u32[]{:S(2)}) collective-permute-start(bf16[384,128]{1,0:T(8,128)(2,1)S(1)} %add.12.refs_0_), channel_id=1, source_target_pairs={{0,6},{1,7},{2,4},{3,5},{4,2},{5,3},{6,0},{7,1},{8,14},{9,15},{10,... | collective-permute-start | bytes 294920 | tf_op jit(solution)/shard_map/ppermute | solution.py:25
  30.9 1.6 %collective-permute-start.12 = (bf16[384,128]{1,0:T(8,128)(2,1)S(1)}, bf16[384,128]{1,0:T(8,128)(2,1)S(1)}, u32[]{:S(2)}, u32[]{:S(2)}) collective-permute-start(bf16[384,128]{1,0:T(8,128)(2,1)S(1)} %add.12.refs_0_), channel_id=1, source_target_pairs={{0,4},{1,5},{2,6},{3,7},{4,0},{5,1},{6,2},{7,3},{8,12},{9,13},{10,... | collective-permute-start | bytes 294920 | tf_op jit(solution)/shard_map/ppermute | solution.py:25
  32.5 0.3 collective-permute-start.11
  32.8 0.0 copy-done.3
  32.8 0.0 copy-done.4
  32.8 0.7 %mask.1.allowed = bf16[256,256]{1,0:T(8,128)(2,1)S(1)} custom-call(s32[3]{0:T(128)S(1)} %pad_add_fusion.where.refs_0_, s32[2,4]{1,0:T(2,128)S(1)} %copy-done.4, s32[2,256]{1,0:T(2,128)S(1)} %copy-done.3, bf16[128,128]{1,0:T(8,128)(2,1)S(1)} %get-tuple-element.38.after.refs_3_), custom_call_target="tpu_custom_call" | custom-call | tf_op jit(solution)/shard_map/mask/pallas_call | solution.py:220
  33.5 4.7 %collective-permute-done.11.right = bf16[256,128]{1,0:T(8,128)(2,1)S(1)} collective-permute-done((bf16[256,128]{1,0:T(8,128)(2,1)S(1)}, bf16[256,128]{1,0:T(8,128)(2,1)S(1)}, u32[]{:S(2)}, u32[]{:S(2)}) %collective-permute-start.11) | collective-permute-done | bytes 65568 | tf_op jit(solution)/shard_map/ppermute | solution.py:25
  38.2 0.0 collective-permute-done.10.refs_1_
  38.2 0.0 collective-permute-done.13.refs_3_
  38.2 0.0 collective-permute-done.12.refs_2_
  38.3 0.8 %couple_first.1 = (bf16[4,256,128]{2,1,0:T(8,128)(2,1)S(1)}, bf16[256,256]{1,0:T(8,128)(2,1)S(1)}) custom-call(s32[3]{0:T(128)S(1)} %pad_add_fusion.where.refs_0_, bf16[256,256]{1,0:T(8,128)(2,1)S(1)} %mask.1.allowed, bf16[384,128]{1,0:T(8,128)(2,1)S(1)} %add.12.refs_0_, bf16[384,128]{1,0:T(8,128)(2,1)S(1)} %collective-permute-done.10.refs_1_, ...), custom_call_target="tpu_custom_call" | custom-call | tf_op jit(solution)/shard_map/couple_first/pallas_call | solution.py:256
  39.0 0.1 collective-permute-start.15
  39.1 0.3 collective-permute-start.17
  39.5 1.8 %collective-permute-start.16 = (bf16[256,128]{1,0:T(8,128)(2,1)S(1)}, bf16[256,128]{1,0:T(8,128)(2,1)S(1)}, u32[]{:S(2)}, u32[]{:S(2)}) collective-permute-start(bf16[256,128]{1,0:T(8,128)(2,1)S(1)} %add.13.refs_0_), channel_id=1, source_target_pairs={{0,4},{1,5},{2,6},{3,7},{4,0},{5,1},{6,2},{7,3},{8,12},{9,13},{10,... | collective-permute-start | bytes 196616 | tf_op jit(solution)/shard_map/ppermute | solution.py:25
  41.3 1.4 %collective-permute-start.14 = (bf16[256,128]{1,0:T(8,128)(2,1)S(1)}, bf16[256,128]{1,0:T(8,128)(2,1)S(1)}, u32[]{:S(2)}, u32[]{:S(2)}) collective-permute-start(bf16[256,128]{1,0:T(8,128)(2,1)S(1)} %add.13.refs_0_), channel_id=1, source_target_pairs={{0,2},{1,3},{2,0},{3,1},{4,6},{5,7},{6,4},{7,5},{8,10},{9,11},{10,... | collective-permute-start | bytes 196616 | tf_op jit(solution)/shard_map/ppermute | solution.py:25
  42.7 0.0 collective-permute-done.15.refs_3_
  42.7 0.0 copy-done
  42.7 2.8 %apply.2.refs_4_ = bf16[2048,1024]{1,0:T(8,128)(2,1)} custom-call(s32[3]{0:T(128)S(1)} %pad_add_fusion.where.refs_0_, bf16[2048,512]{1,0:T(8,128)(2,1)S(1)} %copy-done, bf16[4,256,128]{2,1,0:T(8,128)(2,1)S(1)} %get-tuple-element.60.refs_2_, bf16[4,256,128]{2,1,0:T(8,128)(2,1)S(1)} %collective-permute-done.15.refs_3_), custom_call_target="tpu_custom_call" | custom-call | flops 1073741824 | bytes 4194304 | tf_op jit(solution)/shard_map/apply/pallas_call | solution.py:323
  45.5 0.4 collective-permute-done.14.refs_1_
  45.9 0.0 collective-permute-done.17.refs_3_
  45.9 0.0 collective-permute-done.16.refs_2_
  45.9 0.2 couple.1.refs_2_
  46.2 0.1 collective-permute-start.18
  46.3 1.5 %collective-permute-done.18.refs_3_ = bf16[4,256,128]{2,1,0:T(8,128)(2,1)S(1)} collective-permute-done((bf16[4,256,128]{2,1,0:T(8,128)(2,1)S(1)}, bf16[4,256,128]{2,1,0:T(8,128)(2,1)S(1)}, u32[]{:S(2)}, u32[]{:S(2)}) %collective-permute-start.18) | collective-permute-done | bytes 262176 | tf_op jit(solution)/shard_map/ppermute | solution.py:25
  47.8 2.8 %apply.3 = bf16[2048,1024]{1,0:T(8,128)(2,1)} custom-call(s32[3]{0:T(128)S(1)} %pad_add_fusion.where.refs_0_, bf16[2048,512]{1,0:T(8,128)(2,1)S(1)} %copy-done, bf16[4,256,128]{2,1,0:T(8,128)(2,1)S(1)} %couple.1.refs_2_, bf16[4,256,128]{2,1,0:T(8,128)(2,1)S(1)} %collective-permute-done.18.refs_3_, ...), custom_call_target="tpu_custom_call", output_to_operand_aliasing={{}: (4, {})} | custom-call | flops 1073741824 | bytes 4194304 | tf_op jit(solution)/shard_map/apply/pallas_call | solution.py:323
  (4 shorter events, 0.1 us)
Async XLA Ops:
  0.0 7.6 %collective-permute-start.1 = (f32[256,256]{1,0:T(8,128)}, f32[256,256]{1,0:T(8,128)S(1)}, u32[]{:S(2)}, u32[]{:S(2)}) collective-permute-start(f32[256,256]{1,0:T(8,128)} %bitcast.4), channel_id=1, source_target_pairs={{0,1},{1,0},{2,3},{3,2},{4,5},{5,4},{6,7},{7,6},{8,9},{9,8},{10,11... | collective-permute-start | bytes 786440 | tf_op jit(solution)/shard_map/ppermute | solution.py:25
  0.5 2.8 %copy-start.1 = (bf16[2048,1024]{1,0:T(8,128)(2,1)S(1)}, bf16[2048,1024]{1,0:T(8,128)(2,1)}, u32[]{:S(2)}) copy-start(bf16[2048,1024]{1,0:T(8,128)(2,1)} %columns.3) | copy-start | bytes 12582916
  5.1 2.5 %copy-start.2 = (f32[1,256,256]{2,1,0:T(8,128)S(1)}, f32[1,256,256]{2,1,0:T(8,128)}, u32[]{:S(2)}) copy-start(f32[1,256,256]{2,1,0:T(8,128)} %param.11) | copy-start | bytes 786436
  5.1 2.5 %copy-start.5 = (s32[2]{0:T(128)S(1)}, s32[2]{0:T(128)}, u32[]{:S(2)}) copy-start(s32[2]{0:T(128)} %owners.1) | copy-start | bytes 28
  5.1 27.7 %copy-start.3 = (s32[2,256]{1,0:T(2,128)S(1)}, s32[2,256]{1,0:T(2,128)}, u32[]{:S(2)}) copy-start(s32[2,256]{1,0:T(2,128)} %atom_of.1) | copy-start | bytes 6148
  5.1 27.7 %copy-start.4 = (s32[2,4]{1,0:T(2,128)S(1)}, s32[2,4]{1,0:T(2,128)}, u32[]{:S(2)}) copy-start(s32[2,4]{1,0:T(2,128)} %counts.1) | copy-start | bytes 100
  5.1 2.5 %collective-permute-start = (bf16[4,256,128]{2,1,0:T(8,128)(2,1)S(1)}, bf16[4,256,128]{2,1,0:T(8,128)(2,1)S(1)}, u32[]{:S(2)}, u32[]{:S(2)}) collective-permute-start(bf16[4,256,128]{2,1,0:T(8,128)(2,1)S(1)} %get-tuple-element.35), channel_id=1, source_target_pairs={{0,1},{1,0},{2,3},{3,2},{4,5},{5,4},{6,7},{7,6},{8,9},{9,8},{10,11... | collective-permute-start | bytes 786440 | tf_op jit(solution)/shard_map/ppermute | solution.py:25
  7.1 35.6 %copy-start = (bf16[2048,512]{1,0:T(8,128)(2,1)S(1)}, bf16[2048,512]{1,0:T(8,128)(2,1)}, u32[]{:S(2)}) copy-start(bf16[2048,512]{1,0:T(8,128)(2,1)} %refs_1_.3) | copy-start | bytes 6291460
  7.1 5.4 %collective-permute-start.3 = (bf16[4,256,128]{2,1,0:T(8,128)(2,1)S(1)}, bf16[4,256,128]{2,1,0:T(8,128)(2,1)S(1)}, u32[]{:S(2)}, u32[]{:S(2)}) collective-permute-start(bf16[4,256,128]{2,1,0:T(8,128)(2,1)S(1)} %get-tuple-element.41), channel_id=1, source_target_pairs={{0,1},{1,0},{2,3},{3,2},{4,5},{5,4},{6,7},{7,6},{8,9},{9,8},{10,11... | collective-permute-start | bytes 786440 | tf_op jit(solution)/shard_map/ppermute | solution.py:25
  8.3 6.0 %collective-permute-start.2 = (bf16[384,128]{1,0:T(8,128)(2,1)S(1)}, bf16[384,128]{1,0:T(8,128)(2,1)S(1)}, u32[]{:S(2)}, u32[]{:S(2)}) collective-permute-start(bf16[384,128]{1,0:T(8,128)(2,1)S(1)} %get-tuple-element.39), channel_id=1, source_target_pairs={{0,2},{1,3},{2,0},{3,1},{4,6},{5,7},{6,4},{7,5},{8,10},{9,11},{10,... | collective-permute-start | bytes 294920 | tf_op jit(solution)/shard_map/ppermute | solution.py:25
  10.9 5.6 %collective-permute-start.4 = (bf16[384,128]{1,0:T(8,128)(2,1)S(1)}, bf16[384,128]{1,0:T(8,128)(2,1)S(1)}, u32[]{:S(2)}, u32[]{:S(2)}) collective-permute-start(bf16[384,128]{1,0:T(8,128)(2,1)S(1)} %get-tuple-element.46), channel_id=1, source_target_pairs={{0,4},{1,5},{2,6},{3,7},{4,0},{5,1},{6,2},{7,3},{8,12},{9,13},{10,... | collective-permute-start | bytes 294920 | tf_op jit(solution)/shard_map/ppermute | solution.py:25
  12.5 5.5 %collective-permute-start.5 = (bf16[384,128]{1,0:T(8,128)(2,1)S(1)}, bf16[384,128]{1,0:T(8,128)(2,1)S(1)}, u32[]{:S(2)}, u32[]{:S(2)}) collective-permute-start(bf16[384,128]{1,0:T(8,128)(2,1)S(1)} %get-tuple-element.47), channel_id=1, source_target_pairs={{0,6},{1,7},{2,4},{3,5},{4,2},{5,3},{6,0},{7,1},{8,14},{9,15},{10,... | collective-permute-start | bytes 294920 | tf_op jit(solution)/shard_map/ppermute | solution.py:25
  18.0 10.8 %collective-permute-start.6 = (bf16[384,128]{1,0:T(8,128)(2,1)S(1)}, bf16[384,128]{1,0:T(8,128)(2,1)S(1)}, u32[]{:S(2)}, u32[]{:S(2)}) collective-permute-start(bf16[384,128]{1,0:T(8,128)(2,1)S(1)} %get-tuple-element.49), channel_id=1, source_target_pairs={{0,8},{1,9},{2,10},{3,11},{4,12},{5,13},{6,14},{7,15},{8,0},{9,1},... | collective-permute-start | bytes 294920 | tf_op jit(solution)/shard_map/ppermute | solution.py:25
  20.7 4.3 %collective-permute-start.7 = (bf16[256,128]{1,0:T(8,128)(2,1)S(1)}, bf16[256,128]{1,0:T(8,128)(2,1)S(1)}, u32[]{:S(2)}, u32[]{:S(2)}) collective-permute-start(bf16[256,128]{1,0:T(8,128)(2,1)S(1)} %get-tuple-element.50), channel_id=1, source_target_pairs={{0,2},{1,3},{2,0},{3,1},{4,6},{5,7},{6,4},{7,5},{8,10},{9,11},{10,... | collective-permute-start | bytes 196616 | tf_op jit(solution)/shard_map/ppermute | solution.py:25
  22.1 4.3 %collective-permute-start.8 = (bf16[256,128]{1,0:T(8,128)(2,1)S(1)}, bf16[256,128]{1,0:T(8,128)(2,1)S(1)}, u32[]{:S(2)}, u32[]{:S(2)}) collective-permute-start(bf16[256,128]{1,0:T(8,128)(2,1)S(1)} %get-tuple-element.51), channel_id=1, source_target_pairs={{0,4},{1,5},{2,6},{3,7},{4,0},{5,1},{6,2},{7,3},{8,12},{9,13},{10,... | collective-permute-start | bytes 196616 | tf_op jit(solution)/shard_map/ppermute | solution.py:25
  23.6 5.2 %collective-permute-start.9 = (bf16[256,128]{1,0:T(8,128)(2,1)S(1)}, bf16[256,128]{1,0:T(8,128)(2,1)S(1)}, u32[]{:S(2)}, u32[]{:S(2)}) collective-permute-start(bf16[256,128]{1,0:T(8,128)(2,1)S(1)} %get-tuple-element.52), channel_id=1, source_target_pairs={{0,6},{1,7},{2,4},{3,5},{4,2},{5,3},{6,0},{7,1},{8,14},{9,15},{10,... | collective-permute-start | bytes 196616 | tf_op jit(solution)/shard_map/ppermute | solution.py:25
  28.9 9.3 %collective-permute-start.10 = (bf16[384,128]{1,0:T(8,128)(2,1)S(1)}, bf16[384,128]{1,0:T(8,128)(2,1)S(1)}, u32[]{:S(2)}, u32[]{:S(2)}) collective-permute-start(bf16[384,128]{1,0:T(8,128)(2,1)S(1)} %add.12.refs_0_), channel_id=1, source_target_pairs={{0,2},{1,3},{2,0},{3,1},{4,6},{5,7},{6,4},{7,5},{8,10},{9,11},{10,... | collective-permute-start | bytes 294920 | tf_op jit(solution)/shard_map/ppermute | solution.py:25
  29.5 8.8 %collective-permute-start.13 = (bf16[384,128]{1,0:T(8,128)(2,1)S(1)}, bf16[384,128]{1,0:T(8,128)(2,1)S(1)}, u32[]{:S(2)}, u32[]{:S(2)}) collective-permute-start(bf16[384,128]{1,0:T(8,128)(2,1)S(1)} %add.12.refs_0_), channel_id=1, source_target_pairs={{0,6},{1,7},{2,4},{3,5},{4,2},{5,3},{6,0},{7,1},{8,14},{9,15},{10,... | collective-permute-start | bytes 294920 | tf_op jit(solution)/shard_map/ppermute | solution.py:25
  30.9 7.4 %collective-permute-start.12 = (bf16[384,128]{1,0:T(8,128)(2,1)S(1)}, bf16[384,128]{1,0:T(8,128)(2,1)S(1)}, u32[]{:S(2)}, u32[]{:S(2)}) collective-permute-start(bf16[384,128]{1,0:T(8,128)(2,1)S(1)} %add.12.refs_0_), channel_id=1, source_target_pairs={{0,4},{1,5},{2,6},{3,7},{4,0},{5,1},{6,2},{7,3},{8,12},{9,13},{10,... | collective-permute-start | bytes 294920 | tf_op jit(solution)/shard_map/ppermute | solution.py:25
  32.5 5.8 %collective-permute-start.11 = (bf16[256,128]{1,0:T(8,128)(2,1)S(1)}, bf16[256,128]{1,0:T(8,128)(2,1)S(1)}, u32[]{:S(2)}, u32[]{:S(2)}) collective-permute-start(bf16[256,128]{1,0:T(8,128)(2,1)S(1)} %get-tuple-element.56), channel_id=1, source_target_pairs={{0,8},{1,9},{2,10},{3,11},{4,12},{5,13},{6,14},{7,15},{8,0},{9,1},... | collective-permute-start | bytes 196616 | tf_op jit(solution)/shard_map/ppermute | solution.py:25
  39.0 3.6 %collective-permute-start.15 = (bf16[4,256,128]{2,1,0:T(8,128)(2,1)S(1)}, bf16[4,256,128]{2,1,0:T(8,128)(2,1)S(1)}, u32[]{:S(2)}, u32[]{:S(2)}) collective-permute-start(bf16[4,256,128]{2,1,0:T(8,128)(2,1)S(1)} %get-tuple-element.60.refs_2_), channel_id=1, source_target_pairs={{0,1},{1,0},{2,3},{3,2},{4,5},{5,4},{6,7},{7,6},{8,9},{9,8},{10,11... | collective-permute-start | bytes 786440 | tf_op jit(solution)/shard_map/ppermute | solution.py:25
  39.1 6.8 %collective-permute-start.17 = (bf16[256,128]{1,0:T(8,128)(2,1)S(1)}, bf16[256,128]{1,0:T(8,128)(2,1)S(1)}, u32[]{:S(2)}, u32[]{:S(2)}) collective-permute-start(bf16[256,128]{1,0:T(8,128)(2,1)S(1)} %add.13.refs_0_), channel_id=1, source_target_pairs={{0,6},{1,7},{2,4},{3,5},{4,2},{5,3},{6,0},{7,1},{8,14},{9,15},{10,... | collective-permute-start | bytes 196616 | tf_op jit(solution)/shard_map/ppermute | solution.py:25
  39.5 6.5 %collective-permute-start.16 = (bf16[256,128]{1,0:T(8,128)(2,1)S(1)}, bf16[256,128]{1,0:T(8,128)(2,1)S(1)}, u32[]{:S(2)}, u32[]{:S(2)}) collective-permute-start(bf16[256,128]{1,0:T(8,128)(2,1)S(1)} %add.13.refs_0_), channel_id=1, source_target_pairs={{0,4},{1,5},{2,6},{3,7},{4,0},{5,1},{6,2},{7,3},{8,12},{9,13},{10,... | collective-permute-start | bytes 196616 | tf_op jit(solution)/shard_map/ppermute | solution.py:25
  41.3 4.7 %collective-permute-start.14 = (bf16[256,128]{1,0:T(8,128)(2,1)S(1)}, bf16[256,128]{1,0:T(8,128)(2,1)S(1)}, u32[]{:S(2)}, u32[]{:S(2)}) collective-permute-start(bf16[256,128]{1,0:T(8,128)(2,1)S(1)} %add.13.refs_0_), channel_id=1, source_target_pairs={{0,2},{1,3},{2,0},{3,1},{4,6},{5,7},{6,4},{7,5},{8,10},{9,11},{10,... | collective-permute-start | bytes 196616 | tf_op jit(solution)/shard_map/ppermute | solution.py:25
  46.2 1.6 %collective-permute-start.18 = (bf16[4,256,128]{2,1,0:T(8,128)(2,1)S(1)}, bf16[4,256,128]{2,1,0:T(8,128)(2,1)S(1)}, u32[]{:S(2)}, u32[]{:S(2)}) collective-permute-start(bf16[4,256,128]{2,1,0:T(8,128)(2,1)S(1)} %couple.1.refs_2_), channel_id=1, source_target_pairs={{0,1},{1,0},{2,3},{3,2},{4,5},{5,4},{6,7},{7,6},{8,9},{9,8},{10,11... | collective-permute-start | bytes 786440 | tf_op jit(solution)/shard_map/ppermute | solution.py:25

commit v11 on v8

--- a/solution.py
+++ b/solution.py
@@ -33,8 +33,18 @@
     return swap(x, 1)
 
 
-def swap_square(x, part):
-    return swap(x, 2 * part)
+def swap_chips(x, distance):
+    return swap(x, 2 * distance)
+
+
+def swap_first(x):
+    count = lax.axis_size("pw")
+    return lax.ppermute(x, "pw", [(i, i ^ (2, 4)[i % 2]) for i in range(count)])
+
+
+def swap_second(x):
+    count = lax.axis_size("pw")
+    return lax.ppermute(x, "pw", [(i, i ^ (4, 2)[i % 2]) for i in range(count)])
 
 
 def load_kernel(where, projectors, flipped, slots, sems):
@@ -140,28 +150,51 @@
     )(where, owners, own, sibling, after)
 
 
-def pack_kernel(ours, theirs, quarters, *messages):
-    entries = ours.shape[0] // len(messages)
-    for at, message in enumerate(messages):
-        for entry in range(entries):
-            place = at * entries + entry
-            total = ours[place] + theirs[place].astype(jnp.float32)
-            message[entry * PCAP : (entry + 1) * PCAP] = total.astype(message.dtype)
-        message[entries * PCAP :] = quarters[at + 1]
-
-
-def pack(ours, theirs, quarters):
-    entries, _, width = ours.shape
-    entries //= SQUARE - 1
-    shape = jax.ShapeDtypeStruct((entries * PCAP + quarters.shape[1], width), jnp.bfloat16)
-    return pl.pallas_call(
-        pack_kernel,
-        in_specs=[VMEM] * 3,
-        out_specs=[VMEM] * (SQUARE - 1),
-        out_shape=[shape] * (SQUARE - 1),
-        compiler_params=PARAMS,
-        name="pack",
-    )(ours, theirs, quarters)
+def send_kernel(first, second, where, ours, theirs, quarters, message):
+    entries = ours.shape[0] // (1 if first == second else 2)
+    start, part = (0, first) if first == second else (where[0] * entries, 1 + where[0])
+    for entry in range(entries):
+        total = ours[start + entry] + theirs[start + entry].astype(jnp.float32)
+        message[entry * PCAP : (entry + 1) * PCAP] = total.astype(message.dtype)
+    message[entries * PCAP :] = quarters[part]
+
+
+def send(where, ours, theirs, quarters, parts):
+    count, _, width = ours.shape
+    rows = count // len(parts) * PCAP + quarters.shape[1]
+
+    def kernel(*refs):
+        send_kernel(parts[0], parts[-1], *refs)
+
+    return pl.pallas_call(
+        kernel,
+        in_specs=[SMEM] + [VMEM] * 3,
+        out_specs=VMEM,
+        out_shape=jax.ShapeDtypeStruct((rows, width), jnp.bfloat16),
+        compiler_params=PARAMS,
+        name="send",
+    )(where, ours, theirs, quarters)
+
+
+def forward_kernel(where, ours, theirs, quarters, got, message):
+    entries = ours.shape[0] // 2
+    start = (1 - where[0]) * entries
+    for entry in range(entries):
+        rows = slice(entry * PCAP, (entry + 1) * PCAP)
+        total = ours[start + entry] + theirs[start + entry].astype(jnp.float32)
+        message[rows] = (total + got[rows].astype(jnp.float32)).astype(message.dtype)
+    message[entries * PCAP :] = quarters[2 - where[0]] + got[entries * PCAP :]
+
+
+def forward(where, ours, theirs, quarters, got):
+    return pl.pallas_call(
+        forward_kernel,
+        in_specs=[SMEM] + [VMEM] * 4,
+        out_specs=VMEM,
+        out_shape=jax.ShapeDtypeStruct(got.shape, got.dtype),
+        compiler_params=PARAMS,
+        name="forward",
+    )(where, ours, theirs, quarters, got)
 
 
 def fold_kernel(ours, theirs, quarters, *refs):
@@ -236,7 +269,8 @@
     *messages, out, coupling = refs
     width = out.shape[2]
     entries = out.shape[0] // SQUARE
-    for part, message in enumerate(messages):
+    parts = (0, 1 + where[0], 2 - where[0], 3)
+    for part, message in zip(parts, messages):
         start = pl.multiple_of(((where[1] & 3) ^ part) * QUARTER, QUARTER)
         for cut in range(PCAP // width):
             lanes = slice(cut * width, (cut + 1) * width)
@@ -244,7 +278,7 @@
             coupling[pl.ds(start, QUARTER), lanes] = (
                 message[first : first + QUARTER] * allowed[pl.ds(start, QUARTER), lanes]
             )
-    for part, message in enumerate(messages):
+    for part, message in zip(parts, messages):
         wide = jnp.concatenate([message[e * PCAP : (e + 1) * PCAP] for e in range(entries)], axis=1)
         scaled = jnp.dot(coupling[...], wide, preferred_element_type=jnp.float32).astype(out.dtype)
         for entry in range(entries):
@@ -364,33 +398,43 @@
 
     own_table = couplings[0]
     sibling_table = swap_cores(own_table)
-    sent, kept = tuple(range(1, SQUARE)), (0,)
+    pair = (1, 2)
     if fast:
         flipped = load(where, projectors)
-        theirs, ours = project(where, flipped, band_coeffs, sent)
-        low_theirs, low_ours = project(where, flipped, band_coeffs, kept)
+
+        def partial(parts):
+            return project(where, flipped, band_coeffs, parts)
     else:
-        theirs, ours = project_plain(where, projectors, band_coeffs, sent)
-        low_theirs, low_ours = project_plain(where, projectors, band_coeffs, kept)
+
+        def partial(parts):
+            return project_plain(where, projectors, band_coeffs, parts)
+
+    theirs, ours = partial((3,))
+    theirs = swap_cores(theirs)
+    pair_theirs, pair_ours = partial(pair)
     quarters = choose(where, owners, own_table, sibling_table, width, ours)
-    theirs, low_ours = lax.optimization_barrier((swap_cores(theirs), low_ours))
-    messages = pack(ours, theirs, quarters)
+    got = swap_first(send(where, ours, theirs, quarters, (3,)))
+    pair_theirs = swap_cores(pair_theirs)
+    low_theirs, low_ours = partial((0,))
     low_theirs = swap_cores(low_theirs)
-    gots = [swap_square(message, part) for message, part in zip(messages, sent)]
-    allowed = mask(where, counts, atom_of, messages[0])
-
-    total, message = fold(low_ours, low_theirs, quarters, gots)
-    mine = add(total, swap_square(message, SQUARE))
+    got_first = swap_first(send(where, pair_ours, pair_theirs, quarters, pair))
+    message = forward(where, pair_ours, pair_theirs, quarters, got)
+    got_second = swap_second(message)
+    allowed = mask(where, counts, atom_of, message)
+
+    total, message = fold(low_ours, low_theirs, quarters, [got_first, got_second])
+    mine = add(total, swap_chips(message, SQUARE))
     distance = 2 * SQUARE
     while distance < chips:
         body = mine[: entries * PCAP].reshape(entries, PCAP, width)
         order = [entry ^ (distance // SQUARE) for entry in range(entries)]
         message = jnp.concatenate([body[jnp.array(order)].reshape(-1, width), mine[entries * PCAP :]])
-        mine = add(mine.astype(jnp.float32), swap_square(message, distance))
+        mine = add(mine.astype(jnp.float32), swap_chips(message, distance))
         distance *= 2
 
-    gathered = [mine] + [swap_square(mine, part) for part in sent]
-    scaled = couple(where, allowed, gathered)
+    second = swap_second(mine)
+    first = swap_first(mine)
+    scaled = couple(where, allowed, [mine, first, second, swap_first(second)])
     other = swap_cores(scaled)
     if not fast:
         return apply_plain(where, projectors, scaled, other)

time: 48.3 us -> 50.3 us (1.041)
  Pallas kernels: 14.6 us -> 17 us
  waiting for transfers between devices: 21.9 us -> 21.1 us
    ppermute x11 -> x6, waiting for transfers between devices: 21.9 us -> 8.81 us  [swap(): return lax.ppermute(x, 'pw', [(i, i ^ distance) for i in range(count)])]
    ppermute x0 -> x6, waiting for transfers between devices: none -> 12.3 us  [the longest x4 6.74 us: swap_first(): return lax.ppermute(x, 'pw', [(i, i ^ (2, 4)[i % 2]) for i in range(count)])]
    ppermute x0 -> x6, starting transfers between devices: none -> 7.33 us  [the longest x4 4.74 us: swap_first(): return lax.ppermute(x, 'pw', [(i, i ^ (2, 4)[i % 2]) for i in range(count)])]
    ppermute x11 -> x6, starting transfers between devices: 11.4 us -> 4.34 us  [swap(): return lax.ppermute(x, 'pw', [(i, i ^ distance) for i in range(count)])]
    pallas_call x1 -> x3, Pallas kernels: 0.07 us -> 1.72 us  [the longest x2 1.14 us: send(): pl.pallas_call(kernel, in_specs=[SMEM] + [VMEM] * 3, out_specs=VMEM, out_...]
    pallas_call x2 -> x3, Pallas kernels: 3.79 us -> 4.53 us  [project(): pl.pallas_call(kernel, in_specs=[SMEM, VMEM, VMEM], out_specs=[VMEM, VMEM...]
  transfers between devices with their start and end apart: 11 -> 12, of which waited for: 9 -> 7; matrix products, arithmetic and copies ran while one was open for 0% -> 0% of each run, Pallas kernels for 8% -> 21%
where the time goes in v11:
time: 50.3 us; the launch traced here: 50.1 us
  waiting for transfers between devices  21.1 us (42%)
  Pallas kernels  17 us (34%)
  starting transfers between devices  11.7 us (23%)
    ppermute x6, waiting for transfers between devices, swap(): return lax.ppermute(x, 'pw', [(i, i ^ distance) for i in range(count)])  8.81 us
    ppermute x4, waiting for transfers between devices, swap_first(): return lax.ppermute(x, 'pw', [(i, i ^ (2, 4)[i % 2]) for i in range(count)])  6.74 us
    ppermute x2, waiting for transfers between devices, swap_second(): return lax.ppermute(x, 'pw', [(i, i ^ (4, 2)[i % 2]) for i in range(count)])  5.52 us
    ppermute x4, starting transfers between devices, swap_first(): return lax.ppermute(x, 'pw', [(i, i ^ (2, 4)[i % 2]) for i in range(count)])  4.74 us
    pallas_call x3, Pallas kernels, project(): pl.pallas_call(kernel, in_specs=[SMEM, VMEM, VMEM], out_specs=[VMEM, VMEM...  4.53 us
    ppermute x6, starting transfers between devices, swap(): return lax.ppermute(x, 'pw', [(i, i ^ distance) for i in range(count)])  4.34 us
    pallas_call x1, Pallas kernels, finish(): pl.pallas_call(finish_kernel, in_specs=[SMEM] + [VMEM] * (3 + len(begun))...  4.29 us
    pallas_call x1, Pallas kernels, load(): pl.pallas_call(load_kernel, in_specs=[SMEM, HBM], out_specs=VMEM, out_sha...  2.68 us
  transfers between devices with their start and end apart: 12, of which 7 were waited for; matrix products, arithmetic and copies ran while one was open for 0% of the time, Pallas kernels for 21%

profile of v11, /device:TPU:0, one launch (start us, length us, event | category | flops | bytes accessed | tf_op | source)
XLA Modules:
  0.0 50.1 jit_solution(14199783878830398890)
XLA Ops:
  0.0 0.5 collective-permute-start.1
  0.5 0.1 pad_add_fusion.where.refs_0_
  0.5 0.0 copy-start
  0.5 2.7 %load.1.refs_1_ = bf16[512,2048]{1,0:T(8,128)(2,1)S(1)} custom-call(s32[3]{0:T(128)S(1)} %pad_add_fusion.where.refs_0_, bf16[2048,512]{1,0:T(8,128)(2,1)} %projectors.5), custom_call_target="tpu_custom_call" | custom-call | tf_op jit(solution)/shard_map/load/pallas_call | solution.py:69
  3.2 0.1 copy-done
  3.3 1.3 %project.4 = (bf16[2,256,128]{2,1,0:T(8,128)(2,1)S(1)}, f32[2,256,128]{2,1,0:T(8,128)S(1)}) custom-call(s32[3]{0:T(128)S(1)} %pad_add_fusion.where.refs_0_, bf16[512,2048]{1,0:T(8,128)(2,1)S(1)} %load.1.refs_1_, bf16[2048,1024]{1,0:T(8,128)(2,1)S(1)} %copy-done), custom_call_target="tpu_custom_call" | custom-call | flops 536870912 | bytes 1048576 | tf_op jit(solution)/shard_map/project/pallas_call | solution.py:99
  4.7 0.0 copy-start.2
  4.7 0.0 copy-start.5
  4.7 0.1 collective-permute-start.2
  4.8 1.9 %project.3 = (bf16[4,256,128]{2,1,0:T(8,128)(2,1)S(1)}, f32[4,256,128]{2,1,0:T(8,128)S(1)}) custom-call(s32[3]{0:T(128)S(1)} %pad_add_fusion.where.refs_0_, bf16[512,2048]{1,0:T(8,128)(2,1)S(1)} %load.1.refs_1_, bf16[2048,1024]{1,0:T(8,128)(2,1)S(1)} %copy-done), custom_call_target="tpu_custom_call" | custom-call | flops 1073741824 | bytes 2097152 | tf_op jit(solution)/shard_map/project/pallas_call | solution.py:99
  6.7 0.5 %collective-permute-start = (bf16[4,256,128]{2,1,0:T(8,128)(2,1)S(1)}, bf16[4,256,128]{2,1,0:T(8,128)(2,1)S(1)}, u32[]{:S(2)}, u32[]{:S(2)}) collective-permute-start(bf16[4,256,128]{2,1,0:T(8,128)(2,1)S(1)} %get-tuple-element.17), channel_id=1, source_target_pairs={{0,1},{1,0},{2,3},{3,2},{4,5},{5,4},{6,7},{7,6},{8,9},{9,8},{10,11... | collective-permute-start | bytes 786440 | tf_op jit(solution)/shard_map/ppermute | solution.py:29
  7.2 0.0 collective-permute-done.1.sibling
  7.2 0.0 copy-done.2
  7.2 0.0 copy-done.5
  7.3 0.6 %choose.1.refs_3_.quarters = bf16[4,128,128]{2,1,0:T(8,128)(2,1)S(1)} custom-call(s32[3]{0:T(128)S(1)} %pad_add_fusion.where.refs_0_, s32[2]{0:T(128)S(1)} %copy-done.5, f32[256,256]{1,0:T(8,128)S(1)} %bitcast.5, f32[256,256]{1,0:T(8,128)S(1)} %collective-permute-done.1.sibling, f32[2,256,128]{2,1,0:T(8,128)S(1)} %get-tuple-element.18.after.refs_1_), custom_call_target="tpu_custom_call" | custom-call | tf_op jit(solution)/shard_map/choose/pallas_call | solution.py:143
  7.8 0.0 collective-permute-done.2.refs_2_
  7.9 0.6 %send.2 = bf16[640,128]{1,0:T(8,128)(2,1)S(1)} custom-call(s32[3]{0:T(128)S(1)} %pad_add_fusion.where.refs_0_, f32[2,256,128]{2,1,0:T(8,128)S(1)} %get-tuple-element.18.after.refs_1_, bf16[2,256,128]{2,1,0:T(8,128)(2,1)S(1)} %collective-permute-done.2.refs_2_, bf16[4,128,128]{2,1,0:T(8,128)(2,1)S(1)} %choose.1.refs_3_.quarters), custom_call_target="tpu_custom_call" | custom-call | tf_op jit(solution)/shard_map/send/pallas_call | solution.py:169
  8.4 2.6 %collective-permute-start.3 = (bf16[640,128]{1,0:T(8,128)(2,1)S(1)}, bf16[640,128]{1,0:T(8,128)(2,1)S(1)}, u32[]{:S(2)}, u32[]{:S(2)}) collective-permute-start(bf16[640,128]{1,0:T(8,128)(2,1)S(1)} %send.2), channel_id=1, source_target_pairs={{0,2},{1,5},{2,0},{3,7},{4,6},{5,1},{6,4},{7,3},{8,10},{9,13},{10,... | collective-permute-start | bytes 491528 | tf_op jit(solution)/shard_map/ppermute | solution.py:42
  11.0 0.0 collective-permute-done.theirs.refs_2_
  11.0 0.6 %send.3 = bf16[640,128]{1,0:T(8,128)(2,1)S(1)} custom-call(s32[3]{0:T(128)S(1)} %pad_add_fusion.where.refs_0_, f32[4,256,128]{2,1,0:T(8,128)S(1)} %get-tuple-element.16.ours.refs_1_, bf16[4,256,128]{2,1,0:T(8,128)(2,1)S(1)} %collective-permute-done.theirs.refs_2_, bf16[4,128,128]{2,1,0:T(8,128)(2,1)S(1)} %choose.1.refs_3_.quarters), custom_call_target="tpu_custom_call" | custom-call | tf_op jit(solution)/shard_map/send/pallas_call | solution.py:169
  11.6 0.3 collective-permute-start.5
  11.9 2.4 %collective-permute-done.3.got = bf16[640,128]{1,0:T(8,128)(2,1)S(1)} collective-permute-done((bf16[640,128]{1,0:T(8,128)(2,1)S(1)}, bf16[640,128]{1,0:T(8,128)(2,1)S(1)}, u32[]{:S(2)}, u32[]{:S(2)}) %collective-permute-start.3) | collective-permute-done | bytes 163872 | tf_op jit(solution)/shard_map/ppermute | solution.py:42
  14.3 0.6 %forward.1.after = bf16[640,128]{1,0:T(8,128)(2,1)S(1)} custom-call(s32[3]{0:T(128)S(1)} %pad_add_fusion.where.refs_0_, f32[4,256,128]{2,1,0:T(8,128)S(1)} %get-tuple-element.16.ours.refs_1_, bf16[4,256,128]{2,1,0:T(8,128)(2,1)S(1)} %collective-permute-done.theirs.refs_2_, bf16[4,128,128]{2,1,0:T(8,128)(2,1)S(1)} %choose.1.refs_3_.quarters, ...), custom_call_target="tpu_custom_call" | custom-call | tf_op jit(solution)/shard_map/forward/pallas_call | solution.py:190
  14.9 0.0 copy-start.3
  14.9 0.0 copy-start.4
  14.9 2.1 %collective-permute-start.6 = (bf16[640,128]{1,0:T(8,128)(2,1)S(1)}, bf16[640,128]{1,0:T(8,128)(2,1)S(1)}, u32[]{:S(2)}, u32[]{:S(2)}) collective-permute-start(bf16[640,128]{1,0:T(8,128)(2,1)S(1)} %forward.1.after), channel_id=1, source_target_pairs={{0,4},{1,3},{2,6},{3,1},{4,0},{5,7},{6,2},{7,5},{8,12},{9,11},{10,... | collective-permute-start | bytes 491528 | tf_op jit(solution)/shard_map/ppermute | solution.py:47
  17.1 1.3 %project.5 = (bf16[2,256,128]{2,1,0:T(8,128)(2,1)S(1)}, f32[2,256,128]{2,1,0:T(8,128)S(1)}) custom-call(s32[3]{0:T(128)S(1)} %pad_add_fusion.where.refs_0_, bf16[512,2048]{1,0:T(8,128)(2,1)S(1)} %load.1.refs_1_, bf16[2048,1024]{1,0:T(8,128)(2,1)S(1)} %copy-done), custom_call_target="tpu_custom_call" | custom-call | flops 536870912 | bytes 1048576 | tf_op jit(solution)/shard_map/project/pallas_call | solution.py:99
  18.4 0.0 copy-start.1
  18.4 0.1 collective-permute-start.4
  18.5 1.3 %collective-permute-done.4.theirs = bf16[2,256,128]{2,1,0:T(8,128)(2,1)S(1)} collective-permute-done((bf16[2,256,128]{2,1,0:T(8,128)(2,1)S(1)}, bf16[2,256,128]{2,1,0:T(8,128)(2,1)S(1)}, u32[]{:S(2)}, u32[]{:S(2)}) %collective-permute-start.4) | collective-permute-done | bytes 131104 | tf_op jit(solution)/shard_map/ppermute | solution.py:29
  19.9 0.0 collective-permute-done.5.refs_0_
  19.9 0.5 %collective-permute-done.6.refs_1_ = bf16[640,128]{1,0:T(8,128)(2,1)S(1)} collective-permute-done((bf16[640,128]{1,0:T(8,128)(2,1)S(1)}, bf16[640,128]{1,0:T(8,128)(2,1)S(1)}, u32[]{:S(2)}, u32[]{:S(2)}) %collective-permute-start.6) | collective-permute-done | bytes 163872 | tf_op jit(solution)/shard_map/ppermute | solution.py:47
  20.4 0.1 fold.1
  20.5 3.1 %collective-permute-start.7 = (bf16[640,128]{1,0:T(8,128)(2,1)S(1)}, bf16[640,128]{1,0:T(8,128)(2,1)S(1)}, u32[]{:S(2)}, u32[]{:S(2)}) collective-permute-start(bf16[640,128]{1,0:T(8,128)(2,1)S(1)} %get-tuple-element.23), channel_id=1, source_target_pairs={{0,8},{1,9},{2,10},{3,11},{4,12},{5,13},{6,14},{7,15},{8,0},{9,1},... | collective-permute-start | bytes 491528 | tf_op jit(solution)/shard_map/ppermute | solution.py:29
  23.6 7.1 %collective-permute-done.7.right = bf16[640,128]{1,0:T(8,128)(2,1)S(1)} collective-permute-done((bf16[640,128]{1,0:T(8,128)(2,1)S(1)}, bf16[640,128]{1,0:T(8,128)(2,1)S(1)}, u32[]{:S(2)}, u32[]{:S(2)}) %collective-permute-start.7) | collective-permute-done | bytes 163872 | tf_op jit(solution)/shard_map/ppermute | solution.py:29
  30.7 0.4 collective-permute-start.9
  31.2 1.5 %collective-permute-start.8 = (bf16[640,128]{1,0:T(8,128)(2,1)S(1)}, bf16[640,128]{1,0:T(8,128)(2,1)S(1)}, u32[]{:S(2)}, u32[]{:S(2)}) collective-permute-start(bf16[640,128]{1,0:T(8,128)(2,1)S(1)} %add.11.refs_0_), channel_id=1, source_target_pairs={{0,2},{1,5},{2,0},{3,7},{4,6},{5,1},{6,4},{7,3},{8,10},{9,13},{10,... | collective-permute-start | bytes 491528 | tf_op jit(solution)/shard_map/ppermute | solution.py:42
  32.7 5.0 %collective-permute-done.9.refs_2_ = bf16[640,128]{1,0:T(8,128)(2,1)S(1)} collective-permute-done((bf16[640,128]{1,0:T(8,128)(2,1)S(1)}, bf16[640,128]{1,0:T(8,128)(2,1)S(1)}, u32[]{:S(2)}, u32[]{:S(2)}) %collective-permute-start.9) | collective-permute-done | bytes 163872 | tf_op jit(solution)/shard_map/ppermute | solution.py:47
  37.7 0.3 collective-permute-start.10
  38.0 0.0 copy-done.3
  38.0 0.0 copy-done.4
  38.0 0.7 %mask.1.allowed = bf16[256,256]{1,0:T(8,128)(2,1)S(1)} custom-call(s32[3]{0:T(128)S(1)} %pad_add_fusion.where.refs_0_, s32[2,4]{1,0:T(2,128)S(1)} %copy-done.4, s32[2,256]{1,0:T(2,128)S(1)} %copy-done.3, bf16[640,128]{1,0:T(8,128)(2,1)S(1)} %forward.1.after), custom_call_target="tpu_custom_call" | custom-call | tf_op jit(solution)/shard_map/mask/pallas_call | solution.py:258
  38.7 0.0 collective-permute-done.8.refs_1_
  38.7 4.3 %collective-permute-done.10.refs_3_ = bf16[640,128]{1,0:T(8,128)(2,1)S(1)} collective-permute-done((bf16[640,128]{1,0:T(8,128)(2,1)S(1)}, bf16[640,128]{1,0:T(8,128)(2,1)S(1)}, u32[]{:S(2)}, u32[]{:S(2)}) %collective-permute-start.10) | collective-permute-done | bytes 163872 | tf_op jit(solution)/shard_map/ppermute | solution.py:42
  43.0 0.9 %couple.1.scaled.mine = bf16[8,256,128]{2,1,0:T(8,128)(2,1)S(1)} custom-call(s32[3]{0:T(128)S(1)} %pad_add_fusion.where.refs_0_, bf16[256,256]{1,0:T(8,128)(2,1)S(1)} %mask.1.allowed, bf16[640,128]{1,0:T(8,128)(2,1)S(1)} %add.11.refs_0_, bf16[640,128]{1,0:T(8,128)(2,1)S(1)} %collective-permute-done.8.refs_1_, ...), custom_call_target="tpu_custom_call" | custom-call | tf_op jit(solution)/shard_map/couple/pallas_call | solution.py:291
  43.9 0.1 collective-permute-start.11
  43.9 0.0 copy-done.1
  44.0 1.5 %begin.1 = (f32[2048,256]{1,0:T(8,128)S(1)}, f32[2048,256]{1,0:T(8,128)S(1)}, f32[2048,256]{1,0:T(8,128)S(1)}) custom-call(s32[3]{0:T(128)S(1)} %pad_add_fusion.where.refs_0_, bf16[2048,512]{1,0:T(8,128)(2,1)S(1)} %copy-done.1, bf16[8,256,128]{2,1,0:T(8,128)(2,1)S(1)} %couple.1.scaled.mine), custom_call_target="tpu_custom_call" | custom-call | flops 805306368 | bytes 2097152 | tf_op jit(solution)/shard_map/begin/pallas_call | solution.py:314
  45.5 0.4 collective-permute-done.11.other
  45.8 4.3 %finish.1 = bf16[2048,1024]{1,0:T(8,128)(2,1)} custom-call(s32[3]{0:T(128)S(1)} %pad_add_fusion.where.refs_0_, bf16[2048,512]{1,0:T(8,128)(2,1)S(1)} %copy-done.1, bf16[8,256,128]{2,1,0:T(8,128)(2,1)S(1)} %couple.1.scaled.mine, bf16[8,256,128]{2,1,0:T(8,128)(2,1)S(1)} %collective-permute-done.11.other, f32[2048,256]{1,0:T(8,128)S(1)} %get-tuple-element.24.refs_0_, ...), custom_call_target="tpu_custom_call" | custom-call | flops 1073741824 | bytes 6291456 | tf_op jit(solution)/shard_map/finish/pallas_call | solution.py:362
  (1 shorter events, 0.0 us)
Async XLA Ops:
  0.0 7.2 %collective-permute-start.1 = (f32[256,256]{1,0:T(8,128)}, f32[256,256]{1,0:T(8,128)S(1)}, u32[]{:S(2)}, u32[]{:S(2)}) collective-permute-start(f32[256,256]{1,0:T(8,128)} %bitcast.4), channel_id=1, source_target_pairs={{0,1},{1,0},{2,3},{3,2},{4,5},{5,4},{6,7},{7,6},{8,9},{9,8},{10,11... | collective-permute-start | bytes 786440 | tf_op jit(solution)/shard_map/ppermute | solution.py:29
  0.5 2.8 %copy-start = (bf16[2048,1024]{1,0:T(8,128)(2,1)S(1)}, bf16[2048,1024]{1,0:T(8,128)(2,1)}, u32[]{:S(2)}) copy-start(bf16[2048,1024]{1,0:T(8,128)(2,1)} %refs_2_.5) | copy-start | bytes 12582916
  4.7 2.6 %copy-start.2 = (f32[1,256,256]{2,1,0:T(8,128)S(1)}, f32[1,256,256]{2,1,0:T(8,128)}, u32[]{:S(2)}) copy-start(f32[1,256,256]{2,1,0:T(8,128)} %param.11) | copy-start | bytes 786436
  4.7 2.5 %copy-start.5 = (s32[2]{0:T(128)S(1)}, s32[2]{0:T(128)}, u32[]{:S(2)}) copy-start(s32[2]{0:T(128)} %owners.1) | copy-start | bytes 28
  4.7 3.1 %collective-permute-start.2 = (bf16[2,256,128]{2,1,0:T(8,128)(2,1)S(1)}, bf16[2,256,128]{2,1,0:T(8,128)(2,1)S(1)}, u32[]{:S(2)}, u32[]{:S(2)}) collective-permute-start(bf16[2,256,128]{2,1,0:T(8,128)(2,1)S(1)} %get-tuple-element.19), channel_id=1, source_target_pairs={{0,1},{1,0},{2,3},{3,2},{4,5},{5,4},{6,7},{7,6},{8,9},{9,8},{10,11... | collective-permute-start | bytes 393224 | tf_op jit(solution)/shard_map/ppermute | solution.py:29
  6.7 4.3 %collective-permute-start = (bf16[4,256,128]{2,1,0:T(8,128)(2,1)S(1)}, bf16[4,256,128]{2,1,0:T(8,128)(2,1)S(1)}, u32[]{:S(2)}, u32[]{:S(2)}) collective-permute-start(bf16[4,256,128]{2,1,0:T(8,128)(2,1)S(1)} %get-tuple-element.17), channel_id=1, source_target_pairs={{0,1},{1,0},{2,3},{3,2},{4,5},{5,4},{6,7},{7,6},{8,9},{9,8},{10,11... | collective-permute-start | bytes 786440 | tf_op jit(solution)/shard_map/ppermute | solution.py:29
  8.4 5.9 %collective-permute-start.3 = (bf16[640,128]{1,0:T(8,128)(2,1)S(1)}, bf16[640,128]{1,0:T(8,128)(2,1)S(1)}, u32[]{:S(2)}, u32[]{:S(2)}) collective-permute-start(bf16[640,128]{1,0:T(8,128)(2,1)S(1)} %send.2), channel_id=1, source_target_pairs={{0,2},{1,5},{2,0},{3,7},{4,6},{5,1},{6,4},{7,3},{8,10},{9,13},{10,... | collective-permute-start | bytes 491528 | tf_op jit(solution)/shard_map/ppermute | solution.py:42
  11.6 8.2 %collective-permute-start.5 = (bf16[640,128]{1,0:T(8,128)(2,1)S(1)}, bf16[640,128]{1,0:T(8,128)(2,1)S(1)}, u32[]{:S(2)}, u32[]{:S(2)}) collective-permute-start(bf16[640,128]{1,0:T(8,128)(2,1)S(1)} %send.3), channel_id=1, source_target_pairs={{0,2},{1,5},{2,0},{3,7},{4,6},{5,1},{6,4},{7,3},{8,10},{9,13},{10,... | collective-permute-start | bytes 491528 | tf_op jit(solution)/shard_map/ppermute | solution.py:42
  14.9 23.1 %copy-start.3 = (s32[2,256]{1,0:T(2,128)S(1)}, s32[2,256]{1,0:T(2,128)}, u32[]{:S(2)}) copy-start(s32[2,256]{1,0:T(2,128)} %atom_of.1) | copy-start | bytes 6148
  14.9 23.0 %copy-start.4 = (s32[2,4]{1,0:T(2,128)S(1)}, s32[2,4]{1,0:T(2,128)}, u32[]{:S(2)}) copy-start(s32[2,4]{1,0:T(2,128)} %counts.1) | copy-start | bytes 100
  14.9 5.4 %collective-permute-start.6 = (bf16[640,128]{1,0:T(8,128)(2,1)S(1)}, bf16[640,128]{1,0:T(8,128)(2,1)S(1)}, u32[]{:S(2)}, u32[]{:S(2)}) collective-permute-start(bf16[640,128]{1,0:T(8,128)(2,1)S(1)} %forward.1.after), channel_id=1, source_target_pairs={{0,4},{1,3},{2,6},{3,1},{4,0},{5,7},{6,2},{7,5},{8,12},{9,11},{10,... | collective-permute-start | bytes 491528 | tf_op jit(solution)/shard_map/ppermute | solution.py:47
  18.4 25.5 %copy-start.1 = (bf16[2048,512]{1,0:T(8,128)(2,1)S(1)}, bf16[2048,512]{1,0:T(8,128)(2,1)}, u32[]{:S(2)}) copy-start(bf16[2048,512]{1,0:T(8,128)(2,1)} %projectors.5) | copy-start | bytes 6291460
  18.4 1.4 %collective-permute-start.4 = (bf16[2,256,128]{2,1,0:T(8,128)(2,1)S(1)}, bf16[2,256,128]{2,1,0:T(8,128)(2,1)S(1)}, u32[]{:S(2)}, u32[]{:S(2)}) collective-permute-start(bf16[2,256,128]{2,1,0:T(8,128)(2,1)S(1)} %get-tuple-element.21), channel_id=1, source_target_pairs={{0,1},{1,0},{2,3},{3,2},{4,5},{5,4},{6,7},{7,6},{8,9},{9,8},{10,11... | collective-permute-start | bytes 393224 | tf_op jit(solution)/shard_map/ppermute | solution.py:29
  20.5 10.2 %collective-permute-start.7 = (bf16[640,128]{1,0:T(8,128)(2,1)S(1)}, bf16[640,128]{1,0:T(8,128)(2,1)S(1)}, u32[]{:S(2)}, u32[]{:S(2)}) collective-permute-start(bf16[640,128]{1,0:T(8,128)(2,1)S(1)} %get-tuple-element.23), channel_id=1, source_target_pairs={{0,8},{1,9},{2,10},{3,11},{4,12},{5,13},{6,14},{7,15},{8,0},{9,1},... | collective-permute-start | bytes 491528 | tf_op jit(solution)/shard_map/ppermute | solution.py:29
  30.7 7.0 %collective-permute-start.9 = (bf16[640,128]{1,0:T(8,128)(2,1)S(1)}, bf16[640,128]{1,0:T(8,128)(2,1)S(1)}, u32[]{:S(2)}, u32[]{:S(2)}) collective-permute-start(bf16[640,128]{1,0:T(8,128)(2,1)S(1)} %add.11.refs_0_), channel_id=1, source_target_pairs={{0,4},{1,3},{2,6},{3,1},{4,0},{5,7},{6,2},{7,5},{8,12},{9,11},{10,... | collective-permute-start | bytes 491528 | tf_op jit(solution)/shard_map/ppermute | solution.py:47
  31.2 7.5 %collective-permute-start.8 = (bf16[640,128]{1,0:T(8,128)(2,1)S(1)}, bf16[640,128]{1,0:T(8,128)(2,1)S(1)}, u32[]{:S(2)}, u32[]{:S(2)}) collective-permute-start(bf16[640,128]{1,0:T(8,128)(2,1)S(1)} %add.11.refs_0_), channel_id=1, source_target_pairs={{0,2},{1,5},{2,0},{3,7},{4,6},{5,1},{6,4},{7,3},{8,10},{9,13},{10,... | collective-permute-start | bytes 491528 | tf_op jit(solution)/shard_map/ppermute | solution.py:42
  37.7 5.3 %collective-permute-start.10 = (bf16[640,128]{1,0:T(8,128)(2,1)S(1)}, bf16[640,128]{1,0:T(8,128)(2,1)S(1)}, u32[]{:S(2)}, u32[]{:S(2)}) collective-permute-start(bf16[640,128]{1,0:T(8,128)(2,1)S(1)} %collective-permute-done.9.refs_2_), channel_id=1, source_target_pairs={{0,2},{1,5},{2,0},{3,7},{4,6},{5,1},{6,4},{7,3},{8,10},{9,13},{10,... | collective-permute-start | bytes 491528 | tf_op jit(solution)/shard_map/ppermute | solution.py:42
  43.9 2.0 %collective-permute-start.11 = (bf16[8,256,128]{2,1,0:T(8,128)(2,1)S(1)}, bf16[8,256,128]{2,1,0:T(8,128)(2,1)S(1)}, u32[]{:S(2)}, u32[]{:S(2)}) collective-permute-start(bf16[8,256,128]{2,1,0:T(8,128)(2,1)S(1)} %couple.1.scaled.mine), channel_id=1, source_target_pairs={{0,1},{1,0},{2,3},{3,2},{4,5},{5,4},{6,7},{7,6},{8,9},{9,8},{10,11... | collective-permute-start | bytes 1572872 | tf_op jit(solution)/shard_map/ppermute | solution.py:29

commit v12 on v8

v12 whole, which is shorter than its diff:
```python
import jax
import jax.numpy as jnp
from jax import lax
from jax.experimental import pallas as pl
from jax.experimental.pallas import tpu as pltpu
from jax.sharding import PartitionSpec as P

CHANNELS = 4
CH_CAP = 64
PCAP = 256
LANES = 128
SQUARE = 4
QUARTER = PCAP // SQUARE
ROW_BLOCK = 512
ROW_BLOCKS = (512, 512, 512, 256, 256)
COPY_ROWS = 128
PARAMS = pltpu.CompilerParams(vmem_limit_bytes=40 * 1024 * 1024)
VMEM = pl.BlockSpec(memory_space=pltpu.VMEM)
SMEM = pl.BlockSpec(memory_space=pltpu.SMEM)
HBM = pl.BlockSpec(memory_space=pltpu.HBM)
ANY = pl.BlockSpec(memory_space=pl.ANY)


def place():
    me = lax.axis_index("pw")
    return lax.rem(me, 2), lax.div(me, 2)


def block_of(chip, part, entry):
    return chip ^ (part + SQUARE * entry)


def swap(x, distance):
    count = lax.axis_size("pw")
    return lax.ppermute(x, "pw", [(i, i ^ distance) for i in range(count)])


def swap_cores(x):
    return swap(x, 1)


def swap_square(x, part):
    return swap(x, 2 * part)


def pair_at(columns, rows, part):
    chip = place()[1]
    starts = [pl.multiple_of(block_of(chip, part, entry) * LANES, LANES) for entry in range(2)]
    return jnp.concatenate([columns[rows, pl.ds(start, LANES)] for start in starts], axis=1)


def keep_sums(ours, theirs, at, sums):
    for entry in range(2):
        lanes = slice(entry * LANES, (entry + 1) * LANES)
        ours[2 * at + entry] = sums[:PCAP, lanes]
        theirs[2 * at + entry] = sums[PCAP:, lanes].astype(theirs.dtype)


def project_sent_kernel(projectors, bands, theirs, ours, flipped, columns, slots, totals, slot_sems, column_sems):
    core = place()[0]
    count = slot_sems.shape[0]
    depth = slots.shape[0] // count
    copies = []
    for at in range(count):
        rows = slice(at * depth, (at + 1) * depth)
        copies.append(
            (
                pltpu.make_async_copy(projectors.at[rows], slots.at[rows], slot_sems.at[at]),
                pltpu.make_async_copy(bands.at[rows], columns.at[rows], column_sems.at[at]),
            )
        )
        for copy in copies[-1]:
            copy.start()
    for at in range(count):
        rows = slice(at * depth, (at + 1) * depth)
        copies[at][0].wait()
        for side, group in enumerate((core, 1 - core)):
            start = pl.multiple_of(group * PCAP, PCAP)
            flipped[side * PCAP : (side + 1) * PCAP, rows] = slots[rows, pl.ds(start, PCAP)].T
        copies[at][1].wait()
        for part in range(1, SQUARE):
            sums = jnp.dot(
                flipped[:, rows], pair_at(columns, rows, part), preferred_element_type=jnp.float32
            )
            if at:
                sums = totals[part - 1] + sums
            if at < count - 1:
                totals[part - 1] = sums
            else:
                keep_sums(ours, theirs, part - 1, sums)


def sums_shape(parts):
    shape = (2 * parts, PCAP, LANES)
    return [jax.ShapeDtypeStruct(shape, jnp.bfloat16), jax.ShapeDtypeStruct(shape, jnp.float32)]


def project_sent(projectors, band_coeffs):
    depth, slots = projectors.shape
    bands = band_coeffs.shape[1]
    blocks = 4
    return pl.pallas_call(
        project_sent_kernel,
        in_specs=[HBM, HBM],
        out_specs=[VMEM] * 4,
        out_shape=sums_shape(SQUARE - 1)
        + [
            jax.ShapeDtypeStruct((slots, depth), jnp.bfloat16),
            jax.ShapeDtypeStruct((depth, bands), jnp.bfloat16),
        ],
        scratch_shapes=[
            pltpu.VMEM((depth, slots), jnp.bfloat16),
            pltpu.VMEM((SQUARE - 1, slots, 2 * LANES), jnp.float32),
            pltpu.SemaphoreType.DMA((blocks,)),
            pltpu.SemaphoreType.DMA((blocks,)),
        ],
        compiler_params=PARAMS,
        cost_estimate=pl.CostEstimate(
            flops=2 * depth * slots * bands, bytes_accessed=2 * depth * (bands + slots), transcendentals=0
        ),
        name="project_sent",
    )(
        pltpu.with_memory_space_constraint(projectors, pltpu.HBM),
        pltpu.with_memory_space_constraint(band_coeffs, pltpu.HBM),
    )


def project_kept_kernel(flipped, columns, theirs, ours):
    rows = slice(0, columns.shape[0])
    sums = jnp.dot(flipped[...], pair_at(columns, rows, 0), preferred_element_type=jnp.float32)
    keep_sums(ours, theirs, 0, sums)


def project_kept(flipped, columns):
    slots, depth = flipped.shape
    return pl.pallas_call(
        project_kept_kernel,
        in_specs=[VMEM, VMEM],
        out_specs=[VMEM, VMEM],
        out_shape=sums_shape(1),
        compiler_params=PARAMS,
        cost_estimate=pl.CostEstimate(
            flops=4 * depth * slots * LANES, bytes_accessed=2 * depth * slots, transcendentals=0
        ),
        name="project_kept",
    )(flipped, columns)


def project_plain(projectors, band_coeffs, parts):
    depth, bands = band_coeffs.shape
    chips = lax.axis_size("pw") // 2
    blocks = jnp.stack([block_of(place()[1], q, r) for q in parts for r in range(chips // SQUARE)])
    columns = jnp.take(band_coeffs.reshape(depth, chips, bands // chips), blocks, axis=1)
    outs = []
    core = place()[0]
    for group, dtype in ((1 - core, jnp.bfloat16), (core, jnp.float32)):
        slots = lax.dynamic_slice_in_dim(projectors, group * PCAP, PCAP, 1)
        sums = jnp.einsum("ds,dhw->hsw", slots, columns, preferred_element_type=jnp.float32)
        outs.append(sums.astype(dtype))
    return outs


def choose_kernel(owners, own, sibling, after, out):
    del after
    core, chip = place()
    me = 2 * chip + core
    owner = jnp.where(core == 0, owners[0], owners[1])
    width = out.shape[2]
    for part in range(SQUARE):
        rows = pl.ds(pl.multiple_of(((chip & 3) ^ part) * QUARTER, QUARTER), QUARTER)
        piece = jnp.where(owner == me, own[rows], jnp.where(owner == (me ^ 1), sibling[rows], 0.0))
        for cut in range(PCAP // width):
            out[part, cut * QUARTER : (cut + 1) * QUARTER] = piece[:, cut * width : (cut + 1) * width].astype(
                out.dtype
            )


def choose(owners, own, sibling, width, after):
    return pl.pallas_call(
        choose_kernel,
        in_specs=[SMEM, VMEM, VMEM, ANY],
        out_specs=VMEM,
        out_shape=jax.ShapeDtypeStruct((SQUARE, QUARTER * PCAP // width, width), jnp.bfloat16),
        compiler_params=PARAMS,
        name="choose",
    )(owners, own, sibling, after)


def pack_kernel(ours, theirs, quarters, *messages):
    entries = ours.shape[0] // len(messages)
    for at, message in enumerate(messages):
        for entry in range(entries):
            place = at * entries + entry
            total = ours[place] + theirs[place].astype(jnp.float32)
            message[entry * PCAP : (entry + 1) * PCAP] = total.astype(message.dtype)
        message[entries * PCAP :] = quarters[at + 1]


def pack(ours, theirs, quarters):
    entries, _, width = ours.shape
    entries //= SQUARE - 1
    shape = jax.ShapeDtypeStruct((entries * PCAP + quarters.shape[1], width), jnp.bfloat16)
    return pl.pallas_call(
        pack_kernel,
        in_specs=[VMEM] * 3,
        out_specs=[VMEM] * (SQUARE - 1),
        out_shape=[shape] * (SQUARE - 1),
        compiler_params=PARAMS,
        name="pack",
    )(ours, theirs, quarters)


def fold_kernel(ours, theirs, quarters, *refs):
    *gots, kept, message = refs
    entries = ours.shape[0]
    for entry in range(entries):
        rows = slice(entry * PCAP, (entry + 1) * PCAP)
        total = ours[entry] + theirs[entry].astype(jnp.float32)
        for got in gots:
            total = total + got[rows].astype(jnp.float32)
        kept[rows] = total
        away = entry ^ 1
        message[away * PCAP : (away + 1) * PCAP] = total.astype(message.dtype)
    table = quarters[0]
    for got in gots:
        table = table + got[entries * PCAP :]
    kept[entries * PCAP :] = table.astype(kept.dtype)
    message[entries * PCAP :] = table


def fold(ours, theirs, quarters, gots):
    shape = gots[0].shape
    return pl.pallas_call(
        fold_kernel,
        in_specs=[VMEM] * (3 + len(gots)),
        out_specs=[VMEM, VMEM],
        out_shape=[jax.ShapeDtypeStruct(shape, jnp.float32), jax.ShapeDtypeStruct(shape, jnp.bfloat16)],
        compiler_params=PARAMS,
        name="fold",
    )(ours, theirs, quarters, *gots)


def add_kernel(left, right, out):
    out[...] = (left[...] + right[...].astype(jnp.float32)).astype(out.dtype)


def add(left, right):
    return pl.pallas_call(
        add_kernel,
        in_specs=[VMEM, VMEM],
        out_specs=VMEM,
        out_shape=jax.ShapeDtypeStruct(left.shape, jnp.bfloat16),
        compiler_params=PARAMS,
        name="add",
    )(left, right)


def mask_kernel(counts, atom_of, after, out):
    del after
    core = place()[0]
    slot = lax.broadcasted_iota(jnp.int32, (1, PCAP), 1)
    limit = jnp.zeros((1, PCAP), jnp.int32)
    for channel in range(CHANNELS):
        limit = jnp.where(slot >= channel * CH_CAP, channel * CH_CAP + counts[core, channel], limit)
    atoms = jnp.where(core == 0, atom_of[0:1], atom_of[1:2])
    code = jnp.broadcast_to(jnp.where(slot < limit, atoms, -1), (PCAP, PCAP))
    out[...] = jnp.where((code == code.T) & (code >= 0), 1.0, 0.0).astype(out.dtype)


def mask(counts, atom_of, after):
    return pl.pallas_call(
        mask_kernel,
        in_specs=[SMEM, VMEM, ANY],
        out_specs=VMEM,
        out_shape=jax.ShapeDtypeStruct((PCAP, PCAP), jnp.bfloat16),
        compiler_params=PARAMS,
        name="mask",
    )(counts, atom_of, after)


def couple_kernel(allowed, *refs):
    *messages, out, coupling = refs
    width = out.shape[2]
    entries = out.shape[0] // SQUARE
    corner = place()[1] & 3
    for part, message in enumerate(messages):
        start = pl.multiple_of((corner ^ part) * QUARTER, QUARTER)
        for cut in range(PCAP // width):
            lanes = slice(cut * width, (cut + 1) * width)
            first = entries * PCAP + cut * QUARTER
            coupling[pl.ds(start, QUARTER), lanes] = (
                message[first : first + QUARTER] * allowed[pl.ds(start, QUARTER), lanes]
            )
    for part, message in enumerate(messages):
        wide = jnp.concatenate([message[e * PCAP : (e + 1) * PCAP] for e in range(entries)], axis=1)
        scaled = jnp.dot(coupling[...], wide, preferred_element_type=jnp.float32).astype(out.dtype)
        for entry in range(entries):
            out[part * entries + entry] = scaled[:, entry * width : (entry + 1) * width]


def couple(allowed, messages):
    rows, width = messages[0].shape
    entries = (rows - QUARTER * PCAP // width) // PCAP
    return pl.pallas_call(
        couple_kernel,
        in_specs=[VMEM] * (1 + SQUARE),
        out_specs=VMEM,
        out_shape=jax.ShapeDtypeStruct((SQUARE * entries, PCAP, width), jnp.bfloat16),
        scratch_shapes=[pltpu.VMEM((PCAP, PCAP), jnp.bfloat16)],
        compiler_params=PARAMS,
        name="couple",
    )(allowed, *messages)


def group_slots(group):
    return pl.ds(pl.multiple_of(group * PCAP, PCAP), PCAP)


def wide_pair(scaled, part):
    return jnp.concatenate([scaled[2 * part], scaled[2 * part + 1]], axis=1)


def begin_kernel(projectors, scaled, out):
    slots = group_slots(place()[0])
    for part in range(SQUARE):
        for block in range(projectors.shape[0] // ROW_BLOCK):
            rows = slice(block * ROW_BLOCK, (block + 1) * ROW_BLOCK)
            out[part, rows] = jnp.dot(
                projectors[rows, slots], wide_pair(scaled, part), preferred_element_type=jnp.float32
            )


def begin(projectors, scaled):
    depth, slots = projectors.shape
    return pl.pallas_call(
        begin_kernel,
        in_specs=[VMEM, VMEM],
        out_specs=VMEM,
        out_shape=jax.ShapeDtypeStruct((SQUARE, depth, 2 * LANES), jnp.float32),
        compiler_params=PARAMS,
        cost_estimate=pl.CostEstimate(
            flops=2 * depth * slots * LANES * SQUARE, bytes_accessed=2 * depth * slots, transcendentals=0
        ),
        name="begin",
    )(projectors, scaled)


def finish_kernel(projectors, begun, other, out, blocks, sems):
    core, chip = place()
    slots = group_slots(1 - core)
    copies = []
    first = 0
    for size in ROW_BLOCKS:
        rows = slice(first, first + size)
        first += size
        for part in range(SQUARE):
            sums = begun[part, rows] + jnp.dot(
                projectors[rows, slots], wide_pair(other, part), preferred_element_type=jnp.float32
            )
            for entry in range(2):
                start = pl.multiple_of(block_of(chip, part, entry) * LANES, LANES)
                lanes = slice(entry * LANES, (entry + 1) * LANES)
                blocks[rows, pl.ds(start, LANES)] = sums[:, lanes].astype(blocks.dtype)
        for start in range(rows.start, rows.stop, COPY_ROWS):
            written = slice(start, start + COPY_ROWS)
            copies.append(pltpu.make_async_copy(blocks.at[written], out.at[written], sems.at[len(copies)]))
            copies[-1].start()
    for copy in copies:
        copy.wait()


def finish(projectors, begun, other):
    depth, slots = projectors.shape
    bands = other.shape[0] * LANES
    return pl.pallas_call(
        finish_kernel,
        in_specs=[VMEM] * 3,
        out_specs=HBM,
        out_shape=jax.ShapeDtypeStruct((depth, bands), jnp.bfloat16),
        scratch_shapes=[
            pltpu.VMEM((depth, bands), jnp.bfloat16),
            pltpu.SemaphoreType.DMA((depth // COPY_ROWS,)),
        ],
        compiler_params=PARAMS,
        cost_estimate=pl.CostEstimate(
            flops=depth * slots * bands, bytes_accessed=2 * depth * (slots + bands), transcendentals=0
        ),
        name="finish",
    )(projectors, begun, other)


def apply_plain(projectors, mine, other):
    chips, _, width = mine.shape
    blocks = jnp.stack([block_of(place()[1], q, r) for q in range(SQUARE) for r in range(chips // SQUARE)])
    rows = []
    for group in range(2):
        part = jnp.where(place()[0] == group, mine, other)
        part = jnp.zeros_like(part).at[blocks].set(part)
        rows.append(part.transpose(1, 0, 2).reshape(PCAP, chips * width))
    return jnp.dot(projectors, jnp.concatenate(rows), preferred_element_type=jnp.float32).astype(jnp.bfloat16)


def local(band_coeffs, projectors, counts, atom_of, owners, couplings):
    chips = lax.axis_size("pw") // 2
    entries = chips // SQUARE
    width = band_coeffs.shape[1] // chips
    fast = width == LANES and entries == 2
    own_table = couplings[0]
    sibling_table = swap_cores(own_table)
    sent, kept = tuple(range(1, SQUARE)), (0,)
    if fast:
        theirs, ours, flipped, columns = project_sent(projectors, band_coeffs)
        low_theirs, low_ours = project_kept(flipped, columns)
    else:
        theirs, ours = project_plain(projectors, band_coeffs, sent)
        low_theirs, low_ours = project_plain(projectors, band_coeffs, kept)
    quarters = choose(owners, own_table, sibling_table, width, ours)
    theirs, low_ours = lax.optimization_barrier((swap_cores(theirs), low_ours))
    messages = pack(ours, theirs, quarters)
    low_theirs = swap_cores(low_theirs)
    gots = [swap_square(message, part) for message, part in zip(messages, sent)]
    allowed = mask(counts, atom_of, messages[0])

    total, message = fold(low_ours, low_theirs, quarters, gots)
    mine = add(total, swap_square(message, SQUARE))
    distance = 2 * SQUARE
    while distance < chips:
        body = mine[: entries * PCAP].reshape(entries, PCAP, width)
        order = [entry ^ (distance // SQUARE) for entry in range(entries)]
        message = jnp.concatenate([body[jnp.array(order)].reshape(-1, width), mine[entries * PCAP :]])
        mine = add(mine.astype(jnp.float32), swap_square(message, distance))
        distance *= 2

    gathered = [mine] + [swap_square(mine, part) for part in sent]
    scaled = couple(allowed, gathered)
    other = swap_cores(scaled)
    if not fast:
        return apply_plain(projectors, scaled, other)
    return finish(projectors, begin(projectors, scaled), other)


def solution(mesh):
    placed = (
        P("pw", "group"),
        P("pw", "group"),
        P("group", None),
        P("group", None),
        P("group"),
        P("pw", "group", None),
    )
    return jax.shard_map(
        local, mesh=mesh, in_specs=placed, out_specs=P("pw", "group"), check_vma=False
    )
```

time: 48.3 us -> 46.4 us (0.961)
  Pallas kernels: 14.6 us -> 12.1 us
  waiting for transfers between devices: 21.9 us -> 22.7 us
    pallas_call x8 -> x7, Pallas kernels: 14.4 us -> 11.9 us  [the longest x1 4.98 us: project_sent(): pl.pallas_call(project_sent_kernel, in_specs=[HBM, HBM], out_specs=[VMEM]...]
    ppermute x11, waiting for transfers between devices: 21.9 us -> 22.7 us  [swap(): return lax.ppermute(x, 'pw', [(i, i ^ distance) for i in range(count)])]
  transfers between devices with their start and end apart: 11 -> 11, of which waited for: 9 -> 9; matrix products, arithmetic and copies ran while one was open for 0% -> 0% of each run, Pallas kernels for 8% -> 7%
where the time goes in v12:
time: 46.4 us; the launch traced here: 46.3 us
  waiting for transfers between devices  22.7 us (49%)
  Pallas kernels  12.1 us (26%)
  starting transfers between devices  11.4 us (25%)
    ppermute x11, waiting for transfers between devices, swap(): return lax.ppermute(x, 'pw', [(i, i ^ distance) for i in range(count)])  22.7 us
    ppermute x11, starting transfers between devices, swap(): return lax.ppermute(x, 'pw', [(i, i ^ distance) for i in range(count)])  11.4 us
    pallas_call x1, Pallas kernels, project_sent(): pl.pallas_call(project_sent_kernel, in_specs=[HBM, HBM], out_specs=[VMEM]...  4.98 us
    pallas_call x1, Pallas kernels, finish(): pl.pallas_call(finish_kernel, in_specs=[VMEM] * 3, out_specs=HBM, out_sha...  3.3 us
    pallas_call x1, Pallas kernels, begin(): pl.pallas_call(begin_kernel, in_specs=[VMEM, VMEM], out_specs=VMEM, out_s...  1.25 us
  transfers between devices with their start and end apart: 11, of which 9 were waited for; matrix products, arithmetic and copies ran while one was open for 0% of the time, Pallas kernels for 7%

profile of v12, /device:TPU:0, one launch (start us, length us, event | category | flops | bytes accessed | tf_op | source)
XLA Modules:
  0.0 46.3 jit_solution(1585222342561888232)
XLA Ops:
  0.0 0.0 copy-start.1
  0.0 5.0 %project_sent.1 = (bf16[6,256,128]{2,1,0:T(8,128)(2,1)S(1)}, f32[6,256,128]{2,1,0:T(8,128)S(1)}, bf16[512,2048]{1,0:T(8,128)(2,1)S(1)}, bf16[2048,1024]{1,0:T(8,128)(2,1)S(1)}) custom-call(bf16[2048,512]{1,0:T(8,128)(2,1)} %projectors.5, bf16[2048,1024]{1,0:T(8,128)(2,1)} %bands.1), custom_call_target="tpu_custom_call" | custom-call | flops 2147483648 | bytes 6291456 | tf_op jit(solution)/shard_map/project_sent/pallas_call | solution.py:102
  5.0 0.0 copy-start.4
  5.0 0.5 %collective-permute-start = (bf16[6,256,128]{2,1,0:T(8,128)(2,1)S(1)}, bf16[6,256,128]{2,1,0:T(8,128)(2,1)S(1)}, u32[]{:S(2)}, u32[]{:S(2)}) collective-permute-start(bf16[6,256,128]{2,1,0:T(8,128)(2,1)S(1)} %get-tuple-element.19), channel_id=1, source_target_pairs={{0,1},{1,0},{2,3},{3,2},{4,5},{5,4},{6,7},{7,6},{8,9},{9,8},{10,11... | collective-permute-start | bytes 1179656 | tf_op jit(solution)/shard_map/ppermute | solution.py:35
  5.5 0.0 copy-done.1
  5.5 0.1 collective-permute-start.1
  5.6 0.0 copy-start.2
  5.6 0.0 copy-start.3
  5.6 0.8 %project_kept.1 = (bf16[2,256,128]{2,1,0:T(8,128)(2,1)S(1)}, f32[2,256,128]{2,1,0:T(8,128)S(1)}) custom-call(bf16[512,2048]{1,0:T(8,128)(2,1)S(1)} %get-tuple-element.20.flipped, bf16[2048,1024]{1,0:T(8,128)(2,1)S(1)} %get-tuple-element.21.columns), custom_call_target="tpu_custom_call" | custom-call | flops 536870912 | bytes 2097152 | tf_op jit(solution)/shard_map/project_kept/pallas_call | solution.py:136
  6.4 0.0 copy-start
  6.4 0.8 %collective-permute-done.1.sibling = f32[256,256]{1,0:T(8,128)S(1)} collective-permute-done((f32[256,256]{1,0:T(8,128)S(1)}, f32[256,256]{1,0:T(8,128)S(1)}, u32[]{:S(2)}, u32[]{:S(2)}) %collective-permute-start.1) | collective-permute-done | bytes 262176 | tf_op jit(solution)/shard_map/ppermute | solution.py:35
  7.2 0.0 copy-done.4
  7.3 0.6 %choose.1.quarters = bf16[4,128,128]{2,1,0:T(8,128)(2,1)S(1)} custom-call(s32[2]{0:T(128)S(1)} %copy-done.4, f32[256,256]{1,0:T(8,128)S(1)} %bitcast.2, f32[256,256]{1,0:T(8,128)S(1)} %collective-permute-done.1.sibling, f32[6,256,128]{2,1,0:T(8,128)S(1)} %get-tuple-element.18.after.ours), custom_call_target="tpu_custom_call" | custom-call | tf_op jit(solution)/shard_map/choose/pallas_call | solution.py:179
  7.8 0.0 collective-permute-done.theirs
  7.9 0.1 pack.1
  7.9 3.0 %collective-permute-start.4 = (bf16[640,128]{1,0:T(8,128)(2,1)S(1)}, bf16[640,128]{1,0:T(8,128)(2,1)S(1)}, u32[]{:S(2)}, u32[]{:S(2)}) collective-permute-start(bf16[640,128]{1,0:T(8,128)(2,1)S(1)} %get-tuple-element.27), channel_id=1, source_target_pairs={{0,4},{1,5},{2,6},{3,7},{4,0},{5,1},{6,2},{7,3},{8,12},{9,13},{10,... | collective-permute-start | bytes 491528 | tf_op jit(solution)/shard_map/ppermute | solution.py:35
  10.9 1.4 %collective-permute-start.5 = (bf16[640,128]{1,0:T(8,128)(2,1)S(1)}, bf16[640,128]{1,0:T(8,128)(2,1)S(1)}, u32[]{:S(2)}, u32[]{:S(2)}) collective-permute-start(bf16[640,128]{1,0:T(8,128)(2,1)S(1)} %get-tuple-element.28), channel_id=1, source_target_pairs={{0,6},{1,7},{2,4},{3,5},{4,2},{5,3},{6,0},{7,1},{8,14},{9,15},{10,... | collective-permute-start | bytes 491528 | tf_op jit(solution)/shard_map/ppermute | solution.py:35
  12.3 0.1 collective-permute-start.3
  12.5 0.0 collective-permute-start.2
  12.5 1.3 %collective-permute-done.2.theirs = bf16[2,256,128]{2,1,0:T(8,128)(2,1)S(1)} collective-permute-done((bf16[2,256,128]{2,1,0:T(8,128)(2,1)S(1)}, bf16[2,256,128]{2,1,0:T(8,128)(2,1)S(1)}, u32[]{:S(2)}, u32[]{:S(2)}) %collective-permute-start.2) | collective-permute-done | bytes 131104 | tf_op jit(solution)/shard_map/ppermute | solution.py:35
  13.8 2.1 %collective-permute-done.4.refs_1_ = bf16[640,128]{1,0:T(8,128)(2,1)S(1)} collective-permute-done((bf16[640,128]{1,0:T(8,128)(2,1)S(1)}, bf16[640,128]{1,0:T(8,128)(2,1)S(1)}, u32[]{:S(2)}, u32[]{:S(2)}) %collective-permute-start.4) | collective-permute-done | bytes 163872 | tf_op jit(solution)/shard_map/ppermute | solution.py:35
  15.9 4.3 %collective-permute-done.5.refs_2_ = bf16[640,128]{1,0:T(8,128)(2,1)S(1)} collective-permute-done((bf16[640,128]{1,0:T(8,128)(2,1)S(1)}, bf16[640,128]{1,0:T(8,128)(2,1)S(1)}, u32[]{:S(2)}, u32[]{:S(2)}) %collective-permute-start.5) | collective-permute-done | bytes 163872 | tf_op jit(solution)/shard_map/ppermute | solution.py:35
  20.2 1.4 %collective-permute-done.3.refs_0_ = bf16[640,128]{1,0:T(8,128)(2,1)S(1)} collective-permute-done((bf16[640,128]{1,0:T(8,128)(2,1)S(1)}, bf16[640,128]{1,0:T(8,128)(2,1)S(1)}, u32[]{:S(2)}, u32[]{:S(2)}) %collective-permute-start.3) | collective-permute-done | bytes 163872 | tf_op jit(solution)/shard_map/ppermute | solution.py:35
  21.5 0.1 fold.1
  21.6 2.6 %collective-permute-start.6 = (bf16[640,128]{1,0:T(8,128)(2,1)S(1)}, bf16[640,128]{1,0:T(8,128)(2,1)S(1)}, u32[]{:S(2)}, u32[]{:S(2)}) collective-permute-start(bf16[640,128]{1,0:T(8,128)(2,1)S(1)} %get-tuple-element.30), channel_id=1, source_target_pairs={{0,8},{1,9},{2,10},{3,11},{4,12},{5,13},{6,14},{7,15},{8,0},{9,1},... | collective-permute-start | bytes 491528 | tf_op jit(solution)/shard_map/ppermute | solution.py:35
  24.3 5.8 %collective-permute-done.6.right = bf16[640,128]{1,0:T(8,128)(2,1)S(1)} collective-permute-done((bf16[640,128]{1,0:T(8,128)(2,1)S(1)}, bf16[640,128]{1,0:T(8,128)(2,1)S(1)}, u32[]{:S(2)}, u32[]{:S(2)}) %collective-permute-start.6) | collective-permute-done | bytes 163872 | tf_op jit(solution)/shard_map/ppermute | solution.py:35
  30.1 0.7 %collective-permute-start.9 = (bf16[640,128]{1,0:T(8,128)(2,1)S(1)}, bf16[640,128]{1,0:T(8,128)(2,1)S(1)}, u32[]{:S(2)}, u32[]{:S(2)}) collective-permute-start(bf16[640,128]{1,0:T(8,128)(2,1)S(1)} %add.1.refs_0_), channel_id=1, source_target_pairs={{0,6},{1,7},{2,4},{3,5},{4,2},{5,3},{6,0},{7,1},{8,14},{9,15},{10,... | collective-permute-start | bytes 491528 | tf_op jit(solution)/shard_map/ppermute | solution.py:35
  30.8 2.4 %collective-permute-start.8 = (bf16[640,128]{1,0:T(8,128)(2,1)S(1)}, bf16[640,128]{1,0:T(8,128)(2,1)S(1)}, u32[]{:S(2)}, u32[]{:S(2)}) collective-permute-start(bf16[640,128]{1,0:T(8,128)(2,1)S(1)} %add.1.refs_0_), channel_id=1, source_target_pairs={{0,4},{1,5},{2,6},{3,7},{4,0},{5,1},{6,2},{7,3},{8,12},{9,13},{10,... | collective-permute-start | bytes 491528 | tf_op jit(solution)/shard_map/ppermute | solution.py:35
  33.2 0.5 %collective-permute-start.7 = (bf16[640,128]{1,0:T(8,128)(2,1)S(1)}, bf16[640,128]{1,0:T(8,128)(2,1)S(1)}, u32[]{:S(2)}, u32[]{:S(2)}) collective-permute-start(bf16[640,128]{1,0:T(8,128)(2,1)S(1)} %add.1.refs_0_), channel_id=1, source_target_pairs={{0,2},{1,3},{2,0},{3,1},{4,6},{5,7},{6,4},{7,5},{8,10},{9,11},{10,... | collective-permute-start | bytes 491528 | tf_op jit(solution)/shard_map/ppermute | solution.py:35
  33.7 0.0 copy-done.2
  33.7 0.0 copy-done.3
  33.7 0.7 %mask.1.allowed = bf16[256,256]{1,0:T(8,128)(2,1)S(1)} custom-call(s32[2,4]{1,0:T(2,128)S(1)} %copy-done.3, s32[2,256]{1,0:T(2,128)S(1)} %copy-done.2, bf16[640,128]{1,0:T(8,128)(2,1)S(1)} %get-tuple-element.24.after), custom_call_target="tpu_custom_call" | custom-call | tf_op jit(solution)/shard_map/mask/pallas_call | solution.py:271
  34.4 2.9 %collective-permute-done.9.refs_3_ = bf16[640,128]{1,0:T(8,128)(2,1)S(1)} collective-permute-done((bf16[640,128]{1,0:T(8,128)(2,1)S(1)}, bf16[640,128]{1,0:T(8,128)(2,1)S(1)}, u32[]{:S(2)}, u32[]{:S(2)}) %collective-permute-start.9) | collective-permute-done | bytes 163872 | tf_op jit(solution)/shard_map/ppermute | solution.py:35
  37.3 3.4 %collective-permute-done.8.refs_2_ = bf16[640,128]{1,0:T(8,128)(2,1)S(1)} collective-permute-done((bf16[640,128]{1,0:T(8,128)(2,1)S(1)}, bf16[640,128]{1,0:T(8,128)(2,1)S(1)}, u32[]{:S(2)}, u32[]{:S(2)}) %collective-permute-start.8) | collective-permute-done | bytes 163872 | tf_op jit(solution)/shard_map/ppermute | solution.py:35
  40.7 0.0 collective-permute-done.7.refs_1_
  40.7 0.3 couple.1.scaled
  41.0 0.1 collective-permute-start.10
  41.1 0.0 copy-done
  41.1 1.3 %begin.1.begun = f32[4,2048,256]{2,1,0:T(8,128)S(1)} custom-call(bf16[2048,512]{1,0:T(8,128)(2,1)S(1)} %copy-done, bf16[8,256,128]{2,1,0:T(8,128)(2,1)S(1)} %couple.1.scaled), custom_call_target="tpu_custom_call" | custom-call | flops 1073741824 | bytes 2097152 | tf_op jit(solution)/shard_map/begin/pallas_call | solution.py:335
  42.3 0.6 %collective-permute-done.10.other = bf16[8,256,128]{2,1,0:T(8,128)(2,1)S(1)} collective-permute-done((bf16[8,256,128]{2,1,0:T(8,128)(2,1)S(1)}, bf16[8,256,128]{2,1,0:T(8,128)(2,1)S(1)}, u32[]{:S(2)}, u32[]{:S(2)}) %collective-permute-start.10) | collective-permute-done | bytes 524320 | tf_op jit(solution)/shard_map/ppermute | solution.py:35
  43.0 3.3 %finish.1 = bf16[2048,1024]{1,0:T(8,128)(2,1)} custom-call(bf16[2048,512]{1,0:T(8,128)(2,1)S(1)} %copy-done, f32[4,2048,256]{2,1,0:T(8,128)S(1)} %begin.1.begun, bf16[8,256,128]{2,1,0:T(8,128)(2,1)S(1)} %collective-permute-done.10.other), custom_call_target="tpu_custom_call" | custom-call | flops 1073741824 | bytes 6291456 | tf_op jit(solution)/shard_map/finish/pallas_call | solution.py:375
  (1 shorter events, 0.0 us)
Async XLA Ops:
  0.0 5.5 %copy-start.1 = (f32[1,256,256]{2,1,0:T(8,128)S(1)}, f32[1,256,256]{2,1,0:T(8,128)}, u32[]{:S(2)}) copy-start(f32[1,256,256]{2,1,0:T(8,128)} %param.11) | copy-start | bytes 786436
  5.0 2.3 %copy-start.4 = (s32[2]{0:T(128)S(1)}, s32[2]{0:T(128)}, u32[]{:S(2)}) copy-start(s32[2]{0:T(128)} %owners.1) | copy-start | bytes 28
  5.0 2.8 %collective-permute-start = (bf16[6,256,128]{2,1,0:T(8,128)(2,1)S(1)}, bf16[6,256,128]{2,1,0:T(8,128)(2,1)S(1)}, u32[]{:S(2)}, u32[]{:S(2)}) collective-permute-start(bf16[6,256,128]{2,1,0:T(8,128)(2,1)S(1)} %get-tuple-element.19), channel_id=1, source_target_pairs={{0,1},{1,0},{2,3},{3,2},{4,5},{5,4},{6,7},{7,6},{8,9},{9,8},{10,11... | collective-permute-start | bytes 1179656 | tf_op jit(solution)/shard_map/ppermute | solution.py:35
  5.5 1.7 %collective-permute-start.1 = (f32[256,256]{1,0:T(8,128)S(1)}, f32[256,256]{1,0:T(8,128)S(1)}, u32[]{:S(2)}, u32[]{:S(2)}) collective-permute-start(f32[256,256]{1,0:T(8,128)S(1)} %bitcast.1), channel_id=1, source_target_pairs={{0,1},{1,0},{2,3},{3,2},{4,5},{5,4},{6,7},{7,6},{8,9},{9,8},{10,11... | collective-permute-start | bytes 786440 | tf_op jit(solution)/shard_map/ppermute | solution.py:35
  5.6 28.1 %copy-start.2 = (s32[2,256]{1,0:T(2,128)S(1)}, s32[2,256]{1,0:T(2,128)}, u32[]{:S(2)}) copy-start(s32[2,256]{1,0:T(2,128)} %atom_of.1) | copy-start | bytes 6148
  5.6 28.1 %copy-start.3 = (s32[2,4]{1,0:T(2,128)S(1)}, s32[2,4]{1,0:T(2,128)}, u32[]{:S(2)}) copy-start(s32[2,4]{1,0:T(2,128)} %counts.1) | copy-start | bytes 100
  6.4 34.6 %copy-start = (bf16[2048,512]{1,0:T(8,128)(2,1)S(1)}, bf16[2048,512]{1,0:T(8,128)(2,1)}, u32[]{:S(2)}) copy-start(bf16[2048,512]{1,0:T(8,128)(2,1)} %projectors.5) | copy-start | bytes 6291460
  7.9 8.0 %collective-permute-start.4 = (bf16[640,128]{1,0:T(8,128)(2,1)S(1)}, bf16[640,128]{1,0:T(8,128)(2,1)S(1)}, u32[]{:S(2)}, u32[]{:S(2)}) collective-permute-start(bf16[640,128]{1,0:T(8,128)(2,1)S(1)} %get-tuple-element.27), channel_id=1, source_target_pairs={{0,4},{1,5},{2,6},{3,7},{4,0},{5,1},{6,2},{7,3},{8,12},{9,13},{10,... | collective-permute-start | bytes 491528 | tf_op jit(solution)/shard_map/ppermute | solution.py:35
  10.9 9.3 %collective-permute-start.5 = (bf16[640,128]{1,0:T(8,128)(2,1)S(1)}, bf16[640,128]{1,0:T(8,128)(2,1)S(1)}, u32[]{:S(2)}, u32[]{:S(2)}) collective-permute-start(bf16[640,128]{1,0:T(8,128)(2,1)S(1)} %get-tuple-element.28), channel_id=1, source_target_pairs={{0,6},{1,7},{2,4},{3,5},{4,2},{5,3},{6,0},{7,1},{8,14},{9,15},{10,... | collective-permute-start | bytes 491528 | tf_op jit(solution)/shard_map/ppermute | solution.py:35
  12.3 9.2 %collective-permute-start.3 = (bf16[640,128]{1,0:T(8,128)(2,1)S(1)}, bf16[640,128]{1,0:T(8,128)(2,1)S(1)}, u32[]{:S(2)}, u32[]{:S(2)}) collective-permute-start(bf16[640,128]{1,0:T(8,128)(2,1)S(1)} %get-tuple-element.24.after), channel_id=1, source_target_pairs={{0,2},{1,3},{2,0},{3,1},{4,6},{5,7},{6,4},{7,5},{8,10},{9,11},{10,... | collective-permute-start | bytes 491528 | tf_op jit(solution)/shard_map/ppermute | solution.py:35
  12.5 1.3 %collective-permute-start.2 = (bf16[2,256,128]{2,1,0:T(8,128)(2,1)S(1)}, bf16[2,256,128]{2,1,0:T(8,128)(2,1)S(1)}, u32[]{:S(2)}, u32[]{:S(2)}) collective-permute-start(bf16[2,256,128]{2,1,0:T(8,128)(2,1)S(1)} %get-tuple-element.26), channel_id=1, source_target_pairs={{0,1},{1,0},{2,3},{3,2},{4,5},{5,4},{6,7},{7,6},{8,9},{9,8},{10,11... | collective-permute-start | bytes 393224 | tf_op jit(solution)/shard_map/ppermute | solution.py:35
  21.6 8.5 %collective-permute-start.6 = (bf16[640,128]{1,0:T(8,128)(2,1)S(1)}, bf16[640,128]{1,0:T(8,128)(2,1)S(1)}, u32[]{:S(2)}, u32[]{:S(2)}) collective-permute-start(bf16[640,128]{1,0:T(8,128)(2,1)S(1)} %get-tuple-element.30), channel_id=1, source_target_pairs={{0,8},{1,9},{2,10},{3,11},{4,12},{5,13},{6,14},{7,15},{8,0},{9,1},... | collective-permute-start | bytes 491528 | tf_op jit(solution)/shard_map/ppermute | solution.py:35
  30.1 7.2 %collective-permute-start.9 = (bf16[640,128]{1,0:T(8,128)(2,1)S(1)}, bf16[640,128]{1,0:T(8,128)(2,1)S(1)}, u32[]{:S(2)}, u32[]{:S(2)}) collective-permute-start(bf16[640,128]{1,0:T(8,128)(2,1)S(1)} %add.1.refs_0_), channel_id=1, source_target_pairs={{0,6},{1,7},{2,4},{3,5},{4,2},{5,3},{6,0},{7,1},{8,14},{9,15},{10,... | collective-permute-start | bytes 491528 | tf_op jit(solution)/shard_map/ppermute | solution.py:35
  30.8 9.8 %collective-permute-start.8 = (bf16[640,128]{1,0:T(8,128)(2,1)S(1)}, bf16[640,128]{1,0:T(8,128)(2,1)S(1)}, u32[]{:S(2)}, u32[]{:S(2)}) collective-permute-start(bf16[640,128]{1,0:T(8,128)(2,1)S(1)} %add.1.refs_0_), channel_id=1, source_target_pairs={{0,4},{1,5},{2,6},{3,7},{4,0},{5,1},{6,2},{7,3},{8,12},{9,13},{10,... | collective-permute-start | bytes 491528 | tf_op jit(solution)/shard_map/ppermute | solution.py:35
  33.2 7.5 %collective-permute-start.7 = (bf16[640,128]{1,0:T(8,128)(2,1)S(1)}, bf16[640,128]{1,0:T(8,128)(2,1)S(1)}, u32[]{:S(2)}, u32[]{:S(2)}) collective-permute-start(bf16[640,128]{1,0:T(8,128)(2,1)S(1)} %add.1.refs_0_), channel_id=1, source_target_pairs={{0,2},{1,3},{2,0},{3,1},{4,6},{5,7},{6,4},{7,5},{8,10},{9,11},{10,... | collective-permute-start | bytes 491528 | tf_op jit(solution)/shard_map/ppermute | solution.py:35
  41.0 2.0 %collective-permute-start.10 = (bf16[8,256,128]{2,1,0:T(8,128)(2,1)S(1)}, bf16[8,256,128]{2,1,0:T(8,128)(2,1)S(1)}, u32[]{:S(2)}, u32[]{:S(2)}) collective-permute-start(bf16[8,256,128]{2,1,0:T(8,128)(2,1)S(1)} %couple.1.scaled), channel_id=1, source_target_pairs={{0,1},{1,0},{2,3},{3,2},{4,5},{5,4},{6,7},{7,6},{8,9},{9,8},{10,11... | collective-permute-start | bytes 1572872 | tf_op jit(solution)/shard_map/ppermute | solution.py:35

commit v13 on v12

--- a/solution.py
+++ b/solution.py
@@ -14,6 +14,7 @@
 ROW_BLOCK = 512
 ROW_BLOCKS = (512, 512, 512, 256, 256)
 COPY_ROWS = 128
+GATHERED = (0, 2, 3, 1)
 PARAMS = pltpu.CompilerParams(vmem_limit_bytes=40 * 1024 * 1024)
 VMEM = pl.BlockSpec(memory_space=pltpu.VMEM)
 SMEM = pl.BlockSpec(memory_space=pltpu.SMEM)
@@ -69,15 +70,20 @@
                 pltpu.make_async_copy(bands.at[rows], columns.at[rows], column_sems.at[at]),
             )
         )
-        for copy in copies[-1]:
+    for pair in copies[:2]:
+        for copy in pair:
             copy.start()
     for at in range(count):
         rows = slice(at * depth, (at + 1) * depth)
         copies[at][0].wait()
+        if at + 2 < count:
+            copies[at + 2][0].start()
         for side, group in enumerate((core, 1 - core)):
             start = pl.multiple_of(group * PCAP, PCAP)
             flipped[side * PCAP : (side + 1) * PCAP, rows] = slots[rows, pl.ds(start, PCAP)].T
         copies[at][1].wait()
+        if at + 2 < count:
+            copies[at + 2][1].start()
         for part in range(1, SQUARE):
             sums = jnp.dot(
                 flipped[:, rows], pair_at(columns, rows, part), preferred_element_type=jnp.float32
@@ -164,7 +170,7 @@
     del after
     core, chip = place()
     me = 2 * chip + core
-    owner = jnp.where(core == 0, owners[0], owners[1])
+    owner = jnp.where(core == 0, owners[0:1, :], owners[1:2, :])
     width = out.shape[2]
     for part in range(SQUARE):
         rows = pl.ds(pl.multiple_of(((chip & 3) ^ part) * QUARTER, QUARTER), QUARTER)
@@ -178,12 +184,12 @@
 def choose(owners, own, sibling, width, after):
     return pl.pallas_call(
         choose_kernel,
-        in_specs=[SMEM, VMEM, VMEM, ANY],
+        in_specs=[VMEM, VMEM, VMEM, ANY],
         out_specs=VMEM,
         out_shape=jax.ShapeDtypeStruct((SQUARE, QUARTER * PCAP // width, width), jnp.bfloat16),
         compiler_params=PARAMS,
         name="choose",
-    )(owners, own, sibling, after)
+    )(jnp.broadcast_to(owners[:, None], (owners.shape[0], PCAP)), own, sibling, after)
 
 
 def pack_kernel(ours, theirs, quarters, *messages):
@@ -283,7 +289,7 @@
     width = out.shape[2]
     entries = out.shape[0] // SQUARE
     corner = place()[1] & 3
-    for part, message in enumerate(messages):
+    for part, message in zip(GATHERED, messages):
         start = pl.multiple_of((corner ^ part) * QUARTER, QUARTER)
         for cut in range(PCAP // width):
             lanes = slice(cut * width, (cut + 1) * width)
@@ -291,7 +297,7 @@
             coupling[pl.ds(start, QUARTER), lanes] = (
                 message[first : first + QUARTER] * allowed[pl.ds(start, QUARTER), lanes]
             )
-    for part, message in enumerate(messages):
+    for part, message in zip(GATHERED, messages):
         wide = jnp.concatenate([message[e * PCAP : (e + 1) * PCAP] for e in range(entries)], axis=1)
         scaled = jnp.dot(coupling[...], wide, preferred_element_type=jnp.float32).astype(out.dtype)
         for entry in range(entries):
@@ -410,6 +416,7 @@
     sent, kept = tuple(range(1, SQUARE)), (0,)
     if fast:
         theirs, ours, flipped, columns = project_sent(projectors, band_coeffs)
+        theirs, sibling_table = lax.optimization_barrier((theirs, sibling_table))
         low_theirs, low_ours = project_kept(flipped, columns)
     else:
         theirs, ours = project_plain(projectors, band_coeffs, sent)
@@ -418,7 +425,7 @@
     theirs, low_ours = lax.optimization_barrier((swap_cores(theirs), low_ours))
     messages = pack(ours, theirs, quarters)
     low_theirs = swap_cores(low_theirs)
-    gots = [swap_square(message, part) for message, part in zip(messages, sent)]
+    gots = [swap_square(messages[part - 1], part) for part in (2, 1, 3)]
     allowed = mask(counts, atom_of, messages[0])
 
     total, message = fold(low_ours, low_theirs, quarters, gots)
@@ -431,8 +438,7 @@
         mine = add(mine.astype(jnp.float32), swap_square(message, distance))
         distance *= 2
 
-    gathered = [mine] + [swap_square(mine, part) for part in sent]
-    scaled = couple(allowed, gathered)
+    scaled = couple(allowed, [swap_square(mine, part) if part else mine for part in GATHERED])
     other = swap_cores(scaled)
     if not fast:
         return apply_plain(projectors, scaled, other)

time: 46.4 us -> 46.1 us (level)
  Pallas kernels: 12.1 us -> 11.5 us
    pallas_call x1, Pallas kernels: 0.58 us -> 0.03 us  [choose(): pl.pallas_call(choose_kernel, in_specs=[VMEM, VMEM, VMEM, ANY], out_specs...]
    ppermute x11, waiting for transfers between devices: 22.7 us -> 23.1 us  [swap(): return lax.ppermute(x, 'pw', [(i, i ^ distance) for i in range(count)])]
  transfers between devices with their start and end apart: 11 -> 11, of which waited for: 9 -> 9; matrix products, arithmetic and copies ran while one was open for 0% -> 0% of each run, Pallas kernels for 7% -> 17%
where the time goes in v13:
time: 46.1 us; the launch traced here: 46 us
  waiting for transfers between devices  23.1 us (50%)
  Pallas kernels  11.5 us (25%)
  starting transfers between devices  11.1 us (24%)
    ppermute x11, waiting for transfers between devices, swap(): return lax.ppermute(x, 'pw', [(i, i ^ distance) for i in range(count)])  23.1 us
    ppermute x11, starting transfers between devices, swap(): return lax.ppermute(x, 'pw', [(i, i ^ distance) for i in range(count)])  11.1 us
    pallas_call x1, Pallas kernels, project_sent(): pl.pallas_call(project_sent_kernel, in_specs=[HBM, HBM], out_specs=[VMEM]...  4.95 us
    pallas_call x1, Pallas kernels, finish(): pl.pallas_call(finish_kernel, in_specs=[VMEM] * 3, out_specs=HBM, out_sha...  3.3 us
    pallas_call x1, Pallas kernels, begin(): pl.pallas_call(begin_kernel, in_specs=[VMEM, VMEM], out_specs=VMEM, out_s...  1.25 us
  transfers between devices with their start and end apart: 11, of which 9 were waited for; matrix products, arithmetic and copies ran while one was open for 0% of the time, Pallas kernels for 17%

profile of v13, /device:TPU:0, one launch (start us, length us, event | category | flops | bytes accessed | tf_op | source)
XLA Modules:
  0.0 46.0 jit_solution(1647961813475237687)
XLA Ops:
  0.0 0.5 collective-permute-start
  0.5 4.9 %project_sent.1 = (bf16[6,256,128]{2,1,0:T(8,128)(2,1)S(1)}, f32[6,256,128]{2,1,0:T(8,128)S(1)}, bf16[512,2048]{1,0:T(8,128)(2,1)S(1)}, bf16[2048,1024]{1,0:T(8,128)(2,1)S(1)}) custom-call(bf16[2048,512]{1,0:T(8,128)(2,1)} %projectors.5, bf16[2048,1024]{1,0:T(8,128)(2,1)} %bands.1), custom_call_target="tpu_custom_call" | custom-call | flops 2147483648 | bytes 6291456 | tf_op jit(solution)/shard_map/project_sent/pallas_call | solution.py:108
  5.4 0.0 copy-start.4
  5.4 0.0 copy-start.1
  5.4 0.0 collective-permute-done.sibling
  5.4 0.1 collective-permute-start.1
  5.6 0.0 copy-start.2
  5.6 0.0 copy-start.3
  5.6 0.8 %project_kept.1 = (bf16[2,256,128]{2,1,0:T(8,128)(2,1)S(1)}, f32[2,256,128]{2,1,0:T(8,128)S(1)}) custom-call(bf16[512,2048]{1,0:T(8,128)(2,1)S(1)} %get-tuple-element.23.flipped, bf16[2048,1024]{1,0:T(8,128)(2,1)S(1)} %get-tuple-element.24.columns), custom_call_target="tpu_custom_call" | custom-call | flops 536870912 | bytes 2097152 | tf_op jit(solution)/shard_map/project_kept/pallas_call | solution.py:142
  6.4 0.0 copy-done.4
  6.4 0.0 copy-start
  6.4 0.1 broadcast_in_dim.2.owners
  6.5 0.0 copy-done.1
  6.5 0.7 %collective-permute-done.1.theirs = bf16[6,256,128]{2,1,0:T(8,128)(2,1)S(1)} collective-permute-done((bf16[6,256,128]{2,1,0:T(8,128)(2,1)S(1)}, bf16[6,256,128]{2,1,0:T(8,128)(2,1)S(1)}, u32[]{:S(2)}, u32[]{:S(2)}) %collective-permute-start.1) | collective-permute-done | bytes 393248 | tf_op jit(solution)/shard_map/ppermute | solution.py:36
  7.2 0.1 pack.1
  7.3 2.8 %collective-permute-start.3 = (bf16[640,128]{1,0:T(8,128)(2,1)S(1)}, bf16[640,128]{1,0:T(8,128)(2,1)S(1)}, u32[]{:S(2)}, u32[]{:S(2)}) collective-permute-start(bf16[640,128]{1,0:T(8,128)(2,1)S(1)} %get-tuple-element.31), channel_id=1, source_target_pairs={{0,4},{1,5},{2,6},{3,7},{4,0},{5,1},{6,2},{7,3},{8,12},{9,13},{10,... | collective-permute-start | bytes 491528 | tf_op jit(solution)/shard_map/ppermute | solution.py:36
  10.1 1.4 %collective-permute-start.5 = (bf16[640,128]{1,0:T(8,128)(2,1)S(1)}, bf16[640,128]{1,0:T(8,128)(2,1)S(1)}, u32[]{:S(2)}, u32[]{:S(2)}) collective-permute-start(bf16[640,128]{1,0:T(8,128)(2,1)S(1)} %get-tuple-element.32), channel_id=1, source_target_pairs={{0,6},{1,7},{2,4},{3,5},{4,2},{5,3},{6,0},{7,1},{8,14},{9,15},{10,... | collective-permute-start | bytes 491528 | tf_op jit(solution)/shard_map/ppermute | solution.py:36
  11.5 0.1 collective-permute-start.4
  11.6 0.0 collective-permute-start.2
  11.6 1.3 %collective-permute-done.2.theirs = bf16[2,256,128]{2,1,0:T(8,128)(2,1)S(1)} collective-permute-done((bf16[2,256,128]{2,1,0:T(8,128)(2,1)S(1)}, bf16[2,256,128]{2,1,0:T(8,128)(2,1)S(1)}, u32[]{:S(2)}, u32[]{:S(2)}) %collective-permute-start.2) | collective-permute-done | bytes 131104 | tf_op jit(solution)/shard_map/ppermute | solution.py:36
  13.0 2.1 %collective-permute-done.3.refs_0_ = bf16[640,128]{1,0:T(8,128)(2,1)S(1)} collective-permute-done((bf16[640,128]{1,0:T(8,128)(2,1)S(1)}, bf16[640,128]{1,0:T(8,128)(2,1)S(1)}, u32[]{:S(2)}, u32[]{:S(2)}) %collective-permute-start.3) | collective-permute-done | bytes 163872 | tf_op jit(solution)/shard_map/ppermute | solution.py:36
  15.1 4.5 %collective-permute-done.5.refs_2_ = bf16[640,128]{1,0:T(8,128)(2,1)S(1)} collective-permute-done((bf16[640,128]{1,0:T(8,128)(2,1)S(1)}, bf16[640,128]{1,0:T(8,128)(2,1)S(1)}, u32[]{:S(2)}, u32[]{:S(2)}) %collective-permute-start.5) | collective-permute-done | bytes 163872 | tf_op jit(solution)/shard_map/ppermute | solution.py:36
  19.6 1.4 %collective-permute-done.4.refs_1_ = bf16[640,128]{1,0:T(8,128)(2,1)S(1)} collective-permute-done((bf16[640,128]{1,0:T(8,128)(2,1)S(1)}, bf16[640,128]{1,0:T(8,128)(2,1)S(1)}, u32[]{:S(2)}, u32[]{:S(2)}) %collective-permute-start.4) | collective-permute-done | bytes 163872 | tf_op jit(solution)/shard_map/ppermute | solution.py:36
  20.9 0.1 fold.1
  21.0 2.6 %collective-permute-start.6 = (bf16[640,128]{1,0:T(8,128)(2,1)S(1)}, bf16[640,128]{1,0:T(8,128)(2,1)S(1)}, u32[]{:S(2)}, u32[]{:S(2)}) collective-permute-start(bf16[640,128]{1,0:T(8,128)(2,1)S(1)} %get-tuple-element.34), channel_id=1, source_target_pairs={{0,8},{1,9},{2,10},{3,11},{4,12},{5,13},{6,14},{7,15},{8,0},{9,1},... | collective-permute-start | bytes 491528 | tf_op jit(solution)/shard_map/ppermute | solution.py:36
  23.7 6.8 %collective-permute-done.6.right = bf16[640,128]{1,0:T(8,128)(2,1)S(1)} collective-permute-done((bf16[640,128]{1,0:T(8,128)(2,1)S(1)}, bf16[640,128]{1,0:T(8,128)(2,1)S(1)}, u32[]{:S(2)}, u32[]{:S(2)}) %collective-permute-start.6) | collective-permute-done | bytes 163872 | tf_op jit(solution)/shard_map/ppermute | solution.py:36
  30.5 0.8 %collective-permute-start.9 = (bf16[640,128]{1,0:T(8,128)(2,1)S(1)}, bf16[640,128]{1,0:T(8,128)(2,1)S(1)}, u32[]{:S(2)}, u32[]{:S(2)}) collective-permute-start(bf16[640,128]{1,0:T(8,128)(2,1)S(1)} %add.1.refs_0_), channel_id=1, source_target_pairs={{0,2},{1,3},{2,0},{3,1},{4,6},{5,7},{6,4},{7,5},{8,10},{9,11},{10,... | collective-permute-start | bytes 491528 | tf_op jit(solution)/shard_map/ppermute | solution.py:36
  31.3 1.4 %collective-permute-start.8 = (bf16[640,128]{1,0:T(8,128)(2,1)S(1)}, bf16[640,128]{1,0:T(8,128)(2,1)S(1)}, u32[]{:S(2)}, u32[]{:S(2)}) collective-permute-start(bf16[640,128]{1,0:T(8,128)(2,1)S(1)} %add.1.refs_0_), channel_id=1, source_target_pairs={{0,6},{1,7},{2,4},{3,5},{4,2},{5,3},{6,0},{7,1},{8,14},{9,15},{10,... | collective-permute-start | bytes 491528 | tf_op jit(solution)/shard_map/ppermute | solution.py:36
  32.7 1.4 %collective-permute-start.7 = (bf16[640,128]{1,0:T(8,128)(2,1)S(1)}, bf16[640,128]{1,0:T(8,128)(2,1)S(1)}, u32[]{:S(2)}, u32[]{:S(2)}) collective-permute-start(bf16[640,128]{1,0:T(8,128)(2,1)S(1)} %add.1.refs_0_), channel_id=1, source_target_pairs={{0,4},{1,5},{2,6},{3,7},{4,0},{5,1},{6,2},{7,3},{8,12},{9,13},{10,... | collective-permute-start | bytes 491528 | tf_op jit(solution)/shard_map/ppermute | solution.py:36
  34.1 0.0 copy-done.2
  34.1 0.0 copy-done.3
  34.1 0.7 %mask.1.allowed = bf16[256,256]{1,0:T(8,128)(2,1)S(1)} custom-call(s32[2,4]{1,0:T(2,128)S(1)} %copy-done.3, s32[2,256]{1,0:T(2,128)S(1)} %copy-done.2, bf16[640,128]{1,0:T(8,128)(2,1)S(1)} %get-tuple-element.28.after), custom_call_target="tpu_custom_call" | custom-call | tf_op jit(solution)/shard_map/mask/pallas_call | solution.py:277
  34.8 4.4 %collective-permute-done.9.refs_3_ = bf16[640,128]{1,0:T(8,128)(2,1)S(1)} collective-permute-done((bf16[640,128]{1,0:T(8,128)(2,1)S(1)}, bf16[640,128]{1,0:T(8,128)(2,1)S(1)}, u32[]{:S(2)}, u32[]{:S(2)}) %collective-permute-start.9) | collective-permute-done | bytes 163872 | tf_op jit(solution)/shard_map/ppermute | solution.py:36
  39.2 0.0 collective-permute-done.8.refs_2_
  39.2 1.2 %collective-permute-done.7.refs_1_ = bf16[640,128]{1,0:T(8,128)(2,1)S(1)} collective-permute-done((bf16[640,128]{1,0:T(8,128)(2,1)S(1)}, bf16[640,128]{1,0:T(8,128)(2,1)S(1)}, u32[]{:S(2)}, u32[]{:S(2)}) %collective-permute-start.7) | collective-permute-done | bytes 163872 | tf_op jit(solution)/shard_map/ppermute | solution.py:36
  40.4 0.3 couple.1.scaled
  40.7 0.1 collective-permute-start.10
  40.8 0.0 copy-done
  40.8 1.3 %begin.1.begun = f32[4,2048,256]{2,1,0:T(8,128)S(1)} custom-call(bf16[2048,512]{1,0:T(8,128)(2,1)S(1)} %copy-done, bf16[8,256,128]{2,1,0:T(8,128)(2,1)S(1)} %couple.1.scaled), custom_call_target="tpu_custom_call" | custom-call | flops 1073741824 | bytes 2097152 | tf_op jit(solution)/shard_map/begin/pallas_call | solution.py:341
  42.1 0.6 %collective-permute-done.10.other = bf16[8,256,128]{2,1,0:T(8,128)(2,1)S(1)} collective-permute-done((bf16[8,256,128]{2,1,0:T(8,128)(2,1)S(1)}, bf16[8,256,128]{2,1,0:T(8,128)(2,1)S(1)}, u32[]{:S(2)}, u32[]{:S(2)}) %collective-permute-start.10) | collective-permute-done | bytes 524320 | tf_op jit(solution)/shard_map/ppermute | solution.py:36
  42.7 3.3 %finish.1 = bf16[2048,1024]{1,0:T(8,128)(2,1)} custom-call(bf16[2048,512]{1,0:T(8,128)(2,1)S(1)} %copy-done, f32[4,2048,256]{2,1,0:T(8,128)S(1)} %begin.1.begun, bf16[8,256,128]{2,1,0:T(8,128)(2,1)S(1)} %collective-permute-done.10.other), custom_call_target="tpu_custom_call" | custom-call | flops 1073741824 | bytes 6291456 | tf_op jit(solution)/shard_map/finish/pallas_call | solution.py:381
  (2 shorter events, 0.1 us)
Async XLA Ops:
  0.0 5.4 %collective-permute-start = (f32[256,256]{1,0:T(8,128)}, f32[256,256]{1,0:T(8,128)S(1)}, u32[]{:S(2)}, u32[]{:S(2)}) collective-permute-start(f32[256,256]{1,0:T(8,128)} %bitcast.1), channel_id=1, source_target_pairs={{0,1},{1,0},{2,3},{3,2},{4,5},{5,4},{6,7},{7,6},{8,9},{9,8},{10,11... | collective-permute-start | bytes 786440 | tf_op jit(solution)/shard_map/ppermute | solution.py:36
  5.4 1.0 %copy-start.4 = (s32[2]{0:T(128)S(1)}, s32[2]{0:T(128)}, u32[]{:S(2)}) copy-start(s32[2]{0:T(128)} %param.10) | copy-start | bytes 28
  5.4 1.0 %copy-start.1 = (f32[1,256,256]{2,1,0:T(8,128)S(1)}, f32[1,256,256]{2,1,0:T(8,128)}, u32[]{:S(2)}) copy-start(f32[1,256,256]{2,1,0:T(8,128)} %param.11) | copy-start | bytes 786436
  5.4 1.8 %collective-permute-start.1 = (bf16[6,256,128]{2,1,0:T(8,128)(2,1)S(1)}, bf16[6,256,128]{2,1,0:T(8,128)(2,1)S(1)}, u32[]{:S(2)}, u32[]{:S(2)}) collective-permute-start(bf16[6,256,128]{2,1,0:T(8,128)(2,1)S(1)} %get-tuple-element.22), channel_id=1, source_target_pairs={{0,1},{1,0},{2,3},{3,2},{4,5},{5,4},{6,7},{7,6},{8,9},{9,8},{10,11... | collective-permute-start | bytes 1179656 | tf_op jit(solution)/shard_map/ppermute | solution.py:36
  5.6 28.5 %copy-start.2 = (s32[2,256]{1,0:T(2,128)S(1)}, s32[2,256]{1,0:T(2,128)}, u32[]{:S(2)}) copy-start(s32[2,256]{1,0:T(2,128)} %atom_of.1) | copy-start | bytes 6148
  5.6 28.5 %copy-start.3 = (s32[2,4]{1,0:T(2,128)S(1)}, s32[2,4]{1,0:T(2,128)}, u32[]{:S(2)}) copy-start(s32[2,4]{1,0:T(2,128)} %counts.1) | copy-start | bytes 100
  6.4 34.4 %copy-start = (bf16[2048,512]{1,0:T(8,128)(2,1)S(1)}, bf16[2048,512]{1,0:T(8,128)(2,1)}, u32[]{:S(2)}) copy-start(bf16[2048,512]{1,0:T(8,128)(2,1)} %projectors.5) | copy-start | bytes 6291460
  7.3 7.8 %collective-permute-start.3 = (bf16[640,128]{1,0:T(8,128)(2,1)S(1)}, bf16[640,128]{1,0:T(8,128)(2,1)S(1)}, u32[]{:S(2)}, u32[]{:S(2)}) collective-permute-start(bf16[640,128]{1,0:T(8,128)(2,1)S(1)} %get-tuple-element.31), channel_id=1, source_target_pairs={{0,4},{1,5},{2,6},{3,7},{4,0},{5,1},{6,2},{7,3},{8,12},{9,13},{10,... | collective-permute-start | bytes 491528 | tf_op jit(solution)/shard_map/ppermute | solution.py:36
  10.1 9.5 %collective-permute-start.5 = (bf16[640,128]{1,0:T(8,128)(2,1)S(1)}, bf16[640,128]{1,0:T(8,128)(2,1)S(1)}, u32[]{:S(2)}, u32[]{:S(2)}) collective-permute-start(bf16[640,128]{1,0:T(8,128)(2,1)S(1)} %get-tuple-element.32), channel_id=1, source_target_pairs={{0,6},{1,7},{2,4},{3,5},{4,2},{5,3},{6,0},{7,1},{8,14},{9,15},{10,... | collective-permute-start | bytes 491528 | tf_op jit(solution)/shard_map/ppermute | solution.py:36
  11.5 9.4 %collective-permute-start.4 = (bf16[640,128]{1,0:T(8,128)(2,1)S(1)}, bf16[640,128]{1,0:T(8,128)(2,1)S(1)}, u32[]{:S(2)}, u32[]{:S(2)}) collective-permute-start(bf16[640,128]{1,0:T(8,128)(2,1)S(1)} %get-tuple-element.28.after), channel_id=1, source_target_pairs={{0,2},{1,3},{2,0},{3,1},{4,6},{5,7},{6,4},{7,5},{8,10},{9,11},{10,... | collective-permute-start | bytes 491528 | tf_op jit(solution)/shard_map/ppermute | solution.py:36
  11.6 1.3 %collective-permute-start.2 = (bf16[2,256,128]{2,1,0:T(8,128)(2,1)S(1)}, bf16[2,256,128]{2,1,0:T(8,128)(2,1)S(1)}, u32[]{:S(2)}, u32[]{:S(2)}) collective-permute-start(bf16[2,256,128]{2,1,0:T(8,128)(2,1)S(1)} %get-tuple-element.30), channel_id=1, source_target_pairs={{0,1},{1,0},{2,3},{3,2},{4,5},{5,4},{6,7},{7,6},{8,9},{9,8},{10,11... | collective-permute-start | bytes 393224 | tf_op jit(solution)/shard_map/ppermute | solution.py:36
  21.0 9.5 %collective-permute-start.6 = (bf16[640,128]{1,0:T(8,128)(2,1)S(1)}, bf16[640,128]{1,0:T(8,128)(2,1)S(1)}, u32[]{:S(2)}, u32[]{:S(2)}) collective-permute-start(bf16[640,128]{1,0:T(8,128)(2,1)S(1)} %get-tuple-element.34), channel_id=1, source_target_pairs={{0,8},{1,9},{2,10},{3,11},{4,12},{5,13},{6,14},{7,15},{8,0},{9,1},... | collective-permute-start | bytes 491528 | tf_op jit(solution)/shard_map/ppermute | solution.py:36
  30.5 8.6 %collective-permute-start.9 = (bf16[640,128]{1,0:T(8,128)(2,1)S(1)}, bf16[640,128]{1,0:T(8,128)(2,1)S(1)}, u32[]{:S(2)}, u32[]{:S(2)}) collective-permute-start(bf16[640,128]{1,0:T(8,128)(2,1)S(1)} %add.1.refs_0_), channel_id=1, source_target_pairs={{0,2},{1,3},{2,0},{3,1},{4,6},{5,7},{6,4},{7,5},{8,10},{9,11},{10,... | collective-permute-start | bytes 491528 | tf_op jit(solution)/shard_map/ppermute | solution.py:36
  31.3 7.9 %collective-permute-start.8 = (bf16[640,128]{1,0:T(8,128)(2,1)S(1)}, bf16[640,128]{1,0:T(8,128)(2,1)S(1)}, u32[]{:S(2)}, u32[]{:S(2)}) collective-permute-start(bf16[640,128]{1,0:T(8,128)(2,1)S(1)} %add.1.refs_0_), channel_id=1, source_target_pairs={{0,6},{1,7},{2,4},{3,5},{4,2},{5,3},{6,0},{7,1},{8,14},{9,15},{10,... | collective-permute-start | bytes 491528 | tf_op jit(solution)/shard_map/ppermute | solution.py:36
  32.7 7.7 %collective-permute-start.7 = (bf16[640,128]{1,0:T(8,128)(2,1)S(1)}, bf16[640,128]{1,0:T(8,128)(2,1)S(1)}, u32[]{:S(2)}, u32[]{:S(2)}) collective-permute-start(bf16[640,128]{1,0:T(8,128)(2,1)S(1)} %add.1.refs_0_), channel_id=1, source_target_pairs={{0,4},{1,5},{2,6},{3,7},{4,0},{5,1},{6,2},{7,3},{8,12},{9,13},{10,... | collective-permute-start | bytes 491528 | tf_op jit(solution)/shard_map/ppermute | solution.py:36
  40.7 2.0 %collective-permute-start.10 = (bf16[8,256,128]{2,1,0:T(8,128)(2,1)S(1)}, bf16[8,256,128]{2,1,0:T(8,128)(2,1)S(1)}, u32[]{:S(2)}, u32[]{:S(2)}) collective-permute-start(bf16[8,256,128]{2,1,0:T(8,128)(2,1)S(1)} %couple.1.scaled), channel_id=1, source_target_pairs={{0,1},{1,0},{2,3},{3,2},{4,5},{5,4},{6,7},{7,6},{8,9},{9,8},{10,11... | collective-permute-start | bytes 1572872 | tf_op jit(solution)/shard_map/ppermute | solution.py:36

commit v14 on v13

--- a/solution.py
+++ b/solution.py
@@ -14,7 +14,7 @@
 ROW_BLOCK = 512
 ROW_BLOCKS = (512, 512, 512, 256, 256)
 COPY_ROWS = 128
-GATHERED = (0, 2, 3, 1)
+GATHERED = (0, 1, 2, 3)
 PARAMS = pltpu.CompilerParams(vmem_limit_bytes=40 * 1024 * 1024)
 VMEM = pl.BlockSpec(memory_space=pltpu.VMEM)
 SMEM = pl.BlockSpec(memory_space=pltpu.SMEM)
@@ -40,8 +40,18 @@
     return swap(x, 1)
 
 
-def swap_square(x, part):
-    return swap(x, 2 * part)
+def swap_chips(x, distance):
+    return swap(x, 2 * distance)
+
+
+def swap_first(x):
+    count = lax.axis_size("pw")
+    return lax.ppermute(x, "pw", [(i, i ^ (2, 4)[i % 2]) for i in range(count)])
+
+
+def swap_second(x):
+    count = lax.axis_size("pw")
+    return lax.ppermute(x, "pw", [(i, i ^ (4, 2)[i % 2]) for i in range(count)])
 
 
 def pair_at(columns, rows, part):
@@ -57,99 +67,61 @@
         theirs[2 * at + entry] = sums[PCAP:, lanes].astype(theirs.dtype)
 
 
-def project_sent_kernel(projectors, bands, theirs, ours, flipped, columns, slots, totals, slot_sems, column_sems):
+def load_kernel(projectors, flipped, slots, sems):
     core = place()[0]
-    count = slot_sems.shape[0]
-    depth = slots.shape[0] // count
+    count = sems.shape[0]
+    block = slots.shape[0] // count
     copies = []
     for at in range(count):
-        rows = slice(at * depth, (at + 1) * depth)
-        copies.append(
-            (
-                pltpu.make_async_copy(projectors.at[rows], slots.at[rows], slot_sems.at[at]),
-                pltpu.make_async_copy(bands.at[rows], columns.at[rows], column_sems.at[at]),
-            )
-        )
-    for pair in copies[:2]:
-        for copy in pair:
-            copy.start()
-    for at in range(count):
-        rows = slice(at * depth, (at + 1) * depth)
-        copies[at][0].wait()
-        if at + 2 < count:
-            copies[at + 2][0].start()
+        rows = slice(at * block, (at + 1) * block)
+        copies.append(pltpu.make_async_copy(projectors.at[rows], slots.at[rows], sems.at[at]))
+        copies[-1].start()
+    for at, copy in enumerate(copies):
+        copy.wait()
+        rows = slice(at * block, (at + 1) * block)
         for side, group in enumerate((core, 1 - core)):
             start = pl.multiple_of(group * PCAP, PCAP)
             flipped[side * PCAP : (side + 1) * PCAP, rows] = slots[rows, pl.ds(start, PCAP)].T
-        copies[at][1].wait()
-        if at + 2 < count:
-            copies[at + 2][1].start()
-        for part in range(1, SQUARE):
-            sums = jnp.dot(
-                flipped[:, rows], pair_at(columns, rows, part), preferred_element_type=jnp.float32
-            )
-            if at:
-                sums = totals[part - 1] + sums
-            if at < count - 1:
-                totals[part - 1] = sums
-            else:
-                keep_sums(ours, theirs, part - 1, sums)
-
-
-def sums_shape(parts):
-    shape = (2 * parts, PCAP, LANES)
-    return [jax.ShapeDtypeStruct(shape, jnp.bfloat16), jax.ShapeDtypeStruct(shape, jnp.float32)]
-
-
-def project_sent(projectors, band_coeffs):
+
+
+def load(projectors):
     depth, slots = projectors.shape
-    bands = band_coeffs.shape[1]
-    blocks = 4
-    return pl.pallas_call(
-        project_sent_kernel,
-        in_specs=[HBM, HBM],
-        out_specs=[VMEM] * 4,
-        out_shape=sums_shape(SQUARE - 1)
-        + [
-            jax.ShapeDtypeStruct((slots, depth), jnp.bfloat16),
-            jax.ShapeDtypeStruct((depth, bands), jnp.bfloat16),
-        ],
-        scratch_shapes=[
-            pltpu.VMEM((depth, slots), jnp.bfloat16),
-            pltpu.VMEM((SQUARE - 1, slots, 2 * LANES), jnp.float32),
-            pltpu.SemaphoreType.DMA((blocks,)),
-            pltpu.SemaphoreType.DMA((blocks,)),
-        ],
-        compiler_params=PARAMS,
-        cost_estimate=pl.CostEstimate(
-            flops=2 * depth * slots * bands, bytes_accessed=2 * depth * (bands + slots), transcendentals=0
-        ),
-        name="project_sent",
-    )(
-        pltpu.with_memory_space_constraint(projectors, pltpu.HBM),
-        pltpu.with_memory_space_constraint(band_coeffs, pltpu.HBM),
-    )
-
-
-def project_kept_kernel(flipped, columns, theirs, ours):
+    return pl.pallas_call(
+        load_kernel,
+        in_specs=[HBM],
+        out_specs=VMEM,
+        out_shape=jax.ShapeDtypeStruct((slots, depth), jnp.bfloat16),
+        scratch_shapes=[pltpu.VMEM((depth, slots), jnp.bfloat16), pltpu.SemaphoreType.DMA((4,))],
+        compiler_params=PARAMS,
+        name="load",
+    )(pltpu.with_memory_space_constraint(projectors, pltpu.HBM))
+
+
+def project_kernel(parts, flipped, columns, theirs, ours):
     rows = slice(0, columns.shape[0])
-    sums = jnp.dot(flipped[...], pair_at(columns, rows, 0), preferred_element_type=jnp.float32)
-    keep_sums(ours, theirs, 0, sums)
-
-
-def project_kept(flipped, columns):
+    for at, part in enumerate(parts):
+        sums = jnp.dot(flipped[...], pair_at(columns, rows, part), preferred_element_type=jnp.float32)
+        keep_sums(ours, theirs, at, sums)
+
+
+def project(flipped, band_coeffs, parts):
     slots, depth = flipped.shape
-    return pl.pallas_call(
-        project_kept_kernel,
+    shape = (2 * len(parts), PCAP, LANES)
+
+    def kernel(*refs):
+        project_kernel(parts, *refs)
+
+    return pl.pallas_call(
+        kernel,
         in_specs=[VMEM, VMEM],
         out_specs=[VMEM, VMEM],
-        out_shape=sums_shape(1),
+        out_shape=[jax.ShapeDtypeStruct(shape, jnp.bfloat16), jax.ShapeDtypeStruct(shape, jnp.float32)],
         compiler_params=PARAMS,
         cost_estimate=pl.CostEstimate(
-            flops=4 * depth * slots * LANES, bytes_accessed=2 * depth * slots, transcendentals=0
+            flops=4 * depth * slots * len(parts) * LANES, bytes_accessed=2 * depth * slots, transcendentals=0
         ),
-        name="project_kept",
-    )(flipped, columns)
+        name="project",
+    )(flipped, pltpu.with_memory_space_constraint(band_coeffs, pltpu.VMEM))
 
 
 def project_plain(projectors, band_coeffs, parts):
@@ -192,28 +164,53 @@
     )(jnp.broadcast_to(owners[:, None], (owners.shape[0], PCAP)), own, sibling, after)
 
 
-def pack_kernel(ours, theirs, quarters, *messages):
-    entries = ours.shape[0] // len(messages)
-    for at, message in enumerate(messages):
-        for entry in range(entries):
-            place = at * entries + entry
-            total = ours[place] + theirs[place].astype(jnp.float32)
-            message[entry * PCAP : (entry + 1) * PCAP] = total.astype(message.dtype)
-        message[entries * PCAP :] = quarters[at + 1]
-
-
-def pack(ours, theirs, quarters):
-    entries, _, width = ours.shape
-    entries //= SQUARE - 1
-    shape = jax.ShapeDtypeStruct((entries * PCAP + quarters.shape[1], width), jnp.bfloat16)
-    return pl.pallas_call(
-        pack_kernel,
+def send_kernel(first, second, ours, theirs, quarters, message):
+    entries = ours.shape[0] // (1 if first == second else 2)
+    core = place()[0]
+    start, part = (0, first) if first == second else (core * entries, 1 + core)
+    for entry in range(entries):
+        total = ours[start + entry] + theirs[start + entry].astype(jnp.float32)
+        message[entry * PCAP : (entry + 1) * PCAP] = total.astype(message.dtype)
+    message[entries * PCAP :] = quarters[part]
+
+
+def send(ours, theirs, quarters, parts):
+    count, _, width = ours.shape
+    rows = count // len(parts) * PCAP + quarters.shape[1]
+
+    def kernel(*refs):
+        send_kernel(parts[0], parts[-1], *refs)
+
+    return pl.pallas_call(
+        kernel,
         in_specs=[VMEM] * 3,
-        out_specs=[VMEM] * (SQUARE - 1),
-        out_shape=[shape] * (SQUARE - 1),
-        compiler_params=PARAMS,
-        name="pack",
+        out_specs=VMEM,
+        out_shape=jax.ShapeDtypeStruct((rows, width), jnp.bfloat16),
+        compiler_params=PARAMS,
+        name="send",
     )(ours, theirs, quarters)
+
+
+def forward_kernel(ours, theirs, quarters, got, message):
+    core = place()[0]
+    entries = ours.shape[0] // 2
+    start = (1 - core) * entries
+    for entry in range(entries):
+        rows = slice(entry * PCAP, (entry + 1) * PCAP)
+        total = ours[start + entry] + theirs[start + entry].astype(jnp.float32)
+        message[rows] = (total + got[rows].astype(jnp.float32)).astype(message.dtype)
+    message[entries * PCAP :] = quarters[2 - core] + got[entries * PCAP :]
+
+
+def forward(ours, theirs, quarters, got):
+    return pl.pallas_call(
+        forward_kernel,
+        in_specs=[VMEM] * 4,
+        out_specs=VMEM,
+        out_shape=jax.ShapeDtypeStruct(got.shape, got.dtype),
+        compiler_params=PARAMS,
+        name="forward",
+    )(ours, theirs, quarters, got)
 
 
 def fold_kernel(ours, theirs, quarters, *refs):
@@ -413,32 +410,41 @@
     fast = width == LANES and entries == 2
     own_table = couplings[0]
     sibling_table = swap_cores(own_table)
-    sent, kept = tuple(range(1, SQUARE)), (0,)
     if fast:
-        theirs, ours, flipped, columns = project_sent(projectors, band_coeffs)
-        theirs, sibling_table = lax.optimization_barrier((theirs, sibling_table))
-        low_theirs, low_ours = project_kept(flipped, columns)
+        flipped = load(projectors)
+
+        def partial(parts):
+            return project(flipped, band_coeffs, parts)
     else:
-        theirs, ours = project_plain(projectors, band_coeffs, sent)
-        low_theirs, low_ours = project_plain(projectors, band_coeffs, kept)
+
+        def partial(parts):
+            return project_plain(projectors, band_coeffs, parts)
+
+    theirs, ours = partial((3,))
+    theirs, sibling_table = lax.optimization_barrier((theirs, sibling_table))
+    theirs = swap_cores(theirs)
+    pair_theirs, pair_ours = partial((1, 2))
     quarters = choose(owners, own_table, sibling_table, width, ours)
-    theirs, low_ours = lax.optimization_barrier((swap_cores(theirs), low_ours))
-    messages = pack(ours, theirs, quarters)
+    got = swap_first(send(ours, theirs, quarters, (3,)))
+    pair_theirs = swap_cores(pair_theirs)
+    low_theirs, low_ours = partial((0,))
     low_theirs = swap_cores(low_theirs)
-    gots = [swap_square(messages[part - 1], part) for part in (2, 1, 3)]
-    allowed = mask(counts, atom_of, messages[0])
-
-    total, message = fold(low_ours, low_theirs, quarters, gots)
-    mine = add(total, swap_square(message, SQUARE))
+    got_first = swap_first(send(pair_ours, pair_theirs, quarters, (1, 2)))
+    message = forward(pair_ours, pair_theirs, quarters, got)
+    got_second = swap_second(message)
+    allowed = mask(counts, atom_of, message)
+
+    total, message = fold(low_ours, low_theirs, quarters, [got_first, got_second])
+    mine = add(total, swap_chips(message, SQUARE))
     distance = 2 * SQUARE
     while distance < chips:
         body = mine[: entries * PCAP].reshape(entries, PCAP, width)
         order = [entry ^ (distance // SQUARE) for entry in range(entries)]
         message = jnp.concatenate([body[jnp.array(order)].reshape(-1, width), mine[entries * PCAP :]])
-        mine = add(mine.astype(jnp.float32), swap_square(message, distance))
+        mine = add(mine.astype(jnp.float32), swap_chips(message, distance))
         distance *= 2
 
-    scaled = couple(allowed, [swap_square(mine, part) if part else mine for part in GATHERED])
+    scaled = couple(allowed, [swap_chips(mine, part) if part else mine for part in GATHERED])
     other = swap_cores(scaled)
     if not fast:
         return apply_plain(projectors, scaled, other)

time: 46.1 us -> 43.3 us (0.939)
  waiting for transfers between devices: 23.1 us -> 17.7 us
  starting transfers between devices: 11.1 us -> 14 us
  Pallas kernels: 11.5 us -> 10.8 us
    ppermute x11 -> x9, waiting for transfers between devices: 23.1 us -> 14.4 us  [swap(): return lax.ppermute(x, 'pw', [(i, i ^ distance) for i in range(count)])]
    ppermute x0 -> x3, starting transfers between devices: none -> 6.16 us  [the longest x2 4.03 us: swap_first(): return lax.ppermute(x, 'pw', [(i, i ^ (2, 4)[i % 2]) for i in range(count)])]
    ppermute x0 -> x3, waiting for transfers between devices: none -> 3.36 us  [the longest x2 2.27 us: swap_first(): return lax.ppermute(x, 'pw', [(i, i ^ (2, 4)[i % 2]) for i in range(count)])]
    ppermute x11 -> x9, starting transfers between devices: 11.1 us -> 7.89 us  [swap(): return lax.ppermute(x, 'pw', [(i, i ^ distance) for i in range(count)])]
    pallas_call x3 -> x7, Pallas kernels: 5.81 us -> 5.11 us  [the longest x3 2.91 us: project(): pl.pallas_call(kernel, in_specs=[VMEM, VMEM], out_specs=[VMEM, VMEM], out...]
  transfers between devices with their start and end apart: 11 -> 12, of which waited for: 9 -> 7; matrix products, arithmetic and copies ran while one was open for 0% -> 0% of each run, Pallas kernels for 17% -> 16%
where the time goes in v14:
time: 43.3 us; the launch traced here: 43.1 us
  waiting for transfers between devices  17.7 us (41%)
  starting transfers between devices  14 us (32%)
  Pallas kernels  10.8 us (25%)
    ppermute x9, waiting for transfers between devices, swap(): return lax.ppermute(x, 'pw', [(i, i ^ distance) for i in range(count)])  14.4 us
    ppermute x9, starting transfers between devices, swap(): return lax.ppermute(x, 'pw', [(i, i ^ distance) for i in range(count)])  7.89 us
    ppermute x2, starting transfers between devices, swap_first(): return lax.ppermute(x, 'pw', [(i, i ^ (2, 4)[i % 2]) for i in range(count)])  4.03 us
    pallas_call x1, Pallas kernels, finish(): pl.pallas_call(finish_kernel, in_specs=[VMEM] * 3, out_specs=HBM, out_sha...  3.3 us
    pallas_call x3, Pallas kernels, project(): pl.pallas_call(kernel, in_specs=[VMEM, VMEM], out_specs=[VMEM, VMEM], out...  2.91 us
    ppermute x2, waiting for transfers between devices, swap_first(): return lax.ppermute(x, 'pw', [(i, i ^ (2, 4)[i % 2]) for i in range(count)])  2.27 us
    ppermute x1, starting transfers between devices, swap_second(): return lax.ppermute(x, 'pw', [(i, i ^ (4, 2)[i % 2]) for i in range(count)])  2.13 us
    pallas_call x1, Pallas kernels, load(): pl.pallas_call(load_kernel, in_specs=[HBM], out_specs=VMEM, out_shape=jax...  2.1 us
  transfers between devices with their start and end apart: 12, of which 7 were waited for; matrix products, arithmetic and copies ran while one was open for 0% of the time, Pallas kernels for 16%

profile of v14, /device:TPU:0, one launch (start us, length us, event | category | flops | bytes accessed | tf_op | source)
XLA Modules:
  0.0 43.1 jit_solution(647056237332996715)
XLA Ops:
  0.0 0.0 copy-start
  0.0 0.5 %collective-permute-start.1 = (f32[256,256]{1,0:T(8,128)}, f32[256,256]{1,0:T(8,128)S(1)}, u32[]{:S(2)}, u32[]{:S(2)}) collective-permute-start(f32[256,256]{1,0:T(8,128)} %bitcast.1), channel_id=1, source_target_pairs={{0,1},{1,0},{2,3},{3,2},{4,5},{5,4},{6,7},{7,6},{8,9},{9,8},{10,11... | collective-permute-start | bytes 786440 | tf_op jit(solution)/shard_map/ppermute | solution.py:36
  0.5 2.1 %load.1.refs_0_ = bf16[512,2048]{1,0:T(8,128)(2,1)S(1)} custom-call(bf16[2048,512]{1,0:T(8,128)(2,1)} %projectors.5), custom_call_target="tpu_custom_call" | custom-call | tf_op jit(solution)/shard_map/load/pallas_call | solution.py:89
  2.6 0.3 copy-done
  2.8 0.8 %project.4 = (bf16[2,256,128]{2,1,0:T(8,128)(2,1)S(1)}, f32[2,256,128]{2,1,0:T(8,128)S(1)}) custom-call(bf16[512,2048]{1,0:T(8,128)(2,1)S(1)} %load.1.refs_0_, bf16[2048,1024]{1,0:T(8,128)(2,1)S(1)} %copy-done), custom_call_target="tpu_custom_call" | custom-call | flops 536870912 | bytes 2097152 | tf_op jit(solution)/shard_map/project/pallas_call | solution.py:114
  3.6 0.0 copy-start.5
  3.6 0.0 copy-start.2
  3.6 0.0 collective-permute-done.1.sibling
  3.6 0.5 %collective-permute-start.2 = (bf16[2,256,128]{2,1,0:T(8,128)(2,1)S(1)}, bf16[2,256,128]{2,1,0:T(8,128)(2,1)S(1)}, u32[]{:S(2)}, u32[]{:S(2)}) collective-permute-start(bf16[2,256,128]{2,1,0:T(8,128)(2,1)S(1)} %get-tuple-element.20), channel_id=1, source_target_pairs={{0,1},{1,0},{2,3},{3,2},{4,5},{5,4},{6,7},{7,6},{8,9},{9,8},{10,11... | collective-permute-start | bytes 393224 | tf_op jit(solution)/shard_map/ppermute | solution.py:36
  4.2 1.3 %project.3 = (bf16[4,256,128]{2,1,0:T(8,128)(2,1)S(1)}, f32[4,256,128]{2,1,0:T(8,128)S(1)}) custom-call(bf16[512,2048]{1,0:T(8,128)(2,1)S(1)} %load.1.refs_0_, bf16[2048,1024]{1,0:T(8,128)(2,1)S(1)} %copy-done), custom_call_target="tpu_custom_call" | custom-call | flops 1073741824 | bytes 2097152 | tf_op jit(solution)/shard_map/project/pallas_call | solution.py:114
  5.5 0.1 collective-permute-start
  5.6 0.0 copy-done.5
  5.6 0.1 broadcast_in_dim.2.owners
  5.7 0.0 copy-done.2
  5.7 0.0 collective-permute-done.2.refs_1_
  5.8 3.0 %collective-permute-start.3 = (bf16[640,128]{1,0:T(8,128)(2,1)S(1)}, bf16[640,128]{1,0:T(8,128)(2,1)S(1)}, u32[]{:S(2)}, u32[]{:S(2)}) collective-permute-start(bf16[640,128]{1,0:T(8,128)(2,1)S(1)} %send.2), channel_id=1, source_target_pairs={{0,2},{1,5},{2,0},{3,7},{4,6},{5,1},{6,4},{7,3},{8,10},{9,13},{10,... | collective-permute-start | bytes 491528 | tf_op jit(solution)/shard_map/ppermute | solution.py:49
  8.8 0.0 collective-permute-done.theirs.refs_1_
  8.9 1.0 %collective-permute-start.5 = (bf16[640,128]{1,0:T(8,128)(2,1)S(1)}, bf16[640,128]{1,0:T(8,128)(2,1)S(1)}, u32[]{:S(2)}, u32[]{:S(2)}) collective-permute-start(bf16[640,128]{1,0:T(8,128)(2,1)S(1)} %send.3), channel_id=1, source_target_pairs={{0,2},{1,5},{2,0},{3,7},{4,6},{5,1},{6,4},{7,3},{8,10},{9,13},{10,... | collective-permute-start | bytes 491528 | tf_op jit(solution)/shard_map/ppermute | solution.py:49
  9.9 2.3 %collective-permute-done.3.got = bf16[640,128]{1,0:T(8,128)(2,1)S(1)} collective-permute-done((bf16[640,128]{1,0:T(8,128)(2,1)S(1)}, bf16[640,128]{1,0:T(8,128)(2,1)S(1)}, u32[]{:S(2)}, u32[]{:S(2)}) %collective-permute-start.3) | collective-permute-done | bytes 163872 | tf_op jit(solution)/shard_map/ppermute | solution.py:49
  12.1 0.1 forward.1.after
  12.2 0.0 copy-start.3
  12.2 0.0 copy-start.4
  12.2 0.0 copy-start.1
  12.2 2.1 %collective-permute-start.6 = (bf16[640,128]{1,0:T(8,128)(2,1)S(1)}, bf16[640,128]{1,0:T(8,128)(2,1)S(1)}, u32[]{:S(2)}, u32[]{:S(2)}) collective-permute-start(bf16[640,128]{1,0:T(8,128)(2,1)S(1)} %forward.1.after), channel_id=1, source_target_pairs={{0,4},{1,3},{2,6},{3,1},{4,0},{5,7},{6,2},{7,5},{8,12},{9,11},{10,... | collective-permute-start | bytes 491528 | tf_op jit(solution)/shard_map/ppermute | solution.py:54
  14.3 0.8 %project.5 = (bf16[2,256,128]{2,1,0:T(8,128)(2,1)S(1)}, f32[2,256,128]{2,1,0:T(8,128)S(1)}) custom-call(bf16[512,2048]{1,0:T(8,128)(2,1)S(1)} %load.1.refs_0_, bf16[2048,1024]{1,0:T(8,128)(2,1)S(1)} %copy-done), custom_call_target="tpu_custom_call" | custom-call | flops 536870912 | bytes 2097152 | tf_op jit(solution)/shard_map/project/pallas_call | solution.py:114
  15.1 0.1 collective-permute-start.4
  15.2 1.3 %collective-permute-done.4.theirs = bf16[2,256,128]{2,1,0:T(8,128)(2,1)S(1)} collective-permute-done((bf16[2,256,128]{2,1,0:T(8,128)(2,1)S(1)}, bf16[2,256,128]{2,1,0:T(8,128)(2,1)S(1)}, u32[]{:S(2)}, u32[]{:S(2)}) %collective-permute-start.4) | collective-permute-done | bytes 131104 | tf_op jit(solution)/shard_map/ppermute | solution.py:36
  16.6 0.0 collective-permute-done.5.refs_0_
  16.6 1.1 %collective-permute-done.6.refs_1_ = bf16[640,128]{1,0:T(8,128)(2,1)S(1)} collective-permute-done((bf16[640,128]{1,0:T(8,128)(2,1)S(1)}, bf16[640,128]{1,0:T(8,128)(2,1)S(1)}, u32[]{:S(2)}, u32[]{:S(2)}) %collective-permute-start.6) | collective-permute-done | bytes 163872 | tf_op jit(solution)/shard_map/ppermute | solution.py:54
  17.6 0.1 fold.1
  17.7 3.1 %collective-permute-start.7 = (bf16[640,128]{1,0:T(8,128)(2,1)S(1)}, bf16[640,128]{1,0:T(8,128)(2,1)S(1)}, u32[]{:S(2)}, u32[]{:S(2)}) collective-permute-start(bf16[640,128]{1,0:T(8,128)(2,1)S(1)} %get-tuple-element.24), channel_id=1, source_target_pairs={{0,8},{1,9},{2,10},{3,11},{4,12},{5,13},{6,14},{7,15},{8,0},{9,1},... | collective-permute-start | bytes 491528 | tf_op jit(solution)/shard_map/ppermute | solution.py:36
  20.8 6.5 %collective-permute-done.7.right = bf16[640,128]{1,0:T(8,128)(2,1)S(1)} collective-permute-done((bf16[640,128]{1,0:T(8,128)(2,1)S(1)}, bf16[640,128]{1,0:T(8,128)(2,1)S(1)}, u32[]{:S(2)}, u32[]{:S(2)}) %collective-permute-start.7) | collective-permute-done | bytes 163872 | tf_op jit(solution)/shard_map/ppermute | solution.py:36
  27.4 1.2 %collective-permute-start.10 = (bf16[640,128]{1,0:T(8,128)(2,1)S(1)}, bf16[640,128]{1,0:T(8,128)(2,1)S(1)}, u32[]{:S(2)}, u32[]{:S(2)}) collective-permute-start(bf16[640,128]{1,0:T(8,128)(2,1)S(1)} %add.1.refs_0_), channel_id=1, source_target_pairs={{0,6},{1,7},{2,4},{3,5},{4,2},{5,3},{6,0},{7,1},{8,14},{9,15},{10,... | collective-permute-start | bytes 491528 | tf_op jit(solution)/shard_map/ppermute | solution.py:36
  28.6 1.8 %collective-permute-start.9 = (bf16[640,128]{1,0:T(8,128)(2,1)S(1)}, bf16[640,128]{1,0:T(8,128)(2,1)S(1)}, u32[]{:S(2)}, u32[]{:S(2)}) collective-permute-start(bf16[640,128]{1,0:T(8,128)(2,1)S(1)} %add.1.refs_0_), channel_id=1, source_target_pairs={{0,4},{1,5},{2,6},{3,7},{4,0},{5,1},{6,2},{7,3},{8,12},{9,13},{10,... | collective-permute-start | bytes 491528 | tf_op jit(solution)/shard_map/ppermute | solution.py:36
  30.5 0.5 %collective-permute-start.8 = (bf16[640,128]{1,0:T(8,128)(2,1)S(1)}, bf16[640,128]{1,0:T(8,128)(2,1)S(1)}, u32[]{:S(2)}, u32[]{:S(2)}) collective-permute-start(bf16[640,128]{1,0:T(8,128)(2,1)S(1)} %add.1.refs_0_), channel_id=1, source_target_pairs={{0,2},{1,3},{2,0},{3,1},{4,6},{5,7},{6,4},{7,5},{8,10},{9,11},{10,... | collective-permute-start | bytes 491528 | tf_op jit(solution)/shard_map/ppermute | solution.py:36
  31.0 0.0 copy-done.3
  31.0 0.0 copy-done.4
  31.0 0.7 %mask.1.allowed = bf16[256,256]{1,0:T(8,128)(2,1)S(1)} custom-call(s32[2,4]{1,0:T(2,128)S(1)} %copy-done.4, s32[2,256]{1,0:T(2,128)S(1)} %copy-done.3, bf16[640,128]{1,0:T(8,128)(2,1)S(1)} %forward.1.after), custom_call_target="tpu_custom_call" | custom-call | tf_op jit(solution)/shard_map/mask/pallas_call | solution.py:274
  31.6 3.9 %collective-permute-done.10.refs_3_ = bf16[640,128]{1,0:T(8,128)(2,1)S(1)} collective-permute-done((bf16[640,128]{1,0:T(8,128)(2,1)S(1)}, bf16[640,128]{1,0:T(8,128)(2,1)S(1)}, u32[]{:S(2)}, u32[]{:S(2)}) %collective-permute-start.10) | collective-permute-done | bytes 163872 | tf_op jit(solution)/shard_map/ppermute | solution.py:36
  35.5 2.0 %collective-permute-done.9.refs_2_ = bf16[640,128]{1,0:T(8,128)(2,1)S(1)} collective-permute-done((bf16[640,128]{1,0:T(8,128)(2,1)S(1)}, bf16[640,128]{1,0:T(8,128)(2,1)S(1)}, u32[]{:S(2)}, u32[]{:S(2)}) %collective-permute-start.9) | collective-permute-done | bytes 163872 | tf_op jit(solution)/shard_map/ppermute | solution.py:36
  37.5 0.0 collective-permute-done.8.refs_1_
  37.5 0.3 couple.1.scaled
  37.8 0.1 collective-permute-start.11
  37.9 0.0 copy-done.1
  37.9 1.3 %begin.1.begun = f32[4,2048,256]{2,1,0:T(8,128)S(1)} custom-call(bf16[2048,512]{1,0:T(8,128)(2,1)S(1)} %copy-done.1, bf16[8,256,128]{2,1,0:T(8,128)(2,1)S(1)} %couple.1.scaled), custom_call_target="tpu_custom_call" | custom-call | flops 1073741824 | bytes 2097152 | tf_op jit(solution)/shard_map/begin/pallas_call | solution.py:338
  39.2 0.6 %collective-permute-done.11.other = bf16[8,256,128]{2,1,0:T(8,128)(2,1)S(1)} collective-permute-done((bf16[8,256,128]{2,1,0:T(8,128)(2,1)S(1)}, bf16[8,256,128]{2,1,0:T(8,128)(2,1)S(1)}, u32[]{:S(2)}, u32[]{:S(2)}) %collective-permute-start.11) | collective-permute-done | bytes 524320 | tf_op jit(solution)/shard_map/ppermute | solution.py:36
  39.8 3.3 %finish.1 = bf16[2048,1024]{1,0:T(8,128)(2,1)} custom-call(bf16[2048,512]{1,0:T(8,128)(2,1)S(1)} %copy-done.1, f32[4,2048,256]{2,1,0:T(8,128)S(1)} %begin.1.begun, bf16[8,256,128]{2,1,0:T(8,128)(2,1)S(1)} %collective-permute-done.11.other), custom_call_target="tpu_custom_call" | custom-call | flops 1073741824 | bytes 6291456 | tf_op jit(solution)/shard_map/finish/pallas_call | solution.py:378
  (4 shorter events, 0.1 us)
Async XLA Ops:
  0.0 2.8 %copy-start = (bf16[2048,1024]{1,0:T(8,128)(2,1)S(1)}, bf16[2048,1024]{1,0:T(8,128)(2,1)}, u32[]{:S(2)}) copy-start(bf16[2048,1024]{1,0:T(8,128)(2,1)} %refs_1_.5) | copy-start | bytes 12582916
  0.0 3.6 %collective-permute-start.1 = (f32[256,256]{1,0:T(8,128)}, f32[256,256]{1,0:T(8,128)S(1)}, u32[]{:S(2)}, u32[]{:S(2)}) collective-permute-start(f32[256,256]{1,0:T(8,128)} %bitcast.1), channel_id=1, source_target_pairs={{0,1},{1,0},{2,3},{3,2},{4,5},{5,4},{6,7},{7,6},{8,9},{9,8},{10,11... | collective-permute-start | bytes 786440 | tf_op jit(solution)/shard_map/ppermute | solution.py:36
  3.6 2.0 %copy-start.5 = (s32[2]{0:T(128)S(1)}, s32[2]{0:T(128)}, u32[]{:S(2)}) copy-start(s32[2]{0:T(128)} %param.10) | copy-start | bytes 28
  3.6 2.1 %copy-start.2 = (f32[1,256,256]{2,1,0:T(8,128)S(1)}, f32[1,256,256]{2,1,0:T(8,128)}, u32[]{:S(2)}) copy-start(f32[1,256,256]{2,1,0:T(8,128)} %param.11) | copy-start | bytes 786436
  3.6 2.1 %collective-permute-start.2 = (bf16[2,256,128]{2,1,0:T(8,128)(2,1)S(1)}, bf16[2,256,128]{2,1,0:T(8,128)(2,1)S(1)}, u32[]{:S(2)}, u32[]{:S(2)}) collective-permute-start(bf16[2,256,128]{2,1,0:T(8,128)(2,1)S(1)} %get-tuple-element.20), channel_id=1, source_target_pairs={{0,1},{1,0},{2,3},{3,2},{4,5},{5,4},{6,7},{7,6},{8,9},{9,8},{10,11... | collective-permute-start | bytes 393224 | tf_op jit(solution)/shard_map/ppermute | solution.py:36
  5.5 3.3 %collective-permute-start = (bf16[4,256,128]{2,1,0:T(8,128)(2,1)S(1)}, bf16[4,256,128]{2,1,0:T(8,128)(2,1)S(1)}, u32[]{:S(2)}, u32[]{:S(2)}) collective-permute-start(bf16[4,256,128]{2,1,0:T(8,128)(2,1)S(1)} %get-tuple-element.16), channel_id=1, source_target_pairs={{0,1},{1,0},{2,3},{3,2},{4,5},{5,4},{6,7},{7,6},{8,9},{9,8},{10,11... | collective-permute-start | bytes 786440 | tf_op jit(solution)/shard_map/ppermute | solution.py:36
  5.8 6.3 %collective-permute-start.3 = (bf16[640,128]{1,0:T(8,128)(2,1)S(1)}, bf16[640,128]{1,0:T(8,128)(2,1)S(1)}, u32[]{:S(2)}, u32[]{:S(2)}) collective-permute-start(bf16[640,128]{1,0:T(8,128)(2,1)S(1)} %send.2), channel_id=1, source_target_pairs={{0,2},{1,5},{2,0},{3,7},{4,6},{5,1},{6,4},{7,3},{8,10},{9,13},{10,... | collective-permute-start | bytes 491528 | tf_op jit(solution)/shard_map/ppermute | solution.py:49
  8.9 7.7 %collective-permute-start.5 = (bf16[640,128]{1,0:T(8,128)(2,1)S(1)}, bf16[640,128]{1,0:T(8,128)(2,1)S(1)}, u32[]{:S(2)}, u32[]{:S(2)}) collective-permute-start(bf16[640,128]{1,0:T(8,128)(2,1)S(1)} %send.3), channel_id=1, source_target_pairs={{0,2},{1,5},{2,0},{3,7},{4,6},{5,1},{6,4},{7,3},{8,10},{9,13},{10,... | collective-permute-start | bytes 491528 | tf_op jit(solution)/shard_map/ppermute | solution.py:49
  12.2 18.8 %copy-start.3 = (s32[2,256]{1,0:T(2,128)S(1)}, s32[2,256]{1,0:T(2,128)}, u32[]{:S(2)}) copy-start(s32[2,256]{1,0:T(2,128)} %atom_of.1) | copy-start | bytes 6148
  12.2 18.8 %copy-start.4 = (s32[2,4]{1,0:T(2,128)S(1)}, s32[2,4]{1,0:T(2,128)}, u32[]{:S(2)}) copy-start(s32[2,4]{1,0:T(2,128)} %counts.1) | copy-start | bytes 100
  12.2 25.7 %copy-start.1 = (bf16[2048,512]{1,0:T(8,128)(2,1)S(1)}, bf16[2048,512]{1,0:T(8,128)(2,1)}, u32[]{:S(2)}) copy-start(bf16[2048,512]{1,0:T(8,128)(2,1)} %projectors.5) | copy-start | bytes 6291460
  12.2 5.4 %collective-permute-start.6 = (bf16[640,128]{1,0:T(8,128)(2,1)S(1)}, bf16[640,128]{1,0:T(8,128)(2,1)S(1)}, u32[]{:S(2)}, u32[]{:S(2)}) collective-permute-start(bf16[640,128]{1,0:T(8,128)(2,1)S(1)} %forward.1.after), channel_id=1, source_target_pairs={{0,4},{1,3},{2,6},{3,1},{4,0},{5,7},{6,2},{7,5},{8,12},{9,11},{10,... | collective-permute-start | bytes 491528 | tf_op jit(solution)/shard_map/ppermute | solution.py:54
  15.1 1.4 %collective-permute-start.4 = (bf16[2,256,128]{2,1,0:T(8,128)(2,1)S(1)}, bf16[2,256,128]{2,1,0:T(8,128)(2,1)S(1)}, u32[]{:S(2)}, u32[]{:S(2)}) collective-permute-start(bf16[2,256,128]{2,1,0:T(8,128)(2,1)S(1)} %get-tuple-element.22), channel_id=1, source_target_pairs={{0,1},{1,0},{2,3},{3,2},{4,5},{5,4},{6,7},{7,6},{8,9},{9,8},{10,11... | collective-permute-start | bytes 393224 | tf_op jit(solution)/shard_map/ppermute | solution.py:36
  17.7 9.6 %collective-permute-start.7 = (bf16[640,128]{1,0:T(8,128)(2,1)S(1)}, bf16[640,128]{1,0:T(8,128)(2,1)S(1)}, u32[]{:S(2)}, u32[]{:S(2)}) collective-permute-start(bf16[640,128]{1,0:T(8,128)(2,1)S(1)} %get-tuple-element.24), channel_id=1, source_target_pairs={{0,8},{1,9},{2,10},{3,11},{4,12},{5,13},{6,14},{7,15},{8,0},{9,1},... | collective-permute-start | bytes 491528 | tf_op jit(solution)/shard_map/ppermute | solution.py:36
  27.4 8.1 %collective-permute-start.10 = (bf16[640,128]{1,0:T(8,128)(2,1)S(1)}, bf16[640,128]{1,0:T(8,128)(2,1)S(1)}, u32[]{:S(2)}, u32[]{:S(2)}) collective-permute-start(bf16[640,128]{1,0:T(8,128)(2,1)S(1)} %add.1.refs_0_), channel_id=1, source_target_pairs={{0,6},{1,7},{2,4},{3,5},{4,2},{5,3},{6,0},{7,1},{8,14},{9,15},{10,... | collective-permute-start | bytes 491528 | tf_op jit(solution)/shard_map/ppermute | solution.py:36
  28.6 8.9 %collective-permute-start.9 = (bf16[640,128]{1,0:T(8,128)(2,1)S(1)}, bf16[640,128]{1,0:T(8,128)(2,1)S(1)}, u32[]{:S(2)}, u32[]{:S(2)}) collective-permute-start(bf16[640,128]{1,0:T(8,128)(2,1)S(1)} %add.1.refs_0_), channel_id=1, source_target_pairs={{0,4},{1,5},{2,6},{3,7},{4,0},{5,1},{6,2},{7,3},{8,12},{9,13},{10,... | collective-permute-start | bytes 491528 | tf_op jit(solution)/shard_map/ppermute | solution.py:36
  30.5 7.1 %collective-permute-start.8 = (bf16[640,128]{1,0:T(8,128)(2,1)S(1)}, bf16[640,128]{1,0:T(8,128)(2,1)S(1)}, u32[]{:S(2)}, u32[]{:S(2)}) collective-permute-start(bf16[640,128]{1,0:T(8,128)(2,1)S(1)} %add.1.refs_0_), channel_id=1, source_target_pairs={{0,2},{1,3},{2,0},{3,1},{4,6},{5,7},{6,4},{7,5},{8,10},{9,11},{10,... | collective-permute-start | bytes 491528 | tf_op jit(solution)/shard_map/ppermute | solution.py:36
  37.8 2.0 %collective-permute-start.11 = (bf16[8,256,128]{2,1,0:T(8,128)(2,1)S(1)}, bf16[8,256,128]{2,1,0:T(8,128)(2,1)S(1)}, u32[]{:S(2)}, u32[]{:S(2)}) collective-permute-start(bf16[8,256,128]{2,1,0:T(8,128)(2,1)S(1)} %couple.1.scaled), channel_id=1, source_target_pairs={{0,1},{1,0},{2,3},{3,2},{4,5},{5,4},{6,7},{7,6},{8,9},{9,8},{10,11... | collective-permute-start | bytes 1572872 | tf_op jit(solution)/shard_map/ppermute | solution.py:36

commit v15 on v14

--- a/solution.py
+++ b/solution.py
@@ -12,7 +12,7 @@
 SQUARE = 4
 QUARTER = PCAP // SQUARE
 ROW_BLOCK = 512
-ROW_BLOCKS = (512, 512, 512, 256, 256)
+ROW_BLOCKS = (256, 512, 512, 512, 256)
 COPY_ROWS = 128
 GATHERED = (0, 1, 2, 3)
 PARAMS = pltpu.CompilerParams(vmem_limit_bytes=40 * 1024 * 1024)
@@ -58,13 +58,6 @@
     chip = place()[1]
     starts = [pl.multiple_of(block_of(chip, part, entry) * LANES, LANES) for entry in range(2)]
     return jnp.concatenate([columns[rows, pl.ds(start, LANES)] for start in starts], axis=1)
-
-
-def keep_sums(ours, theirs, at, sums):
-    for entry in range(2):
-        lanes = slice(entry * LANES, (entry + 1) * LANES)
-        ours[2 * at + entry] = sums[:PCAP, lanes]
-        theirs[2 * at + entry] = sums[PCAP:, lanes].astype(theirs.dtype)
 
 
 def load_kernel(projectors, flipped, slots, sems):
@@ -97,40 +90,44 @@
     )(pltpu.with_memory_space_constraint(projectors, pltpu.HBM))
 
 
-def project_kernel(parts, flipped, columns, theirs, ours):
+def project_kernel(part, flipped, columns, theirs, ours):
     rows = slice(0, columns.shape[0])
-    for at, part in enumerate(parts):
-        sums = jnp.dot(flipped[...], pair_at(columns, rows, part), preferred_element_type=jnp.float32)
-        keep_sums(ours, theirs, at, sums)
-
-
-def project(flipped, band_coeffs, parts):
+    sums = jnp.dot(flipped[...], pair_at(columns, rows, part), preferred_element_type=jnp.float32)
+    for entry in range(2):
+        lanes = slice(entry * LANES, (entry + 1) * LANES)
+        ours[entry] = sums[:PCAP, lanes]
+        theirs[entry] = sums[PCAP:, lanes].astype(theirs.dtype)
+
+
+def project(flipped, band_coeffs, part):
     slots, depth = flipped.shape
-    shape = (2 * len(parts), PCAP, LANES)
 
     def kernel(*refs):
-        project_kernel(parts, *refs)
+        project_kernel(part, *refs)
 
     return pl.pallas_call(
         kernel,
         in_specs=[VMEM, VMEM],
         out_specs=[VMEM, VMEM],
-        out_shape=[jax.ShapeDtypeStruct(shape, jnp.bfloat16), jax.ShapeDtypeStruct(shape, jnp.float32)],
+        out_shape=[
+            jax.ShapeDtypeStruct((2, PCAP, LANES), jnp.bfloat16),
+            jax.ShapeDtypeStruct((2, PCAP, LANES), jnp.float32),
+        ],
         compiler_params=PARAMS,
         cost_estimate=pl.CostEstimate(
-            flops=4 * depth * slots * len(parts) * LANES, bytes_accessed=2 * depth * slots, transcendentals=0
+            flops=4 * depth * slots * LANES, bytes_accessed=2 * depth * slots, transcendentals=0
         ),
         name="project",
     )(flipped, pltpu.with_memory_space_constraint(band_coeffs, pltpu.VMEM))
 
 
-def project_plain(projectors, band_coeffs, parts):
+def project_plain(projectors, band_coeffs, part):
     depth, bands = band_coeffs.shape
     chips = lax.axis_size("pw") // 2
-    blocks = jnp.stack([block_of(place()[1], q, r) for q in parts for r in range(chips // SQUARE)])
+    blocks = jnp.stack([block_of(place()[1], part, r) for r in range(chips // SQUARE)])
     columns = jnp.take(band_coeffs.reshape(depth, chips, bands // chips), blocks, axis=1)
+    core = place()[0]
     outs = []
-    core = place()[0]
     for group, dtype in ((1 - core, jnp.bfloat16), (core, jnp.float32)):
         slots = lax.dynamic_slice_in_dim(projectors, group * PCAP, PCAP, 1)
         sums = jnp.einsum("ds,dhw->hsw", slots, columns, preferred_element_type=jnp.float32)
@@ -164,53 +161,64 @@
     )(jnp.broadcast_to(owners[:, None], (owners.shape[0], PCAP)), own, sibling, after)
 
 
-def send_kernel(first, second, ours, theirs, quarters, message):
-    entries = ours.shape[0] // (1 if first == second else 2)
-    core = place()[0]
-    start, part = (0, first) if first == second else (core * entries, 1 + core)
+def send_kernel(ours, theirs, quarters, message):
+    entries = ours.shape[0]
     for entry in range(entries):
-        total = ours[start + entry] + theirs[start + entry].astype(jnp.float32)
+        total = ours[entry] + theirs[entry].astype(jnp.float32)
         message[entry * PCAP : (entry + 1) * PCAP] = total.astype(message.dtype)
-    message[entries * PCAP :] = quarters[part]
-
-
-def send(ours, theirs, quarters, parts):
-    count, _, width = ours.shape
-    rows = count // len(parts) * PCAP + quarters.shape[1]
-
-    def kernel(*refs):
-        send_kernel(parts[0], parts[-1], *refs)
-
-    return pl.pallas_call(
-        kernel,
+    message[entries * PCAP :] = quarters[3]
+
+
+def send(ours, theirs, quarters):
+    entries, _, width = ours.shape
+    return pl.pallas_call(
+        send_kernel,
         in_specs=[VMEM] * 3,
         out_specs=VMEM,
-        out_shape=jax.ShapeDtypeStruct((rows, width), jnp.bfloat16),
+        out_shape=jax.ShapeDtypeStruct((entries * PCAP + quarters.shape[1], width), jnp.bfloat16),
         compiler_params=PARAMS,
         name="send",
     )(ours, theirs, quarters)
 
 
-def forward_kernel(ours, theirs, quarters, got, message):
-    core = place()[0]
-    entries = ours.shape[0] // 2
-    start = (1 - core) * entries
+def put_sums(part, sums, message, got=None):
+    one, two, their_one, their_two = sums
+    entries = one.shape[0]
     for entry in range(entries):
         rows = slice(entry * PCAP, (entry + 1) * PCAP)
-        total = ours[start + entry] + theirs[start + entry].astype(jnp.float32)
-        message[rows] = (total + got[rows].astype(jnp.float32)).astype(message.dtype)
-    message[entries * PCAP :] = quarters[2 - core] + got[entries * PCAP :]
-
-
-def forward(ours, theirs, quarters, got):
-    return pl.pallas_call(
-        forward_kernel,
-        in_specs=[VMEM] * 4,
-        out_specs=VMEM,
-        out_shape=jax.ShapeDtypeStruct(got.shape, got.dtype),
-        compiler_params=PARAMS,
-        name="forward",
-    )(ours, theirs, quarters, got)
+        total = jnp.where(part == 1, one[entry], two[entry])
+        total = total + jnp.where(part == 1, their_one[entry], their_two[entry]).astype(jnp.float32)
+        if got is not None:
+            total = total + got[rows].astype(jnp.float32)
+        message[rows] = total.astype(message.dtype)
+    return slice(entries * PCAP, message.shape[0])
+
+
+def send_first_kernel(*refs):
+    *sums, quarters, message = refs
+    part = 1 + place()[0]
+    rows = put_sums(part, sums, message)
+    message[rows] = quarters[part]
+
+
+def forward_kernel(*refs):
+    *sums, quarters, got, message = refs
+    part = 2 - place()[0]
+    rows = put_sums(part, sums, message, got)
+    message[rows] = quarters[part] + got[rows]
+
+
+def send_pair(sums, quarters, got=None):
+    entries, _, width = sums[0].shape
+    operands = sums + (quarters,) + (() if got is None else (got,))
+    return pl.pallas_call(
+        send_first_kernel if got is None else forward_kernel,
+        in_specs=[VMEM] * len(operands),
+        out_specs=VMEM,
+        out_shape=jax.ShapeDtypeStruct((entries * PCAP + quarters.shape[1], width), jnp.bfloat16),
+        compiler_params=PARAMS,
+        name="send_first" if got is None else "forward",
+    )(*operands)
 
 
 def fold_kernel(ours, theirs, quarters, *refs):
@@ -413,24 +421,29 @@
     if fast:
         flipped = load(projectors)
 
-        def partial(parts):
-            return project(flipped, band_coeffs, parts)
+        def partial(part):
+            return project(flipped, band_coeffs, part)
     else:
 
-        def partial(parts):
-            return project_plain(projectors, band_coeffs, parts)
-
-    theirs, ours = partial((3,))
+        def partial(part):
+            return project_plain(projectors, band_coeffs, part)
+
+    theirs, ours = partial(3)
     theirs, sibling_table = lax.optimization_barrier((theirs, sibling_table))
     theirs = swap_cores(theirs)
-    pair_theirs, pair_ours = partial((1, 2))
+    their_one, one = partial(1)
     quarters = choose(owners, own_table, sibling_table, width, ours)
-    got = swap_first(send(ours, theirs, quarters, (3,)))
-    pair_theirs = swap_cores(pair_theirs)
-    low_theirs, low_ours = partial((0,))
+    theirs, their_one = lax.optimization_barrier((theirs, their_one))
+    message = send(ours, theirs, quarters)
+    got = swap_first(message)
+    if fast:
+        flipped, message = lax.optimization_barrier((flipped, message))
+    their_two, two = partial(2)
+    sums = (one, two, swap_cores(their_one), swap_cores(their_two))
+    low_theirs, low_ours = partial(0)
     low_theirs = swap_cores(low_theirs)
-    got_first = swap_first(send(pair_ours, pair_theirs, quarters, (1, 2)))
-    message = forward(pair_ours, pair_theirs, quarters, got)
+    got_first = swap_first(send_pair(sums, quarters))
+    message = send_pair(sums, quarters, got)
     got_second = swap_second(message)
     allowed = mask(counts, atom_of, message)
 

time: 43.3 us -> 44.5 us (1.028)
  waiting for transfers between devices: 17.7 us -> 18.8 us
    ppermute x9 -> x10, waiting for transfers between devices: 14.4 us -> 17.3 us  [swap(): return lax.ppermute(x, 'pw', [(i, i ^ distance) for i in range(count)])]
    ppermute x2, waiting for transfers between devices: 2.27 us -> 0.95 us  [swap_first(): return lax.ppermute(x, 'pw', [(i, i ^ (2, 4)[i % 2]) for i in range(count)])]
    ppermute x1, waiting for transfers between devices: 1.09 us -> 0.57 us  [swap_second(): return lax.ppermute(x, 'pw', [(i, i ^ (4, 2)[i % 2]) for i in range(count)])]
    ppermute x1, starting transfers between devices: 2.13 us -> 1.66 us  [swap_second(): return lax.ppermute(x, 'pw', [(i, i ^ (4, 2)[i % 2]) for i in range(count)])]
    pallas_call x3 -> x4, Pallas kernels: 2.91 us -> 3.15 us  [project(): pl.pallas_call(kernel, in_specs=[VMEM, VMEM], out_specs=[VMEM, VMEM], out...]
    ppermute x9 -> x10, starting transfers between devices: 7.89 us -> 7.91 us  [swap(): return lax.ppermute(x, 'pw', [(i, i ^ distance) for i in range(count)])]
  transfers between devices with their start and end apart: 12 -> 13, of which waited for: 7 -> 9; matrix products, arithmetic and copies ran while one was open for 0% -> 0% of each run, Pallas kernels for 16% -> 17%
where the time goes in v15:
time: 44.5 us; the launch traced here: 44.4 us
  waiting for transfers between devices  18.8 us (42%)
  starting transfers between devices  13.9 us (31%)
  Pallas kernels  11.2 us (25%)
    ppermute x10, waiting for transfers between devices, swap(): return lax.ppermute(x, 'pw', [(i, i ^ distance) for i in range(count)])  17.3 us
    ppermute x10, starting transfers between devices, swap(): return lax.ppermute(x, 'pw', [(i, i ^ distance) for i in range(count)])  7.91 us
    ppermute x2, starting transfers between devices, swap_first(): return lax.ppermute(x, 'pw', [(i, i ^ (2, 4)[i % 2]) for i in range(count)])  4.3 us
    pallas_call x1, Pallas kernels, finish(): pl.pallas_call(finish_kernel, in_specs=[VMEM] * 3, out_specs=HBM, out_sha...  3.37 us
    pallas_call x4, Pallas kernels, project(): pl.pallas_call(kernel, in_specs=[VMEM, VMEM], out_specs=[VMEM, VMEM], out...  3.15 us
    pallas_call x1, Pallas kernels, load(): pl.pallas_call(load_kernel, in_specs=[HBM], out_specs=VMEM, out_shape=jax...  2.1 us
    ppermute x1, starting transfers between devices, swap_second(): return lax.ppermute(x, 'pw', [(i, i ^ (4, 2)[i % 2]) for i in range(count)])  1.66 us
    pallas_call x1, Pallas kernels, begin(): pl.pallas_call(begin_kernel, in_specs=[VMEM, VMEM], out_specs=VMEM, out_s...  1.25 us
  transfers between devices with their start and end apart: 13, of which 9 were waited for; matrix products, arithmetic and copies ran while one was open for 0% of the time, Pallas kernels for 17%

profile of v15, /device:TPU:0, one launch (start us, length us, event | category | flops | bytes accessed | tf_op | source)
XLA Modules:
  0.0 44.4 jit_solution(15909038280915965834)
XLA Ops:
  0.0 0.0 copy-start
  0.0 0.5 %collective-permute-start = (f32[256,256]{1,0:T(8,128)}, f32[256,256]{1,0:T(8,128)S(1)}, u32[]{:S(2)}, u32[]{:S(2)}) collective-permute-start(f32[256,256]{1,0:T(8,128)} %bitcast.1), channel_id=1, source_target_pairs={{0,1},{1,0},{2,3},{3,2},{4,5},{5,4},{6,7},{7,6},{8,9},{9,8},{10,11... | collective-permute-start | bytes 786440 | tf_op jit(solution)/shard_map/ppermute | solution.py:36
  0.5 2.1 %load.1.refs_0_ = bf16[512,2048]{1,0:T(8,128)(2,1)S(1)} custom-call(bf16[2048,512]{1,0:T(8,128)(2,1)} %projectors.5), custom_call_target="tpu_custom_call" | custom-call | tf_op jit(solution)/shard_map/load/pallas_call | solution.py:82
  2.6 0.3 copy-done
  2.8 0.8 %project.5 = (bf16[2,256,128]{2,1,0:T(8,128)(2,1)S(1)}, f32[2,256,128]{2,1,0:T(8,128)S(1)}) custom-call(bf16[512,2048]{1,0:T(8,128)(2,1)S(1)} %load.1.refs_0_, bf16[2048,1024]{1,0:T(8,128)(2,1)S(1)} %copy-done), custom_call_target="tpu_custom_call" | custom-call | flops 536870912 | bytes 2097152 | tf_op jit(solution)/shard_map/project/pallas_call | solution.py:108
  3.6 0.0 copy-start.5
  3.6 0.0 copy-start.2
  3.6 0.0 collective-permute-done.sibling
  3.6 0.5 %collective-permute-start.1 = (bf16[2,256,128]{2,1,0:T(8,128)(2,1)S(1)}, bf16[2,256,128]{2,1,0:T(8,128)(2,1)S(1)}, u32[]{:S(2)}, u32[]{:S(2)}) collective-permute-start(bf16[2,256,128]{2,1,0:T(8,128)(2,1)S(1)} %get-tuple-element.23), channel_id=1, source_target_pairs={{0,1},{1,0},{2,3},{3,2},{4,5},{5,4},{6,7},{7,6},{8,9},{9,8},{10,11... | collective-permute-start | bytes 393224 | tf_op jit(solution)/shard_map/ppermute | solution.py:36
  4.2 0.8 %project.4 = (bf16[2,256,128]{2,1,0:T(8,128)(2,1)S(1)}, f32[2,256,128]{2,1,0:T(8,128)S(1)}) custom-call(bf16[512,2048]{1,0:T(8,128)(2,1)S(1)} %load.1.refs_0_, bf16[2048,1024]{1,0:T(8,128)(2,1)S(1)} %copy-done), custom_call_target="tpu_custom_call" | custom-call | flops 536870912 | bytes 2097152 | tf_op jit(solution)/shard_map/project/pallas_call | solution.py:108
  5.0 0.0 copy-done.5
  5.0 0.1 broadcast_in_dim.2.owners
  5.0 0.0 copy-done.2
  5.1 0.1 collective-permute-done.1.theirs
  5.2 2.9 %collective-permute-start.4 = (bf16[640,128]{1,0:T(8,128)(2,1)S(1)}, bf16[640,128]{1,0:T(8,128)(2,1)S(1)}, u32[]{:S(2)}, u32[]{:S(2)}) collective-permute-start(bf16[640,128]{1,0:T(8,128)(2,1)S(1)} %send.1), channel_id=1, source_target_pairs={{0,2},{1,5},{2,0},{3,7},{4,6},{5,1},{6,4},{7,3},{8,10},{9,13},{10,... | collective-permute-start | bytes 491528 | tf_op jit(solution)/shard_map/ppermute | solution.py:49
  8.1 0.0 collective-permute-start.2
  8.1 0.8 %project.6 = (bf16[2,256,128]{2,1,0:T(8,128)(2,1)S(1)}, f32[2,256,128]{2,1,0:T(8,128)S(1)}) custom-call(bf16[512,2048]{1,0:T(8,128)(2,1)S(1)} %load.1.refs_0_, bf16[2048,1024]{1,0:T(8,128)(2,1)S(1)} %copy-done), custom_call_target="tpu_custom_call" | custom-call | flops 536870912 | bytes 2097152 | tf_op jit(solution)/shard_map/project/pallas_call | solution.py:108
  8.9 0.6 %collective-permute-start.3 = (bf16[2,256,128]{2,1,0:T(8,128)(2,1)S(1)}, bf16[2,256,128]{2,1,0:T(8,128)(2,1)S(1)}, u32[]{:S(2)}, u32[]{:S(2)}) collective-permute-start(bf16[2,256,128]{2,1,0:T(8,128)(2,1)S(1)} %get-tuple-element.30), channel_id=1, source_target_pairs={{0,1},{1,0},{2,3},{3,2},{4,5},{5,4},{6,7},{7,6},{8,9},{9,8},{10,11... | collective-permute-start | bytes 393224 | tf_op jit(solution)/shard_map/ppermute | solution.py:36
  9.5 0.0 collective-permute-done.2.refs_2_
  9.5 1.0 %collective-permute-done.3.refs_3_ = bf16[2,256,128]{2,1,0:T(8,128)(2,1)S(1)} collective-permute-done((bf16[2,256,128]{2,1,0:T(8,128)(2,1)S(1)}, bf16[2,256,128]{2,1,0:T(8,128)(2,1)S(1)}, u32[]{:S(2)}, u32[]{:S(2)}) %collective-permute-start.3) | collective-permute-done | bytes 131104 | tf_op jit(solution)/shard_map/ppermute | solution.py:36
  10.5 0.1 send_first.1
  10.5 1.4 %collective-permute-start.6 = (bf16[640,128]{1,0:T(8,128)(2,1)S(1)}, bf16[640,128]{1,0:T(8,128)(2,1)S(1)}, u32[]{:S(2)}, u32[]{:S(2)}) collective-permute-start(bf16[640,128]{1,0:T(8,128)(2,1)S(1)} %send_first.1), channel_id=1, source_target_pairs={{0,2},{1,5},{2,0},{3,7},{4,6},{5,1},{6,4},{7,3},{8,10},{9,13},{10,... | collective-permute-start | bytes 491528 | tf_op jit(solution)/shard_map/ppermute | solution.py:49
  11.9 0.0 collective-permute-done.4.refs_5_
  11.9 0.1 forward.1.after
  12.0 0.0 copy-start.3
  12.0 0.0 copy-start.4
  12.0 0.0 copy-start.1
  12.0 1.7 %collective-permute-start.7 = (bf16[640,128]{1,0:T(8,128)(2,1)S(1)}, bf16[640,128]{1,0:T(8,128)(2,1)S(1)}, u32[]{:S(2)}, u32[]{:S(2)}) collective-permute-start(bf16[640,128]{1,0:T(8,128)(2,1)S(1)} %forward.1.after), channel_id=1, source_target_pairs={{0,4},{1,3},{2,6},{3,1},{4,0},{5,7},{6,2},{7,5},{8,12},{9,11},{10,... | collective-permute-start | bytes 491528 | tf_op jit(solution)/shard_map/ppermute | solution.py:54
  13.7 0.8 %project.7 = (bf16[2,256,128]{2,1,0:T(8,128)(2,1)S(1)}, f32[2,256,128]{2,1,0:T(8,128)S(1)}) custom-call(bf16[512,2048]{1,0:T(8,128)(2,1)S(1)} %load.1.refs_0_, bf16[2048,1024]{1,0:T(8,128)(2,1)S(1)} %copy-done), custom_call_target="tpu_custom_call" | custom-call | flops 536870912 | bytes 2097152 | tf_op jit(solution)/shard_map/project/pallas_call | solution.py:108
  14.5 0.1 collective-permute-start.5
  14.5 1.3 %collective-permute-done.5.theirs = bf16[2,256,128]{2,1,0:T(8,128)(2,1)S(1)} collective-permute-done((bf16[2,256,128]{2,1,0:T(8,128)(2,1)S(1)}, bf16[2,256,128]{2,1,0:T(8,128)(2,1)S(1)}, u32[]{:S(2)}, u32[]{:S(2)}) %collective-permute-start.5) | collective-permute-done | bytes 131104 | tf_op jit(solution)/shard_map/ppermute | solution.py:36
  15.9 1.0 %collective-permute-done.6.refs_0_ = bf16[640,128]{1,0:T(8,128)(2,1)S(1)} collective-permute-done((bf16[640,128]{1,0:T(8,128)(2,1)S(1)}, bf16[640,128]{1,0:T(8,128)(2,1)S(1)}, u32[]{:S(2)}, u32[]{:S(2)}) %collective-permute-start.6) | collective-permute-done | bytes 163872 | tf_op jit(solution)/shard_map/ppermute | solution.py:49
  16.8 0.6 %collective-permute-done.7.refs_1_ = bf16[640,128]{1,0:T(8,128)(2,1)S(1)} collective-permute-done((bf16[640,128]{1,0:T(8,128)(2,1)S(1)}, bf16[640,128]{1,0:T(8,128)(2,1)S(1)}, u32[]{:S(2)}, u32[]{:S(2)}) %collective-permute-start.7) | collective-permute-done | bytes 163872 | tf_op jit(solution)/shard_map/ppermute | solution.py:54
  17.4 0.1 fold.1
  17.5 2.7 %collective-permute-start.8 = (bf16[640,128]{1,0:T(8,128)(2,1)S(1)}, bf16[640,128]{1,0:T(8,128)(2,1)S(1)}, u32[]{:S(2)}, u32[]{:S(2)}) collective-permute-start(bf16[640,128]{1,0:T(8,128)(2,1)S(1)} %get-tuple-element.34), channel_id=1, source_target_pairs={{0,8},{1,9},{2,10},{3,11},{4,12},{5,13},{6,14},{7,15},{8,0},{9,1},... | collective-permute-start | bytes 491528 | tf_op jit(solution)/shard_map/ppermute | solution.py:36
  20.1 8.0 %collective-permute-done.8.right = bf16[640,128]{1,0:T(8,128)(2,1)S(1)} collective-permute-done((bf16[640,128]{1,0:T(8,128)(2,1)S(1)}, bf16[640,128]{1,0:T(8,128)(2,1)S(1)}, u32[]{:S(2)}, u32[]{:S(2)}) %collective-permute-start.8) | collective-permute-done | bytes 163872 | tf_op jit(solution)/shard_map/ppermute | solution.py:36
  28.2 1.1 %collective-permute-start.11 = (bf16[640,128]{1,0:T(8,128)(2,1)S(1)}, bf16[640,128]{1,0:T(8,128)(2,1)S(1)}, u32[]{:S(2)}, u32[]{:S(2)}) collective-permute-start(bf16[640,128]{1,0:T(8,128)(2,1)S(1)} %add.1.refs_0_), channel_id=1, source_target_pairs={{0,6},{1,7},{2,4},{3,5},{4,2},{5,3},{6,0},{7,1},{8,14},{9,15},{10,... | collective-permute-start | bytes 491528 | tf_op jit(solution)/shard_map/ppermute | solution.py:36
  29.3 2.0 %collective-permute-start.10 = (bf16[640,128]{1,0:T(8,128)(2,1)S(1)}, bf16[640,128]{1,0:T(8,128)(2,1)S(1)}, u32[]{:S(2)}, u32[]{:S(2)}) collective-permute-start(bf16[640,128]{1,0:T(8,128)(2,1)S(1)} %add.1.refs_0_), channel_id=1, source_target_pairs={{0,4},{1,5},{2,6},{3,7},{4,0},{5,1},{6,2},{7,3},{8,12},{9,13},{10,... | collective-permute-start | bytes 491528 | tf_op jit(solution)/shard_map/ppermute | solution.py:36
  31.3 0.5 %collective-permute-start.9 = (bf16[640,128]{1,0:T(8,128)(2,1)S(1)}, bf16[640,128]{1,0:T(8,128)(2,1)S(1)}, u32[]{:S(2)}, u32[]{:S(2)}) collective-permute-start(bf16[640,128]{1,0:T(8,128)(2,1)S(1)} %add.1.refs_0_), channel_id=1, source_target_pairs={{0,2},{1,3},{2,0},{3,1},{4,6},{5,7},{6,4},{7,5},{8,10},{9,11},{10,... | collective-permute-start | bytes 491528 | tf_op jit(solution)/shard_map/ppermute | solution.py:36
  31.8 0.0 copy-done.3
  31.8 0.0 copy-done.4
  31.8 0.7 %mask.1.allowed = bf16[256,256]{1,0:T(8,128)(2,1)S(1)} custom-call(s32[2,4]{1,0:T(2,128)S(1)} %copy-done.4, s32[2,256]{1,0:T(2,128)S(1)} %copy-done.3, bf16[640,128]{1,0:T(8,128)(2,1)S(1)} %forward.1.after), custom_call_target="tpu_custom_call" | custom-call | tf_op jit(solution)/shard_map/mask/pallas_call | solution.py:282
  32.4 3.9 %collective-permute-done.11.refs_3_ = bf16[640,128]{1,0:T(8,128)(2,1)S(1)} collective-permute-done((bf16[640,128]{1,0:T(8,128)(2,1)S(1)}, bf16[640,128]{1,0:T(8,128)(2,1)S(1)}, u32[]{:S(2)}, u32[]{:S(2)}) %collective-permute-start.11) | collective-permute-done | bytes 163872 | tf_op jit(solution)/shard_map/ppermute | solution.py:36
  36.3 2.4 %collective-permute-done.10.refs_2_ = bf16[640,128]{1,0:T(8,128)(2,1)S(1)} collective-permute-done((bf16[640,128]{1,0:T(8,128)(2,1)S(1)}, bf16[640,128]{1,0:T(8,128)(2,1)S(1)}, u32[]{:S(2)}, u32[]{:S(2)}) %collective-permute-start.10) | collective-permute-done | bytes 163872 | tf_op jit(solution)/shard_map/ppermute | solution.py:36
  38.7 0.0 collective-permute-done.9.refs_1_
  38.7 0.3 couple.1.scaled
  39.0 0.1 collective-permute-start.12
  39.1 0.0 copy-done.1
  39.1 1.3 %begin.1.begun = f32[4,2048,256]{2,1,0:T(8,128)S(1)} custom-call(bf16[2048,512]{1,0:T(8,128)(2,1)S(1)} %copy-done.1, bf16[8,256,128]{2,1,0:T(8,128)(2,1)S(1)} %couple.1.scaled), custom_call_target="tpu_custom_call" | custom-call | flops 1073741824 | bytes 2097152 | tf_op jit(solution)/shard_map/begin/pallas_call | solution.py:346
  40.4 0.6 %collective-permute-done.12.other = bf16[8,256,128]{2,1,0:T(8,128)(2,1)S(1)} collective-permute-done((bf16[8,256,128]{2,1,0:T(8,128)(2,1)S(1)}, bf16[8,256,128]{2,1,0:T(8,128)(2,1)S(1)}, u32[]{:S(2)}, u32[]{:S(2)}) %collective-permute-start.12) | collective-permute-done | bytes 524320 | tf_op jit(solution)/shard_map/ppermute | solution.py:36
  41.0 3.4 %finish.1 = bf16[2048,1024]{1,0:T(8,128)(2,1)} custom-call(bf16[2048,512]{1,0:T(8,128)(2,1)S(1)} %copy-done.1, f32[4,2048,256]{2,1,0:T(8,128)S(1)} %begin.1.begun, bf16[8,256,128]{2,1,0:T(8,128)(2,1)S(1)} %collective-permute-done.12.other), custom_call_target="tpu_custom_call" | custom-call | flops 1073741824 | bytes 6291456 | tf_op jit(solution)/shard_map/finish/pallas_call | solution.py:386
  (3 shorter events, 0.1 us)
Async XLA Ops:
  0.0 2.8 %copy-start = (bf16[2048,1024]{1,0:T(8,128)(2,1)S(1)}, bf16[2048,1024]{1,0:T(8,128)(2,1)}, u32[]{:S(2)}) copy-start(bf16[2048,1024]{1,0:T(8,128)(2,1)} %refs_1_.7) | copy-start | bytes 12582916
  0.0 3.6 %collective-permute-start = (f32[256,256]{1,0:T(8,128)}, f32[256,256]{1,0:T(8,128)S(1)}, u32[]{:S(2)}, u32[]{:S(2)}) collective-permute-start(f32[256,256]{1,0:T(8,128)} %bitcast.1), channel_id=1, source_target_pairs={{0,1},{1,0},{2,3},{3,2},{4,5},{5,4},{6,7},{7,6},{8,9},{9,8},{10,11... | collective-permute-start | bytes 786440 | tf_op jit(solution)/shard_map/ppermute | solution.py:36
  3.6 1.4 %copy-start.5 = (s32[2]{0:T(128)S(1)}, s32[2]{0:T(128)}, u32[]{:S(2)}) copy-start(s32[2]{0:T(128)} %param.10) | copy-start | bytes 28
  3.6 1.4 %copy-start.2 = (f32[1,256,256]{2,1,0:T(8,128)S(1)}, f32[1,256,256]{2,1,0:T(8,128)}, u32[]{:S(2)}) copy-start(f32[1,256,256]{2,1,0:T(8,128)} %param.11) | copy-start | bytes 786436
  3.6 1.5 %collective-permute-start.1 = (bf16[2,256,128]{2,1,0:T(8,128)(2,1)S(1)}, bf16[2,256,128]{2,1,0:T(8,128)(2,1)S(1)}, u32[]{:S(2)}, u32[]{:S(2)}) collective-permute-start(bf16[2,256,128]{2,1,0:T(8,128)(2,1)S(1)} %get-tuple-element.23), channel_id=1, source_target_pairs={{0,1},{1,0},{2,3},{3,2},{4,5},{5,4},{6,7},{7,6},{8,9},{9,8},{10,11... | collective-permute-start | bytes 393224 | tf_op jit(solution)/shard_map/ppermute | solution.py:36
  5.2 6.7 %collective-permute-start.4 = (bf16[640,128]{1,0:T(8,128)(2,1)S(1)}, bf16[640,128]{1,0:T(8,128)(2,1)S(1)}, u32[]{:S(2)}, u32[]{:S(2)}) collective-permute-start(bf16[640,128]{1,0:T(8,128)(2,1)S(1)} %send.1), channel_id=1, source_target_pairs={{0,2},{1,5},{2,0},{3,7},{4,6},{5,1},{6,4},{7,3},{8,10},{9,13},{10,... | collective-permute-start | bytes 491528 | tf_op jit(solution)/shard_map/ppermute | solution.py:49
  8.1 1.4 %collective-permute-start.2 = (bf16[2,256,128]{2,1,0:T(8,128)(2,1)S(1)}, bf16[2,256,128]{2,1,0:T(8,128)(2,1)S(1)}, u32[]{:S(2)}, u32[]{:S(2)}) collective-permute-start(bf16[2,256,128]{2,1,0:T(8,128)(2,1)S(1)} %get-tuple-element.29), channel_id=1, source_target_pairs={{0,1},{1,0},{2,3},{3,2},{4,5},{5,4},{6,7},{7,6},{8,9},{9,8},{10,11... | collective-permute-start | bytes 393224 | tf_op jit(solution)/shard_map/ppermute | solution.py:36
  8.9 1.6 %collective-permute-start.3 = (bf16[2,256,128]{2,1,0:T(8,128)(2,1)S(1)}, bf16[2,256,128]{2,1,0:T(8,128)(2,1)S(1)}, u32[]{:S(2)}, u32[]{:S(2)}) collective-permute-start(bf16[2,256,128]{2,1,0:T(8,128)(2,1)S(1)} %get-tuple-element.30), channel_id=1, source_target_pairs={{0,1},{1,0},{2,3},{3,2},{4,5},{5,4},{6,7},{7,6},{8,9},{9,8},{10,11... | collective-permute-start | bytes 393224 | tf_op jit(solution)/shard_map/ppermute | solution.py:36
  10.5 6.3 %collective-permute-start.6 = (bf16[640,128]{1,0:T(8,128)(2,1)S(1)}, bf16[640,128]{1,0:T(8,128)(2,1)S(1)}, u32[]{:S(2)}, u32[]{:S(2)}) collective-permute-start(bf16[640,128]{1,0:T(8,128)(2,1)S(1)} %send_first.1), channel_id=1, source_target_pairs={{0,2},{1,5},{2,0},{3,7},{4,6},{5,1},{6,4},{7,3},{8,10},{9,13},{10,... | collective-permute-start | bytes 491528 | tf_op jit(solution)/shard_map/ppermute | solution.py:49
  12.0 19.8 %copy-start.3 = (s32[2,256]{1,0:T(2,128)S(1)}, s32[2,256]{1,0:T(2,128)}, u32[]{:S(2)}) copy-start(s32[2,256]{1,0:T(2,128)} %atom_of.1) | copy-start | bytes 6148
  12.0 19.8 %copy-start.4 = (s32[2,4]{1,0:T(2,128)S(1)}, s32[2,4]{1,0:T(2,128)}, u32[]{:S(2)}) copy-start(s32[2,4]{1,0:T(2,128)} %counts.1) | copy-start | bytes 100
  12.0 27.1 %copy-start.1 = (bf16[2048,512]{1,0:T(8,128)(2,1)S(1)}, bf16[2048,512]{1,0:T(8,128)(2,1)}, u32[]{:S(2)}) copy-start(bf16[2048,512]{1,0:T(8,128)(2,1)} %projectors.5) | copy-start | bytes 6291460
  12.0 5.4 %collective-permute-start.7 = (bf16[640,128]{1,0:T(8,128)(2,1)S(1)}, bf16[640,128]{1,0:T(8,128)(2,1)S(1)}, u32[]{:S(2)}, u32[]{:S(2)}) collective-permute-start(bf16[640,128]{1,0:T(8,128)(2,1)S(1)} %forward.1.after), channel_id=1, source_target_pairs={{0,4},{1,3},{2,6},{3,1},{4,0},{5,7},{6,2},{7,5},{8,12},{9,11},{10,... | collective-permute-start | bytes 491528 | tf_op jit(solution)/shard_map/ppermute | solution.py:54
  14.5 1.4 %collective-permute-start.5 = (bf16[2,256,128]{2,1,0:T(8,128)(2,1)S(1)}, bf16[2,256,128]{2,1,0:T(8,128)(2,1)S(1)}, u32[]{:S(2)}, u32[]{:S(2)}) collective-permute-start(bf16[2,256,128]{2,1,0:T(8,128)(2,1)S(1)} %get-tuple-element.32), channel_id=1, source_target_pairs={{0,1},{1,0},{2,3},{3,2},{4,5},{5,4},{6,7},{7,6},{8,9},{9,8},{10,11... | collective-permute-start | bytes 393224 | tf_op jit(solution)/shard_map/ppermute | solution.py:36
  17.5 10.7 %collective-permute-start.8 = (bf16[640,128]{1,0:T(8,128)(2,1)S(1)}, bf16[640,128]{1,0:T(8,128)(2,1)S(1)}, u32[]{:S(2)}, u32[]{:S(2)}) collective-permute-start(bf16[640,128]{1,0:T(8,128)(2,1)S(1)} %get-tuple-element.34), channel_id=1, source_target_pairs={{0,8},{1,9},{2,10},{3,11},{4,12},{5,13},{6,14},{7,15},{8,0},{9,1},... | collective-permute-start | bytes 491528 | tf_op jit(solution)/shard_map/ppermute | solution.py:36
  28.2 8.1 %collective-permute-start.11 = (bf16[640,128]{1,0:T(8,128)(2,1)S(1)}, bf16[640,128]{1,0:T(8,128)(2,1)S(1)}, u32[]{:S(2)}, u32[]{:S(2)}) collective-permute-start(bf16[640,128]{1,0:T(8,128)(2,1)S(1)} %add.1.refs_0_), channel_id=1, source_target_pairs={{0,6},{1,7},{2,4},{3,5},{4,2},{5,3},{6,0},{7,1},{8,14},{9,15},{10,... | collective-permute-start | bytes 491528 | tf_op jit(solution)/shard_map/ppermute | solution.py:36
  29.3 9.4 %collective-permute-start.10 = (bf16[640,128]{1,0:T(8,128)(2,1)S(1)}, bf16[640,128]{1,0:T(8,128)(2,1)S(1)}, u32[]{:S(2)}, u32[]{:S(2)}) collective-permute-start(bf16[640,128]{1,0:T(8,128)(2,1)S(1)} %add.1.refs_0_), channel_id=1, source_target_pairs={{0,4},{1,5},{2,6},{3,7},{4,0},{5,1},{6,2},{7,3},{8,12},{9,13},{10,... | collective-permute-start | bytes 491528 | tf_op jit(solution)/shard_map/ppermute | solution.py:36
  31.3 7.4 %collective-permute-start.9 = (bf16[640,128]{1,0:T(8,128)(2,1)S(1)}, bf16[640,128]{1,0:T(8,128)(2,1)S(1)}, u32[]{:S(2)}, u32[]{:S(2)}) collective-permute-start(bf16[640,128]{1,0:T(8,128)(2,1)S(1)} %add.1.refs_0_), channel_id=1, source_target_pairs={{0,2},{1,3},{2,0},{3,1},{4,6},{5,7},{6,4},{7,5},{8,10},{9,11},{10,... | collective-permute-start | bytes 491528 | tf_op jit(solution)/shard_map/ppermute | solution.py:36
  39.0 2.0 %collective-permute-start.12 = (bf16[8,256,128]{2,1,0:T(8,128)(2,1)S(1)}, bf16[8,256,128]{2,1,0:T(8,128)(2,1)S(1)}, u32[]{:S(2)}, u32[]{:S(2)}) collective-permute-start(bf16[8,256,128]{2,1,0:T(8,128)(2,1)S(1)} %couple.1.scaled), channel_id=1, source_target_pairs={{0,1},{1,0},{2,3},{3,2},{4,5},{5,4},{6,7},{7,6},{8,9},{9,8},{10,11... | collective-permute-start | bytes 1572872 | tf_op jit(solution)/shard_map/ppermute | solution.py:36

commit v16 on v14

--- a/solution.py
+++ b/solution.py
@@ -14,7 +14,6 @@
 ROW_BLOCK = 512
 ROW_BLOCKS = (512, 512, 512, 256, 256)
 COPY_ROWS = 128
-GATHERED = (0, 1, 2, 3)
 PARAMS = pltpu.CompilerParams(vmem_limit_bytes=40 * 1024 * 1024)
 VMEM = pl.BlockSpec(memory_space=pltpu.VMEM)
 SMEM = pl.BlockSpec(memory_space=pltpu.SMEM)
@@ -285,8 +284,10 @@
     *messages, out, coupling = refs
     width = out.shape[2]
     entries = out.shape[0] // SQUARE
-    corner = place()[1] & 3
-    for part, message in zip(GATHERED, messages):
+    core, chip = place()
+    corner = chip & 3
+    parts = (0, 1 + core, 2 - core, 3)
+    for part, message in zip(parts, messages):
         start = pl.multiple_of((corner ^ part) * QUARTER, QUARTER)
         for cut in range(PCAP // width):
             lanes = slice(cut * width, (cut + 1) * width)
@@ -294,7 +295,7 @@
             coupling[pl.ds(start, QUARTER), lanes] = (
                 message[first : first + QUARTER] * allowed[pl.ds(start, QUARTER), lanes]
             )
-    for part, message in zip(GATHERED, messages):
+    for part, message in zip(parts, messages):
         wide = jnp.concatenate([message[e * PCAP : (e + 1) * PCAP] for e in range(entries)], axis=1)
         scaled = jnp.dot(coupling[...], wide, preferred_element_type=jnp.float32).astype(out.dtype)
         for entry in range(entries):
@@ -444,7 +445,7 @@
         mine = add(mine.astype(jnp.float32), swap_chips(message, distance))
         distance *= 2
 
-    scaled = couple(allowed, [swap_chips(mine, part) if part else mine for part in GATHERED])
+    scaled = couple(allowed, [mine, swap_first(mine), swap_second(mine), swap_chips(mine, 3)])
     other = swap_cores(scaled)
     if not fast:
         return apply_plain(projectors, scaled, other)

time: 43.3 us -> 43.3 us (level)
    ppermute x9 -> x7, starting transfers between devices: 7.89 us -> 5.55 us  [swap(): return lax.ppermute(x, 'pw', [(i, i ^ distance) for i in range(count)])]
    ppermute x1 -> x2, waiting for transfers between devices: 1.09 us -> 3.13 us  [swap_second(): return lax.ppermute(x, 'pw', [(i, i ^ (4, 2)[i % 2]) for i in range(count)])]
    ppermute x9 -> x7, waiting for transfers between devices: 14.4 us -> 12.4 us  [swap(): return lax.ppermute(x, 'pw', [(i, i ^ distance) for i in range(count)])]
    ppermute x1 -> x2, starting transfers between devices: 2.13 us -> 3.97 us  [swap_second(): return lax.ppermute(x, 'pw', [(i, i ^ (4, 2)[i % 2]) for i in range(count)])]
    ppermute x2 -> x3, starting transfers between devices: 4.03 us -> 4.53 us  [swap_first(): return lax.ppermute(x, 'pw', [(i, i ^ (2, 4)[i % 2]) for i in range(count)])]
    ppermute x2 -> x3, waiting for transfers between devices: 2.27 us -> 2.28 us  [swap_first(): return lax.ppermute(x, 'pw', [(i, i ^ (2, 4)[i % 2]) for i in range(count)])]
where the time goes in v16:
time: 43.3 us; the launch traced here: 43.1 us
  waiting for transfers between devices  17.8 us (41%)
  starting transfers between devices  14 us (32%)
  Pallas kernels  10.8 us (25%)
    ppermute x7, waiting for transfers between devices, swap(): return lax.ppermute(x, 'pw', [(i, i ^ distance) for i in range(count)])  12.4 us
    ppermute x7, starting transfers between devices, swap(): return lax.ppermute(x, 'pw', [(i, i ^ distance) for i in range(count)])  5.55 us
    ppermute x3, starting transfers between devices, swap_first(): return lax.ppermute(x, 'pw', [(i, i ^ (2, 4)[i % 2]) for i in range(count)])  4.53 us
    ppermute x2, starting transfers between devices, swap_second(): return lax.ppermute(x, 'pw', [(i, i ^ (4, 2)[i % 2]) for i in range(count)])  3.97 us
    pallas_call x1, Pallas kernels, finish(): pl.pallas_call(finish_kernel, in_specs=[VMEM] * 3, out_specs=HBM, out_sha...  3.3 us
    ppermute x2, waiting for transfers between devices, swap_second(): return lax.ppermute(x, 'pw', [(i, i ^ (4, 2)[i % 2]) for i in range(count)])  3.13 us
    pallas_call x3, Pallas kernels, project(): pl.pallas_call(kernel, in_specs=[VMEM, VMEM], out_specs=[VMEM, VMEM], out...  2.91 us
    ppermute x3, waiting for transfers between devices, swap_first(): return lax.ppermute(x, 'pw', [(i, i ^ (2, 4)[i % 2]) for i in range(count)])  2.28 us
  transfers between devices with their start and end apart: 12, of which 7 were waited for; matrix products, arithmetic and copies ran while one was open for 0% of the time, Pallas kernels for 16%

profile of v16, /device:TPU:0, one launch (start us, length us, event | category | flops | bytes accessed | tf_op | source)
XLA Modules:
  0.0 43.1 jit_solution(2176194005430609371)
XLA Ops:
  0.0 0.0 copy-start
  0.0 0.5 %collective-permute-start.1 = (f32[256,256]{1,0:T(8,128)}, f32[256,256]{1,0:T(8,128)S(1)}, u32[]{:S(2)}, u32[]{:S(2)}) collective-permute-start(f32[256,256]{1,0:T(8,128)} %bitcast.1), channel_id=1, source_target_pairs={{0,1},{1,0},{2,3},{3,2},{4,5},{5,4},{6,7},{7,6},{8,9},{9,8},{10,11... | collective-permute-start | bytes 786440 | tf_op jit(solution)/shard_map/ppermute | solution.py:35
  0.5 2.1 %load.1.refs_0_ = bf16[512,2048]{1,0:T(8,128)(2,1)S(1)} custom-call(bf16[2048,512]{1,0:T(8,128)(2,1)} %projectors.5), custom_call_target="tpu_custom_call" | custom-call | tf_op jit(solution)/shard_map/load/pallas_call | solution.py:88
  2.6 0.3 copy-done
  2.8 0.8 %project.4 = (bf16[2,256,128]{2,1,0:T(8,128)(2,1)S(1)}, f32[2,256,128]{2,1,0:T(8,128)S(1)}) custom-call(bf16[512,2048]{1,0:T(8,128)(2,1)S(1)} %load.1.refs_0_, bf16[2048,1024]{1,0:T(8,128)(2,1)S(1)} %copy-done), custom_call_target="tpu_custom_call" | custom-call | flops 536870912 | bytes 2097152 | tf_op jit(solution)/shard_map/project/pallas_call | solution.py:113
  3.6 0.0 copy-start.5
  3.6 0.0 copy-start.2
  3.6 0.0 collective-permute-done.1.sibling
  3.6 0.5 %collective-permute-start.2 = (bf16[2,256,128]{2,1,0:T(8,128)(2,1)S(1)}, bf16[2,256,128]{2,1,0:T(8,128)(2,1)S(1)}, u32[]{:S(2)}, u32[]{:S(2)}) collective-permute-start(bf16[2,256,128]{2,1,0:T(8,128)(2,1)S(1)} %get-tuple-element.20), channel_id=1, source_target_pairs={{0,1},{1,0},{2,3},{3,2},{4,5},{5,4},{6,7},{7,6},{8,9},{9,8},{10,11... | collective-permute-start | bytes 393224 | tf_op jit(solution)/shard_map/ppermute | solution.py:35
  4.2 1.3 %project.3 = (bf16[4,256,128]{2,1,0:T(8,128)(2,1)S(1)}, f32[4,256,128]{2,1,0:T(8,128)S(1)}) custom-call(bf16[512,2048]{1,0:T(8,128)(2,1)S(1)} %load.1.refs_0_, bf16[2048,1024]{1,0:T(8,128)(2,1)S(1)} %copy-done), custom_call_target="tpu_custom_call" | custom-call | flops 1073741824 | bytes 2097152 | tf_op jit(solution)/shard_map/project/pallas_call | solution.py:113
  5.5 0.1 collective-permute-start
  5.6 0.0 copy-done.5
  5.6 0.1 broadcast_in_dim.2.owners
  5.7 0.0 copy-done.2
  5.7 0.0 collective-permute-done.2.refs_1_
  5.8 3.0 %collective-permute-start.3 = (bf16[640,128]{1,0:T(8,128)(2,1)S(1)}, bf16[640,128]{1,0:T(8,128)(2,1)S(1)}, u32[]{:S(2)}, u32[]{:S(2)}) collective-permute-start(bf16[640,128]{1,0:T(8,128)(2,1)S(1)} %send.2), channel_id=1, source_target_pairs={{0,2},{1,5},{2,0},{3,7},{4,6},{5,1},{6,4},{7,3},{8,10},{9,13},{10,... | collective-permute-start | bytes 491528 | tf_op jit(solution)/shard_map/ppermute | solution.py:48
  8.8 0.0 collective-permute-done.theirs.refs_1_
  8.9 1.0 %collective-permute-start.5 = (bf16[640,128]{1,0:T(8,128)(2,1)S(1)}, bf16[640,128]{1,0:T(8,128)(2,1)S(1)}, u32[]{:S(2)}, u32[]{:S(2)}) collective-permute-start(bf16[640,128]{1,0:T(8,128)(2,1)S(1)} %send.3), channel_id=1, source_target_pairs={{0,2},{1,5},{2,0},{3,7},{4,6},{5,1},{6,4},{7,3},{8,10},{9,13},{10,... | collective-permute-start | bytes 491528 | tf_op jit(solution)/shard_map/ppermute | solution.py:48
  9.9 2.3 %collective-permute-done.3.got = bf16[640,128]{1,0:T(8,128)(2,1)S(1)} collective-permute-done((bf16[640,128]{1,0:T(8,128)(2,1)S(1)}, bf16[640,128]{1,0:T(8,128)(2,1)S(1)}, u32[]{:S(2)}, u32[]{:S(2)}) %collective-permute-start.3) | collective-permute-done | bytes 163872 | tf_op jit(solution)/shard_map/ppermute | solution.py:48
  12.1 0.1 forward.1.after
  12.2 0.0 copy-start.3
  12.2 0.0 copy-start.4
  12.2 0.0 copy-start.1
  12.2 2.1 %collective-permute-start.6 = (bf16[640,128]{1,0:T(8,128)(2,1)S(1)}, bf16[640,128]{1,0:T(8,128)(2,1)S(1)}, u32[]{:S(2)}, u32[]{:S(2)}) collective-permute-start(bf16[640,128]{1,0:T(8,128)(2,1)S(1)} %forward.1.after), channel_id=1, source_target_pairs={{0,4},{1,3},{2,6},{3,1},{4,0},{5,7},{6,2},{7,5},{8,12},{9,11},{10,... | collective-permute-start | bytes 491528 | tf_op jit(solution)/shard_map/ppermute | solution.py:53
  14.3 0.8 %project.5 = (bf16[2,256,128]{2,1,0:T(8,128)(2,1)S(1)}, f32[2,256,128]{2,1,0:T(8,128)S(1)}) custom-call(bf16[512,2048]{1,0:T(8,128)(2,1)S(1)} %load.1.refs_0_, bf16[2048,1024]{1,0:T(8,128)(2,1)S(1)} %copy-done), custom_call_target="tpu_custom_call" | custom-call | flops 536870912 | bytes 2097152 | tf_op jit(solution)/shard_map/project/pallas_call | solution.py:113
  15.1 0.1 collective-permute-start.4
  15.2 1.3 %collective-permute-done.4.theirs = bf16[2,256,128]{2,1,0:T(8,128)(2,1)S(1)} collective-permute-done((bf16[2,256,128]{2,1,0:T(8,128)(2,1)S(1)}, bf16[2,256,128]{2,1,0:T(8,128)(2,1)S(1)}, u32[]{:S(2)}, u32[]{:S(2)}) %collective-permute-start.4) | collective-permute-done | bytes 131104 | tf_op jit(solution)/shard_map/ppermute | solution.py:35
  16.6 0.0 collective-permute-done.5.refs_0_
  16.6 1.1 %collective-permute-done.6.refs_1_ = bf16[640,128]{1,0:T(8,128)(2,1)S(1)} collective-permute-done((bf16[640,128]{1,0:T(8,128)(2,1)S(1)}, bf16[640,128]{1,0:T(8,128)(2,1)S(1)}, u32[]{:S(2)}, u32[]{:S(2)}) %collective-permute-start.6) | collective-permute-done | bytes 163872 | tf_op jit(solution)/shard_map/ppermute | solution.py:53
  17.6 0.1 fold.1
  17.7 3.1 %collective-permute-start.7 = (bf16[640,128]{1,0:T(8,128)(2,1)S(1)}, bf16[640,128]{1,0:T(8,128)(2,1)S(1)}, u32[]{:S(2)}, u32[]{:S(2)}) collective-permute-start(bf16[640,128]{1,0:T(8,128)(2,1)S(1)} %get-tuple-element.24), channel_id=1, source_target_pairs={{0,8},{1,9},{2,10},{3,11},{4,12},{5,13},{6,14},{7,15},{8,0},{9,1},... | collective-permute-start | bytes 491528 | tf_op jit(solution)/shard_map/ppermute | solution.py:35
  20.8 6.5 %collective-permute-done.7.right = bf16[640,128]{1,0:T(8,128)(2,1)S(1)} collective-permute-done((bf16[640,128]{1,0:T(8,128)(2,1)S(1)}, bf16[640,128]{1,0:T(8,128)(2,1)S(1)}, u32[]{:S(2)}, u32[]{:S(2)}) %collective-permute-start.7) | collective-permute-done | bytes 163872 | tf_op jit(solution)/shard_map/ppermute | solution.py:35
  27.4 1.2 %collective-permute-start.10 = (bf16[640,128]{1,0:T(8,128)(2,1)S(1)}, bf16[640,128]{1,0:T(8,128)(2,1)S(1)}, u32[]{:S(2)}, u32[]{:S(2)}) collective-permute-start(bf16[640,128]{1,0:T(8,128)(2,1)S(1)} %add.1.refs_0_), channel_id=1, source_target_pairs={{0,6},{1,7},{2,4},{3,5},{4,2},{5,3},{6,0},{7,1},{8,14},{9,15},{10,... | collective-permute-start | bytes 491528 | tf_op jit(solution)/shard_map/ppermute | solution.py:35
  28.6 1.8 %collective-permute-start.9 = (bf16[640,128]{1,0:T(8,128)(2,1)S(1)}, bf16[640,128]{1,0:T(8,128)(2,1)S(1)}, u32[]{:S(2)}, u32[]{:S(2)}) collective-permute-start(bf16[640,128]{1,0:T(8,128)(2,1)S(1)} %add.1.refs_0_), channel_id=1, source_target_pairs={{0,4},{1,3},{2,6},{3,1},{4,0},{5,7},{6,2},{7,5},{8,12},{9,11},{10,... | collective-permute-start | bytes 491528 | tf_op jit(solution)/shard_map/ppermute | solution.py:53
  30.5 0.5 %collective-permute-start.8 = (bf16[640,128]{1,0:T(8,128)(2,1)S(1)}, bf16[640,128]{1,0:T(8,128)(2,1)S(1)}, u32[]{:S(2)}, u32[]{:S(2)}) collective-permute-start(bf16[640,128]{1,0:T(8,128)(2,1)S(1)} %add.1.refs_0_), channel_id=1, source_target_pairs={{0,2},{1,5},{2,0},{3,7},{4,6},{5,1},{6,4},{7,3},{8,10},{9,13},{10,... | collective-permute-start | bytes 491528 | tf_op jit(solution)/shard_map/ppermute | solution.py:48
  31.0 0.0 copy-done.3
  31.0 0.0 copy-done.4
  31.0 0.7 %mask.1.allowed = bf16[256,256]{1,0:T(8,128)(2,1)S(1)} custom-call(s32[2,4]{1,0:T(2,128)S(1)} %copy-done.4, s32[2,256]{1,0:T(2,128)S(1)} %copy-done.3, bf16[640,128]{1,0:T(8,128)(2,1)S(1)} %forward.1.after), custom_call_target="tpu_custom_call" | custom-call | tf_op jit(solution)/shard_map/mask/pallas_call | solution.py:273
  31.6 3.9 %collective-permute-done.10.refs_3_ = bf16[640,128]{1,0:T(8,128)(2,1)S(1)} collective-permute-done((bf16[640,128]{1,0:T(8,128)(2,1)S(1)}, bf16[640,128]{1,0:T(8,128)(2,1)S(1)}, u32[]{:S(2)}, u32[]{:S(2)}) %collective-permute-start.10) | collective-permute-done | bytes 163872 | tf_op jit(solution)/shard_map/ppermute | solution.py:35
  35.5 2.0 %collective-permute-done.9.refs_2_ = bf16[640,128]{1,0:T(8,128)(2,1)S(1)} collective-permute-done((bf16[640,128]{1,0:T(8,128)(2,1)S(1)}, bf16[640,128]{1,0:T(8,128)(2,1)S(1)}, u32[]{:S(2)}, u32[]{:S(2)}) %collective-permute-start.9) | collective-permute-done | bytes 163872 | tf_op jit(solution)/shard_map/ppermute | solution.py:53
  37.5 0.0 collective-permute-done.8.refs_1_
  37.5 0.3 couple.1.scaled
  37.9 0.1 collective-permute-start.11
  37.9 0.0 copy-done.1
  38.0 1.3 %begin.1.begun = f32[4,2048,256]{2,1,0:T(8,128)S(1)} custom-call(bf16[2048,512]{1,0:T(8,128)(2,1)S(1)} %copy-done.1, bf16[8,256,128]{2,1,0:T(8,128)(2,1)S(1)} %couple.1.scaled), custom_call_target="tpu_custom_call" | custom-call | flops 1073741824 | bytes 2097152 | tf_op jit(solution)/shard_map/begin/pallas_call | solution.py:339
  39.2 0.6 %collective-permute-done.11.other = bf16[8,256,128]{2,1,0:T(8,128)(2,1)S(1)} collective-permute-done((bf16[8,256,128]{2,1,0:T(8,128)(2,1)S(1)}, bf16[8,256,128]{2,1,0:T(8,128)(2,1)S(1)}, u32[]{:S(2)}, u32[]{:S(2)}) %collective-permute-start.11) | collective-permute-done | bytes 524320 | tf_op jit(solution)/shard_map/ppermute | solution.py:35
  39.8 3.3 %finish.1 = bf16[2048,1024]{1,0:T(8,128)(2,1)} custom-call(bf16[2048,512]{1,0:T(8,128)(2,1)S(1)} %copy-done.1, f32[4,2048,256]{2,1,0:T(8,128)S(1)} %begin.1.begun, bf16[8,256,128]{2,1,0:T(8,128)(2,1)S(1)} %collective-permute-done.11.other), custom_call_target="tpu_custom_call" | custom-call | flops 1073741824 | bytes 6291456 | tf_op jit(solution)/shard_map/finish/pallas_call | solution.py:379
  (4 shorter events, 0.1 us)
Async XLA Ops:
  0.0 2.8 %copy-start = (bf16[2048,1024]{1,0:T(8,128)(2,1)S(1)}, bf16[2048,1024]{1,0:T(8,128)(2,1)}, u32[]{:S(2)}) copy-start(bf16[2048,1024]{1,0:T(8,128)(2,1)} %refs_1_.5) | copy-start | bytes 12582916
  0.0 3.6 %collective-permute-start.1 = (f32[256,256]{1,0:T(8,128)}, f32[256,256]{1,0:T(8,128)S(1)}, u32[]{:S(2)}, u32[]{:S(2)}) collective-permute-start(f32[256,256]{1,0:T(8,128)} %bitcast.1), channel_id=1, source_target_pairs={{0,1},{1,0},{2,3},{3,2},{4,5},{5,4},{6,7},{7,6},{8,9},{9,8},{10,11... | collective-permute-start | bytes 786440 | tf_op jit(solution)/shard_map/ppermute | solution.py:35
  3.6 2.0 %copy-start.5 = (s32[2]{0:T(128)S(1)}, s32[2]{0:T(128)}, u32[]{:S(2)}) copy-start(s32[2]{0:T(128)} %param.10) | copy-start | bytes 28
  3.6 2.1 %copy-start.2 = (f32[1,256,256]{2,1,0:T(8,128)S(1)}, f32[1,256,256]{2,1,0:T(8,128)}, u32[]{:S(2)}) copy-start(f32[1,256,256]{2,1,0:T(8,128)} %param.11) | copy-start | bytes 786436
  3.6 2.1 %collective-permute-start.2 = (bf16[2,256,128]{2,1,0:T(8,128)(2,1)S(1)}, bf16[2,256,128]{2,1,0:T(8,128)(2,1)S(1)}, u32[]{:S(2)}, u32[]{:S(2)}) collective-permute-start(bf16[2,256,128]{2,1,0:T(8,128)(2,1)S(1)} %get-tuple-element.20), channel_id=1, source_target_pairs={{0,1},{1,0},{2,3},{3,2},{4,5},{5,4},{6,7},{7,6},{8,9},{9,8},{10,11... | collective-permute-start | bytes 393224 | tf_op jit(solution)/shard_map/ppermute | solution.py:35
  5.5 3.3 %collective-permute-start = (bf16[4,256,128]{2,1,0:T(8,128)(2,1)S(1)}, bf16[4,256,128]{2,1,0:T(8,128)(2,1)S(1)}, u32[]{:S(2)}, u32[]{:S(2)}) collective-permute-start(bf16[4,256,128]{2,1,0:T(8,128)(2,1)S(1)} %get-tuple-element.16), channel_id=1, source_target_pairs={{0,1},{1,0},{2,3},{3,2},{4,5},{5,4},{6,7},{7,6},{8,9},{9,8},{10,11... | collective-permute-start | bytes 786440 | tf_op jit(solution)/shard_map/ppermute | solution.py:35
  5.8 6.3 %collective-permute-start.3 = (bf16[640,128]{1,0:T(8,128)(2,1)S(1)}, bf16[640,128]{1,0:T(8,128)(2,1)S(1)}, u32[]{:S(2)}, u32[]{:S(2)}) collective-permute-start(bf16[640,128]{1,0:T(8,128)(2,1)S(1)} %send.2), channel_id=1, source_target_pairs={{0,2},{1,5},{2,0},{3,7},{4,6},{5,1},{6,4},{7,3},{8,10},{9,13},{10,... | collective-permute-start | bytes 491528 | tf_op jit(solution)/shard_map/ppermute | solution.py:48
  8.9 7.7 %collective-permute-start.5 = (bf16[640,128]{1,0:T(8,128)(2,1)S(1)}, bf16[640,128]{1,0:T(8,128)(2,1)S(1)}, u32[]{:S(2)}, u32[]{:S(2)}) collective-permute-start(bf16[640,128]{1,0:T(8,128)(2,1)S(1)} %send.3), channel_id=1, source_target_pairs={{0,2},{1,5},{2,0},{3,7},{4,6},{5,1},{6,4},{7,3},{8,10},{9,13},{10,... | collective-permute-start | bytes 491528 | tf_op jit(solution)/shard_map/ppermute | solution.py:48
  12.2 18.8 %copy-start.3 = (s32[2,256]{1,0:T(2,128)S(1)}, s32[2,256]{1,0:T(2,128)}, u32[]{:S(2)}) copy-start(s32[2,256]{1,0:T(2,128)} %atom_of.1) | copy-start | bytes 6148
  12.2 18.8 %copy-start.4 = (s32[2,4]{1,0:T(2,128)S(1)}, s32[2,4]{1,0:T(2,128)}, u32[]{:S(2)}) copy-start(s32[2,4]{1,0:T(2,128)} %counts.1) | copy-start | bytes 100
  12.2 25.7 %copy-start.1 = (bf16[2048,512]{1,0:T(8,128)(2,1)S(1)}, bf16[2048,512]{1,0:T(8,128)(2,1)}, u32[]{:S(2)}) copy-start(bf16[2048,512]{1,0:T(8,128)(2,1)} %projectors.5) | copy-start | bytes 6291460
  12.2 5.4 %collective-permute-start.6 = (bf16[640,128]{1,0:T(8,128)(2,1)S(1)}, bf16[640,128]{1,0:T(8,128)(2,1)S(1)}, u32[]{:S(2)}, u32[]{:S(2)}) collective-permute-start(bf16[640,128]{1,0:T(8,128)(2,1)S(1)} %forward.1.after), channel_id=1, source_target_pairs={{0,4},{1,3},{2,6},{3,1},{4,0},{5,7},{6,2},{7,5},{8,12},{9,11},{10,... | collective-permute-start | bytes 491528 | tf_op jit(solution)/shard_map/ppermute | solution.py:53
  15.1 1.4 %collective-permute-start.4 = (bf16[2,256,128]{2,1,0:T(8,128)(2,1)S(1)}, bf16[2,256,128]{2,1,0:T(8,128)(2,1)S(1)}, u32[]{:S(2)}, u32[]{:S(2)}) collective-permute-start(bf16[2,256,128]{2,1,0:T(8,128)(2,1)S(1)} %get-tuple-element.22), channel_id=1, source_target_pairs={{0,1},{1,0},{2,3},{3,2},{4,5},{5,4},{6,7},{7,6},{8,9},{9,8},{10,11... | collective-permute-start | bytes 393224 | tf_op jit(solution)/shard_map/ppermute | solution.py:35
  17.7 9.6 %collective-permute-start.7 = (bf16[640,128]{1,0:T(8,128)(2,1)S(1)}, bf16[640,128]{1,0:T(8,128)(2,1)S(1)}, u32[]{:S(2)}, u32[]{:S(2)}) collective-permute-start(bf16[640,128]{1,0:T(8,128)(2,1)S(1)} %get-tuple-element.24), channel_id=1, source_target_pairs={{0,8},{1,9},{2,10},{3,11},{4,12},{5,13},{6,14},{7,15},{8,0},{9,1},... | collective-permute-start | bytes 491528 | tf_op jit(solution)/shard_map/ppermute | solution.py:35
  27.4 8.1 %collective-permute-start.10 = (bf16[640,128]{1,0:T(8,128)(2,1)S(1)}, bf16[640,128]{1,0:T(8,128)(2,1)S(1)}, u32[]{:S(2)}, u32[]{:S(2)}) collective-permute-start(bf16[640,128]{1,0:T(8,128)(2,1)S(1)} %add.1.refs_0_), channel_id=1, source_target_pairs={{0,6},{1,7},{2,4},{3,5},{4,2},{5,3},{6,0},{7,1},{8,14},{9,15},{10,... | collective-permute-start | bytes 491528 | tf_op jit(solution)/shard_map/ppermute | solution.py:35
  28.6 8.9 %collective-permute-start.9 = (bf16[640,128]{1,0:T(8,128)(2,1)S(1)}, bf16[640,128]{1,0:T(8,128)(2,1)S(1)}, u32[]{:S(2)}, u32[]{:S(2)}) collective-permute-start(bf16[640,128]{1,0:T(8,128)(2,1)S(1)} %add.1.refs_0_), channel_id=1, source_target_pairs={{0,4},{1,3},{2,6},{3,1},{4,0},{5,7},{6,2},{7,5},{8,12},{9,11},{10,... | collective-permute-start | bytes 491528 | tf_op jit(solution)/shard_map/ppermute | solution.py:53
  30.5 7.1 %collective-permute-start.8 = (bf16[640,128]{1,0:T(8,128)(2,1)S(1)}, bf16[640,128]{1,0:T(8,128)(2,1)S(1)}, u32[]{:S(2)}, u32[]{:S(2)}) collective-permute-start(bf16[640,128]{1,0:T(8,128)(2,1)S(1)} %add.1.refs_0_), channel_id=1, source_target_pairs={{0,2},{1,5},{2,0},{3,7},{4,6},{5,1},{6,4},{7,3},{8,10},{9,13},{10,... | collective-permute-start | bytes 491528 | tf_op jit(solution)/shard_map/ppermute | solution.py:48
  37.9 2.0 %collective-permute-start.11 = (bf16[8,256,128]{2,1,0:T(8,128)(2,1)S(1)}, bf16[8,256,128]{2,1,0:T(8,128)(2,1)S(1)}, u32[]{:S(2)}, u32[]{:S(2)}) collective-permute-start(bf16[8,256,128]{2,1,0:T(8,128)(2,1)S(1)} %couple.1.scaled), channel_id=1, source_target_pairs={{0,1},{1,0},{2,3},{3,2},{4,5},{5,4},{6,7},{7,6},{8,9},{9,8},{10,11... | collective-permute-start | bytes 1572872 | tf_op jit(solution)/shard_map/ppermute | solution.py:35

commit v17 on v14

--- a/solution.py
+++ b/solution.py
@@ -14,7 +14,6 @@
 ROW_BLOCK = 512
 ROW_BLOCKS = (512, 512, 512, 256, 256)
 COPY_ROWS = 128
-GATHERED = (0, 1, 2, 3)
 PARAMS = pltpu.CompilerParams(vmem_limit_bytes=40 * 1024 * 1024)
 VMEM = pl.BlockSpec(memory_space=pltpu.VMEM)
 SMEM = pl.BlockSpec(memory_space=pltpu.SMEM)
@@ -65,6 +64,14 @@
         lanes = slice(entry * LANES, (entry + 1) * LANES)
         ours[2 * at + entry] = sums[:PCAP, lanes]
         theirs[2 * at + entry] = sums[PCAP:, lanes].astype(theirs.dtype)
+
+
+def exchange_square(x):
+    count = lax.axis_size("pw")
+    groups = [
+        list(range(base + core, base + 2 * SQUARE, 2)) for base in range(0, count, 2 * SQUARE) for core in range(2)
+    ]
+    return lax.all_to_all(x, "pw", 0, 0, axis_index_groups=groups)
 
 
 def load_kernel(projectors, flipped, slots, sems):
@@ -258,6 +265,23 @@
     )(left, right)
 
 
+def add_copies_kernel(left, right, out):
+    total = (left[...] + right[...].astype(jnp.float32)).astype(out.dtype)
+    for at in range(out.shape[0]):
+        out[at] = total
+
+
+def add_copies(left, right):
+    return pl.pallas_call(
+        add_copies_kernel,
+        in_specs=[VMEM, VMEM],
+        out_specs=VMEM,
+        out_shape=jax.ShapeDtypeStruct((SQUARE,) + left.shape, jnp.bfloat16),
+        compiler_params=PARAMS,
+        name="add_copies",
+    )(left, right)
+
+
 def mask_kernel(counts, atom_of, after, out):
     del after
     core = place()[0]
@@ -281,38 +305,36 @@
     )(counts, atom_of, after)
 
 
-def couple_kernel(allowed, *refs):
-    *messages, out, coupling = refs
+def couple_kernel(allowed, messages, out, coupling):
+    corner = place()[1] & 3
     width = out.shape[2]
     entries = out.shape[0] // SQUARE
-    corner = place()[1] & 3
-    for part, message in zip(GATHERED, messages):
-        start = pl.multiple_of((corner ^ part) * QUARTER, QUARTER)
+    for at in range(SQUARE):
         for cut in range(PCAP // width):
+            rows = slice(at * QUARTER, (at + 1) * QUARTER)
             lanes = slice(cut * width, (cut + 1) * width)
             first = entries * PCAP + cut * QUARTER
-            coupling[pl.ds(start, QUARTER), lanes] = (
-                message[first : first + QUARTER] * allowed[pl.ds(start, QUARTER), lanes]
-            )
-    for part, message in zip(GATHERED, messages):
-        wide = jnp.concatenate([message[e * PCAP : (e + 1) * PCAP] for e in range(entries)], axis=1)
+            coupling[rows, lanes] = messages[at, first : first + QUARTER] * allowed[rows, lanes]
+    for at in range(SQUARE):
+        wide = jnp.concatenate([messages[at, e * PCAP : (e + 1) * PCAP] for e in range(entries)], axis=1)
         scaled = jnp.dot(coupling[...], wide, preferred_element_type=jnp.float32).astype(out.dtype)
+        part = corner ^ at
         for entry in range(entries):
             out[part * entries + entry] = scaled[:, entry * width : (entry + 1) * width]
 
 
 def couple(allowed, messages):
-    rows, width = messages[0].shape
+    _, rows, width = messages.shape
     entries = (rows - QUARTER * PCAP // width) // PCAP
     return pl.pallas_call(
         couple_kernel,
-        in_specs=[VMEM] * (1 + SQUARE),
+        in_specs=[VMEM, VMEM],
         out_specs=VMEM,
         out_shape=jax.ShapeDtypeStruct((SQUARE * entries, PCAP, width), jnp.bfloat16),
         scratch_shapes=[pltpu.VMEM((PCAP, PCAP), jnp.bfloat16)],
         compiler_params=PARAMS,
         name="couple",
-    )(allowed, *messages)
+    )(allowed, messages)
 
 
 def group_slots(group):
@@ -435,16 +457,17 @@
     allowed = mask(counts, atom_of, message)
 
     total, message = fold(low_ours, low_theirs, quarters, [got_first, got_second])
-    mine = add(total, swap_chips(message, SQUARE))
+    got = swap_chips(message, SQUARE)
     distance = 2 * SQUARE
     while distance < chips:
-        body = mine[: entries * PCAP].reshape(entries, PCAP, width)
+        total = add(total, got).astype(jnp.float32)
+        body = total[: entries * PCAP].reshape(entries, PCAP, width)
         order = [entry ^ (distance // SQUARE) for entry in range(entries)]
-        message = jnp.concatenate([body[jnp.array(order)].reshape(-1, width), mine[entries * PCAP :]])
-        mine = add(mine.astype(jnp.float32), swap_chips(message, distance))
+        message = jnp.concatenate([body[jnp.array(order)].reshape(-1, width), total[entries * PCAP :]])
+        got = swap_chips(message.astype(jnp.bfloat16), distance)
         distance *= 2
 
-    scaled = couple(allowed, [swap_chips(mine, part) if part else mine for part in GATHERED])
+    scaled = couple(allowed, exchange_square(add_copies(total, got)))
     other = swap_cores(scaled)
     if not fast:
         return apply_plain(projectors, scaled, other)

time: 43.3 us -> 46.9 us (1.083)
  waiting for transfers between devices: 17.7 us -> 20.5 us
  Pallas kernels: 10.8 us -> 11.7 us
    all_to_all x0 -> x1, waiting for transfers between devices: none -> 8.67 us  [exchange_square(): return lax.all_to_all(x, 'pw', 0, 0, axis_index_groups=groups)]
    ppermute x9 -> x6, waiting for transfers between devices: 14.4 us -> 8.51 us  [swap(): return lax.ppermute(x, 'pw', [(i, i ^ distance) for i in range(count)])]
    ppermute x9 -> x6, starting transfers between devices: 7.89 us -> 4.33 us  [swap(): return lax.ppermute(x, 'pw', [(i, i ^ distance) for i in range(count)])]
    all_to_all x0 -> x1, starting transfers between devices: none -> 3.48 us  [exchange_square(): return lax.all_to_all(x, 'pw', 0, 0, axis_index_groups=groups)]
    pallas_call x2, Pallas kernels: 0.34 us -> 1.21 us  [the longest x1 0.88 us: add_copies(): pl.pallas_call(add_copies_kernel, in_specs=[VMEM, VMEM], out_specs=VMEM,...]
  transfers between devices with their start and end apart: 12 -> 10, of which waited for: 7 -> 6; matrix products, arithmetic and copies ran while one was open for 0% -> 0% of each run, Pallas kernels for 16% -> 15%
where the time goes in v17:
time: 46.9 us; the launch traced here: 46.7 us
  waiting for transfers between devices  20.5 us (44%)
  starting transfers between devices  14 us (30%)
  Pallas kernels  11.7 us (25%)
    all_to_all x1, waiting for transfers between devices, exchange_square(): return lax.all_to_all(x, 'pw', 0, 0, axis_index_groups=groups)  8.67 us
    ppermute x6, waiting for transfers between devices, swap(): return lax.ppermute(x, 'pw', [(i, i ^ distance) for i in range(count)])  8.51 us
    ppermute x6, starting transfers between devices, swap(): return lax.ppermute(x, 'pw', [(i, i ^ distance) for i in range(count)])  4.33 us
    ppermute x2, starting transfers between devices, swap_first(): return lax.ppermute(x, 'pw', [(i, i ^ (2, 4)[i % 2]) for i in range(count)])  4.03 us
    all_to_all x1, starting transfers between devices, exchange_square(): return lax.all_to_all(x, 'pw', 0, 0, axis_index_groups=groups)  3.48 us
    pallas_call x1, Pallas kernels, finish(): pl.pallas_call(finish_kernel, in_specs=[VMEM] * 3, out_specs=HBM, out_sha...  3.3 us
    pallas_call x3, Pallas kernels, project(): pl.pallas_call(kernel, in_specs=[VMEM, VMEM], out_specs=[VMEM, VMEM], out...  2.91 us
    ppermute x2, waiting for transfers between devices, swap_first(): return lax.ppermute(x, 'pw', [(i, i ^ (2, 4)[i % 2]) for i in range(count)])  2.27 us
  transfers between devices with their start and end apart: 10, of which 6 were waited for; matrix products, arithmetic and copies ran while one was open for 0% of the time, Pallas kernels for 15%

profile of v17, /device:TPU:0, one launch (start us, length us, event | category | flops | bytes accessed | tf_op | source)
XLA Modules:
  0.0 46.7 jit_solution(12173271806987061409)
XLA Ops:
  0.0 0.0 copy-start
  0.0 0.5 collective-permute-start.1
  0.5 2.1 %load.1.refs_0_ = bf16[512,2048]{1,0:T(8,128)(2,1)S(1)} custom-call(bf16[2048,512]{1,0:T(8,128)(2,1)} %projectors.5), custom_call_target="tpu_custom_call" | custom-call | tf_op jit(solution)/shard_map/load/pallas_call | solution.py:96
  2.6 0.3 copy-done
  2.8 0.8 %project.4 = (bf16[2,256,128]{2,1,0:T(8,128)(2,1)S(1)}, f32[2,256,128]{2,1,0:T(8,128)S(1)}) custom-call(bf16[512,2048]{1,0:T(8,128)(2,1)S(1)} %load.1.refs_0_, bf16[2048,1024]{1,0:T(8,128)(2,1)S(1)} %copy-done), custom_call_target="tpu_custom_call" | custom-call | flops 536870912 | bytes 2097152 | tf_op jit(solution)/shard_map/project/pallas_call | solution.py:121
  3.6 0.0 copy-start.5
  3.6 0.0 copy-start.2
  3.6 0.0 collective-permute-done.1.sibling
  3.6 0.5 %collective-permute-start.2 = (bf16[2,256,128]{2,1,0:T(8,128)(2,1)S(1)}, bf16[2,256,128]{2,1,0:T(8,128)(2,1)S(1)}, u32[]{:S(2)}, u32[]{:S(2)}) collective-permute-start(bf16[2,256,128]{2,1,0:T(8,128)(2,1)S(1)} %get-tuple-element.20), channel_id=1, source_target_pairs={{0,1},{1,0},{2,3},{3,2},{4,5},{5,4},{6,7},{7,6},{8,9},{9,8},{10,11... | collective-permute-start | bytes 393224 | tf_op jit(solution)/shard_map/ppermute | solution.py:35
  4.2 1.3 %project.3 = (bf16[4,256,128]{2,1,0:T(8,128)(2,1)S(1)}, f32[4,256,128]{2,1,0:T(8,128)S(1)}) custom-call(bf16[512,2048]{1,0:T(8,128)(2,1)S(1)} %load.1.refs_0_, bf16[2048,1024]{1,0:T(8,128)(2,1)S(1)} %copy-done), custom_call_target="tpu_custom_call" | custom-call | flops 1073741824 | bytes 2097152 | tf_op jit(solution)/shard_map/project/pallas_call | solution.py:121
  5.5 0.1 collective-permute-start
  5.6 0.0 copy-done.5
  5.6 0.1 broadcast_in_dim.2.owners
  5.7 0.0 copy-done.2
  5.7 0.0 collective-permute-done.2.refs_1_
  5.8 3.0 %collective-permute-start.3 = (bf16[640,128]{1,0:T(8,128)(2,1)S(1)}, bf16[640,128]{1,0:T(8,128)(2,1)S(1)}, u32[]{:S(2)}, u32[]{:S(2)}) collective-permute-start(bf16[640,128]{1,0:T(8,128)(2,1)S(1)} %send.2), channel_id=1, source_target_pairs={{0,2},{1,5},{2,0},{3,7},{4,6},{5,1},{6,4},{7,3},{8,10},{9,13},{10,... | collective-permute-start | bytes 491528 | tf_op jit(solution)/shard_map/ppermute | solution.py:48
  8.8 0.0 collective-permute-done.theirs.refs_1_
  8.9 1.0 %collective-permute-start.5 = (bf16[640,128]{1,0:T(8,128)(2,1)S(1)}, bf16[640,128]{1,0:T(8,128)(2,1)S(1)}, u32[]{:S(2)}, u32[]{:S(2)}) collective-permute-start(bf16[640,128]{1,0:T(8,128)(2,1)S(1)} %send.3), channel_id=1, source_target_pairs={{0,2},{1,5},{2,0},{3,7},{4,6},{5,1},{6,4},{7,3},{8,10},{9,13},{10,... | collective-permute-start | bytes 491528 | tf_op jit(solution)/shard_map/ppermute | solution.py:48
  9.9 2.3 %collective-permute-done.3.got = bf16[640,128]{1,0:T(8,128)(2,1)S(1)} collective-permute-done((bf16[640,128]{1,0:T(8,128)(2,1)S(1)}, bf16[640,128]{1,0:T(8,128)(2,1)S(1)}, u32[]{:S(2)}, u32[]{:S(2)}) %collective-permute-start.3) | collective-permute-done | bytes 163872 | tf_op jit(solution)/shard_map/ppermute | solution.py:48
  12.1 0.1 forward.1.after
  12.2 0.0 copy-start.3
  12.2 0.0 copy-start.4
  12.2 0.0 copy-start.1
  12.2 2.1 %collective-permute-start.6 = (bf16[640,128]{1,0:T(8,128)(2,1)S(1)}, bf16[640,128]{1,0:T(8,128)(2,1)S(1)}, u32[]{:S(2)}, u32[]{:S(2)}) collective-permute-start(bf16[640,128]{1,0:T(8,128)(2,1)S(1)} %forward.1.after), channel_id=1, source_target_pairs={{0,4},{1,3},{2,6},{3,1},{4,0},{5,7},{6,2},{7,5},{8,12},{9,11},{10,... | collective-permute-start | bytes 491528 | tf_op jit(solution)/shard_map/ppermute | solution.py:53
  14.3 0.8 %project.5 = (bf16[2,256,128]{2,1,0:T(8,128)(2,1)S(1)}, f32[2,256,128]{2,1,0:T(8,128)S(1)}) custom-call(bf16[512,2048]{1,0:T(8,128)(2,1)S(1)} %load.1.refs_0_, bf16[2048,1024]{1,0:T(8,128)(2,1)S(1)} %copy-done), custom_call_target="tpu_custom_call" | custom-call | flops 536870912 | bytes 2097152 | tf_op jit(solution)/shard_map/project/pallas_call | solution.py:121
  15.1 0.1 collective-permute-start.4
  15.2 1.3 %collective-permute-done.4.theirs = bf16[2,256,128]{2,1,0:T(8,128)(2,1)S(1)} collective-permute-done((bf16[2,256,128]{2,1,0:T(8,128)(2,1)S(1)}, bf16[2,256,128]{2,1,0:T(8,128)(2,1)S(1)}, u32[]{:S(2)}, u32[]{:S(2)}) %collective-permute-start.4) | collective-permute-done | bytes 131104 | tf_op jit(solution)/shard_map/ppermute | solution.py:35
  16.6 0.0 collective-permute-done.5.refs_0_
  16.6 1.1 %collective-permute-done.6.refs_1_ = bf16[640,128]{1,0:T(8,128)(2,1)S(1)} collective-permute-done((bf16[640,128]{1,0:T(8,128)(2,1)S(1)}, bf16[640,128]{1,0:T(8,128)(2,1)S(1)}, u32[]{:S(2)}, u32[]{:S(2)}) %collective-permute-start.6) | collective-permute-done | bytes 163872 | tf_op jit(solution)/shard_map/ppermute | solution.py:53
  17.6 0.1 fold.1
  17.7 3.1 %collective-permute-start.7 = (bf16[640,128]{1,0:T(8,128)(2,1)S(1)}, bf16[640,128]{1,0:T(8,128)(2,1)S(1)}, u32[]{:S(2)}, u32[]{:S(2)}) collective-permute-start(bf16[640,128]{1,0:T(8,128)(2,1)S(1)} %get-tuple-element.24), channel_id=1, source_target_pairs={{0,8},{1,9},{2,10},{3,11},{4,12},{5,13},{6,14},{7,15},{8,0},{9,1},... | collective-permute-start | bytes 491528 | tf_op jit(solution)/shard_map/ppermute | solution.py:35
  20.8 6.5 %collective-permute-done.7.right = bf16[640,128]{1,0:T(8,128)(2,1)S(1)} collective-permute-done((bf16[640,128]{1,0:T(8,128)(2,1)S(1)}, bf16[640,128]{1,0:T(8,128)(2,1)S(1)}, u32[]{:S(2)}, u32[]{:S(2)}) %collective-permute-start.7) | collective-permute-done | bytes 163872 | tf_op jit(solution)/shard_map/ppermute | solution.py:35
  27.4 0.9 %add_copies.1 = bf16[4,640,128]{2,1,0:T(8,128)(2,1)} custom-call(f32[640,128]{1,0:T(8,128)S(1)} %get-tuple-element.23.left, bf16[640,128]{1,0:T(8,128)(2,1)S(1)} %collective-permute-done.7.right), custom_call_target="tpu_custom_call" | custom-call | tf_op jit(solution)/shard_map/add_copies/pallas_call | solution.py:275
  28.2 3.5 %all-to-all-start = ((bf16[4,640,128]{2,1,0:T(8,128)(2,1)}), bf16[4,640,128]{2,1,0:T(8,128)(2,1)S(1)}, u32[]{:S(2)}, u32[]{:S(2)}) async-start(bf16[4,640,128]{2,1,0:T(8,128)(2,1)} %add_copies.1), calls=%async_computation | async-start | bytes 1310720 | tf_op jit(solution)/shard_map/all_to_all | solution.py:74
  31.7 0.0 copy-done.3
  31.7 0.0 copy-done.4
  31.8 0.7 %mask.1.allowed = bf16[256,256]{1,0:T(8,128)(2,1)S(1)} custom-call(s32[2,4]{1,0:T(2,128)S(1)} %copy-done.4, s32[2,256]{1,0:T(2,128)S(1)} %copy-done.3, bf16[640,128]{1,0:T(8,128)(2,1)S(1)} %forward.1.after), custom_call_target="tpu_custom_call" | custom-call | tf_op jit(solution)/shard_map/mask/pallas_call | solution.py:298
  32.4 8.7 %all-to-all-done.messages = bf16[4,640,128]{2,1,0:T(8,128)(2,1)S(1)} async-done(((bf16[4,640,128]{2,1,0:T(8,128)(2,1)}), bf16[4,640,128]{2,1,0:T(8,128)(2,1)S(1)}, u32[]{:S(2)}, u32[]{:S(2)}) %all-to-all-start) | async-done | bytes 655392 | tf_op jit(solution)/shard_map/all_to_all | solution.py:74
  41.1 0.3 couple.1.scaled
  41.4 0.1 collective-permute-start.8
  41.5 0.0 copy-done.1
  41.5 1.3 %begin.1.begun = f32[4,2048,256]{2,1,0:T(8,128)S(1)} custom-call(bf16[2048,512]{1,0:T(8,128)(2,1)S(1)} %copy-done.1, bf16[8,256,128]{2,1,0:T(8,128)(2,1)S(1)} %couple.1.scaled), custom_call_target="tpu_custom_call" | custom-call | flops 1073741824 | bytes 2097152 | tf_op jit(solution)/shard_map/begin/pallas_call | solution.py:360
  42.8 0.6 %collective-permute-done.8.other = bf16[8,256,128]{2,1,0:T(8,128)(2,1)S(1)} collective-permute-done((bf16[8,256,128]{2,1,0:T(8,128)(2,1)S(1)}, bf16[8,256,128]{2,1,0:T(8,128)(2,1)S(1)}, u32[]{:S(2)}, u32[]{:S(2)}) %collective-permute-start.8) | collective-permute-done | bytes 524320 | tf_op jit(solution)/shard_map/ppermute | solution.py:35
  43.4 3.3 %finish.1 = bf16[2048,1024]{1,0:T(8,128)(2,1)} custom-call(bf16[2048,512]{1,0:T(8,128)(2,1)S(1)} %copy-done.1, f32[4,2048,256]{2,1,0:T(8,128)S(1)} %begin.1.begun, bf16[8,256,128]{2,1,0:T(8,128)(2,1)S(1)} %collective-permute-done.8.other), custom_call_target="tpu_custom_call" | custom-call | flops 1073741824 | bytes 6291456 | tf_op jit(solution)/shard_map/finish/pallas_call | solution.py:400
  (3 shorter events, 0.1 us)
Async XLA Ops:
  0.0 2.8 %copy-start = (bf16[2048,1024]{1,0:T(8,128)(2,1)S(1)}, bf16[2048,1024]{1,0:T(8,128)(2,1)}, u32[]{:S(2)}) copy-start(bf16[2048,1024]{1,0:T(8,128)(2,1)} %refs_1_.5) | copy-start | bytes 12582916
  0.0 3.6 %collective-permute-start.1 = (f32[256,256]{1,0:T(8,128)}, f32[256,256]{1,0:T(8,128)S(1)}, u32[]{:S(2)}, u32[]{:S(2)}) collective-permute-start(f32[256,256]{1,0:T(8,128)} %bitcast.1), channel_id=1, source_target_pairs={{0,1},{1,0},{2,3},{3,2},{4,5},{5,4},{6,7},{7,6},{8,9},{9,8},{10,11... | collective-permute-start | bytes 786440 | tf_op jit(solution)/shard_map/ppermute | solution.py:35
  3.6 2.0 %copy-start.5 = (s32[2]{0:T(128)S(1)}, s32[2]{0:T(128)}, u32[]{:S(2)}) copy-start(s32[2]{0:T(128)} %param.10) | copy-start | bytes 28
  3.6 2.1 %copy-start.2 = (f32[1,256,256]{2,1,0:T(8,128)S(1)}, f32[1,256,256]{2,1,0:T(8,128)}, u32[]{:S(2)}) copy-start(f32[1,256,256]{2,1,0:T(8,128)} %param.11) | copy-start | bytes 786436
  3.6 2.1 %collective-permute-start.2 = (bf16[2,256,128]{2,1,0:T(8,128)(2,1)S(1)}, bf16[2,256,128]{2,1,0:T(8,128)(2,1)S(1)}, u32[]{:S(2)}, u32[]{:S(2)}) collective-permute-start(bf16[2,256,128]{2,1,0:T(8,128)(2,1)S(1)} %get-tuple-element.20), channel_id=1, source_target_pairs={{0,1},{1,0},{2,3},{3,2},{4,5},{5,4},{6,7},{7,6},{8,9},{9,8},{10,11... | collective-permute-start | bytes 393224 | tf_op jit(solution)/shard_map/ppermute | solution.py:35
  5.5 3.3 %collective-permute-start = (bf16[4,256,128]{2,1,0:T(8,128)(2,1)S(1)}, bf16[4,256,128]{2,1,0:T(8,128)(2,1)S(1)}, u32[]{:S(2)}, u32[]{:S(2)}) collective-permute-start(bf16[4,256,128]{2,1,0:T(8,128)(2,1)S(1)} %get-tuple-element.16), channel_id=1, source_target_pairs={{0,1},{1,0},{2,3},{3,2},{4,5},{5,4},{6,7},{7,6},{8,9},{9,8},{10,11... | collective-permute-start | bytes 786440 | tf_op jit(solution)/shard_map/ppermute | solution.py:35
  5.8 6.3 %collective-permute-start.3 = (bf16[640,128]{1,0:T(8,128)(2,1)S(1)}, bf16[640,128]{1,0:T(8,128)(2,1)S(1)}, u32[]{:S(2)}, u32[]{:S(2)}) collective-permute-start(bf16[640,128]{1,0:T(8,128)(2,1)S(1)} %send.2), channel_id=1, source_target_pairs={{0,2},{1,5},{2,0},{3,7},{4,6},{5,1},{6,4},{7,3},{8,10},{9,13},{10,... | collective-permute-start | bytes 491528 | tf_op jit(solution)/shard_map/ppermute | solution.py:48
  8.9 7.7 %collective-permute-start.5 = (bf16[640,128]{1,0:T(8,128)(2,1)S(1)}, bf16[640,128]{1,0:T(8,128)(2,1)S(1)}, u32[]{:S(2)}, u32[]{:S(2)}) collective-permute-start(bf16[640,128]{1,0:T(8,128)(2,1)S(1)} %send.3), channel_id=1, source_target_pairs={{0,2},{1,5},{2,0},{3,7},{4,6},{5,1},{6,4},{7,3},{8,10},{9,13},{10,... | collective-permute-start | bytes 491528 | tf_op jit(solution)/shard_map/ppermute | solution.py:48
  12.2 19.6 %copy-start.3 = (s32[2,256]{1,0:T(2,128)S(1)}, s32[2,256]{1,0:T(2,128)}, u32[]{:S(2)}) copy-start(s32[2,256]{1,0:T(2,128)} %atom_of.1) | copy-start | bytes 6148
  12.2 19.6 %copy-start.4 = (s32[2,4]{1,0:T(2,128)S(1)}, s32[2,4]{1,0:T(2,128)}, u32[]{:S(2)}) copy-start(s32[2,4]{1,0:T(2,128)} %counts.1) | copy-start | bytes 100
  12.2 29.3 %copy-start.1 = (bf16[2048,512]{1,0:T(8,128)(2,1)S(1)}, bf16[2048,512]{1,0:T(8,128)(2,1)}, u32[]{:S(2)}) copy-start(bf16[2048,512]{1,0:T(8,128)(2,1)} %projectors.5) | copy-start | bytes 6291460
  12.2 5.4 %collective-permute-start.6 = (bf16[640,128]{1,0:T(8,128)(2,1)S(1)}, bf16[640,128]{1,0:T(8,128)(2,1)S(1)}, u32[]{:S(2)}, u32[]{:S(2)}) collective-permute-start(bf16[640,128]{1,0:T(8,128)(2,1)S(1)} %forward.1.after), channel_id=1, source_target_pairs={{0,4},{1,3},{2,6},{3,1},{4,0},{5,7},{6,2},{7,5},{8,12},{9,11},{10,... | collective-permute-start | bytes 491528 | tf_op jit(solution)/shard_map/ppermute | solution.py:53
  15.1 1.4 %collective-permute-start.4 = (bf16[2,256,128]{2,1,0:T(8,128)(2,1)S(1)}, bf16[2,256,128]{2,1,0:T(8,128)(2,1)S(1)}, u32[]{:S(2)}, u32[]{:S(2)}) collective-permute-start(bf16[2,256,128]{2,1,0:T(8,128)(2,1)S(1)} %get-tuple-element.22), channel_id=1, source_target_pairs={{0,1},{1,0},{2,3},{3,2},{4,5},{5,4},{6,7},{7,6},{8,9},{9,8},{10,11... | collective-permute-start | bytes 393224 | tf_op jit(solution)/shard_map/ppermute | solution.py:35
  17.7 9.6 %collective-permute-start.7 = (bf16[640,128]{1,0:T(8,128)(2,1)S(1)}, bf16[640,128]{1,0:T(8,128)(2,1)S(1)}, u32[]{:S(2)}, u32[]{:S(2)}) collective-permute-start(bf16[640,128]{1,0:T(8,128)(2,1)S(1)} %get-tuple-element.24), channel_id=1, source_target_pairs={{0,8},{1,9},{2,10},{3,11},{4,12},{5,13},{6,14},{7,15},{8,0},{9,1},... | collective-permute-start | bytes 491528 | tf_op jit(solution)/shard_map/ppermute | solution.py:35
  28.2 12.9 %all-to-all-start = ((bf16[4,640,128]{2,1,0:T(8,128)(2,1)}), bf16[4,640,128]{2,1,0:T(8,128)(2,1)S(1)}, u32[]{:S(2)}, u32[]{:S(2)}) async-start(bf16[4,640,128]{2,1,0:T(8,128)(2,1)} %add_copies.1), calls=%async_computation | async-start | bytes 1310720 | tf_op jit(solution)/shard_map/all_to_all | solution.py:74
  41.4 2.0 %collective-permute-start.8 = (bf16[8,256,128]{2,1,0:T(8,128)(2,1)S(1)}, bf16[8,256,128]{2,1,0:T(8,128)(2,1)S(1)}, u32[]{:S(2)}, u32[]{:S(2)}) collective-permute-start(bf16[8,256,128]{2,1,0:T(8,128)(2,1)S(1)} %couple.1.scaled), channel_id=1, source_target_pairs={{0,1},{1,0},{2,3},{3,2},{4,5},{5,4},{6,7},{7,6},{8,9},{9,8},{10,11... | collective-permute-start | bytes 1572872 | tf_op jit(solution)/shard_map/ppermute | solution.py:35

commit v18 on v16

--- a/solution.py
+++ b/solution.py
@@ -45,12 +45,12 @@
 
 def swap_first(x):
     count = lax.axis_size("pw")
-    return lax.ppermute(x, "pw", [(i, i ^ (2, 4)[i % 2]) for i in range(count)])
+    return lax.ppermute(x, "pw", [(i, i ^ (4, 2)[i % 2]) for i in range(count)])
 
 
 def swap_second(x):
     count = lax.axis_size("pw")
-    return lax.ppermute(x, "pw", [(i, i ^ (4, 2)[i % 2]) for i in range(count)])
+    return lax.ppermute(x, "pw", [(i, i ^ (2, 4)[i % 2]) for i in range(count)])
 
 
 def pair_at(columns, rows, part):
@@ -166,7 +166,7 @@
 def send_kernel(first, second, ours, theirs, quarters, message):
     entries = ours.shape[0] // (1 if first == second else 2)
     core = place()[0]
-    start, part = (0, first) if first == second else (core * entries, 1 + core)
+    start, part = (0, first) if first == second else ((1 - core) * entries, 2 - core)
     for entry in range(entries):
         total = ours[start + entry] + theirs[start + entry].astype(jnp.float32)
         message[entry * PCAP : (entry + 1) * PCAP] = total.astype(message.dtype)
@@ -193,12 +193,12 @@
 def forward_kernel(ours, theirs, quarters, got, message):
     core = place()[0]
     entries = ours.shape[0] // 2
-    start = (1 - core) * entries
+    start = core * entries
     for entry in range(entries):
         rows = slice(entry * PCAP, (entry + 1) * PCAP)
         total = ours[start + entry] + theirs[start + entry].astype(jnp.float32)
         message[rows] = (total + got[rows].astype(jnp.float32)).astype(message.dtype)
-    message[entries * PCAP :] = quarters[2 - core] + got[entries * PCAP :]
+    message[entries * PCAP :] = quarters[1 + core] + got[entries * PCAP :]
 
 
 def forward(ours, theirs, quarters, got):
@@ -286,7 +286,7 @@
     entries = out.shape[0] // SQUARE
     core, chip = place()
     corner = chip & 3
-    parts = (0, 1 + core, 2 - core, 3)
+    parts = (0, 2 - core, 1 + core, 3)
     for part, message in zip(parts, messages):
         start = pl.multiple_of((corner ^ part) * QUARTER, QUARTER)
         for cut in range(PCAP // width):

time: 43.3 us -> 42.6 us (0.984)
  waiting for transfers between devices: 17.8 us -> 17.2 us
  transfers between devices with their start and end apart: 12 -> 12, of which waited for: 7 -> 7; matrix products, arithmetic and copies ran while one was open for 0% -> 0% of each run, Pallas kernels for 16% -> 17%
where the time goes in v18:
time: 42.6 us; the launch traced here: 42.5 us
  waiting for transfers between devices  17.2 us (40%)
  starting transfers between devices  14 us (33%)
  Pallas kernels  10.8 us (25%)
    ppermute x7, waiting for transfers between devices, swap(): return lax.ppermute(x, 'pw', [(i, i ^ distance) for i in range(count)])  12 us
    ppermute x7, starting transfers between devices, swap(): return lax.ppermute(x, 'pw', [(i, i ^ distance) for i in range(count)])  5.48 us
    ppermute x3, starting transfers between devices, swap_first(): return lax.ppermute(x, 'pw', [(i, i ^ (4, 2)[i % 2]) for i in range(count)])  5.42 us
    pallas_call x1, Pallas kernels, finish(): pl.pallas_call(finish_kernel, in_specs=[VMEM] * 3, out_specs=HBM, out_sha...  3.3 us
    ppermute x2, starting transfers between devices, swap_second(): return lax.ppermute(x, 'pw', [(i, i ^ (2, 4)[i % 2]) for i in range(count)])  3.09 us
    pallas_call x3, Pallas kernels, project(): pl.pallas_call(kernel, in_specs=[VMEM, VMEM], out_specs=[VMEM, VMEM], out...  2.91 us
    ppermute x2, waiting for transfers between devices, swap_second(): return lax.ppermute(x, 'pw', [(i, i ^ (2, 4)[i % 2]) for i in range(count)])  2.86 us
    ppermute x3, waiting for transfers between devices, swap_first(): return lax.ppermute(x, 'pw', [(i, i ^ (4, 2)[i % 2]) for i in range(count)])  2.28 us
  transfers between devices with their start and end apart: 12, of which 7 were waited for; matrix products, arithmetic and copies ran while one was open for 0% of the time, Pallas kernels for 17%

profile of v18, /device:TPU:0, one launch (start us, length us, event | category | flops | bytes accessed | tf_op | source)
XLA Modules:
  0.0 42.5 jit_solution(16390899995148701602)
XLA Ops:
  0.0 0.0 copy-start
  0.0 0.5 %collective-permute-start.1 = (f32[256,256]{1,0:T(8,128)}, f32[256,256]{1,0:T(8,128)S(1)}, u32[]{:S(2)}, u32[]{:S(2)}) collective-permute-start(f32[256,256]{1,0:T(8,128)} %bitcast.1), channel_id=1, source_target_pairs={{0,1},{1,0},{2,3},{3,2},{4,5},{5,4},{6,7},{7,6},{8,9},{9,8},{10,11... | collective-permute-start | bytes 786440 | tf_op jit(solution)/shard_map/ppermute | solution.py:35
  0.5 2.1 %load.1.refs_0_ = bf16[512,2048]{1,0:T(8,128)(2,1)S(1)} custom-call(bf16[2048,512]{1,0:T(8,128)(2,1)} %projectors.5), custom_call_target="tpu_custom_call" | custom-call | tf_op jit(solution)/shard_map/load/pallas_call | solution.py:88
  2.6 0.3 copy-done
  2.8 0.8 %project.4 = (bf16[2,256,128]{2,1,0:T(8,128)(2,1)S(1)}, f32[2,256,128]{2,1,0:T(8,128)S(1)}) custom-call(bf16[512,2048]{1,0:T(8,128)(2,1)S(1)} %load.1.refs_0_, bf16[2048,1024]{1,0:T(8,128)(2,1)S(1)} %copy-done), custom_call_target="tpu_custom_call" | custom-call | flops 536870912 | bytes 2097152 | tf_op jit(solution)/shard_map/project/pallas_call | solution.py:113
  3.6 0.0 copy-start.5
  3.6 0.0 copy-start.2
  3.6 0.0 collective-permute-done.1.sibling
  3.6 0.5 %collective-permute-start.2 = (bf16[2,256,128]{2,1,0:T(8,128)(2,1)S(1)}, bf16[2,256,128]{2,1,0:T(8,128)(2,1)S(1)}, u32[]{:S(2)}, u32[]{:S(2)}) collective-permute-start(bf16[2,256,128]{2,1,0:T(8,128)(2,1)S(1)} %get-tuple-element.20), channel_id=1, source_target_pairs={{0,1},{1,0},{2,3},{3,2},{4,5},{5,4},{6,7},{7,6},{8,9},{9,8},{10,11... | collective-permute-start | bytes 393224 | tf_op jit(solution)/shard_map/ppermute | solution.py:35
  4.2 1.3 %project.3 = (bf16[4,256,128]{2,1,0:T(8,128)(2,1)S(1)}, f32[4,256,128]{2,1,0:T(8,128)S(1)}) custom-call(bf16[512,2048]{1,0:T(8,128)(2,1)S(1)} %load.1.refs_0_, bf16[2048,1024]{1,0:T(8,128)(2,1)S(1)} %copy-done), custom_call_target="tpu_custom_call" | custom-call | flops 1073741824 | bytes 2097152 | tf_op jit(solution)/shard_map/project/pallas_call | solution.py:113
  5.5 0.1 collective-permute-start
  5.6 0.0 copy-done.5
  5.6 0.1 broadcast_in_dim.2.owners
  5.7 0.0 copy-done.2
  5.7 0.0 collective-permute-done.2.refs_1_
  5.8 3.1 %collective-permute-start.3 = (bf16[640,128]{1,0:T(8,128)(2,1)S(1)}, bf16[640,128]{1,0:T(8,128)(2,1)S(1)}, u32[]{:S(2)}, u32[]{:S(2)}) collective-permute-start(bf16[640,128]{1,0:T(8,128)(2,1)S(1)} %send.2), channel_id=1, source_target_pairs={{0,4},{1,3},{2,6},{3,1},{4,0},{5,7},{6,2},{7,5},{8,12},{9,11},{10,... | collective-permute-start | bytes 491528 | tf_op jit(solution)/shard_map/ppermute | solution.py:48
  8.9 0.0 collective-permute-done.theirs.refs_1_
  8.9 1.0 %collective-permute-start.5 = (bf16[640,128]{1,0:T(8,128)(2,1)S(1)}, bf16[640,128]{1,0:T(8,128)(2,1)S(1)}, u32[]{:S(2)}, u32[]{:S(2)}) collective-permute-start(bf16[640,128]{1,0:T(8,128)(2,1)S(1)} %send.3), channel_id=1, source_target_pairs={{0,4},{1,3},{2,6},{3,1},{4,0},{5,7},{6,2},{7,5},{8,12},{9,11},{10,... | collective-permute-start | bytes 491528 | tf_op jit(solution)/shard_map/ppermute | solution.py:48
  9.9 2.3 %collective-permute-done.3.got = bf16[640,128]{1,0:T(8,128)(2,1)S(1)} collective-permute-done((bf16[640,128]{1,0:T(8,128)(2,1)S(1)}, bf16[640,128]{1,0:T(8,128)(2,1)S(1)}, u32[]{:S(2)}, u32[]{:S(2)}) %collective-permute-start.3) | collective-permute-done | bytes 163872 | tf_op jit(solution)/shard_map/ppermute | solution.py:48
  12.2 0.1 forward.1.after
  12.2 0.0 copy-start.3
  12.2 0.0 copy-start.4
  12.2 0.0 copy-start.1
  12.3 2.0 %collective-permute-start.6 = (bf16[640,128]{1,0:T(8,128)(2,1)S(1)}, bf16[640,128]{1,0:T(8,128)(2,1)S(1)}, u32[]{:S(2)}, u32[]{:S(2)}) collective-permute-start(bf16[640,128]{1,0:T(8,128)(2,1)S(1)} %forward.1.after), channel_id=1, source_target_pairs={{0,2},{1,5},{2,0},{3,7},{4,6},{5,1},{6,4},{7,3},{8,10},{9,13},{10,... | collective-permute-start | bytes 491528 | tf_op jit(solution)/shard_map/ppermute | solution.py:53
  14.3 0.8 %project.5 = (bf16[2,256,128]{2,1,0:T(8,128)(2,1)S(1)}, f32[2,256,128]{2,1,0:T(8,128)S(1)}) custom-call(bf16[512,2048]{1,0:T(8,128)(2,1)S(1)} %load.1.refs_0_, bf16[2048,1024]{1,0:T(8,128)(2,1)S(1)} %copy-done), custom_call_target="tpu_custom_call" | custom-call | flops 536870912 | bytes 2097152 | tf_op jit(solution)/shard_map/project/pallas_call | solution.py:113
  15.1 0.1 collective-permute-start.4
  15.2 1.3 %collective-permute-done.4.theirs = bf16[2,256,128]{2,1,0:T(8,128)(2,1)S(1)} collective-permute-done((bf16[2,256,128]{2,1,0:T(8,128)(2,1)S(1)}, bf16[2,256,128]{2,1,0:T(8,128)(2,1)S(1)}, u32[]{:S(2)}, u32[]{:S(2)}) %collective-permute-start.4) | collective-permute-done | bytes 131104 | tf_op jit(solution)/shard_map/ppermute | solution.py:35
  16.5 0.0 collective-permute-done.5.refs_0_
  16.5 1.1 %collective-permute-done.6.refs_1_ = bf16[640,128]{1,0:T(8,128)(2,1)S(1)} collective-permute-done((bf16[640,128]{1,0:T(8,128)(2,1)S(1)}, bf16[640,128]{1,0:T(8,128)(2,1)S(1)}, u32[]{:S(2)}, u32[]{:S(2)}) %collective-permute-start.6) | collective-permute-done | bytes 163872 | tf_op jit(solution)/shard_map/ppermute | solution.py:53
  17.6 0.1 fold.1
  17.7 3.1 %collective-permute-start.7 = (bf16[640,128]{1,0:T(8,128)(2,1)S(1)}, bf16[640,128]{1,0:T(8,128)(2,1)S(1)}, u32[]{:S(2)}, u32[]{:S(2)}) collective-permute-start(bf16[640,128]{1,0:T(8,128)(2,1)S(1)} %get-tuple-element.24), channel_id=1, source_target_pairs={{0,8},{1,9},{2,10},{3,11},{4,12},{5,13},{6,14},{7,15},{8,0},{9,1},... | collective-permute-start | bytes 491528 | tf_op jit(solution)/shard_map/ppermute | solution.py:35
  20.8 6.5 %collective-permute-done.7.right = bf16[640,128]{1,0:T(8,128)(2,1)S(1)} collective-permute-done((bf16[640,128]{1,0:T(8,128)(2,1)S(1)}, bf16[640,128]{1,0:T(8,128)(2,1)S(1)}, u32[]{:S(2)}, u32[]{:S(2)}) %collective-permute-start.7) | collective-permute-done | bytes 163872 | tf_op jit(solution)/shard_map/ppermute | solution.py:35
  27.3 1.1 %collective-permute-start.10 = (bf16[640,128]{1,0:T(8,128)(2,1)S(1)}, bf16[640,128]{1,0:T(8,128)(2,1)S(1)}, u32[]{:S(2)}, u32[]{:S(2)}) collective-permute-start(bf16[640,128]{1,0:T(8,128)(2,1)S(1)} %add.1.refs_0_), channel_id=1, source_target_pairs={{0,6},{1,7},{2,4},{3,5},{4,2},{5,3},{6,0},{7,1},{8,14},{9,15},{10,... | collective-permute-start | bytes 491528 | tf_op jit(solution)/shard_map/ppermute | solution.py:35
  28.5 1.1 %collective-permute-start.9 = (bf16[640,128]{1,0:T(8,128)(2,1)S(1)}, bf16[640,128]{1,0:T(8,128)(2,1)S(1)}, u32[]{:S(2)}, u32[]{:S(2)}) collective-permute-start(bf16[640,128]{1,0:T(8,128)(2,1)S(1)} %add.1.refs_0_), channel_id=1, source_target_pairs={{0,2},{1,5},{2,0},{3,7},{4,6},{5,1},{6,4},{7,3},{8,10},{9,13},{10,... | collective-permute-start | bytes 491528 | tf_op jit(solution)/shard_map/ppermute | solution.py:53
  29.6 1.4 %collective-permute-start.8 = (bf16[640,128]{1,0:T(8,128)(2,1)S(1)}, bf16[640,128]{1,0:T(8,128)(2,1)S(1)}, u32[]{:S(2)}, u32[]{:S(2)}) collective-permute-start(bf16[640,128]{1,0:T(8,128)(2,1)S(1)} %add.1.refs_0_), channel_id=1, source_target_pairs={{0,4},{1,3},{2,6},{3,1},{4,0},{5,7},{6,2},{7,5},{8,12},{9,11},{10,... | collective-permute-start | bytes 491528 | tf_op jit(solution)/shard_map/ppermute | solution.py:48
  30.9 0.0 copy-done.3
  30.9 0.0 copy-done.4
  30.9 0.7 %mask.1.allowed = bf16[256,256]{1,0:T(8,128)(2,1)S(1)} custom-call(s32[2,4]{1,0:T(2,128)S(1)} %copy-done.4, s32[2,256]{1,0:T(2,128)S(1)} %copy-done.3, bf16[640,128]{1,0:T(8,128)(2,1)S(1)} %forward.1.after), custom_call_target="tpu_custom_call" | custom-call | tf_op jit(solution)/shard_map/mask/pallas_call | solution.py:273
  31.6 3.6 %collective-permute-done.10.refs_3_ = bf16[640,128]{1,0:T(8,128)(2,1)S(1)} collective-permute-done((bf16[640,128]{1,0:T(8,128)(2,1)S(1)}, bf16[640,128]{1,0:T(8,128)(2,1)S(1)}, u32[]{:S(2)}, u32[]{:S(2)}) %collective-permute-start.10) | collective-permute-done | bytes 163872 | tf_op jit(solution)/shard_map/ppermute | solution.py:35
  35.1 1.7 %collective-permute-done.9.refs_2_ = bf16[640,128]{1,0:T(8,128)(2,1)S(1)} collective-permute-done((bf16[640,128]{1,0:T(8,128)(2,1)S(1)}, bf16[640,128]{1,0:T(8,128)(2,1)S(1)}, u32[]{:S(2)}, u32[]{:S(2)}) %collective-permute-start.9) | collective-permute-done | bytes 163872 | tf_op jit(solution)/shard_map/ppermute | solution.py:53
  36.9 0.0 collective-permute-done.8.refs_1_
  36.9 0.3 couple.1.scaled
  37.2 0.1 collective-permute-start.11
  37.3 0.0 copy-done.1
  37.3 1.3 %begin.1.begun = f32[4,2048,256]{2,1,0:T(8,128)S(1)} custom-call(bf16[2048,512]{1,0:T(8,128)(2,1)S(1)} %copy-done.1, bf16[8,256,128]{2,1,0:T(8,128)(2,1)S(1)} %couple.1.scaled), custom_call_target="tpu_custom_call" | custom-call | flops 1073741824 | bytes 2097152 | tf_op jit(solution)/shard_map/begin/pallas_call | solution.py:339
  38.5 0.6 %collective-permute-done.11.other = bf16[8,256,128]{2,1,0:T(8,128)(2,1)S(1)} collective-permute-done((bf16[8,256,128]{2,1,0:T(8,128)(2,1)S(1)}, bf16[8,256,128]{2,1,0:T(8,128)(2,1)S(1)}, u32[]{:S(2)}, u32[]{:S(2)}) %collective-permute-start.11) | collective-permute-done | bytes 524320 | tf_op jit(solution)/shard_map/ppermute | solution.py:35
  39.2 3.3 %finish.1 = bf16[2048,1024]{1,0:T(8,128)(2,1)} custom-call(bf16[2048,512]{1,0:T(8,128)(2,1)S(1)} %copy-done.1, f32[4,2048,256]{2,1,0:T(8,128)S(1)} %begin.1.begun, bf16[8,256,128]{2,1,0:T(8,128)(2,1)S(1)} %collective-permute-done.11.other), custom_call_target="tpu_custom_call" | custom-call | flops 1073741824 | bytes 6291456 | tf_op jit(solution)/shard_map/finish/pallas_call | solution.py:379
  (4 shorter events, 0.1 us)
Async XLA Ops:
  0.0 2.8 %copy-start = (bf16[2048,1024]{1,0:T(8,128)(2,1)S(1)}, bf16[2048,1024]{1,0:T(8,128)(2,1)}, u32[]{:S(2)}) copy-start(bf16[2048,1024]{1,0:T(8,128)(2,1)} %refs_1_.5) | copy-start | bytes 12582916
  0.0 3.6 %collective-permute-start.1 = (f32[256,256]{1,0:T(8,128)}, f32[256,256]{1,0:T(8,128)S(1)}, u32[]{:S(2)}, u32[]{:S(2)}) collective-permute-start(f32[256,256]{1,0:T(8,128)} %bitcast.1), channel_id=1, source_target_pairs={{0,1},{1,0},{2,3},{3,2},{4,5},{5,4},{6,7},{7,6},{8,9},{9,8},{10,11... | collective-permute-start | bytes 786440 | tf_op jit(solution)/shard_map/ppermute | solution.py:35
  3.6 2.0 %copy-start.5 = (s32[2]{0:T(128)S(1)}, s32[2]{0:T(128)}, u32[]{:S(2)}) copy-start(s32[2]{0:T(128)} %param.10) | copy-start | bytes 28
  3.6 2.1 %copy-start.2 = (f32[1,256,256]{2,1,0:T(8,128)S(1)}, f32[1,256,256]{2,1,0:T(8,128)}, u32[]{:S(2)}) copy-start(f32[1,256,256]{2,1,0:T(8,128)} %param.11) | copy-start | bytes 786436
  3.6 2.1 %collective-permute-start.2 = (bf16[2,256,128]{2,1,0:T(8,128)(2,1)S(1)}, bf16[2,256,128]{2,1,0:T(8,128)(2,1)S(1)}, u32[]{:S(2)}, u32[]{:S(2)}) collective-permute-start(bf16[2,256,128]{2,1,0:T(8,128)(2,1)S(1)} %get-tuple-element.20), channel_id=1, source_target_pairs={{0,1},{1,0},{2,3},{3,2},{4,5},{5,4},{6,7},{7,6},{8,9},{9,8},{10,11... | collective-permute-start | bytes 393224 | tf_op jit(solution)/shard_map/ppermute | solution.py:35
  5.5 3.4 %collective-permute-start = (bf16[4,256,128]{2,1,0:T(8,128)(2,1)S(1)}, bf16[4,256,128]{2,1,0:T(8,128)(2,1)S(1)}, u32[]{:S(2)}, u32[]{:S(2)}) collective-permute-start(bf16[4,256,128]{2,1,0:T(8,128)(2,1)S(1)} %get-tuple-element.16), channel_id=1, source_target_pairs={{0,1},{1,0},{2,3},{3,2},{4,5},{5,4},{6,7},{7,6},{8,9},{9,8},{10,11... | collective-permute-start | bytes 786440 | tf_op jit(solution)/shard_map/ppermute | solution.py:35
  5.8 6.4 %collective-permute-start.3 = (bf16[640,128]{1,0:T(8,128)(2,1)S(1)}, bf16[640,128]{1,0:T(8,128)(2,1)S(1)}, u32[]{:S(2)}, u32[]{:S(2)}) collective-permute-start(bf16[640,128]{1,0:T(8,128)(2,1)S(1)} %send.2), channel_id=1, source_target_pairs={{0,4},{1,3},{2,6},{3,1},{4,0},{5,7},{6,2},{7,5},{8,12},{9,11},{10,... | collective-permute-start | bytes 491528 | tf_op jit(solution)/shard_map/ppermute | solution.py:48
  8.9 7.6 %collective-permute-start.5 = (bf16[640,128]{1,0:T(8,128)(2,1)S(1)}, bf16[640,128]{1,0:T(8,128)(2,1)S(1)}, u32[]{:S(2)}, u32[]{:S(2)}) collective-permute-start(bf16[640,128]{1,0:T(8,128)(2,1)S(1)} %send.3), channel_id=1, source_target_pairs={{0,4},{1,3},{2,6},{3,1},{4,0},{5,7},{6,2},{7,5},{8,12},{9,11},{10,... | collective-permute-start | bytes 491528 | tf_op jit(solution)/shard_map/ppermute | solution.py:48
  12.2 18.7 %copy-start.3 = (s32[2,256]{1,0:T(2,128)S(1)}, s32[2,256]{1,0:T(2,128)}, u32[]{:S(2)}) copy-start(s32[2,256]{1,0:T(2,128)} %atom_of.1) | copy-start | bytes 6148
  12.2 18.7 %copy-start.4 = (s32[2,4]{1,0:T(2,128)S(1)}, s32[2,4]{1,0:T(2,128)}, u32[]{:S(2)}) copy-start(s32[2,4]{1,0:T(2,128)} %counts.1) | copy-start | bytes 100
  12.2 25.0 %copy-start.1 = (bf16[2048,512]{1,0:T(8,128)(2,1)S(1)}, bf16[2048,512]{1,0:T(8,128)(2,1)}, u32[]{:S(2)}) copy-start(bf16[2048,512]{1,0:T(8,128)(2,1)} %projectors.5) | copy-start | bytes 6291460
  12.3 5.4 %collective-permute-start.6 = (bf16[640,128]{1,0:T(8,128)(2,1)S(1)}, bf16[640,128]{1,0:T(8,128)(2,1)S(1)}, u32[]{:S(2)}, u32[]{:S(2)}) collective-permute-start(bf16[640,128]{1,0:T(8,128)(2,1)S(1)} %forward.1.after), channel_id=1, source_target_pairs={{0,2},{1,5},{2,0},{3,7},{4,6},{5,1},{6,4},{7,3},{8,10},{9,13},{10,... | collective-permute-start | bytes 491528 | tf_op jit(solution)/shard_map/ppermute | solution.py:53
  15.1 1.4 %collective-permute-start.4 = (bf16[2,256,128]{2,1,0:T(8,128)(2,1)S(1)}, bf16[2,256,128]{2,1,0:T(8,128)(2,1)S(1)}, u32[]{:S(2)}, u32[]{:S(2)}) collective-permute-start(bf16[2,256,128]{2,1,0:T(8,128)(2,1)S(1)} %get-tuple-element.22), channel_id=1, source_target_pairs={{0,1},{1,0},{2,3},{3,2},{4,5},{5,4},{6,7},{7,6},{8,9},{9,8},{10,11... | collective-permute-start | bytes 393224 | tf_op jit(solution)/shard_map/ppermute | solution.py:35
  17.7 9.6 %collective-permute-start.7 = (bf16[640,128]{1,0:T(8,128)(2,1)S(1)}, bf16[640,128]{1,0:T(8,128)(2,1)S(1)}, u32[]{:S(2)}, u32[]{:S(2)}) collective-permute-start(bf16[640,128]{1,0:T(8,128)(2,1)S(1)} %get-tuple-element.24), channel_id=1, source_target_pairs={{0,8},{1,9},{2,10},{3,11},{4,12},{5,13},{6,14},{7,15},{8,0},{9,1},... | collective-permute-start | bytes 491528 | tf_op jit(solution)/shard_map/ppermute | solution.py:35
  27.3 7.8 %collective-permute-start.10 = (bf16[640,128]{1,0:T(8,128)(2,1)S(1)}, bf16[640,128]{1,0:T(8,128)(2,1)S(1)}, u32[]{:S(2)}, u32[]{:S(2)}) collective-permute-start(bf16[640,128]{1,0:T(8,128)(2,1)S(1)} %add.1.refs_0_), channel_id=1, source_target_pairs={{0,6},{1,7},{2,4},{3,5},{4,2},{5,3},{6,0},{7,1},{8,14},{9,15},{10,... | collective-permute-start | bytes 491528 | tf_op jit(solution)/shard_map/ppermute | solution.py:35
  28.5 8.4 %collective-permute-start.9 = (bf16[640,128]{1,0:T(8,128)(2,1)S(1)}, bf16[640,128]{1,0:T(8,128)(2,1)S(1)}, u32[]{:S(2)}, u32[]{:S(2)}) collective-permute-start(bf16[640,128]{1,0:T(8,128)(2,1)S(1)} %add.1.refs_0_), channel_id=1, source_target_pairs={{0,2},{1,5},{2,0},{3,7},{4,6},{5,1},{6,4},{7,3},{8,10},{9,13},{10,... | collective-permute-start | bytes 491528 | tf_op jit(solution)/shard_map/ppermute | solution.py:53
  29.6 7.3 %collective-permute-start.8 = (bf16[640,128]{1,0:T(8,128)(2,1)S(1)}, bf16[640,128]{1,0:T(8,128)(2,1)S(1)}, u32[]{:S(2)}, u32[]{:S(2)}) collective-permute-start(bf16[640,128]{1,0:T(8,128)(2,1)S(1)} %add.1.refs_0_), channel_id=1, source_target_pairs={{0,4},{1,3},{2,6},{3,1},{4,0},{5,7},{6,2},{7,5},{8,12},{9,11},{10,... | collective-permute-start | bytes 491528 | tf_op jit(solution)/shard_map/ppermute | solution.py:48
  37.2 2.0 %collective-permute-start.11 = (bf16[8,256,128]{2,1,0:T(8,128)(2,1)S(1)}, bf16[8,256,128]{2,1,0:T(8,128)(2,1)S(1)}, u32[]{:S(2)}, u32[]{:S(2)}) collective-permute-start(bf16[8,256,128]{2,1,0:T(8,128)(2,1)S(1)} %couple.1.scaled), channel_id=1, source_target_pairs={{0,1},{1,0},{2,3},{3,2},{4,5},{5,4},{6,7},{7,6},{8,9},{9,8},{10,11... | collective-permute-start | bytes 1572872 | tf_op jit(solution)/shard_map/ppermute | solution.py:35

commit v19 on v18

--- a/solution.py
+++ b/solution.py
@@ -74,7 +74,7 @@
     for at in range(count):
         rows = slice(at * block, (at + 1) * block)
         copies.append(pltpu.make_async_copy(projectors.at[rows], slots.at[rows], sems.at[at]))
-        copies[-1].start()
+        copies[-1].start(priority=at % 2)
     for at, copy in enumerate(copies):
         copy.wait()
         rows = slice(at * block, (at + 1) * block)
@@ -368,7 +368,7 @@
         for start in range(rows.start, rows.stop, COPY_ROWS):
             written = slice(start, start + COPY_ROWS)
             copies.append(pltpu.make_async_copy(blocks.at[written], out.at[written], sems.at[len(copies)]))
-            copies[-1].start()
+            copies[-1].start(priority=len(copies) % 2)
     for copy in copies:
         copy.wait()
 

time: 42.6 us -> 42.6 us (level)
  no operation moved by 1% of the time
where the time goes in v19:
time: 42.6 us; the launch traced here: 42.5 us
  waiting for transfers between devices  17.2 us (40%)
  starting transfers between devices  14 us (33%)
  Pallas kernels  10.9 us (26%)
    ppermute x7, waiting for transfers between devices, swap(): return lax.ppermute(x, 'pw', [(i, i ^ distance) for i in range(count)])  12 us
    ppermute x7, starting transfers between devices, swap(): return lax.ppermute(x, 'pw', [(i, i ^ distance) for i in range(count)])  5.51 us
    ppermute x3, starting transfers between devices, swap_first(): return lax.ppermute(x, 'pw', [(i, i ^ (4, 2)[i % 2]) for i in range(count)])  5.42 us
    pallas_call x1, Pallas kernels, finish(): pl.pallas_call(finish_kernel, in_specs=[VMEM] * 3, out_specs=HBM, out_sha...  3.3 us
    ppermute x2, starting transfers between devices, swap_second(): return lax.ppermute(x, 'pw', [(i, i ^ (2, 4)[i % 2]) for i in range(count)])  3.07 us
    pallas_call x3, Pallas kernels, project(): pl.pallas_call(kernel, in_specs=[VMEM, VMEM], out_specs=[VMEM, VMEM], out...  2.91 us
    ppermute x2, waiting for transfers between devices, swap_second(): return lax.ppermute(x, 'pw', [(i, i ^ (2, 4)[i % 2]) for i in range(count)])  2.86 us
    ppermute x3, waiting for transfers between devices, swap_first(): return lax.ppermute(x, 'pw', [(i, i ^ (4, 2)[i % 2]) for i in range(count)])  2.28 us
  transfers between devices with their start and end apart: 12, of which 7 were waited for; matrix products, arithmetic and copies ran while one was open for 0% of the time, Pallas kernels for 17%

profile of v19, /device:TPU:0, one launch (start us, length us, event | category | flops | bytes accessed | tf_op | source)
XLA Modules:
  0.0 42.5 jit_solution(1059844225207432576)
XLA Ops:
  0.0 0.0 copy-start
  0.0 0.5 %collective-permute-start.1 = (f32[256,256]{1,0:T(8,128)}, f32[256,256]{1,0:T(8,128)S(1)}, u32[]{:S(2)}, u32[]{:S(2)}) collective-permute-start(f32[256,256]{1,0:T(8,128)} %bitcast.1), channel_id=1, source_target_pairs={{0,1},{1,0},{2,3},{3,2},{4,5},{5,4},{6,7},{7,6},{8,9},{9,8},{10,11... | collective-permute-start | bytes 786440 | tf_op jit(solution)/shard_map/ppermute | solution.py:35
  0.5 2.2 %load.1.refs_0_ = bf16[512,2048]{1,0:T(8,128)(2,1)S(1)} custom-call(bf16[2048,512]{1,0:T(8,128)(2,1)} %projectors.5), custom_call_target="tpu_custom_call" | custom-call | tf_op jit(solution)/shard_map/load/pallas_call | solution.py:88
  2.7 0.1 copy-done
  2.8 0.8 %project.4 = (bf16[2,256,128]{2,1,0:T(8,128)(2,1)S(1)}, f32[2,256,128]{2,1,0:T(8,128)S(1)}) custom-call(bf16[512,2048]{1,0:T(8,128)(2,1)S(1)} %load.1.refs_0_, bf16[2048,1024]{1,0:T(8,128)(2,1)S(1)} %copy-done), custom_call_target="tpu_custom_call" | custom-call | flops 536870912 | bytes 2097152 | tf_op jit(solution)/shard_map/project/pallas_call | solution.py:113
  3.6 0.0 copy-start.5
  3.6 0.0 copy-start.2
  3.6 0.0 collective-permute-done.1.sibling
  3.6 0.5 %collective-permute-start.2 = (bf16[2,256,128]{2,1,0:T(8,128)(2,1)S(1)}, bf16[2,256,128]{2,1,0:T(8,128)(2,1)S(1)}, u32[]{:S(2)}, u32[]{:S(2)}) collective-permute-start(bf16[2,256,128]{2,1,0:T(8,128)(2,1)S(1)} %get-tuple-element.20), channel_id=1, source_target_pairs={{0,1},{1,0},{2,3},{3,2},{4,5},{5,4},{6,7},{7,6},{8,9},{9,8},{10,11... | collective-permute-start | bytes 393224 | tf_op jit(solution)/shard_map/ppermute | solution.py:35
  4.2 1.3 %project.3 = (bf16[4,256,128]{2,1,0:T(8,128)(2,1)S(1)}, f32[4,256,128]{2,1,0:T(8,128)S(1)}) custom-call(bf16[512,2048]{1,0:T(8,128)(2,1)S(1)} %load.1.refs_0_, bf16[2048,1024]{1,0:T(8,128)(2,1)S(1)} %copy-done), custom_call_target="tpu_custom_call" | custom-call | flops 1073741824 | bytes 2097152 | tf_op jit(solution)/shard_map/project/pallas_call | solution.py:113
  5.5 0.1 collective-permute-start
  5.6 0.0 copy-done.5
  5.6 0.1 broadcast_in_dim.2.owners
  5.7 0.0 copy-done.2
  5.7 0.0 collective-permute-done.2.refs_1_
  5.8 3.1 %collective-permute-start.3 = (bf16[640,128]{1,0:T(8,128)(2,1)S(1)}, bf16[640,128]{1,0:T(8,128)(2,1)S(1)}, u32[]{:S(2)}, u32[]{:S(2)}) collective-permute-start(bf16[640,128]{1,0:T(8,128)(2,1)S(1)} %send.2), channel_id=1, source_target_pairs={{0,4},{1,3},{2,6},{3,1},{4,0},{5,7},{6,2},{7,5},{8,12},{9,11},{10,... | collective-permute-start | bytes 491528 | tf_op jit(solution)/shard_map/ppermute | solution.py:48
  8.9 0.0 collective-permute-done.theirs.refs_1_
  8.9 1.0 %collective-permute-start.5 = (bf16[640,128]{1,0:T(8,128)(2,1)S(1)}, bf16[640,128]{1,0:T(8,128)(2,1)S(1)}, u32[]{:S(2)}, u32[]{:S(2)}) collective-permute-start(bf16[640,128]{1,0:T(8,128)(2,1)S(1)} %send.3), channel_id=1, source_target_pairs={{0,4},{1,3},{2,6},{3,1},{4,0},{5,7},{6,2},{7,5},{8,12},{9,11},{10,... | collective-permute-start | bytes 491528 | tf_op jit(solution)/shard_map/ppermute | solution.py:48
  9.9 2.3 %collective-permute-done.3.got = bf16[640,128]{1,0:T(8,128)(2,1)S(1)} collective-permute-done((bf16[640,128]{1,0:T(8,128)(2,1)S(1)}, bf16[640,128]{1,0:T(8,128)(2,1)S(1)}, u32[]{:S(2)}, u32[]{:S(2)}) %collective-permute-start.3) | collective-permute-done | bytes 163872 | tf_op jit(solution)/shard_map/ppermute | solution.py:48
  12.2 0.1 forward.1.after
  12.2 0.0 copy-start.3
  12.2 0.0 copy-start.4
  12.2 0.0 copy-start.1
  12.3 2.0 %collective-permute-start.6 = (bf16[640,128]{1,0:T(8,128)(2,1)S(1)}, bf16[640,128]{1,0:T(8,128)(2,1)S(1)}, u32[]{:S(2)}, u32[]{:S(2)}) collective-permute-start(bf16[640,128]{1,0:T(8,128)(2,1)S(1)} %forward.1.after), channel_id=1, source_target_pairs={{0,2},{1,5},{2,0},{3,7},{4,6},{5,1},{6,4},{7,3},{8,10},{9,13},{10,... | collective-permute-start | bytes 491528 | tf_op jit(solution)/shard_map/ppermute | solution.py:53
  14.3 0.8 %project.5 = (bf16[2,256,128]{2,1,0:T(8,128)(2,1)S(1)}, f32[2,256,128]{2,1,0:T(8,128)S(1)}) custom-call(bf16[512,2048]{1,0:T(8,128)(2,1)S(1)} %load.1.refs_0_, bf16[2048,1024]{1,0:T(8,128)(2,1)S(1)} %copy-done), custom_call_target="tpu_custom_call" | custom-call | flops 536870912 | bytes 2097152 | tf_op jit(solution)/shard_map/project/pallas_call | solution.py:113
  15.1 0.1 collective-permute-start.4
  15.2 1.3 %collective-permute-done.4.theirs = bf16[2,256,128]{2,1,0:T(8,128)(2,1)S(1)} collective-permute-done((bf16[2,256,128]{2,1,0:T(8,128)(2,1)S(1)}, bf16[2,256,128]{2,1,0:T(8,128)(2,1)S(1)}, u32[]{:S(2)}, u32[]{:S(2)}) %collective-permute-start.4) | collective-permute-done | bytes 131104 | tf_op jit(solution)/shard_map/ppermute | solution.py:35
  16.5 0.0 collective-permute-done.5.refs_0_
  16.5 1.1 %collective-permute-done.6.refs_1_ = bf16[640,128]{1,0:T(8,128)(2,1)S(1)} collective-permute-done((bf16[640,128]{1,0:T(8,128)(2,1)S(1)}, bf16[640,128]{1,0:T(8,128)(2,1)S(1)}, u32[]{:S(2)}, u32[]{:S(2)}) %collective-permute-start.6) | collective-permute-done | bytes 163872 | tf_op jit(solution)/shard_map/ppermute | solution.py:53
  17.6 0.1 fold.1
  17.7 3.1 %collective-permute-start.7 = (bf16[640,128]{1,0:T(8,128)(2,1)S(1)}, bf16[640,128]{1,0:T(8,128)(2,1)S(1)}, u32[]{:S(2)}, u32[]{:S(2)}) collective-permute-start(bf16[640,128]{1,0:T(8,128)(2,1)S(1)} %get-tuple-element.24), channel_id=1, source_target_pairs={{0,8},{1,9},{2,10},{3,11},{4,12},{5,13},{6,14},{7,15},{8,0},{9,1},... | collective-permute-start | bytes 491528 | tf_op jit(solution)/shard_map/ppermute | solution.py:35
  20.8 6.5 %collective-permute-done.7.right = bf16[640,128]{1,0:T(8,128)(2,1)S(1)} collective-permute-done((bf16[640,128]{1,0:T(8,128)(2,1)S(1)}, bf16[640,128]{1,0:T(8,128)(2,1)S(1)}, u32[]{:S(2)}, u32[]{:S(2)}) %collective-permute-start.7) | collective-permute-done | bytes 163872 | tf_op jit(solution)/shard_map/ppermute | solution.py:35
  27.3 1.2 %collective-permute-start.10 = (bf16[640,128]{1,0:T(8,128)(2,1)S(1)}, bf16[640,128]{1,0:T(8,128)(2,1)S(1)}, u32[]{:S(2)}, u32[]{:S(2)}) collective-permute-start(bf16[640,128]{1,0:T(8,128)(2,1)S(1)} %add.1.refs_0_), channel_id=1, source_target_pairs={{0,6},{1,7},{2,4},{3,5},{4,2},{5,3},{6,0},{7,1},{8,14},{9,15},{10,... | collective-permute-start | bytes 491528 | tf_op jit(solution)/shard_map/ppermute | solution.py:35
  28.5 1.0 %collective-permute-start.9 = (bf16[640,128]{1,0:T(8,128)(2,1)S(1)}, bf16[640,128]{1,0:T(8,128)(2,1)S(1)}, u32[]{:S(2)}, u32[]{:S(2)}) collective-permute-start(bf16[640,128]{1,0:T(8,128)(2,1)S(1)} %add.1.refs_0_), channel_id=1, source_target_pairs={{0,2},{1,5},{2,0},{3,7},{4,6},{5,1},{6,4},{7,3},{8,10},{9,13},{10,... | collective-permute-start | bytes 491528 | tf_op jit(solution)/shard_map/ppermute | solution.py:53
  29.6 1.4 %collective-permute-start.8 = (bf16[640,128]{1,0:T(8,128)(2,1)S(1)}, bf16[640,128]{1,0:T(8,128)(2,1)S(1)}, u32[]{:S(2)}, u32[]{:S(2)}) collective-permute-start(bf16[640,128]{1,0:T(8,128)(2,1)S(1)} %add.1.refs_0_), channel_id=1, source_target_pairs={{0,4},{1,3},{2,6},{3,1},{4,0},{5,7},{6,2},{7,5},{8,12},{9,11},{10,... | collective-permute-start | bytes 491528 | tf_op jit(solution)/shard_map/ppermute | solution.py:48
  30.9 0.0 copy-done.3
  30.9 0.0 copy-done.4
  30.9 0.7 %mask.1.allowed = bf16[256,256]{1,0:T(8,128)(2,1)S(1)} custom-call(s32[2,4]{1,0:T(2,128)S(1)} %copy-done.4, s32[2,256]{1,0:T(2,128)S(1)} %copy-done.3, bf16[640,128]{1,0:T(8,128)(2,1)S(1)} %forward.1.after), custom_call_target="tpu_custom_call" | custom-call | tf_op jit(solution)/shard_map/mask/pallas_call | solution.py:273
  31.6 3.6 %collective-permute-done.10.refs_3_ = bf16[640,128]{1,0:T(8,128)(2,1)S(1)} collective-permute-done((bf16[640,128]{1,0:T(8,128)(2,1)S(1)}, bf16[640,128]{1,0:T(8,128)(2,1)S(1)}, u32[]{:S(2)}, u32[]{:S(2)}) %collective-permute-start.10) | collective-permute-done | bytes 163872 | tf_op jit(solution)/shard_map/ppermute | solution.py:35
  35.1 1.7 %collective-permute-done.9.refs_2_ = bf16[640,128]{1,0:T(8,128)(2,1)S(1)} collective-permute-done((bf16[640,128]{1,0:T(8,128)(2,1)S(1)}, bf16[640,128]{1,0:T(8,128)(2,1)S(1)}, u32[]{:S(2)}, u32[]{:S(2)}) %collective-permute-start.9) | collective-permute-done | bytes 163872 | tf_op jit(solution)/shard_map/ppermute | solution.py:53
  36.9 0.0 collective-permute-done.8.refs_1_
  36.9 0.3 couple.1.scaled
  37.2 0.1 collective-permute-start.11
  37.3 0.0 copy-done.1
  37.3 1.3 %begin.1.begun = f32[4,2048,256]{2,1,0:T(8,128)S(1)} custom-call(bf16[2048,512]{1,0:T(8,128)(2,1)S(1)} %copy-done.1, bf16[8,256,128]{2,1,0:T(8,128)(2,1)S(1)} %couple.1.scaled), custom_call_target="tpu_custom_call" | custom-call | flops 1073741824 | bytes 2097152 | tf_op jit(solution)/shard_map/begin/pallas_call | solution.py:339
  38.5 0.6 %collective-permute-done.11.other = bf16[8,256,128]{2,1,0:T(8,128)(2,1)S(1)} collective-permute-done((bf16[8,256,128]{2,1,0:T(8,128)(2,1)S(1)}, bf16[8,256,128]{2,1,0:T(8,128)(2,1)S(1)}, u32[]{:S(2)}, u32[]{:S(2)}) %collective-permute-start.11) | collective-permute-done | bytes 524320 | tf_op jit(solution)/shard_map/ppermute | solution.py:35
  39.2 3.3 %finish.1 = bf16[2048,1024]{1,0:T(8,128)(2,1)} custom-call(bf16[2048,512]{1,0:T(8,128)(2,1)S(1)} %copy-done.1, f32[4,2048,256]{2,1,0:T(8,128)S(1)} %begin.1.begun, bf16[8,256,128]{2,1,0:T(8,128)(2,1)S(1)} %collective-permute-done.11.other), custom_call_target="tpu_custom_call" | custom-call | flops 1073741824 | bytes 6291456 | tf_op jit(solution)/shard_map/finish/pallas_call | solution.py:379
  (4 shorter events, 0.1 us)
Async XLA Ops:
  0.0 2.8 %copy-start = (bf16[2048,1024]{1,0:T(8,128)(2,1)S(1)}, bf16[2048,1024]{1,0:T(8,128)(2,1)}, u32[]{:S(2)}) copy-start(bf16[2048,1024]{1,0:T(8,128)(2,1)} %refs_1_.5) | copy-start | bytes 12582916
  0.0 3.6 %collective-permute-start.1 = (f32[256,256]{1,0:T(8,128)}, f32[256,256]{1,0:T(8,128)S(1)}, u32[]{:S(2)}, u32[]{:S(2)}) collective-permute-start(f32[256,256]{1,0:T(8,128)} %bitcast.1), channel_id=1, source_target_pairs={{0,1},{1,0},{2,3},{3,2},{4,5},{5,4},{6,7},{7,6},{8,9},{9,8},{10,11... | collective-permute-start | bytes 786440 | tf_op jit(solution)/shard_map/ppermute | solution.py:35
  3.6 2.0 %copy-start.5 = (s32[2]{0:T(128)S(1)}, s32[2]{0:T(128)}, u32[]{:S(2)}) copy-start(s32[2]{0:T(128)} %param.10) | copy-start | bytes 28
  3.6 2.1 %copy-start.2 = (f32[1,256,256]{2,1,0:T(8,128)S(1)}, f32[1,256,256]{2,1,0:T(8,128)}, u32[]{:S(2)}) copy-start(f32[1,256,256]{2,1,0:T(8,128)} %param.11) | copy-start | bytes 786436
  3.6 2.1 %collective-permute-start.2 = (bf16[2,256,128]{2,1,0:T(8,128)(2,1)S(1)}, bf16[2,256,128]{2,1,0:T(8,128)(2,1)S(1)}, u32[]{:S(2)}, u32[]{:S(2)}) collective-permute-start(bf16[2,256,128]{2,1,0:T(8,128)(2,1)S(1)} %get-tuple-element.20), channel_id=1, source_target_pairs={{0,1},{1,0},{2,3},{3,2},{4,5},{5,4},{6,7},{7,6},{8,9},{9,8},{10,11... | collective-permute-start | bytes 393224 | tf_op jit(solution)/shard_map/ppermute | solution.py:35
  5.5 3.4 %collective-permute-start = (bf16[4,256,128]{2,1,0:T(8,128)(2,1)S(1)}, bf16[4,256,128]{2,1,0:T(8,128)(2,1)S(1)}, u32[]{:S(2)}, u32[]{:S(2)}) collective-permute-start(bf16[4,256,128]{2,1,0:T(8,128)(2,1)S(1)} %get-tuple-element.16), channel_id=1, source_target_pairs={{0,1},{1,0},{2,3},{3,2},{4,5},{5,4},{6,7},{7,6},{8,9},{9,8},{10,11... | collective-permute-start | bytes 786440 | tf_op jit(solution)/shard_map/ppermute | solution.py:35
  5.8 6.4 %collective-permute-start.3 = (bf16[640,128]{1,0:T(8,128)(2,1)S(1)}, bf16[640,128]{1,0:T(8,128)(2,1)S(1)}, u32[]{:S(2)}, u32[]{:S(2)}) collective-permute-start(bf16[640,128]{1,0:T(8,128)(2,1)S(1)} %send.2), channel_id=1, source_target_pairs={{0,4},{1,3},{2,6},{3,1},{4,0},{5,7},{6,2},{7,5},{8,12},{9,11},{10,... | collective-permute-start | bytes 491528 | tf_op jit(solution)/shard_map/ppermute | solution.py:48
  8.9 7.6 %collective-permute-start.5 = (bf16[640,128]{1,0:T(8,128)(2,1)S(1)}, bf16[640,128]{1,0:T(8,128)(2,1)S(1)}, u32[]{:S(2)}, u32[]{:S(2)}) collective-permute-start(bf16[640,128]{1,0:T(8,128)(2,1)S(1)} %send.3), channel_id=1, source_target_pairs={{0,4},{1,3},{2,6},{3,1},{4,0},{5,7},{6,2},{7,5},{8,12},{9,11},{10,... | collective-permute-start | bytes 491528 | tf_op jit(solution)/shard_map/ppermute | solution.py:48
  12.2 18.7 %copy-start.3 = (s32[2,256]{1,0:T(2,128)S(1)}, s32[2,256]{1,0:T(2,128)}, u32[]{:S(2)}) copy-start(s32[2,256]{1,0:T(2,128)} %atom_of.1) | copy-start | bytes 6148
  12.2 18.7 %copy-start.4 = (s32[2,4]{1,0:T(2,128)S(1)}, s32[2,4]{1,0:T(2,128)}, u32[]{:S(2)}) copy-start(s32[2,4]{1,0:T(2,128)} %counts.1) | copy-start | bytes 100
  12.2 25.0 %copy-start.1 = (bf16[2048,512]{1,0:T(8,128)(2,1)S(1)}, bf16[2048,512]{1,0:T(8,128)(2,1)}, u32[]{:S(2)}) copy-start(bf16[2048,512]{1,0:T(8,128)(2,1)} %projectors.5) | copy-start | bytes 6291460
  12.3 5.4 %collective-permute-start.6 = (bf16[640,128]{1,0:T(8,128)(2,1)S(1)}, bf16[640,128]{1,0:T(8,128)(2,1)S(1)}, u32[]{:S(2)}, u32[]{:S(2)}) collective-permute-start(bf16[640,128]{1,0:T(8,128)(2,1)S(1)} %forward.1.after), channel_id=1, source_target_pairs={{0,2},{1,5},{2,0},{3,7},{4,6},{5,1},{6,4},{7,3},{8,10},{9,13},{10,... | collective-permute-start | bytes 491528 | tf_op jit(solution)/shard_map/ppermute | solution.py:53
  15.1 1.4 %collective-permute-start.4 = (bf16[2,256,128]{2,1,0:T(8,128)(2,1)S(1)}, bf16[2,256,128]{2,1,0:T(8,128)(2,1)S(1)}, u32[]{:S(2)}, u32[]{:S(2)}) collective-permute-start(bf16[2,256,128]{2,1,0:T(8,128)(2,1)S(1)} %get-tuple-element.22), channel_id=1, source_target_pairs={{0,1},{1,0},{2,3},{3,2},{4,5},{5,4},{6,7},{7,6},{8,9},{9,8},{10,11... | collective-permute-start | bytes 393224 | tf_op jit(solution)/shard_map/ppermute | solution.py:35
  17.7 9.6 %collective-permute-start.7 = (bf16[640,128]{1,0:T(8,128)(2,1)S(1)}, bf16[640,128]{1,0:T(8,128)(2,1)S(1)}, u32[]{:S(2)}, u32[]{:S(2)}) collective-permute-start(bf16[640,128]{1,0:T(8,128)(2,1)S(1)} %get-tuple-element.24), channel_id=1, source_target_pairs={{0,8},{1,9},{2,10},{3,11},{4,12},{5,13},{6,14},{7,15},{8,0},{9,1},... | collective-permute-start | bytes 491528 | tf_op jit(solution)/shard_map/ppermute | solution.py:35
  27.3 7.8 %collective-permute-start.10 = (bf16[640,128]{1,0:T(8,128)(2,1)S(1)}, bf16[640,128]{1,0:T(8,128)(2,1)S(1)}, u32[]{:S(2)}, u32[]{:S(2)}) collective-permute-start(bf16[640,128]{1,0:T(8,128)(2,1)S(1)} %add.1.refs_0_), channel_id=1, source_target_pairs={{0,6},{1,7},{2,4},{3,5},{4,2},{5,3},{6,0},{7,1},{8,14},{9,15},{10,... | collective-permute-start | bytes 491528 | tf_op jit(solution)/shard_map/ppermute | solution.py:35
  28.5 8.3 %collective-permute-start.9 = (bf16[640,128]{1,0:T(8,128)(2,1)S(1)}, bf16[640,128]{1,0:T(8,128)(2,1)S(1)}, u32[]{:S(2)}, u32[]{:S(2)}) collective-permute-start(bf16[640,128]{1,0:T(8,128)(2,1)S(1)} %add.1.refs_0_), channel_id=1, source_target_pairs={{0,2},{1,5},{2,0},{3,7},{4,6},{5,1},{6,4},{7,3},{8,10},{9,13},{10,... | collective-permute-start | bytes 491528 | tf_op jit(solution)/shard_map/ppermute | solution.py:53
  29.6 7.3 %collective-permute-start.8 = (bf16[640,128]{1,0:T(8,128)(2,1)S(1)}, bf16[640,128]{1,0:T(8,128)(2,1)S(1)}, u32[]{:S(2)}, u32[]{:S(2)}) collective-permute-start(bf16[640,128]{1,0:T(8,128)(2,1)S(1)} %add.1.refs_0_), channel_id=1, source_target_pairs={{0,4},{1,3},{2,6},{3,1},{4,0},{5,7},{6,2},{7,5},{8,12},{9,11},{10,... | collective-permute-start | bytes 491528 | tf_op jit(solution)/shard_map/ppermute | solution.py:48
  37.2 2.0 %collective-permute-start.11 = (bf16[8,256,128]{2,1,0:T(8,128)(2,1)S(1)}, bf16[8,256,128]{2,1,0:T(8,128)(2,1)S(1)}, u32[]{:S(2)}, u32[]{:S(2)}) collective-permute-start(bf16[8,256,128]{2,1,0:T(8,128)(2,1)S(1)} %couple.1.scaled), channel_id=1, source_target_pairs={{0,1},{1,0},{2,3},{3,2},{4,5},{5,4},{6,7},{7,6},{8,9},{9,8},{10,11... | collective-permute-start | bytes 1572872 | tf_op jit(solution)/shard_map/ppermute | solution.py:35

commit v20 on v19

--- a/solution.py
+++ b/solution.py
@@ -190,42 +190,49 @@
     )(ours, theirs, quarters)
 
 
-def forward_kernel(ours, theirs, quarters, got, message):
+def forward_kernel(ours, theirs, quarters, got, *messages):
     core = place()[0]
     entries = ours.shape[0] // 2
+    half = entries // 2
     start = core * entries
     for entry in range(entries):
         rows = slice(entry * PCAP, (entry + 1) * PCAP)
         total = ours[start + entry] + theirs[start + entry].astype(jnp.float32)
-        message[rows] = (total + got[rows].astype(jnp.float32)).astype(message.dtype)
-    message[entries * PCAP :] = quarters[1 + core] + got[entries * PCAP :]
+        total = (total + got[rows].astype(jnp.float32)).astype(got.dtype)
+        at = entry % half
+        messages[entry // half][at * PCAP : (at + 1) * PCAP] = total
+    messages[1][half * PCAP :] = quarters[1 + core] + got[entries * PCAP :]
 
 
 def forward(ours, theirs, quarters, got):
+    rows, width = got.shape
+    half = ours.shape[0] // 4 * PCAP
     return pl.pallas_call(
         forward_kernel,
         in_specs=[VMEM] * 4,
-        out_specs=VMEM,
-        out_shape=jax.ShapeDtypeStruct(got.shape, got.dtype),
+        out_specs=[VMEM] * 2,
+        out_shape=[
+            jax.ShapeDtypeStruct((half, width), got.dtype),
+            jax.ShapeDtypeStruct((rows - half, width), got.dtype),
+        ],
         compiler_params=PARAMS,
         name="forward",
     )(ours, theirs, quarters, got)
 
 
-def fold_kernel(ours, theirs, quarters, *refs):
-    *gots, kept, message = refs
+def fold_kernel(ours, theirs, quarters, first, second, third, kept, message):
     entries = ours.shape[0]
+    half = entries // 2
     for entry in range(entries):
         rows = slice(entry * PCAP, (entry + 1) * PCAP)
-        total = ours[entry] + theirs[entry].astype(jnp.float32)
-        for got in gots:
-            total = total + got[rows].astype(jnp.float32)
+        total = ours[entry] + theirs[entry].astype(jnp.float32) + first[rows].astype(jnp.float32)
+        at = entry % half
+        got = (second, third)[entry // half][at * PCAP : (at + 1) * PCAP]
+        total = total + got.astype(jnp.float32)
         kept[rows] = total
         away = entry ^ 1
         message[away * PCAP : (away + 1) * PCAP] = total.astype(message.dtype)
-    table = quarters[0]
-    for got in gots:
-        table = table + got[entries * PCAP :]
+    table = quarters[0] + first[entries * PCAP :] + third[half * PCAP :]
     kept[entries * PCAP :] = table.astype(kept.dtype)
     message[entries * PCAP :] = table
 
@@ -431,11 +438,11 @@
     low_theirs, low_ours = partial((0,))
     low_theirs = swap_cores(low_theirs)
     got_first = swap_first(send(pair_ours, pair_theirs, quarters, (1, 2)))
-    message = forward(pair_ours, pair_theirs, quarters, got)
-    got_second = swap_second(message)
-    allowed = mask(counts, atom_of, message)
-
-    total, message = fold(low_ours, low_theirs, quarters, [got_first, got_second])
+    messages = forward(pair_ours, pair_theirs, quarters, got)
+    got_second = [swap_second(message) for message in messages]
+    allowed = mask(counts, atom_of, messages[0])
+
+    total, message = fold(low_ours, low_theirs, quarters, [got_first] + got_second)
     mine = add(total, swap_chips(message, SQUARE))
     distance = 2 * SQUARE
     while distance < chips:

time: 42.6 us -> 44.1 us (1.035)
  waiting for transfers between devices: 17.2 us -> 20.2 us
  starting transfers between devices: 14 us -> 12.5 us
    ppermute x2 -> x3, waiting for transfers between devices: 2.86 us -> 5.93 us  [swap_second(): return lax.ppermute(x, 'pw', [(i, i ^ (2, 4)[i % 2]) for i in range(count)])]
    ppermute x3, starting transfers between devices: 5.42 us -> 4.36 us  [swap_first(): return lax.ppermute(x, 'pw', [(i, i ^ (4, 2)[i % 2]) for i in range(count)])]
    ppermute x2 -> x3, starting transfers between devices: 3.07 us -> 2.62 us  [swap_second(): return lax.ppermute(x, 'pw', [(i, i ^ (2, 4)[i % 2]) for i in range(count)])]
  transfers between devices with their start and end apart: 12 -> 13, of which waited for: 7 -> 8; matrix products, arithmetic and copies ran while one was open for 0% -> 0% of each run, Pallas kernels for 17% -> 16%
where the time goes in v20:
time: 44.1 us; the launch traced here: 43.9 us
  waiting for transfers between devices  20.2 us (46%)
  starting transfers between devices  12.5 us (28%)
  Pallas kernels  10.9 us (25%)
    ppermute x7, waiting for transfers between devices, swap(): return lax.ppermute(x, 'pw', [(i, i ^ distance) for i in range(count)])  11.9 us
    ppermute x3, waiting for transfers between devices, swap_second(): return lax.ppermute(x, 'pw', [(i, i ^ (2, 4)[i % 2]) for i in range(count)])  5.93 us
    ppermute x7, starting transfers between devices, swap(): return lax.ppermute(x, 'pw', [(i, i ^ distance) for i in range(count)])  5.48 us
    ppermute x3, starting transfers between devices, swap_first(): return lax.ppermute(x, 'pw', [(i, i ^ (4, 2)[i % 2]) for i in range(count)])  4.36 us
    pallas_call x1, Pallas kernels, finish(): pl.pallas_call(finish_kernel, in_specs=[VMEM] * 3, out_specs=HBM, out_sha...  3.3 us
    pallas_call x3, Pallas kernels, project(): pl.pallas_call(kernel, in_specs=[VMEM, VMEM], out_specs=[VMEM, VMEM], out...  2.91 us
    ppermute x3, starting transfers between devices, swap_second(): return lax.ppermute(x, 'pw', [(i, i ^ (2, 4)[i % 2]) for i in range(count)])  2.62 us
    ppermute x3, waiting for transfers between devices, swap_first(): return lax.ppermute(x, 'pw', [(i, i ^ (4, 2)[i % 2]) for i in range(count)])  2.29 us
  transfers between devices with their start and end apart: 13, of which 8 were waited for; matrix products, arithmetic and copies ran while one was open for 0% of the time, Pallas kernels for 16%

profile of v20, /device:TPU:0, one launch (start us, length us, event | category | flops | bytes accessed | tf_op | source)
XLA Modules:
  0.0 43.9 jit_solution(9268443356336998994)
XLA Ops:
  0.0 0.0 copy-start
  0.0 0.5 %collective-permute-start.1 = (f32[256,256]{1,0:T(8,128)}, f32[256,256]{1,0:T(8,128)S(1)}, u32[]{:S(2)}, u32[]{:S(2)}) collective-permute-start(f32[256,256]{1,0:T(8,128)} %bitcast.1), channel_id=1, source_target_pairs={{0,1},{1,0},{2,3},{3,2},{4,5},{5,4},{6,7},{7,6},{8,9},{9,8},{10,11... | collective-permute-start | bytes 786440 | tf_op jit(solution)/shard_map/ppermute | solution.py:35
  0.5 2.2 %load.1.refs_0_ = bf16[512,2048]{1,0:T(8,128)(2,1)S(1)} custom-call(bf16[2048,512]{1,0:T(8,128)(2,1)} %projectors.5), custom_call_target="tpu_custom_call" | custom-call | tf_op jit(solution)/shard_map/load/pallas_call | solution.py:88
  2.7 0.1 copy-done
  2.8 1.3 %project.3 = (bf16[4,256,128]{2,1,0:T(8,128)(2,1)S(1)}, f32[4,256,128]{2,1,0:T(8,128)S(1)}) custom-call(bf16[512,2048]{1,0:T(8,128)(2,1)S(1)} %load.1.refs_0_, bf16[2048,1024]{1,0:T(8,128)(2,1)S(1)} %copy-done), custom_call_target="tpu_custom_call" | custom-call | flops 1073741824 | bytes 2097152 | tf_op jit(solution)/shard_map/project/pallas_call | solution.py:113
  4.2 0.0 copy-start.5
  4.2 0.0 copy-start.2
  4.2 0.5 %collective-permute-start = (bf16[4,256,128]{2,1,0:T(8,128)(2,1)S(1)}, bf16[4,256,128]{2,1,0:T(8,128)(2,1)S(1)}, u32[]{:S(2)}, u32[]{:S(2)}) collective-permute-start(bf16[4,256,128]{2,1,0:T(8,128)(2,1)S(1)} %get-tuple-element.18), channel_id=1, source_target_pairs={{0,1},{1,0},{2,3},{3,2},{4,5},{5,4},{6,7},{7,6},{8,9},{9,8},{10,11... | collective-permute-start | bytes 786440 | tf_op jit(solution)/shard_map/ppermute | solution.py:35
  4.7 0.8 %project.4 = (bf16[2,256,128]{2,1,0:T(8,128)(2,1)S(1)}, f32[2,256,128]{2,1,0:T(8,128)S(1)}) custom-call(bf16[512,2048]{1,0:T(8,128)(2,1)S(1)} %load.1.refs_0_, bf16[2048,1024]{1,0:T(8,128)(2,1)S(1)} %copy-done), custom_call_target="tpu_custom_call" | custom-call | flops 536870912 | bytes 2097152 | tf_op jit(solution)/shard_map/project/pallas_call | solution.py:113
  5.5 0.0 collective-permute-done.1.sibling
  5.5 0.1 collective-permute-start.2
  5.6 0.0 copy-done.5
  5.6 0.1 broadcast_in_dim.2.owners
  5.7 0.0 copy-done.2
  5.8 1.2 %collective-permute-done.2.refs_1_ = bf16[2,256,128]{2,1,0:T(8,128)(2,1)S(1)} collective-permute-done((bf16[2,256,128]{2,1,0:T(8,128)(2,1)S(1)}, bf16[2,256,128]{2,1,0:T(8,128)(2,1)S(1)}, u32[]{:S(2)}, u32[]{:S(2)}) %collective-permute-start.2) | collective-permute-done | bytes 131104 | tf_op jit(solution)/shard_map/ppermute | solution.py:35
  7.0 2.8 %collective-permute-start.3 = (bf16[640,128]{1,0:T(8,128)(2,1)S(1)}, bf16[640,128]{1,0:T(8,128)(2,1)S(1)}, u32[]{:S(2)}, u32[]{:S(2)}) collective-permute-start(bf16[640,128]{1,0:T(8,128)(2,1)S(1)} %send.2), channel_id=1, source_target_pairs={{0,4},{1,3},{2,6},{3,1},{4,0},{5,7},{6,2},{7,5},{8,12},{9,11},{10,... | collective-permute-start | bytes 491528 | tf_op jit(solution)/shard_map/ppermute | solution.py:48
  9.7 0.0 collective-permute-done.theirs.refs_1_
  9.8 0.0 copy-start.3
  9.8 0.0 copy-start.4
  9.8 0.0 copy-start.1
  9.8 0.1 collective-permute-start.5
  9.9 0.8 %project.5 = (bf16[2,256,128]{2,1,0:T(8,128)(2,1)S(1)}, f32[2,256,128]{2,1,0:T(8,128)S(1)}) custom-call(bf16[512,2048]{1,0:T(8,128)(2,1)S(1)} %load.1.refs_0_, bf16[2048,1024]{1,0:T(8,128)(2,1)S(1)} %copy-done), custom_call_target="tpu_custom_call" | custom-call | flops 536870912 | bytes 2097152 | tf_op jit(solution)/shard_map/project/pallas_call | solution.py:113
  10.7 0.1 collective-permute-start.4
  10.8 2.2 %collective-permute-done.3.got = bf16[640,128]{1,0:T(8,128)(2,1)S(1)} collective-permute-done((bf16[640,128]{1,0:T(8,128)(2,1)S(1)}, bf16[640,128]{1,0:T(8,128)(2,1)S(1)}, u32[]{:S(2)}, u32[]{:S(2)}) %collective-permute-start.3) | collective-permute-done | bytes 163872 | tf_op jit(solution)/shard_map/ppermute | solution.py:48
  13.0 0.1 forward.1
  13.1 2.0 %collective-permute-start.7 = (bf16[384,128]{1,0:T(8,128)(2,1)S(1)}, bf16[384,128]{1,0:T(8,128)(2,1)S(1)}, u32[]{:S(2)}, u32[]{:S(2)}) collective-permute-start(bf16[384,128]{1,0:T(8,128)(2,1)S(1)} %get-tuple-element.26), channel_id=1, source_target_pairs={{0,2},{1,5},{2,0},{3,7},{4,6},{5,1},{6,4},{7,3},{8,10},{9,13},{10,... | collective-permute-start | bytes 294920 | tf_op jit(solution)/shard_map/ppermute | solution.py:53
  15.1 0.1 collective-permute-start.6
  15.2 0.0 collective-permute-done.4.theirs
  15.2 0.0 collective-permute-done.5.first
  15.2 4.2 %collective-permute-done.6.second = bf16[256,128]{1,0:T(8,128)(2,1)S(1)} collective-permute-done((bf16[256,128]{1,0:T(8,128)(2,1)S(1)}, bf16[256,128]{1,0:T(8,128)(2,1)S(1)}, u32[]{:S(2)}, u32[]{:S(2)}) %collective-permute-start.6) | collective-permute-done | bytes 65568 | tf_op jit(solution)/shard_map/ppermute | solution.py:53
  19.4 0.0 collective-permute-done.7.third
  19.4 0.1 fold.1
  19.5 2.6 %collective-permute-start.8 = (bf16[640,128]{1,0:T(8,128)(2,1)S(1)}, bf16[640,128]{1,0:T(8,128)(2,1)S(1)}, u32[]{:S(2)}, u32[]{:S(2)}) collective-permute-start(bf16[640,128]{1,0:T(8,128)(2,1)S(1)} %get-tuple-element.28), channel_id=1, source_target_pairs={{0,8},{1,9},{2,10},{3,11},{4,12},{5,13},{6,14},{7,15},{8,0},{9,1},... | collective-permute-start | bytes 491528 | tf_op jit(solution)/shard_map/ppermute | solution.py:35
  22.1 6.4 %collective-permute-done.8.right = bf16[640,128]{1,0:T(8,128)(2,1)S(1)} collective-permute-done((bf16[640,128]{1,0:T(8,128)(2,1)S(1)}, bf16[640,128]{1,0:T(8,128)(2,1)S(1)}, u32[]{:S(2)}, u32[]{:S(2)}) %collective-permute-start.8) | collective-permute-done | bytes 163872 | tf_op jit(solution)/shard_map/ppermute | solution.py:35
  28.5 1.6 %collective-permute-start.11 = (bf16[640,128]{1,0:T(8,128)(2,1)S(1)}, bf16[640,128]{1,0:T(8,128)(2,1)S(1)}, u32[]{:S(2)}, u32[]{:S(2)}) collective-permute-start(bf16[640,128]{1,0:T(8,128)(2,1)S(1)} %add.1.refs_0_), channel_id=1, source_target_pairs={{0,6},{1,7},{2,4},{3,5},{4,2},{5,3},{6,0},{7,1},{8,14},{9,15},{10,... | collective-permute-start | bytes 491528 | tf_op jit(solution)/shard_map/ppermute | solution.py:35
  30.1 0.5 %collective-permute-start.10 = (bf16[640,128]{1,0:T(8,128)(2,1)S(1)}, bf16[640,128]{1,0:T(8,128)(2,1)S(1)}, u32[]{:S(2)}, u32[]{:S(2)}) collective-permute-start(bf16[640,128]{1,0:T(8,128)(2,1)S(1)} %add.1.refs_0_), channel_id=1, source_target_pairs={{0,2},{1,5},{2,0},{3,7},{4,6},{5,1},{6,4},{7,3},{8,10},{9,13},{10,... | collective-permute-start | bytes 491528 | tf_op jit(solution)/shard_map/ppermute | solution.py:53
  30.6 1.5 %collective-permute-start.9 = (bf16[640,128]{1,0:T(8,128)(2,1)S(1)}, bf16[640,128]{1,0:T(8,128)(2,1)S(1)}, u32[]{:S(2)}, u32[]{:S(2)}) collective-permute-start(bf16[640,128]{1,0:T(8,128)(2,1)S(1)} %add.1.refs_0_), channel_id=1, source_target_pairs={{0,4},{1,3},{2,6},{3,1},{4,0},{5,7},{6,2},{7,5},{8,12},{9,11},{10,... | collective-permute-start | bytes 491528 | tf_op jit(solution)/shard_map/ppermute | solution.py:48
  32.1 0.0 copy-done.3
  32.1 0.0 copy-done.4
  32.1 0.7 %mask.1.allowed = bf16[256,256]{1,0:T(8,128)(2,1)S(1)} custom-call(s32[2,4]{1,0:T(2,128)S(1)} %copy-done.4, s32[2,256]{1,0:T(2,128)S(1)} %copy-done.3, bf16[256,128]{1,0:T(8,128)(2,1)S(1)} %get-tuple-element.23.after), custom_call_target="tpu_custom_call" | custom-call | tf_op jit(solution)/shard_map/mask/pallas_call | solution.py:280
  32.7 3.8 %collective-permute-done.11.refs_3_ = bf16[640,128]{1,0:T(8,128)(2,1)S(1)} collective-permute-done((bf16[640,128]{1,0:T(8,128)(2,1)S(1)}, bf16[640,128]{1,0:T(8,128)(2,1)S(1)}, u32[]{:S(2)}, u32[]{:S(2)}) %collective-permute-start.11) | collective-permute-done | bytes 163872 | tf_op jit(solution)/shard_map/ppermute | solution.py:35
  36.5 1.7 %collective-permute-done.10.refs_2_ = bf16[640,128]{1,0:T(8,128)(2,1)S(1)} collective-permute-done((bf16[640,128]{1,0:T(8,128)(2,1)S(1)}, bf16[640,128]{1,0:T(8,128)(2,1)S(1)}, u32[]{:S(2)}, u32[]{:S(2)}) %collective-permute-start.10) | collective-permute-done | bytes 163872 | tf_op jit(solution)/shard_map/ppermute | solution.py:53
  38.3 0.1 collective-permute-done.9.refs_1_
  38.3 0.3 couple.1.scaled
  38.6 0.1 collective-permute-start.12
  38.7 0.0 copy-done.1
  38.7 1.3 %begin.1.begun = f32[4,2048,256]{2,1,0:T(8,128)S(1)} custom-call(bf16[2048,512]{1,0:T(8,128)(2,1)S(1)} %copy-done.1, bf16[8,256,128]{2,1,0:T(8,128)(2,1)S(1)} %couple.1.scaled), custom_call_target="tpu_custom_call" | custom-call | flops 1073741824 | bytes 2097152 | tf_op jit(solution)/shard_map/begin/pallas_call | solution.py:346
  40.0 0.6 %collective-permute-done.12.other = bf16[8,256,128]{2,1,0:T(8,128)(2,1)S(1)} collective-permute-done((bf16[8,256,128]{2,1,0:T(8,128)(2,1)S(1)}, bf16[8,256,128]{2,1,0:T(8,128)(2,1)S(1)}, u32[]{:S(2)}, u32[]{:S(2)}) %collective-permute-start.12) | collective-permute-done | bytes 524320 | tf_op jit(solution)/shard_map/ppermute | solution.py:35
  40.6 3.3 %finish.1 = bf16[2048,1024]{1,0:T(8,128)(2,1)} custom-call(bf16[2048,512]{1,0:T(8,128)(2,1)S(1)} %copy-done.1, f32[4,2048,256]{2,1,0:T(8,128)S(1)} %begin.1.begun, bf16[8,256,128]{2,1,0:T(8,128)(2,1)S(1)} %collective-permute-done.12.other), custom_call_target="tpu_custom_call" | custom-call | flops 1073741824 | bytes 6291456 | tf_op jit(solution)/shard_map/finish/pallas_call | solution.py:386
  (4 shorter events, 0.1 us)
Async XLA Ops:
  0.0 2.8 %copy-start = (bf16[2048,1024]{1,0:T(8,128)(2,1)S(1)}, bf16[2048,1024]{1,0:T(8,128)(2,1)}, u32[]{:S(2)}) copy-start(bf16[2048,1024]{1,0:T(8,128)(2,1)} %refs_1_.5) | copy-start | bytes 12582916
  0.0 5.5 %collective-permute-start.1 = (f32[256,256]{1,0:T(8,128)}, f32[256,256]{1,0:T(8,128)S(1)}, u32[]{:S(2)}, u32[]{:S(2)}) collective-permute-start(f32[256,256]{1,0:T(8,128)} %bitcast.1), channel_id=1, source_target_pairs={{0,1},{1,0},{2,3},{3,2},{4,5},{5,4},{6,7},{7,6},{8,9},{9,8},{10,11... | collective-permute-start | bytes 786440 | tf_op jit(solution)/shard_map/ppermute | solution.py:35
  4.2 1.5 %copy-start.5 = (s32[2]{0:T(128)S(1)}, s32[2]{0:T(128)}, u32[]{:S(2)}) copy-start(s32[2]{0:T(128)} %param.10) | copy-start | bytes 28
  4.2 1.5 %copy-start.2 = (f32[1,256,256]{2,1,0:T(8,128)S(1)}, f32[1,256,256]{2,1,0:T(8,128)}, u32[]{:S(2)}) copy-start(f32[1,256,256]{2,1,0:T(8,128)} %param.11) | copy-start | bytes 786436
  4.2 5.5 %collective-permute-start = (bf16[4,256,128]{2,1,0:T(8,128)(2,1)S(1)}, bf16[4,256,128]{2,1,0:T(8,128)(2,1)S(1)}, u32[]{:S(2)}, u32[]{:S(2)}) collective-permute-start(bf16[4,256,128]{2,1,0:T(8,128)(2,1)S(1)} %get-tuple-element.18), channel_id=1, source_target_pairs={{0,1},{1,0},{2,3},{3,2},{4,5},{5,4},{6,7},{7,6},{8,9},{9,8},{10,11... | collective-permute-start | bytes 786440 | tf_op jit(solution)/shard_map/ppermute | solution.py:35
  5.5 1.4 %collective-permute-start.2 = (bf16[2,256,128]{2,1,0:T(8,128)(2,1)S(1)}, bf16[2,256,128]{2,1,0:T(8,128)(2,1)S(1)}, u32[]{:S(2)}, u32[]{:S(2)}) collective-permute-start(bf16[2,256,128]{2,1,0:T(8,128)(2,1)S(1)} %get-tuple-element.22), channel_id=1, source_target_pairs={{0,1},{1,0},{2,3},{3,2},{4,5},{5,4},{6,7},{7,6},{8,9},{9,8},{10,11... | collective-permute-start | bytes 393224 | tf_op jit(solution)/shard_map/ppermute | solution.py:35
  7.0 6.1 %collective-permute-start.3 = (bf16[640,128]{1,0:T(8,128)(2,1)S(1)}, bf16[640,128]{1,0:T(8,128)(2,1)S(1)}, u32[]{:S(2)}, u32[]{:S(2)}) collective-permute-start(bf16[640,128]{1,0:T(8,128)(2,1)S(1)} %send.2), channel_id=1, source_target_pairs={{0,4},{1,3},{2,6},{3,1},{4,0},{5,7},{6,2},{7,5},{8,12},{9,11},{10,... | collective-permute-start | bytes 491528 | tf_op jit(solution)/shard_map/ppermute | solution.py:48
  9.8 22.3 %copy-start.3 = (s32[2,256]{1,0:T(2,128)S(1)}, s32[2,256]{1,0:T(2,128)}, u32[]{:S(2)}) copy-start(s32[2,256]{1,0:T(2,128)} %atom_of.1) | copy-start | bytes 6148
  9.8 22.3 %copy-start.4 = (s32[2,4]{1,0:T(2,128)S(1)}, s32[2,4]{1,0:T(2,128)}, u32[]{:S(2)}) copy-start(s32[2,4]{1,0:T(2,128)} %counts.1) | copy-start | bytes 100
  9.8 28.9 %copy-start.1 = (bf16[2048,512]{1,0:T(8,128)(2,1)S(1)}, bf16[2048,512]{1,0:T(8,128)(2,1)}, u32[]{:S(2)}) copy-start(bf16[2048,512]{1,0:T(8,128)(2,1)} %projectors.5) | copy-start | bytes 6291460
  9.8 5.4 %collective-permute-start.5 = (bf16[640,128]{1,0:T(8,128)(2,1)S(1)}, bf16[640,128]{1,0:T(8,128)(2,1)S(1)}, u32[]{:S(2)}, u32[]{:S(2)}) collective-permute-start(bf16[640,128]{1,0:T(8,128)(2,1)S(1)} %send.3), channel_id=1, source_target_pairs={{0,4},{1,3},{2,6},{3,1},{4,0},{5,7},{6,2},{7,5},{8,12},{9,11},{10,... | collective-permute-start | bytes 491528 | tf_op jit(solution)/shard_map/ppermute | solution.py:48
  10.7 4.5 %collective-permute-start.4 = (bf16[2,256,128]{2,1,0:T(8,128)(2,1)S(1)}, bf16[2,256,128]{2,1,0:T(8,128)(2,1)S(1)}, u32[]{:S(2)}, u32[]{:S(2)}) collective-permute-start(bf16[2,256,128]{2,1,0:T(8,128)(2,1)S(1)} %get-tuple-element.25), channel_id=1, source_target_pairs={{0,1},{1,0},{2,3},{3,2},{4,5},{5,4},{6,7},{7,6},{8,9},{9,8},{10,11... | collective-permute-start | bytes 393224 | tf_op jit(solution)/shard_map/ppermute | solution.py:35
  13.1 6.3 %collective-permute-start.7 = (bf16[384,128]{1,0:T(8,128)(2,1)S(1)}, bf16[384,128]{1,0:T(8,128)(2,1)S(1)}, u32[]{:S(2)}, u32[]{:S(2)}) collective-permute-start(bf16[384,128]{1,0:T(8,128)(2,1)S(1)} %get-tuple-element.26), channel_id=1, source_target_pairs={{0,2},{1,5},{2,0},{3,7},{4,6},{5,1},{6,4},{7,3},{8,10},{9,13},{10,... | collective-permute-start | bytes 294920 | tf_op jit(solution)/shard_map/ppermute | solution.py:53
  15.1 4.3 %collective-permute-start.6 = (bf16[256,128]{1,0:T(8,128)(2,1)S(1)}, bf16[256,128]{1,0:T(8,128)(2,1)S(1)}, u32[]{:S(2)}, u32[]{:S(2)}) collective-permute-start(bf16[256,128]{1,0:T(8,128)(2,1)S(1)} %get-tuple-element.23.after), channel_id=1, source_target_pairs={{0,2},{1,5},{2,0},{3,7},{4,6},{5,1},{6,4},{7,3},{8,10},{9,13},{10,... | collective-permute-start | bytes 196616 | tf_op jit(solution)/shard_map/ppermute | solution.py:53
  19.5 9.0 %collective-permute-start.8 = (bf16[640,128]{1,0:T(8,128)(2,1)S(1)}, bf16[640,128]{1,0:T(8,128)(2,1)S(1)}, u32[]{:S(2)}, u32[]{:S(2)}) collective-permute-start(bf16[640,128]{1,0:T(8,128)(2,1)S(1)} %get-tuple-element.28), channel_id=1, source_target_pairs={{0,8},{1,9},{2,10},{3,11},{4,12},{5,13},{6,14},{7,15},{8,0},{9,1},... | collective-permute-start | bytes 491528 | tf_op jit(solution)/shard_map/ppermute | solution.py:35
  28.5 8.0 %collective-permute-start.11 = (bf16[640,128]{1,0:T(8,128)(2,1)S(1)}, bf16[640,128]{1,0:T(8,128)(2,1)S(1)}, u32[]{:S(2)}, u32[]{:S(2)}) collective-permute-start(bf16[640,128]{1,0:T(8,128)(2,1)S(1)} %add.1.refs_0_), channel_id=1, source_target_pairs={{0,6},{1,7},{2,4},{3,5},{4,2},{5,3},{6,0},{7,1},{8,14},{9,15},{10,... | collective-permute-start | bytes 491528 | tf_op jit(solution)/shard_map/ppermute | solution.py:35
  30.1 8.2 %collective-permute-start.10 = (bf16[640,128]{1,0:T(8,128)(2,1)S(1)}, bf16[640,128]{1,0:T(8,128)(2,1)S(1)}, u32[]{:S(2)}, u32[]{:S(2)}) collective-permute-start(bf16[640,128]{1,0:T(8,128)(2,1)S(1)} %add.1.refs_0_), channel_id=1, source_target_pairs={{0,2},{1,5},{2,0},{3,7},{4,6},{5,1},{6,4},{7,3},{8,10},{9,13},{10,... | collective-permute-start | bytes 491528 | tf_op jit(solution)/shard_map/ppermute | solution.py:53
  30.6 7.7 %collective-permute-start.9 = (bf16[640,128]{1,0:T(8,128)(2,1)S(1)}, bf16[640,128]{1,0:T(8,128)(2,1)S(1)}, u32[]{:S(2)}, u32[]{:S(2)}) collective-permute-start(bf16[640,128]{1,0:T(8,128)(2,1)S(1)} %add.1.refs_0_), channel_id=1, source_target_pairs={{0,4},{1,3},{2,6},{3,1},{4,0},{5,7},{6,2},{7,5},{8,12},{9,11},{10,... | collective-permute-start | bytes 491528 | tf_op jit(solution)/shard_map/ppermute | solution.py:48
  38.6 2.0 %collective-permute-start.12 = (bf16[8,256,128]{2,1,0:T(8,128)(2,1)S(1)}, bf16[8,256,128]{2,1,0:T(8,128)(2,1)S(1)}, u32[]{:S(2)}, u32[]{:S(2)}) collective-permute-start(bf16[8,256,128]{2,1,0:T(8,128)(2,1)S(1)} %couple.1.scaled), channel_id=1, source_target_pairs={{0,1},{1,0},{2,3},{3,2},{4,5},{5,4},{6,7},{7,6},{8,9},{9,8},{10,11... | collective-permute-start | bytes 1572872 | tf_op jit(solution)/shard_map/ppermute | solution.py:35

commit v21 on v19

--- a/solution.py
+++ b/solution.py
@@ -11,8 +11,8 @@
 LANES = 128
 SQUARE = 4
 QUARTER = PCAP // SQUARE
-ROW_BLOCK = 512
-ROW_BLOCKS = (512, 512, 512, 256, 256)
+ROW_BLOCK = 1024
+ROW_BLOCKS = (512, 1024, 256, 256)
 COPY_ROWS = 128
 PARAMS = pltpu.CompilerParams(vmem_limit_bytes=40 * 1024 * 1024)
 VMEM = pl.BlockSpec(memory_space=pltpu.VMEM)

time: 42.6 us -> 43 us (level)
  no operation moved by 1% of the time
where the time goes in v21:
time: 43 us; the launch traced here: 42.8 us
  waiting for transfers between devices  17.2 us (40%)
  starting transfers between devices  14 us (33%)
  Pallas kernels  11.3 us (26%)
    ppermute x7, waiting for transfers between devices, swap(): return lax.ppermute(x, 'pw', [(i, i ^ distance) for i in range(count)])  12 us
    ppermute x7, starting transfers between devices, swap(): return lax.ppermute(x, 'pw', [(i, i ^ distance) for i in range(count)])  5.51 us
    ppermute x3, starting transfers between devices, swap_first(): return lax.ppermute(x, 'pw', [(i, i ^ (4, 2)[i % 2]) for i in range(count)])  5.42 us
    pallas_call x1, Pallas kernels, finish(): pl.pallas_call(finish_kernel, in_specs=[VMEM] * 3, out_specs=HBM, out_sha...  3.66 us
    ppermute x2, starting transfers between devices, swap_second(): return lax.ppermute(x, 'pw', [(i, i ^ (2, 4)[i % 2]) for i in range(count)])  3.07 us
    pallas_call x3, Pallas kernels, project(): pl.pallas_call(kernel, in_specs=[VMEM, VMEM], out_specs=[VMEM, VMEM], out...  2.91 us
    ppermute x2, waiting for transfers between devices, swap_second(): return lax.ppermute(x, 'pw', [(i, i ^ (2, 4)[i % 2]) for i in range(count)])  2.86 us
    ppermute x3, waiting for transfers between devices, swap_first(): return lax.ppermute(x, 'pw', [(i, i ^ (4, 2)[i % 2]) for i in range(count)])  2.28 us
  transfers between devices with their start and end apart: 12, of which 7 were waited for; matrix products, arithmetic and copies ran while one was open for 0% of the time, Pallas kernels for 17%

profile of v21, /device:TPU:0, one launch (start us, length us, event | category | flops | bytes accessed | tf_op | source)
XLA Modules:
  0.0 42.8 jit_solution(11572284255434150937)
XLA Ops:
  0.0 0.0 copy-start
  0.0 0.5 %collective-permute-start.1 = (f32[256,256]{1,0:T(8,128)}, f32[256,256]{1,0:T(8,128)S(1)}, u32[]{:S(2)}, u32[]{:S(2)}) collective-permute-start(f32[256,256]{1,0:T(8,128)} %bitcast.1), channel_id=1, source_target_pairs={{0,1},{1,0},{2,3},{3,2},{4,5},{5,4},{6,7},{7,6},{8,9},{9,8},{10,11... | collective-permute-start | bytes 786440 | tf_op jit(solution)/shard_map/ppermute | solution.py:35
  0.5 2.2 %load.1.refs_0_ = bf16[512,2048]{1,0:T(8,128)(2,1)S(1)} custom-call(bf16[2048,512]{1,0:T(8,128)(2,1)} %projectors.5), custom_call_target="tpu_custom_call" | custom-call | tf_op jit(solution)/shard_map/load/pallas_call | solution.py:88
  2.7 0.1 copy-done
  2.8 0.8 %project.4 = (bf16[2,256,128]{2,1,0:T(8,128)(2,1)S(1)}, f32[2,256,128]{2,1,0:T(8,128)S(1)}) custom-call(bf16[512,2048]{1,0:T(8,128)(2,1)S(1)} %load.1.refs_0_, bf16[2048,1024]{1,0:T(8,128)(2,1)S(1)} %copy-done), custom_call_target="tpu_custom_call" | custom-call | flops 536870912 | bytes 2097152 | tf_op jit(solution)/shard_map/project/pallas_call | solution.py:113
  3.6 0.0 copy-start.5
  3.6 0.0 copy-start.2
  3.6 0.0 collective-permute-done.1.sibling
  3.6 0.5 %collective-permute-start.2 = (bf16[2,256,128]{2,1,0:T(8,128)(2,1)S(1)}, bf16[2,256,128]{2,1,0:T(8,128)(2,1)S(1)}, u32[]{:S(2)}, u32[]{:S(2)}) collective-permute-start(bf16[2,256,128]{2,1,0:T(8,128)(2,1)S(1)} %get-tuple-element.20), channel_id=1, source_target_pairs={{0,1},{1,0},{2,3},{3,2},{4,5},{5,4},{6,7},{7,6},{8,9},{9,8},{10,11... | collective-permute-start | bytes 393224 | tf_op jit(solution)/shard_map/ppermute | solution.py:35
  4.2 1.3 %project.3 = (bf16[4,256,128]{2,1,0:T(8,128)(2,1)S(1)}, f32[4,256,128]{2,1,0:T(8,128)S(1)}) custom-call(bf16[512,2048]{1,0:T(8,128)(2,1)S(1)} %load.1.refs_0_, bf16[2048,1024]{1,0:T(8,128)(2,1)S(1)} %copy-done), custom_call_target="tpu_custom_call" | custom-call | flops 1073741824 | bytes 2097152 | tf_op jit(solution)/shard_map/project/pallas_call | solution.py:113
  5.5 0.1 collective-permute-start
  5.6 0.0 copy-done.5
  5.6 0.1 broadcast_in_dim.2.owners
  5.7 0.0 copy-done.2
  5.7 0.0 collective-permute-done.2.refs_1_
  5.8 3.1 %collective-permute-start.3 = (bf16[640,128]{1,0:T(8,128)(2,1)S(1)}, bf16[640,128]{1,0:T(8,128)(2,1)S(1)}, u32[]{:S(2)}, u32[]{:S(2)}) collective-permute-start(bf16[640,128]{1,0:T(8,128)(2,1)S(1)} %send.2), channel_id=1, source_target_pairs={{0,4},{1,3},{2,6},{3,1},{4,0},{5,7},{6,2},{7,5},{8,12},{9,11},{10,... | collective-permute-start | bytes 491528 | tf_op jit(solution)/shard_map/ppermute | solution.py:48
  8.9 0.0 collective-permute-done.theirs.refs_1_
  8.9 1.0 %collective-permute-start.5 = (bf16[640,128]{1,0:T(8,128)(2,1)S(1)}, bf16[640,128]{1,0:T(8,128)(2,1)S(1)}, u32[]{:S(2)}, u32[]{:S(2)}) collective-permute-start(bf16[640,128]{1,0:T(8,128)(2,1)S(1)} %send.3), channel_id=1, source_target_pairs={{0,4},{1,3},{2,6},{3,1},{4,0},{5,7},{6,2},{7,5},{8,12},{9,11},{10,... | collective-permute-start | bytes 491528 | tf_op jit(solution)/shard_map/ppermute | solution.py:48
  9.9 2.3 %collective-permute-done.3.got = bf16[640,128]{1,0:T(8,128)(2,1)S(1)} collective-permute-done((bf16[640,128]{1,0:T(8,128)(2,1)S(1)}, bf16[640,128]{1,0:T(8,128)(2,1)S(1)}, u32[]{:S(2)}, u32[]{:S(2)}) %collective-permute-start.3) | collective-permute-done | bytes 163872 | tf_op jit(solution)/shard_map/ppermute | solution.py:48
  12.2 0.1 forward.1.after
  12.2 0.0 copy-start.3
  12.2 0.0 copy-start.4
  12.2 0.0 copy-start.1
  12.3 2.0 %collective-permute-start.6 = (bf16[640,128]{1,0:T(8,128)(2,1)S(1)}, bf16[640,128]{1,0:T(8,128)(2,1)S(1)}, u32[]{:S(2)}, u32[]{:S(2)}) collective-permute-start(bf16[640,128]{1,0:T(8,128)(2,1)S(1)} %forward.1.after), channel_id=1, source_target_pairs={{0,2},{1,5},{2,0},{3,7},{4,6},{5,1},{6,4},{7,3},{8,10},{9,13},{10,... | collective-permute-start | bytes 491528 | tf_op jit(solution)/shard_map/ppermute | solution.py:53
  14.3 0.8 %project.5 = (bf16[2,256,128]{2,1,0:T(8,128)(2,1)S(1)}, f32[2,256,128]{2,1,0:T(8,128)S(1)}) custom-call(bf16[512,2048]{1,0:T(8,128)(2,1)S(1)} %load.1.refs_0_, bf16[2048,1024]{1,0:T(8,128)(2,1)S(1)} %copy-done), custom_call_target="tpu_custom_call" | custom-call | flops 536870912 | bytes 2097152 | tf_op jit(solution)/shard_map/project/pallas_call | solution.py:113
  15.1 0.1 collective-permute-start.4
  15.2 1.3 %collective-permute-done.4.theirs = bf16[2,256,128]{2,1,0:T(8,128)(2,1)S(1)} collective-permute-done((bf16[2,256,128]{2,1,0:T(8,128)(2,1)S(1)}, bf16[2,256,128]{2,1,0:T(8,128)(2,1)S(1)}, u32[]{:S(2)}, u32[]{:S(2)}) %collective-permute-start.4) | collective-permute-done | bytes 131104 | tf_op jit(solution)/shard_map/ppermute | solution.py:35
  16.5 0.0 collective-permute-done.5.refs_0_
  16.5 1.1 %collective-permute-done.6.refs_1_ = bf16[640,128]{1,0:T(8,128)(2,1)S(1)} collective-permute-done((bf16[640,128]{1,0:T(8,128)(2,1)S(1)}, bf16[640,128]{1,0:T(8,128)(2,1)S(1)}, u32[]{:S(2)}, u32[]{:S(2)}) %collective-permute-start.6) | collective-permute-done | bytes 163872 | tf_op jit(solution)/shard_map/ppermute | solution.py:53
  17.6 0.1 fold.1
  17.7 3.1 %collective-permute-start.7 = (bf16[640,128]{1,0:T(8,128)(2,1)S(1)}, bf16[640,128]{1,0:T(8,128)(2,1)S(1)}, u32[]{:S(2)}, u32[]{:S(2)}) collective-permute-start(bf16[640,128]{1,0:T(8,128)(2,1)S(1)} %get-tuple-element.24), channel_id=1, source_target_pairs={{0,8},{1,9},{2,10},{3,11},{4,12},{5,13},{6,14},{7,15},{8,0},{9,1},... | collective-permute-start | bytes 491528 | tf_op jit(solution)/shard_map/ppermute | solution.py:35
  20.8 6.5 %collective-permute-done.7.right = bf16[640,128]{1,0:T(8,128)(2,1)S(1)} collective-permute-done((bf16[640,128]{1,0:T(8,128)(2,1)S(1)}, bf16[640,128]{1,0:T(8,128)(2,1)S(1)}, u32[]{:S(2)}, u32[]{:S(2)}) %collective-permute-start.7) | collective-permute-done | bytes 163872 | tf_op jit(solution)/shard_map/ppermute | solution.py:35
  27.3 1.2 %collective-permute-start.10 = (bf16[640,128]{1,0:T(8,128)(2,1)S(1)}, bf16[640,128]{1,0:T(8,128)(2,1)S(1)}, u32[]{:S(2)}, u32[]{:S(2)}) collective-permute-start(bf16[640,128]{1,0:T(8,128)(2,1)S(1)} %add.1.refs_0_), channel_id=1, source_target_pairs={{0,6},{1,7},{2,4},{3,5},{4,2},{5,3},{6,0},{7,1},{8,14},{9,15},{10,... | collective-permute-start | bytes 491528 | tf_op jit(solution)/shard_map/ppermute | solution.py:35
  28.5 1.0 %collective-permute-start.9 = (bf16[640,128]{1,0:T(8,128)(2,1)S(1)}, bf16[640,128]{1,0:T(8,128)(2,1)S(1)}, u32[]{:S(2)}, u32[]{:S(2)}) collective-permute-start(bf16[640,128]{1,0:T(8,128)(2,1)S(1)} %add.1.refs_0_), channel_id=1, source_target_pairs={{0,2},{1,5},{2,0},{3,7},{4,6},{5,1},{6,4},{7,3},{8,10},{9,13},{10,... | collective-permute-start | bytes 491528 | tf_op jit(solution)/shard_map/ppermute | solution.py:53
  29.6 1.4 %collective-permute-start.8 = (bf16[640,128]{1,0:T(8,128)(2,1)S(1)}, bf16[640,128]{1,0:T(8,128)(2,1)S(1)}, u32[]{:S(2)}, u32[]{:S(2)}) collective-permute-start(bf16[640,128]{1,0:T(8,128)(2,1)S(1)} %add.1.refs_0_), channel_id=1, source_target_pairs={{0,4},{1,3},{2,6},{3,1},{4,0},{5,7},{6,2},{7,5},{8,12},{9,11},{10,... | collective-permute-start | bytes 491528 | tf_op jit(solution)/shard_map/ppermute | solution.py:48
  30.9 0.0 copy-done.3
  30.9 0.0 copy-done.4
  30.9 0.7 %mask.1.allowed = bf16[256,256]{1,0:T(8,128)(2,1)S(1)} custom-call(s32[2,4]{1,0:T(2,128)S(1)} %copy-done.4, s32[2,256]{1,0:T(2,128)S(1)} %copy-done.3, bf16[640,128]{1,0:T(8,128)(2,1)S(1)} %forward.1.after), custom_call_target="tpu_custom_call" | custom-call | tf_op jit(solution)/shard_map/mask/pallas_call | solution.py:273
  31.6 3.6 %collective-permute-done.10.refs_3_ = bf16[640,128]{1,0:T(8,128)(2,1)S(1)} collective-permute-done((bf16[640,128]{1,0:T(8,128)(2,1)S(1)}, bf16[640,128]{1,0:T(8,128)(2,1)S(1)}, u32[]{:S(2)}, u32[]{:S(2)}) %collective-permute-start.10) | collective-permute-done | bytes 163872 | tf_op jit(solution)/shard_map/ppermute | solution.py:35
  35.1 1.7 %collective-permute-done.9.refs_2_ = bf16[640,128]{1,0:T(8,128)(2,1)S(1)} collective-permute-done((bf16[640,128]{1,0:T(8,128)(2,1)S(1)}, bf16[640,128]{1,0:T(8,128)(2,1)S(1)}, u32[]{:S(2)}, u32[]{:S(2)}) %collective-permute-start.9) | collective-permute-done | bytes 163872 | tf_op jit(solution)/shard_map/ppermute | solution.py:53
  36.9 0.0 collective-permute-done.8.refs_1_
  36.9 0.3 couple.1.scaled
  37.2 0.1 collective-permute-start.11
  37.3 0.0 copy-done.1
  37.3 1.2 %begin.1.begun = f32[4,2048,256]{2,1,0:T(8,128)S(1)} custom-call(bf16[2048,512]{1,0:T(8,128)(2,1)S(1)} %copy-done.1, bf16[8,256,128]{2,1,0:T(8,128)(2,1)S(1)} %couple.1.scaled), custom_call_target="tpu_custom_call" | custom-call | flops 1073741824 | bytes 2097152 | tf_op jit(solution)/shard_map/begin/pallas_call | solution.py:339
  38.5 0.6 %collective-permute-done.11.other = bf16[8,256,128]{2,1,0:T(8,128)(2,1)S(1)} collective-permute-done((bf16[8,256,128]{2,1,0:T(8,128)(2,1)S(1)}, bf16[8,256,128]{2,1,0:T(8,128)(2,1)S(1)}, u32[]{:S(2)}, u32[]{:S(2)}) %collective-permute-start.11) | collective-permute-done | bytes 524320 | tf_op jit(solution)/shard_map/ppermute | solution.py:35
  39.2 3.7 %finish.1 = bf16[2048,1024]{1,0:T(8,128)(2,1)} custom-call(bf16[2048,512]{1,0:T(8,128)(2,1)S(1)} %copy-done.1, f32[4,2048,256]{2,1,0:T(8,128)S(1)} %begin.1.begun, bf16[8,256,128]{2,1,0:T(8,128)(2,1)S(1)} %collective-permute-done.11.other), custom_call_target="tpu_custom_call" | custom-call | flops 1073741824 | bytes 6291456 | tf_op jit(solution)/shard_map/finish/pallas_call | solution.py:379
  (4 shorter events, 0.1 us)
Async XLA Ops:
  0.0 2.8 %copy-start = (bf16[2048,1024]{1,0:T(8,128)(2,1)S(1)}, bf16[2048,1024]{1,0:T(8,128)(2,1)}, u32[]{:S(2)}) copy-start(bf16[2048,1024]{1,0:T(8,128)(2,1)} %refs_1_.5) | copy-start | bytes 12582916
  0.0 3.6 %collective-permute-start.1 = (f32[256,256]{1,0:T(8,128)}, f32[256,256]{1,0:T(8,128)S(1)}, u32[]{:S(2)}, u32[]{:S(2)}) collective-permute-start(f32[256,256]{1,0:T(8,128)} %bitcast.1), channel_id=1, source_target_pairs={{0,1},{1,0},{2,3},{3,2},{4,5},{5,4},{6,7},{7,6},{8,9},{9,8},{10,11... | collective-permute-start | bytes 786440 | tf_op jit(solution)/shard_map/ppermute | solution.py:35
  3.6 2.0 %copy-start.5 = (s32[2]{0:T(128)S(1)}, s32[2]{0:T(128)}, u32[]{:S(2)}) copy-start(s32[2]{0:T(128)} %param.10) | copy-start | bytes 28
  3.6 2.1 %copy-start.2 = (f32[1,256,256]{2,1,0:T(8,128)S(1)}, f32[1,256,256]{2,1,0:T(8,128)}, u32[]{:S(2)}) copy-start(f32[1,256,256]{2,1,0:T(8,128)} %param.11) | copy-start | bytes 786436
  3.6 2.1 %collective-permute-start.2 = (bf16[2,256,128]{2,1,0:T(8,128)(2,1)S(1)}, bf16[2,256,128]{2,1,0:T(8,128)(2,1)S(1)}, u32[]{:S(2)}, u32[]{:S(2)}) collective-permute-start(bf16[2,256,128]{2,1,0:T(8,128)(2,1)S(1)} %get-tuple-element.20), channel_id=1, source_target_pairs={{0,1},{1,0},{2,3},{3,2},{4,5},{5,4},{6,7},{7,6},{8,9},{9,8},{10,11... | collective-permute-start | bytes 393224 | tf_op jit(solution)/shard_map/ppermute | solution.py:35
  5.5 3.4 %collective-permute-start = (bf16[4,256,128]{2,1,0:T(8,128)(2,1)S(1)}, bf16[4,256,128]{2,1,0:T(8,128)(2,1)S(1)}, u32[]{:S(2)}, u32[]{:S(2)}) collective-permute-start(bf16[4,256,128]{2,1,0:T(8,128)(2,1)S(1)} %get-tuple-element.16), channel_id=1, source_target_pairs={{0,1},{1,0},{2,3},{3,2},{4,5},{5,4},{6,7},{7,6},{8,9},{9,8},{10,11... | collective-permute-start | bytes 786440 | tf_op jit(solution)/shard_map/ppermute | solution.py:35
  5.8 6.4 %collective-permute-start.3 = (bf16[640,128]{1,0:T(8,128)(2,1)S(1)}, bf16[640,128]{1,0:T(8,128)(2,1)S(1)}, u32[]{:S(2)}, u32[]{:S(2)}) collective-permute-start(bf16[640,128]{1,0:T(8,128)(2,1)S(1)} %send.2), channel_id=1, source_target_pairs={{0,4},{1,3},{2,6},{3,1},{4,0},{5,7},{6,2},{7,5},{8,12},{9,11},{10,... | collective-permute-start | bytes 491528 | tf_op jit(solution)/shard_map/ppermute | solution.py:48
  8.9 7.6 %collective-permute-start.5 = (bf16[640,128]{1,0:T(8,128)(2,1)S(1)}, bf16[640,128]{1,0:T(8,128)(2,1)S(1)}, u32[]{:S(2)}, u32[]{:S(2)}) collective-permute-start(bf16[640,128]{1,0:T(8,128)(2,1)S(1)} %send.3), channel_id=1, source_target_pairs={{0,4},{1,3},{2,6},{3,1},{4,0},{5,7},{6,2},{7,5},{8,12},{9,11},{10,... | collective-permute-start | bytes 491528 | tf_op jit(solution)/shard_map/ppermute | solution.py:48
  12.2 18.7 %copy-start.3 = (s32[2,256]{1,0:T(2,128)S(1)}, s32[2,256]{1,0:T(2,128)}, u32[]{:S(2)}) copy-start(s32[2,256]{1,0:T(2,128)} %atom_of.1) | copy-start | bytes 6148
  12.2 18.7 %copy-start.4 = (s32[2,4]{1,0:T(2,128)S(1)}, s32[2,4]{1,0:T(2,128)}, u32[]{:S(2)}) copy-start(s32[2,4]{1,0:T(2,128)} %counts.1) | copy-start | bytes 100
  12.2 25.0 %copy-start.1 = (bf16[2048,512]{1,0:T(8,128)(2,1)S(1)}, bf16[2048,512]{1,0:T(8,128)(2,1)}, u32[]{:S(2)}) copy-start(bf16[2048,512]{1,0:T(8,128)(2,1)} %projectors.5) | copy-start | bytes 6291460
  12.3 5.4 %collective-permute-start.6 = (bf16[640,128]{1,0:T(8,128)(2,1)S(1)}, bf16[640,128]{1,0:T(8,128)(2,1)S(1)}, u32[]{:S(2)}, u32[]{:S(2)}) collective-permute-start(bf16[640,128]{1,0:T(8,128)(2,1)S(1)} %forward.1.after), channel_id=1, source_target_pairs={{0,2},{1,5},{2,0},{3,7},{4,6},{5,1},{6,4},{7,3},{8,10},{9,13},{10,... | collective-permute-start | bytes 491528 | tf_op jit(solution)/shard_map/ppermute | solution.py:53
  15.1 1.4 %collective-permute-start.4 = (bf16[2,256,128]{2,1,0:T(8,128)(2,1)S(1)}, bf16[2,256,128]{2,1,0:T(8,128)(2,1)S(1)}, u32[]{:S(2)}, u32[]{:S(2)}) collective-permute-start(bf16[2,256,128]{2,1,0:T(8,128)(2,1)S(1)} %get-tuple-element.22), channel_id=1, source_target_pairs={{0,1},{1,0},{2,3},{3,2},{4,5},{5,4},{6,7},{7,6},{8,9},{9,8},{10,11... | collective-permute-start | bytes 393224 | tf_op jit(solution)/shard_map/ppermute | solution.py:35
  17.7 9.6 %collective-permute-start.7 = (bf16[640,128]{1,0:T(8,128)(2,1)S(1)}, bf16[640,128]{1,0:T(8,128)(2,1)S(1)}, u32[]{:S(2)}, u32[]{:S(2)}) collective-permute-start(bf16[640,128]{1,0:T(8,128)(2,1)S(1)} %get-tuple-element.24), channel_id=1, source_target_pairs={{0,8},{1,9},{2,10},{3,11},{4,12},{5,13},{6,14},{7,15},{8,0},{9,1},... | collective-permute-start | bytes 491528 | tf_op jit(solution)/shard_map/ppermute | solution.py:35
  27.3 7.8 %collective-permute-start.10 = (bf16[640,128]{1,0:T(8,128)(2,1)S(1)}, bf16[640,128]{1,0:T(8,128)(2,1)S(1)}, u32[]{:S(2)}, u32[]{:S(2)}) collective-permute-start(bf16[640,128]{1,0:T(8,128)(2,1)S(1)} %add.1.refs_0_), channel_id=1, source_target_pairs={{0,6},{1,7},{2,4},{3,5},{4,2},{5,3},{6,0},{7,1},{8,14},{9,15},{10,... | collective-permute-start | bytes 491528 | tf_op jit(solution)/shard_map/ppermute | solution.py:35
  28.5 8.3 %collective-permute-start.9 = (bf16[640,128]{1,0:T(8,128)(2,1)S(1)}, bf16[640,128]{1,0:T(8,128)(2,1)S(1)}, u32[]{:S(2)}, u32[]{:S(2)}) collective-permute-start(bf16[640,128]{1,0:T(8,128)(2,1)S(1)} %add.1.refs_0_), channel_id=1, source_target_pairs={{0,2},{1,5},{2,0},{3,7},{4,6},{5,1},{6,4},{7,3},{8,10},{9,13},{10,... | collective-permute-start | bytes 491528 | tf_op jit(solution)/shard_map/ppermute | solution.py:53
  29.6 7.3 %collective-permute-start.8 = (bf16[640,128]{1,0:T(8,128)(2,1)S(1)}, bf16[640,128]{1,0:T(8,128)(2,1)S(1)}, u32[]{:S(2)}, u32[]{:S(2)}) collective-permute-start(bf16[640,128]{1,0:T(8,128)(2,1)S(1)} %add.1.refs_0_), channel_id=1, source_target_pairs={{0,4},{1,3},{2,6},{3,1},{4,0},{5,7},{6,2},{7,5},{8,12},{9,11},{10,... | collective-permute-start | bytes 491528 | tf_op jit(solution)/shard_map/ppermute | solution.py:48
  37.2 2.0 %collective-permute-start.11 = (bf16[8,256,128]{2,1,0:T(8,128)(2,1)S(1)}, bf16[8,256,128]{2,1,0:T(8,128)(2,1)S(1)}, u32[]{:S(2)}, u32[]{:S(2)}) collective-permute-start(bf16[8,256,128]{2,1,0:T(8,128)(2,1)S(1)} %couple.1.scaled), channel_id=1, source_target_pairs={{0,1},{1,0},{2,3},{3,2},{4,5},{5,4},{6,7},{7,6},{8,9},{9,8},{10,11... | collective-permute-start | bytes 1572872 | tf_op jit(solution)/shard_map/ppermute | solution.py:35

commit v22 on v19

--- a/solution.py
+++ b/solution.py
@@ -12,7 +12,7 @@
 SQUARE = 4
 QUARTER = PCAP // SQUARE
 ROW_BLOCK = 512
-ROW_BLOCKS = (512, 512, 512, 256, 256)
+ROW_BLOCKS = (256,) * 8
 COPY_ROWS = 128
 PARAMS = pltpu.CompilerParams(vmem_limit_bytes=40 * 1024 * 1024)
 VMEM = pl.BlockSpec(memory_space=pltpu.VMEM)

time: 42.6 us -> 42.4 us (level)
  no operation moved by 1% of the time
where the time goes in v22:
time: 42.4 us; the launch traced here: 42.3 us
  waiting for transfers between devices  17.2 us (41%)
  starting transfers between devices  14 us (33%)
  Pallas kernels  10.7 us (25%)
    ppermute x7, waiting for transfers between devices, swap(): return lax.ppermute(x, 'pw', [(i, i ^ distance) for i in range(count)])  12 us
    ppermute x7, starting transfers between devices, swap(): return lax.ppermute(x, 'pw', [(i, i ^ distance) for i in range(count)])  5.51 us
    ppermute x3, starting transfers between devices, swap_first(): return lax.ppermute(x, 'pw', [(i, i ^ (4, 2)[i % 2]) for i in range(count)])  5.42 us
    pallas_call x1, Pallas kernels, finish(): pl.pallas_call(finish_kernel, in_specs=[VMEM] * 3, out_specs=HBM, out_sha...  3.13 us
    ppermute x2, starting transfers between devices, swap_second(): return lax.ppermute(x, 'pw', [(i, i ^ (2, 4)[i % 2]) for i in range(count)])  3.07 us
    pallas_call x3, Pallas kernels, project(): pl.pallas_call(kernel, in_specs=[VMEM, VMEM], out_specs=[VMEM, VMEM], out...  2.91 us
    ppermute x2, waiting for transfers between devices, swap_second(): return lax.ppermute(x, 'pw', [(i, i ^ (2, 4)[i % 2]) for i in range(count)])  2.86 us
    ppermute x3, waiting for transfers between devices, swap_first(): return lax.ppermute(x, 'pw', [(i, i ^ (4, 2)[i % 2]) for i in range(count)])  2.28 us
  transfers between devices with their start and end apart: 12, of which 7 were waited for; matrix products, arithmetic and copies ran while one was open for 0% of the time, Pallas kernels for 17%

profile of v22, /device:TPU:0, one launch (start us, length us, event | category | flops | bytes accessed | tf_op | source)
XLA Modules:
  0.0 42.3 jit_solution(16801809172825966200)
XLA Ops:
  0.0 0.0 copy-start
  0.0 0.5 %collective-permute-start.1 = (f32[256,256]{1,0:T(8,128)}, f32[256,256]{1,0:T(8,128)S(1)}, u32[]{:S(2)}, u32[]{:S(2)}) collective-permute-start(f32[256,256]{1,0:T(8,128)} %bitcast.1), channel_id=1, source_target_pairs={{0,1},{1,0},{2,3},{3,2},{4,5},{5,4},{6,7},{7,6},{8,9},{9,8},{10,11... | collective-permute-start | bytes 786440 | tf_op jit(solution)/shard_map/ppermute | solution.py:35
  0.5 2.2 %load.1.refs_0_ = bf16[512,2048]{1,0:T(8,128)(2,1)S(1)} custom-call(bf16[2048,512]{1,0:T(8,128)(2,1)} %projectors.5), custom_call_target="tpu_custom_call" | custom-call | tf_op jit(solution)/shard_map/load/pallas_call | solution.py:88
  2.7 0.1 copy-done
  2.8 0.8 %project.4 = (bf16[2,256,128]{2,1,0:T(8,128)(2,1)S(1)}, f32[2,256,128]{2,1,0:T(8,128)S(1)}) custom-call(bf16[512,2048]{1,0:T(8,128)(2,1)S(1)} %load.1.refs_0_, bf16[2048,1024]{1,0:T(8,128)(2,1)S(1)} %copy-done), custom_call_target="tpu_custom_call" | custom-call | flops 536870912 | bytes 2097152 | tf_op jit(solution)/shard_map/project/pallas_call | solution.py:113
  3.6 0.0 copy-start.5
  3.6 0.0 copy-start.2
  3.6 0.0 collective-permute-done.1.sibling
  3.6 0.5 %collective-permute-start.2 = (bf16[2,256,128]{2,1,0:T(8,128)(2,1)S(1)}, bf16[2,256,128]{2,1,0:T(8,128)(2,1)S(1)}, u32[]{:S(2)}, u32[]{:S(2)}) collective-permute-start(bf16[2,256,128]{2,1,0:T(8,128)(2,1)S(1)} %get-tuple-element.20), channel_id=1, source_target_pairs={{0,1},{1,0},{2,3},{3,2},{4,5},{5,4},{6,7},{7,6},{8,9},{9,8},{10,11... | collective-permute-start | bytes 393224 | tf_op jit(solution)/shard_map/ppermute | solution.py:35
  4.2 1.3 %project.3 = (bf16[4,256,128]{2,1,0:T(8,128)(2,1)S(1)}, f32[4,256,128]{2,1,0:T(8,128)S(1)}) custom-call(bf16[512,2048]{1,0:T(8,128)(2,1)S(1)} %load.1.refs_0_, bf16[2048,1024]{1,0:T(8,128)(2,1)S(1)} %copy-done), custom_call_target="tpu_custom_call" | custom-call | flops 1073741824 | bytes 2097152 | tf_op jit(solution)/shard_map/project/pallas_call | solution.py:113
  5.5 0.1 collective-permute-start
  5.6 0.0 copy-done.5
  5.6 0.1 broadcast_in_dim.2.owners
  5.7 0.0 copy-done.2
  5.7 0.0 collective-permute-done.2.refs_1_
  5.8 3.1 %collective-permute-start.3 = (bf16[640,128]{1,0:T(8,128)(2,1)S(1)}, bf16[640,128]{1,0:T(8,128)(2,1)S(1)}, u32[]{:S(2)}, u32[]{:S(2)}) collective-permute-start(bf16[640,128]{1,0:T(8,128)(2,1)S(1)} %send.2), channel_id=1, source_target_pairs={{0,4},{1,3},{2,6},{3,1},{4,0},{5,7},{6,2},{7,5},{8,12},{9,11},{10,... | collective-permute-start | bytes 491528 | tf_op jit(solution)/shard_map/ppermute | solution.py:48
  8.9 0.0 collective-permute-done.theirs.refs_1_
  8.9 1.0 %collective-permute-start.5 = (bf16[640,128]{1,0:T(8,128)(2,1)S(1)}, bf16[640,128]{1,0:T(8,128)(2,1)S(1)}, u32[]{:S(2)}, u32[]{:S(2)}) collective-permute-start(bf16[640,128]{1,0:T(8,128)(2,1)S(1)} %send.3), channel_id=1, source_target_pairs={{0,4},{1,3},{2,6},{3,1},{4,0},{5,7},{6,2},{7,5},{8,12},{9,11},{10,... | collective-permute-start | bytes 491528 | tf_op jit(solution)/shard_map/ppermute | solution.py:48
  9.9 2.3 %collective-permute-done.3.got = bf16[640,128]{1,0:T(8,128)(2,1)S(1)} collective-permute-done((bf16[640,128]{1,0:T(8,128)(2,1)S(1)}, bf16[640,128]{1,0:T(8,128)(2,1)S(1)}, u32[]{:S(2)}, u32[]{:S(2)}) %collective-permute-start.3) | collective-permute-done | bytes 163872 | tf_op jit(solution)/shard_map/ppermute | solution.py:48
  12.2 0.1 forward.1.after
  12.2 0.0 copy-start.3
  12.2 0.0 copy-start.4
  12.2 0.0 copy-start.1
  12.3 2.0 %collective-permute-start.6 = (bf16[640,128]{1,0:T(8,128)(2,1)S(1)}, bf16[640,128]{1,0:T(8,128)(2,1)S(1)}, u32[]{:S(2)}, u32[]{:S(2)}) collective-permute-start(bf16[640,128]{1,0:T(8,128)(2,1)S(1)} %forward.1.after), channel_id=1, source_target_pairs={{0,2},{1,5},{2,0},{3,7},{4,6},{5,1},{6,4},{7,3},{8,10},{9,13},{10,... | collective-permute-start | bytes 491528 | tf_op jit(solution)/shard_map/ppermute | solution.py:53
  14.3 0.8 %project.5 = (bf16[2,256,128]{2,1,0:T(8,128)(2,1)S(1)}, f32[2,256,128]{2,1,0:T(8,128)S(1)}) custom-call(bf16[512,2048]{1,0:T(8,128)(2,1)S(1)} %load.1.refs_0_, bf16[2048,1024]{1,0:T(8,128)(2,1)S(1)} %copy-done), custom_call_target="tpu_custom_call" | custom-call | flops 536870912 | bytes 2097152 | tf_op jit(solution)/shard_map/project/pallas_call | solution.py:113
  15.1 0.1 collective-permute-start.4
  15.2 1.3 %collective-permute-done.4.theirs = bf16[2,256,128]{2,1,0:T(8,128)(2,1)S(1)} collective-permute-done((bf16[2,256,128]{2,1,0:T(8,128)(2,1)S(1)}, bf16[2,256,128]{2,1,0:T(8,128)(2,1)S(1)}, u32[]{:S(2)}, u32[]{:S(2)}) %collective-permute-start.4) | collective-permute-done | bytes 131104 | tf_op jit(solution)/shard_map/ppermute | solution.py:35
  16.5 0.0 collective-permute-done.5.refs_0_
  16.5 1.1 %collective-permute-done.6.refs_1_ = bf16[640,128]{1,0:T(8,128)(2,1)S(1)} collective-permute-done((bf16[640,128]{1,0:T(8,128)(2,1)S(1)}, bf16[640,128]{1,0:T(8,128)(2,1)S(1)}, u32[]{:S(2)}, u32[]{:S(2)}) %collective-permute-start.6) | collective-permute-done | bytes 163872 | tf_op jit(solution)/shard_map/ppermute | solution.py:53
  17.6 0.1 fold.1
  17.7 3.1 %collective-permute-start.7 = (bf16[640,128]{1,0:T(8,128)(2,1)S(1)}, bf16[640,128]{1,0:T(8,128)(2,1)S(1)}, u32[]{:S(2)}, u32[]{:S(2)}) collective-permute-start(bf16[640,128]{1,0:T(8,128)(2,1)S(1)} %get-tuple-element.24), channel_id=1, source_target_pairs={{0,8},{1,9},{2,10},{3,11},{4,12},{5,13},{6,14},{7,15},{8,0},{9,1},... | collective-permute-start | bytes 491528 | tf_op jit(solution)/shard_map/ppermute | solution.py:35
  20.8 6.5 %collective-permute-done.7.right = bf16[640,128]{1,0:T(8,128)(2,1)S(1)} collective-permute-done((bf16[640,128]{1,0:T(8,128)(2,1)S(1)}, bf16[640,128]{1,0:T(8,128)(2,1)S(1)}, u32[]{:S(2)}, u32[]{:S(2)}) %collective-permute-start.7) | collective-permute-done | bytes 163872 | tf_op jit(solution)/shard_map/ppermute | solution.py:35
  27.3 1.2 %collective-permute-start.10 = (bf16[640,128]{1,0:T(8,128)(2,1)S(1)}, bf16[640,128]{1,0:T(8,128)(2,1)S(1)}, u32[]{:S(2)}, u32[]{:S(2)}) collective-permute-start(bf16[640,128]{1,0:T(8,128)(2,1)S(1)} %add.1.refs_0_), channel_id=1, source_target_pairs={{0,6},{1,7},{2,4},{3,5},{4,2},{5,3},{6,0},{7,1},{8,14},{9,15},{10,... | collective-permute-start | bytes 491528 | tf_op jit(solution)/shard_map/ppermute | solution.py:35
  28.5 1.0 %collective-permute-start.9 = (bf16[640,128]{1,0:T(8,128)(2,1)S(1)}, bf16[640,128]{1,0:T(8,128)(2,1)S(1)}, u32[]{:S(2)}, u32[]{:S(2)}) collective-permute-start(bf16[640,128]{1,0:T(8,128)(2,1)S(1)} %add.1.refs_0_), channel_id=1, source_target_pairs={{0,2},{1,5},{2,0},{3,7},{4,6},{5,1},{6,4},{7,3},{8,10},{9,13},{10,... | collective-permute-start | bytes 491528 | tf_op jit(solution)/shard_map/ppermute | solution.py:53
  29.6 1.4 %collective-permute-start.8 = (bf16[640,128]{1,0:T(8,128)(2,1)S(1)}, bf16[640,128]{1,0:T(8,128)(2,1)S(1)}, u32[]{:S(2)}, u32[]{:S(2)}) collective-permute-start(bf16[640,128]{1,0:T(8,128)(2,1)S(1)} %add.1.refs_0_), channel_id=1, source_target_pairs={{0,4},{1,3},{2,6},{3,1},{4,0},{5,7},{6,2},{7,5},{8,12},{9,11},{10,... | collective-permute-start | bytes 491528 | tf_op jit(solution)/shard_map/ppermute | solution.py:48
  30.9 0.0 copy-done.3
  30.9 0.0 copy-done.4
  30.9 0.7 %mask.1.allowed = bf16[256,256]{1,0:T(8,128)(2,1)S(1)} custom-call(s32[2,4]{1,0:T(2,128)S(1)} %copy-done.4, s32[2,256]{1,0:T(2,128)S(1)} %copy-done.3, bf16[640,128]{1,0:T(8,128)(2,1)S(1)} %forward.1.after), custom_call_target="tpu_custom_call" | custom-call | tf_op jit(solution)/shard_map/mask/pallas_call | solution.py:273
  31.6 3.6 %collective-permute-done.10.refs_3_ = bf16[640,128]{1,0:T(8,128)(2,1)S(1)} collective-permute-done((bf16[640,128]{1,0:T(8,128)(2,1)S(1)}, bf16[640,128]{1,0:T(8,128)(2,1)S(1)}, u32[]{:S(2)}, u32[]{:S(2)}) %collective-permute-start.10) | collective-permute-done | bytes 163872 | tf_op jit(solution)/shard_map/ppermute | solution.py:35
  35.1 1.7 %collective-permute-done.9.refs_2_ = bf16[640,128]{1,0:T(8,128)(2,1)S(1)} collective-permute-done((bf16[640,128]{1,0:T(8,128)(2,1)S(1)}, bf16[640,128]{1,0:T(8,128)(2,1)S(1)}, u32[]{:S(2)}, u32[]{:S(2)}) %collective-permute-start.9) | collective-permute-done | bytes 163872 | tf_op jit(solution)/shard_map/ppermute | solution.py:53
  36.9 0.0 collective-permute-done.8.refs_1_
  36.9 0.3 couple.1.scaled
  37.2 0.1 collective-permute-start.11
  37.3 0.0 copy-done.1
  37.3 1.3 %begin.1.begun = f32[4,2048,256]{2,1,0:T(8,128)S(1)} custom-call(bf16[2048,512]{1,0:T(8,128)(2,1)S(1)} %copy-done.1, bf16[8,256,128]{2,1,0:T(8,128)(2,1)S(1)} %couple.1.scaled), custom_call_target="tpu_custom_call" | custom-call | flops 1073741824 | bytes 2097152 | tf_op jit(solution)/shard_map/begin/pallas_call | solution.py:339
  38.5 0.6 %collective-permute-done.11.other = bf16[8,256,128]{2,1,0:T(8,128)(2,1)S(1)} collective-permute-done((bf16[8,256,128]{2,1,0:T(8,128)(2,1)S(1)}, bf16[8,256,128]{2,1,0:T(8,128)(2,1)S(1)}, u32[]{:S(2)}, u32[]{:S(2)}) %collective-permute-start.11) | collective-permute-done | bytes 524320 | tf_op jit(solution)/shard_map/ppermute | solution.py:35
  39.2 3.1 %finish.1 = bf16[2048,1024]{1,0:T(8,128)(2,1)} custom-call(bf16[2048,512]{1,0:T(8,128)(2,1)S(1)} %copy-done.1, f32[4,2048,256]{2,1,0:T(8,128)S(1)} %begin.1.begun, bf16[8,256,128]{2,1,0:T(8,128)(2,1)S(1)} %collective-permute-done.11.other), custom_call_target="tpu_custom_call" | custom-call | flops 1073741824 | bytes 6291456 | tf_op jit(solution)/shard_map/finish/pallas_call | solution.py:379
  (4 shorter events, 0.1 us)
Async XLA Ops:
  0.0 2.8 %copy-start = (bf16[2048,1024]{1,0:T(8,128)(2,1)S(1)}, bf16[2048,1024]{1,0:T(8,128)(2,1)}, u32[]{:S(2)}) copy-start(bf16[2048,1024]{1,0:T(8,128)(2,1)} %refs_1_.5) | copy-start | bytes 12582916
  0.0 3.6 %collective-permute-start.1 = (f32[256,256]{1,0:T(8,128)}, f32[256,256]{1,0:T(8,128)S(1)}, u32[]{:S(2)}, u32[]{:S(2)}) collective-permute-start(f32[256,256]{1,0:T(8,128)} %bitcast.1), channel_id=1, source_target_pairs={{0,1},{1,0},{2,3},{3,2},{4,5},{5,4},{6,7},{7,6},{8,9},{9,8},{10,11... | collective-permute-start | bytes 786440 | tf_op jit(solution)/shard_map/ppermute | solution.py:35
  3.6 2.0 %copy-start.5 = (s32[2]{0:T(128)S(1)}, s32[2]{0:T(128)}, u32[]{:S(2)}) copy-start(s32[2]{0:T(128)} %param.10) | copy-start | bytes 28
  3.6 2.1 %copy-start.2 = (f32[1,256,256]{2,1,0:T(8,128)S(1)}, f32[1,256,256]{2,1,0:T(8,128)}, u32[]{:S(2)}) copy-start(f32[1,256,256]{2,1,0:T(8,128)} %param.11) | copy-start | bytes 786436
  3.6 2.1 %collective-permute-start.2 = (bf16[2,256,128]{2,1,0:T(8,128)(2,1)S(1)}, bf16[2,256,128]{2,1,0:T(8,128)(2,1)S(1)}, u32[]{:S(2)}, u32[]{:S(2)}) collective-permute-start(bf16[2,256,128]{2,1,0:T(8,128)(2,1)S(1)} %get-tuple-element.20), channel_id=1, source_target_pairs={{0,1},{1,0},{2,3},{3,2},{4,5},{5,4},{6,7},{7,6},{8,9},{9,8},{10,11... | collective-permute-start | bytes 393224 | tf_op jit(solution)/shard_map/ppermute | solution.py:35
  5.5 3.4 %collective-permute-start = (bf16[4,256,128]{2,1,0:T(8,128)(2,1)S(1)}, bf16[4,256,128]{2,1,0:T(8,128)(2,1)S(1)}, u32[]{:S(2)}, u32[]{:S(2)}) collective-permute-start(bf16[4,256,128]{2,1,0:T(8,128)(2,1)S(1)} %get-tuple-element.16), channel_id=1, source_target_pairs={{0,1},{1,0},{2,3},{3,2},{4,5},{5,4},{6,7},{7,6},{8,9},{9,8},{10,11... | collective-permute-start | bytes 786440 | tf_op jit(solution)/shard_map/ppermute | solution.py:35
  5.8 6.4 %collective-permute-start.3 = (bf16[640,128]{1,0:T(8,128)(2,1)S(1)}, bf16[640,128]{1,0:T(8,128)(2,1)S(1)}, u32[]{:S(2)}, u32[]{:S(2)}) collective-permute-start(bf16[640,128]{1,0:T(8,128)(2,1)S(1)} %send.2), channel_id=1, source_target_pairs={{0,4},{1,3},{2,6},{3,1},{4,0},{5,7},{6,2},{7,5},{8,12},{9,11},{10,... | collective-permute-start | bytes 491528 | tf_op jit(solution)/shard_map/ppermute | solution.py:48
  8.9 7.6 %collective-permute-start.5 = (bf16[640,128]{1,0:T(8,128)(2,1)S(1)}, bf16[640,128]{1,0:T(8,128)(2,1)S(1)}, u32[]{:S(2)}, u32[]{:S(2)}) collective-permute-start(bf16[640,128]{1,0:T(8,128)(2,1)S(1)} %send.3), channel_id=1, source_target_pairs={{0,4},{1,3},{2,6},{3,1},{4,0},{5,7},{6,2},{7,5},{8,12},{9,11},{10,... | collective-permute-start | bytes 491528 | tf_op jit(solution)/shard_map/ppermute | solution.py:48
  12.2 18.7 %copy-start.3 = (s32[2,256]{1,0:T(2,128)S(1)}, s32[2,256]{1,0:T(2,128)}, u32[]{:S(2)}) copy-start(s32[2,256]{1,0:T(2,128)} %atom_of.1) | copy-start | bytes 6148
  12.2 18.7 %copy-start.4 = (s32[2,4]{1,0:T(2,128)S(1)}, s32[2,4]{1,0:T(2,128)}, u32[]{:S(2)}) copy-start(s32[2,4]{1,0:T(2,128)} %counts.1) | copy-start | bytes 100
  12.2 25.0 %copy-start.1 = (bf16[2048,512]{1,0:T(8,128)(2,1)S(1)}, bf16[2048,512]{1,0:T(8,128)(2,1)}, u32[]{:S(2)}) copy-start(bf16[2048,512]{1,0:T(8,128)(2,1)} %projectors.5) | copy-start | bytes 6291460
  12.3 5.4 %collective-permute-start.6 = (bf16[640,128]{1,0:T(8,128)(2,1)S(1)}, bf16[640,128]{1,0:T(8,128)(2,1)S(1)}, u32[]{:S(2)}, u32[]{:S(2)}) collective-permute-start(bf16[640,128]{1,0:T(8,128)(2,1)S(1)} %forward.1.after), channel_id=1, source_target_pairs={{0,2},{1,5},{2,0},{3,7},{4,6},{5,1},{6,4},{7,3},{8,10},{9,13},{10,... | collective-permute-start | bytes 491528 | tf_op jit(solution)/shard_map/ppermute | solution.py:53
  15.1 1.4 %collective-permute-start.4 = (bf16[2,256,128]{2,1,0:T(8,128)(2,1)S(1)}, bf16[2,256,128]{2,1,0:T(8,128)(2,1)S(1)}, u32[]{:S(2)}, u32[]{:S(2)}) collective-permute-start(bf16[2,256,128]{2,1,0:T(8,128)(2,1)S(1)} %get-tuple-element.22), channel_id=1, source_target_pairs={{0,1},{1,0},{2,3},{3,2},{4,5},{5,4},{6,7},{7,6},{8,9},{9,8},{10,11... | collective-permute-start | bytes 393224 | tf_op jit(solution)/shard_map/ppermute | solution.py:35
  17.7 9.6 %collective-permute-start.7 = (bf16[640,128]{1,0:T(8,128)(2,1)S(1)}, bf16[640,128]{1,0:T(8,128)(2,1)S(1)}, u32[]{:S(2)}, u32[]{:S(2)}) collective-permute-start(bf16[640,128]{1,0:T(8,128)(2,1)S(1)} %get-tuple-element.24), channel_id=1, source_target_pairs={{0,8},{1,9},{2,10},{3,11},{4,12},{5,13},{6,14},{7,15},{8,0},{9,1},... | collective-permute-start | bytes 491528 | tf_op jit(solution)/shard_map/ppermute | solution.py:35
  27.3 7.8 %collective-permute-start.10 = (bf16[640,128]{1,0:T(8,128)(2,1)S(1)}, bf16[640,128]{1,0:T(8,128)(2,1)S(1)}, u32[]{:S(2)}, u32[]{:S(2)}) collective-permute-start(bf16[640,128]{1,0:T(8,128)(2,1)S(1)} %add.1.refs_0_), channel_id=1, source_target_pairs={{0,6},{1,7},{2,4},{3,5},{4,2},{5,3},{6,0},{7,1},{8,14},{9,15},{10,... | collective-permute-start | bytes 491528 | tf_op jit(solution)/shard_map/ppermute | solution.py:35
  28.5 8.3 %collective-permute-start.9 = (bf16[640,128]{1,0:T(8,128)(2,1)S(1)}, bf16[640,128]{1,0:T(8,128)(2,1)S(1)}, u32[]{:S(2)}, u32[]{:S(2)}) collective-permute-start(bf16[640,128]{1,0:T(8,128)(2,1)S(1)} %add.1.refs_0_), channel_id=1, source_target_pairs={{0,2},{1,5},{2,0},{3,7},{4,6},{5,1},{6,4},{7,3},{8,10},{9,13},{10,... | collective-permute-start | bytes 491528 | tf_op jit(solution)/shard_map/ppermute | solution.py:53
  29.6 7.3 %collective-permute-start.8 = (bf16[640,128]{1,0:T(8,128)(2,1)S(1)}, bf16[640,128]{1,0:T(8,128)(2,1)S(1)}, u32[]{:S(2)}, u32[]{:S(2)}) collective-permute-start(bf16[640,128]{1,0:T(8,128)(2,1)S(1)} %add.1.refs_0_), channel_id=1, source_target_pairs={{0,4},{1,3},{2,6},{3,1},{4,0},{5,7},{6,2},{7,5},{8,12},{9,11},{10,... | collective-permute-start | bytes 491528 | tf_op jit(solution)/shard_map/ppermute | solution.py:48
  37.2 2.0 %collective-permute-start.11 = (bf16[8,256,128]{2,1,0:T(8,128)(2,1)S(1)}, bf16[8,256,128]{2,1,0:T(8,128)(2,1)S(1)}, u32[]{:S(2)}, u32[]{:S(2)}) collective-permute-start(bf16[8,256,128]{2,1,0:T(8,128)(2,1)S(1)} %couple.1.scaled), channel_id=1, source_target_pairs={{0,1},{1,0},{2,3},{3,2},{4,5},{5,4},{6,7},{7,6},{8,9},{9,8},{10,11... | collective-permute-start | bytes 1572872 | tf_op jit(solution)/shard_map/ppermute | solution.py:35

commit v23 on v22

--- a/solution.py
+++ b/solution.py
@@ -286,7 +286,7 @@
     entries = out.shape[0] // SQUARE
     core, chip = place()
     corner = chip & 3
-    parts = (0, 2 - core, 1 + core, 3)
+    parts = (0, 3, 1 + core, 2 - core)
     for part, message in zip(parts, messages):
         start = pl.multiple_of((corner ^ part) * QUARTER, QUARTER)
         for cut in range(PCAP // width):
@@ -445,7 +445,7 @@
         mine = add(mine.astype(jnp.float32), swap_chips(message, distance))
         distance *= 2
 
-    scaled = couple(allowed, [mine, swap_first(mine), swap_second(mine), swap_chips(mine, 3)])
+    scaled = couple(allowed, [mine, swap_chips(mine, 3), swap_second(mine), swap_first(mine)])
     other = swap_cores(scaled)
     if not fast:
         return apply_plain(projectors, scaled, other)

time: 42.4 us -> 42.7 us (level)
    ppermute x3, waiting for transfers between devices: 2.28 us -> 5.22 us  [swap_first(): return lax.ppermute(x, 'pw', [(i, i ^ (4, 2)[i % 2]) for i in range(count)])]
    ppermute x2, waiting for transfers between devices: 2.86 us -> 1.14 us  [swap_second(): return lax.ppermute(x, 'pw', [(i, i ^ (2, 4)[i % 2]) for i in range(count)])]
    ppermute x7, waiting for transfers between devices: 12 us -> 11.1 us  [swap(): return lax.ppermute(x, 'pw', [(i, i ^ distance) for i in range(count)])]
    ppermute x7, starting transfers between devices: 5.51 us -> 6.15 us  [swap(): return lax.ppermute(x, 'pw', [(i, i ^ distance) for i in range(count)])]
    ppermute x3, starting transfers between devices: 5.42 us -> 4.81 us  [swap_first(): return lax.ppermute(x, 'pw', [(i, i ^ (4, 2)[i % 2]) for i in range(count)])]
where the time goes in v23:
time: 42.7 us; the launch traced here: 42.6 us
  waiting for transfers between devices  17.4 us (41%)
  starting transfers between devices  14 us (33%)
  Pallas kernels  10.7 us (25%)
    ppermute x7, waiting for transfers between devices, swap(): return lax.ppermute(x, 'pw', [(i, i ^ distance) for i in range(count)])  11.1 us
    ppermute x7, starting transfers between devices, swap(): return lax.ppermute(x, 'pw', [(i, i ^ distance) for i in range(count)])  6.15 us
    ppermute x3, waiting for transfers between devices, swap_first(): return lax.ppermute(x, 'pw', [(i, i ^ (4, 2)[i % 2]) for i in range(count)])  5.22 us
    ppermute x3, starting transfers between devices, swap_first(): return lax.ppermute(x, 'pw', [(i, i ^ (4, 2)[i % 2]) for i in range(count)])  4.81 us
    pallas_call x1, Pallas kernels, finish(): pl.pallas_call(finish_kernel, in_specs=[VMEM] * 3, out_specs=HBM, out_sha...  3.13 us
    ppermute x2, starting transfers between devices, swap_second(): return lax.ppermute(x, 'pw', [(i, i ^ (2, 4)[i % 2]) for i in range(count)])  3.04 us
    pallas_call x3, Pallas kernels, project(): pl.pallas_call(kernel, in_specs=[VMEM, VMEM], out_specs=[VMEM, VMEM], out...  2.91 us
    pallas_call x1, Pallas kernels, load(): pl.pallas_call(load_kernel, in_specs=[HBM], out_specs=VMEM, out_shape=jax...  2.21 us
  transfers between devices with their start and end apart: 12, of which 7 were waited for; matrix products, arithmetic and copies ran while one was open for 0% of the time, Pallas kernels for 17%

profile of v23, /device:TPU:0, one launch (start us, length us, event | category | flops | bytes accessed | tf_op | source)
XLA Modules:
  0.0 42.6 jit_solution(1261101332472209504)
XLA Ops:
  0.0 0.0 copy-start
  0.0 0.5 %collective-permute-start.1 = (f32[256,256]{1,0:T(8,128)}, f32[256,256]{1,0:T(8,128)S(1)}, u32[]{:S(2)}, u32[]{:S(2)}) collective-permute-start(f32[256,256]{1,0:T(8,128)} %bitcast.1), channel_id=1, source_target_pairs={{0,1},{1,0},{2,3},{3,2},{4,5},{5,4},{6,7},{7,6},{8,9},{9,8},{10,11... | collective-permute-start | bytes 786440 | tf_op jit(solution)/shard_map/ppermute | solution.py:35
  0.5 2.2 %load.1.refs_0_ = bf16[512,2048]{1,0:T(8,128)(2,1)S(1)} custom-call(bf16[2048,512]{1,0:T(8,128)(2,1)} %projectors.5), custom_call_target="tpu_custom_call" | custom-call | tf_op jit(solution)/shard_map/load/pallas_call | solution.py:88
  2.7 0.1 copy-done
  2.8 0.8 %project.4 = (bf16[2,256,128]{2,1,0:T(8,128)(2,1)S(1)}, f32[2,256,128]{2,1,0:T(8,128)S(1)}) custom-call(bf16[512,2048]{1,0:T(8,128)(2,1)S(1)} %load.1.refs_0_, bf16[2048,1024]{1,0:T(8,128)(2,1)S(1)} %copy-done), custom_call_target="tpu_custom_call" | custom-call | flops 536870912 | bytes 2097152 | tf_op jit(solution)/shard_map/project/pallas_call | solution.py:113
  3.6 0.0 copy-start.5
  3.6 0.0 copy-start.2
  3.6 0.0 collective-permute-done.1.sibling
  3.6 0.5 %collective-permute-start.2 = (bf16[2,256,128]{2,1,0:T(8,128)(2,1)S(1)}, bf16[2,256,128]{2,1,0:T(8,128)(2,1)S(1)}, u32[]{:S(2)}, u32[]{:S(2)}) collective-permute-start(bf16[2,256,128]{2,1,0:T(8,128)(2,1)S(1)} %get-tuple-element.20), channel_id=1, source_target_pairs={{0,1},{1,0},{2,3},{3,2},{4,5},{5,4},{6,7},{7,6},{8,9},{9,8},{10,11... | collective-permute-start | bytes 393224 | tf_op jit(solution)/shard_map/ppermute | solution.py:35
  4.2 1.3 %project.3 = (bf16[4,256,128]{2,1,0:T(8,128)(2,1)S(1)}, f32[4,256,128]{2,1,0:T(8,128)S(1)}) custom-call(bf16[512,2048]{1,0:T(8,128)(2,1)S(1)} %load.1.refs_0_, bf16[2048,1024]{1,0:T(8,128)(2,1)S(1)} %copy-done), custom_call_target="tpu_custom_call" | custom-call | flops 1073741824 | bytes 2097152 | tf_op jit(solution)/shard_map/project/pallas_call | solution.py:113
  5.5 0.1 collective-permute-start
  5.6 0.0 copy-done.5
  5.6 0.1 broadcast_in_dim.2.owners
  5.7 0.0 copy-done.2
  5.7 0.0 collective-permute-done.2.refs_1_
  5.8 3.1 %collective-permute-start.3 = (bf16[640,128]{1,0:T(8,128)(2,1)S(1)}, bf16[640,128]{1,0:T(8,128)(2,1)S(1)}, u32[]{:S(2)}, u32[]{:S(2)}) collective-permute-start(bf16[640,128]{1,0:T(8,128)(2,1)S(1)} %send.2), channel_id=1, source_target_pairs={{0,4},{1,3},{2,6},{3,1},{4,0},{5,7},{6,2},{7,5},{8,12},{9,11},{10,... | collective-permute-start | bytes 491528 | tf_op jit(solution)/shard_map/ppermute | solution.py:48
  8.9 0.0 collective-permute-done.theirs.refs_1_
  8.9 1.0 %collective-permute-start.5 = (bf16[640,128]{1,0:T(8,128)(2,1)S(1)}, bf16[640,128]{1,0:T(8,128)(2,1)S(1)}, u32[]{:S(2)}, u32[]{:S(2)}) collective-permute-start(bf16[640,128]{1,0:T(8,128)(2,1)S(1)} %send.3), channel_id=1, source_target_pairs={{0,4},{1,3},{2,6},{3,1},{4,0},{5,7},{6,2},{7,5},{8,12},{9,11},{10,... | collective-permute-start | bytes 491528 | tf_op jit(solution)/shard_map/ppermute | solution.py:48
  9.9 2.3 %collective-permute-done.3.got = bf16[640,128]{1,0:T(8,128)(2,1)S(1)} collective-permute-done((bf16[640,128]{1,0:T(8,128)(2,1)S(1)}, bf16[640,128]{1,0:T(8,128)(2,1)S(1)}, u32[]{:S(2)}, u32[]{:S(2)}) %collective-permute-start.3) | collective-permute-done | bytes 163872 | tf_op jit(solution)/shard_map/ppermute | solution.py:48
  12.2 0.1 forward.1.after
  12.2 0.0 copy-start.3
  12.2 0.0 copy-start.4
  12.2 0.0 copy-start.1
  12.3 2.0 %collective-permute-start.6 = (bf16[640,128]{1,0:T(8,128)(2,1)S(1)}, bf16[640,128]{1,0:T(8,128)(2,1)S(1)}, u32[]{:S(2)}, u32[]{:S(2)}) collective-permute-start(bf16[640,128]{1,0:T(8,128)(2,1)S(1)} %forward.1.after), channel_id=1, source_target_pairs={{0,2},{1,5},{2,0},{3,7},{4,6},{5,1},{6,4},{7,3},{8,10},{9,13},{10,... | collective-permute-start | bytes 491528 | tf_op jit(solution)/shard_map/ppermute | solution.py:53
  14.3 0.8 %project.5 = (bf16[2,256,128]{2,1,0:T(8,128)(2,1)S(1)}, f32[2,256,128]{2,1,0:T(8,128)S(1)}) custom-call(bf16[512,2048]{1,0:T(8,128)(2,1)S(1)} %load.1.refs_0_, bf16[2048,1024]{1,0:T(8,128)(2,1)S(1)} %copy-done), custom_call_target="tpu_custom_call" | custom-call | flops 536870912 | bytes 2097152 | tf_op jit(solution)/shard_map/project/pallas_call | solution.py:113
  15.1 0.1 collective-permute-start.4
  15.2 1.3 %collective-permute-done.4.theirs = bf16[2,256,128]{2,1,0:T(8,128)(2,1)S(1)} collective-permute-done((bf16[2,256,128]{2,1,0:T(8,128)(2,1)S(1)}, bf16[2,256,128]{2,1,0:T(8,128)(2,1)S(1)}, u32[]{:S(2)}, u32[]{:S(2)}) %collective-permute-start.4) | collective-permute-done | bytes 131104 | tf_op jit(solution)/shard_map/ppermute | solution.py:35
  16.5 0.0 collective-permute-done.5.refs_0_
  16.5 1.1 %collective-permute-done.6.refs_1_ = bf16[640,128]{1,0:T(8,128)(2,1)S(1)} collective-permute-done((bf16[640,128]{1,0:T(8,128)(2,1)S(1)}, bf16[640,128]{1,0:T(8,128)(2,1)S(1)}, u32[]{:S(2)}, u32[]{:S(2)}) %collective-permute-start.6) | collective-permute-done | bytes 163872 | tf_op jit(solution)/shard_map/ppermute | solution.py:53
  17.6 0.1 fold.1
  17.7 3.1 %collective-permute-start.7 = (bf16[640,128]{1,0:T(8,128)(2,1)S(1)}, bf16[640,128]{1,0:T(8,128)(2,1)S(1)}, u32[]{:S(2)}, u32[]{:S(2)}) collective-permute-start(bf16[640,128]{1,0:T(8,128)(2,1)S(1)} %get-tuple-element.24), channel_id=1, source_target_pairs={{0,8},{1,9},{2,10},{3,11},{4,12},{5,13},{6,14},{7,15},{8,0},{9,1},... | collective-permute-start | bytes 491528 | tf_op jit(solution)/shard_map/ppermute | solution.py:35
  20.8 6.5 %collective-permute-done.7.right = bf16[640,128]{1,0:T(8,128)(2,1)S(1)} collective-permute-done((bf16[640,128]{1,0:T(8,128)(2,1)S(1)}, bf16[640,128]{1,0:T(8,128)(2,1)S(1)}, u32[]{:S(2)}, u32[]{:S(2)}) %collective-permute-start.7) | collective-permute-done | bytes 163872 | tf_op jit(solution)/shard_map/ppermute | solution.py:35
  27.3 0.7 %collective-permute-start.10 = (bf16[640,128]{1,0:T(8,128)(2,1)S(1)}, bf16[640,128]{1,0:T(8,128)(2,1)S(1)}, u32[]{:S(2)}, u32[]{:S(2)}) collective-permute-start(bf16[640,128]{1,0:T(8,128)(2,1)S(1)} %add.1.refs_0_), channel_id=1, source_target_pairs={{0,4},{1,3},{2,6},{3,1},{4,0},{5,7},{6,2},{7,5},{8,12},{9,11},{10,... | collective-permute-start | bytes 491528 | tf_op jit(solution)/shard_map/ppermute | solution.py:48
  28.1 1.0 %collective-permute-start.9 = (bf16[640,128]{1,0:T(8,128)(2,1)S(1)}, bf16[640,128]{1,0:T(8,128)(2,1)S(1)}, u32[]{:S(2)}, u32[]{:S(2)}) collective-permute-start(bf16[640,128]{1,0:T(8,128)(2,1)S(1)} %add.1.refs_0_), channel_id=1, source_target_pairs={{0,2},{1,5},{2,0},{3,7},{4,6},{5,1},{6,4},{7,3},{8,10},{9,13},{10,... | collective-permute-start | bytes 491528 | tf_op jit(solution)/shard_map/ppermute | solution.py:53
  29.1 1.8 %collective-permute-start.8 = (bf16[640,128]{1,0:T(8,128)(2,1)S(1)}, bf16[640,128]{1,0:T(8,128)(2,1)S(1)}, u32[]{:S(2)}, u32[]{:S(2)}) collective-permute-start(bf16[640,128]{1,0:T(8,128)(2,1)S(1)} %add.1.refs_0_), channel_id=1, source_target_pairs={{0,6},{1,7},{2,4},{3,5},{4,2},{5,3},{6,0},{7,1},{8,14},{9,15},{10,... | collective-permute-start | bytes 491528 | tf_op jit(solution)/shard_map/ppermute | solution.py:35
  30.9 0.0 copy-done.3
  30.9 0.0 copy-done.4
  30.9 0.7 %mask.1.allowed = bf16[256,256]{1,0:T(8,128)(2,1)S(1)} custom-call(s32[2,4]{1,0:T(2,128)S(1)} %copy-done.4, s32[2,256]{1,0:T(2,128)S(1)} %copy-done.3, bf16[640,128]{1,0:T(8,128)(2,1)S(1)} %forward.1.after), custom_call_target="tpu_custom_call" | custom-call | tf_op jit(solution)/shard_map/mask/pallas_call | solution.py:273
  31.6 3.0 %collective-permute-done.10.refs_3_ = bf16[640,128]{1,0:T(8,128)(2,1)S(1)} collective-permute-done((bf16[640,128]{1,0:T(8,128)(2,1)S(1)}, bf16[640,128]{1,0:T(8,128)(2,1)S(1)}, u32[]{:S(2)}, u32[]{:S(2)}) %collective-permute-start.10) | collective-permute-done | bytes 163872 | tf_op jit(solution)/shard_map/ppermute | solution.py:48
  34.5 0.0 collective-permute-done.9.refs_2_
  34.5 2.6 %collective-permute-done.8.refs_1_ = bf16[640,128]{1,0:T(8,128)(2,1)S(1)} collective-permute-done((bf16[640,128]{1,0:T(8,128)(2,1)S(1)}, bf16[640,128]{1,0:T(8,128)(2,1)S(1)}, u32[]{:S(2)}, u32[]{:S(2)}) %collective-permute-start.8) | collective-permute-done | bytes 163872 | tf_op jit(solution)/shard_map/ppermute | solution.py:35
  37.1 0.3 couple.1.scaled
  37.5 0.1 collective-permute-start.11
  37.6 0.0 copy-done.1
  37.6 1.3 %begin.1.begun = f32[4,2048,256]{2,1,0:T(8,128)S(1)} custom-call(bf16[2048,512]{1,0:T(8,128)(2,1)S(1)} %copy-done.1, bf16[8,256,128]{2,1,0:T(8,128)(2,1)S(1)} %couple.1.scaled), custom_call_target="tpu_custom_call" | custom-call | flops 1073741824 | bytes 2097152 | tf_op jit(solution)/shard_map/begin/pallas_call | solution.py:339
  38.8 0.6 %collective-permute-done.11.other = bf16[8,256,128]{2,1,0:T(8,128)(2,1)S(1)} collective-permute-done((bf16[8,256,128]{2,1,0:T(8,128)(2,1)S(1)}, bf16[8,256,128]{2,1,0:T(8,128)(2,1)S(1)}, u32[]{:S(2)}, u32[]{:S(2)}) %collective-permute-start.11) | collective-permute-done | bytes 524320 | tf_op jit(solution)/shard_map/ppermute | solution.py:35
  39.4 3.1 %finish.1 = bf16[2048,1024]{1,0:T(8,128)(2,1)} custom-call(bf16[2048,512]{1,0:T(8,128)(2,1)S(1)} %copy-done.1, f32[4,2048,256]{2,1,0:T(8,128)S(1)} %begin.1.begun, bf16[8,256,128]{2,1,0:T(8,128)(2,1)S(1)} %collective-permute-done.11.other), custom_call_target="tpu_custom_call" | custom-call | flops 1073741824 | bytes 6291456 | tf_op jit(solution)/shard_map/finish/pallas_call | solution.py:379
  (4 shorter events, 0.1 us)
Async XLA Ops:
  0.0 2.8 %copy-start = (bf16[2048,1024]{1,0:T(8,128)(2,1)S(1)}, bf16[2048,1024]{1,0:T(8,128)(2,1)}, u32[]{:S(2)}) copy-start(bf16[2048,1024]{1,0:T(8,128)(2,1)} %refs_1_.5) | copy-start | bytes 12582916
  0.0 3.6 %collective-permute-start.1 = (f32[256,256]{1,0:T(8,128)}, f32[256,256]{1,0:T(8,128)S(1)}, u32[]{:S(2)}, u32[]{:S(2)}) collective-permute-start(f32[256,256]{1,0:T(8,128)} %bitcast.1), channel_id=1, source_target_pairs={{0,1},{1,0},{2,3},{3,2},{4,5},{5,4},{6,7},{7,6},{8,9},{9,8},{10,11... | collective-permute-start | bytes 786440 | tf_op jit(solution)/shard_map/ppermute | solution.py:35
  3.6 2.0 %copy-start.5 = (s32[2]{0:T(128)S(1)}, s32[2]{0:T(128)}, u32[]{:S(2)}) copy-start(s32[2]{0:T(128)} %param.10) | copy-start | bytes 28
  3.6 2.1 %copy-start.2 = (f32[1,256,256]{2,1,0:T(8,128)S(1)}, f32[1,256,256]{2,1,0:T(8,128)}, u32[]{:S(2)}) copy-start(f32[1,256,256]{2,1,0:T(8,128)} %param.11) | copy-start | bytes 786436
  3.6 2.1 %collective-permute-start.2 = (bf16[2,256,128]{2,1,0:T(8,128)(2,1)S(1)}, bf16[2,256,128]{2,1,0:T(8,128)(2,1)S(1)}, u32[]{:S(2)}, u32[]{:S(2)}) collective-permute-start(bf16[2,256,128]{2,1,0:T(8,128)(2,1)S(1)} %get-tuple-element.20), channel_id=1, source_target_pairs={{0,1},{1,0},{2,3},{3,2},{4,5},{5,4},{6,7},{7,6},{8,9},{9,8},{10,11... | collective-permute-start | bytes 393224 | tf_op jit(solution)/shard_map/ppermute | solution.py:35
  5.5 3.4 %collective-permute-start = (bf16[4,256,128]{2,1,0:T(8,128)(2,1)S(1)}, bf16[4,256,128]{2,1,0:T(8,128)(2,1)S(1)}, u32[]{:S(2)}, u32[]{:S(2)}) collective-permute-start(bf16[4,256,128]{2,1,0:T(8,128)(2,1)S(1)} %get-tuple-element.16), channel_id=1, source_target_pairs={{0,1},{1,0},{2,3},{3,2},{4,5},{5,4},{6,7},{7,6},{8,9},{9,8},{10,11... | collective-permute-start | bytes 786440 | tf_op jit(solution)/shard_map/ppermute | solution.py:35
  5.8 6.4 %collective-permute-start.3 = (bf16[640,128]{1,0:T(8,128)(2,1)S(1)}, bf16[640,128]{1,0:T(8,128)(2,1)S(1)}, u32[]{:S(2)}, u32[]{:S(2)}) collective-permute-start(bf16[640,128]{1,0:T(8,128)(2,1)S(1)} %send.2), channel_id=1, source_target_pairs={{0,4},{1,3},{2,6},{3,1},{4,0},{5,7},{6,2},{7,5},{8,12},{9,11},{10,... | collective-permute-start | bytes 491528 | tf_op jit(solution)/shard_map/ppermute | solution.py:48
  8.9 7.6 %collective-permute-start.5 = (bf16[640,128]{1,0:T(8,128)(2,1)S(1)}, bf16[640,128]{1,0:T(8,128)(2,1)S(1)}, u32[]{:S(2)}, u32[]{:S(2)}) collective-permute-start(bf16[640,128]{1,0:T(8,128)(2,1)S(1)} %send.3), channel_id=1, source_target_pairs={{0,4},{1,3},{2,6},{3,1},{4,0},{5,7},{6,2},{7,5},{8,12},{9,11},{10,... | collective-permute-start | bytes 491528 | tf_op jit(solution)/shard_map/ppermute | solution.py:48
  12.2 18.7 %copy-start.3 = (s32[2,256]{1,0:T(2,128)S(1)}, s32[2,256]{1,0:T(2,128)}, u32[]{:S(2)}) copy-start(s32[2,256]{1,0:T(2,128)} %atom_of.1) | copy-start | bytes 6148
  12.2 18.7 %copy-start.4 = (s32[2,4]{1,0:T(2,128)S(1)}, s32[2,4]{1,0:T(2,128)}, u32[]{:S(2)}) copy-start(s32[2,4]{1,0:T(2,128)} %counts.1) | copy-start | bytes 100
  12.2 25.3 %copy-start.1 = (bf16[2048,512]{1,0:T(8,128)(2,1)S(1)}, bf16[2048,512]{1,0:T(8,128)(2,1)}, u32[]{:S(2)}) copy-start(bf16[2048,512]{1,0:T(8,128)(2,1)} %projectors.5) | copy-start | bytes 6291460
  12.3 5.4 %collective-permute-start.6 = (bf16[640,128]{1,0:T(8,128)(2,1)S(1)}, bf16[640,128]{1,0:T(8,128)(2,1)S(1)}, u32[]{:S(2)}, u32[]{:S(2)}) collective-permute-start(bf16[640,128]{1,0:T(8,128)(2,1)S(1)} %forward.1.after), channel_id=1, source_target_pairs={{0,2},{1,5},{2,0},{3,7},{4,6},{5,1},{6,4},{7,3},{8,10},{9,13},{10,... | collective-permute-start | bytes 491528 | tf_op jit(solution)/shard_map/ppermute | solution.py:53
  15.1 1.4 %collective-permute-start.4 = (bf16[2,256,128]{2,1,0:T(8,128)(2,1)S(1)}, bf16[2,256,128]{2,1,0:T(8,128)(2,1)S(1)}, u32[]{:S(2)}, u32[]{:S(2)}) collective-permute-start(bf16[2,256,128]{2,1,0:T(8,128)(2,1)S(1)} %get-tuple-element.22), channel_id=1, source_target_pairs={{0,1},{1,0},{2,3},{3,2},{4,5},{5,4},{6,7},{7,6},{8,9},{9,8},{10,11... | collective-permute-start | bytes 393224 | tf_op jit(solution)/shard_map/ppermute | solution.py:35
  17.7 9.6 %collective-permute-start.7 = (bf16[640,128]{1,0:T(8,128)(2,1)S(1)}, bf16[640,128]{1,0:T(8,128)(2,1)S(1)}, u32[]{:S(2)}, u32[]{:S(2)}) collective-permute-start(bf16[640,128]{1,0:T(8,128)(2,1)S(1)} %get-tuple-element.24), channel_id=1, source_target_pairs={{0,8},{1,9},{2,10},{3,11},{4,12},{5,13},{6,14},{7,15},{8,0},{9,1},... | collective-permute-start | bytes 491528 | tf_op jit(solution)/shard_map/ppermute | solution.py:35
  27.3 7.2 %collective-permute-start.10 = (bf16[640,128]{1,0:T(8,128)(2,1)S(1)}, bf16[640,128]{1,0:T(8,128)(2,1)S(1)}, u32[]{:S(2)}, u32[]{:S(2)}) collective-permute-start(bf16[640,128]{1,0:T(8,128)(2,1)S(1)} %add.1.refs_0_), channel_id=1, source_target_pairs={{0,4},{1,3},{2,6},{3,1},{4,0},{5,7},{6,2},{7,5},{8,12},{9,11},{10,... | collective-permute-start | bytes 491528 | tf_op jit(solution)/shard_map/ppermute | solution.py:48
  28.1 6.4 %collective-permute-start.9 = (bf16[640,128]{1,0:T(8,128)(2,1)S(1)}, bf16[640,128]{1,0:T(8,128)(2,1)S(1)}, u32[]{:S(2)}, u32[]{:S(2)}) collective-permute-start(bf16[640,128]{1,0:T(8,128)(2,1)S(1)} %add.1.refs_0_), channel_id=1, source_target_pairs={{0,2},{1,5},{2,0},{3,7},{4,6},{5,1},{6,4},{7,3},{8,10},{9,13},{10,... | collective-permute-start | bytes 491528 | tf_op jit(solution)/shard_map/ppermute | solution.py:53
  29.1 8.1 %collective-permute-start.8 = (bf16[640,128]{1,0:T(8,128)(2,1)S(1)}, bf16[640,128]{1,0:T(8,128)(2,1)S(1)}, u32[]{:S(2)}, u32[]{:S(2)}) collective-permute-start(bf16[640,128]{1,0:T(8,128)(2,1)S(1)} %add.1.refs_0_), channel_id=1, source_target_pairs={{0,6},{1,7},{2,4},{3,5},{4,2},{5,3},{6,0},{7,1},{8,14},{9,15},{10,... | collective-permute-start | bytes 491528 | tf_op jit(solution)/shard_map/ppermute | solution.py:35
  37.5 2.0 %collective-permute-start.11 = (bf16[8,256,128]{2,1,0:T(8,128)(2,1)S(1)}, bf16[8,256,128]{2,1,0:T(8,128)(2,1)S(1)}, u32[]{:S(2)}, u32[]{:S(2)}) collective-permute-start(bf16[8,256,128]{2,1,0:T(8,128)(2,1)S(1)} %couple.1.scaled), channel_id=1, source_target_pairs={{0,1},{1,0},{2,3},{3,2},{4,5},{5,4},{6,7},{7,6},{8,9},{9,8},{10,11... | collective-permute-start | bytes 1572872 | tf_op jit(solution)/shard_map/ppermute | solution.py:35

commit v24 on v22

--- a/solution.py
+++ b/solution.py
@@ -66,34 +66,67 @@
         theirs[2 * at + entry] = sums[PCAP:, lanes].astype(theirs.dtype)
 
 
-def load_kernel(projectors, flipped, slots, sems):
+def load_kernel(projectors, bands, theirs, ours, flipped, columns, slots, totals, slot_sems, column_sems):
     core = place()[0]
-    count = sems.shape[0]
-    block = slots.shape[0] // count
+    count = slot_sems.shape[0]
+    depth = slots.shape[0] // count
     copies = []
     for at in range(count):
-        rows = slice(at * block, (at + 1) * block)
-        copies.append(pltpu.make_async_copy(projectors.at[rows], slots.at[rows], sems.at[at]))
-        copies[-1].start(priority=at % 2)
-    for at, copy in enumerate(copies):
-        copy.wait()
-        rows = slice(at * block, (at + 1) * block)
+        rows = slice(at * depth, (at + 1) * depth)
+        copies.append(
+            (
+                pltpu.make_async_copy(projectors.at[rows], slots.at[rows], slot_sems.at[at]),
+                pltpu.make_async_copy(bands.at[rows], columns.at[rows], column_sems.at[at]),
+            )
+        )
+    for pair in copies[:2]:
+        for copy in pair:
+            copy.start()
+    for at in range(count):
+        rows = slice(at * depth, (at + 1) * depth)
+        copies[at][0].wait()
+        if at + 2 < count:
+            copies[at + 2][0].start()
         for side, group in enumerate((core, 1 - core)):
             start = pl.multiple_of(group * PCAP, PCAP)
             flipped[side * PCAP : (side + 1) * PCAP, rows] = slots[rows, pl.ds(start, PCAP)].T
-
-
-def load(projectors):
+        copies[at][1].wait()
+        if at + 2 < count:
+            copies[at + 2][1].start()
+        sums = jnp.dot(flipped[:, rows], pair_at(columns, rows, 3), preferred_element_type=jnp.float32)
+        if at:
+            sums = totals[...] + sums
+        if at < count - 1:
+            totals[...] = sums
+        else:
+            keep_sums(ours, theirs, 0, sums)
+
+
+def load(projectors, band_coeffs):
     depth, slots = projectors.shape
+    shape = (2, PCAP, LANES)
     return pl.pallas_call(
         load_kernel,
-        in_specs=[HBM],
-        out_specs=VMEM,
-        out_shape=jax.ShapeDtypeStruct((slots, depth), jnp.bfloat16),
-        scratch_shapes=[pltpu.VMEM((depth, slots), jnp.bfloat16), pltpu.SemaphoreType.DMA((4,))],
+        in_specs=[HBM, HBM],
+        out_specs=[VMEM] * 4,
+        out_shape=[
+            jax.ShapeDtypeStruct(shape, jnp.bfloat16),
+            jax.ShapeDtypeStruct(shape, jnp.float32),
+            jax.ShapeDtypeStruct((slots, depth), jnp.bfloat16),
+            jax.ShapeDtypeStruct(band_coeffs.shape, jnp.bfloat16),
+        ],
+        scratch_shapes=[
+            pltpu.VMEM((depth, slots), jnp.bfloat16),
+            pltpu.VMEM((slots, 2 * LANES), jnp.float32),
+            pltpu.SemaphoreType.DMA((4,)),
+            pltpu.SemaphoreType.DMA((4,)),
+        ],
         compiler_params=PARAMS,
         name="load",
-    )(pltpu.with_memory_space_constraint(projectors, pltpu.HBM))
+    )(
+        pltpu.with_memory_space_constraint(projectors, pltpu.HBM),
+        pltpu.with_memory_space_constraint(band_coeffs, pltpu.HBM),
+    )
 
 
 def project_kernel(parts, flipped, columns, theirs, ours):
@@ -120,7 +153,7 @@
             flops=4 * depth * slots * len(parts) * LANES, bytes_accessed=2 * depth * slots, transcendentals=0
         ),
         name="project",
-    )(flipped, pltpu.with_memory_space_constraint(band_coeffs, pltpu.VMEM))
+    )(flipped, band_coeffs)
 
 
 def project_plain(projectors, band_coeffs, parts):
@@ -412,16 +445,17 @@
     own_table = couplings[0]
     sibling_table = swap_cores(own_table)
     if fast:
-        flipped = load(projectors)
+        theirs, ours, flipped, columns = load(projectors, band_coeffs)
 
         def partial(parts):
-            return project(flipped, band_coeffs, parts)
+            return project(flipped, columns, parts)
     else:
 
         def partial(parts):
             return project_plain(projectors, band_coeffs, parts)
 
-    theirs, ours = partial((3,))
+        theirs, ours = partial((3,))
+
     theirs, sibling_table = lax.optimization_barrier((theirs, sibling_table))
     theirs = swap_cores(theirs)
     pair_theirs, pair_ours = partial((1, 2))

time: 42.4 us -> 42.9 us (1.012)
  Pallas kernels: 10.7 us -> 11.5 us
    pallas_call x1, Pallas kernels: 2.21 us -> 3.77 us  [load(): pl.pallas_call(load_kernel, in_specs=[HBM, HBM], out_specs=[VMEM] * 4, ou...]
    pallas_call x3 -> x2, Pallas kernels: 2.91 us -> 2.12 us  [project(): pl.pallas_call(kernel, in_specs=[VMEM, VMEM], out_specs=[VMEM, VMEM], out...]
    ppermute x7, starting transfers between devices: 5.51 us -> 6.08 us  [swap(): return lax.ppermute(x, 'pw', [(i, i ^ distance) for i in range(count)])]
    ppermute x2, starting transfers between devices: 3.07 us -> 2.53 us  [swap_second(): return lax.ppermute(x, 'pw', [(i, i ^ (2, 4)[i % 2]) for i in range(count)])]
  transfers between devices with their start and end apart: 12 -> 12, of which waited for: 7 -> 8; matrix products, arithmetic and copies ran while one was open for 0% -> 0% of each run, Pallas kernels for 17% -> 18%
where the time goes in v24:
time: 42.9 us; the launch traced here: 42.8 us
  waiting for transfers between devices  17.1 us (40%)
  starting transfers between devices  13.9 us (32%)
  Pallas kernels  11.5 us (27%)
    ppermute x7, waiting for transfers between devices, swap(): return lax.ppermute(x, 'pw', [(i, i ^ distance) for i in range(count)])  12.1 us
    ppermute x7, starting transfers between devices, swap(): return lax.ppermute(x, 'pw', [(i, i ^ distance) for i in range(count)])  6.08 us
    ppermute x3, starting transfers between devices, swap_first(): return lax.ppermute(x, 'pw', [(i, i ^ (4, 2)[i % 2]) for i in range(count)])  5.31 us
    pallas_call x1, Pallas kernels, load(): pl.pallas_call(load_kernel, in_specs=[HBM, HBM], out_specs=[VMEM] * 4, ou...  3.77 us
    pallas_call x1, Pallas kernels, finish(): pl.pallas_call(finish_kernel, in_specs=[VMEM] * 3, out_specs=HBM, out_sha...  3.13 us
    ppermute x2, waiting for transfers between devices, swap_second(): return lax.ppermute(x, 'pw', [(i, i ^ (2, 4)[i % 2]) for i in range(count)])  2.86 us
    ppermute x2, starting transfers between devices, swap_second(): return lax.ppermute(x, 'pw', [(i, i ^ (2, 4)[i % 2]) for i in range(count)])  2.53 us
    pallas_call x2, Pallas kernels, project(): pl.pallas_call(kernel, in_specs=[VMEM, VMEM], out_specs=[VMEM, VMEM], out...  2.12 us
  transfers between devices with their start and end apart: 12, of which 8 were waited for; matrix products, arithmetic and copies ran while one was open for 0% of the time, Pallas kernels for 18%

profile of v24, /device:TPU:0, one launch (start us, length us, event | category | flops | bytes accessed | tf_op | source)
XLA Modules:
  0.0 42.8 jit_solution(16830548824058400643)
XLA Ops:
  0.0 0.5 %collective-permute-start.1 = (f32[256,256]{1,0:T(8,128)}, f32[256,256]{1,0:T(8,128)S(1)}, u32[]{:S(2)}, u32[]{:S(2)}) collective-permute-start(f32[256,256]{1,0:T(8,128)} %bitcast.1), channel_id=1, source_target_pairs={{0,1},{1,0},{2,3},{3,2},{4,5},{5,4},{6,7},{7,6},{8,9},{9,8},{10,11... | collective-permute-start | bytes 786440 | tf_op jit(solution)/shard_map/ppermute | solution.py:35
  0.5 3.8 %load.1 = (bf16[2,256,128]{2,1,0:T(8,128)(2,1)S(1)}, f32[2,256,128]{2,1,0:T(8,128)S(1)}, bf16[512,2048]{1,0:T(8,128)(2,1)S(1)}, bf16[2048,1024]{1,0:T(8,128)(2,1)S(1)}) custom-call(bf16[2048,512]{1,0:T(8,128)(2,1)} %projectors.5, bf16[2048,1024]{1,0:T(8,128)(2,1)} %bands.1), custom_call_target="tpu_custom_call" | custom-call | tf_op jit(solution)/shard_map/load/pallas_call | solution.py:108
  4.2 0.0 copy-start.4
  4.2 0.0 copy-start.1
  4.3 0.0 collective-permute-done.1.sibling
  4.3 0.1 collective-permute-start.2
  4.4 1.3 %project.2 = (bf16[4,256,128]{2,1,0:T(8,128)(2,1)S(1)}, f32[4,256,128]{2,1,0:T(8,128)S(1)}) custom-call(bf16[512,2048]{1,0:T(8,128)(2,1)S(1)} %get-tuple-element.17.refs_0_, bf16[2048,1024]{1,0:T(8,128)(2,1)S(1)} %get-tuple-element.18.refs_1_), custom_call_target="tpu_custom_call" | custom-call | flops 1073741824 | bytes 2097152 | tf_op jit(solution)/shard_map/project/pallas_call | solution.py:146
  5.7 0.5 %collective-permute-start = (bf16[4,256,128]{2,1,0:T(8,128)(2,1)S(1)}, bf16[4,256,128]{2,1,0:T(8,128)(2,1)S(1)}, u32[]{:S(2)}, u32[]{:S(2)}) collective-permute-start(bf16[4,256,128]{2,1,0:T(8,128)(2,1)S(1)} %get-tuple-element.20), channel_id=1, source_target_pairs={{0,1},{1,0},{2,3},{3,2},{4,5},{5,4},{6,7},{7,6},{8,9},{9,8},{10,11... | collective-permute-start | bytes 786440 | tf_op jit(solution)/shard_map/ppermute | solution.py:35
  6.3 0.0 copy-done.4
  6.3 0.1 broadcast_in_dim.2.owners
  6.3 0.0 copy-done.1
  6.4 0.0 collective-permute-done.2.refs_1_
  6.4 2.7 %collective-permute-start.3 = (bf16[640,128]{1,0:T(8,128)(2,1)S(1)}, bf16[640,128]{1,0:T(8,128)(2,1)S(1)}, u32[]{:S(2)}, u32[]{:S(2)}) collective-permute-start(bf16[640,128]{1,0:T(8,128)(2,1)S(1)} %send.2), channel_id=1, source_target_pairs={{0,4},{1,3},{2,6},{3,1},{4,0},{5,7},{6,2},{7,5},{8,12},{9,11},{10,... | collective-permute-start | bytes 491528 | tf_op jit(solution)/shard_map/ppermute | solution.py:48
  9.1 0.0 collective-permute-done.theirs.refs_1_
  9.1 1.3 %collective-permute-start.5 = (bf16[640,128]{1,0:T(8,128)(2,1)S(1)}, bf16[640,128]{1,0:T(8,128)(2,1)S(1)}, u32[]{:S(2)}, u32[]{:S(2)}) collective-permute-start(bf16[640,128]{1,0:T(8,128)(2,1)S(1)} %send.3), channel_id=1, source_target_pairs={{0,4},{1,3},{2,6},{3,1},{4,0},{5,7},{6,2},{7,5},{8,12},{9,11},{10,... | collective-permute-start | bytes 491528 | tf_op jit(solution)/shard_map/ppermute | solution.py:48
  10.4 1.9 %collective-permute-done.3.got = bf16[640,128]{1,0:T(8,128)(2,1)S(1)} collective-permute-done((bf16[640,128]{1,0:T(8,128)(2,1)S(1)}, bf16[640,128]{1,0:T(8,128)(2,1)S(1)}, u32[]{:S(2)}, u32[]{:S(2)}) %collective-permute-start.3) | collective-permute-done | bytes 163872 | tf_op jit(solution)/shard_map/ppermute | solution.py:48
  12.4 0.1 forward.1.after
  12.4 0.0 copy-start.2
  12.4 0.0 copy-start.3
  12.4 0.0 copy-start
  12.5 2.0 %collective-permute-start.6 = (bf16[640,128]{1,0:T(8,128)(2,1)S(1)}, bf16[640,128]{1,0:T(8,128)(2,1)S(1)}, u32[]{:S(2)}, u32[]{:S(2)}) collective-permute-start(bf16[640,128]{1,0:T(8,128)(2,1)S(1)} %forward.1.after), channel_id=1, source_target_pairs={{0,2},{1,5},{2,0},{3,7},{4,6},{5,1},{6,4},{7,3},{8,10},{9,13},{10,... | collective-permute-start | bytes 491528 | tf_op jit(solution)/shard_map/ppermute | solution.py:53
  14.5 0.8 %project.3 = (bf16[2,256,128]{2,1,0:T(8,128)(2,1)S(1)}, f32[2,256,128]{2,1,0:T(8,128)S(1)}) custom-call(bf16[512,2048]{1,0:T(8,128)(2,1)S(1)} %get-tuple-element.17.refs_0_, bf16[2048,1024]{1,0:T(8,128)(2,1)S(1)} %get-tuple-element.18.refs_1_), custom_call_target="tpu_custom_call" | custom-call | flops 536870912 | bytes 2097152 | tf_op jit(solution)/shard_map/project/pallas_call | solution.py:146
  15.3 0.1 collective-permute-start.4
  15.4 1.3 %collective-permute-done.4.theirs = bf16[2,256,128]{2,1,0:T(8,128)(2,1)S(1)} collective-permute-done((bf16[2,256,128]{2,1,0:T(8,128)(2,1)S(1)}, bf16[2,256,128]{2,1,0:T(8,128)(2,1)S(1)}, u32[]{:S(2)}, u32[]{:S(2)}) %collective-permute-start.4) | collective-permute-done | bytes 131104 | tf_op jit(solution)/shard_map/ppermute | solution.py:35
  16.7 0.0 collective-permute-done.5.refs_0_
  16.7 1.1 %collective-permute-done.6.refs_1_ = bf16[640,128]{1,0:T(8,128)(2,1)S(1)} collective-permute-done((bf16[640,128]{1,0:T(8,128)(2,1)S(1)}, bf16[640,128]{1,0:T(8,128)(2,1)S(1)}, u32[]{:S(2)}, u32[]{:S(2)}) %collective-permute-start.6) | collective-permute-done | bytes 163872 | tf_op jit(solution)/shard_map/ppermute | solution.py:53
  17.8 0.1 fold.1
  17.9 3.1 %collective-permute-start.7 = (bf16[640,128]{1,0:T(8,128)(2,1)S(1)}, bf16[640,128]{1,0:T(8,128)(2,1)S(1)}, u32[]{:S(2)}, u32[]{:S(2)}) collective-permute-start(bf16[640,128]{1,0:T(8,128)(2,1)S(1)} %get-tuple-element.28), channel_id=1, source_target_pairs={{0,8},{1,9},{2,10},{3,11},{4,12},{5,13},{6,14},{7,15},{8,0},{9,1},... | collective-permute-start | bytes 491528 | tf_op jit(solution)/shard_map/ppermute | solution.py:35
  21.0 6.6 %collective-permute-done.7.right = bf16[640,128]{1,0:T(8,128)(2,1)S(1)} collective-permute-done((bf16[640,128]{1,0:T(8,128)(2,1)S(1)}, bf16[640,128]{1,0:T(8,128)(2,1)S(1)}, u32[]{:S(2)}, u32[]{:S(2)}) %collective-permute-start.7) | collective-permute-done | bytes 163872 | tf_op jit(solution)/shard_map/ppermute | solution.py:35
  27.7 1.7 %collective-permute-start.10 = (bf16[640,128]{1,0:T(8,128)(2,1)S(1)}, bf16[640,128]{1,0:T(8,128)(2,1)S(1)}, u32[]{:S(2)}, u32[]{:S(2)}) collective-permute-start(bf16[640,128]{1,0:T(8,128)(2,1)S(1)} %add.1.refs_0_), channel_id=1, source_target_pairs={{0,6},{1,7},{2,4},{3,5},{4,2},{5,3},{6,0},{7,1},{8,14},{9,15},{10,... | collective-permute-start | bytes 491528 | tf_op jit(solution)/shard_map/ppermute | solution.py:35
  29.4 0.5 %collective-permute-start.9 = (bf16[640,128]{1,0:T(8,128)(2,1)S(1)}, bf16[640,128]{1,0:T(8,128)(2,1)S(1)}, u32[]{:S(2)}, u32[]{:S(2)}) collective-permute-start(bf16[640,128]{1,0:T(8,128)(2,1)S(1)} %add.1.refs_0_), channel_id=1, source_target_pairs={{0,2},{1,5},{2,0},{3,7},{4,6},{5,1},{6,4},{7,3},{8,10},{9,13},{10,... | collective-permute-start | bytes 491528 | tf_op jit(solution)/shard_map/ppermute | solution.py:53
  29.9 1.3 %collective-permute-start.8 = (bf16[640,128]{1,0:T(8,128)(2,1)S(1)}, bf16[640,128]{1,0:T(8,128)(2,1)S(1)}, u32[]{:S(2)}, u32[]{:S(2)}) collective-permute-start(bf16[640,128]{1,0:T(8,128)(2,1)S(1)} %add.1.refs_0_), channel_id=1, source_target_pairs={{0,4},{1,3},{2,6},{3,1},{4,0},{5,7},{6,2},{7,5},{8,12},{9,11},{10,... | collective-permute-start | bytes 491528 | tf_op jit(solution)/shard_map/ppermute | solution.py:48
  31.2 0.0 copy-done.2
  31.2 0.0 copy-done.3
  31.2 0.7 %mask.1.allowed = bf16[256,256]{1,0:T(8,128)(2,1)S(1)} custom-call(s32[2,4]{1,0:T(2,128)S(1)} %copy-done.3, s32[2,256]{1,0:T(2,128)S(1)} %copy-done.2, bf16[640,128]{1,0:T(8,128)(2,1)S(1)} %forward.1.after), custom_call_target="tpu_custom_call" | custom-call | tf_op jit(solution)/shard_map/mask/pallas_call | solution.py:306
  31.9 3.5 %collective-permute-done.10.refs_3_ = bf16[640,128]{1,0:T(8,128)(2,1)S(1)} collective-permute-done((bf16[640,128]{1,0:T(8,128)(2,1)S(1)}, bf16[640,128]{1,0:T(8,128)(2,1)S(1)}, u32[]{:S(2)}, u32[]{:S(2)}) %collective-permute-start.10) | collective-permute-done | bytes 163872 | tf_op jit(solution)/shard_map/ppermute | solution.py:35
  35.4 1.7 %collective-permute-done.9.refs_2_ = bf16[640,128]{1,0:T(8,128)(2,1)S(1)} collective-permute-done((bf16[640,128]{1,0:T(8,128)(2,1)S(1)}, bf16[640,128]{1,0:T(8,128)(2,1)S(1)}, u32[]{:S(2)}, u32[]{:S(2)}) %collective-permute-start.9) | collective-permute-done | bytes 163872 | tf_op jit(solution)/shard_map/ppermute | solution.py:53
  37.1 0.2 collective-permute-done.8.refs_1_
  37.3 0.3 couple.1.scaled
  37.6 0.1 collective-permute-start.11
  37.7 0.0 copy-done
  37.7 1.3 %begin.1.begun = f32[4,2048,256]{2,1,0:T(8,128)S(1)} custom-call(bf16[2048,512]{1,0:T(8,128)(2,1)S(1)} %copy-done, bf16[8,256,128]{2,1,0:T(8,128)(2,1)S(1)} %couple.1.scaled), custom_call_target="tpu_custom_call" | custom-call | flops 1073741824 | bytes 2097152 | tf_op jit(solution)/shard_map/begin/pallas_call | solution.py:372
  39.0 0.6 %collective-permute-done.11.other = bf16[8,256,128]{2,1,0:T(8,128)(2,1)S(1)} collective-permute-done((bf16[8,256,128]{2,1,0:T(8,128)(2,1)S(1)}, bf16[8,256,128]{2,1,0:T(8,128)(2,1)S(1)}, u32[]{:S(2)}, u32[]{:S(2)}) %collective-permute-start.11) | collective-permute-done | bytes 524320 | tf_op jit(solution)/shard_map/ppermute | solution.py:35
  39.6 3.1 %finish.1 = bf16[2048,1024]{1,0:T(8,128)(2,1)} custom-call(bf16[2048,512]{1,0:T(8,128)(2,1)S(1)} %copy-done, f32[4,2048,256]{2,1,0:T(8,128)S(1)} %begin.1.begun, bf16[8,256,128]{2,1,0:T(8,128)(2,1)S(1)} %collective-permute-done.11.other), custom_call_target="tpu_custom_call" | custom-call | flops 1073741824 | bytes 6291456 | tf_op jit(solution)/shard_map/finish/pallas_call | solution.py:412
  (4 shorter events, 0.1 us)
Async XLA Ops:
  0.0 4.3 %collective-permute-start.1 = (f32[256,256]{1,0:T(8,128)}, f32[256,256]{1,0:T(8,128)S(1)}, u32[]{:S(2)}, u32[]{:S(2)}) collective-permute-start(f32[256,256]{1,0:T(8,128)} %bitcast.1), channel_id=1, source_target_pairs={{0,1},{1,0},{2,3},{3,2},{4,5},{5,4},{6,7},{7,6},{8,9},{9,8},{10,11... | collective-permute-start | bytes 786440 | tf_op jit(solution)/shard_map/ppermute | solution.py:35
  4.2 2.0 %copy-start.4 = (s32[2]{0:T(128)S(1)}, s32[2]{0:T(128)}, u32[]{:S(2)}) copy-start(s32[2]{0:T(128)} %param.10) | copy-start | bytes 28
  4.2 2.1 %copy-start.1 = (f32[1,256,256]{2,1,0:T(8,128)S(1)}, f32[1,256,256]{2,1,0:T(8,128)}, u32[]{:S(2)}) copy-start(f32[1,256,256]{2,1,0:T(8,128)} %param.11) | copy-start | bytes 786436
  4.3 2.1 %collective-permute-start.2 = (bf16[2,256,128]{2,1,0:T(8,128)(2,1)S(1)}, bf16[2,256,128]{2,1,0:T(8,128)(2,1)S(1)}, u32[]{:S(2)}, u32[]{:S(2)}) collective-permute-start(bf16[2,256,128]{2,1,0:T(8,128)(2,1)S(1)} %get-tuple-element.24), channel_id=1, source_target_pairs={{0,1},{1,0},{2,3},{3,2},{4,5},{5,4},{6,7},{7,6},{8,9},{9,8},{10,11... | collective-permute-start | bytes 393224 | tf_op jit(solution)/shard_map/ppermute | solution.py:35
  5.7 3.3 %collective-permute-start = (bf16[4,256,128]{2,1,0:T(8,128)(2,1)S(1)}, bf16[4,256,128]{2,1,0:T(8,128)(2,1)S(1)}, u32[]{:S(2)}, u32[]{:S(2)}) collective-permute-start(bf16[4,256,128]{2,1,0:T(8,128)(2,1)S(1)} %get-tuple-element.20), channel_id=1, source_target_pairs={{0,1},{1,0},{2,3},{3,2},{4,5},{5,4},{6,7},{7,6},{8,9},{9,8},{10,11... | collective-permute-start | bytes 786440 | tf_op jit(solution)/shard_map/ppermute | solution.py:35
  6.4 6.0 %collective-permute-start.3 = (bf16[640,128]{1,0:T(8,128)(2,1)S(1)}, bf16[640,128]{1,0:T(8,128)(2,1)S(1)}, u32[]{:S(2)}, u32[]{:S(2)}) collective-permute-start(bf16[640,128]{1,0:T(8,128)(2,1)S(1)} %send.2), channel_id=1, source_target_pairs={{0,4},{1,3},{2,6},{3,1},{4,0},{5,7},{6,2},{7,5},{8,12},{9,11},{10,... | collective-permute-start | bytes 491528 | tf_op jit(solution)/shard_map/ppermute | solution.py:48
  9.1 7.6 %collective-permute-start.5 = (bf16[640,128]{1,0:T(8,128)(2,1)S(1)}, bf16[640,128]{1,0:T(8,128)(2,1)S(1)}, u32[]{:S(2)}, u32[]{:S(2)}) collective-permute-start(bf16[640,128]{1,0:T(8,128)(2,1)S(1)} %send.3), channel_id=1, source_target_pairs={{0,4},{1,3},{2,6},{3,1},{4,0},{5,7},{6,2},{7,5},{8,12},{9,11},{10,... | collective-permute-start | bytes 491528 | tf_op jit(solution)/shard_map/ppermute | solution.py:48
  12.4 18.8 %copy-start.2 = (s32[2,256]{1,0:T(2,128)S(1)}, s32[2,256]{1,0:T(2,128)}, u32[]{:S(2)}) copy-start(s32[2,256]{1,0:T(2,128)} %atom_of.1) | copy-start | bytes 6148
  12.4 18.8 %copy-start.3 = (s32[2,4]{1,0:T(2,128)S(1)}, s32[2,4]{1,0:T(2,128)}, u32[]{:S(2)}) copy-start(s32[2,4]{1,0:T(2,128)} %counts.1) | copy-start | bytes 100
  12.4 25.3 %copy-start = (bf16[2048,512]{1,0:T(8,128)(2,1)S(1)}, bf16[2048,512]{1,0:T(8,128)(2,1)}, u32[]{:S(2)}) copy-start(bf16[2048,512]{1,0:T(8,128)(2,1)} %projectors.5) | copy-start | bytes 6291460
  12.5 5.4 %collective-permute-start.6 = (bf16[640,128]{1,0:T(8,128)(2,1)S(1)}, bf16[640,128]{1,0:T(8,128)(2,1)S(1)}, u32[]{:S(2)}, u32[]{:S(2)}) collective-permute-start(bf16[640,128]{1,0:T(8,128)(2,1)S(1)} %forward.1.after), channel_id=1, source_target_pairs={{0,2},{1,5},{2,0},{3,7},{4,6},{5,1},{6,4},{7,3},{8,10},{9,13},{10,... | collective-permute-start | bytes 491528 | tf_op jit(solution)/shard_map/ppermute | solution.py:53
  15.3 1.4 %collective-permute-start.4 = (bf16[2,256,128]{2,1,0:T(8,128)(2,1)S(1)}, bf16[2,256,128]{2,1,0:T(8,128)(2,1)S(1)}, u32[]{:S(2)}, u32[]{:S(2)}) collective-permute-start(bf16[2,256,128]{2,1,0:T(8,128)(2,1)S(1)} %get-tuple-element.26), channel_id=1, source_target_pairs={{0,1},{1,0},{2,3},{3,2},{4,5},{5,4},{6,7},{7,6},{8,9},{9,8},{10,11... | collective-permute-start | bytes 393224 | tf_op jit(solution)/shard_map/ppermute | solution.py:35
  17.9 9.7 %collective-permute-start.7 = (bf16[640,128]{1,0:T(8,128)(2,1)S(1)}, bf16[640,128]{1,0:T(8,128)(2,1)S(1)}, u32[]{:S(2)}, u32[]{:S(2)}) collective-permute-start(bf16[640,128]{1,0:T(8,128)(2,1)S(1)} %get-tuple-element.28), channel_id=1, source_target_pairs={{0,8},{1,9},{2,10},{3,11},{4,12},{5,13},{6,14},{7,15},{8,0},{9,1},... | collective-permute-start | bytes 491528 | tf_op jit(solution)/shard_map/ppermute | solution.py:35
  27.7 7.7 %collective-permute-start.10 = (bf16[640,128]{1,0:T(8,128)(2,1)S(1)}, bf16[640,128]{1,0:T(8,128)(2,1)S(1)}, u32[]{:S(2)}, u32[]{:S(2)}) collective-permute-start(bf16[640,128]{1,0:T(8,128)(2,1)S(1)} %add.1.refs_0_), channel_id=1, source_target_pairs={{0,6},{1,7},{2,4},{3,5},{4,2},{5,3},{6,0},{7,1},{8,14},{9,15},{10,... | collective-permute-start | bytes 491528 | tf_op jit(solution)/shard_map/ppermute | solution.py:35
  29.4 7.7 %collective-permute-start.9 = (bf16[640,128]{1,0:T(8,128)(2,1)S(1)}, bf16[640,128]{1,0:T(8,128)(2,1)S(1)}, u32[]{:S(2)}, u32[]{:S(2)}) collective-permute-start(bf16[640,128]{1,0:T(8,128)(2,1)S(1)} %add.1.refs_0_), channel_id=1, source_target_pairs={{0,2},{1,5},{2,0},{3,7},{4,6},{5,1},{6,4},{7,3},{8,10},{9,13},{10,... | collective-permute-start | bytes 491528 | tf_op jit(solution)/shard_map/ppermute | solution.py:53
  29.9 7.4 %collective-permute-start.8 = (bf16[640,128]{1,0:T(8,128)(2,1)S(1)}, bf16[640,128]{1,0:T(8,128)(2,1)S(1)}, u32[]{:S(2)}, u32[]{:S(2)}) collective-permute-start(bf16[640,128]{1,0:T(8,128)(2,1)S(1)} %add.1.refs_0_), channel_id=1, source_target_pairs={{0,4},{1,3},{2,6},{3,1},{4,0},{5,7},{6,2},{7,5},{8,12},{9,11},{10,... | collective-permute-start | bytes 491528 | tf_op jit(solution)/shard_map/ppermute | solution.py:48
  37.6 2.0 %collective-permute-start.11 = (bf16[8,256,128]{2,1,0:T(8,128)(2,1)S(1)}, bf16[8,256,128]{2,1,0:T(8,128)(2,1)S(1)}, u32[]{:S(2)}, u32[]{:S(2)}) collective-permute-start(bf16[8,256,128]{2,1,0:T(8,128)(2,1)S(1)} %couple.1.scaled), channel_id=1, source_target_pairs={{0,1},{1,0},{2,3},{3,2},{4,5},{5,4},{6,7},{7,6},{8,9},{9,8},{10,11... | collective-permute-start | bytes 1572872 | tf_op jit(solution)/shard_map/ppermute | solution.py:35

commit v25 on v22

--- a/solution.py
+++ b/solution.py
@@ -12,7 +12,7 @@
 SQUARE = 4
 QUARTER = PCAP // SQUARE
 ROW_BLOCK = 512
-ROW_BLOCKS = (256,) * 8
+ROW_BLOCKS = (128, 128) + (256,) * 6 + (128, 128)
 COPY_ROWS = 128
 PARAMS = pltpu.CompilerParams(vmem_limit_bytes=40 * 1024 * 1024)
 VMEM = pl.BlockSpec(memory_space=pltpu.VMEM)

time: 42.4 us -> 42.5 us (level)
  no operation moved by 1% of the time
where the time goes in v25:
time: 42.5 us; the launch traced here: 42.3 us
  waiting for transfers between devices  17.2 us (40%)
  starting transfers between devices  14 us (33%)
  Pallas kernels  10.8 us (25%)
    ppermute x7, waiting for transfers between devices, swap(): return lax.ppermute(x, 'pw', [(i, i ^ distance) for i in range(count)])  12 us
    ppermute x7, starting transfers between devices, swap(): return lax.ppermute(x, 'pw', [(i, i ^ distance) for i in range(count)])  5.51 us
    ppermute x3, starting transfers between devices, swap_first(): return lax.ppermute(x, 'pw', [(i, i ^ (4, 2)[i % 2]) for i in range(count)])  5.42 us
    pallas_call x1, Pallas kernels, finish(): pl.pallas_call(finish_kernel, in_specs=[VMEM] * 3, out_specs=HBM, out_sha...  3.15 us
    ppermute x2, starting transfers between devices, swap_second(): return lax.ppermute(x, 'pw', [(i, i ^ (2, 4)[i % 2]) for i in range(count)])  3.07 us
    pallas_call x3, Pallas kernels, project(): pl.pallas_call(kernel, in_specs=[VMEM, VMEM], out_specs=[VMEM, VMEM], out...  2.91 us
    ppermute x2, waiting for transfers between devices, swap_second(): return lax.ppermute(x, 'pw', [(i, i ^ (2, 4)[i % 2]) for i in range(count)])  2.86 us
    ppermute x3, waiting for transfers between devices, swap_first(): return lax.ppermute(x, 'pw', [(i, i ^ (4, 2)[i % 2]) for i in range(count)])  2.28 us
  transfers between devices with their start and end apart: 12, of which 7 were waited for; matrix products, arithmetic and copies ran while one was open for 0% of the time, Pallas kernels for 17%

profile of v25, /device:TPU:0, one launch (start us, length us, event | category | flops | bytes accessed | tf_op | source)
XLA Modules:
  0.0 42.3 jit_solution(9061429152626138623)
XLA Ops:
  0.0 0.0 copy-start
  0.0 0.5 %collective-permute-start.1 = (f32[256,256]{1,0:T(8,128)}, f32[256,256]{1,0:T(8,128)S(1)}, u32[]{:S(2)}, u32[]{:S(2)}) collective-permute-start(f32[256,256]{1,0:T(8,128)} %bitcast.1), channel_id=1, source_target_pairs={{0,1},{1,0},{2,3},{3,2},{4,5},{5,4},{6,7},{7,6},{8,9},{9,8},{10,11... | collective-permute-start | bytes 786440 | tf_op jit(solution)/shard_map/ppermute | solution.py:35
  0.5 2.2 %load.1.refs_0_ = bf16[512,2048]{1,0:T(8,128)(2,1)S(1)} custom-call(bf16[2048,512]{1,0:T(8,128)(2,1)} %projectors.5), custom_call_target="tpu_custom_call" | custom-call | tf_op jit(solution)/shard_map/load/pallas_call | solution.py:88
  2.7 0.1 copy-done
  2.8 0.8 %project.4 = (bf16[2,256,128]{2,1,0:T(8,128)(2,1)S(1)}, f32[2,256,128]{2,1,0:T(8,128)S(1)}) custom-call(bf16[512,2048]{1,0:T(8,128)(2,1)S(1)} %load.1.refs_0_, bf16[2048,1024]{1,0:T(8,128)(2,1)S(1)} %copy-done), custom_call_target="tpu_custom_call" | custom-call | flops 536870912 | bytes 2097152 | tf_op jit(solution)/shard_map/project/pallas_call | solution.py:113
  3.6 0.0 copy-start.5
  3.6 0.0 copy-start.2
  3.6 0.0 collective-permute-done.1.sibling
  3.6 0.5 %collective-permute-start.2 = (bf16[2,256,128]{2,1,0:T(8,128)(2,1)S(1)}, bf16[2,256,128]{2,1,0:T(8,128)(2,1)S(1)}, u32[]{:S(2)}, u32[]{:S(2)}) collective-permute-start(bf16[2,256,128]{2,1,0:T(8,128)(2,1)S(1)} %get-tuple-element.20), channel_id=1, source_target_pairs={{0,1},{1,0},{2,3},{3,2},{4,5},{5,4},{6,7},{7,6},{8,9},{9,8},{10,11... | collective-permute-start | bytes 393224 | tf_op jit(solution)/shard_map/ppermute | solution.py:35
  4.2 1.3 %project.3 = (bf16[4,256,128]{2,1,0:T(8,128)(2,1)S(1)}, f32[4,256,128]{2,1,0:T(8,128)S(1)}) custom-call(bf16[512,2048]{1,0:T(8,128)(2,1)S(1)} %load.1.refs_0_, bf16[2048,1024]{1,0:T(8,128)(2,1)S(1)} %copy-done), custom_call_target="tpu_custom_call" | custom-call | flops 1073741824 | bytes 2097152 | tf_op jit(solution)/shard_map/project/pallas_call | solution.py:113
  5.5 0.1 collective-permute-start
  5.6 0.0 copy-done.5
  5.6 0.1 broadcast_in_dim.2.owners
  5.7 0.0 copy-done.2
  5.7 0.0 collective-permute-done.2.refs_1_
  5.8 3.1 %collective-permute-start.3 = (bf16[640,128]{1,0:T(8,128)(2,1)S(1)}, bf16[640,128]{1,0:T(8,128)(2,1)S(1)}, u32[]{:S(2)}, u32[]{:S(2)}) collective-permute-start(bf16[640,128]{1,0:T(8,128)(2,1)S(1)} %send.2), channel_id=1, source_target_pairs={{0,4},{1,3},{2,6},{3,1},{4,0},{5,7},{6,2},{7,5},{8,12},{9,11},{10,... | collective-permute-start | bytes 491528 | tf_op jit(solution)/shard_map/ppermute | solution.py:48
  8.9 0.0 collective-permute-done.theirs.refs_1_
  8.9 1.0 %collective-permute-start.5 = (bf16[640,128]{1,0:T(8,128)(2,1)S(1)}, bf16[640,128]{1,0:T(8,128)(2,1)S(1)}, u32[]{:S(2)}, u32[]{:S(2)}) collective-permute-start(bf16[640,128]{1,0:T(8,128)(2,1)S(1)} %send.3), channel_id=1, source_target_pairs={{0,4},{1,3},{2,6},{3,1},{4,0},{5,7},{6,2},{7,5},{8,12},{9,11},{10,... | collective-permute-start | bytes 491528 | tf_op jit(solution)/shard_map/ppermute | solution.py:48
  9.9 2.3 %collective-permute-done.3.got = bf16[640,128]{1,0:T(8,128)(2,1)S(1)} collective-permute-done((bf16[640,128]{1,0:T(8,128)(2,1)S(1)}, bf16[640,128]{1,0:T(8,128)(2,1)S(1)}, u32[]{:S(2)}, u32[]{:S(2)}) %collective-permute-start.3) | collective-permute-done | bytes 163872 | tf_op jit(solution)/shard_map/ppermute | solution.py:48
  12.2 0.1 forward.1.after
  12.2 0.0 copy-start.3
  12.2 0.0 copy-start.4
  12.2 0.0 copy-start.1
  12.3 2.0 %collective-permute-start.6 = (bf16[640,128]{1,0:T(8,128)(2,1)S(1)}, bf16[640,128]{1,0:T(8,128)(2,1)S(1)}, u32[]{:S(2)}, u32[]{:S(2)}) collective-permute-start(bf16[640,128]{1,0:T(8,128)(2,1)S(1)} %forward.1.after), channel_id=1, source_target_pairs={{0,2},{1,5},{2,0},{3,7},{4,6},{5,1},{6,4},{7,3},{8,10},{9,13},{10,... | collective-permute-start | bytes 491528 | tf_op jit(solution)/shard_map/ppermute | solution.py:53
  14.3 0.8 %project.5 = (bf16[2,256,128]{2,1,0:T(8,128)(2,1)S(1)}, f32[2,256,128]{2,1,0:T(8,128)S(1)}) custom-call(bf16[512,2048]{1,0:T(8,128)(2,1)S(1)} %load.1.refs_0_, bf16[2048,1024]{1,0:T(8,128)(2,1)S(1)} %copy-done), custom_call_target="tpu_custom_call" | custom-call | flops 536870912 | bytes 2097152 | tf_op jit(solution)/shard_map/project/pallas_call | solution.py:113
  15.1 0.1 collective-permute-start.4
  15.2 1.3 %collective-permute-done.4.theirs = bf16[2,256,128]{2,1,0:T(8,128)(2,1)S(1)} collective-permute-done((bf16[2,256,128]{2,1,0:T(8,128)(2,1)S(1)}, bf16[2,256,128]{2,1,0:T(8,128)(2,1)S(1)}, u32[]{:S(2)}, u32[]{:S(2)}) %collective-permute-start.4) | collective-permute-done | bytes 131104 | tf_op jit(solution)/shard_map/ppermute | solution.py:35
  16.5 0.0 collective-permute-done.5.refs_0_
  16.5 1.1 %collective-permute-done.6.refs_1_ = bf16[640,128]{1,0:T(8,128)(2,1)S(1)} collective-permute-done((bf16[640,128]{1,0:T(8,128)(2,1)S(1)}, bf16[640,128]{1,0:T(8,128)(2,1)S(1)}, u32[]{:S(2)}, u32[]{:S(2)}) %collective-permute-start.6) | collective-permute-done | bytes 163872 | tf_op jit(solution)/shard_map/ppermute | solution.py:53
  17.6 0.1 fold.1
  17.7 3.1 %collective-permute-start.7 = (bf16[640,128]{1,0:T(8,128)(2,1)S(1)}, bf16[640,128]{1,0:T(8,128)(2,1)S(1)}, u32[]{:S(2)}, u32[]{:S(2)}) collective-permute-start(bf16[640,128]{1,0:T(8,128)(2,1)S(1)} %get-tuple-element.24), channel_id=1, source_target_pairs={{0,8},{1,9},{2,10},{3,11},{4,12},{5,13},{6,14},{7,15},{8,0},{9,1},... | collective-permute-start | bytes 491528 | tf_op jit(solution)/shard_map/ppermute | solution.py:35
  20.8 6.5 %collective-permute-done.7.right = bf16[640,128]{1,0:T(8,128)(2,1)S(1)} collective-permute-done((bf16[640,128]{1,0:T(8,128)(2,1)S(1)}, bf16[640,128]{1,0:T(8,128)(2,1)S(1)}, u32[]{:S(2)}, u32[]{:S(2)}) %collective-permute-start.7) | collective-permute-done | bytes 163872 | tf_op jit(solution)/shard_map/ppermute | solution.py:35
  27.3 1.2 %collective-permute-start.10 = (bf16[640,128]{1,0:T(8,128)(2,1)S(1)}, bf16[640,128]{1,0:T(8,128)(2,1)S(1)}, u32[]{:S(2)}, u32[]{:S(2)}) collective-permute-start(bf16[640,128]{1,0:T(8,128)(2,1)S(1)} %add.1.refs_0_), channel_id=1, source_target_pairs={{0,6},{1,7},{2,4},{3,5},{4,2},{5,3},{6,0},{7,1},{8,14},{9,15},{10,... | collective-permute-start | bytes 491528 | tf_op jit(solution)/shard_map/ppermute | solution.py:35
  28.5 1.0 %collective-permute-start.9 = (bf16[640,128]{1,0:T(8,128)(2,1)S(1)}, bf16[640,128]{1,0:T(8,128)(2,1)S(1)}, u32[]{:S(2)}, u32[]{:S(2)}) collective-permute-start(bf16[640,128]{1,0:T(8,128)(2,1)S(1)} %add.1.refs_0_), channel_id=1, source_target_pairs={{0,2},{1,5},{2,0},{3,7},{4,6},{5,1},{6,4},{7,3},{8,10},{9,13},{10,... | collective-permute-start | bytes 491528 | tf_op jit(solution)/shard_map/ppermute | solution.py:53
  29.6 1.4 %collective-permute-start.8 = (bf16[640,128]{1,0:T(8,128)(2,1)S(1)}, bf16[640,128]{1,0:T(8,128)(2,1)S(1)}, u32[]{:S(2)}, u32[]{:S(2)}) collective-permute-start(bf16[640,128]{1,0:T(8,128)(2,1)S(1)} %add.1.refs_0_), channel_id=1, source_target_pairs={{0,4},{1,3},{2,6},{3,1},{4,0},{5,7},{6,2},{7,5},{8,12},{9,11},{10,... | collective-permute-start | bytes 491528 | tf_op jit(solution)/shard_map/ppermute | solution.py:48
  30.9 0.0 copy-done.3
  30.9 0.0 copy-done.4
  30.9 0.7 %mask.1.allowed = bf16[256,256]{1,0:T(8,128)(2,1)S(1)} custom-call(s32[2,4]{1,0:T(2,128)S(1)} %copy-done.4, s32[2,256]{1,0:T(2,128)S(1)} %copy-done.3, bf16[640,128]{1,0:T(8,128)(2,1)S(1)} %forward.1.after), custom_call_target="tpu_custom_call" | custom-call | tf_op jit(solution)/shard_map/mask/pallas_call | solution.py:273
  31.6 3.6 %collective-permute-done.10.refs_3_ = bf16[640,128]{1,0:T(8,128)(2,1)S(1)} collective-permute-done((bf16[640,128]{1,0:T(8,128)(2,1)S(1)}, bf16[640,128]{1,0:T(8,128)(2,1)S(1)}, u32[]{:S(2)}, u32[]{:S(2)}) %collective-permute-start.10) | collective-permute-done | bytes 163872 | tf_op jit(solution)/shard_map/ppermute | solution.py:35
  35.1 1.7 %collective-permute-done.9.refs_2_ = bf16[640,128]{1,0:T(8,128)(2,1)S(1)} collective-permute-done((bf16[640,128]{1,0:T(8,128)(2,1)S(1)}, bf16[640,128]{1,0:T(8,128)(2,1)S(1)}, u32[]{:S(2)}, u32[]{:S(2)}) %collective-permute-start.9) | collective-permute-done | bytes 163872 | tf_op jit(solution)/shard_map/ppermute | solution.py:53
  36.9 0.0 collective-permute-done.8.refs_1_
  36.9 0.3 couple.1.scaled
  37.2 0.1 collective-permute-start.11
  37.3 0.0 copy-done.1
  37.3 1.3 %begin.1.begun = f32[4,2048,256]{2,1,0:T(8,128)S(1)} custom-call(bf16[2048,512]{1,0:T(8,128)(2,1)S(1)} %copy-done.1, bf16[8,256,128]{2,1,0:T(8,128)(2,1)S(1)} %couple.1.scaled), custom_call_target="tpu_custom_call" | custom-call | flops 1073741824 | bytes 2097152 | tf_op jit(solution)/shard_map/begin/pallas_call | solution.py:339
  38.5 0.6 %collective-permute-done.11.other = bf16[8,256,128]{2,1,0:T(8,128)(2,1)S(1)} collective-permute-done((bf16[8,256,128]{2,1,0:T(8,128)(2,1)S(1)}, bf16[8,256,128]{2,1,0:T(8,128)(2,1)S(1)}, u32[]{:S(2)}, u32[]{:S(2)}) %collective-permute-start.11) | collective-permute-done | bytes 524320 | tf_op jit(solution)/shard_map/ppermute | solution.py:35
  39.2 3.2 %finish.1 = bf16[2048,1024]{1,0:T(8,128)(2,1)} custom-call(bf16[2048,512]{1,0:T(8,128)(2,1)S(1)} %copy-done.1, f32[4,2048,256]{2,1,0:T(8,128)S(1)} %begin.1.begun, bf16[8,256,128]{2,1,0:T(8,128)(2,1)S(1)} %collective-permute-done.11.other), custom_call_target="tpu_custom_call" | custom-call | flops 1073741824 | bytes 6291456 | tf_op jit(solution)/shard_map/finish/pallas_call | solution.py:379
  (4 shorter events, 0.1 us)
Async XLA Ops:
  0.0 2.8 %copy-start = (bf16[2048,1024]{1,0:T(8,128)(2,1)S(1)}, bf16[2048,1024]{1,0:T(8,128)(2,1)}, u32[]{:S(2)}) copy-start(bf16[2048,1024]{1,0:T(8,128)(2,1)} %refs_1_.5) | copy-start | bytes 12582916
  0.0 3.6 %collective-permute-start.1 = (f32[256,256]{1,0:T(8,128)}, f32[256,256]{1,0:T(8,128)S(1)}, u32[]{:S(2)}, u32[]{:S(2)}) collective-permute-start(f32[256,256]{1,0:T(8,128)} %bitcast.1), channel_id=1, source_target_pairs={{0,1},{1,0},{2,3},{3,2},{4,5},{5,4},{6,7},{7,6},{8,9},{9,8},{10,11... | collective-permute-start | bytes 786440 | tf_op jit(solution)/shard_map/ppermute | solution.py:35
  3.6 2.0 %copy-start.5 = (s32[2]{0:T(128)S(1)}, s32[2]{0:T(128)}, u32[]{:S(2)}) copy-start(s32[2]{0:T(128)} %param.10) | copy-start | bytes 28
  3.6 2.1 %copy-start.2 = (f32[1,256,256]{2,1,0:T(8,128)S(1)}, f32[1,256,256]{2,1,0:T(8,128)}, u32[]{:S(2)}) copy-start(f32[1,256,256]{2,1,0:T(8,128)} %param.11) | copy-start | bytes 786436
  3.6 2.1 %collective-permute-start.2 = (bf16[2,256,128]{2,1,0:T(8,128)(2,1)S(1)}, bf16[2,256,128]{2,1,0:T(8,128)(2,1)S(1)}, u32[]{:S(2)}, u32[]{:S(2)}) collective-permute-start(bf16[2,256,128]{2,1,0:T(8,128)(2,1)S(1)} %get-tuple-element.20), channel_id=1, source_target_pairs={{0,1},{1,0},{2,3},{3,2},{4,5},{5,4},{6,7},{7,6},{8,9},{9,8},{10,11... | collective-permute-start | bytes 393224 | tf_op jit(solution)/shard_map/ppermute | solution.py:35
  5.5 3.4 %collective-permute-start = (bf16[4,256,128]{2,1,0:T(8,128)(2,1)S(1)}, bf16[4,256,128]{2,1,0:T(8,128)(2,1)S(1)}, u32[]{:S(2)}, u32[]{:S(2)}) collective-permute-start(bf16[4,256,128]{2,1,0:T(8,128)(2,1)S(1)} %get-tuple-element.16), channel_id=1, source_target_pairs={{0,1},{1,0},{2,3},{3,2},{4,5},{5,4},{6,7},{7,6},{8,9},{9,8},{10,11... | collective-permute-start | bytes 786440 | tf_op jit(solution)/shard_map/ppermute | solution.py:35
  5.8 6.4 %collective-permute-start.3 = (bf16[640,128]{1,0:T(8,128)(2,1)S(1)}, bf16[640,128]{1,0:T(8,128)(2,1)S(1)}, u32[]{:S(2)}, u32[]{:S(2)}) collective-permute-start(bf16[640,128]{1,0:T(8,128)(2,1)S(1)} %send.2), channel_id=1, source_target_pairs={{0,4},{1,3},{2,6},{3,1},{4,0},{5,7},{6,2},{7,5},{8,12},{9,11},{10,... | collective-permute-start | bytes 491528 | tf_op jit(solution)/shard_map/ppermute | solution.py:48
  8.9 7.6 %collective-permute-start.5 = (bf16[640,128]{1,0:T(8,128)(2,1)S(1)}, bf16[640,128]{1,0:T(8,128)(2,1)S(1)}, u32[]{:S(2)}, u32[]{:S(2)}) collective-permute-start(bf16[640,128]{1,0:T(8,128)(2,1)S(1)} %send.3), channel_id=1, source_target_pairs={{0,4},{1,3},{2,6},{3,1},{4,0},{5,7},{6,2},{7,5},{8,12},{9,11},{10,... | collective-permute-start | bytes 491528 | tf_op jit(solution)/shard_map/ppermute | solution.py:48
  12.2 18.7 %copy-start.3 = (s32[2,256]{1,0:T(2,128)S(1)}, s32[2,256]{1,0:T(2,128)}, u32[]{:S(2)}) copy-start(s32[2,256]{1,0:T(2,128)} %atom_of.1) | copy-start | bytes 6148
  12.2 18.7 %copy-start.4 = (s32[2,4]{1,0:T(2,128)S(1)}, s32[2,4]{1,0:T(2,128)}, u32[]{:S(2)}) copy-start(s32[2,4]{1,0:T(2,128)} %counts.1) | copy-start | bytes 100
  12.2 25.0 %copy-start.1 = (bf16[2048,512]{1,0:T(8,128)(2,1)S(1)}, bf16[2048,512]{1,0:T(8,128)(2,1)}, u32[]{:S(2)}) copy-start(bf16[2048,512]{1,0:T(8,128)(2,1)} %projectors.5) | copy-start | bytes 6291460
  12.3 5.4 %collective-permute-start.6 = (bf16[640,128]{1,0:T(8,128)(2,1)S(1)}, bf16[640,128]{1,0:T(8,128)(2,1)S(1)}, u32[]{:S(2)}, u32[]{:S(2)}) collective-permute-start(bf16[640,128]{1,0:T(8,128)(2,1)S(1)} %forward.1.after), channel_id=1, source_target_pairs={{0,2},{1,5},{2,0},{3,7},{4,6},{5,1},{6,4},{7,3},{8,10},{9,13},{10,... | collective-permute-start | bytes 491528 | tf_op jit(solution)/shard_map/ppermute | solution.py:53
  15.1 1.4 %collective-permute-start.4 = (bf16[2,256,128]{2,1,0:T(8,128)(2,1)S(1)}, bf16[2,256,128]{2,1,0:T(8,128)(2,1)S(1)}, u32[]{:S(2)}, u32[]{:S(2)}) collective-permute-start(bf16[2,256,128]{2,1,0:T(8,128)(2,1)S(1)} %get-tuple-element.22), channel_id=1, source_target_pairs={{0,1},{1,0},{2,3},{3,2},{4,5},{5,4},{6,7},{7,6},{8,9},{9,8},{10,11... | collective-permute-start | bytes 393224 | tf_op jit(solution)/shard_map/ppermute | solution.py:35
  17.7 9.6 %collective-permute-start.7 = (bf16[640,128]{1,0:T(8,128)(2,1)S(1)}, bf16[640,128]{1,0:T(8,128)(2,1)S(1)}, u32[]{:S(2)}, u32[]{:S(2)}) collective-permute-start(bf16[640,128]{1,0:T(8,128)(2,1)S(1)} %get-tuple-element.24), channel_id=1, source_target_pairs={{0,8},{1,9},{2,10},{3,11},{4,12},{5,13},{6,14},{7,15},{8,0},{9,1},... | collective-permute-start | bytes 491528 | tf_op jit(solution)/shard_map/ppermute | solution.py:35
  27.3 7.8 %collective-permute-start.10 = (bf16[640,128]{1,0:T(8,128)(2,1)S(1)}, bf16[640,128]{1,0:T(8,128)(2,1)S(1)}, u32[]{:S(2)}, u32[]{:S(2)}) collective-permute-start(bf16[640,128]{1,0:T(8,128)(2,1)S(1)} %add.1.refs_0_), channel_id=1, source_target_pairs={{0,6},{1,7},{2,4},{3,5},{4,2},{5,3},{6,0},{7,1},{8,14},{9,15},{10,... | collective-permute-start | bytes 491528 | tf_op jit(solution)/shard_map/ppermute | solution.py:35
  28.5 8.3 %collective-permute-start.9 = (bf16[640,128]{1,0:T(8,128)(2,1)S(1)}, bf16[640,128]{1,0:T(8,128)(2,1)S(1)}, u32[]{:S(2)}, u32[]{:S(2)}) collective-permute-start(bf16[640,128]{1,0:T(8,128)(2,1)S(1)} %add.1.refs_0_), channel_id=1, source_target_pairs={{0,2},{1,5},{2,0},{3,7},{4,6},{5,1},{6,4},{7,3},{8,10},{9,13},{10,... | collective-permute-start | bytes 491528 | tf_op jit(solution)/shard_map/ppermute | solution.py:53
  29.6 7.3 %collective-permute-start.8 = (bf16[640,128]{1,0:T(8,128)(2,1)S(1)}, bf16[640,128]{1,0:T(8,128)(2,1)S(1)}, u32[]{:S(2)}, u32[]{:S(2)}) collective-permute-start(bf16[640,128]{1,0:T(8,128)(2,1)S(1)} %add.1.refs_0_), channel_id=1, source_target_pairs={{0,4},{1,3},{2,6},{3,1},{4,0},{5,7},{6,2},{7,5},{8,12},{9,11},{10,... | collective-permute-start | bytes 491528 | tf_op jit(solution)/shard_map/ppermute | solution.py:48
  37.2 2.0 %collective-permute-start.11 = (bf16[8,256,128]{2,1,0:T(8,128)(2,1)S(1)}, bf16[8,256,128]{2,1,0:T(8,128)(2,1)S(1)}, u32[]{:S(2)}, u32[]{:S(2)}) collective-permute-start(bf16[8,256,128]{2,1,0:T(8,128)(2,1)S(1)} %couple.1.scaled), channel_id=1, source_target_pairs={{0,1},{1,0},{2,3},{3,2},{4,5},{5,4},{6,7},{7,6},{8,9},{9,8},{10,11... | collective-permute-start | bytes 1572872 | tf_op jit(solution)/shard_map/ppermute | solution.py:35
